TPU v7x, 32 devices: a whole 2x2x4 slice. The times are simulated.
32 devices in a mesh: grp: 2 (over core), fsdp: 4 (over y, x), dp: 4 (over z).
Axes of the slice: x: 2, y: 2, z: 4, core: 2. Of those that a mesh axis runs over, the one named last changes fastest.
Arguments:
- acts: bfloat16 [2, 2432, 1024], P('grp', None, 'dp'), may hold values from -12 to 12
- modulation: float32 [2, 3, 2432], P('grp'), may hold values from -3 to 3
- w_in: bfloat16 [2, 9728, 2432], P('grp', 'fsdp'), may hold values from -0.125 to 0.125
- w_out: bfloat16 [2, 9728, 2432], P('grp', 'fsdp'), may hold values from -0.0625 to 0.0625
- zero_weight: bfloat16 [2432, 2432], P('fsdp'), may hold values from -0.125 to 0.125
- cotangent: bfloat16 [2, 2432, 1024], P('grp', 'fsdp', 'dp'), may hold values from -0.75 to 0.75
Outputs:
- block_out: bfloat16 [2, 2432, 1024], P('grp', 'fsdp', 'dp')
- input_grad: float32 [2, 2432, 1024], P('grp', 'fsdp', 'dp')
- zero_grad: float32 [2432, 2432], P('fsdp')
All inputs are finite; a program needn't handle non-finite values.
Results may differ from a plain program's by a relative error of at most 0.0048.
Values may be sent and summed in bfloat16 or wider, within the bound.
No kernel may reach another device: no remote copies, remote signals or barrier semaphores. Data moves between devices by JAX's collectives and lax.ppermute only.
A program may use at most 128 MiB of HBM per device.

v0:
```python
from functools import partial

import jax
import jax.numpy as jnp
from jax import lax
from jax.sharding import PartitionSpec as P

EPSILON = 1e-06


def passed_along(value, axis, by):
    length = lax.axis_size(axis)
    pairs = [(i, i + by) for i in range(length) if 0 <= i + by < length]
    return lax.ppermute(value, axis, pairs)


def layer_norm(values, mod_shift, mod_scale):
    token_mean = jnp.mean(values, axis=0, keepdims=True)
    centred = values - token_mean
    variance = jnp.mean(centred * centred, axis=0, keepdims=True)
    return centred * lax.rsqrt(variance + EPSILON) * (1.0 + mod_scale[:, None]) + mod_shift[:, None]


def contract_rows(weights, columns):
    return lax.dot_general(
        weights, columns, (((0,), (0,)), ((), ())), preferred_element_type=jnp.float32
    )


def sum_features(product):
    return lax.psum(product, "fsdp")


def local(acts, modulation, w_in, w_out, zero_weight, cotangent):
    inputs = acts[0]
    mod_shift = modulation[0, 0]
    mod_scale = modulation[0, 1]
    mod_gate = modulation[0, 2]
    w_first = w_in[0]
    w_second = w_out[0]
    own_grads = cotangent[0]
    feature_count, tokens = inputs.shape
    row_count = own_grads.shape[0]
    half_tokens = tokens // 2
    is_control = lax.axis_index("grp") == 0
    offset = lax.axis_index("fsdp") * row_count
    values = inputs.astype(jnp.float32)
    normed = layer_norm(values, mod_shift, mod_scale).astype(jnp.bfloat16)
    pre_act = jnp.dot(w_first, normed, preferred_element_type=jnp.float32)
    hidden = jax.nn.gelu(pre_act, approximate=True).astype(jnp.bfloat16)
    branch_term = contract_rows(w_second, hidden)
    own_values = lax.dynamic_slice_in_dim(values, offset, row_count, 0)
    own_gate = lax.dynamic_slice_in_dim(mod_gate, offset, row_count, 0)
    empty_rows = jnp.zeros((row_count, tokens), jnp.float32)
    branch = sum_features(branch_term)
    full_mixed = (values + mod_gate[:, None] * branch).astype(jnp.bfloat16)
    arrived = passed_along(full_mixed, "grp", 1)
    control_out = jnp.where(is_control, full_mixed, arrived)
    own_branch = lax.dynamic_slice_in_dim(branch, offset, row_count, 0)
    residual = lax.cond(
        is_control,
        lambda: empty_rows,
        lambda: jnp.dot(zero_weight, control_out, preferred_element_type=jnp.float32),
    )
    block_rows = (own_values + own_gate[:, None] * own_branch + residual).astype(jnp.bfloat16)
    received = passed_along(own_grads, "grp", -1)
    grad_rows = jnp.where(is_control, received, own_grads)
    token_start = jnp.where(is_control, 0, half_tokens).astype(jnp.int32)
    grad_part = lax.dynamic_slice_in_dim(grad_rows, token_start, half_tokens, 1)
    hidden_part = lax.dynamic_slice_in_dim(control_out, token_start, half_tokens, 1)
    zero_term = lax.dot_general(
        grad_part, hidden_part, (((1,), (1,)), ((), ())), preferred_element_type=jnp.float32
    )
    zero_grad = lax.psum(zero_term, ("grp", "dp"))
    carried = lax.cond(
        is_control,
        lambda: contract_rows(zero_weight, received),
        lambda: jnp.zeros((feature_count, tokens), jnp.float32),
    )
    own_rows = lax.dynamic_slice_in_dim(carried, offset, row_count, 0) + own_grads.astype(
        jnp.float32
    )
    upstream = sum_features(lax.dynamic_update_slice_in_dim(carried, own_rows, offset, 0))
    gate_grad = (mod_gate[:, None] * upstream).astype(jnp.bfloat16)
    hidden_grad = jnp.dot(w_second, gate_grad, preferred_element_type=jnp.float32)
    gelu_back = jax.vjp(partial(jax.nn.gelu, approximate=True), pre_act)[1]
    pre_grad = gelu_back(hidden_grad)[0].astype(jnp.bfloat16)
    norm_term = contract_rows(w_first, pre_grad)
    norm_grad = lax.psum(norm_term, "fsdp")
    norm_back = jax.vjp(partial(layer_norm, mod_shift=mod_shift, mod_scale=mod_scale), values)[1]
    input_full = upstream + norm_back(norm_grad)[0]
    input_rows = lax.dynamic_slice_in_dim(input_full, offset, row_count, 0)
    return (block_rows[None], input_rows[None], zero_grad)


def solution(mesh):
    placed = (
        P("grp", None, "dp"),
        P("grp", None, None),
        P("grp", "fsdp", None),
        P("grp", "fsdp", None),
        P("fsdp", None),
        P("grp", "fsdp", "dp"),
    )
    return jax.shard_map(
        local,
        mesh=mesh,
        in_specs=placed,
        out_specs=(P("grp", "fsdp", "dp"), P("grp", "fsdp", "dp"), P("fsdp", None)),
        check_vma=False,
    )
```

profile of v0, /device:TPU:0, one launch (start us, length us, event | category | flops | bytes accessed | tf_op | source)
XLA Modules:
  0.0 394.8 jit_solution(7641430809238322186)
XLA Ops:
  7.2 0.0 all-reduce.5.cloned.1.call-start
  7.2 1.2 copy.20
  8.4 1.3 collective-permute-start.1
  9.7 1.7 copy.17
  11.4 0.2 convert_reduce_fusion
  11.6 0.5 multiply_reduce_fusion.1
  12.1 0.0 collective-permute-done.1
  12.1 3.0 conditional.3
  12.1 3.0 fusion.71
  15.1 0.0 copy-start
  15.2 1.4 copy-done
  16.6 0.0 copy-start.4
  16.6 0.2 convert_add_fusion
  16.8 4.5 %dynamic_update_slice.3 = f32[2432,256]{0,1:T(8,128)} dynamic-update-slice(f32[2432,256]{0,1:T(8,128)} %copy-done, f32[608,256]{0,1:T(8,128)S(1)} %convert_add_fusion, s32[]{:T(128)S(6)} %select_n.30, s32[]{:T(128)} %constant.12.clone.1) | dynamic-update-slice | bytes 1245188 | tf_op jit(solution)/shard_map/dynamic_update_slice | solution.py:83
  21.4 0.0 all-reduce.5.cloned.1.call-update
  21.4 0.2 all-reduce.9.cloned.1.call-start
  21.6 0.0 copy-done.4
  21.7 0.1 slice_reduce_fusion.1
  21.7 6.8 %fusion.8 = f32[2432,256]{0,1:T(8,128)S(1)} fusion(bf16[1,2432,2432]{2,1,0:T(8,128)(2,1)} %param.12, bf16[1,2432,256]{1,2,0:T(8,128)(2,1)S(1)} %copy.17, f32[2432]{0:T(1024)S(1)} %get-tuple-element.38, f32[2432]{0:T(1024)S(1)} %get-tuple-element.39, f32[256]{0:T(256)S(1)} %fusion.58, f32[256]{0:T(256)S(1)} %broadcast_multiply_fusion), kind=kOutput, calls=%fused_computation.8 | convolution fusion | flops 3032023040 | bytes 15586304 | tf_op jit(solution)/shard_map/dot_general | solution.py:49
  28.5 0.0 copy-start.5
  28.5 1.6 copy-done.5
  30.1 9.5 %fusion.14 = f32[2432,256]{0,1:T(8,128)} fusion(bf16[1,2432,2432]{2,1,0:T(8,128)(2,1)} %param.13, f32[2432,256]{0,1:T(8,128)S(1)} %fusion.8), kind=kOutput, calls=%fused_computation.10 | convolution fusion | flops 3033890816 | bytes 16809984 | tf_op jit(solution)/shard_map/dot_general | solution.py:25
  39.7 60.6 %all-reduce.5.cloned.1.call-done = f32[2432,256]{0,1:T(8,128)} async-done(((f32[2432,256]{0,1:T(8,128)}), f32[2432,256]{0,1:T(8,128)}) %all-reduce.5.cloned.1.call-update) | async-done | bytes 2490384 | tf_op jit(solution)/shard_map/psum | solution.py:31
  100.3 18.2 %fusion.11 = f32[2432,256]{0,1:T(8,128)} fusion(bf16[1,2432,2432]{2,1,0:T(8,128)(2,1)} %param.12, f32[2432,256]{0,1:T(8,128)} %copy-done.5, bf16[1,2432,2432]{2,1,0:T(8,128)(2,1)} %param.13, f32[2432,256]{0,1:T(8,128)} %all-reduce.5.cloned.1.call-done, f32[2432]{0:T(1024)S(1)} %get-tuple-element.37), kind=kOutput, calls=%fused_computation.9 | convolution fusion | flops 6070272000 | bytes 31139328 | tf_op jit(solution)/shard_map/dot_general | solution.py:25
  118.4 0.0 all-reduce.9.cloned.1.call-update
  118.5 0.3 all-reduce.7.cloned.1.call-start
  118.7 117.0 %all-reduce.9.cloned.1.call-done = (f32[2432,256]{0,1:T(8,128)}, f32[2432,256]{0,1:T(8,128)}) async-done(((f32[2432,256]{0,1:T(8,128)}, f32[2432,256]{0,1:T(8,128)}), (f32[2432,256]{0,1:T(8,128)}, f32[2432,256]{0,1:T(8,128)})) %all-reduce.9.cloned.1.call-update) | async-done | bytes 4980752 | tf_op jit(solution)/shard_map/psum | solution.py:31
  235.8 0.0 copy-start.1
  235.8 2.4 multiply_reduce_fusion
  238.2 0.0 copy-done.1
  238.2 4.2 %fusion.69 = (f32[256]{0:T(256)S(1)}, f32[2432,256]{0,1:T(8,128)}, bf16[2432,256]{0,1:T(8,128)(2,1)S(1)}) fusion(f32[256]{0:T(256)S(1)} %multiply_multiply_fusion.2, f32[256]{0:T(256)S(1)} %broadcast_multiply_fusion, bf16[1,2432,256]{1,2,0:T(8,128)(2,1)S(1)} %copy.17, f32[256]{0:T(256)S(1)} %fusion.58, f32[2432,256]{0,1:T(8,128)S(1)} %copy-done.1, ...), kind=kLoop, calls=%fused_computation.80 | loop fusion | flops 6848256 | bytes 9985024 | tf_op jit(solution)/shard_map/transpose(jvp())/reduce_sum | solution.py:19
  242.4 2.8 collective-permute-start
  245.2 1.6 collective-permute-done
  246.9 0.1 broadcast_select_fusion
  247.0 0.0 copy-start.2
  247.0 1.0 copy-done.2
  248.0 3.5 fusion.52
  251.6 0.0 all-reduce.7.cloned.1.call-update
  251.6 1.6 convert_element_type.35
  253.2 0.0 copy-start.3
  253.2 0.1 dynamic-slice_reduce_fusion
  253.3 1.9 dynamic-slice_add_fusion
  255.2 1.1 copy.24
  256.3 0.0 copy-done.3
  256.3 1.8 fusion.54
  258.1 0.9 copy.25
  259.0 123.7 %all-reduce.7.cloned.1.call-done = f32[608,2432]{1,0:T(8,128)} async-done(((f32[608,2432]{1,0:T(8,128)}), f32[608,2432]{1,0:T(8,128)}) %all-reduce.7.cloned.1.call-update) | async-done | bytes 5914640 | tf_op jit(solution)/shard_map/psum | solution.py:74
  382.7 5.6 %copy.41 = f32[608,2432]{1,0:T(8,128)} copy(f32[608,2432]{1,0:T(8,128)} %all-reduce.7.cloned.1.call-done) | data formatting | bytes 11829248
  (6 shorter events, 0.1 us)
Async XLA Ops:
  7.2 93.1 %all-reduce.5.cloned.1.call-start = ((), (), s32[]{:S(2)}) async-start(), calls=%async_computation | async-start | bytes 4980736 | tf_op jit(solution)/shard_map/psum | solution.py:31
  8.4 3.7 collective-permute-start.1
  15.1 1.4 copy-start
  16.6 5.1 %copy-start.4 = (f32[1,3,2432]{2,0,1:T(1,128)S(1)}, f32[1,3,2432]{2,0,1:T(1,128)}, u32[]{:S(2)}) copy-start(f32[1,3,2432]{2,0,1:T(1,128)} %param.11) | copy-start | bytes 87556
  21.4 214.4 %all-reduce.9.cloned.1.call-start = ((), (), s32[]{:S(2)}) async-start(), calls=%async_computation.2 | async-start | bytes 9961472 | tf_op jit(solution)/shard_map/psum | solution.py:31
  28.5 1.6 copy-start.5
  118.5 264.2 %all-reduce.7.cloned.1.call-start = ((), (), s32[]{:S(2)}) async-start(), calls=%async_computation.1 | async-start | bytes 11829248 | tf_op jit(solution)/shard_map/psum | solution.py:74
  235.8 2.5 copy-start.1
  242.4 4.4 %collective-permute-start = (bf16[2432,256]{0,1:T(8,128)(2,1)S(1)}, bf16[2432,256]{0,1:T(8,128)(2,1)}, u32[]{:S(2)}, u32[]{:S(2)}) collective-permute-start(bf16[2432,256]{0,1:T(8,128)(2,1)S(1)} %get-tuple-element.44), channel_id=1, source_target_pairs={{0,16},{1,17},{2,18},{3,19},{4,20},{5,21},{6,22},{7,23},{8,24},{9,... | collective-permute-start | bytes 3735560 | tf_op jit(solution)/shard_map/ppermute | solution.py:14
  247.0 1.0 copy-start.2
  253.2 3.1 copy-start.3
Sparse Core Ops, SparseCore 0:
  21.5 78.7 all-reduce.4
  118.6 117.1 all-reduce.8
  251.7 130.8 all-reduce.6
where the time goes:
time: 395 us
  waiting for transfers between devices  303 us (77%)
  matrix products  41 us (10%)
  local copies, waits for them, and re-layouts  19.2 us (5%)
  between operations  13.9 us (4%)
  other arithmetic  13.1 us (3%)
  starting transfers between devices  4.59 us (1%)
    psum x2, waiting for transfers between devices, sum_features(): return lax.psum(product, 'fsdp')  178 us
    psum x1, waiting for transfers between devices, local(): zero_grad = lax.psum(zero_term, ('grp', 'dp'))  124 us
    dot_general x2, matrix products, contract_rows(): lax.dot_general(weights, columns, (((0,), (0,)), ((), ())), preferred_ele...  27.7 us
    unnamed x16, local copies, waits for them, and re-layouts  13.5 us
  transfers between devices with their start and end apart: 5, of which 4 were waited for; matrix products, arithmetic and copies ran while one was open for 7% of the time, Pallas kernels for 0%

commit v1 on v0

v1 whole, which is shorter than its diff:
```python
import jax
import jax.numpy as jnp
from jax import lax
from jax.sharding import PartitionSpec as P

EPSILON = 1e-06
SQRT_2_OVER_PI = 0.7978845608028654


def contract_rows(weights, columns):
    return lax.dot_general(
        weights, columns, (((0,), (0,)), ((), ())), preferred_element_type=jnp.float32
    )


def swap_fsdp(value, mask):
    length = lax.axis_size("fsdp")
    return lax.ppermute(value, "fsdp", [(i, i ^ mask) for i in range(length)])


def swap_grp(value):
    return lax.ppermute(value, "grp", [(0, 1), (1, 0)])


def block_of(value, index, rows):
    return lax.dynamic_slice_in_dim(value, index * rows, rows, 0)


def scatter_sum(term, rows, me):
    total = block_of(term, me, rows)
    for mask in range(1, lax.axis_size("fsdp")):
        sent = block_of(term, me ^ mask, rows).astype(jnp.bfloat16)
        total = total + swap_fsdp(sent, mask).astype(jnp.float32)
    return total


def gather_rows(value, me):
    length = lax.axis_size("fsdp")
    rows = value.shape[0]
    full = jnp.zeros((length * rows,) + value.shape[1:], value.dtype)
    full = lax.dynamic_update_slice_in_dim(full, value, me * rows, 0)
    for mask in range(1, length):
        full = lax.dynamic_update_slice_in_dim(full, swap_fsdp(value, mask), (me ^ mask) * rows, 0)
    return full


def gelu_and_slope(v):
    inner = SQRT_2_OVER_PI * (v + 0.044715 * v * v * v)
    t = jnp.tanh(inner)
    slope = 0.5 * (1.0 + t) + 0.5 * v * (1.0 - t * t) * SQRT_2_OVER_PI * (1.0 + 3 * 0.044715 * v * v)
    return 0.5 * v * (1.0 + t), slope


def local(acts, modulation, w_in, w_out, zero_weight, cotangent):
    inputs = acts[0]
    shift, scale, gate = modulation[0, 0], modulation[0, 1], modulation[0, 2]
    w_first, w_second = w_in[0], w_out[0]
    own_cot = cotangent[0]
    features, tokens = inputs.shape
    rows = own_cot.shape[0]
    half = tokens // 2
    group = lax.axis_index("grp")
    is_control = group == 0
    me = lax.axis_index("fsdp")

    mine = lax.dynamic_slice_in_dim(own_cot, group * half, half, 1)
    other = lax.dynamic_slice_in_dim(own_cot, (1 - group) * half, half, 1)
    arrived = swap_grp(other)
    cot1 = jnp.where(is_control, arrived, mine)
    cot0 = jnp.where(is_control, mine, arrived)
    gate0 = jnp.where(is_control, gate, swap_grp(gate))
    own_gate = block_of(gate, me, rows)
    own_gate0 = block_of(gate0, me, rows)

    up_term = contract_rows(zero_weight, cot1)
    up_half = scatter_sum(up_term, rows, me) + cot0.astype(jnp.float32)
    gated = gather_rows((own_gate0[:, None] * up_half).astype(jnp.bfloat16), me)
    cot1_full = gather_rows(cot1, me)
    crossed = swap_grp(jnp.where(is_control, cot1_full, gated))
    gate_grad = jnp.where(
        is_control,
        jnp.concatenate([gated, crossed], 1),
        (gate[:, None] * jnp.concatenate([crossed, cot1_full], 1).astype(jnp.float32)).astype(jnp.bfloat16),
    )
    up_rows = jnp.where(
        is_control,
        jnp.concatenate([up_half, swap_grp(up_half)], 1),
        own_cot.astype(jnp.float32),
    )

    values = inputs.astype(jnp.float32)
    mean = jnp.mean(values, axis=0, keepdims=True)
    centred = values - mean
    inv = lax.rsqrt(jnp.mean(centred * centred, axis=0, keepdims=True) + EPSILON)
    xhat = centred * inv
    normed = (xhat * (1.0 + scale[:, None]) + shift[:, None]).astype(jnp.bfloat16)
    pre_act = jnp.dot(w_first, normed, preferred_element_type=jnp.float32)
    hidden, slope = gelu_and_slope(pre_act)
    branch_term = contract_rows(w_second, hidden.astype(jnp.bfloat16))
    branch = scatter_sum(branch_term, rows, me)
    own_values = block_of(inputs, me, rows).astype(jnp.float32)
    sums = own_values + own_gate[:, None] * branch
    out_rows = sums.astype(jnp.bfloat16)

    out_half = jnp.where(is_control, out_rows[:, :half], swap_grp(out_rows[:, half:]))
    out_full = gather_rows(out_half, me)
    residual = jnp.dot(zero_weight, out_full, preferred_element_type=jnp.float32)
    residual = jnp.concatenate([swap_grp(residual), residual], 1)
    block_rows = jnp.where(is_control, out_rows, (sums + residual).astype(jnp.bfloat16))

    cot_all = lax.all_gather(cot1, "dp")
    out_all = lax.all_gather(out_half, "dp")
    out_all = gather_rows(jnp.swapaxes(out_all, 0, 1), me)
    cot_other, out_other = swap_grp(cot_all), swap_grp(out_all)
    zero_grad = jnp.einsum("dit,jdt->ij", cot_all, out_all, preferred_element_type=jnp.float32)
    zero_other = jnp.einsum("dit,jdt->ij", cot_other, out_other, preferred_element_type=jnp.float32)
    zero_grad = zero_grad + zero_other

    hidden_grad = jnp.dot(w_second, gate_grad, preferred_element_type=jnp.float32)
    pre_grad = (hidden_grad * slope).astype(jnp.bfloat16)
    norm_term = contract_rows(w_first, pre_grad)
    scaled = norm_term * (1.0 + scale[:, None])
    token_sums = jnp.stack([jnp.sum(scaled, 0), jnp.sum(scaled * xhat, 0)])
    total_sums = token_sums
    for mask in range(1, lax.axis_size("fsdp")):
        total_sums = total_sums + swap_fsdp(token_sums, mask)
    norm_grad = scatter_sum(norm_term, rows, me)
    own_xhat = (own_values - mean) * inv
    own_scale = block_of(scale, me, rows)
    total_sums = total_sums / features
    back = inv * (
        norm_grad * (1.0 + own_scale[:, None]) - total_sums[0:1] - own_xhat * total_sums[1:2]
    )
    return (block_rows[None], (up_rows + back)[None], zero_grad)


def solution(mesh):
    placed = (
        P("grp", None, "dp"),
        P("grp", None, None),
        P("grp", "fsdp", None),
        P("grp", "fsdp", None),
        P("fsdp", None),
        P("grp", "fsdp", "dp"),
    )
    return jax.shard_map(
        local,
        mesh=mesh,
        in_specs=placed,
        out_specs=(P("grp", "fsdp", "dp"), P("grp", "fsdp", "dp"), P("fsdp", None)),
        check_vma=False,
    )
```

time: 395 us -> 226 us (0.57)
  waiting for transfers between devices: 303 us -> 22.1 us
  local copies, waits for them, and re-layouts: 19.2 us -> 65.8 us
  blocking collectives: 0 us -> 35.4 us
  starting transfers between devices: 4.59 us -> 32.2 us
  between operations: 13.9 us -> 0.93 us
  matrix products: 41 us -> 51.2 us
    psum x3 -> x0, waiting for transfers between devices: 301 us -> none  [the longest x2 178 us: sum_features(): return lax.psum(product, 'fsdp')]
    dynamic_update_slice x1 -> x16, local copies, waits for them, and re-layouts: 4.54 us -> 46.8 us  [the longest x12 36.1 us: gather_rows(): lax.dynamic_update_slice_in_dim(full, swap_fsdp(value, mask), (me ^ mask)...]
    all_gather x0 -> x2, blocking collectives: none -> 35.4 us  [the longest x1 18.2 us: local(): out_all = lax.all_gather(out_half, 'dp')]
    ppermute x2 -> x32, starting transfers between devices: 4.07 us -> 32.2 us  [the longest x24 30.9 us: swap_fsdp(): return lax.ppermute(value, 'fsdp', [(i, i ^ mask) for i in range(length)])]
    ppermute x2 -> x32, waiting for transfers between devices: 1.65 us -> 22.1 us  [the longest x24 22.1 us: swap_fsdp(): return lax.ppermute(value, 'fsdp', [(i, i ^ mask) for i in range(length)])]
    dot_general x1 -> x3, matrix products: 3.55 us -> 14.8 us  [the longest x1 8.16 us: local(): jnp.einsum('dit,jdt->ij', cot_other, out_other, preferred_element_type=jn...]
    unnamed x16 -> x40, local copies, waits for them, and re-layouts: 13.5 us -> 7.71 us
    convert_element_type x0 -> x3, local copies, waits for them, and re-layouts: none -> 4.72 us  [scatter_sum(): sent = block_of(term, me ^ mask, rows).astype(jnp.bfloat16)]
  transfers between devices with their start and end apart: 5 -> 32, of which waited for: 4 -> 6; matrix products, arithmetic and copies ran while one was open for 7% -> 54% of each run, Pallas kernels for 0% -> 0%
where the time goes in v1:
time: 226 us; the launch traced here: 223 us
  local copies, waits for them, and re-layouts  65.8 us (29%)
  matrix products  51.2 us (23%)
  blocking collectives  35.4 us (16%)
  starting transfers between devices  32.2 us (14%)
  waiting for transfers between devices  22.1 us (10%)
  other arithmetic  15.3 us (7%)
    dynamic_update_slice x12, local copies, waits for them, and re-layouts, gather_rows(): lax.dynamic_update_slice_in_dim(full, swap_fsdp(value, mask), (me ^ mask)...  36.1 us
    ppermute x24, starting transfers between devices, swap_fsdp(): return lax.ppermute(value, 'fsdp', [(i, i ^ mask) for i in range(length)])  30.9 us
    dot_general x3, matrix products, contract_rows(): lax.dot_general(weights, columns, (((0,), (0,)), ((), ())), preferred_ele...  29.5 us
    ppermute x24, waiting for transfers between devices, swap_fsdp(): return lax.ppermute(value, 'fsdp', [(i, i ^ mask) for i in range(length)])  22.1 us
    all_gather x1, blocking collectives, local(): out_all = lax.all_gather(out_half, 'dp')  18.2 us
    all_gather x1, blocking collectives, local(): cot_all = lax.all_gather(cot1, 'dp')  17.2 us
    dynamic_update_slice x4, local copies, waits for them, and re-layouts, gather_rows(): full = lax.dynamic_update_slice_in_dim(full, value, me * rows, 0)  10.6 us
    dot_general x1, matrix products, local(): jnp.einsum('dit,jdt->ij', cot_other, out_other, preferred_element_type=jn...  8.16 us
  transfers between devices with their start and end apart: 32, of which 6 were waited for; matrix products, arithmetic and copies ran while one was open for 54% of the time, Pallas kernels for 0%

profile of v1, /device:TPU:0, one launch (start us, length us, event | category | flops | bytes accessed | tf_op | source)
XLA Modules:
  0.0 223.0 jit_solution(11640406155263410841)
XLA Ops:
  4.0 2.5 %copy.30 = bf16[1,2432,256]{1,2,0:T(8,128)(2,1)} copy(bf16[1,2432,256]{2,1,0:T(8,128)(2,1)} %param.6) | data formatting | bytes 2490368 | tf_op args[0]
  6.5 1.6 convert_reduce_fusion
  8.1 1.8 fusion.27
  9.9 6.9 %fusion.8 = f32[2432,256]{0,1:T(8,128)S(1)} fusion(bf16[1,2432,2432]{2,1,0:T(8,128)(2,1)} %param.8, bf16[1,2432,256]{1,2,0:T(8,128)(2,1)S(1)} %copy-done.2, f32[2432]{0:T(1024)S(1)} %get-tuple-element.32, f32[2432]{0:T(1024)S(1)} %get-tuple-element.33, f32[256]{0:T(256)S(1)} %add_rsqrt_fusion, f32[256]{0:T(256)S(1)} %broadcast_multiply_fusion), kind=kOutput, calls=%fused_computation.9 | convolution fusion | flops 3032023040 | bytes 15586304 | tf_op jit(solution)/shard_map/dot_general | solution.py:97
  16.8 1.5 copy-done.17
  18.2 9.6 %fusion.2 = f32[256,2432]{1,0:T(8,128)} fusion(bf16[1,2432,2432]{2,1,0:T(8,128)(2,1)} %param.9, f32[2432,256]{0,1:T(8,128)S(1)} %fusion.8), kind=kOutput, calls=%fused_computation.2 | convolution fusion | flops 3033890816 | bytes 16809984 | tf_op jit(solution)/shard_map/dot_general | solution.py:11
  27.8 2.9 %fusion.92 = (bf16[608,256]{0,1:T(8,128)(2,1)}, bf16[608,256]{0,1:T(8,128)(2,1)}, bf16[608,256]{0,1:T(8,128)(2,1)}) fusion(f32[256,2432]{1,0:T(8,128)} %fusion.2, s32[]{:T(128)S(6)} %select_n.102, s32[]{:T(128)S(6)} %select_n.104, s32[]{:T(128)S(6)} %select_n.103), kind=kLoop, calls=%fused_computation.93 | loop fusion | bytes 1867788 | tf_op jit(solution)/shard_map/convert_element_type | solution.py:32
  30.7 3.9 %collective-permute-start.2 = (bf16[608,256]{0,1:T(8,128)(2,1)}, bf16[608,256]{0,1:T(8,128)(2,1)}, u32[]{:S(2)}, u32[]{:S(2)}) collective-permute-start(bf16[608,256]{0,1:T(8,128)(2,1)} %get-tuple-element.23), channel_id=1, source_target_pairs={{0,12},{4,8},{8,4},{12,0},{1,13},{5,9},{9,5},{13,1},{2,14},{6,10},... | collective-permute-start | bytes 933896 | tf_op jit(solution)/shard_map/ppermute | solution.py:18
  37.5 2.0 collective-permute-start.17
  39.5 1.6 collective-permute-start.18
  41.2 1.7 fusion.128
  43.8 3.1 %dynamic_update_slice.56 = bf16[2432,128]{0,1:T(8,128)(2,1)} dynamic-update-slice(bf16[2432,128]{0,1:T(8,128)(2,1)} %broadcast.71.clone.1, bf16[608,128]{0,1:T(8,128)(2,1)S(1)} %bitcast_select_fusion.1, s32[]{:T(128)S(6)} %select_n.101, s32[]{:T(128)} %constant.23.clone.1) | dynamic-update-slice | bytes 311300 | tf_op jit(solution)/shard_map/dynamic_update_slice | solution.py:41
  47.0 1.4 fusion.103
  48.4 17.2 %all-gather = bf16[2432,128]{1,0:T(8,128)(2,1)} all-gather(bf16[608,128]{1,0:T(8,128)(2,1)S(1)} %copy.36), channel_id=2, replica_groups=mesh['grp'=2,'fsdp'=4,'dp'=4] {'dp'}, dimensions={0}, use_global_device_ids=true | all-gather | bytes 778240 | tf_op jit(solution)/shard_map/all_gather | solution.py:111
  65.9 2.1 collective-permute-start.10
  69.2 2.8 %fusion.121 = (bf16[608,256]{0,1:T(8,128)(2,1)S(1)}, f32[608,256]{0,1:T(8,128)}) fusion(bf16[608,256]{0,1:T(8,128)(2,1)} %collective-permute-done.2, bf16[608,256]{0,1:T(8,128)(2,1)} %collective-permute-done.1, bf16[608,256]{0,1:T(8,128)(2,1)} %collective-permute-done, f32[256,2432]{1,0:T(8,128)} %fusion.2, s32[]{:T(128)S(6)} %select_n.101, ...), kind=kLoop, calls=%fused_computation.144 | loop fusion | flops 1556480 | bytes 2804100 | tf_op jit(solution)/shard_map/convert_element_type | solution.py:103
  74.8 2.1 multiply_convert_fusion.3
  78.7 3.2 %dynamic_update_slice.52 = bf16[2432,128]{0,1:T(8,128)(2,1)} dynamic-update-slice(bf16[2432,128]{0,1:T(8,128)(2,1)} %broadcast.71.clone.2, bf16[608,128]{0,1:T(8,128)(2,1)} %get-tuple-element.15, s32[]{:T(128)S(6)} %select_n.101, s32[]{:T(128)} %constant.23.clone.1) | dynamic-update-slice | bytes 311300 | tf_op jit(solution)/shard_map/dynamic_update_slice | solution.py:41
  83.2 3.5 %dynamic_update_slice.57 = bf16[2432,128]{0,1:T(8,128)(2,1)} dynamic-update-slice(bf16[2432,128]{0,1:T(8,128)(2,1)} %dynamic_update_slice.56, bf16[608,128]{0,1:T(8,128)(2,1)} %collective-permute-done.17, s32[]{:T(128)S(6)} %select_n.102, s32[]{:T(128)} %constant.23.clone.1) | dynamic-update-slice | bytes 311300 | tf_op jit(solution)/shard_map/dynamic_update_slice | solution.py:43
  86.7 1.6 collective-permute-start.16
  88.3 3.5 %dynamic_update_slice.58 = bf16[2432,128]{0,1:T(8,128)(2,1)} dynamic-update-slice(bf16[2432,128]{0,1:T(8,128)(2,1)} %dynamic_update_slice.57, bf16[608,128]{0,1:T(8,128)(2,1)} %collective-permute-done.18, s32[]{:T(128)S(6)} %select_n.103, s32[]{:T(128)} %constant.23.clone.1) | dynamic-update-slice | bytes 311300 | tf_op jit(solution)/shard_map/dynamic_update_slice | solution.py:43
  91.8 3.0 %dynamic_update_slice.59 = bf16[2432,128]{0,1:T(8,128)(2,1)} dynamic-update-slice(bf16[2432,128]{0,1:T(8,128)(2,1)} %dynamic_update_slice.58, bf16[608,128]{0,1:T(8,128)(2,1)} %collective-permute-done.19, s32[]{:T(128)S(6)} %select_n.104, s32[]{:T(128)} %constant.23.clone.1) | dynamic-update-slice | bytes 311300 | tf_op jit(solution)/shard_map/dynamic_update_slice | solution.py:43
  96.7 3.1 %dynamic_update_slice.48 = bf16[2432,128]{0,1:T(8,128)(2,1)} dynamic-update-slice(bf16[2432,128]{0,1:T(8,128)(2,1)} %broadcast.71.clone, bf16[608,128]{0,1:T(8,128)(2,1)S(1)} %slice_select_fusion, s32[]{:T(128)S(6)} %select_n.101, s32[]{:T(128)} %constant.23.clone.1) | dynamic-update-slice | bytes 311300 | tf_op jit(solution)/shard_map/dynamic_update_slice | solution.py:41
  99.8 2.3 %collective-permute-start.5 = (bf16[608,128]{0,1:T(8,128)(2,1)S(1)}, bf16[608,128]{0,1:T(8,128)(2,1)}, u32[]{:S(2)}, u32[]{:S(2)}) collective-permute-start(bf16[608,128]{0,1:T(8,128)(2,1)S(1)} %slice_select_fusion), channel_id=1, source_target_pairs={{0,8},{4,12},{8,0},{12,4},{1,9},{5,13},{9,1},{13,5},{2,10},{6,14},... | collective-permute-start | bytes 466952 | tf_op jit(solution)/shard_map/ppermute | solution.py:18
  102.1 3.5 %dynamic_update_slice.53 = bf16[2432,128]{0,1:T(8,128)(2,1)} dynamic-update-slice(bf16[2432,128]{0,1:T(8,128)(2,1)} %dynamic_update_slice.52, bf16[608,128]{0,1:T(8,128)(2,1)} %collective-permute-done.14, s32[]{:T(128)S(6)} %select_n.102, s32[]{:T(128)} %constant.23.clone.1) | dynamic-update-slice | bytes 311300 | tf_op jit(solution)/shard_map/dynamic_update_slice | solution.py:43
  107.0 3.5 %dynamic_update_slice.54 = bf16[2432,128]{0,1:T(8,128)(2,1)} dynamic-update-slice(bf16[2432,128]{0,1:T(8,128)(2,1)} %dynamic_update_slice.53, bf16[608,128]{0,1:T(8,128)(2,1)} %collective-permute-done.15, s32[]{:T(128)S(6)} %select_n.103, s32[]{:T(128)} %constant.23.clone.1) | dynamic-update-slice | bytes 311300 | tf_op jit(solution)/shard_map/dynamic_update_slice | solution.py:43
  110.5 18.2 %all-gather.1 = bf16[2432,128]{1,0:T(8,128)(2,1)} all-gather(bf16[608,128]{1,0:T(8,128)(2,1)} %copy.37), channel_id=3, replica_groups=mesh['grp'=2,'fsdp'=4,'dp'=4] {'dp'}, dimensions={0}, use_global_device_ids=true | all-gather | bytes 778240 | tf_op jit(solution)/shard_map/all_gather | solution.py:112
  128.7 3.0 %dynamic_update_slice.55 = bf16[2432,128]{0,1:T(8,128)(2,1)} dynamic-update-slice(bf16[2432,128]{0,1:T(8,128)(2,1)} %dynamic_update_slice.54, bf16[608,128]{0,1:T(8,128)(2,1)} %collective-permute-done.16, s32[]{:T(128)S(6)} %select_n.104, s32[]{:T(128)} %constant.23.clone.1) | dynamic-update-slice | bytes 311300 | tf_op jit(solution)/shard_map/dynamic_update_slice | solution.py:43
  131.7 2.8 %collective-permute-start.28 = (bf16[608,4,128]{2,0,1:T(8,128)(2,1)}, bf16[608,4,128]{2,0,1:T(8,128)(2,1)}, u32[]{:S(2)}, u32[]{:S(2)}) collective-permute-start(bf16[608,4,128]{2,0,1:T(8,128)(2,1)} %bitcast.33), channel_id=1, source_target_pairs={{0,8},{4,12},{8,0},{12,4},{1,9},{5,13},{9,1},{13,5},{2,10},{6,14},... | collective-permute-start | bytes 1867784 | tf_op jit(solution)/shard_map/ppermute | solution.py:18
  134.4 3.5 %dynamic_update_slice.49 = bf16[2432,128]{0,1:T(8,128)(2,1)} dynamic-update-slice(bf16[2432,128]{0,1:T(8,128)(2,1)} %dynamic_update_slice.48, bf16[608,128]{0,1:T(8,128)(2,1)} %collective-permute-done.4, s32[]{:T(128)S(6)} %select_n.102, s32[]{:T(128)} %constant.23.clone.1) | dynamic-update-slice | bytes 311300 | tf_op jit(solution)/shard_map/dynamic_update_slice | solution.py:43
  139.2 3.5 %dynamic_update_slice.50 = bf16[2432,128]{0,1:T(8,128)(2,1)} dynamic-update-slice(bf16[2432,128]{0,1:T(8,128)(2,1)} %dynamic_update_slice.49, bf16[608,128]{0,1:T(8,128)(2,1)} %collective-permute-done.5, s32[]{:T(128)S(6)} %select_n.103, s32[]{:T(128)} %constant.23.clone.1) | dynamic-update-slice | bytes 311300 | tf_op jit(solution)/shard_map/dynamic_update_slice | solution.py:43
  142.8 2.9 %dynamic_update_slice.51 = bf16[2432,128]{0,1:T(8,128)(2,1)} dynamic-update-slice(bf16[2432,128]{0,1:T(8,128)(2,1)} %dynamic_update_slice.50, bf16[608,128]{0,1:T(8,128)(2,1)} %collective-permute-done.6, s32[]{:T(128)S(6)} %select_n.104, s32[]{:T(128)} %constant.23.clone.1) | dynamic-update-slice | bytes 311300 | tf_op jit(solution)/shard_map/dynamic_update_slice | solution.py:43
  145.7 2.2 %convolution_bitcast_fusion = f32[608,128]{0,1:T(8,128)S(1)} fusion(bf16[2432,128]{0,1:T(8,128)(2,1)} %dynamic_update_slice.51, bf16[608,2432]{1,0:T(8,128)(2,1)S(1)} %copy-done), kind=kOutput, calls=%fused_computation.65 | convolution fusion | flops 378535936 | bytes 3891200 | tf_op jit(solution)/shard_map/dot_general | solution.py:107
  152.9 2.1 constant_dynamic-update-slice_fusion.1
  155.0 5.6 %collective-permute-done.28 = bf16[608,4,128]{2,0,1:T(8,128)(2,1)} collective-permute-done((bf16[608,4,128]{2,0,1:T(8,128)(2,1)}, bf16[608,4,128]{2,0,1:T(8,128)(2,1)}, u32[]{:S(2)}, u32[]{:S(2)}) %collective-permute-start.28) | collective-permute-done | bytes 622624 | tf_op jit(solution)/shard_map/ppermute | solution.py:18
  160.6 2.0 constant_dynamic-update-slice_fusion
  162.6 2.1 constant_dynamic-update-slice_fusion.3
  164.7 18.2 %fusion.29 = (f32[256]{0:T(256)S(1)}, f32[256,2432]{1,0:T(8,128)}) fusion(bf16[1,2432,256]{1,2,0:T(8,128)(2,1)S(1)} %copy-done.3, f32[256]{0:T(256)S(1)} %add_rsqrt_fusion, f32[2432]{0:T(1024)S(1)} %get-tuple-element.33, f32[256]{0:T(256)S(1)} %broadcast_multiply_fusion, bf16[1,2432,2432]{2,1,0:T(8,128)(2,1)} %param.8, bf16[1,2432,2432]{2,1,0:T(8,128)(2,1)} %param.9, ...), kind=kOutput, calls=%fused_computation.27 | convolution fusion | flops 6078988288 | bytes 31774720 | tf_op jit(solution)/shard_map/dot_general | solution.py:11
  183.0 2.1 multiply_reduce_fusion
  185.1 1.4 collective-permute-start.26
  186.5 1.7 collective-permute-start.25
  188.7 4.4 %fusion.129 = f32[608,2432,1]{1,0,2:T(8,128)} fusion(bf16[4,608,128]{2,1,0:T(8,128)(2,1)S(1)} %bitcast.146, bf16[2432,4,128]{2,0,1:T(8,128)(2,1)S(1)} %copy-done.5), kind=kOutput, calls=%fused_computation.148 | convolution fusion | flops 1514143744 | bytes 9027584 | tf_op jit(solution)/shard_map/dit,jdt->ij/dot_general | solution.py:115
  193.6 1.4 collective-permute-start.23
  195.0 1.7 collective-permute-start.22
  197.2 7.9 %collective-permute-done.23 = bf16[608,256]{0,1:T(8,128)(2,1)S(1)} collective-permute-done((bf16[608,256]{0,1:T(8,128)(2,1)S(1)}, bf16[608,256]{0,1:T(8,128)(2,1)S(1)}, u32[]{:S(2)}, u32[]{:S(2)}) %collective-permute-start.23) | collective-permute-done | bytes 311328 | tf_op jit(solution)/shard_map/ppermute | solution.py:18
  205.1 6.5 %collective-permute-done.22 = bf16[608,256]{0,1:T(8,128)(2,1)S(1)} collective-permute-done((bf16[608,256]{0,1:T(8,128)(2,1)S(1)}, bf16[608,256]{0,1:T(8,128)(2,1)S(1)}, u32[]{:S(2)}, u32[]{:S(2)}) %collective-permute-start.22) | collective-permute-done | bytes 311328 | tf_op jit(solution)/shard_map/ppermute | solution.py:18
  212.0 1.8 fusion.83
  214.8 8.2 %bitcast_add_fusion = f32[608,2432]{1,0:T(8,128)} fusion(f32[608,2432,1]{1,0,2:T(8,128)} %fusion.129, bf16[4,608,128]{2,1,0:T(8,128)(2,1)} %collective-permute-done.30, bf16[2432,4,128]{2,0,1:T(8,128)(2,1)} %collective-permute-done.31), kind=kOutput, calls=%fused_computation.8 | convolution fusion | flops 1515622400 | bytes 14942208 | tf_op jit(solution)/shard_map/dit,jdt->ij/dot_general | solution.py:116
  (113 shorter events, 27.0 us)
Async XLA Ops:
  0.6 40.6 %copy-start = (bf16[608,2432]{1,0:T(8,128)(2,1)S(1)}, bf16[608,2432]{1,0:T(8,128)(2,1)}, u32[]{:S(2)}) copy-start(bf16[608,2432]{1,0:T(8,128)(2,1)} %param.10) | copy-start | bytes 8871940
  1.6 34.9 %collective-permute-start.13 = (f32[2432]{0:T(1024)S(1)}, f32[2432]{0:T(1024)S(1)}, u32[]{:S(2)}, u32[]{:S(2)}) collective-permute-start(f32[2432]{0:T(1024)S(1)} %get-tuple-element.34), channel_id=1, source_target_pairs={{0,16},{16,0},{1,17},{17,1},{2,18},{18,2},{3,19},{19,3},{4,20},{20... | collective-permute-start | bytes 29192 | tf_op jit(solution)/shard_map/ppermute | solution.py:22
  4.0 32.6 %collective-permute-start.8 = (bf16[608,128]{0,1:T(8,128)(2,1)}, bf16[608,128]{0,1:T(8,128)(2,1)}, u32[]{:S(2)}, u32[]{:S(2)}) collective-permute-start(bf16[608,128]{0,1:T(8,128)(2,1)} %bitcast.148), channel_id=1, source_target_pairs={{0,16},{16,0},{1,17},{17,1},{2,18},{18,2},{3,19},{19,3},{4,20},{20... | collective-permute-start | bytes 466952 | tf_op jit(solution)/shard_map/ppermute | solution.py:22
  6.5 3.4 %copy-start.2 = (bf16[1,2432,256]{1,2,0:T(8,128)(2,1)S(1)}, bf16[1,2432,256]{1,2,0:T(8,128)(2,1)}, u32[]{:S(2)}) copy-start(bf16[1,2432,256]{1,2,0:T(8,128)(2,1)} %copy.30) | copy-start | bytes 3735556
  18.2 17.0 %copy-start.16 = (bf16[1,608,256]{2,1,0:T(8,128)(2,1)S(1)}, bf16[1,608,256]{2,1,0:T(8,128)(2,1)}, u32[]{:S(2)}) copy-start(bf16[1,608,256]{2,1,0:T(8,128)(2,1)} %param.11) | copy-start | bytes 933892
  30.7 35.0 %collective-permute-start.2 = (bf16[608,256]{0,1:T(8,128)(2,1)}, bf16[608,256]{0,1:T(8,128)(2,1)}, u32[]{:S(2)}, u32[]{:S(2)}) collective-permute-start(bf16[608,256]{0,1:T(8,128)(2,1)} %get-tuple-element.23), channel_id=1, source_target_pairs={{0,12},{4,8},{8,4},{12,0},{1,13},{5,9},{9,5},{13,1},{2,14},{6,10},... | collective-permute-start | bytes 933896 | tf_op jit(solution)/shard_map/ppermute | solution.py:18
  34.6 31.3 %collective-permute-start.1 = (bf16[608,256]{0,1:T(8,128)(2,1)}, bf16[608,256]{0,1:T(8,128)(2,1)}, u32[]{:S(2)}, u32[]{:S(2)}) collective-permute-start(bf16[608,256]{0,1:T(8,128)(2,1)} %get-tuple-element.24), channel_id=1, source_target_pairs={{0,8},{4,12},{8,0},{12,4},{1,9},{5,13},{9,1},{13,5},{2,10},{6,14},... | collective-permute-start | bytes 933896 | tf_op jit(solution)/shard_map/ppermute | solution.py:18
  35.1 32.9 %collective-permute-start = (bf16[608,256]{0,1:T(8,128)(2,1)}, bf16[608,256]{0,1:T(8,128)(2,1)}, u32[]{:S(2)}, u32[]{:S(2)}) collective-permute-start(bf16[608,256]{0,1:T(8,128)(2,1)} %get-tuple-element.22), channel_id=1, source_target_pairs={{0,4},{4,0},{8,12},{12,8},{1,5},{5,1},{9,13},{13,9},{2,6},{6,2},{1... | collective-permute-start | bytes 933896 | tf_op jit(solution)/shard_map/ppermute | solution.py:18
  36.3 6.7 %copy-start.12 = (bf16[1,608,128]{1,2,0:T(8,128)(2,1)}, bf16[1,608,128]{1,2,0:T(8,128)(2,1)S(1)}, u32[]{:S(2)}) copy-start(bf16[1,608,128]{1,2,0:T(8,128)(2,1)S(1)} %copy.34) | copy-start | bytes 466948
  37.5 44.3 %collective-permute-start.17 = (bf16[608,128]{0,1:T(8,128)(2,1)S(1)}, bf16[608,128]{0,1:T(8,128)(2,1)}, u32[]{:S(2)}, u32[]{:S(2)}) collective-permute-start(bf16[608,128]{0,1:T(8,128)(2,1)S(1)} %bitcast_select_fusion.1), channel_id=1, source_target_pairs={{0,4},{4,0},{8,12},{12,8},{1,5},{5,1},{9,13},{13,9},{2,6},{6,2},{1... | collective-permute-start | bytes 466952 | tf_op jit(solution)/shard_map/ppermute | solution.py:18
  39.5 47.2 %collective-permute-start.18 = (bf16[608,128]{0,1:T(8,128)(2,1)S(1)}, bf16[608,128]{0,1:T(8,128)(2,1)}, u32[]{:S(2)}, u32[]{:S(2)}) collective-permute-start(bf16[608,128]{0,1:T(8,128)(2,1)S(1)} %bitcast_select_fusion.1), channel_id=1, source_target_pairs={{0,8},{4,12},{8,0},{12,4},{1,9},{5,13},{9,1},{13,5},{2,10},{6,14},... | collective-permute-start | bytes 466952 | tf_op jit(solution)/shard_map/ppermute | solution.py:18
  47.0 27.8 %copy-start.13 = (bf16[1,608,128]{1,2,0:T(8,128)(2,1)S(1)}, bf16[1,608,128]{1,2,0:T(8,128)(2,1)}, u32[]{:S(2)}) copy-start(bf16[1,608,128]{1,2,0:T(8,128)(2,1)} %copy-done.12) | copy-start | bytes 466948
  65.7 7.6 %collective-permute-start.11 = (bf16[608,128]{0,1:T(8,128)(2,1)S(1)}, bf16[608,128]{0,1:T(8,128)(2,1)S(1)}, u32[]{:S(2)}, u32[]{:S(2)}) collective-permute-start(bf16[608,128]{0,1:T(8,128)(2,1)S(1)} %get-tuple-element.26), channel_id=1, source_target_pairs={{0,12},{4,8},{8,4},{12,0},{1,13},{5,9},{9,5},{13,1},{2,14},{6,10},... | collective-permute-start | bytes 466952 | tf_op jit(solution)/shard_map/ppermute | solution.py:18
  65.9 8.9 %collective-permute-start.10 = (bf16[608,128]{0,1:T(8,128)(2,1)S(1)}, bf16[608,128]{0,1:T(8,128)(2,1)S(1)}, u32[]{:S(2)}, u32[]{:S(2)}) collective-permute-start(bf16[608,128]{0,1:T(8,128)(2,1)S(1)} %get-tuple-element.27), channel_id=1, source_target_pairs={{0,8},{4,12},{8,0},{12,4},{1,9},{5,13},{9,1},{13,5},{2,10},{6,14},... | collective-permute-start | bytes 466952 | tf_op jit(solution)/shard_map/ppermute | solution.py:18
  68.0 6.8 %collective-permute-start.9 = (bf16[608,128]{0,1:T(8,128)(2,1)S(1)}, bf16[608,128]{0,1:T(8,128)(2,1)S(1)}, u32[]{:S(2)}, u32[]{:S(2)}) collective-permute-start(bf16[608,128]{0,1:T(8,128)(2,1)S(1)} %get-tuple-element.25), channel_id=1, source_target_pairs={{0,4},{4,0},{8,12},{12,8},{1,5},{5,1},{9,13},{13,9},{2,6},{6,2},{1... | collective-permute-start | bytes 466952 | tf_op jit(solution)/shard_map/ppermute | solution.py:18
  73.2 18.6 %collective-permute-start.19 = (bf16[608,128]{0,1:T(8,128)(2,1)S(1)}, bf16[608,128]{0,1:T(8,128)(2,1)}, u32[]{:S(2)}, u32[]{:S(2)}) collective-permute-start(bf16[608,128]{0,1:T(8,128)(2,1)S(1)} %bitcast_select_fusion.1), channel_id=1, source_target_pairs={{0,12},{4,8},{8,4},{12,0},{1,13},{5,9},{9,5},{13,1},{2,14},{6,10},... | collective-permute-start | bytes 466952 | tf_op jit(solution)/shard_map/ppermute | solution.py:18
  74.8 20.0 %collective-permute-start.3 = (bf16[608,128]{0,1:T(8,128)(2,1)}, bf16[608,128]{0,1:T(8,128)(2,1)}, u32[]{:S(2)}, u32[]{:S(2)}) collective-permute-start(bf16[608,128]{0,1:T(8,128)(2,1)} %slice.29), channel_id=1, source_target_pairs={{0,16},{16,0},{1,17},{17,1},{2,18},{18,2},{3,19},{19,3},{4,20},{20... | collective-permute-start | bytes 466952 | tf_op jit(solution)/shard_map/ppermute | solution.py:22
  76.9 23.0 %collective-permute-start.14 = (bf16[608,128]{0,1:T(8,128)(2,1)}, bf16[608,128]{0,1:T(8,128)(2,1)}, u32[]{:S(2)}, u32[]{:S(2)}) collective-permute-start(bf16[608,128]{0,1:T(8,128)(2,1)} %get-tuple-element.15), channel_id=1, source_target_pairs={{0,4},{4,0},{8,12},{12,8},{1,5},{5,1},{9,13},{13,9},{2,6},{6,2},{1... | collective-permute-start | bytes 466952 | tf_op jit(solution)/shard_map/ppermute | solution.py:18
  81.9 23.8 %collective-permute-start.15 = (bf16[608,128]{0,1:T(8,128)(2,1)}, bf16[608,128]{0,1:T(8,128)(2,1)}, u32[]{:S(2)}, u32[]{:S(2)}) collective-permute-start(bf16[608,128]{0,1:T(8,128)(2,1)} %get-tuple-element.15), channel_id=1, source_target_pairs={{0,8},{4,12},{8,0},{12,4},{1,9},{5,13},{9,1},{13,5},{2,10},{6,14},... | collective-permute-start | bytes 466952 | tf_op jit(solution)/shard_map/ppermute | solution.py:18
  86.7 42.0 %collective-permute-start.16 = (bf16[608,128]{0,1:T(8,128)(2,1)}, bf16[608,128]{0,1:T(8,128)(2,1)}, u32[]{:S(2)}, u32[]{:S(2)}) collective-permute-start(bf16[608,128]{0,1:T(8,128)(2,1)} %get-tuple-element.15), channel_id=1, source_target_pairs={{0,12},{4,8},{8,4},{12,0},{1,13},{5,9},{9,5},{13,1},{2,14},{6,10},... | collective-permute-start | bytes 466952 | tf_op jit(solution)/shard_map/ppermute | solution.py:18
  91.8 101.7 %collective-permute-start.12 = (f32[608,128]{0,1:T(8,128)}, f32[608,128]{0,1:T(8,128)}, u32[]{:S(2)}, u32[]{:S(2)}) collective-permute-start(f32[608,128]{0,1:T(8,128)} %get-tuple-element.16), channel_id=1, source_target_pairs={{0,16},{16,0},{1,17},{17,1},{2,18},{18,2},{3,19},{19,3},{4,20},{20... | collective-permute-start | bytes 933896 | tf_op jit(solution)/shard_map/ppermute | solution.py:22
  94.8 36.8 %collective-permute-start.4 = (bf16[608,128]{0,1:T(8,128)(2,1)S(1)}, bf16[608,128]{0,1:T(8,128)(2,1)}, u32[]{:S(2)}, u32[]{:S(2)}) collective-permute-start(bf16[608,128]{0,1:T(8,128)(2,1)S(1)} %slice_select_fusion), channel_id=1, source_target_pairs={{0,4},{4,0},{8,12},{12,8},{1,5},{5,1},{9,13},{13,9},{2,6},{6,2},{1... | collective-permute-start | bytes 466952 | tf_op jit(solution)/shard_map/ppermute | solution.py:18
  99.8 38.2 %collective-permute-start.5 = (bf16[608,128]{0,1:T(8,128)(2,1)S(1)}, bf16[608,128]{0,1:T(8,128)(2,1)}, u32[]{:S(2)}, u32[]{:S(2)}) collective-permute-start(bf16[608,128]{0,1:T(8,128)(2,1)S(1)} %slice_select_fusion), channel_id=1, source_target_pairs={{0,8},{4,12},{8,0},{12,4},{1,9},{5,13},{9,1},{13,5},{2,10},{6,14},... | collective-permute-start | bytes 466952 | tf_op jit(solution)/shard_map/ppermute | solution.py:18
  105.7 37.1 %collective-permute-start.6 = (bf16[608,128]{0,1:T(8,128)(2,1)S(1)}, bf16[608,128]{0,1:T(8,128)(2,1)}, u32[]{:S(2)}, u32[]{:S(2)}) collective-permute-start(bf16[608,128]{0,1:T(8,128)(2,1)S(1)} %slice_select_fusion), channel_id=1, source_target_pairs={{0,12},{4,8},{8,4},{12,0},{1,13},{5,9},{9,5},{13,1},{2,14},{6,10},... | collective-permute-start | bytes 466952 | tf_op jit(solution)/shard_map/ppermute | solution.py:18
  128.7 24.2 %collective-permute-start.27 = (bf16[608,4,128]{2,0,1:T(8,128)(2,1)}, bf16[608,4,128]{2,0,1:T(8,128)(2,1)}, u32[]{:S(2)}, u32[]{:S(2)}) collective-permute-start(bf16[608,4,128]{2,0,1:T(8,128)(2,1)} %bitcast.33), channel_id=1, source_target_pairs={{0,4},{4,0},{8,12},{12,8},{1,5},{5,1},{9,13},{13,9},{2,6},{6,2},{1... | collective-permute-start | bytes 1867784 | tf_op jit(solution)/shard_map/ppermute | solution.py:18
  131.7 28.9 %collective-permute-start.28 = (bf16[608,4,128]{2,0,1:T(8,128)(2,1)}, bf16[608,4,128]{2,0,1:T(8,128)(2,1)}, u32[]{:S(2)}, u32[]{:S(2)}) collective-permute-start(bf16[608,4,128]{2,0,1:T(8,128)(2,1)} %bitcast.33), channel_id=1, source_target_pairs={{0,8},{4,12},{8,0},{12,4},{1,9},{5,13},{9,1},{13,5},{2,10},{6,14},... | collective-permute-start | bytes 1867784 | tf_op jit(solution)/shard_map/ppermute | solution.py:18
  138.0 24.7 %collective-permute-start.29 = (bf16[608,4,128]{2,0,1:T(8,128)(2,1)}, bf16[608,4,128]{2,0,1:T(8,128)(2,1)}, u32[]{:S(2)}, u32[]{:S(2)}) collective-permute-start(bf16[608,4,128]{2,0,1:T(8,128)(2,1)} %bitcast.33), channel_id=1, source_target_pairs={{0,12},{4,8},{8,4},{12,0},{1,13},{5,9},{9,5},{13,1},{2,14},{6,10},... | collective-permute-start | bytes 1867784 | tf_op jit(solution)/shard_map/ppermute | solution.py:18
  145.7 2.4 %copy-start.9 = (bf16[2432,128]{0,1:T(8,128)(2,1)S(1)}, bf16[2432,128]{0,1:T(8,128)(2,1)}, u32[]{:S(2)}) copy-start(bf16[2432,128]{0,1:T(8,128)(2,1)} %dynamic_update_slice.59) | copy-start | bytes 1867780
  145.7 2.4 %copy-start.11 = (bf16[2432,128]{0,1:T(8,128)(2,1)S(1)}, bf16[2432,128]{0,1:T(8,128)(2,1)}, u32[]{:S(2)}) copy-start(bf16[2432,128]{0,1:T(8,128)(2,1)} %dynamic_update_slice.55) | copy-start | bytes 1867780
  148.0 3.9 %copy-start.8 = (f32[608,256]{0,1:T(8,128)S(1)}, f32[608,256]{0,1:T(8,128)}, u32[]{:S(2)}) copy-start(f32[608,256]{0,1:T(8,128)} %get-tuple-element.18) | copy-start | bytes 1867780
  148.0 2.5 %collective-permute-start.7 = (f32[608,128]{0,1:T(8,128)S(1)}, f32[608,128]{0,1:T(8,128)S(1)}, u32[]{:S(2)}, u32[]{:S(2)}) collective-permute-start(f32[608,128]{0,1:T(8,128)S(1)} %convolution_bitcast_fusion), channel_id=1, source_target_pairs={{0,16},{16,0},{1,17},{17,1},{2,18},{18,2},{3,19},{19,3},{4,20},{20... | collective-permute-start | bytes 933896 | tf_op jit(solution)/shard_map/ppermute | solution.py:22
  150.5 14.2 %collective-permute-start.20 = (bf16[2432,128]{0,1:T(8,128)(2,1)}, bf16[2432,128]{0,1:T(8,128)(2,1)}, u32[]{:S(2)}, u32[]{:S(2)}) collective-permute-start(bf16[2432,128]{0,1:T(8,128)(2,1)} %broadcast_select_fusion), channel_id=1, source_target_pairs={{0,16},{16,0},{1,17},{17,1},{2,18},{18,2},{3,19},{19,3},{4,20},{20... | collective-permute-start | bytes 1867784 | tf_op jit(solution)/shard_map/ppermute | solution.py:22
  152.0 12.7 %copy-start.3 = (bf16[1,2432,256]{1,2,0:T(8,128)(2,1)S(1)}, bf16[1,2432,256]{1,2,0:T(8,128)(2,1)}, u32[]{:S(2)}) copy-start(bf16[1,2432,256]{1,2,0:T(8,128)(2,1)} %copy.30) | copy-start | bytes 3735556
  152.0 12.7 %copy-start.10 = (bf16[2432,128]{0,1:T(8,128)(2,1)S(1)}, bf16[2432,128]{0,1:T(8,128)(2,1)}, u32[]{:S(2)}) copy-start(bf16[2432,128]{0,1:T(8,128)(2,1)} %dynamic_update_slice.59) | copy-start | bytes 1867780
  164.7 50.1 %collective-permute-start.31 = (bf16[2432,4,128]{2,0,1:T(8,128)(2,1)}, bf16[2432,4,128]{2,0,1:T(8,128)(2,1)}, u32[]{:S(2)}, u32[]{:S(2)}) collective-permute-start(bf16[2432,4,128]{2,0,1:T(8,128)(2,1)} %constant_dynamic-update-slice_fusion.3), channel_id=1, source_target_pairs={{0,16},{16,0},{1,17},{17,1},{2,18},{18,2},{3,19},{19,3},{4,20},{20... | collective-permute-start | bytes 7471112 | tf_op jit(solution)/shard_map/ppermute | solution.py:22
  164.7 23.9 %copy-start.7 = (bf16[2432,128]{1,0:T(8,128)(2,1)S(1)}, bf16[2432,128]{1,0:T(8,128)(2,1)}, u32[]{:S(2)}) copy-start(bf16[2432,128]{1,0:T(8,128)(2,1)} %all-gather) | copy-start | bytes 1867780
  183.0 5.7 %copy-start.5 = (bf16[2432,4,128]{2,0,1:T(8,128)(2,1)S(1)}, bf16[2432,4,128]{2,0,1:T(8,128)(2,1)}, u32[]{:S(2)}) copy-start(bf16[2432,4,128]{2,0,1:T(8,128)(2,1)} %constant_dynamic-update-slice_fusion.3) | copy-start | bytes 7471108
  185.1 8.5 %collective-permute-start.26 = (f32[2,256]{1,0:T(2,128)S(1)}, f32[2,256]{1,0:T(2,128)S(1)}, u32[]{:S(2)}, u32[]{:S(2)}) collective-permute-start(f32[2,256]{1,0:T(2,128)S(1)} %pad_maximum_fusion), channel_id=1, source_target_pairs={{0,12},{4,8},{8,4},{12,0},{1,13},{5,9},{9,5},{13,1},{2,14},{6,10},... | collective-permute-start | bytes 6152 | tf_op jit(solution)/shard_map/ppermute | solution.py:18
  186.5 8.5 %collective-permute-start.25 = (f32[2,256]{1,0:T(2,128)S(1)}, f32[2,256]{1,0:T(2,128)S(1)}, u32[]{:S(2)}, u32[]{:S(2)}) collective-permute-start(f32[2,256]{1,0:T(2,128)S(1)} %pad_maximum_fusion), channel_id=1, source_target_pairs={{0,8},{4,12},{8,0},{12,4},{1,9},{5,13},{9,1},{13,5},{2,10},{6,14},... | collective-permute-start | bytes 6152 | tf_op jit(solution)/shard_map/ppermute | solution.py:18
  188.2 8.5 %collective-permute-start.24 = (f32[2,256]{1,0:T(2,128)S(1)}, f32[2,256]{1,0:T(2,128)S(1)}, u32[]{:S(2)}, u32[]{:S(2)}) collective-permute-start(f32[2,256]{1,0:T(2,128)S(1)} %pad_maximum_fusion), channel_id=1, source_target_pairs={{0,4},{4,0},{8,12},{12,8},{1,5},{5,1},{9,13},{13,9},{2,6},{6,2},{1... | collective-permute-start | bytes 6152 | tf_op jit(solution)/shard_map/ppermute | solution.py:18
  188.6 4.4 %copy-start.6 = (f32[256,2432]{1,0:T(8,128)S(1)}, f32[256,2432]{1,0:T(8,128)}, u32[]{:S(2)}) copy-start(f32[256,2432]{1,0:T(8,128)} %get-tuple-element.38) | copy-start | bytes 7471108
  188.7 23.3 %copy-start.14 = (bf16[1,608,256]{1,2,0:T(8,128)(2,1)S(1)}, bf16[1,608,256]{1,2,0:T(8,128)(2,1)}, u32[]{:S(2)}) copy-start(bf16[1,608,256]{1,2,0:T(8,128)(2,1)} %copy.35) | copy-start | bytes 933892
  188.7 23.3 %copy-start.15 = (f32[608,128]{0,1:T(8,128)S(1)}, f32[608,128]{0,1:T(8,128)}, u32[]{:S(2)}) copy-start(f32[608,128]{0,1:T(8,128)} %get-tuple-element.16) | copy-start | bytes 933892
  193.5 21.3 %collective-permute-start.30 = (bf16[4,608,128]{2,1,0:T(8,128)(2,1)S(1)}, bf16[4,608,128]{2,1,0:T(8,128)(2,1)}, u32[]{:S(2)}, u32[]{:S(2)}) collective-permute-start(bf16[4,608,128]{2,1,0:T(8,128)(2,1)S(1)} %bitcast.147), channel_id=1, source_target_pairs={{0,16},{16,0},{1,17},{17,1},{2,18},{18,2},{3,19},{19,3},{4,20},{20... | collective-permute-start | bytes 1867784 | tf_op jit(solution)/shard_map/ppermute | solution.py:22
  193.6 11.5 %collective-permute-start.23 = (bf16[608,256]{0,1:T(8,128)(2,1)S(1)}, bf16[608,256]{0,1:T(8,128)(2,1)S(1)}, u32[]{:S(2)}, u32[]{:S(2)}) collective-permute-start(bf16[608,256]{0,1:T(8,128)(2,1)S(1)} %get-tuple-element.20), channel_id=1, source_target_pairs={{0,12},{4,8},{8,4},{12,0},{1,13},{5,9},{9,5},{13,1},{2,14},{6,10},... | collective-permute-start | bytes 933896 | tf_op jit(solution)/shard_map/ppermute | solution.py:18
  195.0 16.6 %collective-permute-start.22 = (bf16[608,256]{0,1:T(8,128)(2,1)S(1)}, bf16[608,256]{0,1:T(8,128)(2,1)S(1)}, u32[]{:S(2)}, u32[]{:S(2)}) collective-permute-start(bf16[608,256]{0,1:T(8,128)(2,1)S(1)} %get-tuple-element.21), channel_id=1, source_target_pairs={{0,8},{4,12},{8,0},{12,4},{1,9},{5,13},{9,1},{13,5},{2,10},{6,14},... | collective-permute-start | bytes 933896 | tf_op jit(solution)/shard_map/ppermute | solution.py:18
  196.7 15.3 %collective-permute-start.21 = (bf16[608,256]{0,1:T(8,128)(2,1)S(1)}, bf16[608,256]{0,1:T(8,128)(2,1)S(1)}, u32[]{:S(2)}, u32[]{:S(2)}) collective-permute-start(bf16[608,256]{0,1:T(8,128)(2,1)S(1)} %get-tuple-element.19), channel_id=1, source_target_pairs={{0,4},{4,0},{8,12},{12,8},{1,5},{5,1},{9,13},{13,9},{2,6},{6,2},{1... | collective-permute-start | bytes 933896 | tf_op jit(solution)/shard_map/ppermute | solution.py:18
  214.8 8.2 %copy-start.1 = (bf16[608,2432]{1,0:T(8,128)(2,1)S(1)}, bf16[608,2432]{1,0:T(8,128)(2,1)}, u32[]{:S(2)}) copy-start(bf16[608,2432]{1,0:T(8,128)(2,1)} %param.10) | copy-start | bytes 8871940
  (2 other events, 2.9 us)

commit v2 on v1

v2 whole, which is shorter than its diff:
```python
import functools

import jax
import jax.numpy as jnp
from jax import lax
from jax.experimental import pallas as pl
from jax.experimental.pallas import tpu as pltpu
from jax.sharding import PartitionSpec as P

EPSILON = 1e-06
SQRT_2_OVER_PI = 0.7978845608028654
CHUNK = 256
AHEAD = 6
VMEM_LIMIT = 50 * 1024 * 1024


def pieces(extent, size=CHUNK):
    return [(start, min(size, extent - start)) for start in range(0, extent, size)]


def swap_grp(value):
    return lax.ppermute(value, "grp", [(0, 1), (1, 0)])


def trade(blocks, axis):
    return lax.all_to_all(blocks, axis, 0, 0)


def spread(value, axis):
    return trade(jnp.broadcast_to(value[None], (lax.axis_size(axis),) + value.shape), axis)


def block_of(value, index, rows):
    return lax.dynamic_slice_in_dim(value, index * rows, rows, 0)


def split_three(value):
    high = value.astype(jnp.bfloat16)
    rest = value - high.astype(jnp.float32)
    middle = rest.astype(jnp.bfloat16)
    low = (rest - middle.astype(jnp.float32)).astype(jnp.bfloat16)
    return high, middle, low


def gelu_and_slope(v):
    square = v * v
    t = jnp.tanh(SQRT_2_OVER_PI * (v + 0.044715 * (square * v)))
    rise = 0.5 * (1.0 + t)
    slope = rise + 0.5 * v * (1.0 - t * t) * (SQRT_2_OVER_PI * (1.0 + (3 * 0.044715) * square))
    return v * rise, slope


def transposed_product(lhs, rhs):
    return lax.dot_general(lhs, rhs, (((0,), (0,)), ((), ())), preferred_element_type=jnp.float32)


def weight_copies(first, first_buf, second, second_buf, sems):
    copies = []
    for start, size in pieces(first_buf.shape[0]):
        rows = pl.ds(start, size)
        copies.append((first.at[0, rows, :], first_buf.at[rows, :]))
    for start, size in pieces(second_buf.shape[1]):
        columns = pl.ds(start, size)
        copies.append((second.at[0, :, columns], second_buf.at[:, columns]))
    return [pltpu.make_async_copy(a, b, sems.at[k]) for k, (a, b) in enumerate(copies)]


class Stream:
    def __init__(self, copies):
        self.copies, self.next = copies, 0
        for copy in copies[:AHEAD]:
            copy.start()

    def take(self):
        k = self.next
        self.copies[k].wait()
        if k + AHEAD < len(self.copies):
            self.copies[k + AHEAD].start()
        self.next = k + 1


def forward_kernel(acts, mod, w_in, w_out, branch, slope_out, stats, in_buf, out_buf, normed, turned, sems):
    features, tokens = acts.shape[1:]
    stream = Stream(weight_copies(w_in, in_buf, w_out, out_buf, sems))
    parts = pieces(features, 128)
    total = jnp.zeros((1, tokens), jnp.float32)
    for start, size in parts:
        total += jnp.sum(acts[0, pl.ds(start, size), :].astype(jnp.float32), 0, keepdims=True)
    mean = total / features
    total = jnp.zeros((1, tokens), jnp.float32)
    for start, size in parts:
        centred = acts[0, pl.ds(start, size), :].astype(jnp.float32) - mean
        total += jnp.sum(centred * centred, 0, keepdims=True)
    inv = lax.rsqrt(total / features + EPSILON)
    stats[0:1, :] = mean
    stats[1:2, :] = inv
    for start, size in parts:
        rows = pl.ds(start, size)
        xhat = (acts[0, rows, :].astype(jnp.float32) - mean) * inv
        normed[rows, :] = (xhat * (1.0 + mod[rows, 1:2]) + mod[rows, 0:1]).astype(jnp.bfloat16)
    for start, size in pieces(in_buf.shape[0]):
        stream.take()
        rows = pl.ds(start, size)
        pre = jnp.dot(in_buf[rows, :], normed[...], preferred_element_type=jnp.float32)
        hidden, slope = gelu_and_slope(pre)
        slope_out[rows, :] = slope
        turned[:, rows] = hidden.T.astype(jnp.bfloat16)
    for start, size in pieces(features):
        stream.take()
        columns = pl.ds(start, size)
        part = jnp.dot(turned[...], out_buf[:, columns], preferred_element_type=jnp.float32)
        branch[columns, :] = part.T.astype(jnp.bfloat16)


def forward(acts, mod, w_in, w_out):
    features, tokens = acts.shape[1:]
    hidden = w_in.shape[1]
    count = len(pieces(hidden)) + len(pieces(features))
    whole = pl.BlockSpec(memory_space=pltpu.VMEM)
    return pl.pallas_call(
        forward_kernel,
        out_shape=(
            jax.ShapeDtypeStruct((features, tokens), jnp.bfloat16),
            jax.ShapeDtypeStruct((hidden, tokens), jnp.float32),
            jax.ShapeDtypeStruct((2, tokens), jnp.float32),
        ),
        in_specs=[whole, whole, pl.BlockSpec(memory_space=pl.ANY), pl.BlockSpec(memory_space=pl.ANY)],
        out_specs=(whole, whole, whole),
        scratch_shapes=[
            pltpu.VMEM((hidden, features), jnp.bfloat16),
            pltpu.VMEM((hidden, features), jnp.bfloat16),
            pltpu.VMEM((features, tokens), jnp.bfloat16),
            pltpu.VMEM((tokens, hidden), jnp.bfloat16),
            pltpu.SemaphoreType.DMA((count,)),
        ],
        compiler_params=pltpu.CompilerParams(vmem_limit_bytes=VMEM_LIMIT),
        cost_estimate=pl.CostEstimate(
            flops=4 * hidden * features * tokens,
            bytes_accessed=4 * hidden * features + 4 * hidden * tokens + 4 * features * tokens,
            transcendentals=hidden * tokens,
        ),
        name="forward_layers",
    )(acts, mod, w_in, w_out)


def backward_kernel(
    group, rows_each, own, crossed, factor, slope, acts, stats, mod, w_in, w_out,
    sent, in_buf, out_buf, grad, turned, norm, sems,
):
    features, tokens = acts.shape[1:]
    half = tokens // 2
    stream = Stream(weight_copies(w_out, out_buf, w_in, in_buf, sems))
    mine = pl.multiple_of(group[0] * half, half)
    theirs = pl.multiple_of((1 - group[0]) * half, half)
    for start, size in pieces(features, 128):
        rows = pl.ds(start, size)
        grad[rows, pl.ds(mine, half)] = (own[rows, :].astype(jnp.float32) * factor[rows, 0:1]).astype(jnp.bfloat16)
        grad[rows, pl.ds(theirs, half)] = (
            crossed[rows, :].astype(jnp.float32) * factor[rows, 0:1]
        ).astype(jnp.bfloat16)
    for start, size in pieces(out_buf.shape[0]):
        stream.take()
        rows = pl.ds(start, size)
        hidden_grad = jnp.dot(out_buf[rows, :], grad[...], preferred_element_type=jnp.float32)
        turned[:, rows] = (hidden_grad * slope[rows, :]).T.astype(jnp.bfloat16)
    mean, inv = stats[0:1, :], stats[1:2, :]
    plain = jnp.zeros((1, tokens), jnp.float32)
    along = jnp.zeros((1, tokens), jnp.float32)
    for start, size in pieces(features):
        stream.take()
        columns = pl.ds(start, size)
        part = jnp.dot(turned[...], in_buf[:, columns], preferred_element_type=jnp.float32).T
        norm[columns, :] = part
        scaled = part * (1.0 + mod[columns, 1:2])
        xhat = (acts[0, columns, :].astype(jnp.float32) - mean) * inv
        plain += jnp.sum(scaled, 0, keepdims=True)
        along += jnp.sum(scaled * xhat, 0, keepdims=True)
    tail = [part.astype(jnp.float32) for part in split_three(plain) + split_three(along)]
    tail = jnp.concatenate(tail + [jnp.zeros((10, tokens), jnp.float32)], 0).astype(jnp.bfloat16)
    padded = sent.shape[1] - 16
    for block in range(sent.shape[0]):
        rows = norm[pl.ds(block * rows_each, rows_each), :]
        if padded > rows_each:
            rows = jnp.concatenate([rows, jnp.zeros((padded - rows_each, tokens), jnp.float32)], 0)
        sent[block, 0:padded, :] = rows.astype(jnp.bfloat16)
        sent[block, padded:, :] = tail


def backward(group, own, crossed, factor, slope, acts, stats, mod, w_in, w_out, blocks):
    features, tokens = acts.shape[1:]
    hidden = w_in.shape[1]
    count = len(pieces(hidden)) + len(pieces(features))
    rows = features // blocks
    whole = pl.BlockSpec(memory_space=pltpu.VMEM)
    held = pl.BlockSpec(memory_space=pl.ANY)

    def kernel(group, *refs):
        backward_kernel(group, rows, *refs)

    return pl.pallas_call(
        kernel,
        out_shape=jax.ShapeDtypeStruct((blocks, -(-rows // 16) * 16 + 16, tokens), jnp.bfloat16),
        in_specs=[pl.BlockSpec(memory_space=pltpu.SMEM)] + [whole] * 7 + [held] * 2,
        out_specs=whole,
        scratch_shapes=[
            pltpu.VMEM((hidden, features), jnp.bfloat16),
            pltpu.VMEM((hidden, features), jnp.bfloat16),
            pltpu.VMEM((features, tokens), jnp.bfloat16),
            pltpu.VMEM((tokens, hidden), jnp.bfloat16),
            pltpu.VMEM((features, tokens), jnp.float32),
            pltpu.SemaphoreType.DMA((count,)),
        ],
        compiler_params=pltpu.CompilerParams(vmem_limit_bytes=VMEM_LIMIT),
        cost_estimate=pl.CostEstimate(
            flops=4 * hidden * features * tokens,
            bytes_accessed=4 * hidden * features + 4 * hidden * tokens + 6 * features * tokens,
            transcendentals=0,
        ),
        name="backward_layers",
    )(group, own, crossed, factor, slope, acts, stats, mod, w_in, w_out)


def zero_grad_kernel(group, cot, cot_other, out, out_other, grad, lhs, rhs):
    parts, rows, half = cot.shape
    blocks = out.shape[0]
    mine = group[0] * half
    theirs = (1 - group[0]) * half
    for part in range(parts):
        for offset, left, right in ((mine, cot, out), (theirs, cot_other, out_other)):
            lanes = pl.ds(pl.multiple_of(part * 2 * half + offset, half), half)
            lhs[:, lanes] = left[part]
            for block in range(blocks):
                rhs[pl.ds(block * rows, rows), lanes] = right[block, part]
    for start, size in pieces(rhs.shape[0]):
        columns = pl.ds(start, size)
        grad[:, columns] = lax.dot_general(
            lhs[...], rhs[columns, :], (((1,), (1,)), ((), ())), preferred_element_type=jnp.float32
        )


def zero_projection_grad(group, cot, cot_other, out, out_other):
    parts, rows, half = cot.shape
    features = out.shape[0] * rows
    whole = pl.BlockSpec(memory_space=pltpu.VMEM)
    return pl.pallas_call(
        zero_grad_kernel,
        out_shape=jax.ShapeDtypeStruct((rows, features), jnp.float32),
        in_specs=[pl.BlockSpec(memory_space=pltpu.SMEM)] + [whole] * 4,
        out_specs=whole,
        scratch_shapes=[
            pltpu.VMEM((rows, parts * 2 * half), jnp.bfloat16),
            pltpu.VMEM((features, parts * 2 * half), jnp.bfloat16),
        ],
        compiler_params=pltpu.CompilerParams(vmem_limit_bytes=VMEM_LIMIT),
        cost_estimate=pl.CostEstimate(
            flops=4 * parts * half * rows * features,
            bytes_accessed=4 * rows * features + 4 * parts * half * (rows + features),
            transcendentals=0,
        ),
        name="zero_projection_grad",
    )(group, cot, cot_other, out, out_other)


def upstream_kernel(weight, cot, sent):
    blocks, rows, tokens = sent.shape
    full = transposed_product(cot[...], weight[...]).T
    for block in range(blocks):
        sent[block] = full[block * rows : (block + 1) * rows, :].astype(jnp.bfloat16)


def upstream_terms(weight, cot, blocks):
    rows, tokens = cot.shape
    whole = pl.BlockSpec(memory_space=pltpu.VMEM)
    return pl.pallas_call(
        upstream_kernel,
        out_shape=jax.ShapeDtypeStruct((blocks, rows, tokens), jnp.bfloat16),
        in_specs=[whole] * 2,
        out_specs=whole,
        compiler_params=pltpu.CompilerParams(vmem_limit_bytes=VMEM_LIMIT),
        cost_estimate=pl.CostEstimate(
            flops=2 * weight.size * tokens, bytes_accessed=2 * weight.size + 2 * blocks * rows * tokens, transcendentals=0
        ),
        name="upstream_terms",
    )(weight, cot)


def local(acts, modulation, w_in, w_out, zero_weight, cotangent):
    own_cot = cotangent[0]
    features, tokens = acts.shape[1:]
    rows = own_cot.shape[0]
    half = tokens // 2
    blocks = lax.axis_size("fsdp")
    group = lax.axis_index("grp")
    is_control = group == 0
    group_ref = group.astype(jnp.int32)[None]
    me = lax.axis_index("fsdp")
    mod = modulation[0].T
    gate = mod[:, 2:3]

    mine = lax.dynamic_slice_in_dim(own_cot, group * half, half, 1)
    other = lax.dynamic_slice_in_dim(own_cot, (1 - group) * half, half, 1)
    arrived = swap_grp(other)
    cot1 = jnp.where(is_control, arrived, mine)
    cot0 = jnp.where(is_control, mine, arrived)
    own_gate = block_of(gate, me, rows)
    own_gate0 = jnp.where(is_control, own_gate, swap_grp(own_gate))

    up_sent = upstream_terms(zero_weight, cot1, blocks)
    up_got = trade(jnp.concatenate([up_sent, jnp.broadcast_to(cot1[None], up_sent.shape)], 1), "fsdp")
    up_half = jnp.sum(up_got[:, :rows].astype(jnp.float32), 0) + cot0.astype(jnp.float32)
    cot1_full = up_got[:, rows:].reshape(features, half)
    gated = spread((own_gate0 * up_half).astype(jnp.bfloat16), "fsdp").reshape(features, half)
    crossed = swap_grp(jnp.where(is_control, cot1_full, gated))
    kept = jnp.where(is_control, gated, cot1_full)
    factor = jnp.where(is_control, 1.0, gate)
    up_rows = jnp.where(
        is_control,
        jnp.concatenate([up_half, swap_grp(up_half)], 1),
        own_cot.astype(jnp.float32),
    )

    branch_term, slope, stats = forward(acts, mod, w_in, w_out)
    branch = jnp.sum(trade(branch_term.reshape(blocks, rows, tokens), "fsdp").astype(jnp.float32), 0)
    own_values = block_of(acts[0], me, rows).astype(jnp.float32)
    sums = own_values + own_gate * branch
    out_rows = sums.astype(jnp.bfloat16)

    out_half = jnp.where(is_control, out_rows[:, :half], swap_grp(out_rows[:, half:]))
    out_full = spread(out_half, "fsdp").reshape(features, half)
    residual = jnp.dot(zero_weight, out_full, preferred_element_type=jnp.float32)
    residual = jnp.concatenate([swap_grp(residual), residual], 1)
    block_rows = jnp.where(is_control, out_rows, (sums + residual).astype(jnp.bfloat16))

    parts = lax.axis_size("dp")
    all_tokens = spread(jnp.concatenate([cot1, out_half], 0), "dp")
    cot_all = all_tokens[:, :rows]
    out_all = spread(all_tokens[:, rows:], "fsdp")
    zero_grad = zero_projection_grad(group_ref, cot_all, swap_grp(cot_all), out_all, swap_grp(out_all))

    norm_sent = backward(group_ref, kept, crossed, factor, slope, acts, stats, mod, w_in, w_out, blocks)
    norm_got = trade(norm_sent, "fsdp").astype(jnp.float32)
    norm_grad = jnp.sum(norm_got[:, :rows], 0)
    tail = jnp.sum(norm_got[:, -16:], 0)
    plain = (tail[0:1] + tail[1:2] + tail[2:3]) / features
    along = (tail[3:4] + tail[4:5] + tail[5:6]) / features
    mean, inv = stats[0:1], stats[1:2]
    own_scale = block_of(mod[:, 1:2], me, rows)
    back = inv * (norm_grad * (1.0 + own_scale) - plain - (own_values - mean) * inv * along)
    return (block_rows[None], (up_rows + back)[None], zero_grad)


def solution(mesh):
    placed = (
        P("grp", None, "dp"),
        P("grp", None, None),
        P("grp", "fsdp", None),
        P("grp", "fsdp", None),
        P("fsdp", None),
        P("grp", "fsdp", "dp"),
    )
    return jax.shard_map(
        local,
        mesh=mesh,
        in_specs=placed,
        out_specs=(P("grp", "fsdp", "dp"), P("grp", "fsdp", "dp"), P("fsdp", None)),
        check_vma=False,
    )
```

time: 226 us -> 221 us (0.978)
  waiting for transfers between devices: 22.1 us -> 94.9 us
  Pallas kernels: 0 us -> 54.4 us
  matrix products: 51.2 us -> 2.08 us
  local copies, waits for them, and re-layouts: 65.8 us -> 19.5 us
  blocking collectives: 35.4 us -> 0 us
    all_to_all x0 -> x7, waiting for transfers between devices: none -> 92.1 us  [trade(): return lax.all_to_all(blocks, axis, 0, 0)]
    pallas_call x0 -> x4, Pallas kernels: none -> 54.4 us  [the longest x1 22.5 us: backward(): pl.pallas_call(kernel, out_shape=jax.ShapeDtypeStruct((blocks, -(-rows //...]
    dot_general x6 -> x0, matrix products: 49 us -> none  [the longest x3 29.5 us: contract_rows(): lax.dot_general(weights, columns, (((0,), (0,)), ((), ())), preferred_ele...]
    dynamic_update_slice x16 -> x0, local copies, waits for them, and re-layouts: 46.8 us -> none  [the longest x12 36.1 us: gather_rows(): lax.dynamic_update_slice_in_dim(full, swap_fsdp(value, mask), (me ^ mask)...]
    all_gather x2 -> x0, blocking collectives: 35.4 us -> none  [the longest x1 18.2 us: local(): out_all = lax.all_gather(out_half, 'dp')]
    ppermute x24 -> x0, starting transfers between devices: 30.9 us -> none  [swap_fsdp(): return lax.ppermute(value, 'fsdp', [(i, i ^ mask) for i in range(length)])]
    all_to_all x0 -> x7, starting transfers between devices: none -> 29.8 us  [trade(): return lax.all_to_all(blocks, axis, 0, 0)]
    ppermute x24 -> x0, waiting for transfers between devices: 22.1 us -> none  [swap_fsdp(): return lax.ppermute(value, 'fsdp', [(i, i ^ mask) for i in range(length)])]
  transfers between devices with their start and end apart: 32 -> 15, of which waited for: 6 -> 8; matrix products, arithmetic and copies ran while one was open for 54% -> 10% of each run, Pallas kernels for 0% -> 20%
where the time goes in v2:
time: 221 us; the launch traced here: 219 us
  waiting for transfers between devices  94.9 us (43%)
  Pallas kernels  54.4 us (25%)
  starting transfers between devices  31.9 us (14%)
  local copies, waits for them, and re-layouts  19.5 us (9%)
  other arithmetic  15.6 us (7%)
    all_to_all x7, waiting for transfers between devices, trade(): return lax.all_to_all(blocks, axis, 0, 0)  92.1 us
    all_to_all x7, starting transfers between devices, trade(): return lax.all_to_all(blocks, axis, 0, 0)  29.8 us
    pallas_call x1, Pallas kernels, backward(): pl.pallas_call(kernel, out_shape=jax.ShapeDtypeStruct((blocks, -(-rows //...  22.5 us
    pallas_call x1, Pallas kernels, forward(): pl.pallas_call(forward_kernel, out_shape=(jax.ShapeDtypeStruct((features,...  20.9 us
    unnamed x39, local copies, waits for them, and re-layouts  10.3 us
    pallas_call x1, Pallas kernels, zero_projection_grad(): pl.pallas_call(zero_grad_kernel, out_shape=jax.ShapeDtypeStruct((rows, fe...  10.2 us
    broadcast_in_dim x4, local copies, waits for them, and re-layouts, spread(): jnp.broadcast_to(value[None], (lax.axis_size(axis),) + value.shape)  5.95 us
  transfers between devices with their start and end apart: 15, of which 8 were waited for; matrix products, arithmetic and copies ran while one was open for 10% of the time, Pallas kernels for 20%

profile of v2, /device:TPU:0, one launch (start us, length us, event | category | flops | bytes accessed | tf_op | source)
XLA Modules:
  0.0 219.4 jit_solution(11598257761902986472)
XLA Ops:
  0.6 1.0 dynamic-slice_bitcast_fusion
  1.7 0.5 collective-permute-start.2
  2.2 1.2 copy.10
  3.4 20.9 %forward_layers.1 = (bf16[2432,256]{1,0:T(8,128)(2,1)S(1)}, f32[2432,256]{1,0:T(8,128)}, f32[2,256]{1,0:T(2,128)S(1)}) custom-call(bf16[1,2432,256]{2,1,0:T(8,128)(2,1)S(1)} %copy-done.3, f32[2432,3]{1,0:T(8,128)S(1)} %bitcast.52, bf16[1,2432,2432]{2,1,0:T(8,128)(2,1)} %refs_7_.1, bf16[1,2432,2432]{2,1,0:T(8,128)(2,1)} %refs_8_.1), custom_call_target="tpu_custom_call" | custom-call | flops 6056574976 | bytes 28639232 | tf_op jit(solution)/shard_map/forward_layers/pallas_call | solution.py:120
  24.3 1.0 copy-done.8
  25.4 4.7 %all-to-all-start = ((bf16[4,608,256]{2,1,0:T(8,128)(2,1)}), bf16[4,608,256]{2,1,0:T(8,128)(2,1)}, u32[]{:S(2)}, u32[]{:S(2)}) async-start(bf16[4,608,256]{2,1,0:T(8,128)(2,1)} %bitcast.56), calls=%async_computation | async-start | bytes 2490368 | tf_op jit(solution)/shard_map/all_to_all | solution.py:26
  30.1 2.6 %fusion.14 = (f32[2432,1]{1,0:T(8,128)}, f32[2432,1]{1,0:T(8,128)}, f32[2432,1]{1,0:T(8,128)}) fusion(f32[2432,3]{1,0:T(8,128)S(1)} %bitcast.53, pred[]{:T(512)S(6)} %eq.3), kind=kLoop, calls=%fused_computation.43 | loop fusion | flops 2432 | bytes 48641 | tf_op jit(solution)/shard_map/slice | solution.py:347
  32.7 1.0 constant_dynamic-slice_fusion
  34.1 1.4 collective-permute-done.4
  35.4 1.2 select_reduce_fusion
  36.8 1.8 copy-done.1
  38.6 0.8 upstream_terms.1
  39.5 1.1 pad_maximum_fusion
  40.6 6.7 %all-to-all-done = bf16[4,608,256]{2,1,0:T(8,128)(2,1)} async-done(((bf16[4,608,256]{2,1,0:T(8,128)(2,1)}), bf16[4,608,256]{2,1,0:T(8,128)(2,1)}, u32[]{:S(2)}, u32[]{:S(2)}) %all-to-all-start) | async-done | bytes 1245216 | tf_op jit(solution)/shard_map/all_to_all | solution.py:26
  47.3 3.5 %all-to-all-start.2 = ((bf16[4,1216,128]{2,1,0:T(8,128)(2,1)}), bf16[4,1216,128]{2,1,0:T(8,128)(2,1)S(1)}, u32[]{:S(2)}, u32[]{:S(2)}) async-start(bf16[4,1216,128]{2,1,0:T(8,128)(2,1)} %pad_maximum_fusion), calls=%async_computation.2 | async-start | bytes 2490368 | tf_op jit(solution)/shard_map/all_to_all | solution.py:26
  50.9 1.5 convert_reduce_fusion
  52.7 1.4 collective-permute-done
  54.1 0.7 copy-done.15
  54.8 12.2 %all-to-all-done.2 = bf16[4,1216,128]{2,1,0:T(8,128)(2,1)S(1)} async-done(((bf16[4,1216,128]{2,1,0:T(8,128)(2,1)}), bf16[4,1216,128]{2,1,0:T(8,128)(2,1)S(1)}, u32[]{:S(2)}, u32[]{:S(2)}) %all-to-all-start.2) | async-done | bytes 1245216 | tf_op jit(solution)/shard_map/all_to_all | solution.py:26
  67.0 1.2 broadcast_in_dim.21
  68.2 4.9 %all-to-all-start.5 = ((bf16[4,1216,128]{2,1,0:T(8,128)(2,1)}), bf16[4,1216,128]{2,1,0:T(8,128)(2,1)S(1)}, u32[]{:S(2)}, u32[]{:S(2)}) async-start(bf16[4,1216,128]{2,1,0:T(8,128)(2,1)} %broadcast_in_dim.21), calls=%async_computation.5 | async-start | bytes 2490368 | tf_op jit(solution)/shard_map/all_to_all | solution.py:26
  73.1 0.8 multiply_convert_fusion
  74.0 28.2 %all-to-all-done.5 = bf16[4,1216,128]{2,1,0:T(8,128)(2,1)S(1)} async-done(((bf16[4,1216,128]{2,1,0:T(8,128)(2,1)}), bf16[4,1216,128]{2,1,0:T(8,128)(2,1)S(1)}, u32[]{:S(2)}, u32[]{:S(2)}) %all-to-all-start.5) | async-done | bytes 1245216 | tf_op jit(solution)/shard_map/all_to_all | solution.py:26
  102.2 0.9 broadcast_in_dim.19
  103.1 3.5 %all-to-all-start.3 = ((bf16[4,608,128]{2,1,0:T(8,128)(2,1)}), bf16[4,608,128]{2,1,0:T(8,128)(2,1)S(1)}, u32[]{:S(2)}, u32[]{:S(2)}) async-start(bf16[4,608,128]{2,1,0:T(8,128)(2,1)} %broadcast_in_dim.19), calls=%async_computation.3 | async-start | bytes 1245184 | tf_op jit(solution)/shard_map/all_to_all | solution.py:26
  106.6 1.1 fusion.13
  107.7 7.4 %all-to-all-done.3 = bf16[4,608,128]{2,1,0:T(8,128)(2,1)S(1)} async-done(((bf16[4,608,128]{2,1,0:T(8,128)(2,1)}), bf16[4,608,128]{2,1,0:T(8,128)(2,1)S(1)}, u32[]{:S(2)}, u32[]{:S(2)}) %all-to-all-start.3) | async-done | bytes 622624 | tf_op jit(solution)/shard_map/all_to_all | solution.py:26
  115.1 2.9 %broadcast_in_dim.22 = bf16[4,4,608,128]{3,2,1,0:T(8,128)(2,1)} broadcast(bf16[4,608,128]{2,1,0:T(8,128)(2,1)} %get-tuple-element.15), dimensions={1,2,3} | broadcast | bytes 3112960 | tf_op jit(solution)/shard_map/broadcast_in_dim | solution.py:30
  118.0 4.5 %all-to-all-start.6 = ((bf16[4,4,608,128]{3,2,1,0:T(8,128)(2,1)}), bf16[4,4,608,128]{3,2,1,0:T(8,128)(2,1)}, u32[]{:S(2)}, u32[]{:S(2)}) async-start(bf16[4,4,608,128]{3,2,1,0:T(8,128)(2,1)} %broadcast_in_dim.22), calls=%async_computation.6 | async-start | bytes 4980736 | tf_op jit(solution)/shard_map/all_to_all | solution.py:26
  122.6 1.1 broadcast_select_fusion.1
  123.7 26.8 %all-to-all-done.6.out = bf16[4,4,608,128]{3,2,1,0:T(8,128)(2,1)} async-done(((bf16[4,4,608,128]{3,2,1,0:T(8,128)(2,1)}), bf16[4,4,608,128]{3,2,1,0:T(8,128)(2,1)}, u32[]{:S(2)}, u32[]{:S(2)}) %all-to-all-start.6) | async-done | bytes 2490400 | tf_op jit(solution)/shard_map/all_to_all | solution.py:26
  150.5 0.9 broadcast_in_dim.16
  151.5 4.2 %all-to-all-start.1 = ((bf16[4,608,128]{2,1,0:T(8,128)(2,1)}), bf16[4,608,128]{2,1,0:T(8,128)(2,1)}, u32[]{:S(2)}, u32[]{:S(2)}) async-start(bf16[4,608,128]{2,1,0:T(8,128)(2,1)} %broadcast_in_dim.16), calls=%async_computation.1 | async-start | bytes 1245184 | tf_op jit(solution)/shard_map/all_to_all | solution.py:26
  155.6 0.8 copy-done.9
  156.5 1.3 copy-done.4
  157.8 1.3 copy-done.5
  159.0 1.1 copy-done.7
  160.1 1.1 copy-done.10
  161.2 22.5 %backward_layers.1 = bf16[4,624,256]{2,1,0:T(8,128)(2,1)} custom-call(s32[1]{0:T(128)} %bitcast.15.group, bf16[2432,128]{1,0:T(8,128)(2,1)S(1)} %bitcast.55, bf16[2432,128]{1,0:T(8,128)(2,1)S(1)} %copy-done.10, f32[2432,1]{1,0:T(8,128)S(1)} %copy-done.5, f32[2432,256]{1,0:T(8,128)} %get-tuple-element.8.refs_3_, bf16[1,2432,256]{2,1,0:T(8,128)(2,1)S(1)} %copy-done.4, ...), custom_call_target="tpu_custom_call" | custom-call | flops 6056574976 | bytes 29884416 | tf_op jit(solution)/shard_map/backward_layers/pallas_call | solution.py:200
  183.7 4.5 %all-to-all-start.4 = ((bf16[4,624,256]{2,1,0:T(8,128)(2,1)}), bf16[4,624,256]{2,1,0:T(8,128)(2,1)}, u32[]{:S(2)}, u32[]{:S(2)}) async-start(bf16[4,624,256]{2,1,0:T(8,128)(2,1)} %backward_layers.1), calls=%async_computation.4 | async-start | bytes 2555904 | tf_op jit(solution)/shard_map/all_to_all | solution.py:26
  188.3 2.1 fusion.16
  190.4 0.6 collective-permute-start.1
  190.9 1.1 add_reduce_fusion
  192.2 1.9 fusion.10
  194.5 10.8 %all-to-all-done.4 = bf16[4,624,256]{2,1,0:T(8,128)(2,1)} async-done(((bf16[4,624,256]{2,1,0:T(8,128)(2,1)}), bf16[4,624,256]{2,1,0:T(8,128)(2,1)}, u32[]{:S(2)}, u32[]{:S(2)}) %all-to-all-start.4) | async-done | bytes 1277984 | tf_op jit(solution)/shard_map/all_to_all | solution.py:26
  205.3 1.5 convert_element_type.50
  207.1 2.2 fusion.4
  209.2 10.2 %zero_projection_grad.1 = f32[608,2432]{1,0:T(8,128)} custom-call(s32[1]{0:T(128)} %bitcast.15.group, bf16[4,608,128]{2,1,0:T(8,128)(2,1)S(1)} %copy-done.6, bf16[4,608,128]{2,1,0:T(8,128)(2,1)S(1)} %collective-permute-done.6.cot_other, bf16[4,4,608,128]{3,2,1,0:T(8,128)(2,1)} %all-to-all-done.6.out, bf16[4,4,608,128]{3,2,1,0:T(8,128)(2,1)} %collective-permute-done.7.out_other), custom_call_target="tpu_custom_call" | custom-call | flops 3028287488 | bytes 12140544 | tf_op jit(solution)/shard_map/zero_projection_grad/pallas_call | solution.py:245
  (54 shorter events, 1.6 us)
Async XLA Ops:
  0.6 2.7 %copy-start.3 = (bf16[1,2432,256]{2,1,0:T(8,128)(2,1)S(1)}, bf16[1,2432,256]{2,1,0:T(8,128)(2,1)}, u32[]{:S(2)}) copy-start(bf16[1,2432,256]{2,1,0:T(8,128)(2,1)} %refs_4_.1) | copy-start | bytes 3735556
  1.7 35.0 %collective-permute-start.2 = (bf16[608,128]{1,0:T(8,128)(2,1)S(1)}, bf16[608,128]{1,0:T(8,128)(2,1)S(1)}, u32[]{:S(2)}, u32[]{:S(2)}) collective-permute-start(bf16[608,128]{1,0:T(8,128)(2,1)S(1)} %dynamic-slice_bitcast_fusion), channel_id=1, source_target_pairs={{0,16},{16,0},{1,17},{17,1},{2,18},{18,2},{3,19},{19,3},{4,20},{20... | collective-permute-start | bytes 466952 | tf_op jit(solution)/shard_map/ppermute | solution.py:22
  3.4 26.7 %copy-start = (f32[1,3,2432]{1,2,0:T(8,128)}, f32[1,3,2432]{1,2,0:T(8,128)S(1)}, u32[]{:S(2)}) copy-start(f32[1,3,2432]{1,2,0:T(8,128)S(1)} %copy.10) | copy-start | bytes 87556
  24.3 1.0 copy-start.8
  25.4 22.0 %all-to-all-start = ((bf16[4,608,256]{2,1,0:T(8,128)(2,1)}), bf16[4,608,256]{2,1,0:T(8,128)(2,1)}, u32[]{:S(2)}, u32[]{:S(2)}) async-start(bf16[4,608,256]{2,1,0:T(8,128)(2,1)} %bitcast.56), calls=%async_computation | async-start | bytes 2490368 | tf_op jit(solution)/shard_map/all_to_all | solution.py:26
  32.7 4.0 %copy-start.13 = (bf16[1,608,256]{2,1,0:T(8,128)(2,1)S(1)}, bf16[1,608,256]{2,1,0:T(8,128)(2,1)}, u32[]{:S(2)}) copy-start(bf16[1,608,256]{2,1,0:T(8,128)(2,1)} %param.11) | copy-start | bytes 933892
  33.8 1.7 collective-permute-start.4
  36.7 2.7 %copy-start.17 = (bf16[608,128]{1,0:T(8,128)(2,1)}, bf16[608,128]{1,0:T(8,128)(2,1)S(1)}, u32[]{:S(2)}) copy-start(bf16[608,128]{1,0:T(8,128)(2,1)S(1)} %collective-permute-done.2) | copy-start | bytes 466948
  36.8 1.8 copy-start.1
  47.3 19.6 %all-to-all-start.2 = ((bf16[4,1216,128]{2,1,0:T(8,128)(2,1)}), bf16[4,1216,128]{2,1,0:T(8,128)(2,1)S(1)}, u32[]{:S(2)}, u32[]{:S(2)}) async-start(bf16[4,1216,128]{2,1,0:T(8,128)(2,1)} %pad_maximum_fusion), calls=%async_computation.2 | async-start | bytes 2490368 | tf_op jit(solution)/shard_map/all_to_all | solution.py:26
  52.4 2.4 %copy-start.11 = (f32[608,256]{1,0:T(8,128)}, f32[608,256]{1,0:T(8,128)S(1)}, u32[]{:S(2)}) copy-start(f32[608,256]{1,0:T(8,128)S(1)} %convert_reduce_fusion) | copy-start | bytes 1867780
  52.6 1.4 collective-permute-start
  54.1 0.7 copy-start.15
  68.2 5.0 %copy-start.14 = (bf16[1,608,256]{2,1,0:T(8,128)(2,1)S(1)}, bf16[1,608,256]{2,1,0:T(8,128)(2,1)}, u32[]{:S(2)}) copy-start(bf16[1,608,256]{2,1,0:T(8,128)(2,1)} %param.11) | copy-start | bytes 933892
  68.2 5.0 %copy-start.18 = (bf16[608,128]{1,0:T(8,128)(2,1)S(1)}, bf16[608,128]{1,0:T(8,128)(2,1)}, u32[]{:S(2)}) copy-start(bf16[608,128]{1,0:T(8,128)(2,1)} %copy-done.17) | copy-start | bytes 466948
  68.2 34.0 %all-to-all-start.5 = ((bf16[4,1216,128]{2,1,0:T(8,128)(2,1)}), bf16[4,1216,128]{2,1,0:T(8,128)(2,1)S(1)}, u32[]{:S(2)}, u32[]{:S(2)}) async-start(bf16[4,1216,128]{2,1,0:T(8,128)(2,1)} %broadcast_in_dim.21), calls=%async_computation.5 | async-start | bytes 2490368 | tf_op jit(solution)/shard_map/all_to_all | solution.py:26
  103.1 12.0 %all-to-all-start.3 = ((bf16[4,608,128]{2,1,0:T(8,128)(2,1)}), bf16[4,608,128]{2,1,0:T(8,128)(2,1)S(1)}, u32[]{:S(2)}, u32[]{:S(2)}) async-start(bf16[4,608,128]{2,1,0:T(8,128)(2,1)} %broadcast_in_dim.19), calls=%async_computation.3 | async-start | bytes 1245184 | tf_op jit(solution)/shard_map/all_to_all | solution.py:26
  118.0 32.5 %all-to-all-start.6 = ((bf16[4,4,608,128]{3,2,1,0:T(8,128)(2,1)}), bf16[4,4,608,128]{3,2,1,0:T(8,128)(2,1)}, u32[]{:S(2)}, u32[]{:S(2)}) async-start(bf16[4,4,608,128]{3,2,1,0:T(8,128)(2,1)} %broadcast_in_dim.22), calls=%async_computation.6 | async-start | bytes 4980736 | tf_op jit(solution)/shard_map/all_to_all | solution.py:26
  122.5 28.0 %copy-start.16 = (bf16[608,128]{1,0:T(8,128)(2,1)S(1)}, bf16[608,128]{1,0:T(8,128)(2,1)}, u32[]{:S(2)}) copy-start(bf16[608,128]{1,0:T(8,128)(2,1)} %copy-done.15) | copy-start | bytes 466948
  123.7 32.0 %collective-permute-start.5 = (bf16[2432,128]{1,0:T(8,128)(2,1)}, bf16[2432,128]{1,0:T(8,128)(2,1)S(1)}, u32[]{:S(2)}, u32[]{:S(2)}) collective-permute-start(bf16[2432,128]{1,0:T(8,128)(2,1)} %bitcast.17), channel_id=1, source_target_pairs={{0,16},{16,0},{1,17},{17,1},{2,18},{18,2},{3,19},{19,3},{4,20},{20... | collective-permute-start | bytes 1867784 | tf_op jit(solution)/shard_map/ppermute | solution.py:22
  150.5 58.7 %collective-permute-start.7 = (bf16[4,4,608,128]{3,2,1,0:T(8,128)(2,1)}, bf16[4,4,608,128]{3,2,1,0:T(8,128)(2,1)}, u32[]{:S(2)}, u32[]{:S(2)}) collective-permute-start(bf16[4,4,608,128]{3,2,1,0:T(8,128)(2,1)} %all-to-all-done.6.out), channel_id=1, source_target_pairs={{0,16},{16,0},{1,17},{17,1},{2,18},{18,2},{3,19},{19,3},{4,20},{20... | collective-permute-start | bytes 7471112 | tf_op jit(solution)/shard_map/ppermute | solution.py:22
  151.5 32.2 %all-to-all-start.1 = ((bf16[4,608,128]{2,1,0:T(8,128)(2,1)}), bf16[4,608,128]{2,1,0:T(8,128)(2,1)}, u32[]{:S(2)}, u32[]{:S(2)}) async-start(bf16[4,608,128]{2,1,0:T(8,128)(2,1)} %broadcast_in_dim.16), calls=%async_computation.1 | async-start | bytes 1245184 | tf_op jit(solution)/shard_map/all_to_all | solution.py:26
  155.6 0.8 copy-start.9
  156.5 1.3 copy-start.4
  157.8 1.3 copy-start.5
  159.0 1.1 copy-start.7
  160.1 1.1 copy-start.10
  161.2 27.0 %copy-start.2 = (bf16[608,2432]{1,0:T(8,128)(2,1)S(1)}, bf16[608,2432]{1,0:T(8,128)(2,1)}, u32[]{:S(2)}) copy-start(bf16[608,2432]{1,0:T(8,128)(2,1)} %weight.1) | copy-start | bytes 8871940
  183.7 21.6 %all-to-all-start.4 = ((bf16[4,624,256]{2,1,0:T(8,128)(2,1)}), bf16[4,624,256]{2,1,0:T(8,128)(2,1)}, u32[]{:S(2)}, u32[]{:S(2)}) async-start(bf16[4,624,256]{2,1,0:T(8,128)(2,1)} %backward_layers.1), calls=%async_computation.4 | async-start | bytes 2555904 | tf_op jit(solution)/shard_map/all_to_all | solution.py:26
  188.2 4.0 %copy-start.12 = (f32[608,256]{1,0:T(8,128)S(1)}, f32[608,256]{1,0:T(8,128)}, u32[]{:S(2)}) copy-start(f32[608,256]{1,0:T(8,128)} %copy-done.11) | copy-start | bytes 1867780
  190.3 3.8 %copy-start.6 = (bf16[4,608,128]{2,1,0:T(8,128)(2,1)S(1)}, bf16[4,608,128]{2,1,0:T(8,128)(2,1)}, u32[]{:S(2)}) copy-start(bf16[4,608,128]{2,1,0:T(8,128)(2,1)} %get-tuple-element.16.cot) | copy-start | bytes 1867780
  190.4 1.9 collective-permute-start.1
  192.1 15.0 %collective-permute-start.3 = (f32[608,128]{1,0:T(8,128)}, f32[608,128]{1,0:T(8,128)S(1)}, u32[]{:S(2)}, u32[]{:S(2)}) collective-permute-start(f32[608,128]{1,0:T(8,128)} %get-tuple-element.12), channel_id=1, source_target_pairs={{0,16},{16,0},{1,17},{17,1},{2,18},{18,2},{3,19},{19,3},{4,20},{20... | collective-permute-start | bytes 933896 | tf_op jit(solution)/shard_map/ppermute | solution.py:22
  194.1 15.1 %collective-permute-start.6 = (bf16[4,608,128]{2,1,0:T(8,128)(2,1)S(1)}, bf16[4,608,128]{2,1,0:T(8,128)(2,1)S(1)}, u32[]{:S(2)}, u32[]{:S(2)}) collective-permute-start(bf16[4,608,128]{2,1,0:T(8,128)(2,1)S(1)} %copy-done.6), channel_id=1, source_target_pairs={{0,16},{16,0},{1,17},{17,1},{2,18},{18,2},{3,19},{19,3},{4,20},{20... | collective-permute-start | bytes 1867784 | tf_op jit(solution)/shard_map/ppermute | solution.py:22

commit v3 on v0

v3 whole, which is shorter than its diff:
```python
import functools

import jax
import jax.numpy as jnp
from jax import lax
from jax.experimental import pallas as pl
from jax.experimental.pallas import tpu as pltpu
from jax.sharding import PartitionSpec as P

EPSILON = 1e-06
SQRT_2_OVER_PI = 0.7978845608028654
CHUNK = 256
WIDE = 2
AHEAD = 4
MIB = 1024 * 1024
F32, BF16 = jnp.float32, jnp.bfloat16
WHOLE = pl.BlockSpec(memory_space=pltpu.VMEM)
HELD = pl.BlockSpec(memory_space=pltpu.HBM)
SCALARS = pl.BlockSpec(memory_space=pltpu.SMEM)


def pieces(start, stop, size=CHUNK):
    return [(at, min(size, stop - at)) for at in range(start, stop, size)]


def middle(extent):
    step = CHUNK * WIDE
    return max(extent // 2 // step, 1) * step if extent > step else extent // 2 // 128 * 128


def after(value, *others):
    return lax.optimization_barrier((value,) + others)[0]


def swap_grp(value):
    return lax.ppermute(value, "grp", [(0, 1), (1, 0)])


def stages():
    return (lax.axis_size("fsdp") - 1).bit_length()


def step(value, stage):
    length, bits = lax.axis_size("fsdp"), stages()
    pairs = []
    for group, bit in ((0, stage), (1, bits - 1 - stage)):
        pairs += [(group * length + i, group * length + (i ^ (1 << bit))) for i in range(length)]
    return lax.ppermute(value, ("grp", "fsdp"), pairs)


def block_order(group, me):
    length, bits = lax.axis_size("fsdp"), stages()
    turned = [sum(((v >> b) & 1) << (bits - 1 - b) for b in range(bits)) for v in range(length)]
    up, down = jnp.arange(length, dtype=jnp.int32), jnp.array(turned, jnp.int32)
    return me ^ jnp.where(group == 0, up, down)


def gather_dp(value):
    length = lax.axis_size("dp")
    return [value] + [
        lax.ppermute(value, "dp", [(i, i ^ mask) for i in range(length)]) for mask in range(1, length)
    ]


def block_of(value, index, rows):
    return lax.dynamic_slice_in_dim(value, index * rows, rows, 0)


def split_three(value):
    high = value.astype(BF16)
    rest = value - high.astype(F32)
    mid = rest.astype(BF16)
    return high, mid, (rest - mid.astype(F32)).astype(BF16)


def pack_sums(plain, along):
    tail = [part.astype(F32) for part in split_three(plain) + split_three(along)]
    return jnp.concatenate(tail + [jnp.zeros((10, plain.shape[1]), F32)], 0).astype(BF16)


def unpack_sums(tail):
    tail = tail.astype(F32)
    return tail[0:1] + tail[1:2] + tail[2:3], tail[3:4] + tail[4:5] + tail[5:6]


def gelu_and_slope(v):
    square = v * v
    t = jnp.tanh(SQRT_2_OVER_PI * (v + 0.044715 * (square * v)))
    rise = 0.5 * (1.0 + t)
    slope = rise + 0.5 * v * (1.0 - t * t) * (SQRT_2_OVER_PI * (1.0 + (3 * 0.044715) * square))
    return v * rise, slope


class Stream:
    def __init__(self, pairs, sems):
        self.copies = [pltpu.make_async_copy(a, b, sems.at[k]) for k, (a, b) in enumerate(pairs)]
        self.next = 0
        for copy in self.copies[:AHEAD]:
            copy.start()

    def take(self):
        for k in range(self.next, min(self.next + WIDE, len(self.copies))):
            self.copies[k].wait()
            if k + AHEAD < len(self.copies):
                self.copies[k + AHEAD].start()
            self.next = k + 1


def row_stream(weight, buf, start, stop, sems):
    return Stream(
        [(weight.at[0, pl.ds(a, n), :], buf.at[pl.ds(a - start, n), :]) for a, n in pieces(start, stop)], sems
    )


def column_stream(weight, buf, start, stop, sems):
    return Stream(
        [(weight.at[0, :, pl.ds(a, n)], buf.at[:, pl.ds(a - start, n)]) for a, n in pieces(start, stop)], sems
    )


def pipelined(extent, product, finish):
    held = None
    for part in pieces(0, extent, CHUNK * WIDE):
        value = product(*part)
        if held is not None:
            finish(*held)
        held = part + (value,)
    finish(*held)


def params(flops, moved, transcendentals=0, grant=50):
    return dict(
        compiler_params=pltpu.CompilerParams(vmem_limit_bytes=grant * MIB),
        cost_estimate=pl.CostEstimate(flops=flops, bytes_accessed=moved, transcendentals=transcendentals),
    )


def struct(shape, dtype):
    return jax.ShapeDtypeStruct(shape, dtype)


def staging(rows, features, lanes):
    return pltpu.VMEM((features, lanes) if rows % 16 else (8, 128), F32)


def place_blocks(target, lanes, stage, order, blocks, rows, first=0):
    for place, value in enumerate(blocks):
        if rows % 16:
            stage[pl.ds(pl.multiple_of(order[first + place] * rows, 8), rows), :] = value().astype(F32)
        else:
            target[pl.ds(pl.multiple_of(order[first + place] * rows, 16), rows), lanes] = value()
    if rows % 16:
        target[:, lanes] = stage[...].astype(target.dtype)


def normalize(acts, mod, normed, stats):
    features, tokens = acts.shape[1:]
    parts = pieces(0, features, 128)
    total = jnp.zeros((1, tokens), F32)
    for start, size in parts:
        total += jnp.sum(acts[0, pl.ds(start, size), :].astype(F32), 0, keepdims=True)
    mean = total / features
    total = jnp.zeros((1, tokens), F32)
    for start, size in parts:
        centred = acts[0, pl.ds(start, size), :].astype(F32) - mean
        total += jnp.sum(centred * centred, 0, keepdims=True)
    inv = lax.rsqrt(total / features + EPSILON)
    stats[0:1, :] = mean
    stats[1:2, :] = inv
    for start, size in parts:
        rows = pl.ds(start, size)
        xhat = (acts[0, rows, :].astype(F32) - mean) * inv
        normed[rows, :] = (xhat * (1.0 + mod[rows, 1:2]) + mod[rows, 0:1]).astype(BF16)


def expand_products(stream, buf, normed, turned, slope_out):
    def product(at, size):
        stream.take()
        return jnp.dot(buf[pl.ds(at, size), :], normed[...], preferred_element_type=F32)

    def finish(at, size, pre):
        hidden, slope = gelu_and_slope(pre)
        slope_out[pl.ds(at, size), :] = slope
        turned[:, pl.ds(at, size)] = hidden.T.astype(BF16)

    pipelined(slope_out.shape[0], product, finish)


def expand_first_kernel(acts, mod, w_in, normed, stats, turned, slope_out, buf, sems):
    stream = row_stream(w_in, buf, 0, slope_out.shape[0], sems)
    normalize(acts, mod, normed, stats)
    expand_products(stream, buf, normed, turned, slope_out)


def expand_first(acts, mod, w_in, part, name):
    features, tokens = acts.shape[1:]
    return pl.pallas_call(
        expand_first_kernel,
        out_shape=(
            struct((features, tokens), BF16),
            struct((2, tokens), F32),
            struct((tokens, part), BF16),
            struct((part, tokens), F32),
        ),
        in_specs=[WHOLE, WHOLE, HELD],
        out_specs=[WHOLE] * 4,
        scratch_shapes=[pltpu.VMEM((part, features), BF16), pltpu.SemaphoreType.DMA((len(pieces(0, part)),))],
        name=name,
        **params(2 * part * features * tokens, 2 * part * features + 8 * part * tokens, part * tokens),
    )(acts, mod, w_in)


def expand_rest_kernel(start, normed, w_in, turned, slope_out, buf, sems):
    stream = row_stream(w_in, buf, start, start + slope_out.shape[0], sems)
    expand_products(stream, buf, normed, turned, slope_out)


def expand_rest(normed, w_in, start, name):
    features, tokens = normed.shape
    part = w_in.shape[1] - start
    return pl.pallas_call(
        functools.partial(expand_rest_kernel, start),
        out_shape=(struct((tokens, part), BF16), struct((part, tokens), F32)),
        in_specs=[WHOLE, HELD],
        out_specs=(WHOLE, WHOLE),
        scratch_shapes=[
            pltpu.VMEM((part, features), BF16),
            pltpu.SemaphoreType.DMA((len(pieces(start, start + part)),)),
        ],
        name=name,
        **params(2 * part * features * tokens, 2 * part * features + 8 * part * tokens, part * tokens),
    )(normed, w_in)


def write_blocks(order, full, sent, kept):
    for targets, shift in ((kept, 0), (sent, 1)):
        for place, target in enumerate(targets):
            rows = target.shape[0]
            offset = pl.multiple_of(order[2 * place + shift] * rows, 8)
            target[...] = full[pl.ds(offset, rows), :].astype(target.dtype)


def weight_rows_product(left, right, buf):
    split = left.shape[1]

    def product(at, size):
        columns = pl.ds(at, size)
        return jnp.dot(left[...], buf[:split, columns], preferred_element_type=F32) + jnp.dot(
            right[...], buf[split:, columns], preferred_element_type=F32
        )

    return product


def contract_first_kernel(stop, left, right, weight, full, buf, sems):
    stream = column_stream(weight, buf, 0, stop, sems)
    multiply = weight_rows_product(left, right, buf)

    def product(at, size):
        stream.take()
        return multiply(at, size)

    def finish(at, size, value):
        full[pl.ds(at, size), :] = value.T

    pipelined(stop, product, finish)


def contract_first(left, right, weight, stop, name):
    hidden, features = weight.shape[1:]
    tokens = left.shape[0]
    return pl.pallas_call(
        functools.partial(contract_first_kernel, stop),
        out_shape=struct((stop, tokens), F32),
        in_specs=[WHOLE, WHOLE, HELD],
        out_specs=WHOLE,
        scratch_shapes=[pltpu.VMEM((hidden, stop), BF16), pltpu.SemaphoreType.DMA((len(pieces(0, stop)),))],
        name=name,
        **params(2 * hidden * stop * tokens, 2 * hidden * stop + 2 * hidden * tokens + 4 * stop * tokens),
    )(left, right, weight)


def contract_last_kernel(order, left, right, weight, before, *refs):
    outs, (buf, full, sems) = refs[:-3], refs[-3:]
    start, features = before.shape[0], full.shape[0]
    stream = column_stream(weight, buf, start, features, sems)
    multiply = weight_rows_product(left, right, buf)

    def product(at, size):
        stream.take()
        return multiply(at, size)

    def finish(at, size, value):
        full[pl.ds(start + at, size), :] = value.T

    full[:start, :] = before[...]
    pipelined(features - start, product, finish)
    count = len(outs) // 2
    write_blocks(order, full, outs[:count], outs[count:])


def contract_last(order, left, right, weight, before, blocks, name):
    hidden, features = weight.shape[1:]
    tokens, start = left.shape[0], before.shape[0]
    rows, part, count = features // blocks, features - before.shape[0], blocks // 2
    outs = pl.pallas_call(
        contract_last_kernel,
        out_shape=[struct((rows, tokens), BF16)] * count + [struct((rows, tokens), F32)] * count,
        in_specs=[SCALARS, WHOLE, WHOLE, HELD, WHOLE],
        out_specs=[WHOLE] * blocks,
        scratch_shapes=[
            pltpu.VMEM((hidden, part), BF16),
            pltpu.VMEM((features, tokens), F32),
            pltpu.SemaphoreType.DMA((len(pieces(start, features)),)),
        ],
        name=name,
        **params(2 * hidden * part * tokens, 2 * hidden * part + 2 * hidden * tokens + 8 * features * tokens),
    )(order, left, right, weight, before)
    return outs[:count], outs[count:]


def spread_first_kernel(blocks, order, *refs):
    own, other, far, (mod, slope, weight, grad, turned, buf, stage, sems) = (
        refs[:blocks], refs[blocks : 2 * blocks], refs[2 * blocks : 3 * blocks], refs[3 * blocks :]
    )
    part = slope.shape[0]
    stream = row_stream(weight, buf, 0, part, sems)
    rows, half = own[0].shape
    group = order[blocks]
    control = group == 0

    def scaled(value, place, first):
        at = pl.ds(pl.multiple_of(order[first + place] * rows, 8), rows)
        return (value.astype(F32) * jnp.where(control, 1.0, mod[at, 2:3])).astype(BF16)

    def mine(place):
        return scaled(jnp.where(control, own[place][...], other[place][...]), place, 0)

    def theirs(place):
        return scaled(far[place][...], place, blocks + 1)

    for owner, make, first in ((group, mine, 0), (1 - group, theirs, blocks + 1)):
        lanes = pl.ds(pl.multiple_of(owner * half, half), half)
        values = [functools.partial(make, place) for place in range(blocks)]
        place_blocks(grad, lanes, stage, order, values, rows, first)
    spread_products(stream, buf, grad, slope, turned)


def spread_products(stream, buf, grad, slope, turned):
    def product(at, size):
        stream.take()
        return jnp.dot(buf[pl.ds(at, size), :], grad[...], preferred_element_type=F32)

    def finish(at, size, value):
        turned[:, pl.ds(at, size)] = (value * slope[pl.ds(at, size), :]).T.astype(BF16)

    pipelined(slope.shape[0], product, finish)


def spread_first(order, own, other, far, mod, slope, weight, name):
    hidden, features = weight.shape[1:]
    part, tokens = slope.shape
    blocks = len(own)
    return pl.pallas_call(
        functools.partial(spread_first_kernel, blocks),
        out_shape=(struct((features, tokens), BF16), struct((tokens, part), BF16)),
        in_specs=[SCALARS] + [WHOLE] * (3 * blocks + 2) + [HELD],
        out_specs=(WHOLE, WHOLE),
        scratch_shapes=[
            pltpu.VMEM((part, features), BF16),
            staging(own[0].shape[0], features, own[0].shape[1]),
            pltpu.SemaphoreType.DMA((len(pieces(0, part)),)),
        ],
        name=name,
        **params(2 * part * features * tokens, 2 * part * features + 6 * part * tokens + 4 * features * tokens),
    )(order, *own, *other, *far, mod, slope, weight)


def spread_rest_kernel(start, grad, slope, weight, turned, buf, sems):
    stream = row_stream(weight, buf, start, start + slope.shape[0], sems)
    spread_products(stream, buf, grad, slope, turned)


def spread_rest(grad, slope, weight, start, name):
    hidden, features = weight.shape[1:]
    part, tokens = slope.shape
    return pl.pallas_call(
        functools.partial(spread_rest_kernel, start),
        out_shape=struct((tokens, part), BF16),
        in_specs=[WHOLE, WHOLE, HELD],
        out_specs=WHOLE,
        scratch_shapes=[pltpu.VMEM((part, features), BF16), pltpu.SemaphoreType.DMA((len(pieces(start, hidden)),))],
        name=name,
        **params(2 * part * features * tokens, 2 * part * features + 6 * part * tokens + 2 * features * tokens),
    )(grad, slope, weight)


def norm_products(stream, start, stop, left, right, acts, stats, mod, buf, full, base, sums):
    mean, inv = stats[0:1, :], stats[1:2, :]
    multiply = weight_rows_product(left, right, buf)

    def product(at, size):
        stream.take()
        return multiply(at, size)

    def finish(at, size, value):
        rows = pl.ds(start + at, size)
        value = value.T
        full[pl.ds(base + at, size), :] = value
        scaled = value * (1.0 + mod[rows, 1:2])
        xhat = (acts[0, rows, :].astype(F32) - mean) * inv
        sums[0] += jnp.sum(scaled, 0, keepdims=True)
        sums[1] += jnp.sum(scaled * xhat, 0, keepdims=True)

    pipelined(stop - start, product, finish)


def norm_first_kernel(left, right, acts, stats, mod, weight, full, sums_out, buf, sems):
    stop, tokens = full.shape
    stream = column_stream(weight, buf, 0, stop, sems)
    sums = [jnp.zeros((1, tokens), F32), jnp.zeros((1, tokens), F32)]
    norm_products(stream, 0, stop, left, right, acts, stats, mod, buf, full, 0, sums)
    sums_out[0:1, :] = sums[0]
    sums_out[1:2, :] = sums[1]


def norm_first(left, right, acts, stats, mod, weight, stop, name):
    hidden, features = weight.shape[1:]
    tokens = left.shape[0]
    return pl.pallas_call(
        norm_first_kernel,
        out_shape=(struct((stop, tokens), F32), struct((2, tokens), F32)),
        in_specs=[WHOLE] * 5 + [HELD],
        out_specs=(WHOLE, WHOLE),
        scratch_shapes=[pltpu.VMEM((hidden, stop), BF16), pltpu.SemaphoreType.DMA((len(pieces(0, stop)),))],
        name=name,
        **params(2 * hidden * stop * tokens, 2 * hidden * stop + 2 * hidden * tokens + 6 * stop * tokens),
    )(left, right, acts, stats, mod, weight)


def norm_last_kernel(rows, order, left, right, acts, stats, mod, weight, before, sums_before, *refs):
    outs, (sums_out, buf, full, sems) = refs[:-4], refs[-4:]
    start, (features, tokens) = before.shape[0], full.shape
    stream = column_stream(weight, buf, start, features, sems)
    sums = [sums_before[0:1, :], sums_before[1:2, :]]
    full[:start, :] = before[...]
    norm_products(stream, start, features, left, right, acts, stats, mod, buf, full, start, sums)
    count = len(outs) // 2
    padded = outs[0].shape[0] - 16
    tail = pack_sums(*sums)
    for place in range(count):
        offset = pl.multiple_of(order[2 * place] * rows, 8)
        outs[count + place][...] = full[pl.ds(offset, rows), :]
        offset = pl.multiple_of(order[2 * place + 1] * rows, 8)
        block = full[pl.ds(offset, rows), :]
        if padded > rows:
            block = jnp.concatenate([block, jnp.zeros((padded - rows, tokens), F32)], 0)
        outs[place][:padded, :] = block.astype(BF16)
        outs[place][padded:, :] = tail
    sums_out[0:1, :] = sums[0]
    sums_out[1:2, :] = sums[1]


def norm_last(order, left, right, acts, stats, mod, weight, before, sums, blocks, name):
    hidden, features = weight.shape[1:]
    tokens, start = left.shape[0], before.shape[0]
    rows, part, count = features // blocks, features - before.shape[0], blocks // 2
    outs = pl.pallas_call(
        functools.partial(norm_last_kernel, rows),
        out_shape=[struct((-(-rows // 16) * 16 + 16, tokens), BF16)] * count
        + [struct((rows, tokens), F32)] * count
        + [struct((2, tokens), F32)],
        in_specs=[SCALARS] + [WHOLE] * 5 + [HELD] + [WHOLE] * 2,
        out_specs=[WHOLE] * (blocks + 1),
        scratch_shapes=[
            pltpu.VMEM((hidden, part), BF16),
            pltpu.VMEM((features, tokens), F32),
            pltpu.SemaphoreType.DMA((len(pieces(start, features)),)),
        ],
        name=name,
        **params(2 * hidden * part * tokens, 2 * hidden * part + 2 * hidden * tokens + 8 * features * tokens),
    )(order, left, right, acts, stats, mod, weight, before, sums)
    return outs[:count], outs[count:-1], outs[-1]


def fold_kernel(rows, count, *refs):
    got, kept, (sums, *outs) = refs[:count], refs[count : 2 * count], refs[2 * count :]
    more = unpack_sums(got[0][-16:, :])
    plain, along = sums[0:1, :] + more[0], sums[1:2, :] + more[1]
    tail = pack_sums(plain, along)
    padded = got[0].shape[0] - 16
    for place in range(count // 2):
        even, odd = 2 * place, 2 * place + 1
        outs[count // 2 + place][...] = kept[even][...] + got[even][:rows, :].astype(F32)
        block = kept[odd][...] + got[odd][:rows, :].astype(F32)
        if padded > rows:
            block = jnp.concatenate([block, jnp.zeros((padded - rows, block.shape[1]), F32)], 0)
        outs[place][:padded, :] = block.astype(BF16)
        outs[place][padded:, :] = tail
    outs[-1][0:1, :] = plain
    outs[-1][1:2, :] = along


def fold(got, kept, sums):
    count, (rows, tokens) = len(kept), kept[0].shape
    outs = pl.pallas_call(
        functools.partial(fold_kernel, rows, count),
        out_shape=[struct(got[0].shape, BF16)] * (count // 2)
        + [struct((rows, tokens), F32)] * (count // 2)
        + [struct((2, tokens), F32)],
        in_specs=[WHOLE] * (2 * count + 1),
        out_specs=[WHOLE] * (count + 1),
        name="fold",
        **params(2 * count * rows * tokens, 8 * count * rows * tokens, grant=12),
    )(*got, *kept, sums)
    return outs[: count // 2], outs[count // 2 : -1], outs[-1]


def upstream_kernel(blocks, order, weight, own, arrived, *refs):
    outs, (cot0, cot1, cot1_rows, full) = refs[:-4], refs[-4:]
    group = order[blocks]
    control = group == 0
    half = cot0.shape[1]
    lanes = pl.ds(pl.multiple_of(group * half, half), half)
    cot0[...] = jnp.where(control, own[:, lanes], arrived[:, lanes])
    mine = jnp.where(control, arrived[:, lanes], own[:, lanes])
    cot1[...] = mine
    cot1_rows[...] = jnp.where(control, arrived[...], own[...])
    full[...] = lax.dot_general(mine, weight[...], (((0,), (0,)), ((), ())), preferred_element_type=F32).T
    count = blocks // 2
    write_blocks(order, full, outs[:count], outs[count:])


def upstream_terms(order, weight, own, arrived, blocks):
    rows, tokens = own.shape
    half, count = tokens // 2, blocks // 2
    outs = pl.pallas_call(
        functools.partial(upstream_kernel, blocks),
        out_shape=[struct((rows, half), BF16)] * count
        + [struct((rows, half), F32)] * count
        + [struct((rows, half), BF16)] * 2
        + [struct((rows, tokens), BF16)],
        in_specs=[SCALARS] + [WHOLE] * 3,
        out_specs=[WHOLE] * (blocks + 3),
        scratch_shapes=[pltpu.VMEM((weight.shape[1], half), F32)],
        name="upstream_terms",
        **params(2 * weight.size * half, 2 * weight.size + 4 * blocks * rows * half, grant=12),
    )(order, weight, own, arrived)
    return outs[:count], outs[count:blocks], *outs[blocks:]


def residual_kernel(order, weight, *refs):
    stack, (result, full, stage) = refs[:-3], refs[-3:]
    values = [lambda value=value: value[...] for value in stack]
    place_blocks(full, slice(None), stage, order, values, stack[0].shape[0])
    result[...] = jnp.dot(weight[...], full[...], preferred_element_type=F32)


def residual_rows(order, weight, stack):
    blocks, (rows, half) = len(stack), stack[0].shape
    return pl.pallas_call(
        residual_kernel,
        out_shape=struct((rows, half), F32),
        in_specs=[SCALARS] + [WHOLE] * (blocks + 1),
        out_specs=WHOLE,
        scratch_shapes=[pltpu.VMEM((blocks * rows, half), BF16), staging(rows, blocks * rows, half)],
        name="residual_rows",
        **params(2 * weight.size * half, 2 * weight.size + 4 * blocks * rows * half, grant=12),
    )(order, weight, *stack)


def zero_grad_kernel(blocks, parts, order, dp_order, *refs):
    cots, stacks, (out, lhs, rhs, stage, buf, sems) = refs[:parts], refs[parts:-6], refs[-6:]
    near, near_other, far, far_other = (stacks[k * blocks : (k + 1) * blocks] for k in range(4))
    rows, half = near[0].shape
    group = order[blocks]
    for part in range(parts):
        lhs[:, pl.ds(pl.multiple_of(dp_order[part] * 2 * half, 2 * half), 2 * half)] = cots[part][...]
        for side, sources in enumerate((near, near_other) if part == 0 else (far, far_other)):
            at = Ellipsis if part == 0 else part - 1
            values = [lambda source=source, at=at: source[at] for source in sources]
            owner = group if side == 0 else 1 - group
            lanes = pl.ds(pl.multiple_of((dp_order[part] * 2 + owner) * half, half), half)
            place_blocks(rhs, lanes, stage, order, values, rows, side * (blocks + 1))
    copies = []
    for k, (start, size) in enumerate(pieces(0, blocks * rows, CHUNK * WIDE)):
        columns = pl.ds(start, size)
        buf[:, columns] = lax.dot_general(
            lhs[...], rhs[columns, :], (((1,), (1,)), ((), ())), preferred_element_type=F32
        )
        copies.append(pltpu.make_async_copy(buf.at[:, columns], out.at[:, columns], sems.at[k]))
        copies[-1].start()
    for copy in copies:
        copy.wait()


def zero_projection_grad(order, dp_order, cots, near, near_other, far, far_other):
    blocks, (rows, half) = len(near), near[0].shape
    parts = len(cots)
    features, tokens = blocks * rows, parts * 2 * half

    return pl.pallas_call(
        functools.partial(zero_grad_kernel, blocks, parts),
        out_shape=struct((rows, features), F32),
        in_specs=[SCALARS] * 2 + [WHOLE] * (parts + 4 * blocks),
        out_specs=HELD,
        scratch_shapes=[
            pltpu.VMEM((rows, tokens), BF16),
            pltpu.VMEM((features, tokens), BF16),
            staging(rows, features, half),
            pltpu.VMEM((rows, features), F32),
            pltpu.SemaphoreType.DMA((len(pieces(0, features, CHUNK * WIDE)),)),
        ],
        name="zero_projection_grad",
        **params(2 * tokens * rows * features, 4 * rows * features + 2 * tokens * (rows + features), grant=28),
    )(order, dp_order, *cots, *near, *near_other, *far, *far_other)


def steps(values, level, *during):
    got = [step(value, level) for value in values]
    return list(lax.optimization_barrier((tuple(got),) + during)[0]) if during else got


def local(acts, modulation, w_in, w_out, zero_weight, cotangent):
    own_cot = cotangent[0]
    features, tokens = acts.shape[1:]
    hidden = w_in.shape[1]
    rows = own_cot.shape[0]
    half = tokens // 2
    blocks, levels = lax.axis_size("fsdp"), stages()
    parts = lax.axis_size("dp")
    group = lax.axis_index("grp").astype(jnp.int32)
    me = lax.axis_index("fsdp").astype(jnp.int32)
    is_control = group == 0
    places = block_order(group, me)
    order = jnp.concatenate([places, group[None], block_order(1 - group, me)])
    dp_order = lax.axis_index("dp").astype(jnp.int32) ^ jnp.arange(parts, dtype=jnp.int32)
    mod = modulation[0].T
    own_mod = block_of(mod, me, rows)
    own_gate = own_mod[:, 2:3]

    arrived = swap_grp(own_cot)
    gate0 = jnp.where(is_control, modulation[0, 2], swap_grp(modulation[0, 2]))
    own_gate0 = lax.dynamic_slice_in_dim(gate0, me * rows, rows, 0)[:, None]
    split, cut = middle(hidden), middle(features)
    normed, stats, turned_a, slope_a = expand_first(acts, mod, w_in, split, "expand_first")
    arrived = after(arrived, turned_a)

    sent, kept, cot0, cot1, cot1_rows = upstream_terms(order, zero_weight, own_cot, arrived, blocks)
    cots = gather_dp(cot1_rows)
    cot_stack, done = [cot1], ()
    for level in range(levels):
        if level == 0:
            turned_b, slope_b = expand_rest(after(normed, *sent), w_in, split, "expand_rest")
            done = (turned_b,)
        elif level == 1:
            branch = contract_first(after(turned_a, *sent), turned_b, w_out, cut, "contract_first")
            done = (branch,)
        count = len(kept)
        got = steps(list(sent) + cot_stack, level, *done)
        kept = [a + b.astype(F32) for a, b in zip(kept, got)]
        cot_stack = cot_stack + got[count:]
        if level + 1 < levels:
            sent, kept = [value.astype(BF16) for value in kept[1::2]], kept[0::2]
    up_half = kept[0] + cot0.astype(F32)
    gated = [(own_gate0 * up_half).astype(BF16)]

    sent, kept = contract_last(order, after(turned_a, *gated), turned_b, w_out, branch, blocks, "contract_last")
    for level in range(levels):
        gated = gated + (steps(gated, level, sent[0]) if level == 0 else steps(gated, level))
    crossed = [swap_grp(jnp.where(is_control, a, b)) for a, b in zip(cot_stack, gated)]
    up_rows = jnp.where(is_control, jnp.concatenate([up_half, swap_grp(up_half)], 1), own_cot.astype(F32))

    pre_grads = []
    for level in range(levels):
        if level == 0:
            grad, turned = spread_first(
                order, gated, cot_stack, crossed, mod, after(slope_a, *sent, *cots), w_out, "spread_first"
            )
            pre_grads.append(turned)
        elif level == 1:
            pre_grads.append(spread_rest(grad, after(slope_b, *sent), w_out, split, "spread_rest"))
        got = steps(sent, level, pre_grads[-1])
        kept = [a + b.astype(F32) for a, b in zip(kept, got)]
        if level + 1 < levels:
            sent, kept = [value.astype(BF16) for value in kept[1::2]], kept[0::2]
    own_values = block_of(acts[0], me, rows).astype(F32)
    sums = own_values + own_gate * kept[0]
    out_rows = sums.astype(BF16)

    out_half = jnp.where(is_control, out_rows[:, :half], swap_grp(out_rows[:, half:]))
    far = gather_dp(out_half)[1:]
    near = [out_half]
    for level in range(levels):
        tied = after(pre_grads[0], *near)
        if level == 0:
            norm, token_sums = norm_first(tied, pre_grads[1], acts, stats, mod, w_in, cut, "norm_first")
            done = norm
        elif level == 1:
            sent, kept, token_sums = norm_last(
                order, tied, pre_grads[1], acts, stats, mod, w_in, norm, token_sums, blocks, "norm_last"
            )
            done = sent[0]
        near = near + steps(near, level, done)
    near_other = [swap_grp(value) for value in near]
    residual = residual_rows(order, zero_weight, after(near, sent[0]))
    far = [jnp.stack(after(far, residual))]

    for level in range(levels):
        got = steps(sent, level)
        far = far + steps(far, level)
        if level + 1 < levels:
            sent, kept, token_sums = fold(got, kept, token_sums)
    more = unpack_sums(got[0][-16:])
    plain, along = token_sums[0:1] + more[0], token_sums[1:2] + more[1]
    kept = [kept[0] + got[0][:rows].astype(F32)]
    mean, inv = stats[0:1], stats[1:2]
    back = inv * (
        kept[0] * (1.0 + own_mod[:, 1:2]) - plain / features - (own_values - mean) * inv * (along / features)
    )
    residual = jnp.concatenate([swap_grp(residual), residual], 1)
    block_rows = jnp.where(is_control, out_rows, (sums + residual).astype(BF16))

    far_other = [swap_grp(value) for value in far]
    zero_grad = zero_projection_grad(order, dp_order, cots, near, near_other, far, far_other)
    return (block_rows[None], (up_rows + back)[None], zero_grad)


def solution(mesh):
    placed = (
        P("grp", None, "dp"),
        P("grp", None, None),
        P("grp", "fsdp", None),
        P("grp", "fsdp", None),
        P("fsdp", None),
        P("grp", "fsdp", "dp"),
    )
    return jax.shard_map(
        local,
        mesh=mesh,
        in_specs=placed,
        out_specs=(P("grp", "fsdp", "dp"), P("grp", "fsdp", "dp"), P("fsdp", None)),
        check_vma=False,
    )
```

time: 395 us -> 145 us (0.37)
  waiting for transfers between devices: 303 us -> 35.1 us
  Pallas kernels: 0 us -> 58.1 us
  matrix products: 41 us -> 0 us
  starting transfers between devices: 4.59 us -> 36.3 us
  between operations: 13.9 us -> 1.38 us
  local copies, waits for them, and re-layouts: 19.2 us -> 9.52 us
  other arithmetic: 13.1 us -> 4.26 us
    psum x3 -> x0, waiting for transfers between devices: 301 us -> none  [the longest x2 178 us: sum_features(): return lax.psum(product, 'fsdp')]
    pallas_call x0 -> x12, Pallas kernels: none -> 58.1 us  [the longest x1 7.43 us: norm_last(): pl.pallas_call(functools.partial(norm_last_kernel, rows), out_shape=[stru...]
    dot_general x4 -> x0, matrix products: 38 us -> none  [the longest x2 27.7 us: contract_rows(): lax.dot_general(weights, columns, (((0,), (0,)), ((), ())), preferred_ele...]
    ppermute x2 -> x44, waiting for transfers between devices: 1.65 us -> 35.1 us  [the longest x21 27.5 us: step(): return lax.ppermute(value, ('grp', 'fsdp'), pairs)]
    ppermute x2 -> x44, starting transfers between devices: 4.07 us -> 36.3 us  [the longest x21 24.4 us: step(): return lax.ppermute(value, ('grp', 'fsdp'), pairs)]
    reduce_sum x4 -> x0, other arithmetic: 7.32 us -> none  [the longest x1 4.21 us: layer_norm(): centred = values - token_mean]
    unnamed x16 -> x56, local copies, waits for them, and re-layouts: 13.5 us -> 7.9 us
    dynamic_update_slice x1 -> x0, local copies, waits for them, and re-layouts: 4.54 us -> none  [local(): lax.dynamic_update_slice_in_dim(carried, own_rows, offset, 0)]
  transfers between devices with their start and end apart: 5 -> 44, of which waited for: 4 -> 13; matrix products, arithmetic and copies ran while one was open for 7% -> 5% of each run, Pallas kernels for 0% -> 35%
where the time goes in v3:
time: 145 us
  Pallas kernels  58.1 us (40%)
  starting transfers between devices  36.3 us (25%)
  waiting for transfers between devices  35.1 us (24%)
  local copies, waits for them, and re-layouts  9.52 us (7%)
  other arithmetic  4.26 us (3%)
    ppermute x21, waiting for transfers between devices, step(): return lax.ppermute(value, ('grp', 'fsdp'), pairs)  27.5 us
    ppermute x21, starting transfers between devices, step(): return lax.ppermute(value, ('grp', 'fsdp'), pairs)  24.4 us
    ppermute x6, starting transfers between devices, gather_dp(): lax.ppermute(value, 'dp', [(i, i ^ mask) for i in range(length)])  8.77 us
    unnamed x56, local copies, waits for them, and re-layouts  7.9 us
    pallas_call x1, Pallas kernels, norm_last(): pl.pallas_call(functools.partial(norm_last_kernel, rows), out_shape=[stru...  7.43 us
    pallas_call x1, Pallas kernels, zero_projection_grad(): pl.pallas_call(functools.partial(zero_grad_kernel, blocks, parts), out_sh...  7.36 us
    pallas_call x1, Pallas kernels, expand_first(): pl.pallas_call(expand_first_kernel, out_shape=(struct((features, tokens),...  6.61 us
    pallas_call x1, Pallas kernels, spread_first(): pl.pallas_call(functools.partial(spread_first_kernel, blocks), out_shape=...  6.56 us
  transfers between devices with their start and end apart: 44, of which 13 were waited for; matrix products, arithmetic and copies ran while one was open for 5% of the time, Pallas kernels for 35%

profile of v3, /device:TPU:0, one launch (start us, length us, event | category | flops | bytes accessed | tf_op | source)
XLA Modules:
  0.0 144.6 jit_solution(12909029055351316241)
XLA Ops:
  0.6 0.8 slice_reduce_fusion
  2.7 2.2 %copy.11 = f32[1,3,2432]{1,2,0:T(8,128)} copy(f32[1,3,2432]{2,0,1:T(1,128)} %param.9) | data formatting | bytes 58368 | tf_op args[1]
  5.0 6.6 %expand_first.1 = (bf16[2432,256]{1,0:T(8,128)(2,1)S(1)}, f32[2,256]{1,0:T(2,128)S(1)}, bf16[256,1024]{1,0:T(8,128)(2,1)S(1)}, f32[1024,256]{1,0:T(8,128)S(1)}) custom-call(bf16[1,2432,256]{2,1,0:T(8,128)(2,1)S(1)} %copy-done, f32[2432,3]{1,0:T(8,128)} %bitcast.34, bf16[1,2432,2432]{2,1,0:T(8,128)(2,1)} %weight.12), custom_call_target="tpu_custom_call" | custom-call | flops 1275068416 | bytes 7077888 | tf_op jit(solution)/shard_map/expand_first/pallas_call | solution.py:197
  11.7 1.4 upstream_terms.1
  13.1 3.0 %collective-permute-start.6 = (bf16[608,128]{1,0:T(8,128)(2,1)S(1)}, bf16[608,128]{1,0:T(8,128)(2,1)S(1)}, u32[]{:S(2)}, u32[]{:S(2)}) collective-permute-start(bf16[608,128]{1,0:T(8,128)(2,1)S(1)} %get-tuple-element.65.refs_4_), channel_id=1, source_target_pairs={{0,8},{4,12},{8,0},{12,4},{16,20},{20,16},{24,28},{28,24},{1,9},{5... | collective-permute-start | bytes 466952 | tf_op jit(solution)/shard_map/ppermute | solution.py:48
  16.1 1.5 %collective-permute-start.4 = (bf16[608,128]{1,0:T(8,128)(2,1)S(1)}, bf16[608,128]{1,0:T(8,128)(2,1)S(1)}, u32[]{:S(2)}, u32[]{:S(2)}) collective-permute-start(bf16[608,128]{1,0:T(8,128)(2,1)S(1)} %get-tuple-element.65.refs_4_), channel_id=1, source_target_pairs={{0,4},{4,0},{8,12},{12,8},{16,24},{20,28},{24,16},{28,20},{1,5},{5... | collective-permute-start | bytes 466952 | tf_op jit(solution)/shard_map/ppermute | solution.py:48
  18.2 1.5 %collective-permute-start.3 = (bf16[608,128]{1,0:T(8,128)(2,1)S(1)}, bf16[608,128]{1,0:T(8,128)(2,1)S(1)}, u32[]{:S(2)}, u32[]{:S(2)}) collective-permute-start(bf16[608,128]{1,0:T(8,128)(2,1)S(1)} %get-tuple-element.64), channel_id=1, source_target_pairs={{0,4},{4,0},{8,12},{12,8},{16,24},{20,28},{24,16},{28,20},{1,5},{5... | collective-permute-start | bytes 466952 | tf_op jit(solution)/shard_map/ppermute | solution.py:48
  19.7 6.0 %expand_rest.1 = (bf16[256,1408]{1,0:T(8,128)(2,1)S(1)}, f32[1408,256]{1,0:T(8,128)S(1)}) custom-call(bf16[2432,256]{1,0:T(8,128)(2,1)S(1)} %get-tuple-element.67.normed, bf16[1,2432,2432]{2,1,0:T(8,128)(2,1)} %weight.12), custom_call_target="tpu_custom_call" | custom-call | flops 1753219072 | bytes 9732096 | tf_op jit(solution)/shard_map/expand_rest/pallas_call | solution.py:221
  26.3 1.5 %collective-permute-start.7 = (bf16[608,128]{1,0:T(8,128)(2,1)S(1)}, bf16[608,128]{1,0:T(8,128)(2,1)S(1)}, u32[]{:S(2)}, u32[]{:S(2)}) collective-permute-start(bf16[608,128]{1,0:T(8,128)(2,1)S(1)} %collective-permute-done.4.refs_5_), channel_id=1, source_target_pairs={{0,8},{4,12},{8,0},{12,4},{16,20},{20,16},{24,28},{28,24},{1,9},{5... | collective-permute-start | bytes 466952 | tf_op jit(solution)/shard_map/ppermute | solution.py:48
  27.9 3.6 %collective-permute-start.19 = (bf16[608,256]{1,0:T(8,128)(2,1)S(1)}, bf16[608,256]{1,0:T(8,128)(2,1)S(1)}, u32[]{:S(2)}, u32[]{:S(2)}) collective-permute-start(bf16[608,256]{1,0:T(8,128)(2,1)S(1)} %get-tuple-element.84.refs_0_), channel_id=1, source_target_pairs={{0,3},{1,2},{2,1},{3,0},{4,7},{5,6},{6,5},{7,4},{8,11},{9,10},{10,... | collective-permute-start | bytes 933896 | tf_op jit(solution)/shard_map/ppermute | solution.py:61
  31.5 3.6 %contract_first.1.before = f32[1024,256]{1,0:T(8,128)S(1)} custom-call(bf16[256,1024]{1,0:T(8,128)(2,1)S(1)} %get-tuple-element.76.left, bf16[256,1408]{1,0:T(8,128)(2,1)S(1)} %get-tuple-element.68.right, bf16[1,2432,2432]{2,1,0:T(8,128)(2,1)} %weight.10), custom_call_target="tpu_custom_call" | custom-call | flops 1275068416 | bytes 7274496 | tf_op jit(solution)/shard_map/contract_first/pallas_call | solution.py:272
  35.1 1.0 copy-done.3
  36.9 0.8 broadcast_select_fusion.3
  39.1 5.8 %contract_last.1 = (bf16[608,256]{1,0:T(8,128)(2,1)S(1)}, bf16[608,256]{1,0:T(8,128)(2,1)S(1)}, f32[608,256]{1,0:T(8,128)S(1)}, f32[608,256]{1,0:T(8,128)S(1)}) custom-call(s32[9]{0:T(128)S(1)} %pad_add_fusion.order, bf16[256,1024]{1,0:T(8,128)(2,1)S(1)} %get-tuple-element.76.left, bf16[256,1408]{1,0:T(8,128)(2,1)S(1)} %get-tuple-element.68.right, ...), custom_call_target="tpu_custom_call" | custom-call | flops 1753219072 | bytes 13074432 | tf_op jit(solution)/shard_map/contract_last/pallas_call | solution.py:306
  44.9 1.3 collective-permute-start.8
  46.3 1.6 %collective-permute-start.12 = (bf16[608,128]{1,0:T(8,128)(2,1)S(1)}, bf16[608,128]{1,0:T(8,128)(2,1)S(1)}, u32[]{:S(2)}, u32[]{:S(2)}) collective-permute-start(bf16[608,128]{1,0:T(8,128)(2,1)S(1)} %collective-permute-done.10.refs_1_), channel_id=1, source_target_pairs={{0,8},{4,12},{8,0},{12,4},{16,20},{20,16},{24,28},{28,24},{1,9},{5... | collective-permute-start | bytes 466952 | tf_op jit(solution)/shard_map/ppermute | solution.py:48
  48.0 4.0 %collective-permute-done.12.refs_3_ = bf16[608,128]{1,0:T(8,128)(2,1)S(1)} collective-permute-done((bf16[608,128]{1,0:T(8,128)(2,1)S(1)}, bf16[608,128]{1,0:T(8,128)(2,1)S(1)}, u32[]{:S(2)}, u32[]{:S(2)}) %collective-permute-start.12) | collective-permute-done | bytes 155680 | tf_op jit(solution)/shard_map/ppermute | solution.py:48
  52.0 1.1 collective-permute-start.9
  53.1 3.7 %collective-permute-done.18.refs_2_ = bf16[608,256]{1,0:T(8,128)(2,1)S(1)} collective-permute-done((bf16[608,256]{1,0:T(8,128)(2,1)S(1)}, bf16[608,256]{1,0:T(8,128)(2,1)S(1)}, u32[]{:S(2)}, u32[]{:S(2)}) %collective-permute-start.18) | collective-permute-done | bytes 311328 | tf_op jit(solution)/shard_map/ppermute | solution.py:61
  58.9 0.9 collective-permute-done.14.refs_9_
  60.1 6.6 %spread_first.1 = (bf16[2432,256]{1,0:T(8,128)(2,1)}, bf16[256,1024]{1,0:T(8,128)(2,1)S(1)}) custom-call(s32[9]{0:T(128)S(1)} %pad_add_fusion.order, bf16[608,128]{1,0:T(8,128)(2,1)S(1)} %get-tuple-element.120.refs_0_, bf16[608,128]{1,0:T(8,128)(2,1)S(1)} %collective-permute-done.10.refs_1_, bf16[608,128]{1,0:T(8,128)(2,1)S(1)} %collective-permute-done.11.refs_2_, ...), custom_call_target="tpu_custom_call" | custom-call | flops 1275068416 | bytes 9043968 | tf_op jit(solution)/shard_map/spread_first/pallas_call | solution.py:364
  66.9 1.4 collective-permute-start.20
  69.2 5.5 %spread_rest.1.right = bf16[256,1408]{1,0:T(8,128)(2,1)S(1)} custom-call(bf16[2432,256]{1,0:T(8,128)(2,1)S(1)} %copy-done.5, f32[1408,256]{1,0:T(8,128)S(1)} %get-tuple-element.92.slope, bf16[1,2432,2432]{2,1,0:T(8,128)(2,1)} %weight.10), custom_call_target="tpu_custom_call" | custom-call | flops 1753219072 | bytes 10256384 | tf_op jit(solution)/shard_map/spread_rest/pallas_call | solution.py:387
  75.0 1.4 collective-permute-done.21
  76.4 1.0 collective-permute-start.22
  77.4 2.5 %collective-permute-start.36 = (bf16[608,128]{1,0:T(8,128)(2,1)S(1)}, bf16[608,128]{1,0:T(8,128)(2,1)S(1)}, u32[]{:S(2)}, u32[]{:S(2)}) collective-permute-start(bf16[608,128]{1,0:T(8,128)(2,1)S(1)} %slice_select_fusion.refs_0_.refs_4_), channel_id=1, source_target_pairs={{0,3},{1,2},{2,1},{3,0},{4,7},{5,6},{6,5},{7,4},{8,11},{9,10},{10,... | collective-permute-start | bytes 466952 | tf_op jit(solution)/shard_map/ppermute | solution.py:61
  79.9 1.9 %collective-permute-start.34 = (bf16[608,128]{1,0:T(8,128)(2,1)S(1)}, bf16[608,128]{1,0:T(8,128)(2,1)S(1)}, u32[]{:S(2)}, u32[]{:S(2)}) collective-permute-start(bf16[608,128]{1,0:T(8,128)(2,1)S(1)} %slice_select_fusion.refs_0_.refs_4_), channel_id=1, source_target_pairs={{0,1},{1,0},{2,3},{3,2},{4,5},{5,4},{6,7},{7,6},{8,9},{9,8},{10,11... | collective-permute-start | bytes 466952 | tf_op jit(solution)/shard_map/ppermute | solution.py:61
  82.5 4.9 %norm_first.1 = (f32[1024,256]{1,0:T(8,128)S(1)}, f32[2,256]{1,0:T(2,128)S(1)}) custom-call(bf16[256,1024]{1,0:T(8,128)(2,1)S(1)} %get-tuple-element.98.left, bf16[256,1408]{1,0:T(8,128)(2,1)S(1)} %spread_rest.1.right, bf16[1,2432,256]{2,1,0:T(8,128)(2,1)S(1)} %copy-done, f32[2,256]{1,0:T(2,128)S(1)} %get-tuple-element.95.stats, f32[2432,3]{1,0:T(8,128)} %bitcast.36, ...), custom_call_target="tpu_custom_call" | custom-call | flops 1275068416 | bytes 7798784 | tf_op jit(solution)/shard_map/norm_first/pallas_call | solution.py:430
  87.5 1.0 copy-done.6
  88.5 1.3 collective-permute-start.24
  89.8 7.4 %norm_last.1 = (bf16[624,256]{1,0:T(8,128)(2,1)}, bf16[624,256]{1,0:T(8,128)(2,1)}, f32[608,256]{1,0:T(8,128)S(1)}, f32[608,256]{1,0:T(8,128)S(1)}, f32[2,256]{1,0:T(2,128)S(1)}) custom-call(s32[9]{0:T(128)S(1)} %pad_add_fusion.order, bf16[256,1024]{1,0:T(8,128)(2,1)S(1)} %get-tuple-element.98.left, bf16[256,1408]{1,0:T(8,128)(2,1)S(1)} %spread_rest.1.right, ...), custom_call_target="tpu_custom_call" | custom-call | flops 1753219072 | bytes 13074432 | tf_op jit(solution)/shard_map/norm_last/pallas_call | solution.py:468
  97.2 1.5 %residual_rows.1 = f32[608,128]{1,0:T(8,128)S(1)} custom-call(s32[9]{0:T(128)S(1)} %pad_add_fusion.order, bf16[608,2432]{1,0:T(8,128)(2,1)S(1)} %copy-done.2, bf16[608,128]{1,0:T(8,128)(2,1)S(1)} %slice_select_fusion.refs_0_.refs_4_, bf16[608,128]{1,0:T(8,128)(2,1)S(1)} %collective-permute-done.22.refs_1_.refs_5_, ...), custom_call_target="tpu_custom_call" | custom-call | flops 378535936 | bytes 4202496 | tf_op jit(solution)/shard_map/residual_rows/pallas_call | solution.py:561
  98.9 1.2 collective-permute-start.37
  100.1 0.9 collective-permute-start.28
  101.0 1.1 collective-permute-start.27
  102.1 8.9 %collective-permute-done.28.refs_1_ = bf16[624,256]{1,0:T(8,128)(2,1)} collective-permute-done((bf16[624,256]{1,0:T(8,128)(2,1)}, bf16[624,256]{1,0:T(8,128)(2,1)}, u32[]{:S(2)}, u32[]{:S(2)}) %collective-permute-start.28) | collective-permute-done | bytes 319520 | tf_op jit(solution)/shard_map/ppermute | solution.py:48
  111.1 3.4 %collective-permute-done.27.refs_0_ = bf16[624,256]{1,0:T(8,128)(2,1)} collective-permute-done((bf16[624,256]{1,0:T(8,128)(2,1)}, bf16[624,256]{1,0:T(8,128)(2,1)}, u32[]{:S(2)}, u32[]{:S(2)}) %collective-permute-start.27) | collective-permute-done | bytes 319520 | tf_op jit(solution)/shard_map/ppermute | solution.py:48
  114.5 1.1 copy-done.10
  115.6 1.1 copy-done.12
  116.7 1.3 fold.1
  117.9 0.8 collective-permute-start.29
  119.3 1.3 collective-permute-start.38
  121.4 1.0 fusion.8
  122.3 2.7 %collective-permute-done.29 = bf16[624,256]{1,0:T(8,128)(2,1)S(1)} collective-permute-done((bf16[624,256]{1,0:T(8,128)(2,1)S(1)}, bf16[624,256]{1,0:T(8,128)(2,1)S(1)}, u32[]{:S(2)}, u32[]{:S(2)}) %collective-permute-start.29) | collective-permute-done | bytes 319520 | tf_op jit(solution)/shard_map/ppermute | solution.py:48
  126.5 3.5 %collective-permute-done.38.refs_14_ = bf16[3,608,128]{2,1,0:T(8,128)(2,1)S(1)} collective-permute-done((bf16[3,608,128]{2,1,0:T(8,128)(2,1)S(1)}, bf16[3,608,128]{2,1,0:T(8,128)(2,1)S(1)}, u32[]{:S(2)}, u32[]{:S(2)}) %collective-permute-start.38) | collective-permute-done | bytes 466976 | tf_op jit(solution)/shard_map/ppermute | solution.py:48
  130.0 5.0 %collective-permute-done.39.refs_15_ = bf16[3,608,128]{2,1,0:T(8,128)(2,1)S(1)} collective-permute-done((bf16[3,608,128]{2,1,0:T(8,128)(2,1)}, bf16[3,608,128]{2,1,0:T(8,128)(2,1)S(1)}, u32[]{:S(2)}, u32[]{:S(2)}) %collective-permute-start.39) | collective-permute-done | bytes 466976 | tf_op jit(solution)/shard_map/ppermute | solution.py:48
  135.6 1.1 fusion.5
  137.1 7.4 %zero_projection_grad.1 = f32[608,2432]{1,0:T(8,128)} custom-call(s32[9]{0:T(128)S(1)} %pad_add_fusion.order, s32[4]{0:T(128)S(1)} %iota_xor_fusion.dp_order, bf16[608,256]{1,0:T(8,128)(2,1)S(1)} %copy-done.14, bf16[608,256]{1,0:T(8,128)(2,1)S(1)} %copy-done.20, bf16[608,256]{1,0:T(8,128)(2,1)S(1)} %copy-done.18, bf16[608,256]{1,0:T(8,128)(2,1)S(1)} %copy-done.16, ...), custom_call_target="tpu_custom_call" | custom-call | flops 3028287488 | bytes 12140544 | tf_op jit(solution)/shard_map/zero_projection_grad/pallas_call | solution.py:602
  (130 shorter events, 13.1 us)
Async XLA Ops:
  1.5 26.4 %collective-permute-start = (f32[2432]{0:T(1024)S(1)}, f32[2432]{0:T(1024)S(1)}, u32[]{:S(2)}, u32[]{:S(2)}) collective-permute-start(f32[2432]{0:T(1024)S(1)} %slice_reduce_fusion), channel_id=1, source_target_pairs={{0,16},{16,0},{1,17},{17,1},{2,18},{18,2},{3,19},{19,3},{4,20},{20... | collective-permute-start | bytes 29192 | tf_op jit(solution)/shard_map/ppermute | solution.py:36
  2.0 9.7 %collective-permute-start.1 = (bf16[608,256]{1,0:T(8,128)(2,1)}, bf16[608,256]{1,0:T(8,128)(2,1)S(1)}, u32[]{:S(2)}, u32[]{:S(2)}) collective-permute-start(bf16[608,256]{1,0:T(8,128)(2,1)} %bitcast.32), channel_id=1, source_target_pairs={{0,16},{16,0},{1,17},{17,1},{2,18},{18,2},{3,19},{19,3},{4,20},{20... | collective-permute-start | bytes 933896 | tf_op jit(solution)/shard_map/ppermute | solution.py:36
  13.1 23.0 %copy-start.13 = (bf16[608,256]{1,0:T(8,128)(2,1)}, bf16[608,256]{1,0:T(8,128)(2,1)S(1)}, u32[]{:S(2)}) copy-start(bf16[608,256]{1,0:T(8,128)(2,1)S(1)} %get-tuple-element.84.refs_0_) | copy-start | bytes 933892
  13.1 23.0 %collective-permute-start.6 = (bf16[608,128]{1,0:T(8,128)(2,1)S(1)}, bf16[608,128]{1,0:T(8,128)(2,1)S(1)}, u32[]{:S(2)}, u32[]{:S(2)}) collective-permute-start(bf16[608,128]{1,0:T(8,128)(2,1)S(1)} %get-tuple-element.65.refs_4_), channel_id=1, source_target_pairs={{0,8},{4,12},{8,0},{12,4},{16,20},{20,16},{24,28},{28,24},{1,9},{5... | collective-permute-start | bytes 466952 | tf_op jit(solution)/shard_map/ppermute | solution.py:48
  16.1 9.6 %collective-permute-start.4 = (bf16[608,128]{1,0:T(8,128)(2,1)S(1)}, bf16[608,128]{1,0:T(8,128)(2,1)S(1)}, u32[]{:S(2)}, u32[]{:S(2)}) collective-permute-start(bf16[608,128]{1,0:T(8,128)(2,1)S(1)} %get-tuple-element.65.refs_4_), channel_id=1, source_target_pairs={{0,4},{4,0},{8,12},{12,8},{16,24},{20,28},{24,16},{28,20},{1,5},{5... | collective-permute-start | bytes 466952 | tf_op jit(solution)/shard_map/ppermute | solution.py:48
  17.7 8.0 %collective-permute-start.2 = (bf16[608,128]{1,0:T(8,128)(2,1)S(1)}, bf16[608,128]{1,0:T(8,128)(2,1)S(1)}, u32[]{:S(2)}, u32[]{:S(2)}) collective-permute-start(bf16[608,128]{1,0:T(8,128)(2,1)S(1)} %get-tuple-element.63), channel_id=1, source_target_pairs={{0,4},{4,0},{8,12},{12,8},{16,24},{20,28},{24,16},{28,20},{1,5},{5... | collective-permute-start | bytes 466952 | tf_op jit(solution)/shard_map/ppermute | solution.py:48
  18.2 7.5 %collective-permute-start.3 = (bf16[608,128]{1,0:T(8,128)(2,1)S(1)}, bf16[608,128]{1,0:T(8,128)(2,1)S(1)}, u32[]{:S(2)}, u32[]{:S(2)}) collective-permute-start(bf16[608,128]{1,0:T(8,128)(2,1)S(1)} %get-tuple-element.64), channel_id=1, source_target_pairs={{0,4},{4,0},{8,12},{12,8},{16,24},{20,28},{24,16},{28,20},{1,5},{5... | collective-permute-start | bytes 466952 | tf_op jit(solution)/shard_map/ppermute | solution.py:48
  25.8 11.2 %collective-permute-start.5 = (bf16[608,128]{1,0:T(8,128)(2,1)S(1)}, bf16[608,128]{1,0:T(8,128)(2,1)S(1)}, u32[]{:S(2)}, u32[]{:S(2)}) collective-permute-start(bf16[608,128]{1,0:T(8,128)(2,1)S(1)} %add_convert_fusion.1), channel_id=1, source_target_pairs={{0,8},{4,12},{8,0},{12,4},{16,20},{20,16},{24,28},{28,24},{1,9},{5... | collective-permute-start | bytes 466952 | tf_op jit(solution)/shard_map/ppermute | solution.py:48
  26.3 10.6 %collective-permute-start.7 = (bf16[608,128]{1,0:T(8,128)(2,1)S(1)}, bf16[608,128]{1,0:T(8,128)(2,1)S(1)}, u32[]{:S(2)}, u32[]{:S(2)}) collective-permute-start(bf16[608,128]{1,0:T(8,128)(2,1)S(1)} %collective-permute-done.4.refs_5_), channel_id=1, source_target_pairs={{0,8},{4,12},{8,0},{12,4},{16,20},{20,16},{24,28},{28,24},{1,9},{5... | collective-permute-start | bytes 466952 | tf_op jit(solution)/shard_map/ppermute | solution.py:48
  27.9 20.0 %collective-permute-start.19 = (bf16[608,256]{1,0:T(8,128)(2,1)S(1)}, bf16[608,256]{1,0:T(8,128)(2,1)S(1)}, u32[]{:S(2)}, u32[]{:S(2)}) collective-permute-start(bf16[608,256]{1,0:T(8,128)(2,1)S(1)} %get-tuple-element.84.refs_0_), channel_id=1, source_target_pairs={{0,3},{1,2},{2,1},{3,0},{4,7},{5,6},{6,5},{7,4},{8,11},{9,10},{10,... | collective-permute-start | bytes 933896 | tf_op jit(solution)/shard_map/ppermute | solution.py:61
  31.5 25.3 %collective-permute-start.18 = (bf16[608,256]{1,0:T(8,128)(2,1)S(1)}, bf16[608,256]{1,0:T(8,128)(2,1)S(1)}, u32[]{:S(2)}, u32[]{:S(2)}) collective-permute-start(bf16[608,256]{1,0:T(8,128)(2,1)S(1)} %get-tuple-element.84.refs_0_), channel_id=1, source_target_pairs={{0,2},{1,3},{2,0},{3,1},{4,6},{5,7},{6,4},{7,5},{8,10},{9,11},{10,... | collective-permute-start | bytes 933896 | tf_op jit(solution)/shard_map/ppermute | solution.py:61
  36.1 21.4 %collective-permute-start.17 = (bf16[608,256]{1,0:T(8,128)(2,1)S(1)}, bf16[608,256]{1,0:T(8,128)(2,1)S(1)}, u32[]{:S(2)}, u32[]{:S(2)}) collective-permute-start(bf16[608,256]{1,0:T(8,128)(2,1)S(1)} %get-tuple-element.84.refs_0_), channel_id=1, source_target_pairs={{0,1},{1,0},{2,3},{3,2},{4,5},{5,4},{6,7},{7,6},{8,9},{9,8},{10,11... | collective-permute-start | bytes 933896 | tf_op jit(solution)/shard_map/ppermute | solution.py:61
  37.8 8.5 %collective-permute-start.11 = (bf16[608,128]{1,0:T(8,128)(2,1)S(1)}, bf16[608,128]{1,0:T(8,128)(2,1)S(1)}, u32[]{:S(2)}, u32[]{:S(2)}) collective-permute-start(bf16[608,128]{1,0:T(8,128)(2,1)S(1)} %get-tuple-element.120.refs_0_), channel_id=1, source_target_pairs={{0,8},{4,12},{8,0},{12,4},{16,20},{20,16},{24,28},{28,24},{1,9},{5... | collective-permute-start | bytes 466952 | tf_op jit(solution)/shard_map/ppermute | solution.py:48
  38.3 6.6 %collective-permute-start.10 = (bf16[608,128]{1,0:T(8,128)(2,1)S(1)}, bf16[608,128]{1,0:T(8,128)(2,1)S(1)}, u32[]{:S(2)}, u32[]{:S(2)}) collective-permute-start(bf16[608,128]{1,0:T(8,128)(2,1)S(1)} %get-tuple-element.120.refs_0_), channel_id=1, source_target_pairs={{0,4},{4,0},{8,12},{12,8},{16,24},{20,28},{24,16},{28,20},{1,5},{5... | collective-permute-start | bytes 466952 | tf_op jit(solution)/shard_map/ppermute | solution.py:48
  44.9 21.8 %collective-permute-start.8 = (bf16[608,256]{1,0:T(8,128)(2,1)S(1)}, bf16[608,256]{1,0:T(8,128)(2,1)S(1)}, u32[]{:S(2)}, u32[]{:S(2)}) collective-permute-start(bf16[608,256]{1,0:T(8,128)(2,1)S(1)} %get-tuple-element.78), channel_id=1, source_target_pairs={{0,4},{4,0},{8,12},{12,8},{16,24},{20,28},{24,16},{28,20},{1,5},{5... | collective-permute-start | bytes 933896 | tf_op jit(solution)/shard_map/ppermute | solution.py:48
  46.3 5.8 %collective-permute-start.12 = (bf16[608,128]{1,0:T(8,128)(2,1)S(1)}, bf16[608,128]{1,0:T(8,128)(2,1)S(1)}, u32[]{:S(2)}, u32[]{:S(2)}) collective-permute-start(bf16[608,128]{1,0:T(8,128)(2,1)S(1)} %collective-permute-done.10.refs_1_), channel_id=1, source_target_pairs={{0,8},{4,12},{8,0},{12,4},{16,20},{20,16},{24,28},{28,24},{1,9},{5... | collective-permute-start | bytes 466952 | tf_op jit(solution)/shard_map/ppermute | solution.py:48
  47.9 18.8 %copy-start.15 = (bf16[608,256]{1,0:T(8,128)(2,1)}, bf16[608,256]{1,0:T(8,128)(2,1)S(1)}, u32[]{:S(2)}) copy-start(bf16[608,256]{1,0:T(8,128)(2,1)S(1)} %collective-permute-done.19.refs_3_) | copy-start | bytes 933892
  47.9 10.8 %collective-permute-start.13 = (bf16[608,128]{1,0:T(8,128)(2,1)S(1)}, bf16[608,128]{1,0:T(8,128)(2,1)S(1)}, u32[]{:S(2)}, u32[]{:S(2)}) collective-permute-start(bf16[608,128]{1,0:T(8,128)(2,1)S(1)} %get-tuple-element.119), channel_id=1, source_target_pairs={{0,16},{16,0},{1,17},{17,1},{2,18},{18,2},{3,19},{19,3},{4,20},{20... | collective-permute-start | bytes 466952 | tf_op jit(solution)/shard_map/ppermute | solution.py:36
  52.0 14.7 %collective-permute-start.9 = (bf16[608,256]{1,0:T(8,128)(2,1)S(1)}, bf16[608,256]{1,0:T(8,128)(2,1)S(1)}, u32[]{:S(2)}, u32[]{:S(2)}) collective-permute-start(bf16[608,256]{1,0:T(8,128)(2,1)S(1)} %get-tuple-element.79), channel_id=1, source_target_pairs={{0,4},{4,0},{8,12},{12,8},{16,24},{20,28},{24,16},{28,20},{1,5},{5... | collective-permute-start | bytes 933896 | tf_op jit(solution)/shard_map/ppermute | solution.py:48
  57.5 1.4 collective-permute-start.15
  58.3 1.5 %collective-permute-start.14 = (bf16[608,128]{1,0:T(8,128)(2,1)S(1)}, bf16[608,128]{1,0:T(8,128)(2,1)S(1)}, u32[]{:S(2)}, u32[]{:S(2)}) collective-permute-start(bf16[608,128]{1,0:T(8,128)(2,1)S(1)} %broadcast_select_fusion.2), channel_id=1, source_target_pairs={{0,16},{16,0},{1,17},{17,1},{2,18},{18,2},{3,19},{19,3},{4,20},{20... | collective-permute-start | bytes 466952 | tf_op jit(solution)/shard_map/ppermute | solution.py:36
  58.8 1.4 collective-permute-start.16
  66.9 7.8 %collective-permute-start.20 = (bf16[608,256]{1,0:T(8,128)(2,1)S(1)}, bf16[608,256]{1,0:T(8,128)(2,1)S(1)}, u32[]{:S(2)}, u32[]{:S(2)}) collective-permute-start(bf16[608,256]{1,0:T(8,128)(2,1)S(1)} %add_convert_fusion), channel_id=1, source_target_pairs={{0,8},{4,12},{8,0},{12,4},{16,20},{20,16},{24,28},{28,24},{1,9},{5... | collective-permute-start | bytes 933896 | tf_op jit(solution)/shard_map/ppermute | solution.py:48
  75.0 1.4 %collective-permute-start.21 = (bf16[608,128]{1,0:T(8,128)(2,1)S(1)}, bf16[608,128]{1,0:T(8,128)(2,1)S(1)}, u32[]{:S(2)}, u32[]{:S(2)}) collective-permute-start(bf16[608,128]{1,0:T(8,128)(2,1)S(1)} %slice.71), channel_id=1, source_target_pairs={{0,16},{16,0},{1,17},{17,1},{2,18},{18,2},{3,19},{19,3},{4,20},{20... | collective-permute-start | bytes 466952 | tf_op jit(solution)/shard_map/ppermute | solution.py:36
  76.4 12.0 %collective-permute-start.22 = (bf16[608,128]{1,0:T(8,128)(2,1)S(1)}, bf16[608,128]{1,0:T(8,128)(2,1)S(1)}, u32[]{:S(2)}, u32[]{:S(2)}) collective-permute-start(bf16[608,128]{1,0:T(8,128)(2,1)S(1)} %slice_select_fusion.refs_0_.refs_4_), channel_id=1, source_target_pairs={{0,4},{4,0},{8,12},{12,8},{16,24},{20,28},{24,16},{28,20},{1,5},{5... | collective-permute-start | bytes 466952 | tf_op jit(solution)/shard_map/ppermute | solution.py:48
  77.4 21.4 %collective-permute-start.36 = (bf16[608,128]{1,0:T(8,128)(2,1)S(1)}, bf16[608,128]{1,0:T(8,128)(2,1)S(1)}, u32[]{:S(2)}, u32[]{:S(2)}) collective-permute-start(bf16[608,128]{1,0:T(8,128)(2,1)S(1)} %slice_select_fusion.refs_0_.refs_4_), channel_id=1, source_target_pairs={{0,3},{1,2},{2,1},{3,0},{4,7},{5,6},{6,5},{7,4},{8,11},{9,10},{10,... | collective-permute-start | bytes 466952 | tf_op jit(solution)/shard_map/ppermute | solution.py:61
  79.9 18.9 %collective-permute-start.35 = (bf16[608,128]{1,0:T(8,128)(2,1)S(1)}, bf16[608,128]{1,0:T(8,128)(2,1)S(1)}, u32[]{:S(2)}, u32[]{:S(2)}) collective-permute-start(bf16[608,128]{1,0:T(8,128)(2,1)S(1)} %slice_select_fusion.refs_0_.refs_4_), channel_id=1, source_target_pairs={{0,2},{1,3},{2,0},{3,1},{4,6},{5,7},{6,4},{7,5},{8,10},{9,11},{10,... | collective-permute-start | bytes 466952 | tf_op jit(solution)/shard_map/ppermute | solution.py:61
  79.9 18.9 %collective-permute-start.34 = (bf16[608,128]{1,0:T(8,128)(2,1)S(1)}, bf16[608,128]{1,0:T(8,128)(2,1)S(1)}, u32[]{:S(2)}, u32[]{:S(2)}) collective-permute-start(bf16[608,128]{1,0:T(8,128)(2,1)S(1)} %slice_select_fusion.refs_0_.refs_4_), channel_id=1, source_target_pairs={{0,1},{1,0},{2,3},{3,2},{4,5},{5,4},{6,7},{7,6},{8,9},{9,8},{10,11... | collective-permute-start | bytes 466952 | tf_op jit(solution)/shard_map/ppermute | solution.py:61
  81.8 15.4 %collective-permute-start.23 = (bf16[608,128]{1,0:T(8,128)(2,1)S(1)}, bf16[608,128]{1,0:T(8,128)(2,1)S(1)}, u32[]{:S(2)}, u32[]{:S(2)}) collective-permute-start(bf16[608,128]{1,0:T(8,128)(2,1)S(1)} %slice_select_fusion.refs_0_.refs_4_), channel_id=1, source_target_pairs={{0,8},{4,12},{8,0},{12,4},{16,20},{20,16},{24,28},{28,24},{1,9},{5... | collective-permute-start | bytes 466952 | tf_op jit(solution)/shard_map/ppermute | solution.py:48
  88.5 8.7 %collective-permute-start.24 = (bf16[608,128]{1,0:T(8,128)(2,1)S(1)}, bf16[608,128]{1,0:T(8,128)(2,1)S(1)}, u32[]{:S(2)}, u32[]{:S(2)}) collective-permute-start(bf16[608,128]{1,0:T(8,128)(2,1)S(1)} %collective-permute-done.22.refs_1_.refs_5_), channel_id=1, source_target_pairs={{0,8},{4,12},{8,0},{12,4},{16,20},{20,16},{24,28},{28,24},{1,9},{5... | collective-permute-start | bytes 466952 | tf_op jit(solution)/shard_map/ppermute | solution.py:48
  98.8 22.5 %copy-start.1 = (bf16[1,2432,256]{2,1,0:T(8,128)(2,1)S(1)}, bf16[1,2432,256]{2,1,0:T(8,128)(2,1)}, u32[]{:S(2)}) copy-start(bf16[1,2432,256]{2,1,0:T(8,128)(2,1)} %acts.5) | copy-start | bytes 3735556
  98.9 21.7 %collective-permute-start.37 = (bf16[3,608,128]{2,1,0:T(8,128)(2,1)S(1)}, bf16[3,608,128]{2,1,0:T(8,128)(2,1)}, u32[]{:S(2)}, u32[]{:S(2)}) collective-permute-start(bf16[3,608,128]{2,1,0:T(8,128)(2,1)S(1)} %pad_maximum_fusion.refs_12_), channel_id=1, source_target_pairs={{0,4},{4,0},{8,12},{12,8},{16,24},{20,28},{24,16},{28,20},{1,5},{5... | collective-permute-start | bytes 1400840 | tf_op jit(solution)/shard_map/ppermute | solution.py:48
  100.1 11.0 %collective-permute-start.28 = (bf16[624,256]{1,0:T(8,128)(2,1)}, bf16[624,256]{1,0:T(8,128)(2,1)}, u32[]{:S(2)}, u32[]{:S(2)}) collective-permute-start(bf16[624,256]{1,0:T(8,128)(2,1)} %get-tuple-element.107), channel_id=1, source_target_pairs={{0,4},{4,0},{8,12},{12,8},{16,24},{20,28},{24,16},{28,20},{1,5},{5... | collective-permute-start | bytes 958472 | tf_op jit(solution)/shard_map/ppermute | solution.py:48
  101.0 13.5 %collective-permute-start.27 = (bf16[624,256]{1,0:T(8,128)(2,1)}, bf16[624,256]{1,0:T(8,128)(2,1)}, u32[]{:S(2)}, u32[]{:S(2)}) collective-permute-start(bf16[624,256]{1,0:T(8,128)(2,1)} %get-tuple-element.100), channel_id=1, source_target_pairs={{0,4},{4,0},{8,12},{12,8},{16,24},{20,28},{24,16},{28,20},{1,5},{5... | collective-permute-start | bytes 958472 | tf_op jit(solution)/shard_map/ppermute | solution.py:48
  102.1 17.2 %collective-permute-start.25 = (f32[608,128]{1,0:T(8,128)S(1)}, f32[608,128]{1,0:T(8,128)S(1)}, u32[]{:S(2)}, u32[]{:S(2)}) collective-permute-start(f32[608,128]{1,0:T(8,128)S(1)} %residual_rows.1), channel_id=1, source_target_pairs={{0,16},{16,0},{1,17},{17,1},{2,18},{18,2},{3,19},{19,3},{4,20},{20... | collective-permute-start | bytes 933896 | tf_op jit(solution)/shard_map/ppermute | solution.py:36
  117.9 7.1 %collective-permute-start.29 = (bf16[624,256]{1,0:T(8,128)(2,1)S(1)}, bf16[624,256]{1,0:T(8,128)(2,1)S(1)}, u32[]{:S(2)}, u32[]{:S(2)}) collective-permute-start(bf16[624,256]{1,0:T(8,128)(2,1)S(1)} %get-tuple-element.112), channel_id=1, source_target_pairs={{0,8},{4,12},{8,0},{12,4},{16,20},{20,16},{24,28},{28,24},{1,9},{5... | collective-permute-start | bytes 958472 | tf_op jit(solution)/shard_map/ppermute | solution.py:48
  118.8 16.3 %copy-start.8 = (bf16[608,128]{1,0:T(8,128)(2,1)S(1)}, bf16[608,128]{1,0:T(8,128)(2,1)}, u32[]{:S(2)}) copy-start(bf16[608,128]{1,0:T(8,128)(2,1)} %copy-done.7) | copy-start | bytes 466948
  118.8 6.2 %collective-permute-start.26 = (f32[608,128]{1,0:T(8,128)S(1)}, f32[608,128]{1,0:T(8,128)S(1)}, u32[]{:S(2)}, u32[]{:S(2)}) collective-permute-start(f32[608,128]{1,0:T(8,128)S(1)} %copy-done.21), channel_id=1, source_target_pairs={{0,16},{16,0},{1,17},{17,1},{2,18},{18,2},{3,19},{19,3},{4,20},{20... | collective-permute-start | bytes 933896 | tf_op jit(solution)/shard_map/ppermute | solution.py:36
  118.8 6.7 %collective-permute-start.30 = (bf16[608,128]{1,0:T(8,128)(2,1)S(1)}, bf16[608,128]{1,0:T(8,128)(2,1)S(1)}, u32[]{:S(2)}, u32[]{:S(2)}) collective-permute-start(bf16[608,128]{1,0:T(8,128)(2,1)S(1)} %slice_select_fusion.refs_0_.refs_4_), channel_id=1, source_target_pairs={{0,16},{16,0},{1,17},{17,1},{2,18},{18,2},{3,19},{19,3},{4,20},{20... | collective-permute-start | bytes 466952 | tf_op jit(solution)/shard_map/ppermute | solution.py:36
  119.3 10.7 %collective-permute-start.38 = (bf16[3,608,128]{2,1,0:T(8,128)(2,1)S(1)}, bf16[3,608,128]{2,1,0:T(8,128)(2,1)S(1)}, u32[]{:S(2)}, u32[]{:S(2)}) collective-permute-start(bf16[3,608,128]{2,1,0:T(8,128)(2,1)S(1)} %pad_maximum_fusion.refs_12_), channel_id=1, source_target_pairs={{0,8},{4,12},{8,0},{12,4},{16,20},{20,16},{24,28},{28,24},{1,9},{5... | collective-permute-start | bytes 1400840 | tf_op jit(solution)/shard_map/ppermute | solution.py:48
  120.6 14.4 %collective-permute-start.39 = (bf16[3,608,128]{2,1,0:T(8,128)(2,1)}, bf16[3,608,128]{2,1,0:T(8,128)(2,1)S(1)}, u32[]{:S(2)}, u32[]{:S(2)}) collective-permute-start(bf16[3,608,128]{2,1,0:T(8,128)(2,1)} %collective-permute-done.37.refs_13_), channel_id=1, source_target_pairs={{0,8},{4,12},{8,0},{12,4},{16,20},{20,16},{24,28},{28,24},{1,9},{5... | collective-permute-start | bytes 1400840 | tf_op jit(solution)/shard_map/ppermute | solution.py:48
  125.0 1.4 collective-permute-start.31
  125.0 10.0 %collective-permute-start.32 = (bf16[608,128]{1,0:T(8,128)(2,1)S(1)}, bf16[608,128]{1,0:T(8,128)(2,1)S(1)}, u32[]{:S(2)}, u32[]{:S(2)}) collective-permute-start(bf16[608,128]{1,0:T(8,128)(2,1)S(1)} %collective-permute-done.23.refs_2_.refs_6_), channel_id=1, source_target_pairs={{0,16},{16,0},{1,17},{17,1},{2,18},{18,2},{3,19},{19,3},{4,20},{20... | collective-permute-start | bytes 466952 | tf_op jit(solution)/shard_map/ppermute | solution.py:36
  125.5 11.5 %collective-permute-start.40 = (bf16[3,608,128]{2,1,0:T(8,128)(2,1)S(1)}, bf16[3,608,128]{2,1,0:T(8,128)(2,1)S(1)}, u32[]{:S(2)}, u32[]{:S(2)}) collective-permute-start(bf16[3,608,128]{2,1,0:T(8,128)(2,1)S(1)} %pad_maximum_fusion.refs_12_), channel_id=1, source_target_pairs={{0,16},{16,0},{1,17},{17,1},{2,18},{18,2},{3,19},{19,3},{4,20},{20... | collective-permute-start | bytes 1400840 | tf_op jit(solution)/shard_map/ppermute | solution.py:36
  126.4 10.7 %collective-permute-start.41 = (bf16[3,608,128]{2,1,0:T(8,128)(2,1)}, bf16[3,608,128]{2,1,0:T(8,128)(2,1)S(1)}, u32[]{:S(2)}, u32[]{:S(2)}) collective-permute-start(bf16[3,608,128]{2,1,0:T(8,128)(2,1)} %collective-permute-done.37.refs_13_), channel_id=1, source_target_pairs={{0,16},{16,0},{1,17},{17,1},{2,18},{18,2},{3,19},{19,3},{4,20},{20... | collective-permute-start | bytes 1400840 | tf_op jit(solution)/shard_map/ppermute | solution.py:36
  130.0 7.1 %collective-permute-start.42 = (bf16[3,608,128]{2,1,0:T(8,128)(2,1)S(1)}, bf16[3,608,128]{2,1,0:T(8,128)(2,1)S(1)}, u32[]{:S(2)}, u32[]{:S(2)}) collective-permute-start(bf16[3,608,128]{2,1,0:T(8,128)(2,1)S(1)} %collective-permute-done.38.refs_14_), channel_id=1, source_target_pairs={{0,16},{16,0},{1,17},{17,1},{2,18},{18,2},{3,19},{19,3},{4,20},{20... | collective-permute-start | bytes 1400840 | tf_op jit(solution)/shard_map/ppermute | solution.py:36
  135.0 2.1 %collective-permute-start.43 = (bf16[3,608,128]{2,1,0:T(8,128)(2,1)S(1)}, bf16[3,608,128]{2,1,0:T(8,128)(2,1)S(1)}, u32[]{:S(2)}, u32[]{:S(2)}) collective-permute-start(bf16[3,608,128]{2,1,0:T(8,128)(2,1)S(1)} %collective-permute-done.39.refs_15_), channel_id=1, source_target_pairs={{0,16},{16,0},{1,17},{17,1},{2,18},{18,2},{3,19},{19,3},{4,20},{20... | collective-permute-start | bytes 1400840 | tf_op jit(solution)/shard_map/ppermute | solution.py:36
  135.0 2.0 %collective-permute-start.33 = (bf16[608,128]{1,0:T(8,128)(2,1)S(1)}, bf16[608,128]{1,0:T(8,128)(2,1)S(1)}, u32[]{:S(2)}, u32[]{:S(2)}) collective-permute-start(bf16[608,128]{1,0:T(8,128)(2,1)S(1)} %copy-done.8), channel_id=1, source_target_pairs={{0,16},{16,0},{1,17},{17,1},{2,18},{18,2},{3,19},{19,3},{4,20},{20... | collective-permute-start | bytes 466952 | tf_op jit(solution)/shard_map/ppermute | solution.py:36
  (23 other events, 57.6 us)

commit v4 on v3

v4 whole, which is shorter than its diff:
```python
import functools

import jax
import jax.numpy as jnp
from jax import lax
from jax.experimental import pallas as pl
from jax.experimental.pallas import tpu as pltpu
from jax.sharding import PartitionSpec as P

EPSILON = 1e-06
SQRT_2_OVER_PI = 0.7978845608028654
CHUNK = 512
AHEAD = 3
MIB = 1024 * 1024
F32, BF16 = jnp.float32, jnp.bfloat16
WHOLE = pl.BlockSpec(memory_space=pltpu.VMEM)
HELD = pl.BlockSpec(memory_space=pltpu.HBM)
SCALARS = pl.BlockSpec(memory_space=pltpu.SMEM)


def pieces(start, stop, size=CHUNK):
    return [(at, min(size, stop - at)) for at in range(start, stop, size)]


def split_rows(hidden):
    units = hidden // CHUNK
    return CHUNK * max(units // 2, 1), CHUNK * max(units - 1, 1)


def after(value, *others):
    return lax.optimization_barrier((value,) + others)[0]


def swap_grp(value):
    return lax.ppermute(value, "grp", [(0, 1), (1, 0)])


def stages():
    return (lax.axis_size("fsdp") - 1).bit_length()


def step(value, stage):
    length, bits = lax.axis_size("fsdp"), stages()
    pairs = []
    for group, bit in ((0, stage), (1, bits - 1 - stage)):
        pairs += [(group * length + i, group * length + (i ^ (1 << bit))) for i in range(length)]
    return lax.ppermute(value, ("grp", "fsdp"), pairs)


def block_order(group, me):
    length, bits = lax.axis_size("fsdp"), stages()
    turned = [sum(((v >> b) & 1) << (bits - 1 - b) for b in range(bits)) for v in range(length)]
    up, down = jnp.arange(length, dtype=jnp.int32), jnp.array(turned, jnp.int32)
    return me ^ jnp.where(group == 0, up, down)


def send(value, place):
    length, bits = lax.axis_size("fsdp"), stages()
    turned = sum(((place >> b) & 1) << (bits - 1 - b) for b in range(bits))
    pairs = []
    for group, mask in ((0, place), (1, turned)):
        pairs += [(group * length + i, group * length + (i ^ mask)) for i in range(length)]
    return lax.ppermute(value, ("grp", "fsdp"), pairs)


def gather_dp(value):
    length = lax.axis_size("dp")
    return [value] + [
        lax.ppermute(value, "dp", [(i, i ^ mask) for i in range(length)]) for mask in range(1, length)
    ]


def block_of(value, index, rows):
    return lax.dynamic_slice_in_dim(value, index * rows, rows, 0)


def split_three(value):
    high = value.astype(BF16)
    rest = value - high.astype(F32)
    mid = rest.astype(BF16)
    return high, mid, (rest - mid.astype(F32)).astype(BF16)


def pack_sums(plain, along):
    tail = [part.astype(F32) for part in split_three(plain) + split_three(along)]
    return jnp.concatenate(tail + [jnp.zeros((10, plain.shape[1]), F32)], 0).astype(BF16)


def unpack_sums(tail):
    tail = tail.astype(F32)
    return tail[0:1] + tail[1:2] + tail[2:3], tail[3:4] + tail[4:5] + tail[5:6]


def gelu_and_slope(v):
    square = v * v
    t = jnp.tanh(SQRT_2_OVER_PI * (v + 0.044715 * (square * v)))
    rise = 0.5 * (1.0 + t)
    slope = rise + 0.5 * v * (1.0 - t * t) * (SQRT_2_OVER_PI * (1.0 + (3 * 0.044715) * square))
    return v * rise, slope


class Stream:
    def __init__(self, first, first_buf, second, second_buf, parts, base, sems):
        def copy(weight, buf, part):
            return weight.at[0, pl.ds(part[0], part[1]), :], buf.at[pl.ds(part[0] - base, part[1]), :]

        pairs = [copy(first, first_buf, parts[0])]
        for k, part in enumerate(parts):
            if k + 1 < len(parts):
                pairs.append(copy(first, first_buf, parts[k + 1]))
            pairs.append(copy(second, second_buf, part))
        self.copies = [pltpu.make_async_copy(a, b, sems.at[k]) for k, (a, b) in enumerate(pairs)]
        self.next = 0
        for item in self.copies[:AHEAD]:
            item.start()

    def take(self):
        k = self.next
        self.copies[k].wait()
        if k + AHEAD < len(self.copies):
            self.copies[k + AHEAD].start()
        self.next = k + 1


def pipelined(parts, product, finish):
    held = None
    for part in parts:
        value = product(*part)
        if held is not None:
            finish(*held, False)
        held = part + (value,)
    finish(*held, True)


def params(flops, moved, transcendentals=0, grant=50):
    return dict(
        compiler_params=pltpu.CompilerParams(vmem_limit_bytes=grant * MIB),
        cost_estimate=pl.CostEstimate(flops=flops, bytes_accessed=moved, transcendentals=transcendentals),
    )


def struct(shape, dtype):
    return jax.ShapeDtypeStruct(shape, dtype)


def staging(rows, features, lanes):
    return pltpu.VMEM((features, lanes) if rows % 16 else (8, 128), F32)


def place_blocks(target, lanes, stage, order, blocks, rows, first=0):
    for place, value in enumerate(blocks):
        if rows % 16:
            stage[pl.ds(pl.multiple_of(order[first + place] * rows, 8), rows), :] = value().astype(F32)
        else:
            target[pl.ds(pl.multiple_of(order[first + place] * rows, 16), rows), lanes] = value()
    if rows % 16:
        target[:, lanes] = stage[...].astype(target.dtype)


def turn_modulation(modulation, columns):
    for start, size in pieces(0, modulation.shape[2], 128):
        rows = modulation[0, :, pl.ds(start, size)]
        columns[pl.ds(start, size), :] = jnp.concatenate([rows, jnp.zeros((5, size), F32)], 0).T


def normalize(acts, mod, normed, stats):
    features, tokens = acts.shape[1:]
    parts = pieces(0, features, 128)
    total = jnp.zeros((1, tokens), F32)
    for start, size in parts:
        total += jnp.sum(acts[0, pl.ds(start, size), :].astype(F32), 0, keepdims=True)
    mean = total / features
    total = jnp.zeros((1, tokens), F32)
    for start, size in parts:
        centred = acts[0, pl.ds(start, size), :].astype(F32) - mean
        total += jnp.sum(centred * centred, 0, keepdims=True)
    inv = lax.rsqrt(total / features + EPSILON)
    stats[0:1, :] = mean
    stats[1:2, :] = inv
    for start, size in parts:
        rows = pl.ds(start, size)
        xhat = (acts[0, rows, :].astype(F32) - mean) * inv
        normed[rows, :] = (xhat * (1.0 + mod[rows, 1:2]) + mod[rows, 0:1]).astype(BF16)


def accumulate(total, part, weight, before, finish):
    for at, size in pieces(0, weight.shape[1]):
        columns = pl.ds(at, size)
        value = jnp.dot(part, weight[:, columns], preferred_element_type=F32)
        if before is not None:
            value = value + before[:, columns]
        if finish is None:
            total[:, columns] = value
        else:
            finish(at, size, value)


def forward_products(stream, parts, base, normed, in_buf, out_buf, slope_out, total, before, last):
    state = [before]

    def product(at, size):
        stream.take()
        return jnp.dot(in_buf[pl.ds(at - base, size), :], normed[...], preferred_element_type=F32)

    def finish(at, size, pre, final):
        rows = pl.ds(at - base, size)
        hidden, slope = gelu_and_slope(pre)
        slope_out[rows, :] = slope
        stream.take()
        accumulate(total, hidden.T.astype(BF16), out_buf.at[rows, :], state[0], last if final else None)
        state[0] = total

    pipelined(parts, product, finish)


def forward_first_kernel(acts, modulation, w_in, w_out, mod, normed, stats, slope_out, total, in_buf, out_buf, sems):
    parts = pieces(0, slope_out.shape[0])
    stream = Stream(w_in, in_buf, w_out, out_buf, parts, 0, sems)
    turn_modulation(modulation, mod)
    normalize(acts, mod, normed, stats)
    forward_products(stream, parts, 0, normed, in_buf, out_buf, slope_out, total, None, None)


def forward_last_kernel(start, order, normed, before, w_in, w_out, slope_out, *refs):
    outs, (in_buf, out_buf, total, full, sems) = refs[:-5], refs[-5:]
    parts = pieces(start, start + slope_out.shape[0])
    stream = Stream(w_in, in_buf, w_out, out_buf, parts, start, sems)

    def last(at, size, value):
        full[pl.ds(at, size), :] = value.T

    forward_products(stream, parts, start, normed, in_buf, out_buf, slope_out, total, before, last)
    write_blocks(order, full, outs)


def layer_scratch(part, features):
    return [
        pltpu.VMEM((part, features), BF16),
        pltpu.VMEM((part, features), BF16),
    ]


def layer_params(part, features, tokens, transcendentals):
    return params(4 * part * features * tokens, 4 * part * features + 4 * features * tokens, transcendentals)


def forward_first(acts, modulation, w_in, w_out, part, name):
    features, tokens = acts.shape[1:]
    return pl.pallas_call(
        forward_first_kernel,
        out_shape=(
            struct((features, 8), F32),
            struct((features, tokens), BF16),
            struct((2, tokens), F32),
            struct((part, tokens), F32),
            struct((tokens, features), F32),
        ),
        in_specs=[WHOLE, WHOLE, HELD, HELD],
        out_specs=[WHOLE] * 5,
        scratch_shapes=layer_scratch(part, features) + [pltpu.SemaphoreType.DMA((2 * len(pieces(0, part)),))],
        name=name,
        **layer_params(part, features, tokens, part * tokens),
    )(acts, modulation, w_in, w_out)


def forward_last(order, normed, before, w_in, w_out, start, blocks, name):
    hidden, features = w_in.shape[1:]
    tokens, part, rows = before.shape[0], hidden - start, features // blocks
    slope, *outs = pl.pallas_call(
        functools.partial(forward_last_kernel, start),
        out_shape=[struct((part, tokens), F32), struct((rows, tokens), F32)]
        + [struct((rows, tokens), BF16)] * (blocks - 1),
        in_specs=[SCALARS, WHOLE, WHOLE, HELD, HELD],
        out_specs=[WHOLE] * (blocks + 1),
        scratch_shapes=layer_scratch(part, features)
        + [
            pltpu.VMEM((tokens, features), F32),
            pltpu.VMEM((features, tokens), F32),
            pltpu.SemaphoreType.DMA((2 * len(pieces(start, hidden)),)),
        ],
        name=name,
        **layer_params(part, features, tokens, part * tokens),
    )(order, normed, before, w_in, w_out)
    return slope, outs[0], outs[1:]


def write_blocks(order, full, outs):
    for place, target in enumerate(outs):
        rows = target.shape[0]
        offset = pl.multiple_of(order[place] * rows, 8)
        target[...] = full[pl.ds(offset, rows), :].astype(target.dtype)


def backward_products(stream, parts, base, grad, slopes, in_buf, out_buf, total, before, last):
    state = [before]

    def product(at, size):
        stream.take()
        return jnp.dot(out_buf[pl.ds(at - base, size), :], grad[...], preferred_element_type=F32)

    def finish(at, size, value, final):
        rows = pl.ds(at - base, size)
        seen = slopes[0].shape[0]
        slope = slopes[0][pl.ds(at, size), :] if at < seen else slopes[1][pl.ds(at - seen, size), :]
        stream.take()
        accumulate(total, (value * slope).T.astype(BF16), in_buf.at[rows, :], state[0], last if final else None)
        state[0] = total

    pipelined(parts, product, finish)


def backward_first_kernel(blocks, part, order, *refs):
    pieces_in, (slope_a, slope_b, w_in, w_out, grad, total, in_buf, out_buf, stage, sems) = refs[:blocks], refs[blocks:]
    parts = pieces(0, part)
    stream = Stream(w_out, out_buf, w_in, in_buf, parts, 0, sems)
    values = [lambda ref=ref: ref[...] for ref in pieces_in]
    place_blocks(grad, slice(None), stage, order, values, pieces_in[0].shape[0])
    backward_products(stream, parts, 0, grad, (slope_a, slope_b), in_buf, out_buf, total, None, None)


def backward_first(order, gathered, slope_a, slope_b, w_in, w_out, part, name):
    hidden, features = w_in.shape[1:]
    blocks, (rows, tokens) = len(gathered), gathered[0].shape
    return pl.pallas_call(
        functools.partial(backward_first_kernel, blocks, part),
        out_shape=(struct((features, tokens), BF16), struct((tokens, features), F32)),
        in_specs=[SCALARS] + [WHOLE] * (blocks + 2) + [HELD, HELD],
        out_specs=[WHOLE] * 2,
        scratch_shapes=layer_scratch(part, features)
        + [staging(rows, features, tokens), pltpu.SemaphoreType.DMA((2 * len(pieces(0, part)),))],
        name=name,
        **layer_params(part, features, tokens, 0),
    )(order, *gathered, slope_a, slope_b, w_in, w_out)


def backward_last_kernel(start, rows, order, grad, before, slope_a, slope_b, acts, stats, mod, w_in, w_out, *refs):
    outs, (sums_out, in_buf, out_buf, total, full, sems) = refs[:-6], refs[-6:]
    hidden, (features, tokens) = w_in.shape[1], full.shape
    parts = pieces(start, hidden)
    stream = Stream(w_out, out_buf, w_in, in_buf, parts, start, sems)
    mean, inv = stats[0:1, :], stats[1:2, :]
    sums = [jnp.zeros((1, tokens), F32), jnp.zeros((1, tokens), F32)]

    def last(at, size, value):
        at = pl.ds(at, size)
        value = value.T
        full[at, :] = value
        scaled = value * (1.0 + mod[at, 1:2])
        xhat = (acts[0, at, :].astype(F32) - mean) * inv
        sums[0] += jnp.sum(scaled, 0, keepdims=True)
        sums[1] += jnp.sum(scaled * xhat, 0, keepdims=True)

    backward_products(stream, parts, start, grad, (slope_a, slope_b), in_buf, out_buf, total, before, last)
    count = len(outs) // 2
    padded = outs[0].shape[0] - 16
    tail = pack_sums(*sums)
    for place in range(count):
        offset = pl.multiple_of(order[2 * place] * rows, 8)
        outs[count + place][...] = full[pl.ds(offset, rows), :]
        offset = pl.multiple_of(order[2 * place + 1] * rows, 8)
        block = full[pl.ds(offset, rows), :]
        if padded > rows:
            block = jnp.concatenate([block, jnp.zeros((padded - rows, tokens), F32)], 0)
        outs[place][:padded, :] = block.astype(BF16)
        outs[place][padded:, :] = tail
    sums_out[0:1, :] = sums[0]
    sums_out[1:2, :] = sums[1]


def backward_last(order, grad, before, slope_a, slope_b, acts, stats, mod, w_in, w_out, start, blocks, name):
    hidden, features = w_in.shape[1:]
    tokens, part, rows, count = before.shape[0], hidden - start, features // blocks, blocks // 2
    outs = pl.pallas_call(
        functools.partial(backward_last_kernel, start, rows),
        out_shape=[struct((-(-rows // 16) * 16 + 16, tokens), BF16)] * count
        + [struct((rows, tokens), F32)] * count
        + [struct((2, tokens), F32)],
        in_specs=[SCALARS] + [WHOLE] * 7 + [HELD, HELD],
        out_specs=[WHOLE] * (blocks + 1),
        scratch_shapes=layer_scratch(part, features)
        + [
            pltpu.VMEM((tokens, features), F32),
            pltpu.VMEM((features, tokens), F32),
            pltpu.SemaphoreType.DMA((2 * len(pieces(start, hidden)),)),
        ],
        name=name,
        **layer_params(part, features, tokens, 0),
    )(order, grad, before, slope_a, slope_b, acts, stats, mod, w_in, w_out)
    return outs[:count], outs[count:-1], outs[-1]


def fold_kernel(rows, count, *refs):
    got, kept, (sums, *outs) = refs[:count], refs[count : 2 * count], refs[2 * count :]
    more = unpack_sums(got[0][-16:, :])
    plain, along = sums[0:1, :] + more[0], sums[1:2, :] + more[1]
    tail = pack_sums(plain, along)
    padded = got[0].shape[0] - 16
    for place in range(count // 2):
        even, odd = 2 * place, 2 * place + 1
        outs[count // 2 + place][...] = kept[even][...] + got[even][:rows, :].astype(F32)
        block = kept[odd][...] + got[odd][:rows, :].astype(F32)
        if padded > rows:
            block = jnp.concatenate([block, jnp.zeros((padded - rows, block.shape[1]), F32)], 0)
        outs[place][:padded, :] = block.astype(BF16)
        outs[place][padded:, :] = tail
    outs[-1][0:1, :] = plain
    outs[-1][1:2, :] = along


def fold(got, kept, sums):
    count, (rows, tokens) = len(kept), kept[0].shape
    outs = pl.pallas_call(
        functools.partial(fold_kernel, rows, count),
        out_shape=[struct(got[0].shape, BF16)] * (count // 2)
        + [struct((rows, tokens), F32)] * (count // 2)
        + [struct((2, tokens), F32)],
        in_specs=[WHOLE] * (2 * count + 1),
        out_specs=[WHOLE] * (count + 1),
        name="fold",
        **params(2 * count * rows * tokens, 8 * count * rows * tokens, grant=12),
    )(*got, *kept, sums)
    return outs[: count // 2], outs[count // 2 : -1], outs[-1]


def upstream_kernel(blocks, order, weight, own, arrived, *refs):
    outs, (cot0, cot1_rows, full) = refs[:-3], refs[-3:]
    group = order[blocks]
    control = group == 0
    half = cot0.shape[1]
    lanes = pl.ds(pl.multiple_of(group * half, half), half)
    cot0[...] = jnp.where(control, own[:, lanes], arrived[:, lanes])
    mine = jnp.where(control, arrived[:, lanes], own[:, lanes])
    cot1_rows[...] = jnp.where(control, arrived[...], own[...])
    full[...] = lax.dot_general(mine, weight[...], (((0,), (0,)), ((), ())), preferred_element_type=F32).T
    write_blocks(order, full, outs)


def upstream_terms(order, weight, own, arrived, blocks):
    rows, tokens = own.shape
    half = tokens // 2
    outs = pl.pallas_call(
        functools.partial(upstream_kernel, blocks),
        out_shape=[struct((rows, half), F32)]
        + [struct((rows, half), BF16)] * blocks
        + [struct((rows, tokens), BF16)],
        in_specs=[SCALARS] + [WHOLE] * 3,
        out_specs=[WHOLE] * (blocks + 2),
        scratch_shapes=[pltpu.VMEM((weight.shape[1], half), F32)],
        name="upstream_terms",
        **params(2 * weight.size * half, 2 * weight.size + 4 * blocks * rows * half, grant=12),
    )(order, weight, own, arrived)
    return outs[0], outs[1:blocks], *outs[blocks:]


def residual_kernel(order, weight, *refs):
    stack, (result, full, stage) = refs[:-3], refs[-3:]
    values = [lambda value=value: value[...] for value in stack]
    place_blocks(full, slice(None), stage, order, values, stack[0].shape[0])
    result[...] = jnp.dot(weight[...], full[...], preferred_element_type=F32)


def residual_rows(order, weight, stack):
    blocks, (rows, half) = len(stack), stack[0].shape
    return pl.pallas_call(
        residual_kernel,
        out_shape=struct((rows, half), F32),
        in_specs=[SCALARS] + [WHOLE] * (blocks + 1),
        out_specs=WHOLE,
        scratch_shapes=[pltpu.VMEM((blocks * rows, half), BF16), staging(rows, blocks * rows, half)],
        name="residual_rows",
        **params(2 * weight.size * half, 2 * weight.size + 4 * blocks * rows * half, grant=12),
    )(order, weight, *stack)


def zero_grad_kernel(blocks, parts, order, dp_order, *refs):
    cots, stacks, (out, lhs, rhs, stage, buf, sems) = refs[:parts], refs[parts:-6], refs[-6:]
    near, near_other, far, far_other = (stacks[k * blocks : (k + 1) * blocks] for k in range(4))
    rows, half = near[0].shape
    group = order[blocks]
    for part in range(parts):
        lhs[:, pl.ds(pl.multiple_of(dp_order[part] * 2 * half, 2 * half), 2 * half)] = cots[part][...]
        for side, sources in enumerate((near, near_other) if part == 0 else (far, far_other)):
            at = Ellipsis if part == 0 else part - 1
            values = [lambda source=source, at=at: source[at] for source in sources]
            owner = group if side == 0 else 1 - group
            lanes = pl.ds(pl.multiple_of((dp_order[part] * 2 + owner) * half, half), half)
            place_blocks(rhs, lanes, stage, order, values, rows, side * (blocks + 1))
    copies = []
    for k, (start, size) in enumerate(pieces(0, blocks * rows, CHUNK)):
        columns = pl.ds(start, size)
        buf[:, columns] = lax.dot_general(
            lhs[...], rhs[columns, :], (((1,), (1,)), ((), ())), preferred_element_type=F32
        )
        copies.append(pltpu.make_async_copy(buf.at[:, columns], out.at[:, columns], sems.at[k]))
        copies[-1].start()
    for copy in copies:
        copy.wait()


def zero_projection_grad(order, dp_order, cots, near, near_other, far, far_other):
    blocks, (rows, half) = len(near), near[0].shape
    parts = len(cots)
    features, tokens = blocks * rows, parts * 2 * half

    return pl.pallas_call(
        functools.partial(zero_grad_kernel, blocks, parts),
        out_shape=struct((rows, features), F32),
        in_specs=[SCALARS] * 2 + [WHOLE] * (parts + 4 * blocks),
        out_specs=HELD,
        scratch_shapes=[
            pltpu.VMEM((rows, tokens), BF16),
            pltpu.VMEM((features, tokens), BF16),
            staging(rows, features, half),
            pltpu.VMEM((rows, features), F32),
            pltpu.SemaphoreType.DMA((len(pieces(0, features, CHUNK)),)),
        ],
        name="zero_projection_grad",
        **params(2 * tokens * rows * features, 4 * rows * features + 2 * tokens * (rows + features), grant=28),
    )(order, dp_order, *cots, *near, *near_other, *far, *far_other)


def steps(values, level, *during):
    got = [step(value, level) for value in values]
    return list(lax.optimization_barrier((tuple(got),) + during)[0]) if during else got


def direct(values, *during):
    got = [send(value, place + 1) for place, value in enumerate(values)]
    return list(lax.optimization_barrier((tuple(got),) + during)[0])


def local(acts, modulation, w_in, w_out, zero_weight, cotangent):
    own_cot = cotangent[0]
    features, tokens = acts.shape[1:]
    hidden = w_in.shape[1]
    rows = own_cot.shape[0]
    half = tokens // 2
    blocks, levels = lax.axis_size("fsdp"), stages()
    parts = lax.axis_size("dp")
    group = lax.axis_index("grp").astype(jnp.int32)
    me = lax.axis_index("fsdp").astype(jnp.int32)
    is_control = group == 0
    places = block_order(group, me)
    order = jnp.concatenate([places, group[None], block_order(1 - group, me)])
    dp_order = lax.axis_index("dp").astype(jnp.int32) ^ jnp.arange(parts, dtype=jnp.int32)

    arrived = swap_grp(own_cot)
    own_term, sent, cot0, cot1_rows = upstream_terms(order, zero_weight, own_cot, arrived, blocks)
    split, cut = split_rows(hidden)
    mod, normed, stats, slope_a, total = forward_first(
        after(acts, *sent), modulation, w_in, w_out, split, "forward_first"
    )
    own_mod = block_of(mod, me, rows)
    own_gate = own_mod[:, 2:3]
    got = direct(sent, total)
    up_half = own_term + cot0.astype(F32) + sum(value.astype(F32) for value in got)
    up_rows = jnp.where(is_control, jnp.concatenate([up_half, swap_grp(up_half)], 1), own_cot.astype(F32))
    grad_rows = (own_gate * up_rows).astype(BF16)

    slope_b, kept, sent = forward_last(
        order, after(normed, grad_rows), total, w_in, w_out, split, blocks, "forward_last"
    )
    gathered = [grad_rows] + direct([grad_rows] * (blocks - 1), kept)
    cots = gather_dp(cot1_rows)
    grad, total = backward_first(
        order, after(gathered, *sent), slope_a, slope_b, w_in, w_out, cut, "backward_first"
    )
    got = direct(sent, total)
    own_values = block_of(acts[0], me, rows).astype(F32)
    sums = own_values + own_gate * (kept + sum(value.astype(F32) for value in got))
    out_rows = sums.astype(BF16)

    out_half = jnp.where(is_control, out_rows[:, :half], swap_grp(out_rows[:, half:]))
    far = gather_dp(out_half)[1:]
    sent, kept, token_sums = backward_last(
        order, after(grad, out_half, *cots), total, slope_a, slope_b, acts, stats, mod, w_in, w_out, cut, blocks, "backward_last"
    )
    near = [after(out_half, sent[0])]
    for level in range(levels):
        near = near + steps(near, level)
    near_other = [swap_grp(value) for value in near]
    residual = residual_rows(order, zero_weight, near)
    far = [jnp.stack(far)]

    for level in range(levels):
        got = steps(sent, level)
        far = far + steps(far, level)
        if level + 1 < levels:
            sent, kept, token_sums = fold(got, kept, token_sums)
    more = unpack_sums(got[0][-16:])
    plain, along = token_sums[0:1] + more[0], token_sums[1:2] + more[1]
    kept = [kept[0] + got[0][:rows].astype(F32)]
    mean, inv = stats[0:1], stats[1:2]
    back = inv * (
        kept[0] * (1.0 + own_mod[:, 1:2]) - plain / features - (own_values - mean) * inv * (along / features)
    )
    residual = jnp.concatenate([swap_grp(residual), residual], 1)
    block_rows = jnp.where(is_control, out_rows, (sums + residual).astype(BF16))

    far_other = [swap_grp(value) for value in far]
    zero_grad = zero_projection_grad(order, dp_order, cots, near, near_other, far, far_other)
    return (block_rows[None], (up_rows + back)[None], zero_grad)


def solution(mesh):
    placed = (
        P("grp", None, "dp"),
        P("grp", None, None),
        P("grp", "fsdp", None),
        P("grp", "fsdp", None),
        P("fsdp", None),
        P("grp", "fsdp", "dp"),
    )
    return jax.shard_map(
        local,
        mesh=mesh,
        in_specs=placed,
        out_specs=(P("grp", "fsdp", "dp"), P("grp", "fsdp", "dp"), P("fsdp", None)),
        check_vma=False,
    )
```

time: 145 us -> 163 us (1.12)
  waiting for transfers between devices: 35.1 us -> 51.2 us
  other arithmetic: 4.26 us -> 9.12 us
  starting transfers between devices: 36.3 us -> 33 us
    ppermute x6, waiting for transfers between devices: 3.7 us -> 33.2 us  [gather_dp(): lax.ppermute(value, 'dp', [(i, i ^ mask) for i in range(length)])]
    ppermute x21 -> x9, starting transfers between devices: 24.4 us -> 10.2 us  [step(): return lax.ppermute(value, ('grp', 'fsdp'), pairs)]
    ppermute x21 -> x9, waiting for transfers between devices: 27.5 us -> 13.5 us  [step(): return lax.ppermute(value, ('grp', 'fsdp'), pairs)]
    ppermute x0 -> x9, starting transfers between devices: none -> 11.5 us  [send(): return lax.ppermute(value, ('grp', 'fsdp'), pairs)]
    unnamed x56 -> x57, local copies, waits for them, and re-layouts: 7.9 us -> 9.98 us
    ppermute x0 -> x9, waiting for transfers between devices: none -> 1.98 us  [send(): return lax.ppermute(value, ('grp', 'fsdp'), pairs)]
    convert_element_type x1, other arithmetic: 0.19 us -> 2.12 us  [local(): out_rows = sums.astype(BF16)]
    ppermute x17 -> x12, waiting for transfers between devices: 3.87 us -> 2.48 us  [swap_grp(): return lax.ppermute(value, 'grp', [(0, 1), (1, 0)])]
  transfers between devices with their start and end apart: 44 -> 36, of which waited for: 13 -> 11; matrix products, arithmetic and copies ran while one was open for 5% -> 4% of each run, Pallas kernels for 35% -> 23%
where the time goes in v4:
time: 163 us; the launch traced here: 162 us
  Pallas kernels  57.8 us (35%)
  waiting for transfers between devices  51.2 us (31%)
  starting transfers between devices  33 us (20%)
  local copies, waits for them, and re-layouts  10 us (6%)
  other arithmetic  9.12 us (6%)
    ppermute x6, waiting for transfers between devices, gather_dp(): lax.ppermute(value, 'dp', [(i, i ^ mask) for i in range(length)])  33.2 us
    ppermute x9, waiting for transfers between devices, step(): return lax.ppermute(value, ('grp', 'fsdp'), pairs)  13.5 us
    pallas_call x1, Pallas kernels, forward_last(): pl.pallas_call(functools.partial(forward_last_kernel, start), out_shape=[...  12.4 us
    ppermute x9, starting transfers between devices, send(): return lax.ppermute(value, ('grp', 'fsdp'), pairs)  11.5 us
    pallas_call x1, Pallas kernels, backward_last(): pl.pallas_call(functools.partial(backward_last_kernel, start, rows), out_...  11.3 us
    pallas_call x1, Pallas kernels, backward_first(): pl.pallas_call(functools.partial(backward_first_kernel, blocks, part), ou...  11.2 us
    pallas_call x1, Pallas kernels, forward_first(): pl.pallas_call(forward_first_kernel, out_shape=(struct((features, 8), F32...  10.6 us
    ppermute x9, starting transfers between devices, step(): return lax.ppermute(value, ('grp', 'fsdp'), pairs)  10.2 us
  transfers between devices with their start and end apart: 36, of which 11 were waited for; matrix products, arithmetic and copies ran while one was open for 4% of the time, Pallas kernels for 23%

profile of v4, /device:TPU:0, one launch (start us, length us, event | category | flops | bytes accessed | tf_op | source)
XLA Modules:
  0.0 162.3 jit_solution(12778156588693259085)
XLA Ops:
  1.1 0.8 copy.12.modulation
  2.7 1.8 %copy-done = bf16[608,2432]{1,0:T(8,128)(2,1)S(1)} copy-done((bf16[608,2432]{1,0:T(8,128)(2,1)S(1)}, bf16[608,2432]{1,0:T(8,128)(2,1)}, u32[]{:S(2)}) %copy-start) | copy-done | bytes 2957336
  4.5 1.0 copy-done.5
  5.5 1.4 upstream_terms.1
  7.6 2.8 %collective-permute-start.1 = (bf16[608,128]{1,0:T(8,128)(2,1)S(1)}, bf16[608,128]{1,0:T(8,128)(2,1)S(1)}, u32[]{:S(2)}, u32[]{:S(2)}) collective-permute-start(bf16[608,128]{1,0:T(8,128)(2,1)S(1)} %get-tuple-element.46), channel_id=1, source_target_pairs={{0,4},{4,0},{8,12},{12,8},{16,24},{20,28},{24,16},{28,20},{1,5},{5... | collective-permute-start | bytes 466952 | tf_op jit(solution)/shard_map/ppermute | solution.py:63
  10.4 1.5 collective-permute-start.2
  11.9 10.6 %forward_first.1 = (f32[2432,8]{1,0:T(8,128)S(1)}, bf16[2432,256]{1,0:T(8,128)(2,1)S(1)}, f32[2,256]{1,0:T(2,128)S(1)}, f32[1024,256]{1,0:T(8,128)S(1)}, f32[256,2432]{1,0:T(8,128)}) custom-call(bf16[1,2432,256]{2,1,0:T(8,128)(2,1)} %acts.2, f32[1,3,2432]{2,1,0:T(4,128)S(1)} %copy.12.modulation, bf16[1,2432,2432]{2,1,0:T(8,128)(2,1)} %w_in.5, ...), custom_call_target="tpu_custom_call" | custom-call | flops 2550136832 | bytes 12451840 | tf_op jit(solution)/shard_map/forward_first/pallas_call | solution.py:249
  22.6 1.1 copy-done.7
  23.7 0.8 add_add_fusion
  24.9 1.4 collective-permute-done.4
  26.3 0.7 copy-done.26
  27.0 1.1 multiply_convert_fusion.refs_0_
  28.2 3.0 %collective-permute-start.10 = (bf16[608,256]{1,0:T(8,128)(2,1)S(1)}, bf16[608,256]{1,0:T(8,128)(2,1)S(1)}, u32[]{:S(2)}, u32[]{:S(2)}) collective-permute-start(bf16[608,256]{1,0:T(8,128)(2,1)S(1)} %multiply_convert_fusion.refs_0_), channel_id=1, source_target_pairs={{0,12},{4,8},{8,4},{12,0},{16,28},{20,24},{24,20},{28,16},{1,13},{... | collective-permute-start | bytes 933896 | tf_op jit(solution)/shard_map/ppermute | solution.py:63
  31.8 12.4 %forward_last.1 = (f32[1408,256]{1,0:T(8,128)}, f32[608,256]{1,0:T(8,128)S(1)}, bf16[608,256]{1,0:T(8,128)(2,1)S(1)}, bf16[608,256]{1,0:T(8,128)(2,1)S(1)}, bf16[608,256]{1,0:T(8,128)(2,1)S(1)}) custom-call(s32[9]{0:T(128)S(1)} %pad_add_fusion.order, bf16[2432,256]{1,0:T(8,128)(2,1)S(1)} %copy-done.8, f32[256,2432]{1,0:T(8,128)} %get-tuple-element.54.before, ...), custom_call_target="tpu_custom_call" | custom-call | flops 3506438144 | bytes 16187392 | tf_op jit(solution)/shard_map/forward_last/pallas_call | solution.py:269
  44.2 2.0 %collective-permute-start.5 = (bf16[608,256]{1,0:T(8,128)(2,1)S(1)}, bf16[608,256]{1,0:T(8,128)(2,1)S(1)}, u32[]{:S(2)}, u32[]{:S(2)}) collective-permute-start(bf16[608,256]{1,0:T(8,128)(2,1)S(1)} %get-tuple-element.60), channel_id=1, source_target_pairs={{0,4},{4,0},{8,12},{12,8},{16,24},{20,28},{24,16},{28,20},{1,5},{5... | collective-permute-start | bytes 933896 | tf_op jit(solution)/shard_map/ppermute | solution.py:63
  46.2 1.5 collective-permute-start.6
  47.8 11.2 %backward_first.1 = (bf16[2432,256]{1,0:T(8,128)(2,1)S(1)}, f32[256,2432]{1,0:T(8,128)}) custom-call(s32[9]{0:T(128)S(1)} %pad_add_fusion.order, bf16[608,256]{1,0:T(8,128)(2,1)S(1)} %multiply_convert_fusion.refs_0_, bf16[608,256]{1,0:T(8,128)(2,1)S(1)} %collective-permute-done.8.refs_1_, bf16[608,256]{1,0:T(8,128)(2,1)S(1)} %collective-permute-done.9.refs_2_, ...), custom_call_target="tpu_custom_call" | custom-call | flops 3825205248 | bytes 17432576 | tf_op jit(solution)/shard_map/backward_first/pallas_call | solution.py:324
  59.0 2.0 %collective-permute-done.7 = bf16[608,256]{1,0:T(8,128)(2,1)S(1)} collective-permute-done((bf16[608,256]{1,0:T(8,128)(2,1)S(1)}, bf16[608,256]{1,0:T(8,128)(2,1)S(1)}, u32[]{:S(2)}, u32[]{:S(2)}) %collective-permute-start.7) | collective-permute-done | bytes 311328 | tf_op jit(solution)/shard_map/ppermute | solution.py:63
  61.0 2.1 %fusion.16 = (bf16[608,256]{1,0:T(8,128)(2,1)S(1)}, f32[608,256]{1,0:T(8,128)}) fusion(f32[608,256]{1,0:T(8,128)S(1)} %get-tuple-element.59, bf16[608,256]{1,0:T(8,128)(2,1)S(1)} %collective-permute-done.7, bf16[608,256]{1,0:T(8,128)(2,1)S(1)} %collective-permute-done.6, bf16[608,256]{1,0:T(8,128)(2,1)S(1)} %collective-permute-done.5, ...), kind=kLoop, calls=%fused_computation.35 | loop fusion | flops 1556480 | bytes 2804100 | tf_op jit(solution)/shard_map/convert_element_type | solution.py:571
  63.2 3.8 %collective-permute-start.14 = (bf16[608,256]{1,0:T(8,128)(2,1)S(1)}, bf16[608,256]{1,0:T(8,128)(2,1)S(1)}, u32[]{:S(2)}, u32[]{:S(2)}) collective-permute-start(bf16[608,256]{1,0:T(8,128)(2,1)S(1)} %copy-done.15), channel_id=1, source_target_pairs={{0,3},{1,2},{2,1},{3,0},{4,7},{5,6},{6,5},{7,4},{8,11},{9,10},{10,... | collective-permute-start | bytes 933896 | tf_op jit(solution)/shard_map/ppermute | solution.py:69
  67.7 7.7 %collective-permute-done.14.refs_3_ = bf16[608,256]{1,0:T(8,128)(2,1)S(1)} collective-permute-done((bf16[608,256]{1,0:T(8,128)(2,1)S(1)}, bf16[608,256]{1,0:T(8,128)(2,1)S(1)}, u32[]{:S(2)}, u32[]{:S(2)}) %collective-permute-start.14) | collective-permute-done | bytes 311328 | tf_op jit(solution)/shard_map/ppermute | solution.py:69
  75.4 0.7 copy-done.17
  76.1 18.0 %collective-permute-done.13.refs_2_ = bf16[608,256]{1,0:T(8,128)(2,1)S(1)} collective-permute-done((bf16[608,256]{1,0:T(8,128)(2,1)S(1)}, bf16[608,256]{1,0:T(8,128)(2,1)S(1)}, u32[]{:S(2)}, u32[]{:S(2)}) %collective-permute-start.13) | collective-permute-done | bytes 311328 | tf_op jit(solution)/shard_map/ppermute | solution.py:69
  94.1 0.7 copy-done.19
  94.9 0.7 copy-done.21
  95.6 11.3 %backward_last.1 = (bf16[624,256]{1,0:T(8,128)(2,1)}, bf16[624,256]{1,0:T(8,128)(2,1)}, f32[608,256]{1,0:T(8,128)S(1)}, f32[608,256]{1,0:T(8,128)S(1)}, f32[2,256]{1,0:T(2,128)S(1)}) custom-call(s32[9]{0:T(128)S(1)} %pad_add_fusion.order, bf16[2432,256]{1,0:T(8,128)(2,1)} %copy-done.9, f32[256,2432]{1,0:T(8,128)} %get-tuple-element.72.before, ...), custom_call_target="tpu_custom_call" | custom-call | flops 2231369728 | bytes 11206656 | tf_op jit(solution)/shard_map/backward_last/pallas_call | solution.py:373
  107.0 0.8 copy-done.10
  107.8 0.9 copy-done.12
  108.6 1.5 collective-permute-start.15
  110.1 2.5 %collective-permute-start.28 = (bf16[608,128]{1,0:T(8,128)(2,1)S(1)}, bf16[608,128]{1,0:T(8,128)(2,1)S(1)}, u32[]{:S(2)}, u32[]{:S(2)}) collective-permute-start(bf16[608,128]{1,0:T(8,128)(2,1)S(1)} %slice_select_fusion.refs_0_.refs_4_), channel_id=1, source_target_pairs={{0,3},{1,2},{2,1},{3,0},{4,7},{5,6},{6,5},{7,4},{8,11},{9,10},{10,... | collective-permute-start | bytes 466952 | tf_op jit(solution)/shard_map/ppermute | solution.py:69
  112.6 1.9 %collective-permute-start.26 = (bf16[608,128]{1,0:T(8,128)(2,1)S(1)}, bf16[608,128]{1,0:T(8,128)(2,1)S(1)}, u32[]{:S(2)}, u32[]{:S(2)}) collective-permute-start(bf16[608,128]{1,0:T(8,128)(2,1)S(1)} %slice_select_fusion.refs_0_.refs_4_), channel_id=1, source_target_pairs={{0,1},{1,0},{2,3},{3,2},{4,5},{5,4},{6,7},{7,6},{8,9},{9,8},{10,11... | collective-permute-start | bytes 466952 | tf_op jit(solution)/shard_map/ppermute | solution.py:69
  114.5 1.5 collective-permute-start.16
  116.6 2.4 %collective-permute-done.28 = bf16[608,128]{1,0:T(8,128)(2,1)S(1)} collective-permute-done((bf16[608,128]{1,0:T(8,128)(2,1)S(1)}, bf16[608,128]{1,0:T(8,128)(2,1)S(1)}, u32[]{:S(2)}, u32[]{:S(2)}) %collective-permute-start.28) | collective-permute-done | bytes 155680 | tf_op jit(solution)/shard_map/ppermute | solution.py:69
  119.4 5.1 %collective-permute-done.27 = bf16[608,128]{1,0:T(8,128)(2,1)S(1)} collective-permute-done((bf16[608,128]{1,0:T(8,128)(2,1)S(1)}, bf16[608,128]{1,0:T(8,128)(2,1)S(1)}, u32[]{:S(2)}, u32[]{:S(2)}) %collective-permute-start.27) | collective-permute-done | bytes 155680 | tf_op jit(solution)/shard_map/ppermute | solution.py:69
  124.6 1.4 collective-permute-start.17
  126.0 0.8 pad_maximum_fusion.refs_12_
  127.4 3.7 %collective-permute-done.17.refs_3_.refs_7_ = bf16[608,128]{1,0:T(8,128)(2,1)} collective-permute-done((bf16[608,128]{1,0:T(8,128)(2,1)}, bf16[608,128]{1,0:T(8,128)(2,1)}, u32[]{:S(2)}, u32[]{:S(2)}) %collective-permute-start.17) | collective-permute-done | bytes 155680 | tf_op jit(solution)/shard_map/ppermute | solution.py:47
  131.1 2.0 %residual_rows.1 = f32[608,128]{1,0:T(8,128)S(1)} custom-call(s32[9]{0:T(128)S(1)} %pad_add_fusion.order, bf16[608,2432]{1,0:T(8,128)(2,1)S(1)} %copy-done.1, bf16[608,128]{1,0:T(8,128)(2,1)S(1)} %slice_select_fusion.refs_0_.refs_4_, bf16[608,128]{1,0:T(8,128)(2,1)} %collective-permute-done.15.refs_1_.refs_5_, ...), custom_call_target="tpu_custom_call" | custom-call | flops 378535936 | bytes 4202496 | tf_op jit(solution)/shard_map/residual_rows/pallas_call | solution.py:464
  133.3 1.3 fold.1
  134.6 2.2 %collective-permute-start.21 = (bf16[624,256]{1,0:T(8,128)(2,1)S(1)}, bf16[624,256]{1,0:T(8,128)(2,1)S(1)}, u32[]{:S(2)}, u32[]{:S(2)}) collective-permute-start(bf16[624,256]{1,0:T(8,128)(2,1)S(1)} %get-tuple-element.87), channel_id=1, source_target_pairs={{0,8},{4,12},{8,0},{12,4},{16,20},{20,16},{24,28},{28,24},{1,9},{5... | collective-permute-start | bytes 958472 | tf_op jit(solution)/shard_map/ppermute | solution.py:47
  137.6 1.8 %collective-permute-start.31 = (bf16[3,608,128]{2,1,0:T(8,128)(2,1)}, bf16[3,608,128]{2,1,0:T(8,128)(2,1)S(1)}, u32[]{:S(2)}, u32[]{:S(2)}) collective-permute-start(bf16[3,608,128]{2,1,0:T(8,128)(2,1)} %collective-permute-done.29.refs_13_), channel_id=1, source_target_pairs={{0,8},{4,12},{8,0},{12,4},{16,20},{20,16},{24,28},{28,24},{1,9},{5... | collective-permute-start | bytes 1400840 | tf_op jit(solution)/shard_map/ppermute | solution.py:47
  139.4 0.8 fusion.8
  140.2 1.6 collective-permute-done.21
  142.3 1.1 collective-permute-done.24.refs_10_
  143.5 3.3 %collective-permute-done.30.refs_14_ = bf16[3,608,128]{2,1,0:T(8,128)(2,1)S(1)} collective-permute-done((bf16[3,608,128]{2,1,0:T(8,128)(2,1)}, bf16[3,608,128]{2,1,0:T(8,128)(2,1)S(1)}, u32[]{:S(2)}, u32[]{:S(2)}) %collective-permute-start.30) | collective-permute-done | bytes 466976 | tf_op jit(solution)/shard_map/ppermute | solution.py:47
  146.8 5.0 %collective-permute-done.31.refs_15_ = bf16[3,608,128]{2,1,0:T(8,128)(2,1)S(1)} collective-permute-done((bf16[3,608,128]{2,1,0:T(8,128)(2,1)}, bf16[3,608,128]{2,1,0:T(8,128)(2,1)S(1)}, u32[]{:S(2)}, u32[]{:S(2)}) %collective-permute-start.31) | collective-permute-done | bytes 466976 | tf_op jit(solution)/shard_map/ppermute | solution.py:47
  152.4 2.2 %fusion.5 = f32[1,608,256]{2,1,0:T(8,128)} fusion(f32[608,256]{1,0:T(8,128)S(1)} %get-tuple-element.86, f32[608,128]{1,0:T(8,128)S(1)} %copy-done.27, f32[608,128]{1,0:T(8,128)} %add_add_fusion, bf16[624,256]{1,0:T(8,128)(2,1)S(1)} %collective-permute-done.21, f32[256]{0:T(256)S(1)} %bitcast.26, f32[256]{0:T(256)S(1)} %bitcast.28, f32[256]{0:T(256)S(1)} %bitcast.25, ...), kind=kLoop, calls=%fused_computation.7 | loop fusion | flops 2179072 | bytes 2808197 | tf_op jit(solution)/shard_map/broadcast_in_dim | solution.py:602
  154.6 7.5 %zero_projection_grad.1 = f32[608,2432]{1,0:T(8,128)} custom-call(s32[9]{0:T(128)S(1)} %pad_add_fusion.order, s32[4]{0:T(128)S(1)} %iota_xor_fusion.dp_order, bf16[608,256]{1,0:T(8,128)(2,1)S(1)} %copy-done.16, bf16[608,256]{1,0:T(8,128)(2,1)S(1)} %copy-done.22, bf16[608,256]{1,0:T(8,128)(2,1)S(1)} %copy-done.20, bf16[608,256]{1,0:T(8,128)(2,1)S(1)} %copy-done.18, ...), custom_call_target="tpu_custom_call" | custom-call | flops 3028287488 | bytes 12140544 | tf_op jit(solution)/shard_map/zero_projection_grad/pallas_call | solution.py:505
  (104 shorter events, 7.7 us)
Async XLA Ops:
  0.6 2.0 %collective-permute-start = (bf16[608,256]{1,0:T(8,128)(2,1)}, bf16[608,256]{1,0:T(8,128)(2,1)S(1)}, u32[]{:S(2)}, u32[]{:S(2)}) collective-permute-start(bf16[608,256]{1,0:T(8,128)(2,1)} %bitcast.20), channel_id=1, source_target_pairs={{0,16},{16,0},{1,17},{17,1},{2,18},{18,2},{3,19},{19,3},{4,20},{20... | collective-permute-start | bytes 933896 | tf_op jit(solution)/shard_map/ppermute | solution.py:35
  7.6 16.0 %collective-permute-start.1 = (bf16[608,128]{1,0:T(8,128)(2,1)S(1)}, bf16[608,128]{1,0:T(8,128)(2,1)S(1)}, u32[]{:S(2)}, u32[]{:S(2)}) collective-permute-start(bf16[608,128]{1,0:T(8,128)(2,1)S(1)} %get-tuple-element.46), channel_id=1, source_target_pairs={{0,4},{4,0},{8,12},{12,8},{16,24},{20,28},{24,16},{28,20},{1,5},{5... | collective-permute-start | bytes 466952 | tf_op jit(solution)/shard_map/ppermute | solution.py:63
  10.4 13.3 %collective-permute-start.2 = (bf16[608,128]{1,0:T(8,128)(2,1)S(1)}, bf16[608,128]{1,0:T(8,128)(2,1)S(1)}, u32[]{:S(2)}, u32[]{:S(2)}) collective-permute-start(bf16[608,128]{1,0:T(8,128)(2,1)S(1)} %get-tuple-element.47), channel_id=1, source_target_pairs={{0,8},{4,12},{8,0},{12,4},{16,20},{20,16},{24,28},{28,24},{1,9},{5... | collective-permute-start | bytes 466952 | tf_op jit(solution)/shard_map/ppermute | solution.py:63
  11.9 11.7 %collective-permute-start.3 = (bf16[608,128]{1,0:T(8,128)(2,1)S(1)}, bf16[608,128]{1,0:T(8,128)(2,1)S(1)}, u32[]{:S(2)}, u32[]{:S(2)}) collective-permute-start(bf16[608,128]{1,0:T(8,128)(2,1)S(1)} %get-tuple-element.48), channel_id=1, source_target_pairs={{0,12},{4,8},{8,4},{12,0},{16,28},{20,24},{24,20},{28,16},{1,13},{... | collective-permute-start | bytes 466952 | tf_op jit(solution)/shard_map/ppermute | solution.py:63
  23.7 24.1 %copy-start.2 = (f32[1024,256]{1,0:T(8,128)}, f32[1024,256]{1,0:T(8,128)S(1)}, u32[]{:S(2)}) copy-start(f32[1024,256]{1,0:T(8,128)S(1)} %get-tuple-element.70.refs_4_.slope_a) | copy-start | bytes 3145732
  24.5 1.8 %collective-permute-start.4 = (f32[608,128]{1,0:T(8,128)}, f32[608,128]{1,0:T(8,128)S(1)}, u32[]{:S(2)}, u32[]{:S(2)}) collective-permute-start(f32[608,128]{1,0:T(8,128)} %add_add_fusion), channel_id=1, source_target_pairs={{0,16},{16,0},{1,17},{17,1},{2,18},{18,2},{3,19},{19,3},{4,20},{20... | collective-permute-start | bytes 933896 | tf_op jit(solution)/shard_map/ppermute | solution.py:35
  24.5 7.3 %copy-start.8 = (bf16[2432,256]{1,0:T(8,128)(2,1)S(1)}, bf16[2432,256]{1,0:T(8,128)(2,1)}, u32[]{:S(2)}) copy-start(bf16[2432,256]{1,0:T(8,128)(2,1)} %copy-done.7) | copy-start | bytes 3735556
  28.2 19.5 %collective-permute-start.10 = (bf16[608,256]{1,0:T(8,128)(2,1)S(1)}, bf16[608,256]{1,0:T(8,128)(2,1)S(1)}, u32[]{:S(2)}, u32[]{:S(2)}) collective-permute-start(bf16[608,256]{1,0:T(8,128)(2,1)S(1)} %multiply_convert_fusion.refs_0_), channel_id=1, source_target_pairs={{0,12},{4,8},{8,4},{12,0},{16,28},{20,24},{24,20},{28,16},{1,13},{... | collective-permute-start | bytes 933896 | tf_op jit(solution)/shard_map/ppermute | solution.py:63
  31.2 16.6 %collective-permute-start.9 = (bf16[608,256]{1,0:T(8,128)(2,1)S(1)}, bf16[608,256]{1,0:T(8,128)(2,1)S(1)}, u32[]{:S(2)}, u32[]{:S(2)}) collective-permute-start(bf16[608,256]{1,0:T(8,128)(2,1)S(1)} %multiply_convert_fusion.refs_0_), channel_id=1, source_target_pairs={{0,8},{4,12},{8,0},{12,4},{16,20},{20,16},{24,28},{28,24},{1,9},{5... | collective-permute-start | bytes 933896 | tf_op jit(solution)/shard_map/ppermute | solution.py:63
  31.7 16.1 %collective-permute-start.8 = (bf16[608,256]{1,0:T(8,128)(2,1)S(1)}, bf16[608,256]{1,0:T(8,128)(2,1)S(1)}, u32[]{:S(2)}, u32[]{:S(2)}) collective-permute-start(bf16[608,256]{1,0:T(8,128)(2,1)S(1)} %multiply_convert_fusion.refs_0_), channel_id=1, source_target_pairs={{0,4},{4,0},{8,12},{12,8},{16,24},{20,28},{24,16},{28,20},{1,5},{5... | collective-permute-start | bytes 933896 | tf_op jit(solution)/shard_map/ppermute | solution.py:63
  44.2 14.8 %collective-permute-start.5 = (bf16[608,256]{1,0:T(8,128)(2,1)S(1)}, bf16[608,256]{1,0:T(8,128)(2,1)S(1)}, u32[]{:S(2)}, u32[]{:S(2)}) collective-permute-start(bf16[608,256]{1,0:T(8,128)(2,1)S(1)} %get-tuple-element.60), channel_id=1, source_target_pairs={{0,4},{4,0},{8,12},{12,8},{16,24},{20,28},{24,16},{28,20},{1,5},{5... | collective-permute-start | bytes 933896 | tf_op jit(solution)/shard_map/ppermute | solution.py:63
  46.2 12.8 %collective-permute-start.6 = (bf16[608,256]{1,0:T(8,128)(2,1)S(1)}, bf16[608,256]{1,0:T(8,128)(2,1)S(1)}, u32[]{:S(2)}, u32[]{:S(2)}) collective-permute-start(bf16[608,256]{1,0:T(8,128)(2,1)S(1)} %get-tuple-element.61), channel_id=1, source_target_pairs={{0,8},{4,12},{8,0},{12,4},{16,20},{20,16},{24,28},{28,24},{1,9},{5... | collective-permute-start | bytes 933896 | tf_op jit(solution)/shard_map/ppermute | solution.py:63
  47.7 13.3 %collective-permute-start.7 = (bf16[608,256]{1,0:T(8,128)(2,1)S(1)}, bf16[608,256]{1,0:T(8,128)(2,1)S(1)}, u32[]{:S(2)}, u32[]{:S(2)}) collective-permute-start(bf16[608,256]{1,0:T(8,128)(2,1)S(1)} %get-tuple-element.62), channel_id=1, source_target_pairs={{0,12},{4,8},{8,4},{12,0},{16,28},{20,24},{24,20},{28,16},{1,13},{... | collective-permute-start | bytes 933896 | tf_op jit(solution)/shard_map/ppermute | solution.py:63
  61.0 34.6 %copy-start.3 = (f32[1024,256]{1,0:T(8,128)S(1)}, f32[1024,256]{1,0:T(8,128)}, u32[]{:S(2)}) copy-start(f32[1024,256]{1,0:T(8,128)} %copy-done.2) | copy-start | bytes 3145732
  63.1 32.5 %copy-start.23 = (bf16[608,256]{1,0:T(8,128)(2,1)}, bf16[608,256]{1,0:T(8,128)(2,1)S(1)}, u32[]{:S(2)}) copy-start(bf16[608,256]{1,0:T(8,128)(2,1)S(1)} %get-tuple-element.91) | copy-start | bytes 933892
  63.1 4.5 %collective-permute-start.11 = (bf16[608,128]{1,0:T(8,128)(2,1)S(1)}, bf16[608,128]{1,0:T(8,128)(2,1)S(1)}, u32[]{:S(2)}, u32[]{:S(2)}) collective-permute-start(bf16[608,128]{1,0:T(8,128)(2,1)S(1)} %slice.65), channel_id=1, source_target_pairs={{0,16},{16,0},{1,17},{17,1},{2,18},{18,2},{3,19},{19,3},{4,20},{20... | collective-permute-start | bytes 466952 | tf_op jit(solution)/shard_map/ppermute | solution.py:35
  63.2 12.2 %collective-permute-start.14 = (bf16[608,256]{1,0:T(8,128)(2,1)S(1)}, bf16[608,256]{1,0:T(8,128)(2,1)S(1)}, u32[]{:S(2)}, u32[]{:S(2)}) collective-permute-start(bf16[608,256]{1,0:T(8,128)(2,1)S(1)} %copy-done.15), channel_id=1, source_target_pairs={{0,3},{1,2},{2,1},{3,0},{4,7},{5,6},{6,5},{7,4},{8,11},{9,10},{10,... | collective-permute-start | bytes 933896 | tf_op jit(solution)/shard_map/ppermute | solution.py:69
  67.0 27.1 %collective-permute-start.13 = (bf16[608,256]{1,0:T(8,128)(2,1)S(1)}, bf16[608,256]{1,0:T(8,128)(2,1)S(1)}, u32[]{:S(2)}, u32[]{:S(2)}) collective-permute-start(bf16[608,256]{1,0:T(8,128)(2,1)S(1)} %copy-done.15), channel_id=1, source_target_pairs={{0,2},{1,3},{2,0},{3,1},{4,6},{5,7},{6,4},{7,5},{8,10},{9,11},{10,... | collective-permute-start | bytes 933896 | tf_op jit(solution)/shard_map/ppermute | solution.py:69
  67.0 27.8 %collective-permute-start.12 = (bf16[608,256]{1,0:T(8,128)(2,1)S(1)}, bf16[608,256]{1,0:T(8,128)(2,1)S(1)}, u32[]{:S(2)}, u32[]{:S(2)}) collective-permute-start(bf16[608,256]{1,0:T(8,128)(2,1)S(1)} %copy-done.15), channel_id=1, source_target_pairs={{0,1},{1,0},{2,3},{3,2},{4,5},{5,4},{6,7},{7,6},{8,9},{9,8},{10,11... | collective-permute-start | bytes 933896 | tf_op jit(solution)/shard_map/ppermute | solution.py:69
  95.6 35.5 %copy-start.1 = (bf16[608,2432]{1,0:T(8,128)(2,1)S(1)}, bf16[608,2432]{1,0:T(8,128)(2,1)}, u32[]{:S(2)}) copy-start(bf16[608,2432]{1,0:T(8,128)(2,1)} %weight.3) | copy-start | bytes 8871940
  108.6 7.4 %collective-permute-start.15 = (bf16[608,128]{1,0:T(8,128)(2,1)S(1)}, bf16[608,128]{1,0:T(8,128)(2,1)}, u32[]{:S(2)}, u32[]{:S(2)}) collective-permute-start(bf16[608,128]{1,0:T(8,128)(2,1)S(1)} %slice_select_fusion.refs_0_.refs_4_), channel_id=1, source_target_pairs={{0,4},{4,0},{8,12},{12,8},{16,24},{20,28},{24,16},{28,20},{1,5},{5... | collective-permute-start | bytes 466952 | tf_op jit(solution)/shard_map/ppermute | solution.py:47
  110.1 8.8 %collective-permute-start.28 = (bf16[608,128]{1,0:T(8,128)(2,1)S(1)}, bf16[608,128]{1,0:T(8,128)(2,1)S(1)}, u32[]{:S(2)}, u32[]{:S(2)}) collective-permute-start(bf16[608,128]{1,0:T(8,128)(2,1)S(1)} %slice_select_fusion.refs_0_.refs_4_), channel_id=1, source_target_pairs={{0,3},{1,2},{2,1},{3,0},{4,7},{5,6},{6,5},{7,4},{8,11},{9,10},{10,... | collective-permute-start | bytes 466952 | tf_op jit(solution)/shard_map/ppermute | solution.py:69
  112.6 12.0 %collective-permute-start.27 = (bf16[608,128]{1,0:T(8,128)(2,1)S(1)}, bf16[608,128]{1,0:T(8,128)(2,1)S(1)}, u32[]{:S(2)}, u32[]{:S(2)}) collective-permute-start(bf16[608,128]{1,0:T(8,128)(2,1)S(1)} %slice_select_fusion.refs_0_.refs_4_), channel_id=1, source_target_pairs={{0,2},{1,3},{2,0},{3,1},{4,6},{5,7},{6,4},{7,5},{8,10},{9,11},{10,... | collective-permute-start | bytes 466952 | tf_op jit(solution)/shard_map/ppermute | solution.py:69
  112.6 13.4 %collective-permute-start.26 = (bf16[608,128]{1,0:T(8,128)(2,1)S(1)}, bf16[608,128]{1,0:T(8,128)(2,1)S(1)}, u32[]{:S(2)}, u32[]{:S(2)}) collective-permute-start(bf16[608,128]{1,0:T(8,128)(2,1)S(1)} %slice_select_fusion.refs_0_.refs_4_), channel_id=1, source_target_pairs={{0,1},{1,0},{2,3},{3,2},{4,5},{5,4},{6,7},{7,6},{8,9},{9,8},{10,11... | collective-permute-start | bytes 466952 | tf_op jit(solution)/shard_map/ppermute | solution.py:69
  114.5 12.9 %collective-permute-start.16 = (bf16[608,128]{1,0:T(8,128)(2,1)S(1)}, bf16[608,128]{1,0:T(8,128)(2,1)}, u32[]{:S(2)}, u32[]{:S(2)}) collective-permute-start(bf16[608,128]{1,0:T(8,128)(2,1)S(1)} %slice_select_fusion.refs_0_.refs_4_), channel_id=1, source_target_pairs={{0,8},{4,12},{8,0},{12,4},{16,20},{20,16},{24,28},{28,24},{1,9},{5... | collective-permute-start | bytes 466952 | tf_op jit(solution)/shard_map/ppermute | solution.py:47
  116.0 17.2 %collective-permute-start.19 = (bf16[624,256]{1,0:T(8,128)(2,1)}, bf16[624,256]{1,0:T(8,128)(2,1)}, u32[]{:S(2)}, u32[]{:S(2)}) collective-permute-start(bf16[624,256]{1,0:T(8,128)(2,1)} %get-tuple-element.80), channel_id=1, source_target_pairs={{0,4},{4,0},{8,12},{12,8},{16,24},{20,28},{24,16},{28,20},{1,5},{5... | collective-permute-start | bytes 958472 | tf_op jit(solution)/shard_map/ppermute | solution.py:47
  118.9 14.3 %collective-permute-start.20 = (bf16[624,256]{1,0:T(8,128)(2,1)}, bf16[624,256]{1,0:T(8,128)(2,1)}, u32[]{:S(2)}, u32[]{:S(2)}) collective-permute-start(bf16[624,256]{1,0:T(8,128)(2,1)} %get-tuple-element.82), channel_id=1, source_target_pairs={{0,4},{4,0},{8,12},{12,8},{16,24},{20,28},{24,16},{28,20},{1,5},{5... | collective-permute-start | bytes 958472 | tf_op jit(solution)/shard_map/ppermute | solution.py:47
  124.6 6.5 %collective-permute-start.17 = (bf16[608,128]{1,0:T(8,128)(2,1)}, bf16[608,128]{1,0:T(8,128)(2,1)}, u32[]{:S(2)}, u32[]{:S(2)}) collective-permute-start(bf16[608,128]{1,0:T(8,128)(2,1)} %collective-permute-done.15.refs_1_.refs_5_), channel_id=1, source_target_pairs={{0,8},{4,12},{8,0},{12,4},{16,20},{20,16},{24,28},{28,24},{1,9},{5... | collective-permute-start | bytes 466952 | tf_op jit(solution)/shard_map/ppermute | solution.py:47
  126.8 10.7 %collective-permute-start.29 = (bf16[3,608,128]{2,1,0:T(8,128)(2,1)}, bf16[3,608,128]{2,1,0:T(8,128)(2,1)}, u32[]{:S(2)}, u32[]{:S(2)}) collective-permute-start(bf16[3,608,128]{2,1,0:T(8,128)(2,1)} %pad_maximum_fusion.refs_12_), channel_id=1, source_target_pairs={{0,4},{4,0},{8,12},{12,8},{16,24},{20,28},{24,16},{28,20},{1,5},{5... | collective-permute-start | bytes 1400840 | tf_op jit(solution)/shard_map/ppermute | solution.py:47
  133.2 6.2 %copy-start.24 = (bf16[608,256]{1,0:T(8,128)(2,1)S(1)}, bf16[608,256]{1,0:T(8,128)(2,1)}, u32[]{:S(2)}) copy-start(bf16[608,256]{1,0:T(8,128)(2,1)} %copy-done.23) | copy-start | bytes 933892
  133.2 6.2 %copy-start.25 = (f32[608,256]{1,0:T(8,128)S(1)}, f32[608,256]{1,0:T(8,128)}, u32[]{:S(2)}) copy-start(f32[608,256]{1,0:T(8,128)} %get-tuple-element.92) | copy-start | bytes 1867780
  133.2 4.1 %collective-permute-start.18 = (f32[608,128]{1,0:T(8,128)S(1)}, f32[608,128]{1,0:T(8,128)S(1)}, u32[]{:S(2)}, u32[]{:S(2)}) collective-permute-start(f32[608,128]{1,0:T(8,128)S(1)} %residual_rows.1), channel_id=1, source_target_pairs={{0,16},{16,0},{1,17},{17,1},{2,18},{18,2},{3,19},{19,3},{4,20},{20... | collective-permute-start | bytes 933896 | tf_op jit(solution)/shard_map/ppermute | solution.py:35
  133.3 19.1 %copy-start.27 = (f32[608,128]{1,0:T(8,128)S(1)}, f32[608,128]{1,0:T(8,128)}, u32[]{:S(2)}) copy-start(f32[608,128]{1,0:T(8,128)} %copy-done.26) | copy-start | bytes 933892
  134.6 7.1 %collective-permute-start.21 = (bf16[624,256]{1,0:T(8,128)(2,1)S(1)}, bf16[624,256]{1,0:T(8,128)(2,1)S(1)}, u32[]{:S(2)}, u32[]{:S(2)}) collective-permute-start(bf16[624,256]{1,0:T(8,128)(2,1)S(1)} %get-tuple-element.87), channel_id=1, source_target_pairs={{0,8},{4,12},{8,0},{12,4},{16,20},{20,16},{24,28},{28,24},{1,9},{5... | collective-permute-start | bytes 958472 | tf_op jit(solution)/shard_map/ppermute | solution.py:47
  136.8 5.0 %collective-permute-start.22 = (bf16[608,128]{1,0:T(8,128)(2,1)S(1)}, bf16[608,128]{1,0:T(8,128)(2,1)S(1)}, u32[]{:S(2)}, u32[]{:S(2)}) collective-permute-start(bf16[608,128]{1,0:T(8,128)(2,1)S(1)} %slice_select_fusion.refs_0_.refs_4_), channel_id=1, source_target_pairs={{0,16},{16,0},{1,17},{17,1},{2,18},{18,2},{3,19},{19,3},{4,20},{20... | collective-permute-start | bytes 466952 | tf_op jit(solution)/shard_map/ppermute | solution.py:35
  137.0 17.5 %collective-permute-start.32 = (bf16[3,608,128]{2,1,0:T(8,128)(2,1)}, bf16[3,608,128]{2,1,0:T(8,128)(2,1)S(1)}, u32[]{:S(2)}, u32[]{:S(2)}) collective-permute-start(bf16[3,608,128]{2,1,0:T(8,128)(2,1)} %pad_maximum_fusion.refs_12_), channel_id=1, source_target_pairs={{0,16},{16,0},{1,17},{17,1},{2,18},{18,2},{3,19},{19,3},{4,20},{20... | collective-permute-start | bytes 1400840 | tf_op jit(solution)/shard_map/ppermute | solution.py:35
  137.3 9.5 %collective-permute-start.30 = (bf16[3,608,128]{2,1,0:T(8,128)(2,1)}, bf16[3,608,128]{2,1,0:T(8,128)(2,1)S(1)}, u32[]{:S(2)}, u32[]{:S(2)}) collective-permute-start(bf16[3,608,128]{2,1,0:T(8,128)(2,1)} %pad_maximum_fusion.refs_12_), channel_id=1, source_target_pairs={{0,8},{4,12},{8,0},{12,4},{16,20},{20,16},{24,28},{28,24},{1,9},{5... | collective-permute-start | bytes 1400840 | tf_op jit(solution)/shard_map/ppermute | solution.py:47
  137.6 14.2 %collective-permute-start.31 = (bf16[3,608,128]{2,1,0:T(8,128)(2,1)}, bf16[3,608,128]{2,1,0:T(8,128)(2,1)S(1)}, u32[]{:S(2)}, u32[]{:S(2)}) collective-permute-start(bf16[3,608,128]{2,1,0:T(8,128)(2,1)} %collective-permute-done.29.refs_13_), channel_id=1, source_target_pairs={{0,8},{4,12},{8,0},{12,4},{16,20},{20,16},{24,28},{28,24},{1,9},{5... | collective-permute-start | bytes 1400840 | tf_op jit(solution)/shard_map/ppermute | solution.py:47
  140.2 14.4 %copy-start.16 = (bf16[608,256]{1,0:T(8,128)(2,1)S(1)}, bf16[608,256]{1,0:T(8,128)(2,1)}, u32[]{:S(2)}) copy-start(bf16[608,256]{1,0:T(8,128)(2,1)} %copy-done.14) | copy-start | bytes 933892
  140.2 14.4 %copy-start.18 = (bf16[608,256]{1,0:T(8,128)(2,1)S(1)}, bf16[608,256]{1,0:T(8,128)(2,1)}, u32[]{:S(2)}) copy-start(bf16[608,256]{1,0:T(8,128)(2,1)} %copy-done.17) | copy-start | bytes 933892
  140.2 14.4 %copy-start.20 = (bf16[608,256]{1,0:T(8,128)(2,1)S(1)}, bf16[608,256]{1,0:T(8,128)(2,1)}, u32[]{:S(2)}) copy-start(bf16[608,256]{1,0:T(8,128)(2,1)} %copy-done.19) | copy-start | bytes 933892
  140.2 14.4 %copy-start.22 = (bf16[608,256]{1,0:T(8,128)(2,1)S(1)}, bf16[608,256]{1,0:T(8,128)(2,1)}, u32[]{:S(2)}) copy-start(bf16[608,256]{1,0:T(8,128)(2,1)} %copy-done.21) | copy-start | bytes 933892
  141.8 1.6 collective-permute-start.24
  141.8 10.0 %collective-permute-start.23 = (bf16[608,128]{1,0:T(8,128)(2,1)}, bf16[608,128]{1,0:T(8,128)(2,1)S(1)}, u32[]{:S(2)}, u32[]{:S(2)}) collective-permute-start(bf16[608,128]{1,0:T(8,128)(2,1)} %collective-permute-done.15.refs_1_.refs_5_), channel_id=1, source_target_pairs={{0,16},{16,0},{1,17},{17,1},{2,18},{18,2},{3,19},{19,3},{4,20},{20... | collective-permute-start | bytes 466952 | tf_op jit(solution)/shard_map/ppermute | solution.py:35
  143.4 11.2 %collective-permute-start.33 = (bf16[3,608,128]{2,1,0:T(8,128)(2,1)}, bf16[3,608,128]{2,1,0:T(8,128)(2,1)S(1)}, u32[]{:S(2)}, u32[]{:S(2)}) collective-permute-start(bf16[3,608,128]{2,1,0:T(8,128)(2,1)} %collective-permute-done.29.refs_13_), channel_id=1, source_target_pairs={{0,16},{16,0},{1,17},{17,1},{2,18},{18,2},{3,19},{19,3},{4,20},{20... | collective-permute-start | bytes 1400840 | tf_op jit(solution)/shard_map/ppermute | solution.py:35
  146.8 7.8 %collective-permute-start.34 = (bf16[3,608,128]{2,1,0:T(8,128)(2,1)S(1)}, bf16[3,608,128]{2,1,0:T(8,128)(2,1)S(1)}, u32[]{:S(2)}, u32[]{:S(2)}) collective-permute-start(bf16[3,608,128]{2,1,0:T(8,128)(2,1)S(1)} %collective-permute-done.30.refs_14_), channel_id=1, source_target_pairs={{0,16},{16,0},{1,17},{17,1},{2,18},{18,2},{3,19},{19,3},{4,20},{20... | collective-permute-start | bytes 1400840 | tf_op jit(solution)/shard_map/ppermute | solution.py:35
  151.8 2.8 %collective-permute-start.35 = (bf16[3,608,128]{2,1,0:T(8,128)(2,1)S(1)}, bf16[3,608,128]{2,1,0:T(8,128)(2,1)S(1)}, u32[]{:S(2)}, u32[]{:S(2)}) collective-permute-start(bf16[3,608,128]{2,1,0:T(8,128)(2,1)S(1)} %collective-permute-done.31.refs_15_), channel_id=1, source_target_pairs={{0,16},{16,0},{1,17},{17,1},{2,18},{18,2},{3,19},{19,3},{4,20},{20... | collective-permute-start | bytes 1400840 | tf_op jit(solution)/shard_map/ppermute | solution.py:35
  151.8 2.8 %collective-permute-start.25 = (bf16[608,128]{1,0:T(8,128)(2,1)}, bf16[608,128]{1,0:T(8,128)(2,1)S(1)}, u32[]{:S(2)}, u32[]{:S(2)}) collective-permute-start(bf16[608,128]{1,0:T(8,128)(2,1)} %collective-permute-done.17.refs_3_.refs_7_), channel_id=1, source_target_pairs={{0,16},{16,0},{1,17},{17,1},{2,18},{18,2},{3,19},{19,3},{4,20},{20... | collective-permute-start | bytes 466952 | tf_op jit(solution)/shard_map/ppermute | solution.py:35
  (16 other events, 35.2 us)

commit v5 on v4

--- a/solution.py
+++ b/solution.py
@@ -180,7 +180,11 @@
     for start, size in parts:
         rows = pl.ds(start, size)
         xhat = (acts[0, rows, :].astype(F32) - mean) * inv
-        normed[rows, :] = (xhat * (1.0 + mod[rows, 1:2]) + mod[rows, 0:1]).astype(BF16)
+        normed[:, rows] = (xhat * (1.0 + mod[rows, 1:2]) + mod[rows, 0:1]).T.astype(BF16)
+
+
+def against_rows(columns, weight):
+    return lax.dot_general(columns, weight, (((1,), (1,)), ((), ())), preferred_element_type=F32)
 
 
 def accumulate(total, part, weight, before, finish):
@@ -200,21 +204,21 @@
 
     def product(at, size):
         stream.take()
-        return jnp.dot(in_buf[pl.ds(at - base, size), :], normed[...], preferred_element_type=F32)
+        return against_rows(normed[...], in_buf[pl.ds(at - base, size), :])
 
     def finish(at, size, pre, final):
         rows = pl.ds(at - base, size)
         hidden, slope = gelu_and_slope(pre)
-        slope_out[rows, :] = slope
+        slope_out[:, rows] = slope
         stream.take()
-        accumulate(total, hidden.T.astype(BF16), out_buf.at[rows, :], state[0], last if final else None)
+        accumulate(total, hidden.astype(BF16), out_buf.at[rows, :], state[0], last if final else None)
         state[0] = total
 
     pipelined(parts, product, finish)
 
 
 def forward_first_kernel(acts, modulation, w_in, w_out, mod, normed, stats, slope_out, total, in_buf, out_buf, sems):
-    parts = pieces(0, slope_out.shape[0])
+    parts = pieces(0, slope_out.shape[1])
     stream = Stream(w_in, in_buf, w_out, out_buf, parts, 0, sems)
     turn_modulation(modulation, mod)
     normalize(acts, mod, normed, stats)
@@ -223,7 +227,7 @@
 
 def forward_last_kernel(start, order, normed, before, w_in, w_out, slope_out, *refs):
     outs, (in_buf, out_buf, total, full, sems) = refs[:-5], refs[-5:]
-    parts = pieces(start, start + slope_out.shape[0])
+    parts = pieces(start, start + slope_out.shape[1])
     stream = Stream(w_in, in_buf, w_out, out_buf, parts, start, sems)
 
     def last(at, size, value):
@@ -250,9 +254,9 @@
         forward_first_kernel,
         out_shape=(
             struct((features, 8), F32),
-            struct((features, tokens), BF16),
+            struct((tokens, features), BF16),
             struct((2, tokens), F32),
-            struct((part, tokens), F32),
+            struct((tokens, part), F32),
             struct((tokens, features), F32),
         ),
         in_specs=[WHOLE, WHOLE, HELD, HELD],
@@ -268,7 +272,7 @@
     tokens, part, rows = before.shape[0], hidden - start, features // blocks
     slope, *outs = pl.pallas_call(
         functools.partial(forward_last_kernel, start),
-        out_shape=[struct((part, tokens), F32), struct((rows, tokens), F32)]
+        out_shape=[struct((tokens, part), F32), struct((rows, tokens), F32)]
         + [struct((rows, tokens), BF16)] * (blocks - 1),
         in_specs=[SCALARS, WHOLE, WHOLE, HELD, HELD],
         out_specs=[WHOLE] * (blocks + 1),
@@ -296,25 +300,28 @@
 
     def product(at, size):
         stream.take()
-        return jnp.dot(out_buf[pl.ds(at - base, size), :], grad[...], preferred_element_type=F32)
+        return against_rows(grad[...], out_buf[pl.ds(at - base, size), :])
 
     def finish(at, size, value, final):
         rows = pl.ds(at - base, size)
-        seen = slopes[0].shape[0]
-        slope = slopes[0][pl.ds(at, size), :] if at < seen else slopes[1][pl.ds(at - seen, size), :]
+        seen = slopes[0].shape[1]
+        slope = slopes[0][:, pl.ds(at, size)] if at < seen else slopes[1][:, pl.ds(at - seen, size)]
         stream.take()
-        accumulate(total, (value * slope).T.astype(BF16), in_buf.at[rows, :], state[0], last if final else None)
+        accumulate(total, (value * slope).astype(BF16), in_buf.at[rows, :], state[0], last if final else None)
         state[0] = total
 
     pipelined(parts, product, finish)
 
 
 def backward_first_kernel(blocks, part, order, *refs):
-    pieces_in, (slope_a, slope_b, w_in, w_out, grad, total, in_buf, out_buf, stage, sems) = refs[:blocks], refs[blocks:]
+    pieces_in, (slope_a, slope_b, w_in, w_out, grad, total, in_buf, out_buf, full, stage, sems) = refs[:blocks], refs[blocks:]
     parts = pieces(0, part)
     stream = Stream(w_out, out_buf, w_in, in_buf, parts, 0, sems)
     values = [lambda ref=ref: ref[...] for ref in pieces_in]
-    place_blocks(grad, slice(None), stage, order, values, pieces_in[0].shape[0])
+    place_blocks(full, slice(None), stage, order, values, pieces_in[0].shape[0])
+    for start, size in pieces(0, full.shape[0], 128):
+        rows = pl.ds(start, size)
+        grad[:, rows] = full[rows, :].astype(F32).T.astype(BF16)
     backward_products(stream, parts, 0, grad, (slope_a, slope_b), in_buf, out_buf, total, None, None)
 
 
@@ -323,11 +330,15 @@
     blocks, (rows, tokens) = len(gathered), gathered[0].shape
     return pl.pallas_call(
         functools.partial(backward_first_kernel, blocks, part),
-        out_shape=(struct((features, tokens), BF16), struct((tokens, features), F32)),
+        out_shape=(struct((tokens, features), BF16), struct((tokens, features), F32)),
         in_specs=[SCALARS] + [WHOLE] * (blocks + 2) + [HELD, HELD],
         out_specs=[WHOLE] * 2,
         scratch_shapes=layer_scratch(part, features)
-        + [staging(rows, features, tokens), pltpu.SemaphoreType.DMA((2 * len(pieces(0, part)),))],
+        + [
+            pltpu.VMEM((features, tokens), BF16),
+            staging(rows, features, tokens),
+            pltpu.SemaphoreType.DMA((2 * len(pieces(0, part)),)),
+        ],
         name=name,
         **layer_params(part, features, tokens, 0),
     )(order, *gathered, slope_a, slope_b, w_in, w_out)
@@ -563,7 +574,7 @@
     gathered = [grad_rows] + direct([grad_rows] * (blocks - 1), kept)
     cots = gather_dp(cot1_rows)
     grad, total = backward_first(
-        order, after(gathered, *sent), slope_a, slope_b, w_in, w_out, cut, "backward_first"
+        order, after(gathered, *sent, *cots), slope_a, slope_b, w_in, w_out, cut, "backward_first"
     )
     got = direct(sent, total)
     own_values = block_of(acts[0], me, rows).astype(F32)
@@ -573,10 +584,11 @@
     out_half = jnp.where(is_control, out_rows[:, :half], swap_grp(out_rows[:, half:]))
     far = gather_dp(out_half)[1:]
     sent, kept, token_sums = backward_last(
-        order, after(grad, out_half, *cots), total, slope_a, slope_b, acts, stats, mod, w_in, w_out, cut, blocks, "backward_last"
-    )
-    near = [after(out_half, sent[0])]
-    for level in range(levels):
+        order, after(grad, out_half), total, slope_a, slope_b, acts, stats, mod, w_in, w_out, cut, blocks, "backward_last"
+    )
+    near = [out_half, step(out_half, 0)]
+    far, near, sent, kept, token_sums = lax.optimization_barrier((far, near, sent, kept, token_sums))
+    for level in range(1, levels):
         near = near + steps(near, level)
     near_other = [swap_grp(value) for value in near]
     residual = residual_rows(order, zero_weight, near)

time: 163 us -> 132 us (0.81)
  waiting for transfers between devices: 51.2 us -> 28.3 us
  Pallas kernels: 57.8 us -> 53.1 us
  local copies, waits for them, and re-layouts: 10 us -> 6.41 us
    ppermute x6, waiting for transfers between devices: 33.2 us -> 5.08 us  [gather_dp(): lax.ppermute(value, 'dp', [(i, i ^ mask) for i in range(length)])]
    ppermute x9, waiting for transfers between devices: 13.5 us -> 17.3 us  [step(): return lax.ppermute(value, ('grp', 'fsdp'), pairs)]
    unnamed x57 -> x55, local copies, waits for them, and re-layouts: 9.98 us -> 6.39 us
    ppermute x9, starting transfers between devices: 11.5 us -> 13.4 us  [send(): return lax.ppermute(value, ('grp', 'fsdp'), pairs)]
    ppermute x9, starting transfers between devices: 10.2 us -> 8.58 us  [step(): return lax.ppermute(value, ('grp', 'fsdp'), pairs)]
  transfers between devices with their start and end apart: 36 -> 36, of which waited for: 11 -> 11; matrix products, arithmetic and copies ran while one was open for 4% -> 4% of each run, Pallas kernels for 23% -> 34%
where the time goes in v5:
time: 132 us; the launch traced here: 131 us
  Pallas kernels  53.1 us (40%)
  starting transfers between devices  33.6 us (25%)
  waiting for transfers between devices  28.3 us (21%)
  other arithmetic  8.57 us (6%)
  local copies, waits for them, and re-layouts  6.41 us (5%)
    ppermute x9, waiting for transfers between devices, step(): return lax.ppermute(value, ('grp', 'fsdp'), pairs)  17.3 us
    ppermute x9, starting transfers between devices, send(): return lax.ppermute(value, ('grp', 'fsdp'), pairs)  13.4 us
    pallas_call x1, Pallas kernels, forward_last(): pl.pallas_call(functools.partial(forward_last_kernel, start), out_shape=[...  11.3 us
    pallas_call x1, Pallas kernels, backward_last(): pl.pallas_call(functools.partial(backward_last_kernel, start, rows), out_...  10.4 us
    pallas_call x1, Pallas kernels, backward_first(): pl.pallas_call(functools.partial(backward_first_kernel, blocks, part), ou...  10.1 us
    pallas_call x1, Pallas kernels, forward_first(): pl.pallas_call(forward_first_kernel, out_shape=(struct((features, 8), F32...  9.09 us
    ppermute x6, starting transfers between devices, gather_dp(): lax.ppermute(value, 'dp', [(i, i ^ mask) for i in range(length)])  8.77 us
    ppermute x9, starting transfers between devices, step(): return lax.ppermute(value, ('grp', 'fsdp'), pairs)  8.58 us
  transfers between devices with their start and end apart: 36, of which 11 were waited for; matrix products, arithmetic and copies ran while one was open for 4% of the time, Pallas kernels for 34%

profile of v5, /device:TPU:0, one launch (start us, length us, event | category | flops | bytes accessed | tf_op | source)
XLA Modules:
  0.0 131.2 jit_solution(13197478252739222315)
XLA Ops:
  1.1 0.8 copy.12.modulation
  1.9 0.7 fusion.14
  2.7 1.8 %copy-done = bf16[608,2432]{1,0:T(8,128)(2,1)S(1)} copy-done((bf16[608,2432]{1,0:T(8,128)(2,1)S(1)}, bf16[608,2432]{1,0:T(8,128)(2,1)}, u32[]{:S(2)}) %copy-start) | copy-done | bytes 2957336
  4.5 1.0 copy-done.5
  5.5 1.4 %upstream_terms.1 = (f32[608,128]{1,0:T(8,128)S(1)}, bf16[608,128]{1,0:T(8,128)(2,1)S(1)}, bf16[608,128]{1,0:T(8,128)(2,1)S(1)}, bf16[608,128]{1,0:T(8,128)(2,1)...) custom-call(s32[9]{0:T(128)S(1)} %pad_add_fusion.order, bf16[608,2432]{1,0:T(8,128)(2,1)S(1)} %copy-done, ...), custom_call_target="tpu_custom_call" | custom-call | flops 378535936 | bytes 4202496 | tf_op jit(solution)/shard_map/upstream_terms/pallas_call | solution.py:452
  6.9 2.9 %collective-permute-start.1 = (bf16[608,128]{1,0:T(8,128)(2,1)S(1)}, bf16[608,128]{1,0:T(8,128)(2,1)S(1)}, u32[]{:S(2)}, u32[]{:S(2)}) collective-permute-start(bf16[608,128]{1,0:T(8,128)(2,1)S(1)} %get-tuple-element.55), channel_id=1, source_target_pairs={{0,4},{4,0},{8,12},{12,8},{16,24},{20,28},{24,16},{28,20},{1,5},{5... | collective-permute-start | bytes 466952 | tf_op jit(solution)/shard_map/ppermute | solution.py:63
  9.8 1.5 %collective-permute-start.2 = (bf16[608,128]{1,0:T(8,128)(2,1)S(1)}, bf16[608,128]{1,0:T(8,128)(2,1)S(1)}, u32[]{:S(2)}, u32[]{:S(2)}) collective-permute-start(bf16[608,128]{1,0:T(8,128)(2,1)S(1)} %get-tuple-element.56), channel_id=1, source_target_pairs={{0,8},{4,12},{8,0},{12,4},{16,20},{20,16},{24,28},{28,24},{1,9},{5... | collective-permute-start | bytes 466952 | tf_op jit(solution)/shard_map/ppermute | solution.py:63
  11.3 9.1 %forward_first.1 = (f32[2432,8]{1,0:T(8,128)S(1)}, bf16[256,2432]{1,0:T(8,128)(2,1)S(1)}, f32[2,256]{1,0:T(2,128)S(1)}, f32[256,1024]{1,0:T(8,128)S(1)}, f32[256,2432]{1,0:T(8,128)}) custom-call(bf16[1,2432,256]{2,1,0:T(8,128)(2,1)} %acts.2, f32[1,3,2432]{2,1,0:T(4,128)S(1)} %copy.12.modulation, bf16[1,2432,2432]{2,1,0:T(8,128)(2,1)} %w_in.5, ...), custom_call_target="tpu_custom_call" | custom-call | flops 2550136832 | bytes 12451840 | tf_op jit(solution)/shard_map/forward_first/pallas_call | solution.py:253
  20.4 1.1 copy-done.7
  22.1 1.3 collective-permute-done.4
  23.4 1.1 multiply_convert_fusion.refs_0_
  24.6 3.0 %collective-permute-start.10 = (bf16[608,256]{1,0:T(8,128)(2,1)S(1)}, bf16[608,256]{1,0:T(8,128)(2,1)S(1)}, u32[]{:S(2)}, u32[]{:S(2)}) collective-permute-start(bf16[608,256]{1,0:T(8,128)(2,1)S(1)} %multiply_convert_fusion.refs_0_), channel_id=1, source_target_pairs={{0,12},{4,8},{8,4},{12,0},{16,28},{20,24},{24,20},{28,16},{1,13},{... | collective-permute-start | bytes 933896 | tf_op jit(solution)/shard_map/ppermute | solution.py:63
  27.5 3.6 %collective-permute-start.13 = (bf16[608,256]{1,0:T(8,128)(2,1)S(1)}, bf16[608,256]{1,0:T(8,128)(2,1)S(1)}, u32[]{:S(2)}, u32[]{:S(2)}) collective-permute-start(bf16[608,256]{1,0:T(8,128)(2,1)S(1)} %get-tuple-element.75.refs_0_), channel_id=1, source_target_pairs={{0,3},{1,2},{2,1},{3,0},{4,7},{5,6},{6,5},{7,4},{8,11},{9,10},{10,... | collective-permute-start | bytes 933896 | tf_op jit(solution)/shard_map/ppermute | solution.py:69
  31.1 0.8 collective-permute-start.11
  32.4 3.3 %collective-permute-done.10.refs_3_ = bf16[608,256]{1,0:T(8,128)(2,1)S(1)} collective-permute-done((bf16[608,256]{1,0:T(8,128)(2,1)S(1)}, bf16[608,256]{1,0:T(8,128)(2,1)S(1)}, u32[]{:S(2)}, u32[]{:S(2)}) %collective-permute-start.10) | collective-permute-done | bytes 311328 | tf_op jit(solution)/shard_map/ppermute | solution.py:63
  35.7 2.0 %collective-permute-start.8 = (bf16[608,256]{1,0:T(8,128)(2,1)S(1)}, bf16[608,256]{1,0:T(8,128)(2,1)S(1)}, u32[]{:S(2)}, u32[]{:S(2)}) collective-permute-start(bf16[608,256]{1,0:T(8,128)(2,1)S(1)} %multiply_convert_fusion.refs_0_), channel_id=1, source_target_pairs={{0,4},{4,0},{8,12},{12,8},{16,24},{20,28},{24,16},{28,20},{1,5},{5... | collective-permute-start | bytes 933896 | tf_op jit(solution)/shard_map/ppermute | solution.py:63
  37.7 11.3 %forward_last.1 = (f32[256,1408]{1,0:T(8,128)}, f32[608,256]{1,0:T(8,128)S(1)}, bf16[608,256]{1,0:T(8,128)(2,1)S(1)}, bf16[608,256]{1,0:T(8,128)(2,1)S(1)}, bf16[608,256]{1,0:T(8,128)(2,1)S(1)}) custom-call(s32[9]{0:T(128)S(1)} %pad_add_fusion.order, bf16[256,2432]{1,0:T(8,128)(2,1)S(1)} %copy-done.8, f32[256,2432]{1,0:T(8,128)} %get-tuple-element.63.before, ...), custom_call_target="tpu_custom_call" | custom-call | flops 3506438144 | bytes 16187392 | tf_op jit(solution)/shard_map/forward_last/pallas_call | solution.py:273
  49.1 2.0 %collective-permute-start.6 = (bf16[608,256]{1,0:T(8,128)(2,1)S(1)}, bf16[608,256]{1,0:T(8,128)(2,1)S(1)}, u32[]{:S(2)}, u32[]{:S(2)}) collective-permute-start(bf16[608,256]{1,0:T(8,128)(2,1)S(1)} %get-tuple-element.70), channel_id=1, source_target_pairs={{0,8},{4,12},{8,0},{12,4},{16,20},{20,16},{24,28},{28,24},{1,9},{5... | collective-permute-start | bytes 933896 | tf_op jit(solution)/shard_map/ppermute | solution.py:63
  51.2 1.4 %collective-permute-start.7 = (bf16[608,256]{1,0:T(8,128)(2,1)S(1)}, bf16[608,256]{1,0:T(8,128)(2,1)S(1)}, u32[]{:S(2)}, u32[]{:S(2)}) collective-permute-start(bf16[608,256]{1,0:T(8,128)(2,1)S(1)} %get-tuple-element.71), channel_id=1, source_target_pairs={{0,12},{4,8},{8,4},{12,0},{16,28},{20,24},{24,20},{28,16},{1,13},{... | collective-permute-start | bytes 933896 | tf_op jit(solution)/shard_map/ppermute | solution.py:63
  52.6 5.1 %collective-permute-done.12.refs_2_ = bf16[608,256]{1,0:T(8,128)(2,1)S(1)} collective-permute-done((bf16[608,256]{1,0:T(8,128)(2,1)S(1)}, bf16[608,256]{1,0:T(8,128)(2,1)S(1)}, u32[]{:S(2)}, u32[]{:S(2)}) %collective-permute-start.12) | collective-permute-done | bytes 311328 | tf_op jit(solution)/shard_map/ppermute | solution.py:69
  57.7 10.1 %backward_first.1 = (bf16[256,2432]{1,0:T(8,128)(2,1)S(1)}, f32[256,2432]{1,0:T(8,128)}) custom-call(s32[9]{0:T(128)S(1)} %pad_add_fusion.order, bf16[608,256]{1,0:T(8,128)(2,1)S(1)} %multiply_convert_fusion.refs_0_, bf16[608,256]{1,0:T(8,128)(2,1)S(1)} %collective-permute-done.8.refs_1_, bf16[608,256]{1,0:T(8,128)(2,1)S(1)} %collective-permute-done.9.refs_2_, ...), custom_call_target="tpu_custom_call" | custom-call | flops 3825205248 | bytes 17432576 | tf_op jit(solution)/shard_map/backward_first/pallas_call | solution.py:331
  67.9 2.3 %fusion.16 = (bf16[608,256]{1,0:T(8,128)(2,1)S(1)}, f32[608,256]{1,0:T(8,128)}) fusion(f32[608,256]{1,0:T(8,128)S(1)} %get-tuple-element.68, bf16[608,256]{1,0:T(8,128)(2,1)S(1)} %collective-permute-done.7, bf16[608,256]{1,0:T(8,128)(2,1)S(1)} %collective-permute-done.6, bf16[608,256]{1,0:T(8,128)(2,1)S(1)} %collective-permute-done.5, ...), kind=kLoop, calls=%fused_computation.35 | loop fusion | flops 1556480 | bytes 2804100 | tf_op jit(solution)/shard_map/convert_element_type | solution.py:582
  70.4 1.4 %collective-permute-done.14 = bf16[608,128]{1,0:T(8,128)(2,1)S(1)} collective-permute-done((bf16[608,128]{1,0:T(8,128)(2,1)S(1)}, bf16[608,128]{1,0:T(8,128)(2,1)S(1)}, u32[]{:S(2)}, u32[]{:S(2)}) %collective-permute-start.14) | collective-permute-done | bytes 155680 | tf_op jit(solution)/shard_map/ppermute | solution.py:35
  71.7 0.6 collective-permute-start.18
  72.3 2.5 %collective-permute-start.17 = (bf16[608,128]{1,0:T(8,128)(2,1)S(1)}, bf16[608,128]{1,0:T(8,128)(2,1)S(1)}, u32[]{:S(2)}, u32[]{:S(2)}) collective-permute-start(bf16[608,128]{1,0:T(8,128)(2,1)S(1)} %slice_select_fusion.refs_0_.refs_4_), channel_id=1, source_target_pairs={{0,3},{1,2},{2,1},{3,0},{4,7},{5,6},{6,5},{7,4},{8,11},{9,10},{10,... | collective-permute-start | bytes 466952 | tf_op jit(solution)/shard_map/ppermute | solution.py:69
  74.8 1.9 %collective-permute-start.15 = (bf16[608,128]{1,0:T(8,128)(2,1)S(1)}, bf16[608,128]{1,0:T(8,128)(2,1)S(1)}, u32[]{:S(2)}, u32[]{:S(2)}) collective-permute-start(bf16[608,128]{1,0:T(8,128)(2,1)S(1)} %slice_select_fusion.refs_0_.refs_4_), channel_id=1, source_target_pairs={{0,1},{1,0},{2,3},{3,2},{4,5},{5,4},{6,7},{7,6},{8,9},{9,8},{10,11... | collective-permute-start | bytes 466952 | tf_op jit(solution)/shard_map/ppermute | solution.py:69
  76.7 10.4 %backward_last.1 = (bf16[624,256]{1,0:T(8,128)(2,1)}, bf16[624,256]{1,0:T(8,128)(2,1)}, f32[608,256]{1,0:T(8,128)S(1)}, f32[608,256]{1,0:T(8,128)S(1)}, f32[2,256]{1,0:T(2,128)S(1)}) custom-call(s32[9]{0:T(128)S(1)} %pad_add_fusion.order, bf16[256,2432]{1,0:T(8,128)(2,1)} %copy-done.9, f32[256,2432]{1,0:T(8,128)} %get-tuple-element.82.before, ...), custom_call_target="tpu_custom_call" | custom-call | flops 2231369728 | bytes 11206656 | tf_op jit(solution)/shard_map/backward_last/pallas_call | solution.py:384
  87.1 0.8 copy-done.10
  87.9 0.9 copy-done.12
  89.4 1.5 %collective-permute-start.20 = (bf16[608,128]{1,0:T(8,128)(2,1)}, bf16[608,128]{1,0:T(8,128)(2,1)}, u32[]{:S(2)}, u32[]{:S(2)}) collective-permute-start(bf16[608,128]{1,0:T(8,128)(2,1)} %collective-permute-done.18.refs_1_.refs_5_), channel_id=1, source_target_pairs={{0,8},{4,12},{8,0},{12,4},{16,20},{20,16},{24,28},{28,24},{1,9},{5... | collective-permute-start | bytes 466952 | tf_op jit(solution)/shard_map/ppermute | solution.py:47
  90.9 1.5 %collective-permute-start.22 = (bf16[624,256]{1,0:T(8,128)(2,1)}, bf16[624,256]{1,0:T(8,128)(2,1)}, u32[]{:S(2)}, u32[]{:S(2)}) collective-permute-start(bf16[624,256]{1,0:T(8,128)(2,1)} %get-tuple-element.96), channel_id=1, source_target_pairs={{0,4},{4,0},{8,12},{12,8},{16,24},{20,28},{24,16},{28,20},{1,5},{5... | collective-permute-start | bytes 958472 | tf_op jit(solution)/shard_map/ppermute | solution.py:47
  92.9 0.8 pad_maximum_fusion.refs_12_
  93.8 1.5 %collective-permute-start.29 = (bf16[3,608,128]{2,1,0:T(8,128)(2,1)}, bf16[3,608,128]{2,1,0:T(8,128)(2,1)}, u32[]{:S(2)}, u32[]{:S(2)}) collective-permute-start(bf16[3,608,128]{2,1,0:T(8,128)(2,1)} %pad_maximum_fusion.refs_12_), channel_id=1, source_target_pairs={{0,4},{4,0},{8,12},{12,8},{16,24},{20,28},{24,16},{28,20},{1,5},{5... | collective-permute-start | bytes 1400840 | tf_op jit(solution)/shard_map/ppermute | solution.py:47
  95.3 0.6 collective-permute-done.19.refs_2_.refs_6_
  95.9 3.3 %collective-permute-done.20.refs_3_.refs_7_ = bf16[608,128]{1,0:T(8,128)(2,1)} collective-permute-done((bf16[608,128]{1,0:T(8,128)(2,1)}, bf16[608,128]{1,0:T(8,128)(2,1)}, u32[]{:S(2)}, u32[]{:S(2)}) %collective-permute-start.20) | collective-permute-done | bytes 155680 | tf_op jit(solution)/shard_map/ppermute | solution.py:47
  99.2 2.0 %residual_rows.1 = f32[608,128]{1,0:T(8,128)S(1)} custom-call(s32[9]{0:T(128)S(1)} %pad_add_fusion.order, bf16[608,2432]{1,0:T(8,128)(2,1)S(1)} %copy-done.1, bf16[608,128]{1,0:T(8,128)(2,1)S(1)} %slice_select_fusion.refs_0_.refs_4_, bf16[608,128]{1,0:T(8,128)(2,1)} %collective-permute-done.18.refs_1_.refs_5_, ...), custom_call_target="tpu_custom_call" | custom-call | flops 378535936 | bytes 4202496 | tf_op jit(solution)/shard_map/residual_rows/pallas_call | solution.py:475
  101.6 1.2 fold.1
  102.9 0.7 collective-permute-start.24
  103.6 0.9 collective-permute-start.25
  104.5 1.1 collective-permute-start.30
  105.6 1.1 collective-permute-done.29.refs_13_
  107.3 0.8 fusion.8
  108.1 2.6 %collective-permute-done.24 = bf16[624,256]{1,0:T(8,128)(2,1)S(1)} collective-permute-done((bf16[624,256]{1,0:T(8,128)(2,1)S(1)}, bf16[624,256]{1,0:T(8,128)(2,1)S(1)}, u32[]{:S(2)}, u32[]{:S(2)}) %collective-permute-start.24) | collective-permute-done | bytes 319520 | tf_op jit(solution)/shard_map/ppermute | solution.py:47
  111.3 4.4 %collective-permute-done.30.refs_14_ = bf16[3,608,128]{2,1,0:T(8,128)(2,1)S(1)} collective-permute-done((bf16[3,608,128]{2,1,0:T(8,128)(2,1)}, bf16[3,608,128]{2,1,0:T(8,128)(2,1)S(1)}, u32[]{:S(2)}, u32[]{:S(2)}) %collective-permute-start.30) | collective-permute-done | bytes 466976 | tf_op jit(solution)/shard_map/ppermute | solution.py:47
  115.8 5.0 %collective-permute-done.31.refs_15_ = bf16[3,608,128]{2,1,0:T(8,128)(2,1)S(1)} collective-permute-done((bf16[3,608,128]{2,1,0:T(8,128)(2,1)}, bf16[3,608,128]{2,1,0:T(8,128)(2,1)S(1)}, u32[]{:S(2)}, u32[]{:S(2)}) %collective-permute-start.31) | collective-permute-done | bytes 466976 | tf_op jit(solution)/shard_map/ppermute | solution.py:47
  120.8 0.6 collective-permute-start.28
  121.4 2.2 %fusion.5 = f32[1,608,256]{2,1,0:T(8,128)} fusion(f32[608,256]{1,0:T(8,128)S(1)} %get-tuple-element.101, f32[608,128]{1,0:T(8,128)} %collective-permute-done.4, f32[608,128]{1,0:T(8,128)S(1)} %copy-done.23, bf16[624,256]{1,0:T(8,128)(2,1)S(1)} %collective-permute-done.24, f32[256]{0:T(256)S(1)} %bitcast.26, f32[256]{0:T(256)S(1)} %bitcast.28, ...), kind=kLoop, calls=%fused_computation.7 | loop fusion | flops 2179072 | bytes 2808197 | tf_op jit(solution)/shard_map/broadcast_in_dim | solution.py:614
  123.6 7.5 %zero_projection_grad.1 = f32[608,2432]{1,0:T(8,128)} custom-call(s32[9]{0:T(128)S(1)} %pad_add_fusion.order, s32[4]{0:T(128)S(1)} %iota_xor_fusion.dp_order, bf16[608,256]{1,0:T(8,128)(2,1)S(1)} %copy-done.15, bf16[608,256]{1,0:T(8,128)(2,1)S(1)} %copy-done.21, bf16[608,256]{1,0:T(8,128)(2,1)S(1)} %copy-done.19, bf16[608,256]{1,0:T(8,128)(2,1)S(1)} %copy-done.17, ...), custom_call_target="tpu_custom_call" | custom-call | flops 3028287488 | bytes 12140544 | tf_op jit(solution)/shard_map/zero_projection_grad/pallas_call | solution.py:516
  (102 shorter events, 4.7 us)
Async XLA Ops:
  0.6 2.0 %collective-permute-start = (bf16[608,256]{1,0:T(8,128)(2,1)}, bf16[608,256]{1,0:T(8,128)(2,1)S(1)}, u32[]{:S(2)}, u32[]{:S(2)}) collective-permute-start(bf16[608,256]{1,0:T(8,128)(2,1)} %bitcast.20), channel_id=1, source_target_pairs={{0,16},{16,0},{1,17},{17,1},{2,18},{18,2},{3,19},{19,3},{4,20},{20... | collective-permute-start | bytes 933896 | tf_op jit(solution)/shard_map/ppermute | solution.py:35
  6.9 24.2 %copy-start.14 = (bf16[608,256]{1,0:T(8,128)(2,1)}, bf16[608,256]{1,0:T(8,128)(2,1)S(1)}, u32[]{:S(2)}) copy-start(bf16[608,256]{1,0:T(8,128)(2,1)S(1)} %get-tuple-element.75.refs_0_) | copy-start | bytes 933892
  6.9 14.6 %collective-permute-start.1 = (bf16[608,128]{1,0:T(8,128)(2,1)S(1)}, bf16[608,128]{1,0:T(8,128)(2,1)S(1)}, u32[]{:S(2)}, u32[]{:S(2)}) collective-permute-start(bf16[608,128]{1,0:T(8,128)(2,1)S(1)} %get-tuple-element.55), channel_id=1, source_target_pairs={{0,4},{4,0},{8,12},{12,8},{16,24},{20,28},{24,16},{28,20},{1,5},{5... | collective-permute-start | bytes 466952 | tf_op jit(solution)/shard_map/ppermute | solution.py:63
  9.8 11.7 %collective-permute-start.2 = (bf16[608,128]{1,0:T(8,128)(2,1)S(1)}, bf16[608,128]{1,0:T(8,128)(2,1)S(1)}, u32[]{:S(2)}, u32[]{:S(2)}) collective-permute-start(bf16[608,128]{1,0:T(8,128)(2,1)S(1)} %get-tuple-element.56), channel_id=1, source_target_pairs={{0,8},{4,12},{8,0},{12,4},{16,20},{20,16},{24,28},{28,24},{1,9},{5... | collective-permute-start | bytes 466952 | tf_op jit(solution)/shard_map/ppermute | solution.py:63
  11.3 10.2 %collective-permute-start.3 = (bf16[608,128]{1,0:T(8,128)(2,1)S(1)}, bf16[608,128]{1,0:T(8,128)(2,1)S(1)}, u32[]{:S(2)}, u32[]{:S(2)}) collective-permute-start(bf16[608,128]{1,0:T(8,128)(2,1)S(1)} %get-tuple-element.57), channel_id=1, source_target_pairs={{0,12},{4,8},{8,4},{12,0},{16,28},{20,24},{24,20},{28,16},{1,13},{... | collective-permute-start | bytes 466952 | tf_op jit(solution)/shard_map/ppermute | solution.py:63
  21.5 36.2 %copy-start.2 = (f32[256,1024]{1,0:T(8,128)}, f32[256,1024]{1,0:T(8,128)S(1)}, u32[]{:S(2)}) copy-start(f32[256,1024]{1,0:T(8,128)S(1)} %get-tuple-element.80.refs_4_.slope_a) | copy-start | bytes 3145732
  21.6 14.1 %copy-start.22 = (f32[608,128]{1,0:T(8,128)}, f32[608,128]{1,0:T(8,128)S(1)}, u32[]{:S(2)}) copy-start(f32[608,128]{1,0:T(8,128)S(1)} %add_add_fusion) | copy-start | bytes 933892
  21.6 1.8 %collective-permute-start.4 = (f32[608,128]{1,0:T(8,128)S(1)}, f32[608,128]{1,0:T(8,128)}, u32[]{:S(2)}, u32[]{:S(2)}) collective-permute-start(f32[608,128]{1,0:T(8,128)S(1)} %add_add_fusion), channel_id=1, source_target_pairs={{0,16},{16,0},{1,17},{17,1},{2,18},{18,2},{3,19},{19,3},{4,20},{20... | collective-permute-start | bytes 933896 | tf_op jit(solution)/shard_map/ppermute | solution.py:35
  21.7 16.0 %copy-start.8 = (bf16[256,2432]{1,0:T(8,128)(2,1)S(1)}, bf16[256,2432]{1,0:T(8,128)(2,1)}, u32[]{:S(2)}) copy-start(bf16[256,2432]{1,0:T(8,128)(2,1)} %copy-done.7) | copy-start | bytes 3735556
  24.6 11.1 %collective-permute-start.10 = (bf16[608,256]{1,0:T(8,128)(2,1)S(1)}, bf16[608,256]{1,0:T(8,128)(2,1)S(1)}, u32[]{:S(2)}, u32[]{:S(2)}) collective-permute-start(bf16[608,256]{1,0:T(8,128)(2,1)S(1)} %multiply_convert_fusion.refs_0_), channel_id=1, source_target_pairs={{0,12},{4,8},{8,4},{12,0},{16,28},{20,24},{24,20},{28,16},{1,13},{... | collective-permute-start | bytes 933896 | tf_op jit(solution)/shard_map/ppermute | solution.py:63
  27.5 23.6 %collective-permute-start.13 = (bf16[608,256]{1,0:T(8,128)(2,1)S(1)}, bf16[608,256]{1,0:T(8,128)(2,1)S(1)}, u32[]{:S(2)}, u32[]{:S(2)}) collective-permute-start(bf16[608,256]{1,0:T(8,128)(2,1)S(1)} %get-tuple-element.75.refs_0_), channel_id=1, source_target_pairs={{0,3},{1,2},{2,1},{3,0},{4,7},{5,6},{6,5},{7,4},{8,11},{9,10},{10,... | collective-permute-start | bytes 933896 | tf_op jit(solution)/shard_map/ppermute | solution.py:69
  31.1 26.6 %collective-permute-start.12 = (bf16[608,256]{1,0:T(8,128)(2,1)S(1)}, bf16[608,256]{1,0:T(8,128)(2,1)S(1)}, u32[]{:S(2)}, u32[]{:S(2)}) collective-permute-start(bf16[608,256]{1,0:T(8,128)(2,1)S(1)} %get-tuple-element.75.refs_0_), channel_id=1, source_target_pairs={{0,2},{1,3},{2,0},{3,1},{4,6},{5,7},{6,4},{7,5},{8,10},{9,11},{10,... | collective-permute-start | bytes 933896 | tf_op jit(solution)/shard_map/ppermute | solution.py:69
  31.1 26.6 %collective-permute-start.11 = (bf16[608,256]{1,0:T(8,128)(2,1)S(1)}, bf16[608,256]{1,0:T(8,128)(2,1)S(1)}, u32[]{:S(2)}, u32[]{:S(2)}) collective-permute-start(bf16[608,256]{1,0:T(8,128)(2,1)S(1)} %get-tuple-element.75.refs_0_), channel_id=1, source_target_pairs={{0,1},{1,0},{2,3},{3,2},{4,5},{5,4},{6,7},{7,6},{8,9},{9,8},{10,11... | collective-permute-start | bytes 933896 | tf_op jit(solution)/shard_map/ppermute | solution.py:69
  31.9 17.1 %collective-permute-start.9 = (bf16[608,256]{1,0:T(8,128)(2,1)S(1)}, bf16[608,256]{1,0:T(8,128)(2,1)S(1)}, u32[]{:S(2)}, u32[]{:S(2)}) collective-permute-start(bf16[608,256]{1,0:T(8,128)(2,1)S(1)} %multiply_convert_fusion.refs_0_), channel_id=1, source_target_pairs={{0,8},{4,12},{8,0},{12,4},{16,20},{20,16},{24,28},{28,24},{1,9},{5... | collective-permute-start | bytes 933896 | tf_op jit(solution)/shard_map/ppermute | solution.py:63
  35.7 13.5 %collective-permute-start.8 = (bf16[608,256]{1,0:T(8,128)(2,1)S(1)}, bf16[608,256]{1,0:T(8,128)(2,1)S(1)}, u32[]{:S(2)}, u32[]{:S(2)}) collective-permute-start(bf16[608,256]{1,0:T(8,128)(2,1)S(1)} %multiply_convert_fusion.refs_0_), channel_id=1, source_target_pairs={{0,4},{4,0},{8,12},{12,8},{16,24},{20,28},{24,16},{28,20},{1,5},{5... | collective-permute-start | bytes 933896 | tf_op jit(solution)/shard_map/ppermute | solution.py:63
  49.0 18.8 %collective-permute-start.5 = (bf16[608,256]{1,0:T(8,128)(2,1)S(1)}, bf16[608,256]{1,0:T(8,128)(2,1)S(1)}, u32[]{:S(2)}, u32[]{:S(2)}) collective-permute-start(bf16[608,256]{1,0:T(8,128)(2,1)S(1)} %get-tuple-element.69), channel_id=1, source_target_pairs={{0,4},{4,0},{8,12},{12,8},{16,24},{20,28},{24,16},{28,20},{1,5},{5... | collective-permute-start | bytes 933896 | tf_op jit(solution)/shard_map/ppermute | solution.py:63
  49.1 18.7 %collective-permute-start.6 = (bf16[608,256]{1,0:T(8,128)(2,1)S(1)}, bf16[608,256]{1,0:T(8,128)(2,1)S(1)}, u32[]{:S(2)}, u32[]{:S(2)}) collective-permute-start(bf16[608,256]{1,0:T(8,128)(2,1)S(1)} %get-tuple-element.70), channel_id=1, source_target_pairs={{0,8},{4,12},{8,0},{12,4},{16,20},{20,16},{24,28},{28,24},{1,9},{5... | collective-permute-start | bytes 933896 | tf_op jit(solution)/shard_map/ppermute | solution.py:63
  51.2 16.7 %copy-start.16 = (bf16[608,256]{1,0:T(8,128)(2,1)}, bf16[608,256]{1,0:T(8,128)(2,1)S(1)}, u32[]{:S(2)}) copy-start(bf16[608,256]{1,0:T(8,128)(2,1)S(1)} %collective-permute-done.13.refs_3_) | copy-start | bytes 933892
  51.2 16.7 %collective-permute-start.7 = (bf16[608,256]{1,0:T(8,128)(2,1)S(1)}, bf16[608,256]{1,0:T(8,128)(2,1)S(1)}, u32[]{:S(2)}, u32[]{:S(2)}) collective-permute-start(bf16[608,256]{1,0:T(8,128)(2,1)S(1)} %get-tuple-element.71), channel_id=1, source_target_pairs={{0,12},{4,8},{8,4},{12,0},{16,28},{20,24},{24,20},{28,16},{1,13},{... | collective-permute-start | bytes 933896 | tf_op jit(solution)/shard_map/ppermute | solution.py:63
  57.7 10.2 %copy-start.20 = (bf16[608,256]{1,0:T(8,128)(2,1)}, bf16[608,256]{1,0:T(8,128)(2,1)S(1)}, u32[]{:S(2)}) copy-start(bf16[608,256]{1,0:T(8,128)(2,1)S(1)} %collective-permute-done.11.refs_1_) | copy-start | bytes 933892
  70.3 1.4 %collective-permute-start.14 = (bf16[608,128]{1,0:T(8,128)(2,1)S(1)}, bf16[608,128]{1,0:T(8,128)(2,1)S(1)}, u32[]{:S(2)}, u32[]{:S(2)}) collective-permute-start(bf16[608,128]{1,0:T(8,128)(2,1)S(1)} %slice.65), channel_id=1, source_target_pairs={{0,16},{16,0},{1,17},{17,1},{2,18},{18,2},{3,19},{19,3},{4,20},{20... | collective-permute-start | bytes 466952 | tf_op jit(solution)/shard_map/ppermute | solution.py:35
  71.7 17.1 %collective-permute-start.18 = (bf16[608,128]{1,0:T(8,128)(2,1)S(1)}, bf16[608,128]{1,0:T(8,128)(2,1)}, u32[]{:S(2)}, u32[]{:S(2)}) collective-permute-start(bf16[608,128]{1,0:T(8,128)(2,1)S(1)} %slice_select_fusion.refs_0_.refs_4_), channel_id=1, source_target_pairs={{0,4},{4,0},{8,12},{12,8},{16,24},{20,28},{24,16},{28,20},{1,5},{5... | collective-permute-start | bytes 466952 | tf_op jit(solution)/shard_map/ppermute | solution.py:47
  72.3 16.5 %collective-permute-start.17 = (bf16[608,128]{1,0:T(8,128)(2,1)S(1)}, bf16[608,128]{1,0:T(8,128)(2,1)S(1)}, u32[]{:S(2)}, u32[]{:S(2)}) collective-permute-start(bf16[608,128]{1,0:T(8,128)(2,1)S(1)} %slice_select_fusion.refs_0_.refs_4_), channel_id=1, source_target_pairs={{0,3},{1,2},{2,1},{3,0},{4,7},{5,6},{6,5},{7,4},{8,11},{9,10},{10,... | collective-permute-start | bytes 466952 | tf_op jit(solution)/shard_map/ppermute | solution.py:69
  74.8 14.0 %collective-permute-start.16 = (bf16[608,128]{1,0:T(8,128)(2,1)S(1)}, bf16[608,128]{1,0:T(8,128)(2,1)S(1)}, u32[]{:S(2)}, u32[]{:S(2)}) collective-permute-start(bf16[608,128]{1,0:T(8,128)(2,1)S(1)} %slice_select_fusion.refs_0_.refs_4_), channel_id=1, source_target_pairs={{0,2},{1,3},{2,0},{3,1},{4,6},{5,7},{6,4},{7,5},{8,10},{9,11},{10,... | collective-permute-start | bytes 466952 | tf_op jit(solution)/shard_map/ppermute | solution.py:69
  74.8 14.0 %collective-permute-start.15 = (bf16[608,128]{1,0:T(8,128)(2,1)S(1)}, bf16[608,128]{1,0:T(8,128)(2,1)S(1)}, u32[]{:S(2)}, u32[]{:S(2)}) collective-permute-start(bf16[608,128]{1,0:T(8,128)(2,1)S(1)} %slice_select_fusion.refs_0_.refs_4_), channel_id=1, source_target_pairs={{0,1},{1,0},{2,3},{3,2},{4,5},{5,4},{6,7},{7,6},{8,9},{9,8},{10,11... | collective-permute-start | bytes 466952 | tf_op jit(solution)/shard_map/ppermute | solution.py:69
  76.7 22.5 %copy-start.1 = (bf16[608,2432]{1,0:T(8,128)(2,1)S(1)}, bf16[608,2432]{1,0:T(8,128)(2,1)}, u32[]{:S(2)}) copy-start(bf16[608,2432]{1,0:T(8,128)(2,1)} %weight.3) | copy-start | bytes 8871940
  88.8 7.1 %collective-permute-start.19 = (bf16[608,128]{1,0:T(8,128)(2,1)S(1)}, bf16[608,128]{1,0:T(8,128)(2,1)}, u32[]{:S(2)}, u32[]{:S(2)}) collective-permute-start(bf16[608,128]{1,0:T(8,128)(2,1)S(1)} %slice_select_fusion.refs_0_.refs_4_), channel_id=1, source_target_pairs={{0,8},{4,12},{8,0},{12,4},{16,20},{20,16},{24,28},{28,24},{1,9},{5... | collective-permute-start | bytes 466952 | tf_op jit(solution)/shard_map/ppermute | solution.py:47
  89.4 9.8 %collective-permute-start.20 = (bf16[608,128]{1,0:T(8,128)(2,1)}, bf16[608,128]{1,0:T(8,128)(2,1)}, u32[]{:S(2)}, u32[]{:S(2)}) collective-permute-start(bf16[608,128]{1,0:T(8,128)(2,1)} %collective-permute-done.18.refs_1_.refs_5_), channel_id=1, source_target_pairs={{0,8},{4,12},{8,0},{12,4},{16,20},{20,16},{24,28},{28,24},{1,9},{5... | collective-permute-start | bytes 466952 | tf_op jit(solution)/shard_map/ppermute | solution.py:47
  90.9 10.5 %collective-permute-start.22 = (bf16[624,256]{1,0:T(8,128)(2,1)}, bf16[624,256]{1,0:T(8,128)(2,1)}, u32[]{:S(2)}, u32[]{:S(2)}) collective-permute-start(bf16[624,256]{1,0:T(8,128)(2,1)} %get-tuple-element.96), channel_id=1, source_target_pairs={{0,4},{4,0},{8,12},{12,8},{16,24},{20,28},{24,16},{28,20},{1,5},{5... | collective-permute-start | bytes 958472 | tf_op jit(solution)/shard_map/ppermute | solution.py:47
  92.4 9.2 %collective-permute-start.23 = (bf16[624,256]{1,0:T(8,128)(2,1)}, bf16[624,256]{1,0:T(8,128)(2,1)}, u32[]{:S(2)}, u32[]{:S(2)}) collective-permute-start(bf16[624,256]{1,0:T(8,128)(2,1)} %get-tuple-element.97), channel_id=1, source_target_pairs={{0,4},{4,0},{8,12},{12,8},{16,24},{20,28},{24,16},{28,20},{1,5},{5... | collective-permute-start | bytes 958472 | tf_op jit(solution)/shard_map/ppermute | solution.py:47
  93.8 12.9 %collective-permute-start.29 = (bf16[3,608,128]{2,1,0:T(8,128)(2,1)}, bf16[3,608,128]{2,1,0:T(8,128)(2,1)}, u32[]{:S(2)}, u32[]{:S(2)}) collective-permute-start(bf16[3,608,128]{2,1,0:T(8,128)(2,1)} %pad_maximum_fusion.refs_12_), channel_id=1, source_target_pairs={{0,4},{4,0},{8,12},{12,8},{16,24},{20,28},{24,16},{28,20},{1,5},{5... | collective-permute-start | bytes 1400840 | tf_op jit(solution)/shard_map/ppermute | solution.py:47
  101.3 3.2 %collective-permute-start.21 = (f32[608,128]{1,0:T(8,128)S(1)}, f32[608,128]{1,0:T(8,128)S(1)}, u32[]{:S(2)}, u32[]{:S(2)}) collective-permute-start(f32[608,128]{1,0:T(8,128)S(1)} %residual_rows.1), channel_id=1, source_target_pairs={{0,16},{16,0},{1,17},{17,1},{2,18},{18,2},{3,19},{19,3},{4,20},{20... | collective-permute-start | bytes 933896 | tf_op jit(solution)/shard_map/ppermute | solution.py:35
  101.4 20.0 %copy-start.23 = (f32[608,128]{1,0:T(8,128)S(1)}, f32[608,128]{1,0:T(8,128)}, u32[]{:S(2)}) copy-start(f32[608,128]{1,0:T(8,128)} %copy-done.22) | copy-start | bytes 933892
  102.9 7.9 %collective-permute-start.24 = (bf16[624,256]{1,0:T(8,128)(2,1)S(1)}, bf16[624,256]{1,0:T(8,128)(2,1)S(1)}, u32[]{:S(2)}, u32[]{:S(2)}) collective-permute-start(bf16[624,256]{1,0:T(8,128)(2,1)S(1)} %get-tuple-element.102), channel_id=1, source_target_pairs={{0,8},{4,12},{8,0},{12,4},{16,20},{20,16},{24,28},{28,24},{1,9},{5... | collective-permute-start | bytes 958472 | tf_op jit(solution)/shard_map/ppermute | solution.py:47
  103.6 7.2 %collective-permute-start.25 = (bf16[608,128]{1,0:T(8,128)(2,1)S(1)}, bf16[608,128]{1,0:T(8,128)(2,1)S(1)}, u32[]{:S(2)}, u32[]{:S(2)}) collective-permute-start(bf16[608,128]{1,0:T(8,128)(2,1)S(1)} %slice_select_fusion.refs_0_.refs_4_), channel_id=1, source_target_pairs={{0,16},{16,0},{1,17},{17,1},{2,18},{18,2},{3,19},{19,3},{4,20},{20... | collective-permute-start | bytes 466952 | tf_op jit(solution)/shard_map/ppermute | solution.py:35
  104.5 6.8 %collective-permute-start.26 = (bf16[608,128]{1,0:T(8,128)(2,1)}, bf16[608,128]{1,0:T(8,128)(2,1)S(1)}, u32[]{:S(2)}, u32[]{:S(2)}) collective-permute-start(bf16[608,128]{1,0:T(8,128)(2,1)} %collective-permute-done.18.refs_1_.refs_5_), channel_id=1, source_target_pairs={{0,16},{16,0},{1,17},{17,1},{2,18},{18,2},{3,19},{19,3},{4,20},{20... | collective-permute-start | bytes 466952 | tf_op jit(solution)/shard_map/ppermute | solution.py:35
  104.5 11.3 %collective-permute-start.30 = (bf16[3,608,128]{2,1,0:T(8,128)(2,1)}, bf16[3,608,128]{2,1,0:T(8,128)(2,1)S(1)}, u32[]{:S(2)}, u32[]{:S(2)}) collective-permute-start(bf16[3,608,128]{2,1,0:T(8,128)(2,1)} %pad_maximum_fusion.refs_12_), channel_id=1, source_target_pairs={{0,8},{4,12},{8,0},{12,4},{16,20},{20,16},{24,28},{28,24},{1,9},{5... | collective-permute-start | bytes 1400840 | tf_op jit(solution)/shard_map/ppermute | solution.py:47
  106.7 14.0 %collective-permute-start.31 = (bf16[3,608,128]{2,1,0:T(8,128)(2,1)}, bf16[3,608,128]{2,1,0:T(8,128)(2,1)S(1)}, u32[]{:S(2)}, u32[]{:S(2)}) collective-permute-start(bf16[3,608,128]{2,1,0:T(8,128)(2,1)} %collective-permute-done.29.refs_13_), channel_id=1, source_target_pairs={{0,8},{4,12},{8,0},{12,4},{16,20},{20,16},{24,28},{28,24},{1,9},{5... | collective-permute-start | bytes 1400840 | tf_op jit(solution)/shard_map/ppermute | solution.py:47
  108.1 15.4 %copy-start.15 = (bf16[608,256]{1,0:T(8,128)(2,1)S(1)}, bf16[608,256]{1,0:T(8,128)(2,1)}, u32[]{:S(2)}) copy-start(bf16[608,256]{1,0:T(8,128)(2,1)} %copy-done.14) | copy-start | bytes 933892
  108.1 15.4 %copy-start.17 = (bf16[608,256]{1,0:T(8,128)(2,1)S(1)}, bf16[608,256]{1,0:T(8,128)(2,1)}, u32[]{:S(2)}) copy-start(bf16[608,256]{1,0:T(8,128)(2,1)} %copy-done.16) | copy-start | bytes 933892
  108.1 15.4 %copy-start.19 = (bf16[608,256]{1,0:T(8,128)(2,1)S(1)}, bf16[608,256]{1,0:T(8,128)(2,1)}, u32[]{:S(2)}) copy-start(bf16[608,256]{1,0:T(8,128)(2,1)} %copy-done.18) | copy-start | bytes 933892
  108.1 15.5 %copy-start.21 = (bf16[608,256]{1,0:T(8,128)(2,1)S(1)}, bf16[608,256]{1,0:T(8,128)(2,1)}, u32[]{:S(2)}) copy-start(bf16[608,256]{1,0:T(8,128)(2,1)} %copy-done.20) | copy-start | bytes 933892
  110.7 12.8 %collective-permute-start.32 = (bf16[3,608,128]{2,1,0:T(8,128)(2,1)}, bf16[3,608,128]{2,1,0:T(8,128)(2,1)S(1)}, u32[]{:S(2)}, u32[]{:S(2)}) collective-permute-start(bf16[3,608,128]{2,1,0:T(8,128)(2,1)} %pad_maximum_fusion.refs_12_), channel_id=1, source_target_pairs={{0,16},{16,0},{1,17},{17,1},{2,18},{18,2},{3,19},{19,3},{4,20},{20... | collective-permute-start | bytes 1400840 | tf_op jit(solution)/shard_map/ppermute | solution.py:35
  110.8 10.0 %collective-permute-start.27 = (bf16[608,128]{1,0:T(8,128)(2,1)}, bf16[608,128]{1,0:T(8,128)(2,1)S(1)}, u32[]{:S(2)}, u32[]{:S(2)}) collective-permute-start(bf16[608,128]{1,0:T(8,128)(2,1)} %collective-permute-done.19.refs_2_.refs_6_), channel_id=1, source_target_pairs={{0,16},{16,0},{1,17},{17,1},{2,18},{18,2},{3,19},{19,3},{4,20},{20... | collective-permute-start | bytes 466952 | tf_op jit(solution)/shard_map/ppermute | solution.py:35
  111.3 12.3 %collective-permute-start.33 = (bf16[3,608,128]{2,1,0:T(8,128)(2,1)}, bf16[3,608,128]{2,1,0:T(8,128)(2,1)S(1)}, u32[]{:S(2)}, u32[]{:S(2)}) collective-permute-start(bf16[3,608,128]{2,1,0:T(8,128)(2,1)} %collective-permute-done.29.refs_13_), channel_id=1, source_target_pairs={{0,16},{16,0},{1,17},{17,1},{2,18},{18,2},{3,19},{19,3},{4,20},{20... | collective-permute-start | bytes 1400840 | tf_op jit(solution)/shard_map/ppermute | solution.py:35
  115.7 7.8 %collective-permute-start.34 = (bf16[3,608,128]{2,1,0:T(8,128)(2,1)S(1)}, bf16[3,608,128]{2,1,0:T(8,128)(2,1)S(1)}, u32[]{:S(2)}, u32[]{:S(2)}) collective-permute-start(bf16[3,608,128]{2,1,0:T(8,128)(2,1)S(1)} %collective-permute-done.30.refs_14_), channel_id=1, source_target_pairs={{0,16},{16,0},{1,17},{17,1},{2,18},{18,2},{3,19},{19,3},{4,20},{20... | collective-permute-start | bytes 1400840 | tf_op jit(solution)/shard_map/ppermute | solution.py:35
  120.8 2.8 %collective-permute-start.35 = (bf16[3,608,128]{2,1,0:T(8,128)(2,1)S(1)}, bf16[3,608,128]{2,1,0:T(8,128)(2,1)S(1)}, u32[]{:S(2)}, u32[]{:S(2)}) collective-permute-start(bf16[3,608,128]{2,1,0:T(8,128)(2,1)S(1)} %collective-permute-done.31.refs_15_), channel_id=1, source_target_pairs={{0,16},{16,0},{1,17},{17,1},{2,18},{18,2},{3,19},{19,3},{4,20},{20... | collective-permute-start | bytes 1400840 | tf_op jit(solution)/shard_map/ppermute | solution.py:35
  120.8 2.7 %collective-permute-start.28 = (bf16[608,128]{1,0:T(8,128)(2,1)}, bf16[608,128]{1,0:T(8,128)(2,1)S(1)}, u32[]{:S(2)}, u32[]{:S(2)}) collective-permute-start(bf16[608,128]{1,0:T(8,128)(2,1)} %collective-permute-done.20.refs_3_.refs_7_), channel_id=1, source_target_pairs={{0,16},{16,0},{1,17},{17,1},{2,18},{18,2},{3,19},{19,3},{4,20},{20... | collective-permute-start | bytes 466952 | tf_op jit(solution)/shard_map/ppermute | solution.py:35
  (15 other events, 63.2 us)

commit v6 on v5

--- a/solution.py
+++ b/solution.py
@@ -24,7 +24,7 @@
 
 def split_rows(hidden):
     units = hidden // CHUNK
-    return CHUNK * max(units // 2, 1), CHUNK * max(units - 1, 1)
+    return CHUNK * max(units // 2, 1), (hidden - 1) // CHUNK * CHUNK
 
 
 def after(value, *others):
@@ -217,11 +217,9 @@
     pipelined(parts, product, finish)
 
 
-def forward_first_kernel(acts, modulation, w_in, w_out, mod, normed, stats, slope_out, total, in_buf, out_buf, sems):
+def forward_first_kernel(normed, w_in, w_out, slope_out, total, in_buf, out_buf, sems):
     parts = pieces(0, slope_out.shape[1])
     stream = Stream(w_in, in_buf, w_out, out_buf, parts, 0, sems)
-    turn_modulation(modulation, mod)
-    normalize(acts, mod, normed, stats)
     forward_products(stream, parts, 0, normed, in_buf, out_buf, slope_out, total, None, None)
 
 
@@ -248,23 +246,17 @@
     return params(4 * part * features * tokens, 4 * part * features + 4 * features * tokens, transcendentals)
 
 
-def forward_first(acts, modulation, w_in, w_out, part, name):
-    features, tokens = acts.shape[1:]
+def forward_first(normed, w_in, w_out, part, name):
+    tokens, features = normed.shape
     return pl.pallas_call(
         forward_first_kernel,
-        out_shape=(
-            struct((features, 8), F32),
-            struct((tokens, features), BF16),
-            struct((2, tokens), F32),
-            struct((tokens, part), F32),
-            struct((tokens, features), F32),
-        ),
-        in_specs=[WHOLE, WHOLE, HELD, HELD],
-        out_specs=[WHOLE] * 5,
+        out_shape=(struct((tokens, part), F32), struct((tokens, features), F32)),
+        in_specs=[WHOLE, HELD, HELD],
+        out_specs=[WHOLE] * 2,
         scratch_shapes=layer_scratch(part, features) + [pltpu.SemaphoreType.DMA((2 * len(pieces(0, part)),))],
         name=name,
         **layer_params(part, features, tokens, part * tokens),
-    )(acts, modulation, w_in, w_out)
+    )(normed, w_in, w_out)
 
 
 def forward_last(order, normed, before, w_in, w_out, start, blocks, name):
@@ -433,33 +425,50 @@
     return outs[: count // 2], outs[count // 2 : -1], outs[-1]
 
 
-def upstream_kernel(blocks, order, weight, own, arrived, *refs):
-    outs, (cot0, cot1_rows, full) = refs[:-3], refs[-3:]
+def prepare_kernel(blocks, order, acts, modulation, own, arrived, weight, *refs):
+    outs, (mod, normed, stats, cot0, cot1, cot1_rows, full, buf, sem) = refs[:blocks], refs[blocks:]
+    load = pltpu.make_async_copy(weight, buf, sem)
+    load.start()
     group = order[blocks]
     control = group == 0
     half = cot0.shape[1]
     lanes = pl.ds(pl.multiple_of(group * half, half), half)
     cot0[...] = jnp.where(control, own[:, lanes], arrived[:, lanes])
     mine = jnp.where(control, arrived[:, lanes], own[:, lanes])
+    cot1[...] = mine
     cot1_rows[...] = jnp.where(control, arrived[...], own[...])
-    full[...] = lax.dot_general(mine, weight[...], (((0,), (0,)), ((), ())), preferred_element_type=F32).T
+    turn_modulation(modulation, mod)
+    normalize(acts, mod, normed, stats)
+    load.wait()
+    full[...] = lax.dot_general(mine, buf[...], (((0,), (0,)), ((), ())), preferred_element_type=F32).T
     write_blocks(order, full, outs)
 
 
-def upstream_terms(order, weight, own, arrived, blocks):
+def prepare(order, acts, modulation, own, arrived, weight, blocks):
     rows, tokens = own.shape
-    half = tokens // 2
+    half, features = tokens // 2, weight.shape[1]
     outs = pl.pallas_call(
-        functools.partial(upstream_kernel, blocks),
+        functools.partial(prepare_kernel, blocks),
         out_shape=[struct((rows, half), F32)]
-        + [struct((rows, half), BF16)] * blocks
-        + [struct((rows, tokens), BF16)],
-        in_specs=[SCALARS] + [WHOLE] * 3,
-        out_specs=[WHOLE] * (blocks + 2),
-        scratch_shapes=[pltpu.VMEM((weight.shape[1], half), F32)],
-        name="upstream_terms",
-        **params(2 * weight.size * half, 2 * weight.size + 4 * blocks * rows * half, grant=12),
-    )(order, weight, own, arrived)
+        + [struct((rows, half), BF16)] * (blocks - 1)
+        + [
+            struct((features, 8), F32),
+            struct((tokens, features), BF16),
+            struct((2, tokens), F32),
+            struct((rows, half), BF16),
+            struct((rows, half), BF16),
+            struct((rows, tokens), BF16),
+        ],
+        in_specs=[SCALARS] + [WHOLE] * 4 + [HELD],
+        out_specs=[WHOLE] * (blocks + 6),
+        scratch_shapes=[
+            pltpu.VMEM((features, half), F32),
+            pltpu.VMEM(weight.shape, BF16),
+            pltpu.SemaphoreType.DMA(()),
+        ],
+        name="prepare",
+        **params(2 * weight.size * half, 2 * weight.size + 4 * blocks * rows * half, grant=50),
+    )(order, acts, modulation, own, arrived, weight)
     return outs[0], outs[1:blocks], *outs[blocks:]
 
 
@@ -483,51 +492,66 @@
     )(order, weight, *stack)
 
 
-def zero_grad_kernel(blocks, parts, order, dp_order, *refs):
-    cots, stacks, (out, lhs, rhs, stage, buf, sems) = refs[:parts], refs[parts:-6], refs[-6:]
-    near, near_other, far, far_other = (stacks[k * blocks : (k + 1) * blocks] for k in range(4))
-    rows, half = near[0].shape
+def zero_grad_kernel(blocks, first, count, order, dp_order, *refs):
+    cots, refs = (refs[:count], refs[count : 2 * count]), refs[2 * count :]
+    stacks = []
+    while len(refs) > (7 if first else 4):
+        stacks.append((refs[:blocks], refs[blocks : 2 * blocks]))
+        refs = refs[2 * blocks :]
+    before = None
+    if first:
+        before, out, lhs, rhs, stage, buf, sems = refs
+    else:
+        buf, lhs, rhs, stage = refs
+    rows, half = cots[0][0].shape
     group = order[blocks]
-    for part in range(parts):
-        lhs[:, pl.ds(pl.multiple_of(dp_order[part] * 2 * half, 2 * half), 2 * half)] = cots[part][...]
-        for side, sources in enumerate((near, near_other) if part == 0 else (far, far_other)):
-            at = Ellipsis if part == 0 else part - 1
-            values = [lambda source=source, at=at: source[at] for source in sources]
-            owner = group if side == 0 else 1 - group
-            lanes = pl.ds(pl.multiple_of((dp_order[part] * 2 + owner) * half, half), half)
+    for part in range(count):
+        slot = part // 2 * 2 + (dp_order[first + part] & 1)
+        for side, owner in enumerate((group, 1 - group)):
+            lanes = pl.ds(pl.multiple_of((slot * 2 + owner) * half, half), half)
+            lhs[:, lanes] = cots[side][part][...]
+            if len(stacks) == count:
+                values = [lambda source=source: source[...] for source in stacks[part][side]]
+            else:
+                values = [lambda source=source, part=part: source[part] for source in stacks[0][side]]
             place_blocks(rhs, lanes, stage, order, values, rows, side * (blocks + 1))
     copies = []
-    for k, (start, size) in enumerate(pieces(0, blocks * rows, CHUNK)):
+    for k, (start, size) in enumerate(pieces(0, blocks * rows)):
         columns = pl.ds(start, size)
-        buf[:, columns] = lax.dot_general(
-            lhs[...], rhs[columns, :], (((1,), (1,)), ((), ())), preferred_element_type=F32
-        )
-        copies.append(pltpu.make_async_copy(buf.at[:, columns], out.at[:, columns], sems.at[k]))
-        copies[-1].start()
+        value = against_rows(lhs[...], rhs[columns, :])
+        buf[:, columns] = value if before is None else before[:, columns] + value
+        if before is not None:
+            copies.append(pltpu.make_async_copy(buf.at[:, columns], out.at[:, columns], sems.at[k]))
+            copies[-1].start()
     for copy in copies:
         copy.wait()
 
 
-def zero_projection_grad(order, dp_order, cots, near, near_other, far, far_other):
-    blocks, (rows, half) = len(near), near[0].shape
-    parts = len(cots)
-    features, tokens = blocks * rows, parts * 2 * half
-
+def zero_projection_grad(order, dp_order, first, cots, cots_other, stacks, before, name):
+    blocks, (rows, half) = len(stacks[0][0]), cots[0].shape
+    count = len(cots)
+    features, tokens = blocks * rows, count * 2 * half
+    flat = [block for pair in stacks for side in pair for block in side]
+    extra = [] if before is None else [before]
+    scratch = [
+        pltpu.VMEM((rows, tokens), BF16),
+        pltpu.VMEM((features, tokens), BF16),
+        staging(rows, features, half),
+    ]
+    if extra:
+        scratch += [
+            pltpu.VMEM((rows, features), F32),
+            pltpu.SemaphoreType.DMA((len(pieces(0, features)),)),
+        ]
     return pl.pallas_call(
-        functools.partial(zero_grad_kernel, blocks, parts),
+        functools.partial(zero_grad_kernel, blocks, first, count),
         out_shape=struct((rows, features), F32),
-        in_specs=[SCALARS] * 2 + [WHOLE] * (parts + 4 * blocks),
-        out_specs=HELD,
-        scratch_shapes=[
-            pltpu.VMEM((rows, tokens), BF16),
-            pltpu.VMEM((features, tokens), BF16),
-            staging(rows, features, half),
-            pltpu.VMEM((rows, features), F32),
-            pltpu.SemaphoreType.DMA((len(pieces(0, features, CHUNK)),)),
-        ],
-        name="zero_projection_grad",
+        in_specs=[SCALARS] * 2 + [WHOLE] * (2 * count + len(flat) + len(extra)),
+        out_specs=HELD if extra else WHOLE,
+        scratch_shapes=scratch,
+        name=name,
         **params(2 * tokens * rows * features, 4 * rows * features + 2 * tokens * (rows + features), grant=28),
-    )(order, dp_order, *cots, *near, *near_other, *far, *far_other)
+    )(order, dp_order, *cots, *cots_other, *flat, *extra)
 
 
 def steps(values, level, *during):
@@ -556,25 +580,25 @@
     dp_order = lax.axis_index("dp").astype(jnp.int32) ^ jnp.arange(parts, dtype=jnp.int32)
 
     arrived = swap_grp(own_cot)
-    own_term, sent, cot0, cot1_rows = upstream_terms(order, zero_weight, own_cot, arrived, blocks)
+    own_term, sent, mod, normed, stats, cot0, cot1, cot1_rows = prepare(
+        order, acts, modulation, own_cot, arrived, zero_weight, blocks
+    )
     split, cut = split_rows(hidden)
-    mod, normed, stats, slope_a, total = forward_first(
-        after(acts, *sent), modulation, w_in, w_out, split, "forward_first"
-    )
+    slope_a, total = forward_first(after(normed, *sent), w_in, w_out, split, "forward_first")
     own_mod = block_of(mod, me, rows)
     own_gate = own_mod[:, 2:3]
+    cots = gather_dp(cot1)
     got = direct(sent, total)
     up_half = own_term + cot0.astype(F32) + sum(value.astype(F32) for value in got)
     up_rows = jnp.where(is_control, jnp.concatenate([up_half, swap_grp(up_half)], 1), own_cot.astype(F32))
     grad_rows = (own_gate * up_rows).astype(BF16)
 
     slope_b, kept, sent = forward_last(
-        order, after(normed, grad_rows), total, w_in, w_out, split, blocks, "forward_last"
+        order, after(normed, grad_rows, *cots), total, w_in, w_out, split, blocks, "forward_last"
     )
     gathered = [grad_rows] + direct([grad_rows] * (blocks - 1), kept)
-    cots = gather_dp(cot1_rows)
     grad, total = backward_first(
-        order, after(gathered, *sent, *cots), slope_a, slope_b, w_in, w_out, cut, "backward_first"
+        order, after(gathered, *sent), slope_a, slope_b, w_in, w_out, cut, "backward_first"
     )
     got = direct(sent, total)
     own_values = block_of(acts[0], me, rows).astype(F32)
@@ -592,11 +616,12 @@
         near = near + steps(near, level)
     near_other = [swap_grp(value) for value in near]
     residual = residual_rows(order, zero_weight, near)
-    far = [jnp.stack(far)]
-
+    cots_other = [swap_grp(value) for value in cots]
+
+    gathers = [[far[0]], [jnp.stack(far[1:])]]
     for level in range(levels):
         got = steps(sent, level)
-        far = far + steps(far, level)
+        gathers = [blocks_so_far + steps(blocks_so_far, level) for blocks_so_far in gathers]
         if level + 1 < levels:
             sent, kept, token_sums = fold(got, kept, token_sums)
     more = unpack_sums(got[0][-16:])
@@ -609,8 +634,13 @@
     residual = jnp.concatenate([swap_grp(residual), residual], 1)
     block_rows = jnp.where(is_control, out_rows, (sums + residual).astype(BF16))
 
-    far_other = [swap_grp(value) for value in far]
-    zero_grad = zero_projection_grad(order, dp_order, cots, near, near_other, far, far_other)
+    stacks = [(near, near_other)] + [(mine, [swap_grp(value) for value in mine]) for mine in gathers]
+    zero_grad = zero_projection_grad(
+        order, dp_order, 0, cots[:2], cots_other[:2], stacks[:2], None, "zero_projection_grad_first"
+    )
+    zero_grad = zero_projection_grad(
+        order, dp_order, 2, cots[2:], cots_other[2:], stacks[2:], zero_grad, "zero_projection_grad_last"
+    )
     return (block_rows[None], (up_rows + back)[None], zero_grad)
 
 

time: 132 us -> 136 us (1.030)
  waiting for transfers between devices: 28.3 us -> 18.2 us
  local copies, waits for them, and re-layouts: 6.41 us -> 12 us
  starting transfers between devices: 33.6 us -> 38.4 us
  Pallas kernels: 53.1 us -> 55.8 us
    ppermute x9 -> x12, waiting for transfers between devices: 17.3 us -> 8.77 us  [step(): return lax.ppermute(value, ('grp', 'fsdp'), pairs)]
    unnamed x55 -> x77, local copies, waits for them, and re-layouts: 6.39 us -> 12 us
    ppermute x9 -> x12, starting transfers between devices: 8.58 us -> 13 us  [step(): return lax.ppermute(value, ('grp', 'fsdp'), pairs)]
    pallas_call x3 -> x4, Pallas kernels: 18 us -> 21.8 us  [the longest x2 8.38 us: zero_projection_grad(): pl.pallas_call(functools.partial(zero_grad_kernel, blocks, first, count),...]
    ppermute x9, waiting for transfers between devices: 3.29 us -> 0.64 us  [send(): return lax.ppermute(value, ('grp', 'fsdp'), pairs)]
    ppermute x6, waiting for transfers between devices: 5.08 us -> 7.38 us  [gather_dp(): lax.ppermute(value, 'dp', [(i, i ^ mask) for i in range(length)])]
    pallas_call x1, Pallas kernels: 10.4 us -> 8.15 us  [backward_last(): pl.pallas_call(functools.partial(backward_last_kernel, start, rows), out_...]
    pallas_call x1, Pallas kernels: 10.1 us -> 11.7 us  [backward_first(): pl.pallas_call(functools.partial(backward_first_kernel, blocks, part), ou...]
  transfers between devices with their start and end apart: 36 -> 47, of which waited for: 11 -> 11; matrix products, arithmetic and copies ran while one was open for 4% -> 5% of each run, Pallas kernels for 34% -> 33%
where the time goes in v6:
time: 136 us; the launch traced here: 135 us
  Pallas kernels  55.8 us (41%)
  starting transfers between devices  38.4 us (28%)
  waiting for transfers between devices  18.2 us (13%)
  local copies, waits for them, and re-layouts  12 us (9%)
  other arithmetic  9.59 us (7%)
    ppermute x12, starting transfers between devices, step(): return lax.ppermute(value, ('grp', 'fsdp'), pairs)  13 us
    ppermute x9, starting transfers between devices, send(): return lax.ppermute(value, ('grp', 'fsdp'), pairs)  12.5 us
    unnamed x77, local copies, waits for them, and re-layouts  12 us
    pallas_call x1, Pallas kernels, backward_first(): pl.pallas_call(functools.partial(backward_first_kernel, blocks, part), ou...  11.7 us
    pallas_call x1, Pallas kernels, forward_last(): pl.pallas_call(functools.partial(forward_last_kernel, start), out_shape=[...  11.4 us
    ppermute x6, starting transfers between devices, gather_dp(): lax.ppermute(value, 'dp', [(i, i ^ mask) for i in range(length)])  9.03 us
    ppermute x12, waiting for transfers between devices, step(): return lax.ppermute(value, ('grp', 'fsdp'), pairs)  8.77 us
    pallas_call x2, Pallas kernels, zero_projection_grad(): pl.pallas_call(functools.partial(zero_grad_kernel, blocks, first, count),...  8.38 us
  transfers between devices with their start and end apart: 47, of which 11 were waited for; matrix products, arithmetic and copies ran while one was open for 5% of the time, Pallas kernels for 33%

profile of v6, /device:TPU:0, one launch (start us, length us, event | category | flops | bytes accessed | tf_op | source)
XLA Modules:
  0.0 135.3 jit_solution(14141685179814415874)
XLA Ops:
  1.1 0.8 copy.12.modulation
  2.7 1.0 copy-done.6
  3.6 6.0 %prepare.1 = (f32[608,128]{1,0:T(8,128)S(1)}, bf16[608,128]{1,0:T(8,128)(2,1)S(1)}, bf16[608,128]{1,0:T(8,128)(2,1)S(1)}, bf16[608,128]{1,0:T(8,128)(2,1)S(1)}, ...) custom-call(s32[9]{0:T(128)S(1)} %pad_add_fusion.order, ...), custom_call_target="tpu_custom_call" | custom-call | flops 378535936 | bytes 4202496 | tf_op jit(solution)/shard_map/prepare/pallas_call | solution.py:450
  10.3 2.8 %collective-permute-start.1 = (bf16[608,128]{1,0:T(8,128)(2,1)S(1)}, bf16[608,128]{1,0:T(8,128)(2,1)S(1)}, u32[]{:S(2)}, u32[]{:S(2)}) collective-permute-start(bf16[608,128]{1,0:T(8,128)(2,1)S(1)} %get-tuple-element.59), channel_id=1, source_target_pairs={{0,4},{4,0},{8,12},{12,8},{16,24},{20,28},{24,16},{28,20},{1,5},{5... | collective-permute-start | bytes 466952 | tf_op jit(solution)/shard_map/ppermute | solution.py:63
  13.1 1.5 %collective-permute-start.2 = (bf16[608,128]{1,0:T(8,128)(2,1)S(1)}, bf16[608,128]{1,0:T(8,128)(2,1)S(1)}, u32[]{:S(2)}, u32[]{:S(2)}) collective-permute-start(bf16[608,128]{1,0:T(8,128)(2,1)S(1)} %get-tuple-element.60), channel_id=1, source_target_pairs={{0,8},{4,12},{8,0},{12,4},{16,20},{20,16},{24,28},{28,24},{1,9},{5... | collective-permute-start | bytes 466952 | tf_op jit(solution)/shard_map/ppermute | solution.py:63
  14.6 1.3 copy-done.1
  15.9 7.4 %forward_first.1 = (f32[256,1024]{1,0:T(8,128)S(1)}, f32[256,2432]{1,0:T(8,128)}) custom-call(bf16[256,2432]{1,0:T(8,128)(2,1)S(1)} %copy-done.1, bf16[1,2432,2432]{2,1,0:T(8,128)(2,1)} %w_in.5, bf16[1,2432,2432]{2,1,0:T(8,128)(2,1)} %w_out.5), custom_call_target="tpu_custom_call" | custom-call | flops 2550136832 | bytes 12451840 | tf_op jit(solution)/shard_map/forward_first/pallas_call | solution.py:251
  23.4 0.8 add_add_fusion
  24.2 4.1 %collective-permute-start.7 = (bf16[608,128]{1,0:T(8,128)(2,1)}, bf16[608,128]{1,0:T(8,128)(2,1)}, u32[]{:S(2)}, u32[]{:S(2)}) collective-permute-start(bf16[608,128]{1,0:T(8,128)(2,1)} %copy-done.16), channel_id=1, source_target_pairs={{0,3},{1,2},{2,1},{3,0},{4,7},{5,6},{6,5},{7,4},{8,11},{9,10},{10,... | collective-permute-start | bytes 466952 | tf_op jit(solution)/shard_map/ppermute | solution.py:69
  29.2 1.3 multiply_convert_fusion.refs_0_
  30.6 2.7 %collective-permute-start.13 = (bf16[608,256]{1,0:T(8,128)(2,1)S(1)}, bf16[608,256]{1,0:T(8,128)(2,1)S(1)}, u32[]{:S(2)}, u32[]{:S(2)}) collective-permute-start(bf16[608,256]{1,0:T(8,128)(2,1)S(1)} %multiply_convert_fusion.refs_0_), channel_id=1, source_target_pairs={{0,12},{4,8},{8,4},{12,0},{16,28},{20,24},{24,20},{28,16},{1,13},{... | collective-permute-start | bytes 933896 | tf_op jit(solution)/shard_map/ppermute | solution.py:63
  33.8 1.4 %collective-permute-start.11 = (bf16[608,256]{1,0:T(8,128)(2,1)S(1)}, bf16[608,256]{1,0:T(8,128)(2,1)S(1)}, u32[]{:S(2)}, u32[]{:S(2)}) collective-permute-start(bf16[608,256]{1,0:T(8,128)(2,1)S(1)} %multiply_convert_fusion.refs_0_), channel_id=1, source_target_pairs={{0,4},{4,0},{8,12},{12,8},{16,24},{20,28},{24,16},{28,20},{1,5},{5... | collective-permute-start | bytes 933896 | tf_op jit(solution)/shard_map/ppermute | solution.py:63
  35.2 7.1 %collective-permute-done.6.refs_0_ = bf16[608,128]{1,0:T(8,128)(2,1)S(1)} collective-permute-done((bf16[608,128]{1,0:T(8,128)(2,1)}, bf16[608,128]{1,0:T(8,128)(2,1)S(1)}, u32[]{:S(2)}, u32[]{:S(2)}) %collective-permute-start.6) | collective-permute-done | bytes 155680 | tf_op jit(solution)/shard_map/ppermute | solution.py:69
  43.0 11.4 %forward_last.1 = (f32[256,1408]{1,0:T(8,128)}, f32[608,256]{1,0:T(8,128)S(1)}, bf16[608,256]{1,0:T(8,128)(2,1)S(1)}, bf16[608,256]{1,0:T(8,128)(2,1)S(1)}, bf16[608,256]{1,0:T(8,128)(2,1)S(1)}) custom-call(s32[9]{0:T(128)S(1)} %pad_add_fusion.order, bf16[256,2432]{1,0:T(8,128)(2,1)S(1)} %copy-done.2, f32[256,2432]{1,0:T(8,128)} %get-tuple-element.63.before, ...), custom_call_target="tpu_custom_call" | custom-call | flops 3506438144 | bytes 16187392 | tf_op jit(solution)/shard_map/forward_last/pallas_call | solution.py:265
  54.4 1.6 %collective-permute-start.8 = (bf16[608,256]{1,0:T(8,128)(2,1)S(1)}, bf16[608,256]{1,0:T(8,128)(2,1)S(1)}, u32[]{:S(2)}, u32[]{:S(2)}) collective-permute-start(bf16[608,256]{1,0:T(8,128)(2,1)S(1)} %get-tuple-element.70), channel_id=1, source_target_pairs={{0,4},{4,0},{8,12},{12,8},{16,24},{20,28},{24,16},{28,20},{1,5},{5... | collective-permute-start | bytes 933896 | tf_op jit(solution)/shard_map/ppermute | solution.py:63
  56.0 1.5 %collective-permute-start.9 = (bf16[608,256]{1,0:T(8,128)(2,1)S(1)}, bf16[608,256]{1,0:T(8,128)(2,1)S(1)}, u32[]{:S(2)}, u32[]{:S(2)}) collective-permute-start(bf16[608,256]{1,0:T(8,128)(2,1)S(1)} %get-tuple-element.71), channel_id=1, source_target_pairs={{0,8},{4,12},{8,0},{12,4},{16,20},{20,16},{24,28},{28,24},{1,9},{5... | collective-permute-start | bytes 933896 | tf_op jit(solution)/shard_map/ppermute | solution.py:63
  58.0 11.7 %backward_first.1 = (bf16[256,2432]{1,0:T(8,128)(2,1)S(1)}, f32[256,2432]{1,0:T(8,128)}) custom-call(s32[9]{0:T(128)S(1)} %pad_add_fusion.order, bf16[608,256]{1,0:T(8,128)(2,1)S(1)} %multiply_convert_fusion.refs_0_, bf16[608,256]{1,0:T(8,128)(2,1)S(1)} %collective-permute-done.11.refs_1_, bf16[608,256]{1,0:T(8,128)(2,1)S(1)} %collective-permute-done.12.refs_2_, ...), custom_call_target="tpu_custom_call" | custom-call | flops 5100273664 | bytes 22413312 | tf_op jit(solution)/shard_map/backward_first/pallas_call | solution.py:323
  69.7 1.0 copy-done.8
  71.3 2.1 %fusion.16 = (bf16[608,256]{1,0:T(8,128)(2,1)S(1)}, f32[608,256]{1,0:T(8,128)}) fusion(f32[608,256]{1,0:T(8,128)S(1)} %get-tuple-element.69, bf16[608,256]{1,0:T(8,128)(2,1)S(1)} %collective-permute-done.10, bf16[608,256]{1,0:T(8,128)(2,1)S(1)} %collective-permute-done.9, bf16[608,256]{1,0:T(8,128)(2,1)S(1)} %collective-permute-done.8, ...), kind=kLoop, calls=%fused_computation.35 | loop fusion | flops 1556480 | bytes 2804100 | tf_op jit(solution)/shard_map/convert_element_type | solution.py:606
  73.6 1.4 %collective-permute-done.14 = bf16[608,128]{1,0:T(8,128)(2,1)S(1)} collective-permute-done((bf16[608,128]{1,0:T(8,128)(2,1)S(1)}, bf16[608,128]{1,0:T(8,128)(2,1)S(1)}, u32[]{:S(2)}, u32[]{:S(2)}) %collective-permute-start.14) | collective-permute-done | bytes 155680 | tf_op jit(solution)/shard_map/ppermute | solution.py:35
  74.9 1.6 %collective-permute-start.18 = (bf16[608,128]{1,0:T(8,128)(2,1)S(1)}, bf16[608,128]{1,0:T(8,128)(2,1)S(1)}, u32[]{:S(2)}, u32[]{:S(2)}) collective-permute-start(bf16[608,128]{1,0:T(8,128)(2,1)S(1)} %slice_select_fusion.refs_0_.refs_4_), channel_id=1, source_target_pairs={{0,4},{4,0},{8,12},{12,8},{16,24},{20,28},{24,16},{28,20},{1,5},{5... | collective-permute-start | bytes 466952 | tf_op jit(solution)/shard_map/ppermute | solution.py:47
  76.5 2.5 %collective-permute-start.17 = (bf16[608,128]{1,0:T(8,128)(2,1)S(1)}, bf16[608,128]{1,0:T(8,128)(2,1)S(1)}, u32[]{:S(2)}, u32[]{:S(2)}) collective-permute-start(bf16[608,128]{1,0:T(8,128)(2,1)S(1)} %slice_select_fusion.refs_0_.refs_4_), channel_id=1, source_target_pairs={{0,3},{1,2},{2,1},{3,0},{4,7},{5,6},{6,5},{7,4},{8,11},{9,10},{10,... | collective-permute-start | bytes 466952 | tf_op jit(solution)/shard_map/ppermute | solution.py:69
  79.0 1.9 %collective-permute-start.15 = (bf16[608,128]{1,0:T(8,128)(2,1)S(1)}, bf16[608,128]{1,0:T(8,128)(2,1)}, u32[]{:S(2)}, u32[]{:S(2)}) collective-permute-start(bf16[608,128]{1,0:T(8,128)(2,1)S(1)} %slice_select_fusion.refs_0_.refs_4_), channel_id=1, source_target_pairs={{0,1},{1,0},{2,3},{3,2},{4,5},{5,4},{6,7},{7,6},{8,9},{9,8},{10,11... | collective-permute-start | bytes 466952 | tf_op jit(solution)/shard_map/ppermute | solution.py:69
  81.4 8.2 %backward_last.1 = (bf16[624,256]{1,0:T(8,128)(2,1)}, bf16[624,256]{1,0:T(8,128)(2,1)}, f32[608,256]{1,0:T(8,128)S(1)}, f32[608,256]{1,0:T(8,128)S(1)}, f32[2,256]{1,0:T(2,128)S(1)}) custom-call(s32[9]{0:T(128)S(1)} %pad_add_fusion.order, bf16[256,2432]{1,0:T(8,128)(2,1)} %copy-done.8, f32[256,2432]{1,0:T(8,128)} %get-tuple-element.82.before, ...), custom_call_target="tpu_custom_call" | custom-call | flops 956301312 | bytes 6225920 | tf_op jit(solution)/shard_map/backward_last/pallas_call | solution.py:376
  89.6 0.8 copy-done.12
  90.4 0.9 copy-done.14
  92.2 1.4 %collective-permute-start.19 = (bf16[608,128]{1,0:T(8,128)(2,1)S(1)}, bf16[608,128]{1,0:T(8,128)(2,1)S(1)}, u32[]{:S(2)}, u32[]{:S(2)}) collective-permute-start(bf16[608,128]{1,0:T(8,128)(2,1)S(1)} %slice_select_fusion.refs_0_.refs_4_), channel_id=1, source_target_pairs={{0,8},{4,12},{8,0},{12,4},{16,20},{20,16},{24,28},{28,24},{1,9},{5... | collective-permute-start | bytes 466952 | tf_op jit(solution)/shard_map/ppermute | solution.py:47
  96.6 1.4 %collective-permute-start.41 = (bf16[608,128]{1,0:T(8,128)(2,1)}, bf16[608,128]{1,0:T(8,128)(2,1)}, u32[]{:S(2)}, u32[]{:S(2)}) collective-permute-start(bf16[608,128]{1,0:T(8,128)(2,1)} %collective-permute-done.15.refs_12_), channel_id=1, source_target_pairs={{0,8},{4,12},{8,0},{12,4},{16,20},{20,16},{24,28},{28,24},{1,9},{5... | collective-permute-start | bytes 466952 | tf_op jit(solution)/shard_map/ppermute | solution.py:47
  98.0 0.9 collective-permute-start.40
  99.6 1.1 collective-permute-start.22
  100.7 0.9 collective-permute-start.23
  102.3 1.1 collective-permute-done.41.refs_14_
  103.5 1.7 %collective-permute-start.42 = (bf16[608,128]{1,0:T(8,128)(2,1)}, bf16[608,128]{1,0:T(8,128)(2,1)S(1)}, u32[]{:S(2)}, u32[]{:S(2)}) collective-permute-start(bf16[608,128]{1,0:T(8,128)(2,1)} %collective-permute-done.40.refs_13_), channel_id=1, source_target_pairs={{0,8},{4,12},{8,0},{12,4},{16,20},{20,16},{24,28},{28,24},{1,9},{5... | collective-permute-start | bytes 466952 | tf_op jit(solution)/shard_map/ppermute | solution.py:47
  105.2 1.0 pad_maximum_fusion.refs_4_
  106.5 0.9 copy-done.10
  107.4 1.5 %residual_rows.1 = f32[608,128]{1,0:T(8,128)S(1)} custom-call(s32[9]{0:T(128)S(1)} %pad_add_fusion.order, bf16[608,2432]{1,0:T(8,128)(2,1)S(1)} %copy-done, bf16[608,128]{1,0:T(8,128)(2,1)S(1)} %slice_select_fusion.refs_0_.refs_4_, bf16[608,128]{1,0:T(8,128)(2,1)S(1)} %collective-permute-done.18.refs_1_.refs_5_, ...), custom_call_target="tpu_custom_call" | custom-call | flops 378535936 | bytes 4202496 | tf_op jit(solution)/shard_map/residual_rows/pallas_call | solution.py:484
  109.1 1.6 %collective-permute-done.42.refs_15_ = bf16[608,128]{1,0:T(8,128)(2,1)S(1)} collective-permute-done((bf16[608,128]{1,0:T(8,128)(2,1)}, bf16[608,128]{1,0:T(8,128)(2,1)S(1)}, u32[]{:S(2)}, u32[]{:S(2)}) %collective-permute-start.42) | collective-permute-done | bytes 155680 | tf_op jit(solution)/shard_map/ppermute | solution.py:47
  111.2 0.8 collective-permute-done.23.refs_1_
  112.3 1.2 fold.1
  113.9 1.2 collective-permute-start.28
  115.3 1.2 collective-permute-start.29
  116.5 0.8 collective-permute-start.24
  117.4 3.7 %zero_projection_grad_first.1.refs_12_ = f32[608,2432]{1,0:T(8,128)S(1)} custom-call(s32[9]{0:T(128)S(1)} %pad_add_fusion.order, s32[4]{0:T(128)S(1)} %iota_xor_fusion.dp_order, bf16[608,128]{1,0:T(8,128)(2,1)S(1)} %copy-done.18, bf16[608,128]{1,0:T(8,128)(2,1)S(1)} %copy-done.20, bf16[608,128]{1,0:T(8,128)(2,1)S(1)} %copy-done.22, ...), custom_call_target="tpu_custom_call" | custom-call | flops 1514143744 | bytes 9027584 | tf_op jit(solution)/shard_map/zero_projection_grad_first/pallas_call | solution.py:546
  121.2 0.9 fusion.8
  122.6 1.5 %collective-permute-done.29.refs_7_ = bf16[2,608,128]{2,1,0:T(8,128)(2,1)S(1)} collective-permute-done((bf16[2,608,128]{2,1,0:T(8,128)(2,1)S(1)}, bf16[2,608,128]{2,1,0:T(8,128)(2,1)S(1)}, u32[]{:S(2)}, u32[]{:S(2)}) %collective-permute-start.29) | collective-permute-done | bytes 311328 | tf_op jit(solution)/shard_map/ppermute | solution.py:47
  124.1 3.4 %collective-permute-done.24 = bf16[624,256]{1,0:T(8,128)(2,1)S(1)} collective-permute-done((bf16[624,256]{1,0:T(8,128)(2,1)S(1)}, bf16[624,256]{1,0:T(8,128)(2,1)S(1)}, u32[]{:S(2)}, u32[]{:S(2)}) %collective-permute-start.24) | collective-permute-done | bytes 319520 | tf_op jit(solution)/shard_map/ppermute | solution.py:47
  128.2 2.3 %fusion.5 = f32[1,608,256]{2,1,0:T(8,128)} fusion(f32[608,256]{1,0:T(8,128)S(1)} %get-tuple-element.101, f32[608,128]{1,0:T(8,128)} %collective-permute-done.4, f32[608,128]{1,0:T(8,128)} %add_add_fusion, bf16[624,256]{1,0:T(8,128)(2,1)S(1)} %collective-permute-done.24, f32[256]{0:T(256)S(1)} %bitcast.24, f32[256]{0:T(256)S(1)} %bitcast.26, ...), kind=kLoop, calls=%fused_computation.7 | loop fusion | flops 2179072 | bytes 2808197 | tf_op jit(solution)/shard_map/broadcast_in_dim | solution.py:644
  130.5 4.6 %zero_projection_grad_last.1 = f32[608,2432]{1,0:T(8,128)} custom-call(s32[9]{0:T(128)S(1)} %pad_add_fusion.order, s32[4]{0:T(128)S(1)} %iota_xor_fusion.dp_order, bf16[608,128]{1,0:T(8,128)(2,1)S(1)} %copy-done.32, bf16[608,128]{1,0:T(8,128)(2,1)} %collective-permute-done.7.refs_1_, bf16[608,128]{1,0:T(8,128)(2,1)S(1)} %collective-permute-done.25.refs_2_, ...), custom_call_target="tpu_custom_call" | custom-call | flops 1514143744 | bytes 9027584 | tf_op jit(solution)/shard_map/zero_projection_grad_last/pallas_call | solution.py:546
  (147 shorter events, 14.1 us)
Async XLA Ops:
  0.6 2.0 %collective-permute-start = (bf16[608,256]{1,0:T(8,128)(2,1)}, bf16[608,256]{1,0:T(8,128)(2,1)S(1)}, u32[]{:S(2)}, u32[]{:S(2)}) collective-permute-start(bf16[608,256]{1,0:T(8,128)(2,1)} %bitcast.19), channel_id=1, source_target_pairs={{0,16},{16,0},{1,17},{17,1},{2,18},{18,2},{3,19},{19,3},{4,20},{20... | collective-permute-start | bytes 933896 | tf_op jit(solution)/shard_map/ppermute | solution.py:35
  10.3 13.0 %collective-permute-start.1 = (bf16[608,128]{1,0:T(8,128)(2,1)S(1)}, bf16[608,128]{1,0:T(8,128)(2,1)S(1)}, u32[]{:S(2)}, u32[]{:S(2)}) collective-permute-start(bf16[608,128]{1,0:T(8,128)(2,1)S(1)} %get-tuple-element.59), channel_id=1, source_target_pairs={{0,4},{4,0},{8,12},{12,8},{16,24},{20,28},{24,16},{28,20},{1,5},{5... | collective-permute-start | bytes 466952 | tf_op jit(solution)/shard_map/ppermute | solution.py:63
  13.1 10.3 %collective-permute-start.2 = (bf16[608,128]{1,0:T(8,128)(2,1)S(1)}, bf16[608,128]{1,0:T(8,128)(2,1)S(1)}, u32[]{:S(2)}, u32[]{:S(2)}) collective-permute-start(bf16[608,128]{1,0:T(8,128)(2,1)S(1)} %get-tuple-element.60), channel_id=1, source_target_pairs={{0,8},{4,12},{8,0},{12,4},{16,20},{20,16},{24,28},{28,24},{1,9},{5... | collective-permute-start | bytes 466952 | tf_op jit(solution)/shard_map/ppermute | solution.py:63
  14.6 8.8 %collective-permute-start.3 = (bf16[608,128]{1,0:T(8,128)(2,1)S(1)}, bf16[608,128]{1,0:T(8,128)(2,1)S(1)}, u32[]{:S(2)}, u32[]{:S(2)}) collective-permute-start(bf16[608,128]{1,0:T(8,128)(2,1)S(1)} %get-tuple-element.61), channel_id=1, source_target_pairs={{0,12},{4,8},{8,4},{12,0},{16,28},{20,24},{24,20},{28,16},{1,13},{... | collective-permute-start | bytes 466952 | tf_op jit(solution)/shard_map/ppermute | solution.py:63
  24.2 5.1 %collective-permute-start.4 = (f32[608,128]{1,0:T(8,128)}, f32[608,128]{1,0:T(8,128)}, u32[]{:S(2)}, u32[]{:S(2)}) collective-permute-start(f32[608,128]{1,0:T(8,128)} %add_add_fusion), channel_id=1, source_target_pairs={{0,16},{16,0},{1,17},{17,1},{2,18},{18,2},{3,19},{19,3},{4,20},{20... | collective-permute-start | bytes 933896 | tf_op jit(solution)/shard_map/ppermute | solution.py:35
  24.2 9.6 %collective-permute-start.7 = (bf16[608,128]{1,0:T(8,128)(2,1)}, bf16[608,128]{1,0:T(8,128)(2,1)}, u32[]{:S(2)}, u32[]{:S(2)}) collective-permute-start(bf16[608,128]{1,0:T(8,128)(2,1)} %copy-done.16), channel_id=1, source_target_pairs={{0,3},{1,2},{2,1},{3,0},{4,7},{5,6},{6,5},{7,4},{8,11},{9,10},{10,... | collective-permute-start | bytes 466952 | tf_op jit(solution)/shard_map/ppermute | solution.py:69
  28.2 14.1 %collective-permute-start.6 = (bf16[608,128]{1,0:T(8,128)(2,1)}, bf16[608,128]{1,0:T(8,128)(2,1)S(1)}, u32[]{:S(2)}, u32[]{:S(2)}) collective-permute-start(bf16[608,128]{1,0:T(8,128)(2,1)} %copy-done.16), channel_id=1, source_target_pairs={{0,2},{1,3},{2,0},{3,1},{4,6},{5,7},{6,4},{7,5},{8,10},{9,11},{10,... | collective-permute-start | bytes 466952 | tf_op jit(solution)/shard_map/ppermute | solution.py:69
  28.2 14.7 %collective-permute-start.5 = (bf16[608,128]{1,0:T(8,128)(2,1)}, bf16[608,128]{1,0:T(8,128)(2,1)S(1)}, u32[]{:S(2)}, u32[]{:S(2)}) collective-permute-start(bf16[608,128]{1,0:T(8,128)(2,1)} %copy-done.16), channel_id=1, source_target_pairs={{0,1},{1,0},{2,3},{3,2},{4,5},{5,4},{6,7},{7,6},{8,9},{9,8},{10,11... | collective-permute-start | bytes 466952 | tf_op jit(solution)/shard_map/ppermute | solution.py:69
  30.6 27.0 %collective-permute-start.13 = (bf16[608,256]{1,0:T(8,128)(2,1)S(1)}, bf16[608,256]{1,0:T(8,128)(2,1)S(1)}, u32[]{:S(2)}, u32[]{:S(2)}) collective-permute-start(bf16[608,256]{1,0:T(8,128)(2,1)S(1)} %multiply_convert_fusion.refs_0_), channel_id=1, source_target_pairs={{0,12},{4,8},{8,4},{12,0},{16,28},{20,24},{24,20},{28,16},{1,13},{... | collective-permute-start | bytes 933896 | tf_op jit(solution)/shard_map/ppermute | solution.py:63
  33.3 24.7 %collective-permute-start.12 = (bf16[608,256]{1,0:T(8,128)(2,1)S(1)}, bf16[608,256]{1,0:T(8,128)(2,1)S(1)}, u32[]{:S(2)}, u32[]{:S(2)}) collective-permute-start(bf16[608,256]{1,0:T(8,128)(2,1)S(1)} %multiply_convert_fusion.refs_0_), channel_id=1, source_target_pairs={{0,8},{4,12},{8,0},{12,4},{16,20},{20,16},{24,28},{28,24},{1,9},{5... | collective-permute-start | bytes 933896 | tf_op jit(solution)/shard_map/ppermute | solution.py:63
  33.8 24.2 %collective-permute-start.11 = (bf16[608,256]{1,0:T(8,128)(2,1)S(1)}, bf16[608,256]{1,0:T(8,128)(2,1)S(1)}, u32[]{:S(2)}, u32[]{:S(2)}) collective-permute-start(bf16[608,256]{1,0:T(8,128)(2,1)S(1)} %multiply_convert_fusion.refs_0_), channel_id=1, source_target_pairs={{0,4},{4,0},{8,12},{12,8},{16,24},{20,28},{24,16},{28,20},{1,5},{5... | collective-permute-start | bytes 933896 | tf_op jit(solution)/shard_map/ppermute | solution.py:63
  43.0 37.9 %copy-start.19 = (bf16[608,128]{1,0:T(8,128)(2,1)}, bf16[608,128]{1,0:T(8,128)(2,1)S(1)}, u32[]{:S(2)}) copy-start(bf16[608,128]{1,0:T(8,128)(2,1)S(1)} %collective-permute-done.5.refs_1_) | copy-start | bytes 466948
  54.4 16.3 %collective-permute-start.8 = (bf16[608,256]{1,0:T(8,128)(2,1)S(1)}, bf16[608,256]{1,0:T(8,128)(2,1)S(1)}, u32[]{:S(2)}, u32[]{:S(2)}) collective-permute-start(bf16[608,256]{1,0:T(8,128)(2,1)S(1)} %get-tuple-element.70), channel_id=1, source_target_pairs={{0,4},{4,0},{8,12},{12,8},{16,24},{20,28},{24,16},{28,20},{1,5},{5... | collective-permute-start | bytes 933896 | tf_op jit(solution)/shard_map/ppermute | solution.py:63
  56.0 14.7 %collective-permute-start.9 = (bf16[608,256]{1,0:T(8,128)(2,1)S(1)}, bf16[608,256]{1,0:T(8,128)(2,1)S(1)}, u32[]{:S(2)}, u32[]{:S(2)}) collective-permute-start(bf16[608,256]{1,0:T(8,128)(2,1)S(1)} %get-tuple-element.71), channel_id=1, source_target_pairs={{0,8},{4,12},{8,0},{12,4},{16,20},{20,16},{24,28},{28,24},{1,9},{5... | collective-permute-start | bytes 933896 | tf_op jit(solution)/shard_map/ppermute | solution.py:63
  57.5 13.8 %collective-permute-start.10 = (bf16[608,256]{1,0:T(8,128)(2,1)S(1)}, bf16[608,256]{1,0:T(8,128)(2,1)S(1)}, u32[]{:S(2)}, u32[]{:S(2)}) collective-permute-start(bf16[608,256]{1,0:T(8,128)(2,1)S(1)} %get-tuple-element.72), channel_id=1, source_target_pairs={{0,12},{4,8},{8,4},{12,0},{16,28},{20,24},{24,20},{28,16},{1,13},{... | collective-permute-start | bytes 933896 | tf_op jit(solution)/shard_map/ppermute | solution.py:63
  73.5 1.4 %collective-permute-start.14 = (bf16[608,128]{1,0:T(8,128)(2,1)S(1)}, bf16[608,128]{1,0:T(8,128)(2,1)S(1)}, u32[]{:S(2)}, u32[]{:S(2)}) collective-permute-start(bf16[608,128]{1,0:T(8,128)(2,1)S(1)} %slice.65), channel_id=1, source_target_pairs={{0,16},{16,0},{1,17},{17,1},{2,18},{18,2},{3,19},{19,3},{4,20},{20... | collective-permute-start | bytes 466952 | tf_op jit(solution)/shard_map/ppermute | solution.py:35
  74.9 6.0 %collective-permute-start.18 = (bf16[608,128]{1,0:T(8,128)(2,1)S(1)}, bf16[608,128]{1,0:T(8,128)(2,1)S(1)}, u32[]{:S(2)}, u32[]{:S(2)}) collective-permute-start(bf16[608,128]{1,0:T(8,128)(2,1)S(1)} %slice_select_fusion.refs_0_.refs_4_), channel_id=1, source_target_pairs={{0,4},{4,0},{8,12},{12,8},{16,24},{20,28},{24,16},{28,20},{1,5},{5... | collective-permute-start | bytes 466952 | tf_op jit(solution)/shard_map/ppermute | solution.py:47
  76.5 14.8 %collective-permute-start.17 = (bf16[608,128]{1,0:T(8,128)(2,1)S(1)}, bf16[608,128]{1,0:T(8,128)(2,1)S(1)}, u32[]{:S(2)}, u32[]{:S(2)}) collective-permute-start(bf16[608,128]{1,0:T(8,128)(2,1)S(1)} %slice_select_fusion.refs_0_.refs_4_), channel_id=1, source_target_pairs={{0,3},{1,2},{2,1},{3,0},{4,7},{5,6},{6,5},{7,4},{8,11},{9,10},{10,... | collective-permute-start | bytes 466952 | tf_op jit(solution)/shard_map/ppermute | solution.py:69
  79.0 12.5 %collective-permute-start.16 = (bf16[608,128]{1,0:T(8,128)(2,1)S(1)}, bf16[608,128]{1,0:T(8,128)(2,1)S(1)}, u32[]{:S(2)}, u32[]{:S(2)}) collective-permute-start(bf16[608,128]{1,0:T(8,128)(2,1)S(1)} %slice_select_fusion.refs_0_.refs_4_), channel_id=1, source_target_pairs={{0,2},{1,3},{2,0},{3,1},{4,6},{5,7},{6,4},{7,5},{8,10},{9,11},{10,... | collective-permute-start | bytes 466952 | tf_op jit(solution)/shard_map/ppermute | solution.py:69
  79.0 12.5 %collective-permute-start.15 = (bf16[608,128]{1,0:T(8,128)(2,1)S(1)}, bf16[608,128]{1,0:T(8,128)(2,1)}, u32[]{:S(2)}, u32[]{:S(2)}) collective-permute-start(bf16[608,128]{1,0:T(8,128)(2,1)S(1)} %slice_select_fusion.refs_0_.refs_4_), channel_id=1, source_target_pairs={{0,1},{1,0},{2,3},{3,2},{4,5},{5,4},{6,7},{7,6},{8,9},{9,8},{10,11... | collective-permute-start | bytes 466952 | tf_op jit(solution)/shard_map/ppermute | solution.py:69
  80.9 13.0 %collective-permute-start.34 = (bf16[608,128]{1,0:T(8,128)(2,1)S(1)}, bf16[608,128]{1,0:T(8,128)(2,1)S(1)}, u32[]{:S(2)}, u32[]{:S(2)}) collective-permute-start(bf16[608,128]{1,0:T(8,128)(2,1)S(1)} %copy-done.17), channel_id=1, source_target_pairs={{0,16},{16,0},{1,17},{17,1},{2,18},{18,2},{3,19},{19,3},{4,20},{20... | collective-permute-start | bytes 466952 | tf_op jit(solution)/shard_map/ppermute | solution.py:35
  80.9 14.2 %collective-permute-start.35 = (bf16[608,128]{1,0:T(8,128)(2,1)S(1)}, bf16[608,128]{1,0:T(8,128)(2,1)S(1)}, u32[]{:S(2)}, u32[]{:S(2)}) collective-permute-start(bf16[608,128]{1,0:T(8,128)(2,1)S(1)} %collective-permute-done.5.refs_1_), channel_id=1, source_target_pairs={{0,16},{16,0},{1,17},{17,1},{2,18},{18,2},{3,19},{19,3},{4,20},{20... | collective-permute-start | bytes 466952 | tf_op jit(solution)/shard_map/ppermute | solution.py:35
  92.2 3.7 %collective-permute-start.36 = (bf16[608,128]{1,0:T(8,128)(2,1)S(1)}, bf16[608,128]{1,0:T(8,128)(2,1)S(1)}, u32[]{:S(2)}, u32[]{:S(2)}) collective-permute-start(bf16[608,128]{1,0:T(8,128)(2,1)S(1)} %slice_select_fusion.refs_0_.refs_4_), channel_id=1, source_target_pairs={{0,16},{16,0},{1,17},{17,1},{2,18},{18,2},{3,19},{19,3},{4,20},{20... | collective-permute-start | bytes 466952 | tf_op jit(solution)/shard_map/ppermute | solution.py:35
  92.2 5.8 %collective-permute-start.19 = (bf16[608,128]{1,0:T(8,128)(2,1)S(1)}, bf16[608,128]{1,0:T(8,128)(2,1)S(1)}, u32[]{:S(2)}, u32[]{:S(2)}) collective-permute-start(bf16[608,128]{1,0:T(8,128)(2,1)S(1)} %slice_select_fusion.refs_0_.refs_4_), channel_id=1, source_target_pairs={{0,8},{4,12},{8,0},{12,4},{16,20},{20,16},{24,28},{28,24},{1,9},{5... | collective-permute-start | bytes 466952 | tf_op jit(solution)/shard_map/ppermute | solution.py:47
  93.6 5.4 %collective-permute-start.37 = (bf16[608,128]{1,0:T(8,128)(2,1)S(1)}, bf16[608,128]{1,0:T(8,128)(2,1)S(1)}, u32[]{:S(2)}, u32[]{:S(2)}) collective-permute-start(bf16[608,128]{1,0:T(8,128)(2,1)S(1)} %collective-permute-done.18.refs_1_.refs_5_), channel_id=1, source_target_pairs={{0,16},{16,0},{1,17},{17,1},{2,18},{18,2},{3,19},{19,3},{4,20},{20... | collective-permute-start | bytes 466952 | tf_op jit(solution)/shard_map/ppermute | solution.py:35
  94.6 6.1 %collective-permute-start.20 = (bf16[608,128]{1,0:T(8,128)(2,1)S(1)}, bf16[608,128]{1,0:T(8,128)(2,1)S(1)}, u32[]{:S(2)}, u32[]{:S(2)}) collective-permute-start(bf16[608,128]{1,0:T(8,128)(2,1)S(1)} %collective-permute-done.18.refs_1_.refs_5_), channel_id=1, source_target_pairs={{0,8},{4,12},{8,0},{12,4},{16,20},{20,16},{24,28},{28,24},{1,9},{5... | collective-permute-start | bytes 466952 | tf_op jit(solution)/shard_map/ppermute | solution.py:47
  95.8 5.9 %collective-permute-start.43 = (bf16[608,128]{1,0:T(8,128)(2,1)}, bf16[608,128]{1,0:T(8,128)(2,1)S(1)}, u32[]{:S(2)}, u32[]{:S(2)}) collective-permute-start(bf16[608,128]{1,0:T(8,128)(2,1)} %collective-permute-done.15.refs_12_), channel_id=1, source_target_pairs={{0,16},{16,0},{1,17},{17,1},{2,18},{18,2},{3,19},{19,3},{4,20},{20... | collective-permute-start | bytes 466952 | tf_op jit(solution)/shard_map/ppermute | solution.py:35
  96.6 6.8 %collective-permute-start.41 = (bf16[608,128]{1,0:T(8,128)(2,1)}, bf16[608,128]{1,0:T(8,128)(2,1)}, u32[]{:S(2)}, u32[]{:S(2)}) collective-permute-start(bf16[608,128]{1,0:T(8,128)(2,1)} %collective-permute-done.15.refs_12_), channel_id=1, source_target_pairs={{0,8},{4,12},{8,0},{12,4},{16,20},{20,16},{24,28},{28,24},{1,9},{5... | collective-permute-start | bytes 466952 | tf_op jit(solution)/shard_map/ppermute | solution.py:47
  98.0 5.5 %collective-permute-start.40 = (bf16[608,128]{1,0:T(8,128)(2,1)}, bf16[608,128]{1,0:T(8,128)(2,1)}, u32[]{:S(2)}, u32[]{:S(2)}) collective-permute-start(bf16[608,128]{1,0:T(8,128)(2,1)} %collective-permute-done.15.refs_12_), channel_id=1, source_target_pairs={{0,4},{4,0},{8,12},{12,8},{16,24},{20,28},{24,16},{28,20},{1,5},{5... | collective-permute-start | bytes 466952 | tf_op jit(solution)/shard_map/ppermute | solution.py:47
  99.6 11.1 %collective-permute-start.22 = (bf16[624,256]{1,0:T(8,128)(2,1)}, bf16[624,256]{1,0:T(8,128)(2,1)}, u32[]{:S(2)}, u32[]{:S(2)}) collective-permute-start(bf16[624,256]{1,0:T(8,128)(2,1)} %get-tuple-element.96), channel_id=1, source_target_pairs={{0,4},{4,0},{8,12},{12,8},{16,24},{20,28},{24,16},{28,20},{1,5},{5... | collective-permute-start | bytes 958472 | tf_op jit(solution)/shard_map/ppermute | solution.py:47
  100.7 11.4 %collective-permute-start.23 = (bf16[624,256]{1,0:T(8,128)(2,1)}, bf16[624,256]{1,0:T(8,128)(2,1)}, u32[]{:S(2)}, u32[]{:S(2)}) collective-permute-start(bf16[624,256]{1,0:T(8,128)(2,1)} %get-tuple-element.97), channel_id=1, source_target_pairs={{0,4},{4,0},{8,12},{12,8},{16,24},{20,28},{24,16},{28,20},{1,5},{5... | collective-permute-start | bytes 958472 | tf_op jit(solution)/shard_map/ppermute | solution.py:47
  102.3 3.9 %collective-permute-start.38 = (bf16[608,128]{1,0:T(8,128)(2,1)S(1)}, bf16[608,128]{1,0:T(8,128)(2,1)}, u32[]{:S(2)}, u32[]{:S(2)}) collective-permute-start(bf16[608,128]{1,0:T(8,128)(2,1)S(1)} %collective-permute-done.19.refs_2_.refs_6_), channel_id=1, source_target_pairs={{0,16},{16,0},{1,17},{17,1},{2,18},{18,2},{3,19},{19,3},{4,20},{20... | collective-permute-start | bytes 466952 | tf_op jit(solution)/shard_map/ppermute | solution.py:35
  103.4 5.6 %collective-permute-start.39 = (bf16[608,128]{1,0:T(8,128)(2,1)}, bf16[608,128]{1,0:T(8,128)(2,1)S(1)}, u32[]{:S(2)}, u32[]{:S(2)}) collective-permute-start(bf16[608,128]{1,0:T(8,128)(2,1)} %copy-done.9), channel_id=1, source_target_pairs={{0,16},{16,0},{1,17},{17,1},{2,18},{18,2},{3,19},{19,3},{4,20},{20... | collective-permute-start | bytes 466952 | tf_op jit(solution)/shard_map/ppermute | solution.py:35
  103.5 7.2 %collective-permute-start.42 = (bf16[608,128]{1,0:T(8,128)(2,1)}, bf16[608,128]{1,0:T(8,128)(2,1)S(1)}, u32[]{:S(2)}, u32[]{:S(2)}) collective-permute-start(bf16[608,128]{1,0:T(8,128)(2,1)} %collective-permute-done.40.refs_13_), channel_id=1, source_target_pairs={{0,8},{4,12},{8,0},{12,4},{16,20},{20,16},{24,28},{28,24},{1,9},{5... | collective-permute-start | bytes 466952 | tf_op jit(solution)/shard_map/ppermute | solution.py:47
  106.2 9.0 %collective-permute-start.27 = (bf16[2,608,128]{2,1,0:T(8,128)(2,1)S(1)}, bf16[2,608,128]{2,1,0:T(8,128)(2,1)S(1)}, u32[]{:S(2)}, u32[]{:S(2)}) collective-permute-start(bf16[2,608,128]{2,1,0:T(8,128)(2,1)S(1)} %pad_maximum_fusion.refs_4_), channel_id=1, source_target_pairs={{0,4},{4,0},{8,12},{12,8},{16,24},{20,28},{24,16},{28,20},{1,5},{5... | collective-permute-start | bytes 933896 | tf_op jit(solution)/shard_map/ppermute | solution.py:47
  109.1 12.1 %collective-permute-start.21 = (f32[608,128]{1,0:T(8,128)S(1)}, f32[608,128]{1,0:T(8,128)S(1)}, u32[]{:S(2)}, u32[]{:S(2)}) collective-permute-start(f32[608,128]{1,0:T(8,128)S(1)} %residual_rows.1), channel_id=1, source_target_pairs={{0,16},{16,0},{1,17},{17,1},{2,18},{18,2},{3,19},{19,3},{4,20},{20... | collective-permute-start | bytes 933896 | tf_op jit(solution)/shard_map/ppermute | solution.py:35
  110.7 3.2 %collective-permute-start.44 = (bf16[608,128]{1,0:T(8,128)(2,1)}, bf16[608,128]{1,0:T(8,128)(2,1)S(1)}, u32[]{:S(2)}, u32[]{:S(2)}) collective-permute-start(bf16[608,128]{1,0:T(8,128)(2,1)} %collective-permute-done.40.refs_13_), channel_id=1, source_target_pairs={{0,16},{16,0},{1,17},{17,1},{2,18},{18,2},{3,19},{19,3},{4,20},{20... | collective-permute-start | bytes 466952 | tf_op jit(solution)/shard_map/ppermute | solution.py:35
  110.7 2.9 %collective-permute-start.45 = (bf16[608,128]{1,0:T(8,128)(2,1)}, bf16[608,128]{1,0:T(8,128)(2,1)S(1)}, u32[]{:S(2)}, u32[]{:S(2)}) collective-permute-start(bf16[608,128]{1,0:T(8,128)(2,1)} %collective-permute-done.41.refs_14_), channel_id=1, source_target_pairs={{0,16},{16,0},{1,17},{17,1},{2,18},{18,2},{3,19},{19,3},{4,20},{20... | collective-permute-start | bytes 466952 | tf_op jit(solution)/shard_map/ppermute | solution.py:35
  112.0 4.4 %collective-permute-start.46 = (bf16[608,128]{1,0:T(8,128)(2,1)S(1)}, bf16[608,128]{1,0:T(8,128)(2,1)S(1)}, u32[]{:S(2)}, u32[]{:S(2)}) collective-permute-start(bf16[608,128]{1,0:T(8,128)(2,1)S(1)} %collective-permute-done.42.refs_15_), channel_id=1, source_target_pairs={{0,16},{16,0},{1,17},{17,1},{2,18},{18,2},{3,19},{19,3},{4,20},{20... | collective-permute-start | bytes 466952 | tf_op jit(solution)/shard_map/ppermute | solution.py:35
  113.6 14.0 %collective-permute-start.26 = (bf16[608,128]{1,0:T(8,128)(2,1)}, bf16[608,128]{1,0:T(8,128)(2,1)S(1)}, u32[]{:S(2)}, u32[]{:S(2)}) collective-permute-start(bf16[608,128]{1,0:T(8,128)(2,1)} %collective-permute-done.7.refs_1_), channel_id=1, source_target_pairs={{0,16},{16,0},{1,17},{17,1},{2,18},{18,2},{3,19},{19,3},{4,20},{20... | collective-permute-start | bytes 466952 | tf_op jit(solution)/shard_map/ppermute | solution.py:35
  113.9 8.2 %collective-permute-start.28 = (bf16[2,608,128]{2,1,0:T(8,128)(2,1)S(1)}, bf16[2,608,128]{2,1,0:T(8,128)(2,1)S(1)}, u32[]{:S(2)}, u32[]{:S(2)}) collective-permute-start(bf16[2,608,128]{2,1,0:T(8,128)(2,1)S(1)} %pad_maximum_fusion.refs_4_), channel_id=1, source_target_pairs={{0,8},{4,12},{8,0},{12,4},{16,20},{20,16},{24,28},{28,24},{1,9},{5... | collective-permute-start | bytes 933896 | tf_op jit(solution)/shard_map/ppermute | solution.py:47
  115.3 8.8 %collective-permute-start.29 = (bf16[2,608,128]{2,1,0:T(8,128)(2,1)S(1)}, bf16[2,608,128]{2,1,0:T(8,128)(2,1)S(1)}, u32[]{:S(2)}, u32[]{:S(2)}) collective-permute-start(bf16[2,608,128]{2,1,0:T(8,128)(2,1)S(1)} %collective-permute-done.27.refs_5_), channel_id=1, source_target_pairs={{0,8},{4,12},{8,0},{12,4},{16,20},{20,16},{24,28},{28,24},{1,9},{5... | collective-permute-start | bytes 933896 | tf_op jit(solution)/shard_map/ppermute | solution.py:47
  116.5 11.1 %collective-permute-start.24 = (bf16[624,256]{1,0:T(8,128)(2,1)S(1)}, bf16[624,256]{1,0:T(8,128)(2,1)S(1)}, u32[]{:S(2)}, u32[]{:S(2)}) collective-permute-start(bf16[624,256]{1,0:T(8,128)(2,1)S(1)} %get-tuple-element.102), channel_id=1, source_target_pairs={{0,8},{4,12},{8,0},{12,4},{16,20},{20,16},{24,28},{28,24},{1,9},{5... | collective-permute-start | bytes 958472 | tf_op jit(solution)/shard_map/ppermute | solution.py:47
  121.2 9.3 %collective-permute-start.30 = (bf16[2,608,128]{2,1,0:T(8,128)(2,1)S(1)}, bf16[2,608,128]{2,1,0:T(8,128)(2,1)S(1)}, u32[]{:S(2)}, u32[]{:S(2)}) collective-permute-start(bf16[2,608,128]{2,1,0:T(8,128)(2,1)S(1)} %pad_maximum_fusion.refs_4_), channel_id=1, source_target_pairs={{0,16},{16,0},{1,17},{17,1},{2,18},{18,2},{3,19},{19,3},{4,20},{20... | collective-permute-start | bytes 933896 | tf_op jit(solution)/shard_map/ppermute | solution.py:35
  122.1 8.4 %collective-permute-start.31 = (bf16[2,608,128]{2,1,0:T(8,128)(2,1)S(1)}, bf16[2,608,128]{2,1,0:T(8,128)(2,1)S(1)}, u32[]{:S(2)}, u32[]{:S(2)}) collective-permute-start(bf16[2,608,128]{2,1,0:T(8,128)(2,1)S(1)} %collective-permute-done.27.refs_5_), channel_id=1, source_target_pairs={{0,16},{16,0},{1,17},{17,1},{2,18},{18,2},{3,19},{19,3},{4,20},{20... | collective-permute-start | bytes 933896 | tf_op jit(solution)/shard_map/ppermute | solution.py:35
  124.1 6.3 %collective-permute-start.32 = (bf16[2,608,128]{2,1,0:T(8,128)(2,1)S(1)}, bf16[2,608,128]{2,1,0:T(8,128)(2,1)S(1)}, u32[]{:S(2)}, u32[]{:S(2)}) collective-permute-start(bf16[2,608,128]{2,1,0:T(8,128)(2,1)S(1)} %collective-permute-done.28.refs_6_), channel_id=1, source_target_pairs={{0,16},{16,0},{1,17},{17,1},{2,18},{18,2},{3,19},{19,3},{4,20},{20... | collective-permute-start | bytes 933896 | tf_op jit(solution)/shard_map/ppermute | solution.py:35
  127.5 2.9 %collective-permute-start.33 = (bf16[2,608,128]{2,1,0:T(8,128)(2,1)S(1)}, bf16[2,608,128]{2,1,0:T(8,128)(2,1)S(1)}, u32[]{:S(2)}, u32[]{:S(2)}) collective-permute-start(bf16[2,608,128]{2,1,0:T(8,128)(2,1)S(1)} %collective-permute-done.29.refs_7_), channel_id=1, source_target_pairs={{0,16},{16,0},{1,17},{17,1},{2,18},{18,2},{3,19},{19,3},{4,20},{20... | collective-permute-start | bytes 933896 | tf_op jit(solution)/shard_map/ppermute | solution.py:35
  127.6 2.9 %collective-permute-start.25 = (bf16[608,128]{1,0:T(8,128)(2,1)S(1)}, bf16[608,128]{1,0:T(8,128)(2,1)S(1)}, u32[]{:S(2)}, u32[]{:S(2)}) collective-permute-start(bf16[608,128]{1,0:T(8,128)(2,1)S(1)} %copy-done.32), channel_id=1, source_target_pairs={{0,16},{16,0},{1,17},{17,1},{2,18},{18,2},{3,19},{19,3},{4,20},{20... | collective-permute-start | bytes 466952 | tf_op jit(solution)/shard_map/ppermute | solution.py:35
  (37 other events, 247.5 us)

commit v7 on v6

--- a/solution.py
+++ b/solution.py
@@ -163,7 +163,7 @@
         columns[pl.ds(start, size), :] = jnp.concatenate([rows, jnp.zeros((5, size), F32)], 0).T
 
 
-def normalize(acts, mod, normed, stats):
+def normalize(acts, modulation, normed, stats):
     features, tokens = acts.shape[1:]
     parts = pieces(0, features, 128)
     total = jnp.zeros((1, tokens), F32)
@@ -180,7 +180,8 @@
     for start, size in parts:
         rows = pl.ds(start, size)
         xhat = (acts[0, rows, :].astype(F32) - mean) * inv
-        normed[:, rows] = (xhat * (1.0 + mod[rows, 1:2]) + mod[rows, 0:1]).T.astype(BF16)
+        shift, scale = modulation[0, 0:1, rows], modulation[0, 1:2, rows]
+        normed[:, rows] = (xhat.T * (1.0 + scale) + shift).astype(BF16)
 
 
 def against_rows(columns, weight):
@@ -217,9 +218,10 @@
     pipelined(parts, product, finish)
 
 
-def forward_first_kernel(normed, w_in, w_out, slope_out, total, in_buf, out_buf, sems):
+def forward_first_kernel(normed, modulation, w_in, w_out, slope_out, total, mod, in_buf, out_buf, sems):
     parts = pieces(0, slope_out.shape[1])
     stream = Stream(w_in, in_buf, w_out, out_buf, parts, 0, sems)
+    turn_modulation(modulation, mod)
     forward_products(stream, parts, 0, normed, in_buf, out_buf, slope_out, total, None, None)
 
 
@@ -246,17 +248,17 @@
     return params(4 * part * features * tokens, 4 * part * features + 4 * features * tokens, transcendentals)
 
 
-def forward_first(normed, w_in, w_out, part, name):
+def forward_first(normed, modulation, w_in, w_out, part, name):
     tokens, features = normed.shape
     return pl.pallas_call(
         forward_first_kernel,
-        out_shape=(struct((tokens, part), F32), struct((tokens, features), F32)),
-        in_specs=[WHOLE, HELD, HELD],
-        out_specs=[WHOLE] * 2,
+        out_shape=(struct((tokens, part), F32), struct((tokens, features), F32), struct((features, 8), F32)),
+        in_specs=[WHOLE, WHOLE, HELD, HELD],
+        out_specs=[WHOLE] * 3,
         scratch_shapes=layer_scratch(part, features) + [pltpu.SemaphoreType.DMA((2 * len(pieces(0, part)),))],
         name=name,
         **layer_params(part, features, tokens, part * tokens),
-    )(normed, w_in, w_out)
+    )(normed, modulation, w_in, w_out)
 
 
 def forward_last(order, normed, before, w_in, w_out, start, blocks, name):
@@ -426,7 +428,7 @@
 
 
 def prepare_kernel(blocks, order, acts, modulation, own, arrived, weight, *refs):
-    outs, (mod, normed, stats, cot0, cot1, cot1_rows, full, buf, sem) = refs[:blocks], refs[blocks:]
+    outs, (normed, stats, cot0, cot1, full, buf, sem) = refs[:blocks], refs[blocks:]
     load = pltpu.make_async_copy(weight, buf, sem)
     load.start()
     group = order[blocks]
@@ -436,9 +438,7 @@
     cot0[...] = jnp.where(control, own[:, lanes], arrived[:, lanes])
     mine = jnp.where(control, arrived[:, lanes], own[:, lanes])
     cot1[...] = mine
-    cot1_rows[...] = jnp.where(control, arrived[...], own[...])
-    turn_modulation(modulation, mod)
-    normalize(acts, mod, normed, stats)
+    normalize(acts, modulation, normed, stats)
     load.wait()
     full[...] = lax.dot_general(mine, buf[...], (((0,), (0,)), ((), ())), preferred_element_type=F32).T
     write_blocks(order, full, outs)
@@ -452,15 +452,13 @@
         out_shape=[struct((rows, half), F32)]
         + [struct((rows, half), BF16)] * (blocks - 1)
         + [
-            struct((features, 8), F32),
             struct((tokens, features), BF16),
             struct((2, tokens), F32),
             struct((rows, half), BF16),
             struct((rows, half), BF16),
-            struct((rows, tokens), BF16),
         ],
         in_specs=[SCALARS] + [WHOLE] * 4 + [HELD],
-        out_specs=[WHOLE] * (blocks + 6),
+        out_specs=[WHOLE] * (blocks + 4),
         scratch_shapes=[
             pltpu.VMEM((features, half), F32),
             pltpu.VMEM(weight.shape, BF16),
@@ -495,26 +493,42 @@
 def zero_grad_kernel(blocks, first, count, order, dp_order, *refs):
     cots, refs = (refs[:count], refs[count : 2 * count]), refs[2 * count :]
     stacks = []
-    while len(refs) > (7 if first else 4):
+    while len(refs) > (9 if first else 6):
         stacks.append((refs[:blocks], refs[blocks : 2 * blocks]))
         refs = refs[2 * blocks :]
     before = None
     if first:
-        before, out, lhs, rhs, stage, buf, sems = refs
+        before, out, lhs, rhs, stage, parked, loads, buf, sems = refs
     else:
-        buf, lhs, rhs, stage = refs
+        buf, lhs, rhs, stage, parked, loads = refs
     rows, half = cots[0][0].shape
     group = order[blocks]
+    moves, places = [], []
     for part in range(count):
         slot = part // 2 * 2 + (dp_order[first + part] & 1)
         for side, owner in enumerate((group, 1 - group)):
             lanes = pl.ds(pl.multiple_of((slot * 2 + owner) * half, half), half)
-            lhs[:, lanes] = cots[side][part][...]
-            if len(stacks) == count:
-                values = [lambda source=source: source[...] for source in stacks[part][side]]
-            else:
-                values = [lambda source=source, part=part: source[part] for source in stacks[0][side]]
-            place_blocks(rhs, lanes, stage, order, values, rows, side * (blocks + 1))
+            moves.append((cots[side][part], lhs.at[:, lanes]))
+            values = []
+            for place in range(blocks):
+                source = stacks[part][side][place] if len(stacks) == count else stacks[0][side][place].at[part]
+                if rows % 16:
+                    at = (part * 2 + side) * blocks + place
+                    target = parked.at[at]
+                    values.append(lambda at=at: parked[at])
+                else:
+                    offset = pl.multiple_of(order[side * (blocks + 1) + place] * rows, 16)
+                    target = rhs.at[pl.ds(offset, rows), lanes]
+                moves.append((source, target))
+            places.append((lanes, values, side * (blocks + 1)))
+    moves = [pltpu.make_async_copy(a, b, loads.at[k]) for k, (a, b) in enumerate(moves)]
+    for move in moves:
+        move.start()
+    for move in moves:
+        move.wait()
+    if rows % 16:
+        for lanes, values, shift in places:
+            place_blocks(rhs, lanes, stage, order, values, rows, shift)
     copies = []
     for k, (start, size) in enumerate(pieces(0, blocks * rows)):
         columns = pl.ds(start, size)
@@ -537,6 +551,8 @@
         pltpu.VMEM((rows, tokens), BF16),
         pltpu.VMEM((features, tokens), BF16),
         staging(rows, features, half),
+        pltpu.VMEM((count * 2 * blocks, rows, half) if rows % 16 else (1, 8, 128), BF16),
+        pltpu.SemaphoreType.DMA((count * 2 * (blocks + 1),)),
     ]
     if extra:
         scratch += [
@@ -546,7 +562,7 @@
     return pl.pallas_call(
         functools.partial(zero_grad_kernel, blocks, first, count),
         out_shape=struct((rows, features), F32),
-        in_specs=[SCALARS] * 2 + [WHOLE] * (2 * count + len(flat) + len(extra)),
+        in_specs=[SCALARS] * 2 + [HELD] * (2 * count + len(flat)) + [WHOLE] * len(extra),
         out_specs=HELD if extra else WHOLE,
         scratch_shapes=scratch,
         name=name,
@@ -580,21 +596,20 @@
     dp_order = lax.axis_index("dp").astype(jnp.int32) ^ jnp.arange(parts, dtype=jnp.int32)
 
     arrived = swap_grp(own_cot)
-    own_term, sent, mod, normed, stats, cot0, cot1, cot1_rows = prepare(
+    own_term, sent, normed, stats, cot0, cot1 = prepare(
         order, acts, modulation, own_cot, arrived, zero_weight, blocks
     )
     split, cut = split_rows(hidden)
-    slope_a, total = forward_first(after(normed, *sent), w_in, w_out, split, "forward_first")
+    slope_a, total, mod = forward_first(after(normed, *sent), modulation, w_in, w_out, split, "forward_first")
     own_mod = block_of(mod, me, rows)
     own_gate = own_mod[:, 2:3]
-    cots = gather_dp(cot1)
     got = direct(sent, total)
     up_half = own_term + cot0.astype(F32) + sum(value.astype(F32) for value in got)
     up_rows = jnp.where(is_control, jnp.concatenate([up_half, swap_grp(up_half)], 1), own_cot.astype(F32))
     grad_rows = (own_gate * up_rows).astype(BF16)
 
     slope_b, kept, sent = forward_last(
-        order, after(normed, grad_rows, *cots), total, w_in, w_out, split, blocks, "forward_last"
+        order, after(normed, grad_rows), total, w_in, w_out, split, blocks, "forward_last"
     )
     gathered = [grad_rows] + direct([grad_rows] * (blocks - 1), kept)
     grad, total = backward_first(
@@ -616,6 +631,7 @@
         near = near + steps(near, level)
     near_other = [swap_grp(value) for value in near]
     residual = residual_rows(order, zero_weight, near)
+    cots = gather_dp(after(cot1, token_sums))
     cots_other = [swap_grp(value) for value in cots]
 
     gathers = [[far[0]], [jnp.stack(far[1:])]]

time: 136 us -> 128 us (0.941)
  local copies, waits for them, and re-layouts: 12 us -> 8.09 us
  starting transfers between devices: 38.4 us -> 35.9 us
  Pallas kernels: 55.8 us -> 53.8 us
  waiting for transfers between devices: 18.2 us -> 20.1 us
    unnamed x77 -> x65, local copies, waits for them, and re-layouts: 12 us -> 8.08 us
    pallas_call x1, Pallas kernels: 5.98 us -> 3.99 us  [prepare(): pl.pallas_call(functools.partial(prepare_kernel, blocks), out_shape=[stru...]
    ppermute x20, waiting for transfers between devices: 1.42 us -> 2.93 us  [swap_grp(): return lax.ppermute(value, 'grp', [(0, 1), (1, 0)])]
  transfers between devices with their start and end apart: 47 -> 47, of which waited for: 11 -> 10; matrix products, arithmetic and copies ran while one was open for 5% -> 4% of each run, Pallas kernels for 33% -> 35%
where the time goes in v7:
time: 128 us
  Pallas kernels  53.8 us (42%)
  starting transfers between devices  35.9 us (28%)
  waiting for transfers between devices  20.1 us (16%)
  other arithmetic  8.66 us (7%)
  local copies, waits for them, and re-layouts  8.09 us (6%)
    pallas_call x1, Pallas kernels, backward_first(): pl.pallas_call(functools.partial(backward_first_kernel, blocks, part), ou...  11.7 us
    ppermute x12, starting transfers between devices, step(): return lax.ppermute(value, ('grp', 'fsdp'), pairs)  11.7 us
    ppermute x9, starting transfers between devices, send(): return lax.ppermute(value, ('grp', 'fsdp'), pairs)  11.6 us
    pallas_call x1, Pallas kernels, forward_last(): pl.pallas_call(functools.partial(forward_last_kernel, start), out_shape=[...  11.3 us
    ppermute x6, waiting for transfers between devices, gather_dp(): lax.ppermute(value, 'dp', [(i, i ^ mask) for i in range(length)])  8.59 us
    pallas_call x2, Pallas kernels, zero_projection_grad(): pl.pallas_call(functools.partial(zero_grad_kernel, blocks, first, count),...  8.51 us
    ppermute x6, starting transfers between devices, gather_dp(): lax.ppermute(value, 'dp', [(i, i ^ mask) for i in range(length)])  8.27 us
    pallas_call x1, Pallas kernels, backward_last(): pl.pallas_call(functools.partial(backward_last_kernel, start, rows), out_...  8.14 us
  transfers between devices with their start and end apart: 47, of which 10 were waited for; matrix products, arithmetic and copies ran while one was open for 4% of the time, Pallas kernels for 35%

profile of v7, /device:TPU:0, one launch (start us, length us, event | category | flops | bytes accessed | tf_op | source)
XLA Modules:
  0.0 127.9 jit_solution(17922772615845848210)
XLA Ops:
  1.1 0.8 copy.13.modulation
  1.9 0.7 fusion.14
  2.7 1.0 copy-done.4
  3.6 4.0 %prepare.1 = (f32[608,128]{1,0:T(8,128)S(1)}, bf16[608,128]{1,0:T(8,128)(2,1)S(1)}, bf16[608,128]{1,0:T(8,128)(2,1)S(1)}, bf16[608,128]{1,0:T(8,128)(2,1)S(1)}, ...) custom-call(s32[9]{0:T(128)S(1)} %pad_add_fusion.order, ...), custom_call_target="tpu_custom_call" | custom-call | flops 378535936 | bytes 4202496 | tf_op jit(solution)/shard_map/prepare/pallas_call | solution.py:450
  7.6 2.9 %collective-permute-start.1 = (bf16[608,128]{1,0:T(8,128)(2,1)S(1)}, bf16[608,128]{1,0:T(8,128)(2,1)S(1)}, u32[]{:S(2)}, u32[]{:S(2)}) collective-permute-start(bf16[608,128]{1,0:T(8,128)(2,1)S(1)} %get-tuple-element.57), channel_id=1, source_target_pairs={{0,4},{4,0},{8,12},{12,8},{16,24},{20,28},{24,16},{28,20},{1,5},{5... | collective-permute-start | bytes 466952 | tf_op jit(solution)/shard_map/ppermute | solution.py:63
  10.5 1.5 %collective-permute-start.2 = (bf16[608,128]{1,0:T(8,128)(2,1)S(1)}, bf16[608,128]{1,0:T(8,128)(2,1)S(1)}, u32[]{:S(2)}, u32[]{:S(2)}) collective-permute-start(bf16[608,128]{1,0:T(8,128)(2,1)S(1)} %get-tuple-element.58), channel_id=1, source_target_pairs={{0,8},{4,12},{8,0},{12,4},{16,20},{20,16},{24,28},{28,24},{1,9},{5... | collective-permute-start | bytes 466952 | tf_op jit(solution)/shard_map/ppermute | solution.py:63
  12.0 7.4 %forward_first.1 = (f32[256,1024]{1,0:T(8,128)S(1)}, f32[256,2432]{1,0:T(8,128)}, f32[2432,8]{1,0:T(8,128)S(1)}) custom-call(bf16[256,2432]{1,0:T(8,128)(2,1)S(1)} %get-tuple-element.68.normed, f32[1,3,2432]{2,1,0:T(4,128)S(1)} %copy.13.modulation, bf16[1,2432,2432]{2,1,0:T(8,128)(2,1)} %w_in.5, bf16[1,2432,2432]{2,1,0:T(8,128)(2,1)} %w_out.5), custom_call_target="tpu_custom_call" | custom-call | flops 2550136832 | bytes 12451840 | tf_op jit(solution)/shard_map/forward_first/pallas_call | solution.py:253
  19.5 0.9 add_add_fusion
  20.9 1.5 %collective-permute-done.4 = f32[608,128]{1,0:T(8,128)} collective-permute-done((f32[608,128]{1,0:T(8,128)}, f32[608,128]{1,0:T(8,128)}, u32[]{:S(2)}, u32[]{:S(2)}) %collective-permute-start.4) | collective-permute-done | bytes 311328 | tf_op jit(solution)/shard_map/ppermute | solution.py:35
  22.4 1.3 %multiply_convert_fusion.refs_0_ = bf16[608,256]{1,0:T(8,128)(2,1)S(1)} fusion(f32[608,128]{1,0:T(8,128)} %collective-permute-done.4, f32[608,128]{1,0:T(8,128)} %add_add_fusion, f32[608]{0:T(1024)S(1)} %get-tuple-element.110, pred[]{:T(512)S(6)} %eq.7, bf16[1,608,256]{2,1,0:T(8,128)(2,1)} %param.13), kind=kLoop, calls=%fused_computation.11 | loop fusion | flops 778240 | bytes 1247617 | tf_op jit(solution)/shard_map/convert_element_type | solution.py:609
  23.7 3.0 %collective-permute-start.10 = (bf16[608,256]{1,0:T(8,128)(2,1)S(1)}, bf16[608,256]{1,0:T(8,128)(2,1)S(1)}, u32[]{:S(2)}, u32[]{:S(2)}) collective-permute-start(bf16[608,256]{1,0:T(8,128)(2,1)S(1)} %multiply_convert_fusion.refs_0_), channel_id=1, source_target_pairs={{0,12},{4,8},{8,4},{12,0},{16,28},{20,24},{24,20},{28,16},{1,13},{... | collective-permute-start | bytes 933896 | tf_op jit(solution)/shard_map/ppermute | solution.py:63
  27.3 11.3 %forward_last.1 = (f32[256,1408]{1,0:T(8,128)}, f32[608,256]{1,0:T(8,128)S(1)}, bf16[608,256]{1,0:T(8,128)(2,1)S(1)}, bf16[608,256]{1,0:T(8,128)(2,1)S(1)}, bf16[608,256]{1,0:T(8,128)(2,1)S(1)}) custom-call(s32[9]{0:T(128)S(1)} %pad_add_fusion.order, bf16[256,2432]{1,0:T(8,128)(2,1)S(1)} %get-tuple-element.68.normed, f32[256,2432]{1,0:T(8,128)} %get-tuple-element.64.before, ...), custom_call_target="tpu_custom_call" | custom-call | flops 3506438144 | bytes 16187392 | tf_op jit(solution)/shard_map/forward_last/pallas_call | solution.py:267
  38.7 2.0 %collective-permute-start.5 = (bf16[608,256]{1,0:T(8,128)(2,1)S(1)}, bf16[608,256]{1,0:T(8,128)(2,1)S(1)}, u32[]{:S(2)}, u32[]{:S(2)}) collective-permute-start(bf16[608,256]{1,0:T(8,128)(2,1)S(1)} %get-tuple-element.70), channel_id=1, source_target_pairs={{0,4},{4,0},{8,12},{12,8},{16,24},{20,28},{24,16},{28,20},{1,5},{5... | collective-permute-start | bytes 933896 | tf_op jit(solution)/shard_map/ppermute | solution.py:63
  40.6 1.5 %collective-permute-start.6 = (bf16[608,256]{1,0:T(8,128)(2,1)S(1)}, bf16[608,256]{1,0:T(8,128)(2,1)S(1)}, u32[]{:S(2)}, u32[]{:S(2)}) collective-permute-start(bf16[608,256]{1,0:T(8,128)(2,1)S(1)} %get-tuple-element.71), channel_id=1, source_target_pairs={{0,8},{4,12},{8,0},{12,4},{16,20},{20,16},{24,28},{28,24},{1,9},{5... | collective-permute-start | bytes 933896 | tf_op jit(solution)/shard_map/ppermute | solution.py:63
  42.2 11.7 %backward_first.1 = (bf16[256,2432]{1,0:T(8,128)(2,1)S(1)}, f32[256,2432]{1,0:T(8,128)}) custom-call(s32[9]{0:T(128)S(1)} %pad_add_fusion.order, bf16[608,256]{1,0:T(8,128)(2,1)S(1)} %multiply_convert_fusion.refs_0_, bf16[608,256]{1,0:T(8,128)(2,1)S(1)} %collective-permute-done.8.refs_1_, bf16[608,256]{1,0:T(8,128)(2,1)S(1)} %collective-permute-done.9.refs_2_, ...), custom_call_target="tpu_custom_call" | custom-call | flops 5100273664 | bytes 22413312 | tf_op jit(solution)/shard_map/backward_first/pallas_call | solution.py:325
  54.0 1.0 copy-done.6
  55.5 2.1 %fusion.16 = (bf16[608,256]{1,0:T(8,128)(2,1)S(1)}, f32[608,256]{1,0:T(8,128)}) fusion(f32[608,256]{1,0:T(8,128)S(1)} %get-tuple-element.69, bf16[608,256]{1,0:T(8,128)(2,1)S(1)} %collective-permute-done.7, bf16[608,256]{1,0:T(8,128)(2,1)S(1)} %collective-permute-done.6, bf16[608,256]{1,0:T(8,128)(2,1)S(1)} %collective-permute-done.5, ...), kind=kLoop, calls=%fused_computation.35 | loop fusion | flops 1556480 | bytes 2804100 | tf_op jit(solution)/shard_map/convert_element_type | solution.py:621
  57.6 1.4 %collective-permute-done.11 = bf16[608,128]{1,0:T(8,128)(2,1)S(1)} collective-permute-done((bf16[608,128]{1,0:T(8,128)(2,1)S(1)}, bf16[608,128]{1,0:T(8,128)(2,1)S(1)}, u32[]{:S(2)}, u32[]{:S(2)}) %collective-permute-start.11) | collective-permute-done | bytes 155680 | tf_op jit(solution)/shard_map/ppermute | solution.py:35
  59.0 1.7 %collective-permute-start.15 = (bf16[608,128]{1,0:T(8,128)(2,1)S(1)}, bf16[608,128]{1,0:T(8,128)(2,1)S(1)}, u32[]{:S(2)}, u32[]{:S(2)}) collective-permute-start(bf16[608,128]{1,0:T(8,128)(2,1)S(1)} %slice_select_fusion.refs_0_.refs_4_), channel_id=1, source_target_pairs={{0,4},{4,0},{8,12},{12,8},{16,24},{20,28},{24,16},{28,20},{1,5},{5... | collective-permute-start | bytes 466952 | tf_op jit(solution)/shard_map/ppermute | solution.py:47
  60.7 3.6 %collective-permute-start.14 = (bf16[608,128]{1,0:T(8,128)(2,1)S(1)}, bf16[608,128]{1,0:T(8,128)(2,1)S(1)}, u32[]{:S(2)}, u32[]{:S(2)}) collective-permute-start(bf16[608,128]{1,0:T(8,128)(2,1)S(1)} %slice_select_fusion.refs_0_.refs_4_), channel_id=1, source_target_pairs={{0,3},{1,2},{2,1},{3,0},{4,7},{5,6},{6,5},{7,4},{8,11},{9,10},{10,... | collective-permute-start | bytes 466952 | tf_op jit(solution)/shard_map/ppermute | solution.py:69
  64.3 0.8 collective-permute-start.12
  65.1 8.1 %backward_last.1 = (bf16[624,256]{1,0:T(8,128)(2,1)}, bf16[624,256]{1,0:T(8,128)(2,1)}, f32[608,256]{1,0:T(8,128)S(1)}, f32[608,256]{1,0:T(8,128)S(1)}, f32[2,256]{1,0:T(2,128)S(1)}) custom-call(s32[9]{0:T(128)S(1)} %pad_add_fusion.order, bf16[256,2432]{1,0:T(8,128)(2,1)} %copy-done.6, f32[256,2432]{1,0:T(8,128)} %get-tuple-element.82.before, ...), custom_call_target="tpu_custom_call" | custom-call | flops 956301312 | bytes 6225920 | tf_op jit(solution)/shard_map/backward_last/pallas_call | solution.py:378
  73.3 0.8 copy-done.10
  74.1 0.9 copy-done.12
  74.9 2.6 %collective-permute-done.13 = bf16[608,128]{1,0:T(8,128)(2,1)S(1)} collective-permute-done((bf16[608,128]{1,0:T(8,128)(2,1)S(1)}, bf16[608,128]{1,0:T(8,128)(2,1)S(1)}, u32[]{:S(2)}, u32[]{:S(2)}) %collective-permute-start.13) | collective-permute-done | bytes 155680 | tf_op jit(solution)/shard_map/ppermute | solution.py:69
  78.6 0.9 collective-permute-start.37
  79.5 0.7 copy-done.17
  80.8 3.2 %collective-permute-done.33.refs_1_ = bf16[608,128]{1,0:T(8,128)(2,1)S(1)} collective-permute-done((bf16[608,128]{1,0:T(8,128)(2,1)S(1)}, bf16[608,128]{1,0:T(8,128)(2,1)S(1)}, u32[]{:S(2)}, u32[]{:S(2)}) %collective-permute-start.33) | collective-permute-done | bytes 155680 | tf_op jit(solution)/shard_map/ppermute | solution.py:69
  84.1 1.5 %collective-permute-start.19 = (bf16[624,256]{1,0:T(8,128)(2,1)}, bf16[624,256]{1,0:T(8,128)(2,1)}, u32[]{:S(2)}, u32[]{:S(2)}) collective-permute-start(bf16[624,256]{1,0:T(8,128)(2,1)} %get-tuple-element.96), channel_id=1, source_target_pairs={{0,4},{4,0},{8,12},{12,8},{16,24},{20,28},{24,16},{28,20},{1,5},{5... | collective-permute-start | bytes 958472 | tf_op jit(solution)/shard_map/ppermute | solution.py:47
  88.6 1.5 %collective-permute-start.40 = (bf16[608,128]{1,0:T(8,128)(2,1)}, bf16[608,128]{1,0:T(8,128)(2,1)}, u32[]{:S(2)}, u32[]{:S(2)}) collective-permute-start(bf16[608,128]{1,0:T(8,128)(2,1)} %collective-permute-done.12.refs_12_), channel_id=1, source_target_pairs={{0,4},{4,0},{8,12},{12,8},{16,24},{20,28},{24,16},{28,20},{1,5},{5... | collective-permute-start | bytes 466952 | tf_op jit(solution)/shard_map/ppermute | solution.py:47
  90.1 4.6 %collective-permute-done.41.refs_14_ = bf16[608,128]{1,0:T(8,128)(2,1)} collective-permute-done((bf16[608,128]{1,0:T(8,128)(2,1)}, bf16[608,128]{1,0:T(8,128)(2,1)}, u32[]{:S(2)}, u32[]{:S(2)}) %collective-permute-start.41) | collective-permute-done | bytes 155680 | tf_op jit(solution)/shard_map/ppermute | solution.py:47
  94.7 0.9 copy-done.8
  95.6 1.5 %residual_rows.1 = f32[608,128]{1,0:T(8,128)S(1)} custom-call(s32[9]{0:T(128)S(1)} %pad_add_fusion.order, bf16[608,2432]{1,0:T(8,128)(2,1)S(1)} %copy-done, bf16[608,128]{1,0:T(8,128)(2,1)S(1)} %slice_select_fusion.refs_0_.refs_4_, bf16[608,128]{1,0:T(8,128)(2,1)S(1)} %collective-permute-done.15.refs_1_.refs_5_, ...), custom_call_target="tpu_custom_call" | custom-call | flops 378535936 | bytes 4202496 | tf_op jit(solution)/shard_map/residual_rows/pallas_call | solution.py:482
  97.2 0.9 collective-permute-done.40.refs_13_
  98.2 1.6 %collective-permute-start.26 = (bf16[2,608,128]{2,1,0:T(8,128)(2,1)S(1)}, bf16[2,608,128]{2,1,0:T(8,128)(2,1)S(1)}, u32[]{:S(2)}, u32[]{:S(2)}) collective-permute-start(bf16[2,608,128]{2,1,0:T(8,128)(2,1)S(1)} %pad_maximum_fusion.refs_4_), channel_id=1, source_target_pairs={{0,4},{4,0},{8,12},{12,8},{16,24},{20,28},{24,16},{28,20},{1,5},{5... | collective-permute-start | bytes 933896 | tf_op jit(solution)/shard_map/ppermute | solution.py:47
  100.8 1.3 fold.1
  102.1 2.5 %collective-permute-start.23 = (bf16[608,128]{1,0:T(8,128)(2,1)S(1)}, bf16[608,128]{1,0:T(8,128)(2,1)S(1)}, u32[]{:S(2)}, u32[]{:S(2)}) collective-permute-start(bf16[608,128]{1,0:T(8,128)(2,1)S(1)} %copy-done.16), channel_id=1, source_target_pairs={{0,3},{1,2},{2,1},{3,0},{4,7},{5,6},{6,5},{7,4},{8,11},{9,10},{10,... | collective-permute-start | bytes 466952 | tf_op jit(solution)/shard_map/ppermute | solution.py:69
  104.7 1.7 %collective-permute-done.42.refs_15_ = bf16[608,128]{1,0:T(8,128)(2,1)S(1)} collective-permute-done((bf16[608,128]{1,0:T(8,128)(2,1)}, bf16[608,128]{1,0:T(8,128)(2,1)S(1)}, u32[]{:S(2)}, u32[]{:S(2)}) %collective-permute-start.42) | collective-permute-done | bytes 155680 | tf_op jit(solution)/shard_map/ppermute | solution.py:47
  106.6 0.7 collective-permute-start.21
  107.4 0.8 fusion.8
  108.2 1.3 %collective-permute-start.22 = (bf16[608,128]{1,0:T(8,128)(2,1)S(1)}, bf16[608,128]{1,0:T(8,128)(2,1)S(1)}, u32[]{:S(2)}, u32[]{:S(2)}) collective-permute-start(bf16[608,128]{1,0:T(8,128)(2,1)S(1)} %copy-done.16), channel_id=1, source_target_pairs={{0,2},{1,3},{2,0},{3,1},{4,6},{5,7},{6,4},{7,5},{8,10},{9,11},{10,... | collective-permute-start | bytes 466952 | tf_op jit(solution)/shard_map/ppermute | solution.py:69
  109.5 1.3 %collective-permute-start.27 = (bf16[2,608,128]{2,1,0:T(8,128)(2,1)S(1)}, bf16[2,608,128]{2,1,0:T(8,128)(2,1)S(1)}, u32[]{:S(2)}, u32[]{:S(2)}) collective-permute-start(bf16[2,608,128]{2,1,0:T(8,128)(2,1)S(1)} %pad_maximum_fusion.refs_4_), channel_id=1, source_target_pairs={{0,8},{4,12},{8,0},{12,4},{16,20},{20,16},{24,28},{28,24},{1,9},{5... | collective-permute-start | bytes 933896 | tf_op jit(solution)/shard_map/ppermute | solution.py:47
  110.8 0.7 collective-permute-start.28
  111.5 4.0 %zero_projection_grad_first.1.refs_12_ = f32[608,2432]{1,0:T(8,128)S(1)} custom-call(s32[9]{0:T(128)S(1)} %pad_add_fusion.order, s32[4]{0:T(128)S(1)} %iota_xor_fusion.dp_order, bf16[608,128]{1,0:T(8,128)(2,1)S(1)} %copy-done.16, bf16[608,128]{1,0:T(8,128)(2,1)S(1)} %copy-done.20, bf16[608,128]{1,0:T(8,128)(2,1)S(1)} %copy-done.18, ...), custom_call_target="tpu_custom_call" | custom-call | flops 1514143744 | bytes 9027584 | tf_op jit(solution)/shard_map/zero_projection_grad_first/pallas_call | solution.py:562
  116.2 2.8 %collective-permute-done.22.refs_0_ = bf16[608,128]{1,0:T(8,128)(2,1)S(1)} collective-permute-done((bf16[608,128]{1,0:T(8,128)(2,1)S(1)}, bf16[608,128]{1,0:T(8,128)(2,1)S(1)}, u32[]{:S(2)}, u32[]{:S(2)}) %collective-permute-start.22) | collective-permute-done | bytes 155680 | tf_op jit(solution)/shard_map/ppermute | solution.py:69
  119.4 0.9 collective-permute-done.28.refs_7_
  120.9 2.3 %fusion.5 = f32[1,608,256]{2,1,0:T(8,128)} fusion(f32[608,256]{1,0:T(8,128)S(1)} %get-tuple-element.101, f32[608,128]{1,0:T(8,128)} %collective-permute-done.4, f32[608,128]{1,0:T(8,128)} %add_add_fusion, bf16[624,256]{1,0:T(8,128)(2,1)S(1)} %collective-permute-done.21, f32[256]{0:T(256)S(1)} %bitcast.24, f32[256]{0:T(256)S(1)} %bitcast.26, ...), kind=kLoop, calls=%fused_computation.7 | loop fusion | flops 2179072 | bytes 2808197 | tf_op jit(solution)/shard_map/broadcast_in_dim | solution.py:660
  123.2 4.5 %zero_projection_grad_last.1 = f32[608,2432]{1,0:T(8,128)} custom-call(s32[9]{0:T(128)S(1)} %pad_add_fusion.order, s32[4]{0:T(128)S(1)} %iota_xor_fusion.dp_order, bf16[608,128]{1,0:T(8,128)(2,1)S(1)} %collective-permute-done.22.refs_0_, bf16[608,128]{1,0:T(8,128)(2,1)S(1)} %collective-permute-done.23.refs_1_, ...), custom_call_target="tpu_custom_call" | custom-call | flops 1514143744 | bytes 9027584 | tf_op jit(solution)/shard_map/zero_projection_grad_last/pallas_call | solution.py:562
  (135 shorter events, 10.3 us)
Async XLA Ops:
  0.6 2.0 %collective-permute-start = (bf16[608,256]{1,0:T(8,128)(2,1)}, bf16[608,256]{1,0:T(8,128)(2,1)S(1)}, u32[]{:S(2)}, u32[]{:S(2)}) collective-permute-start(bf16[608,256]{1,0:T(8,128)(2,1)} %bitcast.19), channel_id=1, source_target_pairs={{0,16},{16,0},{1,17},{17,1},{2,18},{18,2},{3,19},{19,3},{4,20},{20... | collective-permute-start | bytes 933896 | tf_op jit(solution)/shard_map/ppermute | solution.py:35
  7.6 11.8 %collective-permute-start.1 = (bf16[608,128]{1,0:T(8,128)(2,1)S(1)}, bf16[608,128]{1,0:T(8,128)(2,1)S(1)}, u32[]{:S(2)}, u32[]{:S(2)}) collective-permute-start(bf16[608,128]{1,0:T(8,128)(2,1)S(1)} %get-tuple-element.57), channel_id=1, source_target_pairs={{0,4},{4,0},{8,12},{12,8},{16,24},{20,28},{24,16},{28,20},{1,5},{5... | collective-permute-start | bytes 466952 | tf_op jit(solution)/shard_map/ppermute | solution.py:63
  10.5 9.0 %collective-permute-start.2 = (bf16[608,128]{1,0:T(8,128)(2,1)S(1)}, bf16[608,128]{1,0:T(8,128)(2,1)S(1)}, u32[]{:S(2)}, u32[]{:S(2)}) collective-permute-start(bf16[608,128]{1,0:T(8,128)(2,1)S(1)} %get-tuple-element.58), channel_id=1, source_target_pairs={{0,8},{4,12},{8,0},{12,4},{16,20},{20,16},{24,28},{28,24},{1,9},{5... | collective-permute-start | bytes 466952 | tf_op jit(solution)/shard_map/ppermute | solution.py:63
  12.0 7.5 %collective-permute-start.3 = (bf16[608,128]{1,0:T(8,128)(2,1)S(1)}, bf16[608,128]{1,0:T(8,128)(2,1)S(1)}, u32[]{:S(2)}, u32[]{:S(2)}) collective-permute-start(bf16[608,128]{1,0:T(8,128)(2,1)S(1)} %get-tuple-element.59), channel_id=1, source_target_pairs={{0,12},{4,8},{8,4},{12,0},{16,28},{20,24},{24,20},{28,16},{1,13},{... | collective-permute-start | bytes 466952 | tf_op jit(solution)/shard_map/ppermute | solution.py:63
  20.5 1.9 %collective-permute-start.4 = (f32[608,128]{1,0:T(8,128)}, f32[608,128]{1,0:T(8,128)}, u32[]{:S(2)}, u32[]{:S(2)}) collective-permute-start(f32[608,128]{1,0:T(8,128)} %add_add_fusion), channel_id=1, source_target_pairs={{0,16},{16,0},{1,17},{17,1},{2,18},{18,2},{3,19},{19,3},{4,20},{20... | collective-permute-start | bytes 933896 | tf_op jit(solution)/shard_map/ppermute | solution.py:35
  23.7 18.4 %collective-permute-start.10 = (bf16[608,256]{1,0:T(8,128)(2,1)S(1)}, bf16[608,256]{1,0:T(8,128)(2,1)S(1)}, u32[]{:S(2)}, u32[]{:S(2)}) collective-permute-start(bf16[608,256]{1,0:T(8,128)(2,1)S(1)} %multiply_convert_fusion.refs_0_), channel_id=1, source_target_pairs={{0,12},{4,8},{8,4},{12,0},{16,28},{20,24},{24,20},{28,16},{1,13},{... | collective-permute-start | bytes 933896 | tf_op jit(solution)/shard_map/ppermute | solution.py:63
  26.7 15.5 %collective-permute-start.9 = (bf16[608,256]{1,0:T(8,128)(2,1)S(1)}, bf16[608,256]{1,0:T(8,128)(2,1)S(1)}, u32[]{:S(2)}, u32[]{:S(2)}) collective-permute-start(bf16[608,256]{1,0:T(8,128)(2,1)S(1)} %multiply_convert_fusion.refs_0_), channel_id=1, source_target_pairs={{0,8},{4,12},{8,0},{12,4},{16,20},{20,16},{24,28},{28,24},{1,9},{5... | collective-permute-start | bytes 933896 | tf_op jit(solution)/shard_map/ppermute | solution.py:63
  27.2 15.0 %collective-permute-start.8 = (bf16[608,256]{1,0:T(8,128)(2,1)S(1)}, bf16[608,256]{1,0:T(8,128)(2,1)S(1)}, u32[]{:S(2)}, u32[]{:S(2)}) collective-permute-start(bf16[608,256]{1,0:T(8,128)(2,1)S(1)} %multiply_convert_fusion.refs_0_), channel_id=1, source_target_pairs={{0,4},{4,0},{8,12},{12,8},{16,24},{20,28},{24,16},{28,20},{1,5},{5... | collective-permute-start | bytes 933896 | tf_op jit(solution)/shard_map/ppermute | solution.py:63
  38.7 16.3 %collective-permute-start.5 = (bf16[608,256]{1,0:T(8,128)(2,1)S(1)}, bf16[608,256]{1,0:T(8,128)(2,1)S(1)}, u32[]{:S(2)}, u32[]{:S(2)}) collective-permute-start(bf16[608,256]{1,0:T(8,128)(2,1)S(1)} %get-tuple-element.70), channel_id=1, source_target_pairs={{0,4},{4,0},{8,12},{12,8},{16,24},{20,28},{24,16},{28,20},{1,5},{5... | collective-permute-start | bytes 933896 | tf_op jit(solution)/shard_map/ppermute | solution.py:63
  40.6 14.4 %collective-permute-start.6 = (bf16[608,256]{1,0:T(8,128)(2,1)S(1)}, bf16[608,256]{1,0:T(8,128)(2,1)S(1)}, u32[]{:S(2)}, u32[]{:S(2)}) collective-permute-start(bf16[608,256]{1,0:T(8,128)(2,1)S(1)} %get-tuple-element.71), channel_id=1, source_target_pairs={{0,8},{4,12},{8,0},{12,4},{16,20},{20,16},{24,28},{28,24},{1,9},{5... | collective-permute-start | bytes 933896 | tf_op jit(solution)/shard_map/ppermute | solution.py:63
  42.2 13.3 %collective-permute-start.7 = (bf16[608,256]{1,0:T(8,128)(2,1)S(1)}, bf16[608,256]{1,0:T(8,128)(2,1)S(1)}, u32[]{:S(2)}, u32[]{:S(2)}) collective-permute-start(bf16[608,256]{1,0:T(8,128)(2,1)S(1)} %get-tuple-element.72), channel_id=1, source_target_pairs={{0,12},{4,8},{8,4},{12,0},{16,28},{20,24},{24,20},{28,16},{1,13},{... | collective-permute-start | bytes 933896 | tf_op jit(solution)/shard_map/ppermute | solution.py:63
  57.6 1.4 %collective-permute-start.11 = (bf16[608,128]{1,0:T(8,128)(2,1)S(1)}, bf16[608,128]{1,0:T(8,128)(2,1)S(1)}, u32[]{:S(2)}, u32[]{:S(2)}) collective-permute-start(bf16[608,128]{1,0:T(8,128)(2,1)S(1)} %slice.65), channel_id=1, source_target_pairs={{0,16},{16,0},{1,17},{17,1},{2,18},{18,2},{3,19},{19,3},{4,20},{20... | collective-permute-start | bytes 466952 | tf_op jit(solution)/shard_map/ppermute | solution.py:35
  59.0 15.9 %collective-permute-start.15 = (bf16[608,128]{1,0:T(8,128)(2,1)S(1)}, bf16[608,128]{1,0:T(8,128)(2,1)S(1)}, u32[]{:S(2)}, u32[]{:S(2)}) collective-permute-start(bf16[608,128]{1,0:T(8,128)(2,1)S(1)} %slice_select_fusion.refs_0_.refs_4_), channel_id=1, source_target_pairs={{0,4},{4,0},{8,12},{12,8},{16,24},{20,28},{24,16},{28,20},{1,5},{5... | collective-permute-start | bytes 466952 | tf_op jit(solution)/shard_map/ppermute | solution.py:47
  60.7 14.2 %collective-permute-start.14 = (bf16[608,128]{1,0:T(8,128)(2,1)S(1)}, bf16[608,128]{1,0:T(8,128)(2,1)S(1)}, u32[]{:S(2)}, u32[]{:S(2)}) collective-permute-start(bf16[608,128]{1,0:T(8,128)(2,1)S(1)} %slice_select_fusion.refs_0_.refs_4_), channel_id=1, source_target_pairs={{0,3},{1,2},{2,1},{3,0},{4,7},{5,6},{6,5},{7,4},{8,11},{9,10},{10,... | collective-permute-start | bytes 466952 | tf_op jit(solution)/shard_map/ppermute | solution.py:69
  64.3 13.2 %collective-permute-start.13 = (bf16[608,128]{1,0:T(8,128)(2,1)S(1)}, bf16[608,128]{1,0:T(8,128)(2,1)S(1)}, u32[]{:S(2)}, u32[]{:S(2)}) collective-permute-start(bf16[608,128]{1,0:T(8,128)(2,1)S(1)} %slice_select_fusion.refs_0_.refs_4_), channel_id=1, source_target_pairs={{0,2},{1,3},{2,0},{3,1},{4,6},{5,7},{6,4},{7,5},{8,10},{9,11},{10,... | collective-permute-start | bytes 466952 | tf_op jit(solution)/shard_map/ppermute | solution.py:69
  64.3 13.2 %collective-permute-start.12 = (bf16[608,128]{1,0:T(8,128)(2,1)S(1)}, bf16[608,128]{1,0:T(8,128)(2,1)}, u32[]{:S(2)}, u32[]{:S(2)}) collective-permute-start(bf16[608,128]{1,0:T(8,128)(2,1)S(1)} %slice_select_fusion.refs_0_.refs_4_), channel_id=1, source_target_pairs={{0,1},{1,0},{2,3},{3,2},{4,5},{5,4},{6,7},{7,6},{8,9},{9,8},{10,11... | collective-permute-start | bytes 466952 | tf_op jit(solution)/shard_map/ppermute | solution.py:69
  65.1 29.6 %copy-start = (bf16[608,2432]{1,0:T(8,128)(2,1)S(1)}, bf16[608,2432]{1,0:T(8,128)(2,1)}, u32[]{:S(2)}) copy-start(bf16[608,2432]{1,0:T(8,128)(2,1)} %weight.3) | copy-start | bytes 8871940
  77.5 2.0 %collective-permute-start.34 = (bf16[608,128]{1,0:T(8,128)(2,1)S(1)}, bf16[608,128]{1,0:T(8,128)(2,1)S(1)}, u32[]{:S(2)}, u32[]{:S(2)}) collective-permute-start(bf16[608,128]{1,0:T(8,128)(2,1)S(1)} %copy-done.15), channel_id=1, source_target_pairs={{0,16},{16,0},{1,17},{17,1},{2,18},{18,2},{3,19},{19,3},{4,20},{20... | collective-permute-start | bytes 466952 | tf_op jit(solution)/shard_map/ppermute | solution.py:35
  77.6 6.4 %collective-permute-start.33 = (bf16[608,128]{1,0:T(8,128)(2,1)S(1)}, bf16[608,128]{1,0:T(8,128)(2,1)S(1)}, u32[]{:S(2)}, u32[]{:S(2)}) collective-permute-start(bf16[608,128]{1,0:T(8,128)(2,1)S(1)} %copy-done.15), channel_id=1, source_target_pairs={{0,1},{1,0},{2,3},{3,2},{4,5},{5,4},{6,7},{7,6},{8,9},{9,8},{10,11... | collective-permute-start | bytes 466952 | tf_op jit(solution)/shard_map/ppermute | solution.py:69
  77.7 7.9 %collective-permute-start.36 = (bf16[608,128]{1,0:T(8,128)(2,1)S(1)}, bf16[608,128]{1,0:T(8,128)(2,1)S(1)}, u32[]{:S(2)}, u32[]{:S(2)}) collective-permute-start(bf16[608,128]{1,0:T(8,128)(2,1)S(1)} %slice_select_fusion.refs_0_.refs_4_), channel_id=1, source_target_pairs={{0,16},{16,0},{1,17},{17,1},{2,18},{18,2},{3,19},{19,3},{4,20},{20... | collective-permute-start | bytes 466952 | tf_op jit(solution)/shard_map/ppermute | solution.py:35
  78.1 8.6 %collective-permute-start.16 = (bf16[608,128]{1,0:T(8,128)(2,1)S(1)}, bf16[608,128]{1,0:T(8,128)(2,1)S(1)}, u32[]{:S(2)}, u32[]{:S(2)}) collective-permute-start(bf16[608,128]{1,0:T(8,128)(2,1)S(1)} %slice_select_fusion.refs_0_.refs_4_), channel_id=1, source_target_pairs={{0,8},{4,12},{8,0},{12,4},{16,20},{20,16},{24,28},{28,24},{1,9},{5... | collective-permute-start | bytes 466952 | tf_op jit(solution)/shard_map/ppermute | solution.py:47
  78.6 8.1 %collective-permute-start.37 = (bf16[608,128]{1,0:T(8,128)(2,1)S(1)}, bf16[608,128]{1,0:T(8,128)(2,1)S(1)}, u32[]{:S(2)}, u32[]{:S(2)}) collective-permute-start(bf16[608,128]{1,0:T(8,128)(2,1)S(1)} %collective-permute-done.15.refs_1_.refs_5_), channel_id=1, source_target_pairs={{0,16},{16,0},{1,17},{17,1},{2,18},{18,2},{3,19},{19,3},{4,20},{20... | collective-permute-start | bytes 466952 | tf_op jit(solution)/shard_map/ppermute | solution.py:35
  80.2 7.8 %collective-permute-start.17 = (bf16[608,128]{1,0:T(8,128)(2,1)S(1)}, bf16[608,128]{1,0:T(8,128)(2,1)S(1)}, u32[]{:S(2)}, u32[]{:S(2)}) collective-permute-start(bf16[608,128]{1,0:T(8,128)(2,1)S(1)} %collective-permute-done.15.refs_1_.refs_5_), channel_id=1, source_target_pairs={{0,8},{4,12},{8,0},{12,4},{16,20},{20,16},{24,28},{28,24},{1,9},{5... | collective-permute-start | bytes 466952 | tf_op jit(solution)/shard_map/ppermute | solution.py:47
  84.1 15.7 %collective-permute-start.19 = (bf16[624,256]{1,0:T(8,128)(2,1)}, bf16[624,256]{1,0:T(8,128)(2,1)}, u32[]{:S(2)}, u32[]{:S(2)}) collective-permute-start(bf16[624,256]{1,0:T(8,128)(2,1)} %get-tuple-element.96), channel_id=1, source_target_pairs={{0,4},{4,0},{8,12},{12,8},{16,24},{20,28},{24,16},{28,20},{1,5},{5... | collective-permute-start | bytes 958472 | tf_op jit(solution)/shard_map/ppermute | solution.py:47
  86.2 14.1 %collective-permute-start.20 = (bf16[624,256]{1,0:T(8,128)(2,1)}, bf16[624,256]{1,0:T(8,128)(2,1)}, u32[]{:S(2)}, u32[]{:S(2)}) collective-permute-start(bf16[624,256]{1,0:T(8,128)(2,1)} %get-tuple-element.97), channel_id=1, source_target_pairs={{0,4},{4,0},{8,12},{12,8},{16,24},{20,28},{24,16},{28,20},{1,5},{5... | collective-permute-start | bytes 958472 | tf_op jit(solution)/shard_map/ppermute | solution.py:47
  86.8 3.4 %collective-permute-start.43 = (bf16[608,128]{1,0:T(8,128)(2,1)}, bf16[608,128]{1,0:T(8,128)(2,1)}, u32[]{:S(2)}, u32[]{:S(2)}) collective-permute-start(bf16[608,128]{1,0:T(8,128)(2,1)} %collective-permute-done.12.refs_12_), channel_id=1, source_target_pairs={{0,16},{16,0},{1,17},{17,1},{2,18},{18,2},{3,19},{19,3},{4,20},{20... | collective-permute-start | bytes 466952 | tf_op jit(solution)/shard_map/ppermute | solution.py:35
  87.4 7.3 %collective-permute-start.41 = (bf16[608,128]{1,0:T(8,128)(2,1)}, bf16[608,128]{1,0:T(8,128)(2,1)}, u32[]{:S(2)}, u32[]{:S(2)}) collective-permute-start(bf16[608,128]{1,0:T(8,128)(2,1)} %collective-permute-done.12.refs_12_), channel_id=1, source_target_pairs={{0,8},{4,12},{8,0},{12,4},{16,20},{20,16},{24,28},{28,24},{1,9},{5... | collective-permute-start | bytes 466952 | tf_op jit(solution)/shard_map/ppermute | solution.py:47
  88.6 9.5 %collective-permute-start.40 = (bf16[608,128]{1,0:T(8,128)(2,1)}, bf16[608,128]{1,0:T(8,128)(2,1)}, u32[]{:S(2)}, u32[]{:S(2)}) collective-permute-start(bf16[608,128]{1,0:T(8,128)(2,1)} %collective-permute-done.12.refs_12_), channel_id=1, source_target_pairs={{0,4},{4,0},{8,12},{12,8},{16,24},{20,28},{24,16},{28,20},{1,5},{5... | collective-permute-start | bytes 466952 | tf_op jit(solution)/shard_map/ppermute | solution.py:47
  90.1 8.1 %collective-permute-start.35 = (bf16[608,128]{1,0:T(8,128)(2,1)}, bf16[608,128]{1,0:T(8,128)(2,1)S(1)}, u32[]{:S(2)}, u32[]{:S(2)}) collective-permute-start(bf16[608,128]{1,0:T(8,128)(2,1)} %copy-done.19), channel_id=1, source_target_pairs={{0,16},{16,0},{1,17},{17,1},{2,18},{18,2},{3,19},{19,3},{4,20},{20... | collective-permute-start | bytes 466952 | tf_op jit(solution)/shard_map/ppermute | solution.py:35
  94.7 5.1 %collective-permute-start.38 = (bf16[608,128]{1,0:T(8,128)(2,1)S(1)}, bf16[608,128]{1,0:T(8,128)(2,1)S(1)}, u32[]{:S(2)}, u32[]{:S(2)}) collective-permute-start(bf16[608,128]{1,0:T(8,128)(2,1)S(1)} %collective-permute-done.16.refs_2_.refs_6_), channel_id=1, source_target_pairs={{0,16},{16,0},{1,17},{17,1},{2,18},{18,2},{3,19},{19,3},{4,20},{20... | collective-permute-start | bytes 466952 | tf_op jit(solution)/shard_map/ppermute | solution.py:35
  98.1 8.5 %collective-permute-start.18 = (f32[608,128]{1,0:T(8,128)S(1)}, f32[608,128]{1,0:T(8,128)S(1)}, u32[]{:S(2)}, u32[]{:S(2)}) collective-permute-start(f32[608,128]{1,0:T(8,128)S(1)} %residual_rows.1), channel_id=1, source_target_pairs={{0,16},{16,0},{1,17},{17,1},{2,18},{18,2},{3,19},{19,3},{4,20},{20... | collective-permute-start | bytes 933896 | tf_op jit(solution)/shard_map/ppermute | solution.py:35
  98.2 11.3 %collective-permute-start.26 = (bf16[2,608,128]{2,1,0:T(8,128)(2,1)S(1)}, bf16[2,608,128]{2,1,0:T(8,128)(2,1)S(1)}, u32[]{:S(2)}, u32[]{:S(2)}) collective-permute-start(bf16[2,608,128]{2,1,0:T(8,128)(2,1)S(1)} %pad_maximum_fusion.refs_4_), channel_id=1, source_target_pairs={{0,4},{4,0},{8,12},{12,8},{16,24},{20,28},{24,16},{28,20},{1,5},{5... | collective-permute-start | bytes 933896 | tf_op jit(solution)/shard_map/ppermute | solution.py:47
  99.8 2.3 %collective-permute-start.39 = (bf16[608,128]{1,0:T(8,128)(2,1)S(1)}, bf16[608,128]{1,0:T(8,128)(2,1)S(1)}, u32[]{:S(2)}, u32[]{:S(2)}) collective-permute-start(bf16[608,128]{1,0:T(8,128)(2,1)S(1)} %copy-done.9), channel_id=1, source_target_pairs={{0,16},{16,0},{1,17},{17,1},{2,18},{18,2},{3,19},{19,3},{4,20},{20... | collective-permute-start | bytes 466952 | tf_op jit(solution)/shard_map/ppermute | solution.py:35
  99.8 4.9 %collective-permute-start.45 = (bf16[608,128]{1,0:T(8,128)(2,1)}, bf16[608,128]{1,0:T(8,128)(2,1)S(1)}, u32[]{:S(2)}, u32[]{:S(2)}) collective-permute-start(bf16[608,128]{1,0:T(8,128)(2,1)} %collective-permute-done.41.refs_14_), channel_id=1, source_target_pairs={{0,16},{16,0},{1,17},{17,1},{2,18},{18,2},{3,19},{19,3},{4,20},{20... | collective-permute-start | bytes 466952 | tf_op jit(solution)/shard_map/ppermute | solution.py:35
  100.3 6.1 %collective-permute-start.42 = (bf16[608,128]{1,0:T(8,128)(2,1)}, bf16[608,128]{1,0:T(8,128)(2,1)S(1)}, u32[]{:S(2)}, u32[]{:S(2)}) collective-permute-start(bf16[608,128]{1,0:T(8,128)(2,1)} %collective-permute-done.40.refs_13_), channel_id=1, source_target_pairs={{0,8},{4,12},{8,0},{12,4},{16,20},{20,16},{24,28},{28,24},{1,9},{5... | collective-permute-start | bytes 466952 | tf_op jit(solution)/shard_map/ppermute | solution.py:47
  102.1 13.5 %collective-permute-start.23 = (bf16[608,128]{1,0:T(8,128)(2,1)S(1)}, bf16[608,128]{1,0:T(8,128)(2,1)S(1)}, u32[]{:S(2)}, u32[]{:S(2)}) collective-permute-start(bf16[608,128]{1,0:T(8,128)(2,1)S(1)} %copy-done.16), channel_id=1, source_target_pairs={{0,3},{1,2},{2,1},{3,0},{4,7},{5,6},{6,5},{7,4},{8,11},{9,10},{10,... | collective-permute-start | bytes 466952 | tf_op jit(solution)/shard_map/ppermute | solution.py:69
  104.7 3.5 %collective-permute-start.44 = (bf16[608,128]{1,0:T(8,128)(2,1)}, bf16[608,128]{1,0:T(8,128)(2,1)S(1)}, u32[]{:S(2)}, u32[]{:S(2)}) collective-permute-start(bf16[608,128]{1,0:T(8,128)(2,1)} %collective-permute-done.40.refs_13_), channel_id=1, source_target_pairs={{0,16},{16,0},{1,17},{17,1},{2,18},{18,2},{3,19},{19,3},{4,20},{20... | collective-permute-start | bytes 466952 | tf_op jit(solution)/shard_map/ppermute | solution.py:35
  106.4 4.5 %collective-permute-start.46 = (bf16[608,128]{1,0:T(8,128)(2,1)S(1)}, bf16[608,128]{1,0:T(8,128)(2,1)S(1)}, u32[]{:S(2)}, u32[]{:S(2)}) collective-permute-start(bf16[608,128]{1,0:T(8,128)(2,1)S(1)} %collective-permute-done.42.refs_15_), channel_id=1, source_target_pairs={{0,16},{16,0},{1,17},{17,1},{2,18},{18,2},{3,19},{19,3},{4,20},{20... | collective-permute-start | bytes 466952 | tf_op jit(solution)/shard_map/ppermute | solution.py:35
  106.6 9.0 %collective-permute-start.21 = (bf16[624,256]{1,0:T(8,128)(2,1)S(1)}, bf16[624,256]{1,0:T(8,128)(2,1)S(1)}, u32[]{:S(2)}, u32[]{:S(2)}) collective-permute-start(bf16[624,256]{1,0:T(8,128)(2,1)S(1)} %get-tuple-element.102), channel_id=1, source_target_pairs={{0,8},{4,12},{8,0},{12,4},{16,20},{20,16},{24,28},{28,24},{1,9},{5... | collective-permute-start | bytes 958472 | tf_op jit(solution)/shard_map/ppermute | solution.py:47
  108.2 10.7 %collective-permute-start.22 = (bf16[608,128]{1,0:T(8,128)(2,1)S(1)}, bf16[608,128]{1,0:T(8,128)(2,1)S(1)}, u32[]{:S(2)}, u32[]{:S(2)}) collective-permute-start(bf16[608,128]{1,0:T(8,128)(2,1)S(1)} %copy-done.16), channel_id=1, source_target_pairs={{0,2},{1,3},{2,0},{3,1},{4,6},{5,7},{6,4},{7,5},{8,10},{9,11},{10,... | collective-permute-start | bytes 466952 | tf_op jit(solution)/shard_map/ppermute | solution.py:69
  109.5 9.5 %collective-permute-start.27 = (bf16[2,608,128]{2,1,0:T(8,128)(2,1)S(1)}, bf16[2,608,128]{2,1,0:T(8,128)(2,1)S(1)}, u32[]{:S(2)}, u32[]{:S(2)}) collective-permute-start(bf16[2,608,128]{2,1,0:T(8,128)(2,1)S(1)} %pad_maximum_fusion.refs_4_), channel_id=1, source_target_pairs={{0,8},{4,12},{8,0},{12,4},{16,20},{20,16},{24,28},{28,24},{1,9},{5... | collective-permute-start | bytes 933896 | tf_op jit(solution)/shard_map/ppermute | solution.py:47
  110.8 9.5 %collective-permute-start.28 = (bf16[2,608,128]{2,1,0:T(8,128)(2,1)S(1)}, bf16[2,608,128]{2,1,0:T(8,128)(2,1)S(1)}, u32[]{:S(2)}, u32[]{:S(2)}) collective-permute-start(bf16[2,608,128]{2,1,0:T(8,128)(2,1)S(1)} %collective-permute-done.26.refs_5_), channel_id=1, source_target_pairs={{0,8},{4,12},{8,0},{12,4},{16,20},{20,16},{24,28},{28,24},{1,9},{5... | collective-permute-start | bytes 933896 | tf_op jit(solution)/shard_map/ppermute | solution.py:47
  115.6 7.6 %collective-permute-start.29 = (bf16[2,608,128]{2,1,0:T(8,128)(2,1)S(1)}, bf16[2,608,128]{2,1,0:T(8,128)(2,1)S(1)}, u32[]{:S(2)}, u32[]{:S(2)}) collective-permute-start(bf16[2,608,128]{2,1,0:T(8,128)(2,1)S(1)} %pad_maximum_fusion.refs_4_), channel_id=1, source_target_pairs={{0,16},{16,0},{1,17},{17,1},{2,18},{18,2},{3,19},{19,3},{4,20},{20... | collective-permute-start | bytes 933896 | tf_op jit(solution)/shard_map/ppermute | solution.py:35
  115.7 4.7 %collective-permute-start.25 = (bf16[608,128]{1,0:T(8,128)(2,1)S(1)}, bf16[608,128]{1,0:T(8,128)(2,1)S(1)}, u32[]{:S(2)}, u32[]{:S(2)}) collective-permute-start(bf16[608,128]{1,0:T(8,128)(2,1)S(1)} %collective-permute-done.23.refs_1_), channel_id=1, source_target_pairs={{0,16},{16,0},{1,17},{17,1},{2,18},{18,2},{3,19},{19,3},{4,20},{20... | collective-permute-start | bytes 466952 | tf_op jit(solution)/shard_map/ppermute | solution.py:35
  118.9 4.3 %collective-permute-start.30 = (bf16[2,608,128]{2,1,0:T(8,128)(2,1)S(1)}, bf16[2,608,128]{2,1,0:T(8,128)(2,1)S(1)}, u32[]{:S(2)}, u32[]{:S(2)}) collective-permute-start(bf16[2,608,128]{2,1,0:T(8,128)(2,1)S(1)} %collective-permute-done.26.refs_5_), channel_id=1, source_target_pairs={{0,16},{16,0},{1,17},{17,1},{2,18},{18,2},{3,19},{19,3},{4,20},{20... | collective-permute-start | bytes 933896 | tf_op jit(solution)/shard_map/ppermute | solution.py:35
  119.0 4.2 %collective-permute-start.31 = (bf16[2,608,128]{2,1,0:T(8,128)(2,1)S(1)}, bf16[2,608,128]{2,1,0:T(8,128)(2,1)S(1)}, u32[]{:S(2)}, u32[]{:S(2)}) collective-permute-start(bf16[2,608,128]{2,1,0:T(8,128)(2,1)S(1)} %collective-permute-done.27.refs_6_), channel_id=1, source_target_pairs={{0,16},{16,0},{1,17},{17,1},{2,18},{18,2},{3,19},{19,3},{4,20},{20... | collective-permute-start | bytes 933896 | tf_op jit(solution)/shard_map/ppermute | solution.py:35
  120.3 2.9 %collective-permute-start.32 = (bf16[2,608,128]{2,1,0:T(8,128)(2,1)S(1)}, bf16[2,608,128]{2,1,0:T(8,128)(2,1)S(1)}, u32[]{:S(2)}, u32[]{:S(2)}) collective-permute-start(bf16[2,608,128]{2,1,0:T(8,128)(2,1)S(1)} %collective-permute-done.28.refs_7_), channel_id=1, source_target_pairs={{0,16},{16,0},{1,17},{17,1},{2,18},{18,2},{3,19},{19,3},{4,20},{20... | collective-permute-start | bytes 933896 | tf_op jit(solution)/shard_map/ppermute | solution.py:35
  120.3 2.8 %collective-permute-start.24 = (bf16[608,128]{1,0:T(8,128)(2,1)S(1)}, bf16[608,128]{1,0:T(8,128)(2,1)S(1)}, u32[]{:S(2)}, u32[]{:S(2)}) collective-permute-start(bf16[608,128]{1,0:T(8,128)(2,1)S(1)} %collective-permute-done.22.refs_0_), channel_id=1, source_target_pairs={{0,16},{16,0},{1,17},{17,1},{2,18},{18,2},{3,19},{19,3},{4,20},{20... | collective-permute-start | bytes 466952 | tf_op jit(solution)/shard_map/ppermute | solution.py:35
  (31 other events, 187.1 us)

commit v8 on v7

--- a/solution.py
+++ b/solution.py
@@ -622,24 +622,28 @@
 
     out_half = jnp.where(is_control, out_rows[:, :half], swap_grp(out_rows[:, half:]))
     far = gather_dp(out_half)[1:]
+    near = [out_half] + [send(out_half, place) for place in range(1, blocks)]
     sent, kept, token_sums = backward_last(
         order, after(grad, out_half), total, slope_a, slope_b, acts, stats, mod, w_in, w_out, cut, blocks, "backward_last"
     )
-    near = [out_half, step(out_half, 0)]
     far, near, sent, kept, token_sums = lax.optimization_barrier((far, near, sent, kept, token_sums))
-    for level in range(1, levels):
-        near = near + steps(near, level)
-    near_other = [swap_grp(value) for value in near]
-    residual = residual_rows(order, zero_weight, near)
-    cots = gather_dp(after(cot1, token_sums))
-    cots_other = [swap_grp(value) for value in cots]
 
     gathers = [[far[0]], [jnp.stack(far[1:])]]
+    last = gather_dp(near[-1])[1:]
+    lasts = [last[0], jnp.stack(last[1:])]
     for level in range(levels):
         got = steps(sent, level)
-        gathers = [blocks_so_far + steps(blocks_so_far, level) for blocks_so_far in gathers]
-        if level + 1 < levels:
+        final = level + 1 == levels
+        for gather, end in zip(gathers, lasts):
+            gather += steps(gather[:-1], level) + [end] if final else steps(gather, level)
+        if level == 0:
+            cot1, near = after((cot1, near), got)
+            cots = gather_dp(cot1)
+            near_other = [swap_grp(value) for value in near]
+            residual = residual_rows(order, zero_weight, near)
+        if not final:
             sent, kept, token_sums = fold(got, kept, token_sums)
+    cots_other = [swap_grp(value) for value in cots]
     more = unpack_sums(got[0][-16:])
     plain, along = token_sums[0:1] + more[0], token_sums[1:2] + more[1]
     kept = [kept[0] + got[0][:rows].astype(F32)]

time: 128 us -> 147 us (1.15)
  local copies, waits for them, and re-layouts: 8.09 us -> 15.3 us
  starting transfers between devices: 35.9 us -> 42.5 us
  waiting for transfers between devices: 20.1 us -> 25.4 us
    ppermute x6 -> x9, waiting for transfers between devices: 8.59 us -> 18.7 us  [gather_dp(): lax.ppermute(value, 'dp', [(i, i ^ mask) for i in range(length)])]
    unnamed x65 -> x113, local copies, waits for them, and re-layouts: 8.08 us -> 15.3 us
    ppermute x12 -> x7, waiting for transfers between devices: 8.09 us -> 2.53 us  [step(): return lax.ppermute(value, ('grp', 'fsdp'), pairs)]
    ppermute x6 -> x9, starting transfers between devices: 8.27 us -> 12.8 us  [gather_dp(): lax.ppermute(value, 'dp', [(i, i ^ mask) for i in range(length)])]
    ppermute x9 -> x12, starting transfers between devices: 11.6 us -> 15.1 us  [send(): return lax.ppermute(value, ('grp', 'fsdp'), pairs)]
    ppermute x12 -> x7, starting transfers between devices: 11.7 us -> 10.7 us  [step(): return lax.ppermute(value, ('grp', 'fsdp'), pairs)]
  transfers between devices with their start and end apart: 47 -> 48, of which waited for: 10 -> 13; matrix products, arithmetic and copies ran while one was open for 4% -> 2% of each run, Pallas kernels for 35% -> 34%
where the time goes in v8:
time: 147 us; the launch traced here: 146 us
  Pallas kernels  53.2 us (36%)
  starting transfers between devices  42.5 us (29%)
  waiting for transfers between devices  25.4 us (17%)
  local copies, waits for them, and re-layouts  15.3 us (10%)
  other arithmetic  8.7 us (6%)
    ppermute x9, waiting for transfers between devices, gather_dp(): lax.ppermute(value, 'dp', [(i, i ^ mask) for i in range(length)])  18.7 us
    unnamed x113, local copies, waits for them, and re-layouts  15.3 us
    ppermute x12, starting transfers between devices, send(): return lax.ppermute(value, ('grp', 'fsdp'), pairs)  15.1 us
    ppermute x9, starting transfers between devices, gather_dp(): lax.ppermute(value, 'dp', [(i, i ^ mask) for i in range(length)])  12.8 us
    pallas_call x1, Pallas kernels, backward_first(): pl.pallas_call(functools.partial(backward_first_kernel, blocks, part), ou...  11.7 us
    pallas_call x1, Pallas kernels, forward_last(): pl.pallas_call(functools.partial(forward_last_kernel, start), out_shape=[...  11.4 us
    ppermute x7, starting transfers between devices, step(): return lax.ppermute(value, ('grp', 'fsdp'), pairs)  10.7 us
    pallas_call x2, Pallas kernels, zero_projection_grad(): pl.pallas_call(functools.partial(zero_grad_kernel, blocks, first, count),...  9 us
  transfers between devices with their start and end apart: 48, of which 13 were waited for; matrix products, arithmetic and copies ran while one was open for 2% of the time, Pallas kernels for 34%

profile of v8, /device:TPU:0, one launch (start us, length us, event | category | flops | bytes accessed | tf_op | source)
XLA Modules:
  0.0 146.3 jit_solution(7486993379442311409)
XLA Ops:
  1.1 0.8 copy.13.modulation
  2.7 1.0 copy-done.4
  3.6 4.0 %prepare.1 = (f32[608,128]{1,0:T(8,128)S(1)}, bf16[608,128]{1,0:T(8,128)(2,1)S(1)}, bf16[608,128]{1,0:T(8,128)(2,1)S(1)}, bf16[608,128]{1,0:T(8,128)(2,1)S(1)}, ...) custom-call(s32[9]{0:T(128)S(1)} %pad_add_fusion.order, ...), custom_call_target="tpu_custom_call" | custom-call | flops 378535936 | bytes 4202496 | tf_op jit(solution)/shard_map/prepare/pallas_call | solution.py:450
  7.6 2.9 %collective-permute-start.1 = (bf16[608,128]{1,0:T(8,128)(2,1)S(1)}, bf16[608,128]{1,0:T(8,128)(2,1)S(1)}, u32[]{:S(2)}, u32[]{:S(2)}) collective-permute-start(bf16[608,128]{1,0:T(8,128)(2,1)S(1)} %get-tuple-element.63), channel_id=1, source_target_pairs={{0,4},{4,0},{8,12},{12,8},{16,24},{20,28},{24,16},{28,20},{1,5},{5... | collective-permute-start | bytes 466952 | tf_op jit(solution)/shard_map/ppermute | solution.py:63
  10.5 1.5 %collective-permute-start.2 = (bf16[608,128]{1,0:T(8,128)(2,1)S(1)}, bf16[608,128]{1,0:T(8,128)(2,1)S(1)}, u32[]{:S(2)}, u32[]{:S(2)}) collective-permute-start(bf16[608,128]{1,0:T(8,128)(2,1)S(1)} %get-tuple-element.64), channel_id=1, source_target_pairs={{0,8},{4,12},{8,0},{12,4},{16,20},{20,16},{24,28},{28,24},{1,9},{5... | collective-permute-start | bytes 466952 | tf_op jit(solution)/shard_map/ppermute | solution.py:63
  12.0 7.4 %forward_first.1 = (f32[256,1024]{1,0:T(8,128)S(1)}, f32[256,2432]{1,0:T(8,128)}, f32[2432,8]{1,0:T(8,128)S(1)}) custom-call(bf16[256,2432]{1,0:T(8,128)(2,1)S(1)} %get-tuple-element.74.normed, f32[1,3,2432]{2,1,0:T(4,128)S(1)} %copy.13.modulation, bf16[1,2432,2432]{2,1,0:T(8,128)(2,1)} %w_in.5, bf16[1,2432,2432]{2,1,0:T(8,128)(2,1)} %w_out.5), custom_call_target="tpu_custom_call" | custom-call | flops 2550136832 | bytes 12451840 | tf_op jit(solution)/shard_map/forward_first/pallas_call | solution.py:253
  19.5 0.9 add_add_fusion
  20.9 1.5 %collective-permute-done.4 = f32[608,128]{1,0:T(8,128)} collective-permute-done((f32[608,128]{1,0:T(8,128)}, f32[608,128]{1,0:T(8,128)}, u32[]{:S(2)}, u32[]{:S(2)}) %collective-permute-start.4) | collective-permute-done | bytes 311328 | tf_op jit(solution)/shard_map/ppermute | solution.py:35
  22.4 1.3 multiply_convert_fusion.refs_0_
  23.7 3.0 %collective-permute-start.10 = (bf16[608,256]{1,0:T(8,128)(2,1)S(1)}, bf16[608,256]{1,0:T(8,128)(2,1)S(1)}, u32[]{:S(2)}, u32[]{:S(2)}) collective-permute-start(bf16[608,256]{1,0:T(8,128)(2,1)S(1)} %multiply_convert_fusion.refs_0_), channel_id=1, source_target_pairs={{0,12},{4,8},{8,4},{12,0},{16,28},{20,24},{24,20},{28,16},{1,13},{... | collective-permute-start | bytes 933896 | tf_op jit(solution)/shard_map/ppermute | solution.py:63
  27.3 11.4 %forward_last.1 = (f32[256,1408]{1,0:T(8,128)}, f32[608,256]{1,0:T(8,128)S(1)}, bf16[608,256]{1,0:T(8,128)(2,1)S(1)}, bf16[608,256]{1,0:T(8,128)(2,1)S(1)}, bf16[608,256]{1,0:T(8,128)(2,1)S(1)}) custom-call(s32[9]{0:T(128)S(1)} %pad_add_fusion.order, bf16[256,2432]{1,0:T(8,128)(2,1)S(1)} %get-tuple-element.74.normed, f32[256,2432]{1,0:T(8,128)} %get-tuple-element.70.before, ...), custom_call_target="tpu_custom_call" | custom-call | flops 3506438144 | bytes 16187392 | tf_op jit(solution)/shard_map/forward_last/pallas_call | solution.py:267
  38.7 1.9 %collective-permute-start.5 = (bf16[608,256]{1,0:T(8,128)(2,1)S(1)}, bf16[608,256]{1,0:T(8,128)(2,1)S(1)}, u32[]{:S(2)}, u32[]{:S(2)}) collective-permute-start(bf16[608,256]{1,0:T(8,128)(2,1)S(1)} %get-tuple-element.76), channel_id=1, source_target_pairs={{0,4},{4,0},{8,12},{12,8},{16,24},{20,28},{24,16},{28,20},{1,5},{5... | collective-permute-start | bytes 933896 | tf_op jit(solution)/shard_map/ppermute | solution.py:63
  40.6 1.5 %collective-permute-start.6 = (bf16[608,256]{1,0:T(8,128)(2,1)S(1)}, bf16[608,256]{1,0:T(8,128)(2,1)S(1)}, u32[]{:S(2)}, u32[]{:S(2)}) collective-permute-start(bf16[608,256]{1,0:T(8,128)(2,1)S(1)} %get-tuple-element.77), channel_id=1, source_target_pairs={{0,8},{4,12},{8,0},{12,4},{16,20},{20,16},{24,28},{28,24},{1,9},{5... | collective-permute-start | bytes 933896 | tf_op jit(solution)/shard_map/ppermute | solution.py:63
  42.2 11.7 %backward_first.1 = (bf16[256,2432]{1,0:T(8,128)(2,1)S(1)}, f32[256,2432]{1,0:T(8,128)}) custom-call(s32[9]{0:T(128)S(1)} %pad_add_fusion.order, bf16[608,256]{1,0:T(8,128)(2,1)S(1)} %multiply_convert_fusion.refs_0_, bf16[608,256]{1,0:T(8,128)(2,1)S(1)} %collective-permute-done.8.refs_1_, bf16[608,256]{1,0:T(8,128)(2,1)S(1)} %collective-permute-done.9.refs_2_, ...), custom_call_target="tpu_custom_call" | custom-call | flops 5100273664 | bytes 22413312 | tf_op jit(solution)/shard_map/backward_first/pallas_call | solution.py:325
  53.9 1.0 copy-done.6
  55.4 2.1 %fusion.16 = (bf16[608,256]{1,0:T(8,128)(2,1)S(1)}, f32[608,256]{1,0:T(8,128)}) fusion(f32[608,256]{1,0:T(8,128)S(1)} %get-tuple-element.75, bf16[608,256]{1,0:T(8,128)(2,1)S(1)} %collective-permute-done.7, bf16[608,256]{1,0:T(8,128)(2,1)S(1)} %collective-permute-done.6, bf16[608,256]{1,0:T(8,128)(2,1)S(1)} %collective-permute-done.5, ...), kind=kLoop, calls=%fused_computation.36 | loop fusion | flops 1556480 | bytes 2804100 | tf_op jit(solution)/shard_map/convert_element_type | solution.py:621
  57.6 1.4 collective-permute-done.11
  59.0 2.6 %collective-permute-start.17 = (bf16[608,128]{1,0:T(8,128)(2,1)S(1)}, bf16[608,128]{1,0:T(8,128)(2,1)}, u32[]{:S(2)}, u32[]{:S(2)}) collective-permute-start(bf16[608,128]{1,0:T(8,128)(2,1)S(1)} %slice_select_fusion.refs_0_.refs_4_), channel_id=1, source_target_pairs={{0,12},{4,8},{8,4},{12,0},{16,28},{20,24},{24,20},{28,16},{1,13},{... | collective-permute-start | bytes 466952 | tf_op jit(solution)/shard_map/ppermute | solution.py:63
  62.6 3.7 %collective-permute-start.14 = (bf16[608,128]{1,0:T(8,128)(2,1)S(1)}, bf16[608,128]{1,0:T(8,128)(2,1)S(1)}, u32[]{:S(2)}, u32[]{:S(2)}) collective-permute-start(bf16[608,128]{1,0:T(8,128)(2,1)S(1)} %slice_select_fusion.refs_0_.refs_4_), channel_id=1, source_target_pairs={{0,3},{1,2},{2,1},{3,0},{4,7},{5,6},{6,5},{7,4},{8,11},{9,10},{10,... | collective-permute-start | bytes 466952 | tf_op jit(solution)/shard_map/ppermute | solution.py:69
  67.0 1.7 %collective-permute-start.12 = (bf16[608,128]{1,0:T(8,128)(2,1)S(1)}, bf16[608,128]{1,0:T(8,128)(2,1)S(1)}, u32[]{:S(2)}, u32[]{:S(2)}) collective-permute-start(bf16[608,128]{1,0:T(8,128)(2,1)S(1)} %slice_select_fusion.refs_0_.refs_4_), channel_id=1, source_target_pairs={{0,1},{1,0},{2,3},{3,2},{4,5},{5,4},{6,7},{7,6},{8,9},{9,8},{10,11... | collective-permute-start | bytes 466952 | tf_op jit(solution)/shard_map/ppermute | solution.py:69
  68.7 7.3 %backward_last.1 = (bf16[624,256]{1,0:T(8,128)(2,1)S(1)}, bf16[624,256]{1,0:T(8,128)(2,1)S(1)}, f32[608,256]{1,0:T(8,128)S(1)}, f32[608,256]{1,0:T(8,128)S(1)}, f32[2,256]{1,0:T(2,128)S(1)}) custom-call(s32[9]{0:T(128)S(1)} %pad_add_fusion.order, bf16[256,2432]{1,0:T(8,128)(2,1)} %copy-done.6, f32[256,2432]{1,0:T(8,128)} %get-tuple-element.88.before, ...), custom_call_target="tpu_custom_call" | custom-call | flops 956301312 | bytes 6225920 | tf_op jit(solution)/shard_map/backward_last/pallas_call | solution.py:378
  76.0 0.8 copy-done.17
  76.9 2.1 %collective-permute-done.13 = bf16[608,128]{1,0:T(8,128)(2,1)S(1)} collective-permute-done((bf16[608,128]{1,0:T(8,128)(2,1)S(1)}, bf16[608,128]{1,0:T(8,128)(2,1)S(1)}, u32[]{:S(2)}, u32[]{:S(2)}) %collective-permute-start.13) | collective-permute-done | bytes 155680 | tf_op jit(solution)/shard_map/ppermute | solution.py:69
  78.9 2.5 %collective-permute-start.29 = (bf16[608,128]{1,0:T(8,128)(2,1)}, bf16[608,128]{1,0:T(8,128)(2,1)S(1)}, u32[]{:S(2)}, u32[]{:S(2)}) collective-permute-start(bf16[608,128]{1,0:T(8,128)(2,1)} %collective-permute-done.17.refs_3_.refs_7_), channel_id=1, source_target_pairs={{0,3},{1,2},{2,1},{3,0},{4,7},{5,6},{6,5},{7,4},{8,11},{9,10},{10,... | collective-permute-start | bytes 466952 | tf_op jit(solution)/shard_map/ppermute | solution.py:69
  81.4 1.0 collective-permute-start.28
  82.4 1.5 %collective-permute-start.42 = (bf16[608,128]{1,0:T(8,128)(2,1)S(1)}, bf16[608,128]{1,0:T(8,128)(2,1)S(1)}, u32[]{:S(2)}, u32[]{:S(2)}) collective-permute-start(bf16[608,128]{1,0:T(8,128)(2,1)S(1)} %collective-permute-done.12.refs_12_), channel_id=1, source_target_pairs={{0,8},{4,12},{8,0},{12,4},{16,20},{20,16},{24,28},{28,24},{1,9},{5... | collective-permute-start | bytes 466952 | tf_op jit(solution)/shard_map/ppermute | solution.py:47
  84.0 2.1 %collective-permute-done.43.refs_15_ = bf16[608,128]{1,0:T(8,128)(2,1)S(1)} collective-permute-done((bf16[608,128]{1,0:T(8,128)(2,1)}, bf16[608,128]{1,0:T(8,128)(2,1)S(1)}, u32[]{:S(2)}, u32[]{:S(2)}) %collective-permute-start.43) | collective-permute-done | bytes 155680 | tf_op jit(solution)/shard_map/ppermute | solution.py:69
  86.0 1.5 %collective-permute-start.18 = (bf16[624,256]{1,0:T(8,128)(2,1)S(1)}, bf16[624,256]{1,0:T(8,128)(2,1)S(1)}, u32[]{:S(2)}, u32[]{:S(2)}) collective-permute-start(bf16[624,256]{1,0:T(8,128)(2,1)S(1)} %get-tuple-element.105), channel_id=1, source_target_pairs={{0,4},{4,0},{8,12},{12,8},{16,24},{20,28},{24,16},{28,20},{1,5},{5... | collective-permute-start | bytes 958472 | tf_op jit(solution)/shard_map/ppermute | solution.py:47
  87.5 1.8 %collective-permute-done.29 = bf16[608,128]{1,0:T(8,128)(2,1)S(1)} collective-permute-done((bf16[608,128]{1,0:T(8,128)(2,1)}, bf16[608,128]{1,0:T(8,128)(2,1)S(1)}, u32[]{:S(2)}, u32[]{:S(2)}) %collective-permute-start.29) | collective-permute-done | bytes 155680 | tf_op jit(solution)/shard_map/ppermute | solution.py:69
  89.3 1.5 %collective-permute-start.19 = (bf16[624,256]{1,0:T(8,128)(2,1)S(1)}, bf16[624,256]{1,0:T(8,128)(2,1)S(1)}, u32[]{:S(2)}, u32[]{:S(2)}) collective-permute-start(bf16[624,256]{1,0:T(8,128)(2,1)S(1)} %get-tuple-element.106), channel_id=1, source_target_pairs={{0,4},{4,0},{8,12},{12,8},{16,24},{20,28},{24,16},{28,20},{1,5},{5... | collective-permute-start | bytes 958472 | tf_op jit(solution)/shard_map/ppermute | solution.py:47
  90.8 4.5 %collective-permute-done.28 = bf16[608,128]{1,0:T(8,128)(2,1)S(1)} collective-permute-done((bf16[608,128]{1,0:T(8,128)(2,1)}, bf16[608,128]{1,0:T(8,128)(2,1)S(1)}, u32[]{:S(2)}, u32[]{:S(2)}) %collective-permute-start.28) | collective-permute-done | bytes 155680 | tf_op jit(solution)/shard_map/ppermute | solution.py:69
  95.4 1.5 %collective-permute-start.41 = (bf16[608,128]{1,0:T(8,128)(2,1)S(1)}, bf16[608,128]{1,0:T(8,128)(2,1)S(1)}, u32[]{:S(2)}, u32[]{:S(2)}) collective-permute-start(bf16[608,128]{1,0:T(8,128)(2,1)S(1)} %collective-permute-done.12.refs_12_), channel_id=1, source_target_pairs={{0,4},{4,0},{8,12},{12,8},{16,24},{20,28},{24,16},{28,20},{1,5},{5... | collective-permute-start | bytes 466952 | tf_op jit(solution)/shard_map/ppermute | solution.py:47
  101.3 1.5 %collective-permute-start.27 = (bf16[2,608,128]{2,1,0:T(8,128)(2,1)S(1)}, bf16[2,608,128]{2,1,0:T(8,128)(2,1)S(1)}, u32[]{:S(2)}, u32[]{:S(2)}) collective-permute-start(bf16[2,608,128]{2,1,0:T(8,128)(2,1)S(1)} %pad_maximum_fusion.refs_4_), channel_id=1, source_target_pairs={{0,8},{4,12},{8,0},{12,4},{16,20},{20,16},{24,28},{28,24},{1,9},{5... | collective-permute-start | bytes 933896 | tf_op jit(solution)/shard_map/ppermute | solution.py:47
  102.8 1.5 %collective-permute-start.26 = (bf16[2,608,128]{2,1,0:T(8,128)(2,1)S(1)}, bf16[2,608,128]{2,1,0:T(8,128)(2,1)S(1)}, u32[]{:S(2)}, u32[]{:S(2)}) collective-permute-start(bf16[2,608,128]{2,1,0:T(8,128)(2,1)S(1)} %pad_maximum_fusion.refs_4_), channel_id=1, source_target_pairs={{0,4},{4,0},{8,12},{12,8},{16,24},{20,28},{24,16},{28,20},{1,5},{5... | collective-permute-start | bytes 933896 | tf_op jit(solution)/shard_map/ppermute | solution.py:47
  107.7 0.7 copy-done.23
  109.0 1.8 %collective-permute-done.27.refs_6_ = bf16[2,608,128]{2,1,0:T(8,128)(2,1)S(1)} collective-permute-done((bf16[2,608,128]{2,1,0:T(8,128)(2,1)S(1)}, bf16[2,608,128]{2,1,0:T(8,128)(2,1)S(1)}, u32[]{:S(2)}, u32[]{:S(2)}) %collective-permute-start.27) | collective-permute-done | bytes 311328 | tf_op jit(solution)/shard_map/ppermute | solution.py:47
  111.0 1.9 %collective-permute-start.34 = (bf16[608,128]{1,0:T(8,128)(2,1)}, bf16[608,128]{1,0:T(8,128)(2,1)}, u32[]{:S(2)}, u32[]{:S(2)}) collective-permute-start(bf16[608,128]{1,0:T(8,128)(2,1)} %get-tuple-element.117.refs_0_), channel_id=1, source_target_pairs={{0,1},{1,0},{2,3},{3,2},{4,5},{5,4},{6,7},{7,6},{8,9},{9,8},{10,11... | collective-permute-start | bytes 466952 | tf_op jit(solution)/shard_map/ppermute | solution.py:69
  115.5 2.0 %collective-permute-start.23 = (bf16[608,128]{1,0:T(8,128)(2,1)}, bf16[608,128]{1,0:T(8,128)(2,1)}, u32[]{:S(2)}, u32[]{:S(2)}) collective-permute-start(bf16[608,128]{1,0:T(8,128)(2,1)} %get-tuple-element.117.refs_0_), channel_id=1, source_target_pairs={{0,3},{1,2},{2,1},{3,0},{4,7},{5,6},{6,5},{7,4},{8,11},{9,10},{10,... | collective-permute-start | bytes 466952 | tf_op jit(solution)/shard_map/ppermute | solution.py:69
  118.3 0.9 copy-done.10
  119.2 0.9 copy-done.13
  120.2 2.3 %residual_rows.1 = f32[608,128]{1,0:T(8,128)S(1)} custom-call(s32[9]{0:T(128)S(1)} %pad_add_fusion.order, bf16[608,2432]{1,0:T(8,128)(2,1)S(1)} %copy-done, bf16[608,128]{1,0:T(8,128)(2,1)S(1)} %slice_select_fusion.refs_0_.refs_4_, bf16[608,128]{1,0:T(8,128)(2,1)S(1)} %copy-done.13, bf16[608,128]{1,0:T(8,128)(2,1)S(1)} %copy-done.10, ...), custom_call_target="tpu_custom_call" | custom-call | flops 378535936 | bytes 4202496 | tf_op jit(solution)/shard_map/residual_rows/pallas_call | solution.py:482
  123.2 1.4 collective-permute-done.23.refs_1_
  124.6 6.9 %collective-permute-done.22.refs_0_ = bf16[608,128]{1,0:T(8,128)(2,1)} collective-permute-done((bf16[608,128]{1,0:T(8,128)(2,1)}, bf16[608,128]{1,0:T(8,128)(2,1)}, u32[]{:S(2)}, u32[]{:S(2)}) %collective-permute-start.22) | collective-permute-done | bytes 155680 | tf_op jit(solution)/shard_map/ppermute | solution.py:69
  132.4 3.9 %zero_projection_grad_first.1.refs_12_ = f32[608,2432]{1,0:T(8,128)S(1)} custom-call(s32[9]{0:T(128)S(1)} %pad_add_fusion.order, s32[4]{0:T(128)S(1)} %iota_xor_fusion.dp_order, bf16[608,128]{1,0:T(8,128)(2,1)} %get-tuple-element.117.refs_0_, bf16[608,128]{1,0:T(8,128)(2,1)} %collective-permute-done.34.refs_1_, ...), custom_call_target="tpu_custom_call" | custom-call | flops 1514143744 | bytes 9027584 | tf_op jit(solution)/shard_map/zero_projection_grad_first/pallas_call | solution.py:562
  136.3 1.6 %collective-permute-start.21 = (bf16[624,256]{1,0:T(8,128)(2,1)S(1)}, bf16[624,256]{1,0:T(8,128)(2,1)S(1)}, u32[]{:S(2)}, u32[]{:S(2)}) collective-permute-start(bf16[624,256]{1,0:T(8,128)(2,1)S(1)} %get-tuple-element.115), channel_id=1, source_target_pairs={{0,8},{4,12},{8,0},{12,4},{16,20},{20,16},{24,28},{28,24},{1,9},{5... | collective-permute-start | bytes 958472 | tf_op jit(solution)/shard_map/ppermute | solution.py:47
  138.0 5.1 %zero_projection_grad_last.1 = f32[608,2432]{1,0:T(8,128)} custom-call(s32[9]{0:T(128)S(1)} %pad_add_fusion.order, s32[4]{0:T(128)S(1)} %iota_xor_fusion.dp_order, bf16[608,128]{1,0:T(8,128)(2,1)} %collective-permute-done.22.refs_0_, bf16[608,128]{1,0:T(8,128)(2,1)} %collective-permute-done.23.refs_1_, bf16[608,128]{1,0:T(8,128)(2,1)S(1)} %collective-permute-done.24.refs_2_, ...), custom_call_target="tpu_custom_call" | custom-call | flops 1514143744 | bytes 9027584 | tf_op jit(solution)/shard_map/zero_projection_grad_last/pallas_call | solution.py:562
  143.1 0.8 fusion.8
  144.0 2.3 %fusion.5 = f32[1,608,256]{2,1,0:T(8,128)} fusion(f32[608,256]{1,0:T(8,128)S(1)} %get-tuple-element.114, f32[608,128]{1,0:T(8,128)} %collective-permute-done.4, f32[608,128]{1,0:T(8,128)} %add_add_fusion, bf16[624,256]{1,0:T(8,128)(2,1)S(1)} %collective-permute-done.21, f32[256]{0:T(256)S(1)} %bitcast.28, f32[256]{0:T(256)S(1)} %bitcast.30, ...), kind=kLoop, calls=%fused_computation.7 | loop fusion | flops 2179072 | bytes 2808197 | tf_op jit(solution)/shard_map/broadcast_in_dim | solution.py:664
  (186 shorter events, 18.0 us)
Async XLA Ops:
  0.6 2.0 %collective-permute-start = (bf16[608,256]{1,0:T(8,128)(2,1)}, bf16[608,256]{1,0:T(8,128)(2,1)S(1)}, u32[]{:S(2)}, u32[]{:S(2)}) collective-permute-start(bf16[608,256]{1,0:T(8,128)(2,1)} %bitcast.21), channel_id=1, source_target_pairs={{0,16},{16,0},{1,17},{17,1},{2,18},{18,2},{3,19},{19,3},{4,20},{20... | collective-permute-start | bytes 933896 | tf_op jit(solution)/shard_map/ppermute | solution.py:35
  7.6 11.8 %collective-permute-start.1 = (bf16[608,128]{1,0:T(8,128)(2,1)S(1)}, bf16[608,128]{1,0:T(8,128)(2,1)S(1)}, u32[]{:S(2)}, u32[]{:S(2)}) collective-permute-start(bf16[608,128]{1,0:T(8,128)(2,1)S(1)} %get-tuple-element.63), channel_id=1, source_target_pairs={{0,4},{4,0},{8,12},{12,8},{16,24},{20,28},{24,16},{28,20},{1,5},{5... | collective-permute-start | bytes 466952 | tf_op jit(solution)/shard_map/ppermute | solution.py:63
  10.5 9.0 %collective-permute-start.2 = (bf16[608,128]{1,0:T(8,128)(2,1)S(1)}, bf16[608,128]{1,0:T(8,128)(2,1)S(1)}, u32[]{:S(2)}, u32[]{:S(2)}) collective-permute-start(bf16[608,128]{1,0:T(8,128)(2,1)S(1)} %get-tuple-element.64), channel_id=1, source_target_pairs={{0,8},{4,12},{8,0},{12,4},{16,20},{20,16},{24,28},{28,24},{1,9},{5... | collective-permute-start | bytes 466952 | tf_op jit(solution)/shard_map/ppermute | solution.py:63
  12.0 7.5 %collective-permute-start.3 = (bf16[608,128]{1,0:T(8,128)(2,1)S(1)}, bf16[608,128]{1,0:T(8,128)(2,1)S(1)}, u32[]{:S(2)}, u32[]{:S(2)}) collective-permute-start(bf16[608,128]{1,0:T(8,128)(2,1)S(1)} %get-tuple-element.65), channel_id=1, source_target_pairs={{0,12},{4,8},{8,4},{12,0},{16,28},{20,24},{24,20},{28,16},{1,13},{... | collective-permute-start | bytes 466952 | tf_op jit(solution)/shard_map/ppermute | solution.py:63
  20.4 1.9 %collective-permute-start.4 = (f32[608,128]{1,0:T(8,128)}, f32[608,128]{1,0:T(8,128)}, u32[]{:S(2)}, u32[]{:S(2)}) collective-permute-start(f32[608,128]{1,0:T(8,128)} %add_add_fusion), channel_id=1, source_target_pairs={{0,16},{16,0},{1,17},{17,1},{2,18},{18,2},{3,19},{19,3},{4,20},{20... | collective-permute-start | bytes 933896 | tf_op jit(solution)/shard_map/ppermute | solution.py:35
  23.7 18.4 %collective-permute-start.10 = (bf16[608,256]{1,0:T(8,128)(2,1)S(1)}, bf16[608,256]{1,0:T(8,128)(2,1)S(1)}, u32[]{:S(2)}, u32[]{:S(2)}) collective-permute-start(bf16[608,256]{1,0:T(8,128)(2,1)S(1)} %multiply_convert_fusion.refs_0_), channel_id=1, source_target_pairs={{0,12},{4,8},{8,4},{12,0},{16,28},{20,24},{24,20},{28,16},{1,13},{... | collective-permute-start | bytes 933896 | tf_op jit(solution)/shard_map/ppermute | solution.py:63
  26.7 15.6 %collective-permute-start.9 = (bf16[608,256]{1,0:T(8,128)(2,1)S(1)}, bf16[608,256]{1,0:T(8,128)(2,1)S(1)}, u32[]{:S(2)}, u32[]{:S(2)}) collective-permute-start(bf16[608,256]{1,0:T(8,128)(2,1)S(1)} %multiply_convert_fusion.refs_0_), channel_id=1, source_target_pairs={{0,8},{4,12},{8,0},{12,4},{16,20},{20,16},{24,28},{28,24},{1,9},{5... | collective-permute-start | bytes 933896 | tf_op jit(solution)/shard_map/ppermute | solution.py:63
  27.2 15.1 %collective-permute-start.8 = (bf16[608,256]{1,0:T(8,128)(2,1)S(1)}, bf16[608,256]{1,0:T(8,128)(2,1)S(1)}, u32[]{:S(2)}, u32[]{:S(2)}) collective-permute-start(bf16[608,256]{1,0:T(8,128)(2,1)S(1)} %multiply_convert_fusion.refs_0_), channel_id=1, source_target_pairs={{0,4},{4,0},{8,12},{12,8},{16,24},{20,28},{24,16},{28,20},{1,5},{5... | collective-permute-start | bytes 933896 | tf_op jit(solution)/shard_map/ppermute | solution.py:63
  38.7 16.3 %collective-permute-start.5 = (bf16[608,256]{1,0:T(8,128)(2,1)S(1)}, bf16[608,256]{1,0:T(8,128)(2,1)S(1)}, u32[]{:S(2)}, u32[]{:S(2)}) collective-permute-start(bf16[608,256]{1,0:T(8,128)(2,1)S(1)} %get-tuple-element.76), channel_id=1, source_target_pairs={{0,4},{4,0},{8,12},{12,8},{16,24},{20,28},{24,16},{28,20},{1,5},{5... | collective-permute-start | bytes 933896 | tf_op jit(solution)/shard_map/ppermute | solution.py:63
  40.6 14.4 %collective-permute-start.6 = (bf16[608,256]{1,0:T(8,128)(2,1)S(1)}, bf16[608,256]{1,0:T(8,128)(2,1)S(1)}, u32[]{:S(2)}, u32[]{:S(2)}) collective-permute-start(bf16[608,256]{1,0:T(8,128)(2,1)S(1)} %get-tuple-element.77), channel_id=1, source_target_pairs={{0,8},{4,12},{8,0},{12,4},{16,20},{20,16},{24,28},{28,24},{1,9},{5... | collective-permute-start | bytes 933896 | tf_op jit(solution)/shard_map/ppermute | solution.py:63
  42.1 13.3 %collective-permute-start.7 = (bf16[608,256]{1,0:T(8,128)(2,1)S(1)}, bf16[608,256]{1,0:T(8,128)(2,1)S(1)}, u32[]{:S(2)}, u32[]{:S(2)}) collective-permute-start(bf16[608,256]{1,0:T(8,128)(2,1)S(1)} %get-tuple-element.78), channel_id=1, source_target_pairs={{0,12},{4,8},{8,4},{12,0},{16,28},{20,24},{24,20},{28,16},{1,13},{... | collective-permute-start | bytes 933896 | tf_op jit(solution)/shard_map/ppermute | solution.py:63
  57.6 1.4 collective-permute-start.11
  59.0 7.9 %collective-permute-start.17 = (bf16[608,128]{1,0:T(8,128)(2,1)S(1)}, bf16[608,128]{1,0:T(8,128)(2,1)}, u32[]{:S(2)}, u32[]{:S(2)}) collective-permute-start(bf16[608,128]{1,0:T(8,128)(2,1)S(1)} %slice_select_fusion.refs_0_.refs_4_), channel_id=1, source_target_pairs={{0,12},{4,8},{8,4},{12,0},{16,28},{20,24},{24,20},{28,16},{1,13},{... | collective-permute-start | bytes 466952 | tf_op jit(solution)/shard_map/ppermute | solution.py:63
  61.7 15.2 %collective-permute-start.16 = (bf16[608,128]{1,0:T(8,128)(2,1)S(1)}, bf16[608,128]{1,0:T(8,128)(2,1)S(1)}, u32[]{:S(2)}, u32[]{:S(2)}) collective-permute-start(bf16[608,128]{1,0:T(8,128)(2,1)S(1)} %slice_select_fusion.refs_0_.refs_4_), channel_id=1, source_target_pairs={{0,8},{4,12},{8,0},{12,4},{16,20},{20,16},{24,28},{28,24},{1,9},{5... | collective-permute-start | bytes 466952 | tf_op jit(solution)/shard_map/ppermute | solution.py:63
  62.2 14.7 %collective-permute-start.15 = (bf16[608,128]{1,0:T(8,128)(2,1)S(1)}, bf16[608,128]{1,0:T(8,128)(2,1)S(1)}, u32[]{:S(2)}, u32[]{:S(2)}) collective-permute-start(bf16[608,128]{1,0:T(8,128)(2,1)S(1)} %slice_select_fusion.refs_0_.refs_4_), channel_id=1, source_target_pairs={{0,4},{4,0},{8,12},{12,8},{16,24},{20,28},{24,16},{28,20},{1,5},{5... | collective-permute-start | bytes 466952 | tf_op jit(solution)/shard_map/ppermute | solution.py:63
  62.6 14.3 %collective-permute-start.14 = (bf16[608,128]{1,0:T(8,128)(2,1)S(1)}, bf16[608,128]{1,0:T(8,128)(2,1)S(1)}, u32[]{:S(2)}, u32[]{:S(2)}) collective-permute-start(bf16[608,128]{1,0:T(8,128)(2,1)S(1)} %slice_select_fusion.refs_0_.refs_4_), channel_id=1, source_target_pairs={{0,3},{1,2},{2,1},{3,0},{4,7},{5,6},{6,5},{7,4},{8,11},{9,10},{10,... | collective-permute-start | bytes 466952 | tf_op jit(solution)/shard_map/ppermute | solution.py:69
  66.3 12.6 %collective-permute-start.13 = (bf16[608,128]{1,0:T(8,128)(2,1)S(1)}, bf16[608,128]{1,0:T(8,128)(2,1)S(1)}, u32[]{:S(2)}, u32[]{:S(2)}) collective-permute-start(bf16[608,128]{1,0:T(8,128)(2,1)S(1)} %slice_select_fusion.refs_0_.refs_4_), channel_id=1, source_target_pairs={{0,2},{1,3},{2,0},{3,1},{4,6},{5,7},{6,4},{7,5},{8,10},{9,11},{10,... | collective-permute-start | bytes 466952 | tf_op jit(solution)/shard_map/ppermute | solution.py:69
  67.0 12.0 %collective-permute-start.12 = (bf16[608,128]{1,0:T(8,128)(2,1)S(1)}, bf16[608,128]{1,0:T(8,128)(2,1)S(1)}, u32[]{:S(2)}, u32[]{:S(2)}) collective-permute-start(bf16[608,128]{1,0:T(8,128)(2,1)S(1)} %slice_select_fusion.refs_0_.refs_4_), channel_id=1, source_target_pairs={{0,1},{1,0},{2,3},{3,2},{4,5},{5,4},{6,7},{7,6},{8,9},{9,8},{10,11... | collective-permute-start | bytes 466952 | tf_op jit(solution)/shard_map/ppermute | solution.py:69
  78.9 7.1 %collective-permute-start.43 = (bf16[608,128]{1,0:T(8,128)(2,1)}, bf16[608,128]{1,0:T(8,128)(2,1)S(1)}, u32[]{:S(2)}, u32[]{:S(2)}) collective-permute-start(bf16[608,128]{1,0:T(8,128)(2,1)} %collective-permute-done.17.refs_3_.refs_7_), channel_id=1, source_target_pairs={{0,1},{1,0},{2,3},{3,2},{4,5},{5,4},{6,7},{7,6},{8,9},{9,8},{10,11... | collective-permute-start | bytes 466952 | tf_op jit(solution)/shard_map/ppermute | solution.py:69
  78.9 10.4 %collective-permute-start.29 = (bf16[608,128]{1,0:T(8,128)(2,1)}, bf16[608,128]{1,0:T(8,128)(2,1)S(1)}, u32[]{:S(2)}, u32[]{:S(2)}) collective-permute-start(bf16[608,128]{1,0:T(8,128)(2,1)} %collective-permute-done.17.refs_3_.refs_7_), channel_id=1, source_target_pairs={{0,3},{1,2},{2,1},{3,0},{4,7},{5,6},{6,5},{7,4},{8,11},{9,10},{10,... | collective-permute-start | bytes 466952 | tf_op jit(solution)/shard_map/ppermute | solution.py:69
  81.4 13.9 %collective-permute-start.28 = (bf16[608,128]{1,0:T(8,128)(2,1)}, bf16[608,128]{1,0:T(8,128)(2,1)S(1)}, u32[]{:S(2)}, u32[]{:S(2)}) collective-permute-start(bf16[608,128]{1,0:T(8,128)(2,1)} %collective-permute-done.17.refs_3_.refs_7_), channel_id=1, source_target_pairs={{0,2},{1,3},{2,0},{3,1},{4,6},{5,7},{6,4},{7,5},{8,10},{9,11},{10,... | collective-permute-start | bytes 466952 | tf_op jit(solution)/shard_map/ppermute | solution.py:69
  82.4 15.1 %collective-permute-start.44 = (bf16[608,128]{1,0:T(8,128)(2,1)S(1)}, bf16[608,128]{1,0:T(8,128)(2,1)S(1)}, u32[]{:S(2)}, u32[]{:S(2)}) collective-permute-start(bf16[608,128]{1,0:T(8,128)(2,1)S(1)} %collective-permute-done.12.refs_12_), channel_id=1, source_target_pairs={{0,16},{16,0},{1,17},{17,1},{2,18},{18,2},{3,19},{19,3},{4,20},{20... | collective-permute-start | bytes 466952 | tf_op jit(solution)/shard_map/ppermute | solution.py:35
  82.4 16.5 %collective-permute-start.42 = (bf16[608,128]{1,0:T(8,128)(2,1)S(1)}, bf16[608,128]{1,0:T(8,128)(2,1)S(1)}, u32[]{:S(2)}, u32[]{:S(2)}) collective-permute-start(bf16[608,128]{1,0:T(8,128)(2,1)S(1)} %collective-permute-done.12.refs_12_), channel_id=1, source_target_pairs={{0,8},{4,12},{8,0},{12,4},{16,20},{20,16},{24,28},{28,24},{1,9},{5... | collective-permute-start | bytes 466952 | tf_op jit(solution)/shard_map/ppermute | solution.py:47
  86.0 18.3 %collective-permute-start.18 = (bf16[624,256]{1,0:T(8,128)(2,1)S(1)}, bf16[624,256]{1,0:T(8,128)(2,1)S(1)}, u32[]{:S(2)}, u32[]{:S(2)}) collective-permute-start(bf16[624,256]{1,0:T(8,128)(2,1)S(1)} %get-tuple-element.105), channel_id=1, source_target_pairs={{0,4},{4,0},{8,12},{12,8},{16,24},{20,28},{24,16},{28,20},{1,5},{5... | collective-permute-start | bytes 958472 | tf_op jit(solution)/shard_map/ppermute | solution.py:47
  89.3 15.8 %collective-permute-start.19 = (bf16[624,256]{1,0:T(8,128)(2,1)S(1)}, bf16[624,256]{1,0:T(8,128)(2,1)S(1)}, u32[]{:S(2)}, u32[]{:S(2)}) collective-permute-start(bf16[624,256]{1,0:T(8,128)(2,1)S(1)} %get-tuple-element.106), channel_id=1, source_target_pairs={{0,4},{4,0},{8,12},{12,8},{16,24},{20,28},{24,16},{28,20},{1,5},{5... | collective-permute-start | bytes 958472 | tf_op jit(solution)/shard_map/ppermute | solution.py:47
  95.4 5.2 %collective-permute-start.41 = (bf16[608,128]{1,0:T(8,128)(2,1)S(1)}, bf16[608,128]{1,0:T(8,128)(2,1)S(1)}, u32[]{:S(2)}, u32[]{:S(2)}) collective-permute-start(bf16[608,128]{1,0:T(8,128)(2,1)S(1)} %collective-permute-done.12.refs_12_), channel_id=1, source_target_pairs={{0,4},{4,0},{8,12},{12,8},{16,24},{20,28},{24,16},{28,20},{1,5},{5... | collective-permute-start | bytes 466952 | tf_op jit(solution)/shard_map/ppermute | solution.py:47
  98.2 2.4 %collective-permute-start.47 = (bf16[608,128]{1,0:T(8,128)(2,1)S(1)}, bf16[608,128]{1,0:T(8,128)(2,1)S(1)}, u32[]{:S(2)}, u32[]{:S(2)}) collective-permute-start(bf16[608,128]{1,0:T(8,128)(2,1)S(1)} %collective-permute-done.43.refs_15_), channel_id=1, source_target_pairs={{0,16},{16,0},{1,17},{17,1},{2,18},{18,2},{3,19},{19,3},{4,20},{20... | collective-permute-start | bytes 466952 | tf_op jit(solution)/shard_map/ppermute | solution.py:35
  98.9 3.9 %collective-permute-start.46 = (bf16[608,128]{1,0:T(8,128)(2,1)S(1)}, bf16[608,128]{1,0:T(8,128)(2,1)S(1)}, u32[]{:S(2)}, u32[]{:S(2)}) collective-permute-start(bf16[608,128]{1,0:T(8,128)(2,1)S(1)} %collective-permute-done.42.refs_14_), channel_id=1, source_target_pairs={{0,16},{16,0},{1,17},{17,1},{2,18},{18,2},{3,19},{19,3},{4,20},{20... | collective-permute-start | bytes 466952 | tf_op jit(solution)/shard_map/ppermute | solution.py:35
  100.6 7.1 %collective-permute-start.30 = (bf16[2,608,128]{2,1,0:T(8,128)(2,1)S(1)}, bf16[2,608,128]{2,1,0:T(8,128)(2,1)S(1)}, u32[]{:S(2)}, u32[]{:S(2)}) collective-permute-start(bf16[2,608,128]{2,1,0:T(8,128)(2,1)S(1)} %pad_maximum_fusion.refs_4_), channel_id=1, source_target_pairs={{0,16},{16,0},{1,17},{17,1},{2,18},{18,2},{3,19},{19,3},{4,20},{20... | collective-permute-start | bytes 933896 | tf_op jit(solution)/shard_map/ppermute | solution.py:35
  101.3 9.5 %collective-permute-start.27 = (bf16[2,608,128]{2,1,0:T(8,128)(2,1)S(1)}, bf16[2,608,128]{2,1,0:T(8,128)(2,1)S(1)}, u32[]{:S(2)}, u32[]{:S(2)}) collective-permute-start(bf16[2,608,128]{2,1,0:T(8,128)(2,1)S(1)} %pad_maximum_fusion.refs_4_), channel_id=1, source_target_pairs={{0,8},{4,12},{8,0},{12,4},{16,20},{20,16},{24,28},{28,24},{1,9},{5... | collective-permute-start | bytes 933896 | tf_op jit(solution)/shard_map/ppermute | solution.py:47
  102.8 8.2 %collective-permute-start.26 = (bf16[2,608,128]{2,1,0:T(8,128)(2,1)S(1)}, bf16[2,608,128]{2,1,0:T(8,128)(2,1)S(1)}, u32[]{:S(2)}, u32[]{:S(2)}) collective-permute-start(bf16[2,608,128]{2,1,0:T(8,128)(2,1)S(1)} %pad_maximum_fusion.refs_4_), channel_id=1, source_target_pairs={{0,4},{4,0},{8,12},{12,8},{16,24},{20,28},{24,16},{28,20},{1,5},{5... | collective-permute-start | bytes 933896 | tf_op jit(solution)/shard_map/ppermute | solution.py:47
  105.1 2.0 %collective-permute-start.45 = (bf16[608,128]{1,0:T(8,128)(2,1)S(1)}, bf16[608,128]{1,0:T(8,128)(2,1)S(1)}, u32[]{:S(2)}, u32[]{:S(2)}) collective-permute-start(bf16[608,128]{1,0:T(8,128)(2,1)S(1)} %collective-permute-done.41.refs_13_), channel_id=1, source_target_pairs={{0,16},{16,0},{1,17},{17,1},{2,18},{18,2},{3,19},{19,3},{4,20},{20... | collective-permute-start | bytes 466952 | tf_op jit(solution)/shard_map/ppermute | solution.py:35
  105.8 7.1 %collective-permute-start.33 = (bf16[2,608,128]{2,1,0:T(8,128)(2,1)S(1)}, bf16[2,608,128]{2,1,0:T(8,128)(2,1)S(1)}, u32[]{:S(2)}, u32[]{:S(2)}) collective-permute-start(bf16[2,608,128]{2,1,0:T(8,128)(2,1)S(1)} %pad_maximum_fusion.1.refs_7_), channel_id=1, source_target_pairs={{0,16},{16,0},{1,17},{17,1},{2,18},{18,2},{3,19},{19,3},{4,20},{20... | collective-permute-start | bytes 933896 | tf_op jit(solution)/shard_map/ppermute | solution.py:35
  107.7 5.9 %collective-permute-start.37 = (bf16[608,128]{1,0:T(8,128)(2,1)S(1)}, bf16[608,128]{1,0:T(8,128)(2,1)S(1)}, u32[]{:S(2)}, u32[]{:S(2)}) collective-permute-start(bf16[608,128]{1,0:T(8,128)(2,1)S(1)} %slice_select_fusion.refs_0_.refs_4_), channel_id=1, source_target_pairs={{0,16},{16,0},{1,17},{17,1},{2,18},{18,2},{3,19},{19,3},{4,20},{20... | collective-permute-start | bytes 466952 | tf_op jit(solution)/shard_map/ppermute | solution.py:35
  108.5 6.3 %collective-permute-start.38 = (bf16[608,128]{1,0:T(8,128)(2,1)S(1)}, bf16[608,128]{1,0:T(8,128)(2,1)S(1)}, u32[]{:S(2)}, u32[]{:S(2)}) collective-permute-start(bf16[608,128]{1,0:T(8,128)(2,1)S(1)} %collective-permute-done.15.refs_1_.refs_5_), channel_id=1, source_target_pairs={{0,16},{16,0},{1,17},{17,1},{2,18},{18,2},{3,19},{19,3},{4,20},{20... | collective-permute-start | bytes 466952 | tf_op jit(solution)/shard_map/ppermute | solution.py:35
  110.8 6.7 %collective-permute-start.39 = (bf16[608,128]{1,0:T(8,128)(2,1)S(1)}, bf16[608,128]{1,0:T(8,128)(2,1)S(1)}, u32[]{:S(2)}, u32[]{:S(2)}) collective-permute-start(bf16[608,128]{1,0:T(8,128)(2,1)S(1)} %collective-permute-done.16.refs_2_.refs_6_), channel_id=1, source_target_pairs={{0,16},{16,0},{1,17},{17,1},{2,18},{18,2},{3,19},{19,3},{4,20},{20... | collective-permute-start | bytes 466952 | tf_op jit(solution)/shard_map/ppermute | solution.py:35
  111.0 7.1 %collective-permute-start.34 = (bf16[608,128]{1,0:T(8,128)(2,1)}, bf16[608,128]{1,0:T(8,128)(2,1)}, u32[]{:S(2)}, u32[]{:S(2)}) collective-permute-start(bf16[608,128]{1,0:T(8,128)(2,1)} %get-tuple-element.117.refs_0_), channel_id=1, source_target_pairs={{0,1},{1,0},{2,3},{3,2},{4,5},{5,4},{6,7},{7,6},{8,9},{9,8},{10,11... | collective-permute-start | bytes 466952 | tf_op jit(solution)/shard_map/ppermute | solution.py:69
  113.6 8.9 %collective-permute-start.40 = (bf16[608,128]{1,0:T(8,128)(2,1)}, bf16[608,128]{1,0:T(8,128)(2,1)}, u32[]{:S(2)}, u32[]{:S(2)}) collective-permute-start(bf16[608,128]{1,0:T(8,128)(2,1)} %collective-permute-done.17.refs_3_.refs_7_), channel_id=1, source_target_pairs={{0,16},{16,0},{1,17},{17,1},{2,18},{18,2},{3,19},{19,3},{4,20},{20... | collective-permute-start | bytes 466952 | tf_op jit(solution)/shard_map/ppermute | solution.py:35
  114.3 8.8 %collective-permute-start.35 = (bf16[608,128]{1,0:T(8,128)(2,1)}, bf16[608,128]{1,0:T(8,128)(2,1)}, u32[]{:S(2)}, u32[]{:S(2)}) collective-permute-start(bf16[608,128]{1,0:T(8,128)(2,1)} %get-tuple-element.117.refs_0_), channel_id=1, source_target_pairs={{0,16},{16,0},{1,17},{17,1},{2,18},{18,2},{3,19},{19,3},{4,20},{20... | collective-permute-start | bytes 466952 | tf_op jit(solution)/shard_map/ppermute | solution.py:35
  115.5 9.1 %collective-permute-start.23 = (bf16[608,128]{1,0:T(8,128)(2,1)}, bf16[608,128]{1,0:T(8,128)(2,1)}, u32[]{:S(2)}, u32[]{:S(2)}) collective-permute-start(bf16[608,128]{1,0:T(8,128)(2,1)} %get-tuple-element.117.refs_0_), channel_id=1, source_target_pairs={{0,3},{1,2},{2,1},{3,0},{4,7},{5,6},{6,5},{7,4},{8,11},{9,10},{10,... | collective-permute-start | bytes 466952 | tf_op jit(solution)/shard_map/ppermute | solution.py:69
  118.1 13.4 %collective-permute-start.22 = (bf16[608,128]{1,0:T(8,128)(2,1)}, bf16[608,128]{1,0:T(8,128)(2,1)}, u32[]{:S(2)}, u32[]{:S(2)}) collective-permute-start(bf16[608,128]{1,0:T(8,128)(2,1)} %get-tuple-element.117.refs_0_), channel_id=1, source_target_pairs={{0,2},{1,3},{2,0},{3,1},{4,6},{5,7},{6,4},{7,5},{8,10},{9,11},{10,... | collective-permute-start | bytes 466952 | tf_op jit(solution)/shard_map/ppermute | solution.py:69
  118.2 13.3 %collective-permute-start.36 = (bf16[608,128]{1,0:T(8,128)(2,1)}, bf16[608,128]{1,0:T(8,128)(2,1)}, u32[]{:S(2)}, u32[]{:S(2)}) collective-permute-start(bf16[608,128]{1,0:T(8,128)(2,1)} %collective-permute-done.34.refs_1_), channel_id=1, source_target_pairs={{0,16},{16,0},{1,17},{17,1},{2,18},{18,2},{3,19},{19,3},{4,20},{20... | collective-permute-start | bytes 466952 | tf_op jit(solution)/shard_map/ppermute | solution.py:35
  122.6 13.7 %collective-permute-start.32 = (bf16[2,608,128]{2,1,0:T(8,128)(2,1)S(1)}, bf16[2,608,128]{2,1,0:T(8,128)(2,1)S(1)}, u32[]{:S(2)}, u32[]{:S(2)}) collective-permute-start(bf16[2,608,128]{2,1,0:T(8,128)(2,1)S(1)} %copy-done.26), channel_id=1, source_target_pairs={{0,16},{16,0},{1,17},{17,1},{2,18},{18,2},{3,19},{19,3},{4,20},{20... | collective-permute-start | bytes 933896 | tf_op jit(solution)/shard_map/ppermute | solution.py:35
  123.1 14.8 %collective-permute-start.31 = (bf16[2,608,128]{2,1,0:T(8,128)(2,1)S(1)}, bf16[2,608,128]{2,1,0:T(8,128)(2,1)S(1)}, u32[]{:S(2)}, u32[]{:S(2)}) collective-permute-start(bf16[2,608,128]{2,1,0:T(8,128)(2,1)S(1)} %copy-done.28), channel_id=1, source_target_pairs={{0,16},{16,0},{1,17},{17,1},{2,18},{18,2},{3,19},{19,3},{4,20},{20... | collective-permute-start | bytes 933896 | tf_op jit(solution)/shard_map/ppermute | solution.py:35
  124.6 18.5 %collective-permute-start.20 = (f32[608,128]{1,0:T(8,128)S(1)}, f32[608,128]{1,0:T(8,128)S(1)}, u32[]{:S(2)}, u32[]{:S(2)}) collective-permute-start(f32[608,128]{1,0:T(8,128)S(1)} %residual_rows.1), channel_id=1, source_target_pairs={{0,16},{16,0},{1,17},{17,1},{2,18},{18,2},{3,19},{19,3},{4,20},{20... | collective-permute-start | bytes 933896 | tf_op jit(solution)/shard_map/ppermute | solution.py:35
  131.5 6.4 %collective-permute-start.25 = (bf16[608,128]{1,0:T(8,128)(2,1)}, bf16[608,128]{1,0:T(8,128)(2,1)S(1)}, u32[]{:S(2)}, u32[]{:S(2)}) collective-permute-start(bf16[608,128]{1,0:T(8,128)(2,1)} %collective-permute-done.23.refs_1_), channel_id=1, source_target_pairs={{0,16},{16,0},{1,17},{17,1},{2,18},{18,2},{3,19},{19,3},{4,20},{20... | collective-permute-start | bytes 466952 | tf_op jit(solution)/shard_map/ppermute | solution.py:35
  131.5 6.4 %collective-permute-start.24 = (bf16[608,128]{1,0:T(8,128)(2,1)}, bf16[608,128]{1,0:T(8,128)(2,1)S(1)}, u32[]{:S(2)}, u32[]{:S(2)}) collective-permute-start(bf16[608,128]{1,0:T(8,128)(2,1)} %collective-permute-done.22.refs_0_), channel_id=1, source_target_pairs={{0,16},{16,0},{1,17},{17,1},{2,18},{18,2},{3,19},{19,3},{4,20},{20... | collective-permute-start | bytes 466952 | tf_op jit(solution)/shard_map/ppermute | solution.py:35
  136.3 7.6 %collective-permute-start.21 = (bf16[624,256]{1,0:T(8,128)(2,1)S(1)}, bf16[624,256]{1,0:T(8,128)(2,1)S(1)}, u32[]{:S(2)}, u32[]{:S(2)}) collective-permute-start(bf16[624,256]{1,0:T(8,128)(2,1)S(1)} %get-tuple-element.115), channel_id=1, source_target_pairs={{0,8},{4,12},{8,0},{12,4},{16,20},{20,16},{24,28},{28,24},{1,9},{5... | collective-permute-start | bytes 958472 | tf_op jit(solution)/shard_map/ppermute | solution.py:47
  (56 other events, 502.9 us)

commit v9 on v7

--- a/solution.py
+++ b/solution.py
@@ -15,6 +15,7 @@
 F32, BF16 = jnp.float32, jnp.bfloat16
 WHOLE = pl.BlockSpec(memory_space=pltpu.VMEM)
 HELD = pl.BlockSpec(memory_space=pltpu.HBM)
+ANYWHERE = pl.BlockSpec(memory_space=pl.ANY)
 SCALARS = pl.BlockSpec(memory_space=pltpu.SMEM)
 
 
@@ -428,7 +429,7 @@
 
 
 def prepare_kernel(blocks, order, acts, modulation, own, arrived, weight, *refs):
-    outs, (normed, stats, cot0, cot1, full, buf, sem) = refs[:blocks], refs[blocks:]
+    outs, (normed, stats, cot0, cot1_rows, full, buf, sem) = refs[:blocks], refs[blocks:]
     load = pltpu.make_async_copy(weight, buf, sem)
     load.start()
     group = order[blocks]
@@ -437,7 +438,7 @@
     lanes = pl.ds(pl.multiple_of(group * half, half), half)
     cot0[...] = jnp.where(control, own[:, lanes], arrived[:, lanes])
     mine = jnp.where(control, arrived[:, lanes], own[:, lanes])
-    cot1[...] = mine
+    cot1_rows[...] = jnp.where(control, arrived[...], own[...])
     normalize(acts, modulation, normed, stats)
     load.wait()
     full[...] = lax.dot_general(mine, buf[...], (((0,), (0,)), ((), ())), preferred_element_type=F32).T
@@ -455,7 +456,7 @@
             struct((tokens, features), BF16),
             struct((2, tokens), F32),
             struct((rows, half), BF16),
-            struct((rows, half), BF16),
+            struct((rows, tokens), BF16),
         ],
         in_specs=[SCALARS] + [WHOLE] * 4 + [HELD],
         out_specs=[WHOLE] * (blocks + 4),
@@ -472,13 +473,13 @@
 
 def residual_kernel(order, weight, *refs):
     stack, (result, full, stage) = refs[:-3], refs[-3:]
-    values = [lambda value=value: value[...] for value in stack]
-    place_blocks(full, slice(None), stage, order, values, stack[0].shape[0])
+    values = [lambda value=value: value[0] for value in stack]
+    place_blocks(full, slice(None), stage, order, values, stack[0].shape[1])
     result[...] = jnp.dot(weight[...], full[...], preferred_element_type=F32)
 
 
 def residual_rows(order, weight, stack):
-    blocks, (rows, half) = len(stack), stack[0].shape
+    blocks, (_, rows, half) = len(stack), stack[0].shape
     return pl.pallas_call(
         residual_kernel,
         out_shape=struct((rows, half), F32),
@@ -491,27 +492,24 @@
 
 
 def zero_grad_kernel(blocks, first, count, order, dp_order, *refs):
-    cots, refs = (refs[:count], refs[count : 2 * count]), refs[2 * count :]
-    stacks = []
-    while len(refs) > (9 if first else 6):
-        stacks.append((refs[:blocks], refs[blocks : 2 * blocks]))
-        refs = refs[2 * blocks :]
+    cots, refs = refs[:count], refs[count:]
+    sides, refs = (refs[:blocks], refs[blocks : 2 * blocks]), refs[2 * blocks :]
     before = None
     if first:
         before, out, lhs, rhs, stage, parked, loads, buf, sems = refs
     else:
         buf, lhs, rhs, stage, parked, loads = refs
-    rows, half = cots[0][0].shape
+    rows, half = sides[0][0].shape[1:]
     group = order[blocks]
     moves, places = [], []
     for part in range(count):
         slot = part // 2 * 2 + (dp_order[first + part] & 1)
+        both = pl.ds(pl.multiple_of(slot * 2 * half, 2 * half), 2 * half)
+        moves.append((cots[part], lhs.at[:, both]))
         for side, owner in enumerate((group, 1 - group)):
             lanes = pl.ds(pl.multiple_of((slot * 2 + owner) * half, half), half)
-            moves.append((cots[side][part], lhs.at[:, lanes]))
             values = []
             for place in range(blocks):
-                source = stacks[part][side][place] if len(stacks) == count else stacks[0][side][place].at[part]
                 if rows % 16:
                     at = (part * 2 + side) * blocks + place
                     target = parked.at[at]
@@ -519,7 +517,7 @@
                 else:
                     offset = pl.multiple_of(order[side * (blocks + 1) + place] * rows, 16)
                     target = rhs.at[pl.ds(offset, rows), lanes]
-                moves.append((source, target))
+                moves.append((sides[side][place].at[part], target))
             places.append((lanes, values, side * (blocks + 1)))
     moves = [pltpu.make_async_copy(a, b, loads.at[k]) for k, (a, b) in enumerate(moves)]
     for move in moves:
@@ -541,18 +539,16 @@
         copy.wait()
 
 
-def zero_projection_grad(order, dp_order, first, cots, cots_other, stacks, before, name):
-    blocks, (rows, half) = len(stacks[0][0]), cots[0].shape
-    count = len(cots)
+def zero_projection_grad(order, dp_order, first, cots, mine, other, before, name):
+    blocks, (count, rows, half) = len(mine), mine[0].shape
     features, tokens = blocks * rows, count * 2 * half
-    flat = [block for pair in stacks for side in pair for block in side]
     extra = [] if before is None else [before]
     scratch = [
         pltpu.VMEM((rows, tokens), BF16),
         pltpu.VMEM((features, tokens), BF16),
         staging(rows, features, half),
         pltpu.VMEM((count * 2 * blocks, rows, half) if rows % 16 else (1, 8, 128), BF16),
-        pltpu.SemaphoreType.DMA((count * 2 * (blocks + 1),)),
+        pltpu.SemaphoreType.DMA((count * (2 * blocks + 1),)),
     ]
     if extra:
         scratch += [
@@ -562,12 +558,12 @@
     return pl.pallas_call(
         functools.partial(zero_grad_kernel, blocks, first, count),
         out_shape=struct((rows, features), F32),
-        in_specs=[SCALARS] * 2 + [HELD] * (2 * count + len(flat)) + [WHOLE] * len(extra),
+        in_specs=[SCALARS] * 2 + [ANYWHERE] * (count + 2 * blocks) + [WHOLE] * len(extra),
         out_specs=HELD if extra else WHOLE,
         scratch_shapes=scratch,
         name=name,
         **params(2 * tokens * rows * features, 4 * rows * features + 2 * tokens * (rows + features), grant=28),
-    )(order, dp_order, *cots, *cots_other, *flat, *extra)
+    )(order, dp_order, *cots, *mine, *other, *extra)
 
 
 def steps(values, level, *during):
@@ -596,7 +592,7 @@
     dp_order = lax.axis_index("dp").astype(jnp.int32) ^ jnp.arange(parts, dtype=jnp.int32)
 
     arrived = swap_grp(own_cot)
-    own_term, sent, normed, stats, cot0, cot1 = prepare(
+    own_term, sent, normed, stats, cot0, cot1_rows = prepare(
         order, acts, modulation, own_cot, arrived, zero_weight, blocks
     )
     split, cut = split_rows(hidden)
@@ -625,19 +621,13 @@
     sent, kept, token_sums = backward_last(
         order, after(grad, out_half), total, slope_a, slope_b, acts, stats, mod, w_in, w_out, cut, blocks, "backward_last"
     )
-    near = [out_half, step(out_half, 0)]
-    far, near, sent, kept, token_sums = lax.optimization_barrier((far, near, sent, kept, token_sums))
-    for level in range(1, levels):
-        near = near + steps(near, level)
-    near_other = [swap_grp(value) for value in near]
-    residual = residual_rows(order, zero_weight, near)
-    cots = gather_dp(after(cot1, token_sums))
-    cots_other = [swap_grp(value) for value in cots]
-
-    gathers = [[far[0]], [jnp.stack(far[1:])]]
+    far, out_half, sent, kept, token_sums = lax.optimization_barrier((far, out_half, sent, kept, token_sums))
+
+    gathers = [[jnp.stack([out_half, far[0]])], [jnp.stack(far[1:])]]
+    cots = gather_dp(after(cot1_rows, token_sums))
     for level in range(levels):
         got = steps(sent, level)
-        gathers = [blocks_so_far + steps(blocks_so_far, level) for blocks_so_far in gathers]
+        gathers = [gather + steps(gather, level) for gather in gathers]
         if level + 1 < levels:
             sent, kept, token_sums = fold(got, kept, token_sums)
     more = unpack_sums(got[0][-16:])
@@ -647,15 +637,16 @@
     back = inv * (
         kept[0] * (1.0 + own_mod[:, 1:2]) - plain / features - (own_values - mean) * inv * (along / features)
     )
+    residual = residual_rows(order, zero_weight, gathers[0])
     residual = jnp.concatenate([swap_grp(residual), residual], 1)
     block_rows = jnp.where(is_control, out_rows, (sums + residual).astype(BF16))
 
-    stacks = [(near, near_other)] + [(mine, [swap_grp(value) for value in mine]) for mine in gathers]
+    others = [[swap_grp(value) for value in gather] for gather in gathers]
     zero_grad = zero_projection_grad(
-        order, dp_order, 0, cots[:2], cots_other[:2], stacks[:2], None, "zero_projection_grad_first"
+        order, dp_order, 0, cots[:2], gathers[0], others[0], None, "zero_projection_grad_first"
     )
     zero_grad = zero_projection_grad(
-        order, dp_order, 2, cots[2:], cots_other[2:], stacks[2:], zero_grad, "zero_projection_grad_last"
+        order, dp_order, 2, cots[2:], gathers[1], others[1], zero_grad, "zero_projection_grad_last"
     )
     return (block_rows[None], (up_rows + back)[None], zero_grad)
 

time: 128 us -> 152 us (1.19)
  waiting for transfers between devices: 20.1 us -> 52.6 us
  local copies, waits for them, and re-layouts: 8.09 us -> 2.61 us
  starting transfers between devices: 35.9 us -> 31.6 us
  other arithmetic: 8.66 us -> 10.4 us
    ppermute x6, waiting for transfers between devices: 8.59 us -> 31 us  [gather_dp(): lax.ppermute(value, 'dp', [(i, i ^ mask) for i in range(length)])]
    ppermute x12 -> x9, waiting for transfers between devices: 8.09 us -> 17.1 us  [step(): return lax.ppermute(value, ('grp', 'fsdp'), pairs)]
    unnamed x65 -> x25, local copies, waits for them, and re-layouts: 8.08 us -> 2.6 us
    ppermute x20 -> x12, starting transfers between devices: 4.4 us -> 2.32 us  [swap_grp(): return lax.ppermute(value, 'grp', [(0, 1), (1, 0)])]
    ppermute x12 -> x9, starting transfers between devices: 11.7 us -> 10.7 us  [step(): return lax.ppermute(value, ('grp', 'fsdp'), pairs)]
  transfers between devices with their start and end apart: 47 -> 36, of which waited for: 10 -> 13; matrix products, arithmetic and copies ran while one was open for 4% -> 5% of each run, Pallas kernels for 35% -> 30%
where the time goes in v9:
time: 152 us
  Pallas kernels  53.3 us (35%)
  waiting for transfers between devices  52.6 us (35%)
  starting transfers between devices  31.6 us (21%)
  other arithmetic  10.4 us (7%)
  local copies, waits for them, and re-layouts  2.61 us (2%)
    ppermute x6, waiting for transfers between devices, gather_dp(): lax.ppermute(value, 'dp', [(i, i ^ mask) for i in range(length)])  31 us
    ppermute x9, waiting for transfers between devices, step(): return lax.ppermute(value, ('grp', 'fsdp'), pairs)  17.1 us
    pallas_call x1, Pallas kernels, backward_first(): pl.pallas_call(functools.partial(backward_first_kernel, blocks, part), ou...  11.7 us
    ppermute x9, starting transfers between devices, send(): return lax.ppermute(value, ('grp', 'fsdp'), pairs)  11.6 us
    pallas_call x1, Pallas kernels, forward_last(): pl.pallas_call(functools.partial(forward_last_kernel, start), out_shape=[...  11.4 us
    ppermute x9, starting transfers between devices, step(): return lax.ppermute(value, ('grp', 'fsdp'), pairs)  10.7 us
    pallas_call x2, Pallas kernels, zero_projection_grad(): pl.pallas_call(functools.partial(zero_grad_kernel, blocks, first, count),...  8.53 us
    pallas_call x1, Pallas kernels, forward_first(): pl.pallas_call(forward_first_kernel, out_shape=(struct((tokens, part), F3...  7.43 us
  transfers between devices with their start and end apart: 36, of which 13 were waited for; matrix products, arithmetic and copies ran while one was open for 5% of the time, Pallas kernels for 30%

profile of v9, /device:TPU:0, one launch (start us, length us, event | category | flops | bytes accessed | tf_op | source)
XLA Modules:
  0.0 151.6 jit_solution(15936521870687452629)
XLA Ops:
  0.6 0.5 collective-permute-start
  1.1 0.8 copy.13.modulation
  1.9 0.7 fusion.14
  2.7 1.0 copy-done.2
  3.6 4.0 %prepare.1 = (f32[608,128]{1,0:T(8,128)S(1)}, bf16[608,128]{1,0:T(8,128)(2,1)S(1)}, bf16[608,128]{1,0:T(8,128)(2,1)S(1)}, bf16[608,128]{1,0:T(8,128)(2,1)S(1)}, ...) custom-call(s32[9]{0:T(128)S(1)} %pad_add_fusion.order, ...), custom_call_target="tpu_custom_call" | custom-call | flops 378535936 | bytes 4202496 | tf_op jit(solution)/shard_map/prepare/pallas_call | solution.py:451
  7.6 2.9 %collective-permute-start.1 = (bf16[608,128]{1,0:T(8,128)(2,1)S(1)}, bf16[608,128]{1,0:T(8,128)(2,1)S(1)}, u32[]{:S(2)}, u32[]{:S(2)}) collective-permute-start(bf16[608,128]{1,0:T(8,128)(2,1)S(1)} %get-tuple-element.56), channel_id=1, source_target_pairs={{0,4},{4,0},{8,12},{12,8},{16,24},{20,28},{24,16},{28,20},{1,5},{5... | collective-permute-start | bytes 466952 | tf_op jit(solution)/shard_map/ppermute | solution.py:64
  10.5 1.5 %collective-permute-start.2 = (bf16[608,128]{1,0:T(8,128)(2,1)S(1)}, bf16[608,128]{1,0:T(8,128)(2,1)S(1)}, u32[]{:S(2)}, u32[]{:S(2)}) collective-permute-start(bf16[608,128]{1,0:T(8,128)(2,1)S(1)} %get-tuple-element.57), channel_id=1, source_target_pairs={{0,8},{4,12},{8,0},{12,4},{16,20},{20,16},{24,28},{28,24},{1,9},{5... | collective-permute-start | bytes 466952 | tf_op jit(solution)/shard_map/ppermute | solution.py:64
  12.0 7.4 %forward_first.1 = (f32[256,1024]{1,0:T(8,128)S(1)}, f32[256,2432]{1,0:T(8,128)}, f32[2432,8]{1,0:T(8,128)S(1)}) custom-call(bf16[256,2432]{1,0:T(8,128)(2,1)S(1)} %get-tuple-element.67.normed, f32[1,3,2432]{2,1,0:T(4,128)S(1)} %copy.13.modulation, bf16[1,2432,2432]{2,1,0:T(8,128)(2,1)} %w_in.5, bf16[1,2432,2432]{2,1,0:T(8,128)(2,1)} %w_out.5), custom_call_target="tpu_custom_call" | custom-call | flops 2550136832 | bytes 12451840 | tf_op jit(solution)/shard_map/forward_first/pallas_call | solution.py:254
  19.5 1.0 add_add_fusion
  20.9 1.5 collective-permute-done.4
  22.4 1.3 multiply_convert_fusion.refs_0_
  23.8 3.0 %collective-permute-start.10 = (bf16[608,256]{1,0:T(8,128)(2,1)S(1)}, bf16[608,256]{1,0:T(8,128)(2,1)S(1)}, u32[]{:S(2)}, u32[]{:S(2)}) collective-permute-start(bf16[608,256]{1,0:T(8,128)(2,1)S(1)} %multiply_convert_fusion.refs_0_), channel_id=1, source_target_pairs={{0,12},{4,8},{8,4},{12,0},{16,28},{20,24},{24,20},{28,16},{1,13},{... | collective-permute-start | bytes 933896 | tf_op jit(solution)/shard_map/ppermute | solution.py:64
  27.4 11.4 %forward_last.1 = (f32[256,1408]{1,0:T(8,128)}, f32[608,256]{1,0:T(8,128)S(1)}, bf16[608,256]{1,0:T(8,128)(2,1)S(1)}, bf16[608,256]{1,0:T(8,128)(2,1)S(1)}, bf16[608,256]{1,0:T(8,128)(2,1)S(1)}) custom-call(s32[9]{0:T(128)S(1)} %pad_add_fusion.order, bf16[256,2432]{1,0:T(8,128)(2,1)S(1)} %get-tuple-element.67.normed, f32[256,2432]{1,0:T(8,128)} %get-tuple-element.63.before, ...), custom_call_target="tpu_custom_call" | custom-call | flops 3506438144 | bytes 16187392 | tf_op jit(solution)/shard_map/forward_last/pallas_call | solution.py:268
  38.8 2.0 %collective-permute-start.5 = (bf16[608,256]{1,0:T(8,128)(2,1)S(1)}, bf16[608,256]{1,0:T(8,128)(2,1)S(1)}, u32[]{:S(2)}, u32[]{:S(2)}) collective-permute-start(bf16[608,256]{1,0:T(8,128)(2,1)S(1)} %get-tuple-element.69), channel_id=1, source_target_pairs={{0,4},{4,0},{8,12},{12,8},{16,24},{20,28},{24,16},{28,20},{1,5},{5... | collective-permute-start | bytes 933896 | tf_op jit(solution)/shard_map/ppermute | solution.py:64
  40.7 1.5 %collective-permute-start.6 = (bf16[608,256]{1,0:T(8,128)(2,1)S(1)}, bf16[608,256]{1,0:T(8,128)(2,1)S(1)}, u32[]{:S(2)}, u32[]{:S(2)}) collective-permute-start(bf16[608,256]{1,0:T(8,128)(2,1)S(1)} %get-tuple-element.70), channel_id=1, source_target_pairs={{0,8},{4,12},{8,0},{12,4},{16,20},{20,16},{24,28},{28,24},{1,9},{5... | collective-permute-start | bytes 933896 | tf_op jit(solution)/shard_map/ppermute | solution.py:64
  42.3 11.7 %backward_first.1 = (bf16[256,2432]{1,0:T(8,128)(2,1)S(1)}, f32[256,2432]{1,0:T(8,128)}) custom-call(s32[9]{0:T(128)S(1)} %pad_add_fusion.order, bf16[608,256]{1,0:T(8,128)(2,1)S(1)} %multiply_convert_fusion.refs_0_, bf16[608,256]{1,0:T(8,128)(2,1)S(1)} %collective-permute-done.8.refs_1_, bf16[608,256]{1,0:T(8,128)(2,1)S(1)} %collective-permute-done.9.refs_2_, ...), custom_call_target="tpu_custom_call" | custom-call | flops 5100273664 | bytes 22413312 | tf_op jit(solution)/shard_map/backward_first/pallas_call | solution.py:326
  54.1 1.5 collective-permute-done.7
  55.5 2.0 %fusion.16 = (bf16[608,256]{1,0:T(8,128)(2,1)S(1)}, f32[608,256]{1,0:T(8,128)}) fusion(f32[608,256]{1,0:T(8,128)S(1)} %get-tuple-element.68, bf16[608,256]{1,0:T(8,128)(2,1)S(1)} %collective-permute-done.7, bf16[608,256]{1,0:T(8,128)(2,1)S(1)} %collective-permute-done.6, bf16[608,256]{1,0:T(8,128)(2,1)S(1)} %collective-permute-done.5, ...), kind=kLoop, calls=%fused_computation.36 | loop fusion | flops 1556480 | bytes 2804100 | tf_op jit(solution)/shard_map/convert_element_type | solution.py:617
  57.7 1.4 collective-permute-done.11
  59.1 3.8 %collective-permute-start.14 = (bf16[608,128]{1,0:T(8,128)(2,1)S(1)}, bf16[608,128]{1,0:T(8,128)(2,1)S(1)}, u32[]{:S(2)}, u32[]{:S(2)}) collective-permute-start(bf16[608,128]{1,0:T(8,128)(2,1)S(1)} %slice_select_fusion), channel_id=1, source_target_pairs={{0,3},{1,2},{2,1},{3,0},{4,7},{5,6},{6,5},{7,4},{8,11},{9,10},{10,... | collective-permute-start | bytes 466952 | tf_op jit(solution)/shard_map/ppermute | solution.py:70
  62.9 0.7 collective-permute-start.12
  63.5 7.2 %backward_last.1 = (bf16[624,256]{1,0:T(8,128)(2,1)S(1)}, bf16[624,256]{1,0:T(8,128)(2,1)S(1)}, f32[608,256]{1,0:T(8,128)S(1)}, f32[608,256]{1,0:T(8,128)S(1)}, f32[2,256]{1,0:T(2,128)S(1)}) custom-call(s32[9]{0:T(128)S(1)} %pad_add_fusion.order, bf16[256,2432]{1,0:T(8,128)(2,1)} %copy-done.4, f32[256,2432]{1,0:T(8,128)} %get-tuple-element.81.before, ...), custom_call_target="tpu_custom_call" | custom-call | flops 956301312 | bytes 6225920 | tf_op jit(solution)/shard_map/backward_last/pallas_call | solution.py:379
  70.7 5.7 %collective-permute-done.13 = bf16[608,128]{1,0:T(8,128)(2,1)} collective-permute-done((bf16[608,128]{1,0:T(8,128)(2,1)S(1)}, bf16[608,128]{1,0:T(8,128)(2,1)}, u32[]{:S(2)}, u32[]{:S(2)}) %collective-permute-start.13) | collective-permute-done | bytes 155680 | tf_op jit(solution)/shard_map/ppermute | solution.py:70
  76.4 1.5 collective-permute-start.19
  77.9 0.5 collective-permute-start.20
  78.5 1.6 %collective-permute-start.15 = (bf16[2,608,128]{2,1,0:T(8,128)(2,1)S(1)}, bf16[2,608,128]{2,1,0:T(8,128)(2,1)}, u32[]{:S(2)}, u32[]{:S(2)}) collective-permute-start(bf16[2,608,128]{2,1,0:T(8,128)(2,1)S(1)} %pad_maximum_fusion.refs_0_.refs_2_), channel_id=1, source_target_pairs={{0,4},{4,0},{8,12},{12,8},{16,24},{20,28},{24,16},{28,20},{1,5},{5... | collective-permute-start | bytes 933896 | tf_op jit(solution)/shard_map/ppermute | solution.py:48
  80.1 3.4 %collective-permute-done.19.refs_0_ = bf16[624,256]{1,0:T(8,128)(2,1)S(1)} collective-permute-done((bf16[624,256]{1,0:T(8,128)(2,1)S(1)}, bf16[624,256]{1,0:T(8,128)(2,1)S(1)}, u32[]{:S(2)}, u32[]{:S(2)}) %collective-permute-start.19) | collective-permute-done | bytes 319520 | tf_op jit(solution)/shard_map/ppermute | solution.py:48
  83.4 3.4 %collective-permute-done.20.refs_1_ = bf16[624,256]{1,0:T(8,128)(2,1)S(1)} collective-permute-done((bf16[624,256]{1,0:T(8,128)(2,1)S(1)}, bf16[624,256]{1,0:T(8,128)(2,1)S(1)}, u32[]{:S(2)}, u32[]{:S(2)}) %collective-permute-start.20) | collective-permute-done | bytes 319520 | tf_op jit(solution)/shard_map/ppermute | solution.py:48
  86.8 0.8 fold.1
  87.7 0.8 copy-done.5
  88.5 1.5 %collective-permute-start.21 = (bf16[624,256]{1,0:T(8,128)(2,1)}, bf16[624,256]{1,0:T(8,128)(2,1)}, u32[]{:S(2)}, u32[]{:S(2)}) collective-permute-start(bf16[624,256]{1,0:T(8,128)(2,1)} %get-tuple-element.101), channel_id=1, source_target_pairs={{0,8},{4,12},{8,0},{12,4},{16,20},{20,16},{24,28},{28,24},{1,9},{5... | collective-permute-start | bytes 958472 | tf_op jit(solution)/shard_map/ppermute | solution.py:48
  90.6 1.5 %collective-permute-start.17 = (bf16[2,608,128]{2,1,0:T(8,128)(2,1)}, bf16[2,608,128]{2,1,0:T(8,128)(2,1)}, u32[]{:S(2)}, u32[]{:S(2)}) collective-permute-start(bf16[2,608,128]{2,1,0:T(8,128)(2,1)} %collective-permute-done.15.refs_1_.refs_3_), channel_id=1, source_target_pairs={{0,8},{4,12},{8,0},{12,4},{16,20},{20,16},{24,28},{28,24},{1,9},{5... | collective-permute-start | bytes 933896 | tf_op jit(solution)/shard_map/ppermute | solution.py:48
  92.2 0.9 pad_maximum_fusion.1.refs_2_
  93.2 0.6 collective-permute-start.25
  93.8 5.4 %collective-permute-done.16.refs_2_.refs_4_ = bf16[2,608,128]{2,1,0:T(8,128)(2,1)} collective-permute-done((bf16[2,608,128]{2,1,0:T(8,128)(2,1)S(1)}, bf16[2,608,128]{2,1,0:T(8,128)(2,1)}, u32[]{:S(2)}, u32[]{:S(2)}) %collective-permute-start.16) | collective-permute-done | bytes 311328 | tf_op jit(solution)/shard_map/ppermute | solution.py:48
  99.2 1.5 collective-permute-start.24
  100.6 4.4 %collective-permute-done.17.refs_3_.refs_5_ = bf16[2,608,128]{2,1,0:T(8,128)(2,1)} collective-permute-done((bf16[2,608,128]{2,1,0:T(8,128)(2,1)}, bf16[2,608,128]{2,1,0:T(8,128)(2,1)}, u32[]{:S(2)}, u32[]{:S(2)}) %collective-permute-start.17) | collective-permute-done | bytes 311328 | tf_op jit(solution)/shard_map/ppermute | solution.py:48
  105.1 2.2 %residual_rows.1 = f32[608,128]{1,0:T(8,128)S(1)} custom-call(s32[9]{0:T(128)S(1)} %pad_add_fusion.order, bf16[608,2432]{1,0:T(8,128)(2,1)S(1)} %copy-done, bf16[2,608,128]{2,1,0:T(8,128)(2,1)S(1)} %pad_maximum_fusion.refs_0_.refs_2_, bf16[2,608,128]{2,1,0:T(8,128)(2,1)} %collective-permute-done.15.refs_1_.refs_3_, ...), custom_call_target="tpu_custom_call" | custom-call | flops 378535936 | bytes 4202496 | tf_op jit(solution)/shard_map/residual_rows/pallas_call | solution.py:483
  107.3 0.7 slice_convert_fusion
  109.1 1.5 %collective-permute-start.26 = (bf16[2,608,128]{2,1,0:T(8,128)(2,1)S(1)}, bf16[2,608,128]{2,1,0:T(8,128)(2,1)S(1)}, u32[]{:S(2)}, u32[]{:S(2)}) collective-permute-start(bf16[2,608,128]{2,1,0:T(8,128)(2,1)S(1)} %collective-permute-done.24.refs_3_), channel_id=1, source_target_pairs={{0,8},{4,12},{8,0},{12,4},{16,20},{20,16},{24,28},{28,24},{1,9},{5... | collective-permute-start | bytes 933896 | tf_op jit(solution)/shard_map/ppermute | solution.py:48
  110.6 4.4 %collective-permute-done.31.refs_1_ = bf16[608,256]{1,0:T(8,128)(2,1)S(1)} collective-permute-done((bf16[608,256]{1,0:T(8,128)(2,1)}, bf16[608,256]{1,0:T(8,128)(2,1)S(1)}, u32[]{:S(2)}, u32[]{:S(2)}) %collective-permute-start.31) | collective-permute-done | bytes 311328 | tf_op jit(solution)/shard_map/ppermute | solution.py:70
  115.6 2.4 %fusion.5 = f32[1,608,256]{2,1,0:T(8,128)} fusion(f32[608,256]{1,0:T(8,128)S(1)} %copy-done.6, f32[608,128]{1,0:T(8,128)} %collective-permute-done.4, f32[608,128]{1,0:T(8,128)} %add_add_fusion, bf16[624,256]{1,0:T(8,128)(2,1)} %collective-permute-done.21, f32[256]{0:T(256)S(1)} %bitcast.27, f32[256]{0:T(256)S(1)} %bitcast.29, f32[256]{0:T(256)S(1)} %bitcast.26, ...), kind=kLoop, calls=%fused_computation.7 | loop fusion | flops 2179072 | bytes 2808197 | tf_op jit(solution)/shard_map/broadcast_in_dim | solution.py:651
  118.0 2.5 %collective-permute-start.23 = (bf16[608,256]{1,0:T(8,128)(2,1)S(1)}, bf16[608,256]{1,0:T(8,128)(2,1)S(1)}, u32[]{:S(2)}, u32[]{:S(2)}) collective-permute-start(bf16[608,256]{1,0:T(8,128)(2,1)S(1)} %copy-done.8), channel_id=1, source_target_pairs={{0,3},{1,2},{2,1},{3,0},{4,7},{5,6},{6,5},{7,4},{8,11},{9,10},{10,... | collective-permute-start | bytes 933896 | tf_op jit(solution)/shard_map/ppermute | solution.py:70
  121.2 4.1 %zero_projection_grad_first.1.refs_10_ = f32[608,2432]{1,0:T(8,128)S(1)} custom-call(s32[9]{0:T(128)S(1)} %pad_add_fusion.order, s32[4]{0:T(128)S(1)} %iota_xor_fusion.dp_order, bf16[608,256]{1,0:T(8,128)(2,1)S(1)} %copy-done.8, bf16[608,256]{1,0:T(8,128)(2,1)S(1)} %collective-permute-done.31.refs_1_, ...), custom_call_target="tpu_custom_call" | custom-call | flops 1514143744 | bytes 9027584 | tf_op jit(solution)/shard_map/zero_projection_grad_first/pallas_call | solution.py:558
  125.3 0.8 fusion.8
  126.2 4.0 %collective-permute-done.23.refs_1_ = bf16[608,256]{1,0:T(8,128)(2,1)S(1)} collective-permute-done((bf16[608,256]{1,0:T(8,128)(2,1)S(1)}, bf16[608,256]{1,0:T(8,128)(2,1)S(1)}, u32[]{:S(2)}, u32[]{:S(2)}) %collective-permute-start.23) | collective-permute-done | bytes 311328 | tf_op jit(solution)/shard_map/ppermute | solution.py:70
  130.2 16.9 %collective-permute-done.22.refs_0_ = bf16[608,256]{1,0:T(8,128)(2,1)S(1)} collective-permute-done((bf16[608,256]{1,0:T(8,128)(2,1)S(1)}, bf16[608,256]{1,0:T(8,128)(2,1)S(1)}, u32[]{:S(2)}, u32[]{:S(2)}) %collective-permute-start.22) | collective-permute-done | bytes 311328 | tf_op jit(solution)/shard_map/ppermute | solution.py:70
  147.1 4.4 %zero_projection_grad_last.1 = f32[608,2432]{1,0:T(8,128)} custom-call(s32[9]{0:T(128)S(1)} %pad_add_fusion.order, s32[4]{0:T(128)S(1)} %iota_xor_fusion.dp_order, bf16[608,256]{1,0:T(8,128)(2,1)S(1)} %collective-permute-done.22.refs_0_, bf16[608,256]{1,0:T(8,128)(2,1)S(1)} %collective-permute-done.23.refs_1_, ...), custom_call_target="tpu_custom_call" | custom-call | flops 1514143744 | bytes 9027584 | tf_op jit(solution)/shard_map/zero_projection_grad_last/pallas_call | solution.py:558
  (74 shorter events, 4.3 us)
Async XLA Ops:
  0.6 2.0 %collective-permute-start = (bf16[608,256]{1,0:T(8,128)(2,1)}, bf16[608,256]{1,0:T(8,128)(2,1)S(1)}, u32[]{:S(2)}, u32[]{:S(2)}) collective-permute-start(bf16[608,256]{1,0:T(8,128)(2,1)} %bitcast.21), channel_id=1, source_target_pairs={{0,16},{16,0},{1,17},{17,1},{2,18},{18,2},{3,19},{19,3},{4,20},{20... | collective-permute-start | bytes 933896 | tf_op jit(solution)/shard_map/ppermute | solution.py:36
  2.7 1.0 copy-start.2
  7.6 11.8 %copy-start.7 = (bf16[608,256]{1,0:T(8,128)(2,1)}, bf16[608,256]{1,0:T(8,128)(2,1)S(1)}, u32[]{:S(2)}) copy-start(bf16[608,256]{1,0:T(8,128)(2,1)S(1)} %get-tuple-element.104.refs_0_) | copy-start | bytes 933892
  7.6 11.9 %collective-permute-start.1 = (bf16[608,128]{1,0:T(8,128)(2,1)S(1)}, bf16[608,128]{1,0:T(8,128)(2,1)S(1)}, u32[]{:S(2)}, u32[]{:S(2)}) collective-permute-start(bf16[608,128]{1,0:T(8,128)(2,1)S(1)} %get-tuple-element.56), channel_id=1, source_target_pairs={{0,4},{4,0},{8,12},{12,8},{16,24},{20,28},{24,16},{28,20},{1,5},{5... | collective-permute-start | bytes 466952 | tf_op jit(solution)/shard_map/ppermute | solution.py:64
  10.5 9.0 %collective-permute-start.2 = (bf16[608,128]{1,0:T(8,128)(2,1)S(1)}, bf16[608,128]{1,0:T(8,128)(2,1)S(1)}, u32[]{:S(2)}, u32[]{:S(2)}) collective-permute-start(bf16[608,128]{1,0:T(8,128)(2,1)S(1)} %get-tuple-element.57), channel_id=1, source_target_pairs={{0,8},{4,12},{8,0},{12,4},{16,20},{20,16},{24,28},{28,24},{1,9},{5... | collective-permute-start | bytes 466952 | tf_op jit(solution)/shard_map/ppermute | solution.py:64
  12.0 7.5 %collective-permute-start.3 = (bf16[608,128]{1,0:T(8,128)(2,1)S(1)}, bf16[608,128]{1,0:T(8,128)(2,1)S(1)}, u32[]{:S(2)}, u32[]{:S(2)}) collective-permute-start(bf16[608,128]{1,0:T(8,128)(2,1)S(1)} %get-tuple-element.58), channel_id=1, source_target_pairs={{0,12},{4,8},{8,4},{12,0},{16,28},{20,24},{24,20},{28,16},{1,13},{... | collective-permute-start | bytes 466952 | tf_op jit(solution)/shard_map/ppermute | solution.py:64
  19.5 4.3 %copy-start.1 = (f32[2432,8]{1,0:T(8,128)}, f32[2432,8]{1,0:T(8,128)S(1)}, u32[]{:S(2)}) copy-start(f32[2432,8]{1,0:T(8,128)S(1)} %get-tuple-element.60.mod) | copy-start | bytes 233476
  20.5 1.9 %collective-permute-start.4 = (f32[608,128]{1,0:T(8,128)}, f32[608,128]{1,0:T(8,128)}, u32[]{:S(2)}, u32[]{:S(2)}) collective-permute-start(f32[608,128]{1,0:T(8,128)} %add_add_fusion), channel_id=1, source_target_pairs={{0,16},{16,0},{1,17},{17,1},{2,18},{18,2},{3,19},{19,3},{4,20},{20... | collective-permute-start | bytes 933896 | tf_op jit(solution)/shard_map/ppermute | solution.py:36
  23.8 18.5 %collective-permute-start.10 = (bf16[608,256]{1,0:T(8,128)(2,1)S(1)}, bf16[608,256]{1,0:T(8,128)(2,1)S(1)}, u32[]{:S(2)}, u32[]{:S(2)}) collective-permute-start(bf16[608,256]{1,0:T(8,128)(2,1)S(1)} %multiply_convert_fusion.refs_0_), channel_id=1, source_target_pairs={{0,12},{4,8},{8,4},{12,0},{16,28},{20,24},{24,20},{28,16},{1,13},{... | collective-permute-start | bytes 933896 | tf_op jit(solution)/shard_map/ppermute | solution.py:64
  26.7 15.6 %collective-permute-start.9 = (bf16[608,256]{1,0:T(8,128)(2,1)S(1)}, bf16[608,256]{1,0:T(8,128)(2,1)S(1)}, u32[]{:S(2)}, u32[]{:S(2)}) collective-permute-start(bf16[608,256]{1,0:T(8,128)(2,1)S(1)} %multiply_convert_fusion.refs_0_), channel_id=1, source_target_pairs={{0,8},{4,12},{8,0},{12,4},{16,20},{20,16},{24,28},{28,24},{1,9},{5... | collective-permute-start | bytes 933896 | tf_op jit(solution)/shard_map/ppermute | solution.py:64
  27.2 15.1 %collective-permute-start.8 = (bf16[608,256]{1,0:T(8,128)(2,1)S(1)}, bf16[608,256]{1,0:T(8,128)(2,1)S(1)}, u32[]{:S(2)}, u32[]{:S(2)}) collective-permute-start(bf16[608,256]{1,0:T(8,128)(2,1)S(1)} %multiply_convert_fusion.refs_0_), channel_id=1, source_target_pairs={{0,4},{4,0},{8,12},{12,8},{16,24},{20,28},{24,16},{28,20},{1,5},{5... | collective-permute-start | bytes 933896 | tf_op jit(solution)/shard_map/ppermute | solution.py:64
  38.8 15.3 %collective-permute-start.5 = (bf16[608,256]{1,0:T(8,128)(2,1)S(1)}, bf16[608,256]{1,0:T(8,128)(2,1)S(1)}, u32[]{:S(2)}, u32[]{:S(2)}) collective-permute-start(bf16[608,256]{1,0:T(8,128)(2,1)S(1)} %get-tuple-element.69), channel_id=1, source_target_pairs={{0,4},{4,0},{8,12},{12,8},{16,24},{20,28},{24,16},{28,20},{1,5},{5... | collective-permute-start | bytes 933896 | tf_op jit(solution)/shard_map/ppermute | solution.py:64
  40.7 13.3 %collective-permute-start.6 = (bf16[608,256]{1,0:T(8,128)(2,1)S(1)}, bf16[608,256]{1,0:T(8,128)(2,1)S(1)}, u32[]{:S(2)}, u32[]{:S(2)}) collective-permute-start(bf16[608,256]{1,0:T(8,128)(2,1)S(1)} %get-tuple-element.70), channel_id=1, source_target_pairs={{0,8},{4,12},{8,0},{12,4},{16,20},{20,16},{24,28},{28,24},{1,9},{5... | collective-permute-start | bytes 933896 | tf_op jit(solution)/shard_map/ppermute | solution.py:64
  42.2 13.3 %collective-permute-start.7 = (bf16[608,256]{1,0:T(8,128)(2,1)S(1)}, bf16[608,256]{1,0:T(8,128)(2,1)S(1)}, u32[]{:S(2)}, u32[]{:S(2)}) collective-permute-start(bf16[608,256]{1,0:T(8,128)(2,1)S(1)} %get-tuple-element.71), channel_id=1, source_target_pairs={{0,12},{4,8},{8,4},{12,0},{16,28},{20,24},{24,20},{28,16},{1,13},{... | collective-permute-start | bytes 933896 | tf_op jit(solution)/shard_map/ppermute | solution.py:64
  54.0 3.5 %copy-start.4 = (bf16[256,2432]{1,0:T(8,128)(2,1)}, bf16[256,2432]{1,0:T(8,128)(2,1)S(1)}, u32[]{:S(2)}) copy-start(bf16[256,2432]{1,0:T(8,128)(2,1)S(1)} %get-tuple-element.86.grad) | copy-start | bytes 3735556
  57.6 6.0 %copy-start.9 = (bf16[608,256]{1,0:T(8,128)(2,1)}, bf16[608,256]{1,0:T(8,128)(2,1)S(1)}, u32[]{:S(2)}) copy-start(bf16[608,256]{1,0:T(8,128)(2,1)S(1)} %get-tuple-element.109) | copy-start | bytes 933892
  57.6 1.4 collective-permute-start.11
  59.1 11.7 %collective-permute-start.14 = (bf16[608,128]{1,0:T(8,128)(2,1)S(1)}, bf16[608,128]{1,0:T(8,128)(2,1)S(1)}, u32[]{:S(2)}, u32[]{:S(2)}) collective-permute-start(bf16[608,128]{1,0:T(8,128)(2,1)S(1)} %slice_select_fusion), channel_id=1, source_target_pairs={{0,3},{1,2},{2,1},{3,0},{4,7},{5,6},{6,5},{7,4},{8,11},{9,10},{10,... | collective-permute-start | bytes 466952 | tf_op jit(solution)/shard_map/ppermute | solution.py:70
  62.8 13.6 %collective-permute-start.13 = (bf16[608,128]{1,0:T(8,128)(2,1)S(1)}, bf16[608,128]{1,0:T(8,128)(2,1)}, u32[]{:S(2)}, u32[]{:S(2)}) collective-permute-start(bf16[608,128]{1,0:T(8,128)(2,1)S(1)} %slice_select_fusion), channel_id=1, source_target_pairs={{0,2},{1,3},{2,0},{3,1},{4,6},{5,7},{6,4},{7,5},{8,10},{9,11},{10,... | collective-permute-start | bytes 466952 | tf_op jit(solution)/shard_map/ppermute | solution.py:70
  62.9 13.6 %collective-permute-start.12 = (bf16[608,128]{1,0:T(8,128)(2,1)S(1)}, bf16[608,128]{1,0:T(8,128)(2,1)S(1)}, u32[]{:S(2)}, u32[]{:S(2)}) collective-permute-start(bf16[608,128]{1,0:T(8,128)(2,1)S(1)} %slice_select_fusion), channel_id=1, source_target_pairs={{0,1},{1,0},{2,3},{3,2},{4,5},{5,4},{6,7},{7,6},{8,9},{9,8},{10,11... | collective-permute-start | bytes 466952 | tf_op jit(solution)/shard_map/ppermute | solution.py:70
  76.4 7.0 %collective-permute-start.19 = (bf16[624,256]{1,0:T(8,128)(2,1)S(1)}, bf16[624,256]{1,0:T(8,128)(2,1)S(1)}, u32[]{:S(2)}, u32[]{:S(2)}) collective-permute-start(bf16[624,256]{1,0:T(8,128)(2,1)S(1)} %get-tuple-element.95), channel_id=1, source_target_pairs={{0,4},{4,0},{8,12},{12,8},{16,24},{20,28},{24,16},{28,20},{1,5},{5... | collective-permute-start | bytes 958472 | tf_op jit(solution)/shard_map/ppermute | solution.py:48
  77.9 8.9 %collective-permute-start.20 = (bf16[624,256]{1,0:T(8,128)(2,1)S(1)}, bf16[624,256]{1,0:T(8,128)(2,1)S(1)}, u32[]{:S(2)}, u32[]{:S(2)}) collective-permute-start(bf16[624,256]{1,0:T(8,128)(2,1)S(1)} %get-tuple-element.96), channel_id=1, source_target_pairs={{0,4},{4,0},{8,12},{12,8},{16,24},{20,28},{24,16},{28,20},{1,5},{5... | collective-permute-start | bytes 958472 | tf_op jit(solution)/shard_map/ppermute | solution.py:48
  78.5 26.6 %copy-start = (bf16[608,2432]{1,0:T(8,128)(2,1)S(1)}, bf16[608,2432]{1,0:T(8,128)(2,1)}, u32[]{:S(2)}) copy-start(bf16[608,2432]{1,0:T(8,128)(2,1)} %weight.3) | copy-start | bytes 8871940
  78.5 12.1 %collective-permute-start.15 = (bf16[2,608,128]{2,1,0:T(8,128)(2,1)S(1)}, bf16[2,608,128]{2,1,0:T(8,128)(2,1)}, u32[]{:S(2)}, u32[]{:S(2)}) collective-permute-start(bf16[2,608,128]{2,1,0:T(8,128)(2,1)S(1)} %pad_maximum_fusion.refs_0_.refs_2_), channel_id=1, source_target_pairs={{0,4},{4,0},{8,12},{12,8},{16,24},{20,28},{24,16},{28,20},{1,5},{5... | collective-permute-start | bytes 933896 | tf_op jit(solution)/shard_map/ppermute | solution.py:48
  87.7 0.8 copy-start.5
  88.5 16.5 %collective-permute-start.21 = (bf16[624,256]{1,0:T(8,128)(2,1)}, bf16[624,256]{1,0:T(8,128)(2,1)}, u32[]{:S(2)}, u32[]{:S(2)}) collective-permute-start(bf16[624,256]{1,0:T(8,128)(2,1)} %get-tuple-element.101), channel_id=1, source_target_pairs={{0,8},{4,12},{8,0},{12,4},{16,20},{20,16},{24,28},{28,24},{1,9},{5... | collective-permute-start | bytes 958472 | tf_op jit(solution)/shard_map/ppermute | solution.py:48
  90.0 9.1 %collective-permute-start.16 = (bf16[2,608,128]{2,1,0:T(8,128)(2,1)S(1)}, bf16[2,608,128]{2,1,0:T(8,128)(2,1)}, u32[]{:S(2)}, u32[]{:S(2)}) collective-permute-start(bf16[2,608,128]{2,1,0:T(8,128)(2,1)S(1)} %pad_maximum_fusion.refs_0_.refs_2_), channel_id=1, source_target_pairs={{0,8},{4,12},{8,0},{12,4},{16,20},{20,16},{24,28},{28,24},{1,9},{5... | collective-permute-start | bytes 933896 | tf_op jit(solution)/shard_map/ppermute | solution.py:48
  90.6 14.4 %collective-permute-start.17 = (bf16[2,608,128]{2,1,0:T(8,128)(2,1)}, bf16[2,608,128]{2,1,0:T(8,128)(2,1)}, u32[]{:S(2)}, u32[]{:S(2)}) collective-permute-start(bf16[2,608,128]{2,1,0:T(8,128)(2,1)} %collective-permute-done.15.refs_1_.refs_3_), channel_id=1, source_target_pairs={{0,8},{4,12},{8,0},{12,4},{16,20},{20,16},{24,28},{28,24},{1,9},{5... | collective-permute-start | bytes 933896 | tf_op jit(solution)/shard_map/ppermute | solution.py:48
  93.1 15.0 %collective-permute-start.27 = (bf16[2,608,128]{2,1,0:T(8,128)(2,1)S(1)}, bf16[2,608,128]{2,1,0:T(8,128)(2,1)S(1)}, u32[]{:S(2)}, u32[]{:S(2)}) collective-permute-start(bf16[2,608,128]{2,1,0:T(8,128)(2,1)S(1)} %pad_maximum_fusion.1.refs_2_), channel_id=1, source_target_pairs={{0,16},{16,0},{1,17},{17,1},{2,18},{18,2},{3,19},{19,3},{4,20},{20... | collective-permute-start | bytes 933896 | tf_op jit(solution)/shard_map/ppermute | solution.py:36
  93.2 15.9 %collective-permute-start.25 = (bf16[2,608,128]{2,1,0:T(8,128)(2,1)S(1)}, bf16[2,608,128]{2,1,0:T(8,128)(2,1)S(1)}, u32[]{:S(2)}, u32[]{:S(2)}) collective-permute-start(bf16[2,608,128]{2,1,0:T(8,128)(2,1)S(1)} %pad_maximum_fusion.1.refs_2_), channel_id=1, source_target_pairs={{0,8},{4,12},{8,0},{12,4},{16,20},{20,16},{24,28},{28,24},{1,9},{5... | collective-permute-start | bytes 933896 | tf_op jit(solution)/shard_map/ppermute | solution.py:48
  99.2 9.9 %collective-permute-start.24 = (bf16[2,608,128]{2,1,0:T(8,128)(2,1)S(1)}, bf16[2,608,128]{2,1,0:T(8,128)(2,1)S(1)}, u32[]{:S(2)}, u32[]{:S(2)}) collective-permute-start(bf16[2,608,128]{2,1,0:T(8,128)(2,1)S(1)} %pad_maximum_fusion.1.refs_2_), channel_id=1, source_target_pairs={{0,4},{4,0},{8,12},{12,8},{16,24},{20,28},{24,16},{28,20},{1,5},{5... | collective-permute-start | bytes 933896 | tf_op jit(solution)/shard_map/ppermute | solution.py:48
  105.0 10.0 %collective-permute-start.32 = (bf16[2,608,128]{2,1,0:T(8,128)(2,1)S(1)}, bf16[2,608,128]{2,1,0:T(8,128)(2,1)S(1)}, u32[]{:S(2)}, u32[]{:S(2)}) collective-permute-start(bf16[2,608,128]{2,1,0:T(8,128)(2,1)S(1)} %pad_maximum_fusion.refs_0_.refs_2_), channel_id=1, source_target_pairs={{0,16},{16,0},{1,17},{17,1},{2,18},{18,2},{3,19},{19,3},{4,20},{20... | collective-permute-start | bytes 933896 | tf_op jit(solution)/shard_map/ppermute | solution.py:36
  105.0 10.0 %collective-permute-start.31 = (bf16[608,256]{1,0:T(8,128)(2,1)}, bf16[608,256]{1,0:T(8,128)(2,1)S(1)}, u32[]{:S(2)}, u32[]{:S(2)}) collective-permute-start(bf16[608,256]{1,0:T(8,128)(2,1)} %copy-done.7), channel_id=1, source_target_pairs={{0,1},{1,0},{2,3},{3,2},{4,5},{5,4},{6,7},{7,6},{8,9},{9,8},{10,11... | collective-permute-start | bytes 933896 | tf_op jit(solution)/shard_map/ppermute | solution.py:70
  105.1 10.5 %copy-start.3 = (bf16[1,608,256]{2,1,0:T(8,128)(2,1)S(1)}, bf16[1,608,256]{2,1,0:T(8,128)(2,1)}, u32[]{:S(2)}) copy-start(bf16[1,608,256]{2,1,0:T(8,128)(2,1)} %param.13) | copy-start | bytes 933892
  105.1 10.5 %copy-start.6 = (f32[608,256]{1,0:T(8,128)S(1)}, f32[608,256]{1,0:T(8,128)}, u32[]{:S(2)}) copy-start(f32[608,256]{1,0:T(8,128)} %copy-done.5) | copy-start | bytes 1867780
  107.3 10.6 %copy-start.8 = (bf16[608,256]{1,0:T(8,128)(2,1)S(1)}, bf16[608,256]{1,0:T(8,128)(2,1)}, u32[]{:S(2)}) copy-start(bf16[608,256]{1,0:T(8,128)(2,1)} %copy-done.7) | copy-start | bytes 933892
  108.1 12.4 %collective-permute-start.34 = (bf16[2,608,128]{2,1,0:T(8,128)(2,1)}, bf16[2,608,128]{2,1,0:T(8,128)(2,1)S(1)}, u32[]{:S(2)}, u32[]{:S(2)}) collective-permute-start(bf16[2,608,128]{2,1,0:T(8,128)(2,1)} %collective-permute-done.16.refs_2_.refs_4_), channel_id=1, source_target_pairs={{0,16},{16,0},{1,17},{17,1},{2,18},{18,2},{3,19},{19,3},{4,20},{20... | collective-permute-start | bytes 933896 | tf_op jit(solution)/shard_map/ppermute | solution.py:36
  109.1 11.5 %collective-permute-start.33 = (bf16[2,608,128]{2,1,0:T(8,128)(2,1)}, bf16[2,608,128]{2,1,0:T(8,128)(2,1)S(1)}, u32[]{:S(2)}, u32[]{:S(2)}) collective-permute-start(bf16[2,608,128]{2,1,0:T(8,128)(2,1)} %collective-permute-done.15.refs_1_.refs_3_), channel_id=1, source_target_pairs={{0,16},{16,0},{1,17},{17,1},{2,18},{18,2},{3,19},{19,3},{4,20},{20... | collective-permute-start | bytes 933896 | tf_op jit(solution)/shard_map/ppermute | solution.py:36
  109.1 8.9 %collective-permute-start.26 = (bf16[2,608,128]{2,1,0:T(8,128)(2,1)S(1)}, bf16[2,608,128]{2,1,0:T(8,128)(2,1)S(1)}, u32[]{:S(2)}, u32[]{:S(2)}) collective-permute-start(bf16[2,608,128]{2,1,0:T(8,128)(2,1)S(1)} %collective-permute-done.24.refs_3_), channel_id=1, source_target_pairs={{0,8},{4,12},{8,0},{12,4},{16,20},{20,16},{24,28},{28,24},{1,9},{5... | collective-permute-start | bytes 933896 | tf_op jit(solution)/shard_map/ppermute | solution.py:48
  115.0 5.6 %collective-permute-start.18 = (f32[608,128]{1,0:T(8,128)S(1)}, f32[608,128]{1,0:T(8,128)S(1)}, u32[]{:S(2)}, u32[]{:S(2)}) collective-permute-start(f32[608,128]{1,0:T(8,128)S(1)} %residual_rows.1), channel_id=1, source_target_pairs={{0,16},{16,0},{1,17},{17,1},{2,18},{18,2},{3,19},{19,3},{4,20},{20... | collective-permute-start | bytes 933896 | tf_op jit(solution)/shard_map/ppermute | solution.py:36
  115.0 6.1 %collective-permute-start.35 = (bf16[2,608,128]{2,1,0:T(8,128)(2,1)}, bf16[2,608,128]{2,1,0:T(8,128)(2,1)S(1)}, u32[]{:S(2)}, u32[]{:S(2)}) collective-permute-start(bf16[2,608,128]{2,1,0:T(8,128)(2,1)} %collective-permute-done.17.refs_3_.refs_5_), channel_id=1, source_target_pairs={{0,16},{16,0},{1,17},{17,1},{2,18},{18,2},{3,19},{19,3},{4,20},{20... | collective-permute-start | bytes 933896 | tf_op jit(solution)/shard_map/ppermute | solution.py:36
  118.0 7.4 %copy-start.10 = (bf16[608,256]{1,0:T(8,128)(2,1)S(1)}, bf16[608,256]{1,0:T(8,128)(2,1)}, u32[]{:S(2)}) copy-start(bf16[608,256]{1,0:T(8,128)(2,1)} %copy-done.9) | copy-start | bytes 933892
  118.0 7.4 %copy-start.11 = (f32[608,256]{1,0:T(8,128)S(1)}, f32[608,256]{1,0:T(8,128)}, u32[]{:S(2)}) copy-start(f32[608,256]{1,0:T(8,128)} %get-tuple-element.110) | copy-start | bytes 1867780
  118.0 12.2 %collective-permute-start.23 = (bf16[608,256]{1,0:T(8,128)(2,1)S(1)}, bf16[608,256]{1,0:T(8,128)(2,1)S(1)}, u32[]{:S(2)}, u32[]{:S(2)}) collective-permute-start(bf16[608,256]{1,0:T(8,128)(2,1)S(1)} %copy-done.8), channel_id=1, source_target_pairs={{0,3},{1,2},{2,1},{3,0},{4,7},{5,6},{6,5},{7,4},{8,11},{9,10},{10,... | collective-permute-start | bytes 933896 | tf_op jit(solution)/shard_map/ppermute | solution.py:70
  120.5 26.5 %collective-permute-start.22 = (bf16[608,256]{1,0:T(8,128)(2,1)S(1)}, bf16[608,256]{1,0:T(8,128)(2,1)S(1)}, u32[]{:S(2)}, u32[]{:S(2)}) collective-permute-start(bf16[608,256]{1,0:T(8,128)(2,1)S(1)} %copy-done.8), channel_id=1, source_target_pairs={{0,2},{1,3},{2,0},{3,1},{4,6},{5,7},{6,4},{7,5},{8,10},{9,11},{10,... | collective-permute-start | bytes 933896 | tf_op jit(solution)/shard_map/ppermute | solution.py:70
  120.5 26.5 %collective-permute-start.28 = (bf16[2,608,128]{2,1,0:T(8,128)(2,1)S(1)}, bf16[2,608,128]{2,1,0:T(8,128)(2,1)S(1)}, u32[]{:S(2)}, u32[]{:S(2)}) collective-permute-start(bf16[2,608,128]{2,1,0:T(8,128)(2,1)S(1)} %collective-permute-done.24.refs_3_), channel_id=1, source_target_pairs={{0,16},{16,0},{1,17},{17,1},{2,18},{18,2},{3,19},{19,3},{4,20},{20... | collective-permute-start | bytes 933896 | tf_op jit(solution)/shard_map/ppermute | solution.py:36
  120.6 26.4 %collective-permute-start.29 = (bf16[2,608,128]{2,1,0:T(8,128)(2,1)S(1)}, bf16[2,608,128]{2,1,0:T(8,128)(2,1)S(1)}, u32[]{:S(2)}, u32[]{:S(2)}) collective-permute-start(bf16[2,608,128]{2,1,0:T(8,128)(2,1)S(1)} %collective-permute-done.25.refs_4_), channel_id=1, source_target_pairs={{0,16},{16,0},{1,17},{17,1},{2,18},{18,2},{3,19},{19,3},{4,20},{20... | collective-permute-start | bytes 933896 | tf_op jit(solution)/shard_map/ppermute | solution.py:36
  121.1 25.9 %collective-permute-start.30 = (bf16[2,608,128]{2,1,0:T(8,128)(2,1)S(1)}, bf16[2,608,128]{2,1,0:T(8,128)(2,1)S(1)}, u32[]{:S(2)}, u32[]{:S(2)}) collective-permute-start(bf16[2,608,128]{2,1,0:T(8,128)(2,1)S(1)} %collective-permute-done.26.refs_5_), channel_id=1, source_target_pairs={{0,16},{16,0},{1,17},{17,1},{2,18},{18,2},{3,19},{19,3},{4,20},{20... | collective-permute-start | bytes 933896 | tf_op jit(solution)/shard_map/ppermute | solution.py:36

commit v10 on v8

--- a/solution.py
+++ b/solution.py
@@ -15,6 +15,7 @@
 F32, BF16 = jnp.float32, jnp.bfloat16
 WHOLE = pl.BlockSpec(memory_space=pltpu.VMEM)
 HELD = pl.BlockSpec(memory_space=pltpu.HBM)
+ANYWHERE = pl.BlockSpec(memory_space=pl.ANY)
 SCALARS = pl.BlockSpec(memory_space=pltpu.SMEM)
 
 
@@ -562,7 +563,7 @@
     return pl.pallas_call(
         functools.partial(zero_grad_kernel, blocks, first, count),
         out_shape=struct((rows, features), F32),
-        in_specs=[SCALARS] * 2 + [HELD] * (2 * count + len(flat)) + [WHOLE] * len(extra),
+        in_specs=[SCALARS] * 2 + [ANYWHERE] * (2 * count + len(flat)) + [WHOLE] * len(extra),
         out_specs=HELD if extra else WHOLE,
         scratch_shapes=scratch,
         name=name,
@@ -629,21 +630,19 @@
     far, near, sent, kept, token_sums = lax.optimization_barrier((far, near, sent, kept, token_sums))
 
     gathers = [[far[0]], [jnp.stack(far[1:])]]
-    last = gather_dp(near[-1])[1:]
-    lasts = [last[0], jnp.stack(last[1:])]
+    cots = gather_dp(after(cot1, token_sums))
     for level in range(levels):
         got = steps(sent, level)
-        final = level + 1 == levels
-        for gather, end in zip(gathers, lasts):
-            gather += steps(gather[:-1], level) + [end] if final else steps(gather, level)
+        gathers = [gather + steps(gather, level) for gather in gathers]
         if level == 0:
-            cot1, near = after((cot1, near), got)
-            cots = gather_dp(cot1)
+            got, gathers, cots = lax.optimization_barrier((got, gathers, cots))
+        if level + 1 < levels:
+            sent, kept, token_sums = fold(got, kept, token_sums)
+        if level == 0:
+            near = after(near, sent[0])
             near_other = [swap_grp(value) for value in near]
+            cots_other = [swap_grp(value) for value in cots]
             residual = residual_rows(order, zero_weight, near)
-        if not final:
-            sent, kept, token_sums = fold(got, kept, token_sums)
-    cots_other = [swap_grp(value) for value in cots]
     more = unpack_sums(got[0][-16:])
     plain, along = token_sums[0:1] + more[0], token_sums[1:2] + more[1]
     kept = [kept[0] + got[0][:rows].astype(F32)]

time: 147 us -> 134 us (0.912)
  local copies, waits for them, and re-layouts: 15.3 us -> 8.22 us
  waiting for transfers between devices: 25.4 us -> 21.8 us
  starting transfers between devices: 42.5 us -> 41 us
    ppermute x9 -> x6, waiting for transfers between devices: 18.7 us -> 8.46 us  [gather_dp(): lax.ppermute(value, 'dp', [(i, i ^ mask) for i in range(length)])]
    unnamed x113 -> x65, local copies, waits for them, and re-layouts: 15.3 us -> 8.2 us
    ppermute x7 -> x9, waiting for transfers between devices: 2.53 us -> 8.41 us  [step(): return lax.ppermute(value, ('grp', 'fsdp'), pairs)]
    ppermute x9 -> x6, starting transfers between devices: 12.8 us -> 11.1 us  [gather_dp(): lax.ppermute(value, 'dp', [(i, i ^ mask) for i in range(length)])]
    ppermute x7 -> x9, starting transfers between devices: 10.7 us -> 10.6 us  [step(): return lax.ppermute(value, ('grp', 'fsdp'), pairs)]
  transfers between devices with their start and end apart: 48 -> 47, of which waited for: 13 -> 13; matrix products, arithmetic and copies ran while one was open for 2% -> 4% of each run, Pallas kernels for 34% -> 33%
where the time goes in v10:
time: 134 us; the launch traced here: 133 us
  Pallas kernels  52.4 us (39%)
  starting transfers between devices  41 us (31%)
  waiting for transfers between devices  21.8 us (16%)
  other arithmetic  8.7 us (6%)
  local copies, waits for them, and re-layouts  8.22 us (6%)
    ppermute x12, starting transfers between devices, send(): return lax.ppermute(value, ('grp', 'fsdp'), pairs)  15.1 us
    pallas_call x1, Pallas kernels, backward_first(): pl.pallas_call(functools.partial(backward_first_kernel, blocks, part), ou...  11.7 us
    pallas_call x1, Pallas kernels, forward_last(): pl.pallas_call(functools.partial(forward_last_kernel, start), out_shape=[...  11.3 us
    ppermute x6, starting transfers between devices, gather_dp(): lax.ppermute(value, 'dp', [(i, i ^ mask) for i in range(length)])  11.1 us
    ppermute x9, starting transfers between devices, step(): return lax.ppermute(value, ('grp', 'fsdp'), pairs)  10.6 us
    pallas_call x2, Pallas kernels, zero_projection_grad(): pl.pallas_call(functools.partial(zero_grad_kernel, blocks, first, count),...  8.55 us
    ppermute x6, waiting for transfers between devices, gather_dp(): lax.ppermute(value, 'dp', [(i, i ^ mask) for i in range(length)])  8.46 us
    ppermute x9, waiting for transfers between devices, step(): return lax.ppermute(value, ('grp', 'fsdp'), pairs)  8.41 us
  transfers between devices with their start and end apart: 47, of which 13 were waited for; matrix products, arithmetic and copies ran while one was open for 4% of the time, Pallas kernels for 33%

profile of v10, /device:TPU:0, one launch (start us, length us, event | category | flops | bytes accessed | tf_op | source)
XLA Modules:
  0.0 133.4 jit_solution(10684063018172063622)
XLA Ops:
  1.1 0.8 copy.13.modulation
  1.9 0.7 fusion.14
  2.7 1.0 copy-done.4
  3.6 4.0 %prepare.1 = (f32[608,128]{1,0:T(8,128)S(1)}, bf16[608,128]{1,0:T(8,128)(2,1)S(1)}, bf16[608,128]{1,0:T(8,128)(2,1)S(1)}, bf16[608,128]{1,0:T(8,128)(2,1)S(1)}, ...) custom-call(s32[9]{0:T(128)S(1)} %pad_add_fusion.order, ...), custom_call_target="tpu_custom_call" | custom-call | flops 378535936 | bytes 4202496 | tf_op jit(solution)/shard_map/prepare/pallas_call | solution.py:451
  7.6 2.9 %collective-permute-start.1 = (bf16[608,128]{1,0:T(8,128)(2,1)S(1)}, bf16[608,128]{1,0:T(8,128)(2,1)S(1)}, u32[]{:S(2)}, u32[]{:S(2)}) collective-permute-start(bf16[608,128]{1,0:T(8,128)(2,1)S(1)} %get-tuple-element.73), channel_id=1, source_target_pairs={{0,4},{4,0},{8,12},{12,8},{16,24},{20,28},{24,16},{28,20},{1,5},{5... | collective-permute-start | bytes 466952 | tf_op jit(solution)/shard_map/ppermute | solution.py:64
  10.5 1.5 %collective-permute-start.2 = (bf16[608,128]{1,0:T(8,128)(2,1)S(1)}, bf16[608,128]{1,0:T(8,128)(2,1)S(1)}, u32[]{:S(2)}, u32[]{:S(2)}) collective-permute-start(bf16[608,128]{1,0:T(8,128)(2,1)S(1)} %get-tuple-element.74), channel_id=1, source_target_pairs={{0,8},{4,12},{8,0},{12,4},{16,20},{20,16},{24,28},{28,24},{1,9},{5... | collective-permute-start | bytes 466952 | tf_op jit(solution)/shard_map/ppermute | solution.py:64
  12.0 7.4 %forward_first.1 = (f32[256,1024]{1,0:T(8,128)S(1)}, f32[256,2432]{1,0:T(8,128)}, f32[2432,8]{1,0:T(8,128)S(1)}) custom-call(bf16[256,2432]{1,0:T(8,128)(2,1)S(1)} %get-tuple-element.84.normed, f32[1,3,2432]{2,1,0:T(4,128)S(1)} %copy.13.modulation, bf16[1,2432,2432]{2,1,0:T(8,128)(2,1)} %w_in.5, bf16[1,2432,2432]{2,1,0:T(8,128)(2,1)} %w_out.5), custom_call_target="tpu_custom_call" | custom-call | flops 2550136832 | bytes 12451840 | tf_op jit(solution)/shard_map/forward_first/pallas_call | solution.py:254
  19.5 0.9 add_add_fusion
  20.9 1.5 %collective-permute-done.4 = f32[608,128]{1,0:T(8,128)} collective-permute-done((f32[608,128]{1,0:T(8,128)}, f32[608,128]{1,0:T(8,128)}, u32[]{:S(2)}, u32[]{:S(2)}) %collective-permute-start.4) | collective-permute-done | bytes 311328 | tf_op jit(solution)/shard_map/ppermute | solution.py:36
  22.4 1.3 multiply_convert_fusion.refs_0_
  23.7 3.0 %collective-permute-start.10 = (bf16[608,256]{1,0:T(8,128)(2,1)S(1)}, bf16[608,256]{1,0:T(8,128)(2,1)S(1)}, u32[]{:S(2)}, u32[]{:S(2)}) collective-permute-start(bf16[608,256]{1,0:T(8,128)(2,1)S(1)} %multiply_convert_fusion.refs_0_), channel_id=1, source_target_pairs={{0,12},{4,8},{8,4},{12,0},{16,28},{20,24},{24,20},{28,16},{1,13},{... | collective-permute-start | bytes 933896 | tf_op jit(solution)/shard_map/ppermute | solution.py:64
  27.3 11.3 %forward_last.1 = (f32[256,1408]{1,0:T(8,128)}, f32[608,256]{1,0:T(8,128)S(1)}, bf16[608,256]{1,0:T(8,128)(2,1)S(1)}, bf16[608,256]{1,0:T(8,128)(2,1)S(1)}, bf16[608,256]{1,0:T(8,128)(2,1)S(1)}) custom-call(s32[9]{0:T(128)S(1)} %pad_add_fusion.order, bf16[256,2432]{1,0:T(8,128)(2,1)S(1)} %get-tuple-element.84.normed, f32[256,2432]{1,0:T(8,128)} %get-tuple-element.80.before, ...), custom_call_target="tpu_custom_call" | custom-call | flops 3506438144 | bytes 16187392 | tf_op jit(solution)/shard_map/forward_last/pallas_call | solution.py:268
  38.7 1.9 %collective-permute-start.5 = (bf16[608,256]{1,0:T(8,128)(2,1)S(1)}, bf16[608,256]{1,0:T(8,128)(2,1)S(1)}, u32[]{:S(2)}, u32[]{:S(2)}) collective-permute-start(bf16[608,256]{1,0:T(8,128)(2,1)S(1)} %get-tuple-element.86), channel_id=1, source_target_pairs={{0,4},{4,0},{8,12},{12,8},{16,24},{20,28},{24,16},{28,20},{1,5},{5... | collective-permute-start | bytes 933896 | tf_op jit(solution)/shard_map/ppermute | solution.py:64
  40.6 1.5 %collective-permute-start.6 = (bf16[608,256]{1,0:T(8,128)(2,1)S(1)}, bf16[608,256]{1,0:T(8,128)(2,1)S(1)}, u32[]{:S(2)}, u32[]{:S(2)}) collective-permute-start(bf16[608,256]{1,0:T(8,128)(2,1)S(1)} %get-tuple-element.87), channel_id=1, source_target_pairs={{0,8},{4,12},{8,0},{12,4},{16,20},{20,16},{24,28},{28,24},{1,9},{5... | collective-permute-start | bytes 933896 | tf_op jit(solution)/shard_map/ppermute | solution.py:64
  42.2 11.7 %backward_first.1 = (bf16[256,2432]{1,0:T(8,128)(2,1)S(1)}, f32[256,2432]{1,0:T(8,128)}) custom-call(s32[9]{0:T(128)S(1)} %pad_add_fusion.order, bf16[608,256]{1,0:T(8,128)(2,1)S(1)} %multiply_convert_fusion.refs_0_, bf16[608,256]{1,0:T(8,128)(2,1)S(1)} %collective-permute-done.8.refs_1_, bf16[608,256]{1,0:T(8,128)(2,1)S(1)} %collective-permute-done.9.refs_2_, ...), custom_call_target="tpu_custom_call" | custom-call | flops 5100273664 | bytes 22413312 | tf_op jit(solution)/shard_map/backward_first/pallas_call | solution.py:326
  53.9 1.0 copy-done.6
  55.4 2.1 %fusion.16 = (bf16[608,256]{1,0:T(8,128)(2,1)S(1)}, f32[608,256]{1,0:T(8,128)}) fusion(f32[608,256]{1,0:T(8,128)S(1)} %get-tuple-element.85, bf16[608,256]{1,0:T(8,128)(2,1)S(1)} %collective-permute-done.7, bf16[608,256]{1,0:T(8,128)(2,1)S(1)} %collective-permute-done.6, bf16[608,256]{1,0:T(8,128)(2,1)S(1)} %collective-permute-done.5, ...), kind=kLoop, calls=%fused_computation.35 | loop fusion | flops 1556480 | bytes 2804100 | tf_op jit(solution)/shard_map/convert_element_type | solution.py:622
  57.6 1.4 %collective-permute-done.11 = bf16[608,128]{1,0:T(8,128)(2,1)S(1)} collective-permute-done((bf16[608,128]{1,0:T(8,128)(2,1)S(1)}, bf16[608,128]{1,0:T(8,128)(2,1)S(1)}, u32[]{:S(2)}, u32[]{:S(2)}) %collective-permute-start.11) | collective-permute-done | bytes 155680 | tf_op jit(solution)/shard_map/ppermute | solution.py:36
  59.0 2.6 %collective-permute-start.17 = (bf16[608,128]{1,0:T(8,128)(2,1)S(1)}, bf16[608,128]{1,0:T(8,128)(2,1)}, u32[]{:S(2)}, u32[]{:S(2)}) collective-permute-start(bf16[608,128]{1,0:T(8,128)(2,1)S(1)} %slice_select_fusion.refs_0_.refs_4_), channel_id=1, source_target_pairs={{0,12},{4,8},{8,4},{12,0},{16,28},{20,24},{24,20},{28,16},{1,13},{... | collective-permute-start | bytes 466952 | tf_op jit(solution)/shard_map/ppermute | solution.py:64
  62.6 3.7 %collective-permute-start.14 = (bf16[608,128]{1,0:T(8,128)(2,1)S(1)}, bf16[608,128]{1,0:T(8,128)(2,1)S(1)}, u32[]{:S(2)}, u32[]{:S(2)}) collective-permute-start(bf16[608,128]{1,0:T(8,128)(2,1)S(1)} %slice_select_fusion.refs_0_.refs_4_), channel_id=1, source_target_pairs={{0,3},{1,2},{2,1},{3,0},{4,7},{5,6},{6,5},{7,4},{8,11},{9,10},{10,... | collective-permute-start | bytes 466952 | tf_op jit(solution)/shard_map/ppermute | solution.py:70
  66.3 0.7 collective-permute-done.17.refs_3_.refs_7_
  66.9 1.7 %collective-permute-start.12 = (bf16[608,128]{1,0:T(8,128)(2,1)S(1)}, bf16[608,128]{1,0:T(8,128)(2,1)}, u32[]{:S(2)}, u32[]{:S(2)}) collective-permute-start(bf16[608,128]{1,0:T(8,128)(2,1)S(1)} %slice_select_fusion.refs_0_.refs_4_), channel_id=1, source_target_pairs={{0,1},{1,0},{2,3},{3,2},{4,5},{5,4},{6,7},{7,6},{8,9},{9,8},{10,11... | collective-permute-start | bytes 466952 | tf_op jit(solution)/shard_map/ppermute | solution.py:70
  68.6 7.3 %backward_last.1 = (bf16[624,256]{1,0:T(8,128)(2,1)S(1)}, bf16[624,256]{1,0:T(8,128)(2,1)S(1)}, f32[608,256]{1,0:T(8,128)S(1)}, f32[608,256]{1,0:T(8,128)S(1)}, f32[2,256]{1,0:T(2,128)S(1)}) custom-call(s32[9]{0:T(128)S(1)} %pad_add_fusion.order, bf16[256,2432]{1,0:T(8,128)(2,1)} %copy-done.6, f32[256,2432]{1,0:T(8,128)} %get-tuple-element.98.before, ...), custom_call_target="tpu_custom_call" | custom-call | flops 956301312 | bytes 6225920 | tf_op jit(solution)/shard_map/backward_last/pallas_call | solution.py:379
  76.0 2.9 %collective-permute-done.13 = bf16[608,128]{1,0:T(8,128)(2,1)S(1)} collective-permute-done((bf16[608,128]{1,0:T(8,128)(2,1)S(1)}, bf16[608,128]{1,0:T(8,128)(2,1)S(1)}, u32[]{:S(2)}, u32[]{:S(2)}) %collective-permute-start.13) | collective-permute-done | bytes 155680 | tf_op jit(solution)/shard_map/ppermute | solution.py:70
  78.9 2.5 %collective-permute-start.24 = (bf16[608,128]{1,0:T(8,128)(2,1)}, bf16[608,128]{1,0:T(8,128)(2,1)S(1)}, u32[]{:S(2)}, u32[]{:S(2)}) collective-permute-start(bf16[608,128]{1,0:T(8,128)(2,1)} %get-tuple-element.137.refs_0_), channel_id=1, source_target_pairs={{0,3},{1,2},{2,1},{3,0},{4,7},{5,6},{6,5},{7,4},{8,11},{9,10},{10,... | collective-permute-start | bytes 466952 | tf_op jit(solution)/shard_map/ppermute | solution.py:70
  81.5 1.4 %collective-permute-start.18 = (bf16[624,256]{1,0:T(8,128)(2,1)S(1)}, bf16[624,256]{1,0:T(8,128)(2,1)S(1)}, u32[]{:S(2)}, u32[]{:S(2)}) collective-permute-start(bf16[624,256]{1,0:T(8,128)(2,1)S(1)} %get-tuple-element.114), channel_id=1, source_target_pairs={{0,4},{4,0},{8,12},{12,8},{16,24},{20,28},{24,16},{28,20},{1,5},{5... | collective-permute-start | bytes 958472 | tf_op jit(solution)/shard_map/ppermute | solution.py:48
  83.5 1.5 %collective-permute-start.21 = (bf16[2,608,128]{2,1,0:T(8,128)(2,1)S(1)}, bf16[2,608,128]{2,1,0:T(8,128)(2,1)S(1)}, u32[]{:S(2)}, u32[]{:S(2)}) collective-permute-start(bf16[2,608,128]{2,1,0:T(8,128)(2,1)S(1)} %pad_maximum_fusion.refs_4_), channel_id=1, source_target_pairs={{0,4},{4,0},{8,12},{12,8},{16,24},{20,28},{24,16},{28,20},{1,5},{5... | collective-permute-start | bytes 933896 | tf_op jit(solution)/shard_map/ppermute | solution.py:48
  85.0 2.9 %collective-permute-done.24.refs_1_ = bf16[608,128]{1,0:T(8,128)(2,1)S(1)} collective-permute-done((bf16[608,128]{1,0:T(8,128)(2,1)}, bf16[608,128]{1,0:T(8,128)(2,1)S(1)}, u32[]{:S(2)}, u32[]{:S(2)}) %collective-permute-start.24) | collective-permute-done | bytes 155680 | tf_op jit(solution)/shard_map/ppermute | solution.py:70
  87.9 3.1 %collective-permute-start.22 = (bf16[608,128]{1,0:T(8,128)(2,1)}, bf16[608,128]{1,0:T(8,128)(2,1)}, u32[]{:S(2)}, u32[]{:S(2)}) collective-permute-start(bf16[608,128]{1,0:T(8,128)(2,1)} %get-tuple-element.137.refs_0_), channel_id=1, source_target_pairs={{0,1},{1,0},{2,3},{3,2},{4,5},{5,4},{6,7},{7,6},{8,9},{9,8},{10,11... | collective-permute-start | bytes 466952 | tf_op jit(solution)/shard_map/ppermute | solution.py:70
  91.1 2.5 %collective-permute-done.23.refs_0_ = bf16[608,128]{1,0:T(8,128)(2,1)S(1)} collective-permute-done((bf16[608,128]{1,0:T(8,128)(2,1)}, bf16[608,128]{1,0:T(8,128)(2,1)S(1)}, u32[]{:S(2)}, u32[]{:S(2)}) %collective-permute-start.23) | collective-permute-done | bytes 155680 | tf_op jit(solution)/shard_map/ppermute | solution.py:70
  93.5 1.5 %collective-permute-start.20 = (bf16[608,128]{1,0:T(8,128)(2,1)}, bf16[608,128]{1,0:T(8,128)(2,1)}, u32[]{:S(2)}, u32[]{:S(2)}) collective-permute-start(bf16[608,128]{1,0:T(8,128)(2,1)} %collective-permute-done.12.refs_12_), channel_id=1, source_target_pairs={{0,4},{4,0},{8,12},{12,8},{16,24},{20,28},{24,16},{28,20},{1,5},{5... | collective-permute-start | bytes 466952 | tf_op jit(solution)/shard_map/ppermute | solution.py:48
  95.2 3.8 %collective-permute-done.20.refs_13_ = bf16[608,128]{1,0:T(8,128)(2,1)} collective-permute-done((bf16[608,128]{1,0:T(8,128)(2,1)}, bf16[608,128]{1,0:T(8,128)(2,1)}, u32[]{:S(2)}, u32[]{:S(2)}) %collective-permute-start.20) | collective-permute-done | bytes 155680 | tf_op jit(solution)/shard_map/ppermute | solution.py:48
  99.2 0.8 copy-done.13
  100.1 0.7 copy-done.27
  102.2 0.7 copy-done.17
  103.0 0.7 copy-done.19
  103.7 1.5 %collective-permute-start.41 = (bf16[608,128]{1,0:T(8,128)(2,1)}, bf16[608,128]{1,0:T(8,128)(2,1)}, u32[]{:S(2)}, u32[]{:S(2)}) collective-permute-start(bf16[608,128]{1,0:T(8,128)(2,1)} %collective-permute-done.12.refs_12_), channel_id=1, source_target_pairs={{0,8},{4,12},{8,0},{12,4},{16,20},{20,16},{24,28},{28,24},{1,9},{5... | collective-permute-start | bytes 466952 | tf_op jit(solution)/shard_map/ppermute | solution.py:48
  106.4 0.9 copy-done.8
  107.3 0.9 copy-done.11
  108.2 2.0 %residual_rows.1 = f32[608,128]{1,0:T(8,128)S(1)} custom-call(s32[9]{0:T(128)S(1)} %pad_add_fusion.order, bf16[608,2432]{1,0:T(8,128)(2,1)S(1)} %copy-done, bf16[608,128]{1,0:T(8,128)(2,1)S(1)} %slice_select_fusion.refs_0_.refs_4_, bf16[608,128]{1,0:T(8,128)(2,1)S(1)} %copy-done.11, bf16[608,128]{1,0:T(8,128)(2,1)S(1)} %copy-done.8, ...), custom_call_target="tpu_custom_call" | custom-call | flops 378535936 | bytes 4202496 | tf_op jit(solution)/shard_map/residual_rows/pallas_call | solution.py:483
  112.1 1.5 %collective-permute-start.29 = (bf16[2,608,128]{2,1,0:T(8,128)(2,1)S(1)}, bf16[2,608,128]{2,1,0:T(8,128)(2,1)S(1)}, u32[]{:S(2)}, u32[]{:S(2)}) collective-permute-start(bf16[2,608,128]{2,1,0:T(8,128)(2,1)S(1)} %pad_maximum_fusion.refs_4_), channel_id=1, source_target_pairs={{0,8},{4,12},{8,0},{12,4},{16,20},{20,16},{24,28},{28,24},{1,9},{5... | collective-permute-start | bytes 933896 | tf_op jit(solution)/shard_map/ppermute | solution.py:48
  113.7 0.7 collective-permute-start.26
  114.4 1.3 collective-permute-start.30
  115.7 4.1 %zero_projection_grad_first.1.refs_12_ = f32[608,2432]{1,0:T(8,128)S(1)} custom-call(s32[9]{0:T(128)S(1)} %pad_add_fusion.order, s32[4]{0:T(128)S(1)} %iota_xor_fusion.dp_order, bf16[608,128]{1,0:T(8,128)(2,1)} %get-tuple-element.137.refs_0_, bf16[608,128]{1,0:T(8,128)(2,1)} %collective-permute-done.22.refs_1_, ...), custom_call_target="tpu_custom_call" | custom-call | flops 1514143744 | bytes 9027584 | tf_op jit(solution)/shard_map/zero_projection_grad_first/pallas_call | solution.py:563
  120.0 0.8 fusion.8
  121.3 4.5 %collective-permute-done.30.refs_7_ = bf16[2,608,128]{2,1,0:T(8,128)(2,1)S(1)} collective-permute-done((bf16[2,608,128]{2,1,0:T(8,128)(2,1)S(1)}, bf16[2,608,128]{2,1,0:T(8,128)(2,1)S(1)}, u32[]{:S(2)}, u32[]{:S(2)}) %collective-permute-start.30) | collective-permute-done | bytes 311328 | tf_op jit(solution)/shard_map/ppermute | solution.py:48
  126.5 2.3 %fusion.5 = f32[1,608,256]{2,1,0:T(8,128)} fusion(f32[608,256]{1,0:T(8,128)S(1)} %copy-done.14, f32[608,128]{1,0:T(8,128)} %collective-permute-done.4, f32[608,128]{1,0:T(8,128)} %add_add_fusion, bf16[624,256]{1,0:T(8,128)(2,1)S(1)} %collective-permute-done.26, f32[256]{0:T(256)S(1)} %bitcast.24, f32[256]{0:T(256)S(1)} %bitcast.26, f32[256]{0:T(256)S(1)} %bitcast.23, ...), kind=kLoop, calls=%fused_computation.7 | loop fusion | flops 2179072 | bytes 2808197 | tf_op jit(solution)/shard_map/broadcast_in_dim | solution.py:663
  128.8 4.5 %zero_projection_grad_last.1 = f32[608,2432]{1,0:T(8,128)} custom-call(s32[9]{0:T(128)S(1)} %pad_add_fusion.order, s32[4]{0:T(128)S(1)} %iota_xor_fusion.dp_order, bf16[608,128]{1,0:T(8,128)(2,1)S(1)} %copy-done.26, bf16[608,128]{1,0:T(8,128)(2,1)S(1)} %copy-done.24, bf16[608,128]{1,0:T(8,128)(2,1)S(1)} %collective-permute-done.27.refs_2_, ...), custom_call_target="tpu_custom_call" | custom-call | flops 1514143744 | bytes 9027584 | tf_op jit(solution)/shard_map/zero_projection_grad_last/pallas_call | solution.py:563
  (135 shorter events, 10.1 us)
Async XLA Ops:
  0.6 2.0 %collective-permute-start = (bf16[608,256]{1,0:T(8,128)(2,1)}, bf16[608,256]{1,0:T(8,128)(2,1)S(1)}, u32[]{:S(2)}, u32[]{:S(2)}) collective-permute-start(bf16[608,256]{1,0:T(8,128)(2,1)} %bitcast.19), channel_id=1, source_target_pairs={{0,16},{16,0},{1,17},{17,1},{2,18},{18,2},{3,19},{19,3},{4,20},{20... | collective-permute-start | bytes 933896 | tf_op jit(solution)/shard_map/ppermute | solution.py:36
  7.6 11.8 %collective-permute-start.1 = (bf16[608,128]{1,0:T(8,128)(2,1)S(1)}, bf16[608,128]{1,0:T(8,128)(2,1)S(1)}, u32[]{:S(2)}, u32[]{:S(2)}) collective-permute-start(bf16[608,128]{1,0:T(8,128)(2,1)S(1)} %get-tuple-element.73), channel_id=1, source_target_pairs={{0,4},{4,0},{8,12},{12,8},{16,24},{20,28},{24,16},{28,20},{1,5},{5... | collective-permute-start | bytes 466952 | tf_op jit(solution)/shard_map/ppermute | solution.py:64
  10.5 9.0 %collective-permute-start.2 = (bf16[608,128]{1,0:T(8,128)(2,1)S(1)}, bf16[608,128]{1,0:T(8,128)(2,1)S(1)}, u32[]{:S(2)}, u32[]{:S(2)}) collective-permute-start(bf16[608,128]{1,0:T(8,128)(2,1)S(1)} %get-tuple-element.74), channel_id=1, source_target_pairs={{0,8},{4,12},{8,0},{12,4},{16,20},{20,16},{24,28},{28,24},{1,9},{5... | collective-permute-start | bytes 466952 | tf_op jit(solution)/shard_map/ppermute | solution.py:64
  12.0 7.5 %collective-permute-start.3 = (bf16[608,128]{1,0:T(8,128)(2,1)S(1)}, bf16[608,128]{1,0:T(8,128)(2,1)S(1)}, u32[]{:S(2)}, u32[]{:S(2)}) collective-permute-start(bf16[608,128]{1,0:T(8,128)(2,1)S(1)} %get-tuple-element.75), channel_id=1, source_target_pairs={{0,12},{4,8},{8,4},{12,0},{16,28},{20,24},{24,20},{28,16},{1,13},{... | collective-permute-start | bytes 466952 | tf_op jit(solution)/shard_map/ppermute | solution.py:64
  20.4 1.9 %collective-permute-start.4 = (f32[608,128]{1,0:T(8,128)}, f32[608,128]{1,0:T(8,128)}, u32[]{:S(2)}, u32[]{:S(2)}) collective-permute-start(f32[608,128]{1,0:T(8,128)} %add_add_fusion), channel_id=1, source_target_pairs={{0,16},{16,0},{1,17},{17,1},{2,18},{18,2},{3,19},{19,3},{4,20},{20... | collective-permute-start | bytes 933896 | tf_op jit(solution)/shard_map/ppermute | solution.py:36
  23.7 18.4 %collective-permute-start.10 = (bf16[608,256]{1,0:T(8,128)(2,1)S(1)}, bf16[608,256]{1,0:T(8,128)(2,1)S(1)}, u32[]{:S(2)}, u32[]{:S(2)}) collective-permute-start(bf16[608,256]{1,0:T(8,128)(2,1)S(1)} %multiply_convert_fusion.refs_0_), channel_id=1, source_target_pairs={{0,12},{4,8},{8,4},{12,0},{16,28},{20,24},{24,20},{28,16},{1,13},{... | collective-permute-start | bytes 933896 | tf_op jit(solution)/shard_map/ppermute | solution.py:64
  26.7 15.5 %collective-permute-start.9 = (bf16[608,256]{1,0:T(8,128)(2,1)S(1)}, bf16[608,256]{1,0:T(8,128)(2,1)S(1)}, u32[]{:S(2)}, u32[]{:S(2)}) collective-permute-start(bf16[608,256]{1,0:T(8,128)(2,1)S(1)} %multiply_convert_fusion.refs_0_), channel_id=1, source_target_pairs={{0,8},{4,12},{8,0},{12,4},{16,20},{20,16},{24,28},{28,24},{1,9},{5... | collective-permute-start | bytes 933896 | tf_op jit(solution)/shard_map/ppermute | solution.py:64
  27.2 15.1 %collective-permute-start.8 = (bf16[608,256]{1,0:T(8,128)(2,1)S(1)}, bf16[608,256]{1,0:T(8,128)(2,1)S(1)}, u32[]{:S(2)}, u32[]{:S(2)}) collective-permute-start(bf16[608,256]{1,0:T(8,128)(2,1)S(1)} %multiply_convert_fusion.refs_0_), channel_id=1, source_target_pairs={{0,4},{4,0},{8,12},{12,8},{16,24},{20,28},{24,16},{28,20},{1,5},{5... | collective-permute-start | bytes 933896 | tf_op jit(solution)/shard_map/ppermute | solution.py:64
  38.7 16.3 %collective-permute-start.5 = (bf16[608,256]{1,0:T(8,128)(2,1)S(1)}, bf16[608,256]{1,0:T(8,128)(2,1)S(1)}, u32[]{:S(2)}, u32[]{:S(2)}) collective-permute-start(bf16[608,256]{1,0:T(8,128)(2,1)S(1)} %get-tuple-element.86), channel_id=1, source_target_pairs={{0,4},{4,0},{8,12},{12,8},{16,24},{20,28},{24,16},{28,20},{1,5},{5... | collective-permute-start | bytes 933896 | tf_op jit(solution)/shard_map/ppermute | solution.py:64
  40.6 14.4 %collective-permute-start.6 = (bf16[608,256]{1,0:T(8,128)(2,1)S(1)}, bf16[608,256]{1,0:T(8,128)(2,1)S(1)}, u32[]{:S(2)}, u32[]{:S(2)}) collective-permute-start(bf16[608,256]{1,0:T(8,128)(2,1)S(1)} %get-tuple-element.87), channel_id=1, source_target_pairs={{0,8},{4,12},{8,0},{12,4},{16,20},{20,16},{24,28},{28,24},{1,9},{5... | collective-permute-start | bytes 933896 | tf_op jit(solution)/shard_map/ppermute | solution.py:64
  42.1 13.3 %collective-permute-start.7 = (bf16[608,256]{1,0:T(8,128)(2,1)S(1)}, bf16[608,256]{1,0:T(8,128)(2,1)S(1)}, u32[]{:S(2)}, u32[]{:S(2)}) collective-permute-start(bf16[608,256]{1,0:T(8,128)(2,1)S(1)} %get-tuple-element.88), channel_id=1, source_target_pairs={{0,12},{4,8},{8,4},{12,0},{16,28},{20,24},{24,20},{28,16},{1,13},{... | collective-permute-start | bytes 933896 | tf_op jit(solution)/shard_map/ppermute | solution.py:64
  57.5 1.4 %collective-permute-start.11 = (bf16[608,128]{1,0:T(8,128)(2,1)S(1)}, bf16[608,128]{1,0:T(8,128)(2,1)S(1)}, u32[]{:S(2)}, u32[]{:S(2)}) collective-permute-start(bf16[608,128]{1,0:T(8,128)(2,1)S(1)} %slice.65), channel_id=1, source_target_pairs={{0,16},{16,0},{1,17},{17,1},{2,18},{18,2},{3,19},{19,3},{4,20},{20... | collective-permute-start | bytes 466952 | tf_op jit(solution)/shard_map/ppermute | solution.py:36
  59.0 7.9 %collective-permute-start.17 = (bf16[608,128]{1,0:T(8,128)(2,1)S(1)}, bf16[608,128]{1,0:T(8,128)(2,1)}, u32[]{:S(2)}, u32[]{:S(2)}) collective-permute-start(bf16[608,128]{1,0:T(8,128)(2,1)S(1)} %slice_select_fusion.refs_0_.refs_4_), channel_id=1, source_target_pairs={{0,12},{4,8},{8,4},{12,0},{16,28},{20,24},{24,20},{28,16},{1,13},{... | collective-permute-start | bytes 466952 | tf_op jit(solution)/shard_map/ppermute | solution.py:64
  61.6 14.4 %collective-permute-start.16 = (bf16[608,128]{1,0:T(8,128)(2,1)S(1)}, bf16[608,128]{1,0:T(8,128)(2,1)S(1)}, u32[]{:S(2)}, u32[]{:S(2)}) collective-permute-start(bf16[608,128]{1,0:T(8,128)(2,1)S(1)} %slice_select_fusion.refs_0_.refs_4_), channel_id=1, source_target_pairs={{0,8},{4,12},{8,0},{12,4},{16,20},{20,16},{24,28},{28,24},{1,9},{5... | collective-permute-start | bytes 466952 | tf_op jit(solution)/shard_map/ppermute | solution.py:64
  62.1 13.9 %collective-permute-start.15 = (bf16[608,128]{1,0:T(8,128)(2,1)S(1)}, bf16[608,128]{1,0:T(8,128)(2,1)S(1)}, u32[]{:S(2)}, u32[]{:S(2)}) collective-permute-start(bf16[608,128]{1,0:T(8,128)(2,1)S(1)} %slice_select_fusion.refs_0_.refs_4_), channel_id=1, source_target_pairs={{0,4},{4,0},{8,12},{12,8},{16,24},{20,28},{24,16},{28,20},{1,5},{5... | collective-permute-start | bytes 466952 | tf_op jit(solution)/shard_map/ppermute | solution.py:64
  62.6 13.5 %collective-permute-start.14 = (bf16[608,128]{1,0:T(8,128)(2,1)S(1)}, bf16[608,128]{1,0:T(8,128)(2,1)S(1)}, u32[]{:S(2)}, u32[]{:S(2)}) collective-permute-start(bf16[608,128]{1,0:T(8,128)(2,1)S(1)} %slice_select_fusion.refs_0_.refs_4_), channel_id=1, source_target_pairs={{0,3},{1,2},{2,1},{3,0},{4,7},{5,6},{6,5},{7,4},{8,11},{9,10},{10,... | collective-permute-start | bytes 466952 | tf_op jit(solution)/shard_map/ppermute | solution.py:70
  66.3 12.6 %collective-permute-start.13 = (bf16[608,128]{1,0:T(8,128)(2,1)S(1)}, bf16[608,128]{1,0:T(8,128)(2,1)S(1)}, u32[]{:S(2)}, u32[]{:S(2)}) collective-permute-start(bf16[608,128]{1,0:T(8,128)(2,1)S(1)} %slice_select_fusion.refs_0_.refs_4_), channel_id=1, source_target_pairs={{0,2},{1,3},{2,0},{3,1},{4,6},{5,7},{6,4},{7,5},{8,10},{9,11},{10,... | collective-permute-start | bytes 466952 | tf_op jit(solution)/shard_map/ppermute | solution.py:70
  66.9 12.0 %collective-permute-start.12 = (bf16[608,128]{1,0:T(8,128)(2,1)S(1)}, bf16[608,128]{1,0:T(8,128)(2,1)}, u32[]{:S(2)}, u32[]{:S(2)}) collective-permute-start(bf16[608,128]{1,0:T(8,128)(2,1)S(1)} %slice_select_fusion.refs_0_.refs_4_), channel_id=1, source_target_pairs={{0,1},{1,0},{2,3},{3,2},{4,5},{5,4},{6,7},{7,6},{8,9},{9,8},{10,11... | collective-permute-start | bytes 466952 | tf_op jit(solution)/shard_map/ppermute | solution.py:70
  68.6 37.7 %copy-start = (bf16[608,2432]{1,0:T(8,128)(2,1)S(1)}, bf16[608,2432]{1,0:T(8,128)(2,1)}, u32[]{:S(2)}) copy-start(bf16[608,2432]{1,0:T(8,128)(2,1)} %weight.3) | copy-start | bytes 8871940
  78.9 9.0 %collective-permute-start.24 = (bf16[608,128]{1,0:T(8,128)(2,1)}, bf16[608,128]{1,0:T(8,128)(2,1)S(1)}, u32[]{:S(2)}, u32[]{:S(2)}) collective-permute-start(bf16[608,128]{1,0:T(8,128)(2,1)} %get-tuple-element.137.refs_0_), channel_id=1, source_target_pairs={{0,3},{1,2},{2,1},{3,0},{4,7},{5,6},{6,5},{7,4},{8,11},{9,10},{10,... | collective-permute-start | bytes 466952 | tf_op jit(solution)/shard_map/ppermute | solution.py:70
  81.5 12.1 %collective-permute-start.23 = (bf16[608,128]{1,0:T(8,128)(2,1)}, bf16[608,128]{1,0:T(8,128)(2,1)S(1)}, u32[]{:S(2)}, u32[]{:S(2)}) collective-permute-start(bf16[608,128]{1,0:T(8,128)(2,1)} %get-tuple-element.137.refs_0_), channel_id=1, source_target_pairs={{0,2},{1,3},{2,0},{3,1},{4,6},{5,7},{6,4},{7,5},{8,10},{9,11},{10,... | collective-permute-start | bytes 466952 | tf_op jit(solution)/shard_map/ppermute | solution.py:70
  81.5 17.6 %collective-permute-start.18 = (bf16[624,256]{1,0:T(8,128)(2,1)S(1)}, bf16[624,256]{1,0:T(8,128)(2,1)S(1)}, u32[]{:S(2)}, u32[]{:S(2)}) collective-permute-start(bf16[624,256]{1,0:T(8,128)(2,1)S(1)} %get-tuple-element.114), channel_id=1, source_target_pairs={{0,4},{4,0},{8,12},{12,8},{16,24},{20,28},{24,16},{28,20},{1,5},{5... | collective-permute-start | bytes 958472 | tf_op jit(solution)/shard_map/ppermute | solution.py:48
  82.9 16.2 %collective-permute-start.19 = (bf16[624,256]{1,0:T(8,128)(2,1)S(1)}, bf16[624,256]{1,0:T(8,128)(2,1)S(1)}, u32[]{:S(2)}, u32[]{:S(2)}) collective-permute-start(bf16[624,256]{1,0:T(8,128)(2,1)S(1)} %get-tuple-element.115), channel_id=1, source_target_pairs={{0,4},{4,0},{8,12},{12,8},{16,24},{20,28},{24,16},{28,20},{1,5},{5... | collective-permute-start | bytes 958472 | tf_op jit(solution)/shard_map/ppermute | solution.py:48
  83.5 15.5 %collective-permute-start.21 = (bf16[2,608,128]{2,1,0:T(8,128)(2,1)S(1)}, bf16[2,608,128]{2,1,0:T(8,128)(2,1)S(1)}, u32[]{:S(2)}, u32[]{:S(2)}) collective-permute-start(bf16[2,608,128]{2,1,0:T(8,128)(2,1)S(1)} %pad_maximum_fusion.refs_4_), channel_id=1, source_target_pairs={{0,4},{4,0},{8,12},{12,8},{16,24},{20,28},{24,16},{28,20},{1,5},{5... | collective-permute-start | bytes 933896 | tf_op jit(solution)/shard_map/ppermute | solution.py:48
  87.9 7.3 %collective-permute-start.22 = (bf16[608,128]{1,0:T(8,128)(2,1)}, bf16[608,128]{1,0:T(8,128)(2,1)}, u32[]{:S(2)}, u32[]{:S(2)}) collective-permute-start(bf16[608,128]{1,0:T(8,128)(2,1)} %get-tuple-element.137.refs_0_), channel_id=1, source_target_pairs={{0,1},{1,0},{2,3},{3,2},{4,5},{5,4},{6,7},{7,6},{8,9},{9,8},{10,11... | collective-permute-start | bytes 466952 | tf_op jit(solution)/shard_map/ppermute | solution.py:70
  93.5 5.5 %collective-permute-start.20 = (bf16[608,128]{1,0:T(8,128)(2,1)}, bf16[608,128]{1,0:T(8,128)(2,1)}, u32[]{:S(2)}, u32[]{:S(2)}) collective-permute-start(bf16[608,128]{1,0:T(8,128)(2,1)} %collective-permute-done.12.refs_12_), channel_id=1, source_target_pairs={{0,4},{4,0},{8,12},{12,8},{16,24},{20,28},{24,16},{28,20},{1,5},{5... | collective-permute-start | bytes 466952 | tf_op jit(solution)/shard_map/ppermute | solution.py:48
  100.8 1.4 %collective-permute-start.37 = (bf16[608,128]{1,0:T(8,128)(2,1)S(1)}, bf16[608,128]{1,0:T(8,128)(2,1)S(1)}, u32[]{:S(2)}, u32[]{:S(2)}) collective-permute-start(bf16[608,128]{1,0:T(8,128)(2,1)S(1)} %slice_select_fusion.refs_0_.refs_4_), channel_id=1, source_target_pairs={{0,16},{16,0},{1,17},{17,1},{2,18},{18,2},{3,19},{19,3},{4,20},{20... | collective-permute-start | bytes 466952 | tf_op jit(solution)/shard_map/ppermute | solution.py:36
  100.8 2.2 %collective-permute-start.38 = (bf16[608,128]{1,0:T(8,128)(2,1)S(1)}, bf16[608,128]{1,0:T(8,128)(2,1)S(1)}, u32[]{:S(2)}, u32[]{:S(2)}) collective-permute-start(bf16[608,128]{1,0:T(8,128)(2,1)S(1)} %collective-permute-done.15.refs_1_.refs_5_), channel_id=1, source_target_pairs={{0,16},{16,0},{1,17},{17,1},{2,18},{18,2},{3,19},{19,3},{4,20},{20... | collective-permute-start | bytes 466952 | tf_op jit(solution)/shard_map/ppermute | solution.py:36
  101.3 3.9 %collective-permute-start.39 = (bf16[608,128]{1,0:T(8,128)(2,1)S(1)}, bf16[608,128]{1,0:T(8,128)(2,1)S(1)}, u32[]{:S(2)}, u32[]{:S(2)}) collective-permute-start(bf16[608,128]{1,0:T(8,128)(2,1)S(1)} %collective-permute-done.16.refs_2_.refs_6_), channel_id=1, source_target_pairs={{0,16},{16,0},{1,17},{17,1},{2,18},{18,2},{3,19},{19,3},{4,20},{20... | collective-permute-start | bytes 466952 | tf_op jit(solution)/shard_map/ppermute | solution.py:36
  101.3 9.0 %collective-permute-start.40 = (bf16[608,128]{1,0:T(8,128)(2,1)}, bf16[608,128]{1,0:T(8,128)(2,1)}, u32[]{:S(2)}, u32[]{:S(2)}) collective-permute-start(bf16[608,128]{1,0:T(8,128)(2,1)} %collective-permute-done.17.refs_3_.refs_7_), channel_id=1, source_target_pairs={{0,16},{16,0},{1,17},{17,1},{2,18},{18,2},{3,19},{19,3},{4,20},{20... | collective-permute-start | bytes 466952 | tf_op jit(solution)/shard_map/ppermute | solution.py:36
  101.8 8.5 %collective-permute-start.35 = (bf16[608,128]{1,0:T(8,128)(2,1)}, bf16[608,128]{1,0:T(8,128)(2,1)}, u32[]{:S(2)}, u32[]{:S(2)}) collective-permute-start(bf16[608,128]{1,0:T(8,128)(2,1)} %get-tuple-element.137.refs_0_), channel_id=1, source_target_pairs={{0,16},{16,0},{1,17},{17,1},{2,18},{18,2},{3,19},{19,3},{4,20},{20... | collective-permute-start | bytes 466952 | tf_op jit(solution)/shard_map/ppermute | solution.py:36
  102.8 8.0 %collective-permute-start.36 = (bf16[608,128]{1,0:T(8,128)(2,1)}, bf16[608,128]{1,0:T(8,128)(2,1)}, u32[]{:S(2)}, u32[]{:S(2)}) collective-permute-start(bf16[608,128]{1,0:T(8,128)(2,1)} %collective-permute-done.22.refs_1_), channel_id=1, source_target_pairs={{0,16},{16,0},{1,17},{17,1},{2,18},{18,2},{3,19},{19,3},{4,20},{20... | collective-permute-start | bytes 466952 | tf_op jit(solution)/shard_map/ppermute | solution.py:36
  103.7 7.3 %collective-permute-start.41 = (bf16[608,128]{1,0:T(8,128)(2,1)}, bf16[608,128]{1,0:T(8,128)(2,1)}, u32[]{:S(2)}, u32[]{:S(2)}) collective-permute-start(bf16[608,128]{1,0:T(8,128)(2,1)} %collective-permute-done.12.refs_12_), channel_id=1, source_target_pairs={{0,8},{4,12},{8,0},{12,4},{16,20},{20,16},{24,28},{28,24},{1,9},{5... | collective-permute-start | bytes 466952 | tf_op jit(solution)/shard_map/ppermute | solution.py:48
  105.9 5.5 %collective-permute-start.42 = (bf16[608,128]{1,0:T(8,128)(2,1)}, bf16[608,128]{1,0:T(8,128)(2,1)}, u32[]{:S(2)}, u32[]{:S(2)}) collective-permute-start(bf16[608,128]{1,0:T(8,128)(2,1)} %collective-permute-done.20.refs_13_), channel_id=1, source_target_pairs={{0,8},{4,12},{8,0},{12,4},{16,20},{20,16},{24,28},{28,24},{1,9},{5... | collective-permute-start | bytes 466952 | tf_op jit(solution)/shard_map/ppermute | solution.py:48
  110.3 1.7 %collective-permute-start.43 = (bf16[608,128]{1,0:T(8,128)(2,1)}, bf16[608,128]{1,0:T(8,128)(2,1)S(1)}, u32[]{:S(2)}, u32[]{:S(2)}) collective-permute-start(bf16[608,128]{1,0:T(8,128)(2,1)} %collective-permute-done.12.refs_12_), channel_id=1, source_target_pairs={{0,16},{16,0},{1,17},{17,1},{2,18},{18,2},{3,19},{19,3},{4,20},{20... | collective-permute-start | bytes 466952 | tf_op jit(solution)/shard_map/ppermute | solution.py:36
  110.3 1.8 %collective-permute-start.44 = (bf16[608,128]{1,0:T(8,128)(2,1)}, bf16[608,128]{1,0:T(8,128)(2,1)S(1)}, u32[]{:S(2)}, u32[]{:S(2)}) collective-permute-start(bf16[608,128]{1,0:T(8,128)(2,1)} %collective-permute-done.20.refs_13_), channel_id=1, source_target_pairs={{0,16},{16,0},{1,17},{17,1},{2,18},{18,2},{3,19},{19,3},{4,20},{20... | collective-permute-start | bytes 466952 | tf_op jit(solution)/shard_map/ppermute | solution.py:36
  110.8 9.0 %collective-permute-start.25 = (f32[608,128]{1,0:T(8,128)S(1)}, f32[608,128]{1,0:T(8,128)S(1)}, u32[]{:S(2)}, u32[]{:S(2)}) collective-permute-start(f32[608,128]{1,0:T(8,128)S(1)} %residual_rows.1), channel_id=1, source_target_pairs={{0,16},{16,0},{1,17},{17,1},{2,18},{18,2},{3,19},{19,3},{4,20},{20... | collective-permute-start | bytes 933896 | tf_op jit(solution)/shard_map/ppermute | solution.py:36
  110.9 2.7 %collective-permute-start.45 = (bf16[608,128]{1,0:T(8,128)(2,1)}, bf16[608,128]{1,0:T(8,128)(2,1)S(1)}, u32[]{:S(2)}, u32[]{:S(2)}) collective-permute-start(bf16[608,128]{1,0:T(8,128)(2,1)} %collective-permute-done.41.refs_14_), channel_id=1, source_target_pairs={{0,16},{16,0},{1,17},{17,1},{2,18},{18,2},{3,19},{19,3},{4,20},{20... | collective-permute-start | bytes 466952 | tf_op jit(solution)/shard_map/ppermute | solution.py:36
  111.4 3.0 %collective-permute-start.46 = (bf16[608,128]{1,0:T(8,128)(2,1)}, bf16[608,128]{1,0:T(8,128)(2,1)S(1)}, u32[]{:S(2)}, u32[]{:S(2)}) collective-permute-start(bf16[608,128]{1,0:T(8,128)(2,1)} %collective-permute-done.42.refs_15_), channel_id=1, source_target_pairs={{0,16},{16,0},{1,17},{17,1},{2,18},{18,2},{3,19},{19,3},{4,20},{20... | collective-permute-start | bytes 466952 | tf_op jit(solution)/shard_map/ppermute | solution.py:36
  111.9 16.8 %collective-permute-start.31 = (bf16[2,608,128]{2,1,0:T(8,128)(2,1)S(1)}, bf16[2,608,128]{2,1,0:T(8,128)(2,1)S(1)}, u32[]{:S(2)}, u32[]{:S(2)}) collective-permute-start(bf16[2,608,128]{2,1,0:T(8,128)(2,1)S(1)} %pad_maximum_fusion.refs_4_), channel_id=1, source_target_pairs={{0,16},{16,0},{1,17},{17,1},{2,18},{18,2},{3,19},{19,3},{4,20},{20... | collective-permute-start | bytes 933896 | tf_op jit(solution)/shard_map/ppermute | solution.py:36
  112.1 8.7 %collective-permute-start.29 = (bf16[2,608,128]{2,1,0:T(8,128)(2,1)S(1)}, bf16[2,608,128]{2,1,0:T(8,128)(2,1)S(1)}, u32[]{:S(2)}, u32[]{:S(2)}) collective-permute-start(bf16[2,608,128]{2,1,0:T(8,128)(2,1)S(1)} %pad_maximum_fusion.refs_4_), channel_id=1, source_target_pairs={{0,8},{4,12},{8,0},{12,4},{16,20},{20,16},{24,28},{28,24},{1,9},{5... | collective-permute-start | bytes 933896 | tf_op jit(solution)/shard_map/ppermute | solution.py:48
  113.7 12.1 %collective-permute-start.26 = (bf16[624,256]{1,0:T(8,128)(2,1)S(1)}, bf16[624,256]{1,0:T(8,128)(2,1)S(1)}, u32[]{:S(2)}, u32[]{:S(2)}) collective-permute-start(bf16[624,256]{1,0:T(8,128)(2,1)S(1)} %copy-done.28), channel_id=1, source_target_pairs={{0,8},{4,12},{8,0},{12,4},{16,20},{20,16},{24,28},{28,24},{1,9},{5... | collective-permute-start | bytes 958472 | tf_op jit(solution)/shard_map/ppermute | solution.py:48
  114.4 11.4 %collective-permute-start.30 = (bf16[2,608,128]{2,1,0:T(8,128)(2,1)S(1)}, bf16[2,608,128]{2,1,0:T(8,128)(2,1)S(1)}, u32[]{:S(2)}, u32[]{:S(2)}) collective-permute-start(bf16[2,608,128]{2,1,0:T(8,128)(2,1)S(1)} %copy-done.16), channel_id=1, source_target_pairs={{0,8},{4,12},{8,0},{12,4},{16,20},{20,16},{24,28},{28,24},{1,9},{5... | collective-permute-start | bytes 933896 | tf_op jit(solution)/shard_map/ppermute | solution.py:48
  119.9 8.9 %collective-permute-start.32 = (bf16[2,608,128]{2,1,0:T(8,128)(2,1)S(1)}, bf16[2,608,128]{2,1,0:T(8,128)(2,1)S(1)}, u32[]{:S(2)}, u32[]{:S(2)}) collective-permute-start(bf16[2,608,128]{2,1,0:T(8,128)(2,1)S(1)} %copy-done.16), channel_id=1, source_target_pairs={{0,16},{16,0},{1,17},{17,1},{2,18},{18,2},{3,19},{19,3},{4,20},{20... | collective-permute-start | bytes 933896 | tf_op jit(solution)/shard_map/ppermute | solution.py:36
  120.8 5.5 %collective-permute-start.27 = (bf16[608,128]{1,0:T(8,128)(2,1)S(1)}, bf16[608,128]{1,0:T(8,128)(2,1)S(1)}, u32[]{:S(2)}, u32[]{:S(2)}) collective-permute-start(bf16[608,128]{1,0:T(8,128)(2,1)S(1)} %copy-done.26), channel_id=1, source_target_pairs={{0,16},{16,0},{1,17},{17,1},{2,18},{18,2},{3,19},{19,3},{4,20},{20... | collective-permute-start | bytes 466952 | tf_op jit(solution)/shard_map/ppermute | solution.py:36
  125.8 2.9 %collective-permute-start.33 = (bf16[2,608,128]{2,1,0:T(8,128)(2,1)S(1)}, bf16[2,608,128]{2,1,0:T(8,128)(2,1)S(1)}, u32[]{:S(2)}, u32[]{:S(2)}) collective-permute-start(bf16[2,608,128]{2,1,0:T(8,128)(2,1)S(1)} %collective-permute-done.29.refs_6_), channel_id=1, source_target_pairs={{0,16},{16,0},{1,17},{17,1},{2,18},{18,2},{3,19},{19,3},{4,20},{20... | collective-permute-start | bytes 933896 | tf_op jit(solution)/shard_map/ppermute | solution.py:36
  125.8 2.9 %collective-permute-start.34 = (bf16[2,608,128]{2,1,0:T(8,128)(2,1)S(1)}, bf16[2,608,128]{2,1,0:T(8,128)(2,1)S(1)}, u32[]{:S(2)}, u32[]{:S(2)}) collective-permute-start(bf16[2,608,128]{2,1,0:T(8,128)(2,1)S(1)} %collective-permute-done.30.refs_7_), channel_id=1, source_target_pairs={{0,16},{16,0},{1,17},{17,1},{2,18},{18,2},{3,19},{19,3},{4,20},{20... | collective-permute-start | bytes 933896 | tf_op jit(solution)/shard_map/ppermute | solution.py:36
  126.4 2.4 %collective-permute-start.28 = (bf16[608,128]{1,0:T(8,128)(2,1)S(1)}, bf16[608,128]{1,0:T(8,128)(2,1)S(1)}, u32[]{:S(2)}, u32[]{:S(2)}) collective-permute-start(bf16[608,128]{1,0:T(8,128)(2,1)S(1)} %copy-done.24), channel_id=1, source_target_pairs={{0,16},{16,0},{1,17},{17,1},{2,18},{18,2},{3,19},{19,3},{4,20},{20... | collective-permute-start | bytes 466952 | tf_op jit(solution)/shard_map/ppermute | solution.py:36
  (31 other events, 243.3 us)

commit v11 on v9

--- a/solution.py
+++ b/solution.py
@@ -24,8 +24,7 @@
 
 
 def split_rows(hidden):
-    units = hidden // CHUNK
-    return CHUNK * max(units // 2, 1), (hidden - 1) // CHUNK * CHUNK
+    return CHUNK * max(hidden // CHUNK // 2, 1)
 
 
 def after(value, *others):
@@ -64,10 +63,10 @@
     return lax.ppermute(value, ("grp", "fsdp"), pairs)
 
 
-def gather_dp(value):
+def gather_dp(value, first=1, stop=None):
     length = lax.axis_size("dp")
-    return [value] + [
-        lax.ppermute(value, "dp", [(i, i ^ mask) for i in range(length)]) for mask in range(1, length)
+    return [
+        lax.ppermute(value, "dp", [(i, i ^ mask) for i in range(length)]) for mask in range(first, stop or length)
     ]
 
 
@@ -308,42 +307,18 @@
     pipelined(parts, product, finish)
 
 
-def backward_first_kernel(blocks, part, order, *refs):
-    pieces_in, (slope_a, slope_b, w_in, w_out, grad, total, in_buf, out_buf, full, stage, sems) = refs[:blocks], refs[blocks:]
-    parts = pieces(0, part)
+def backward_kernel(blocks, rows, order, *refs):
+    gathered, refs = refs[:blocks], refs[blocks:]
+    slope_a, slope_b, acts, stats, mod, w_in, w_out, *refs = refs
+    outs, (sums_out, in_buf, out_buf, total, full, grad, gate_grad, stage, sems) = refs[:-9], refs[-9:]
+    hidden, (features, tokens) = w_in.shape[1], full.shape
+    parts = pieces(0, hidden)
     stream = Stream(w_out, out_buf, w_in, in_buf, parts, 0, sems)
-    values = [lambda ref=ref: ref[...] for ref in pieces_in]
-    place_blocks(full, slice(None), stage, order, values, pieces_in[0].shape[0])
-    for start, size in pieces(0, full.shape[0], 128):
-        rows = pl.ds(start, size)
-        grad[:, rows] = full[rows, :].astype(F32).T.astype(BF16)
-    backward_products(stream, parts, 0, grad, (slope_a, slope_b), in_buf, out_buf, total, None, None)
-
-
-def backward_first(order, gathered, slope_a, slope_b, w_in, w_out, part, name):
-    hidden, features = w_in.shape[1:]
-    blocks, (rows, tokens) = len(gathered), gathered[0].shape
-    return pl.pallas_call(
-        functools.partial(backward_first_kernel, blocks, part),
-        out_shape=(struct((tokens, features), BF16), struct((tokens, features), F32)),
-        in_specs=[SCALARS] + [WHOLE] * (blocks + 2) + [HELD, HELD],
-        out_specs=[WHOLE] * 2,
-        scratch_shapes=layer_scratch(part, features)
-        + [
-            pltpu.VMEM((features, tokens), BF16),
-            staging(rows, features, tokens),
-            pltpu.SemaphoreType.DMA((2 * len(pieces(0, part)),)),
-        ],
-        name=name,
-        **layer_params(part, features, tokens, 0),
-    )(order, *gathered, slope_a, slope_b, w_in, w_out)
-
-
-def backward_last_kernel(start, rows, order, grad, before, slope_a, slope_b, acts, stats, mod, w_in, w_out, *refs):
-    outs, (sums_out, in_buf, out_buf, total, full, sems) = refs[:-6], refs[-6:]
-    hidden, (features, tokens) = w_in.shape[1], full.shape
-    parts = pieces(start, hidden)
-    stream = Stream(w_out, out_buf, w_in, in_buf, parts, start, sems)
+    values = [lambda ref=ref: ref[...] for ref in gathered]
+    place_blocks(gate_grad, slice(None), stage, order, values, rows)
+    for start, size in pieces(0, features, 128):
+        some = pl.ds(start, size)
+        grad[:, some] = gate_grad[some, :].astype(F32).T.astype(BF16)
     mean, inv = stats[0:1, :], stats[1:2, :]
     sums = [jnp.zeros((1, tokens), F32), jnp.zeros((1, tokens), F32)]
 
@@ -356,7 +331,7 @@
         sums[0] += jnp.sum(scaled, 0, keepdims=True)
         sums[1] += jnp.sum(scaled * xhat, 0, keepdims=True)
 
-    backward_products(stream, parts, start, grad, (slope_a, slope_b), in_buf, out_buf, total, before, last)
+    backward_products(stream, parts, 0, grad, (slope_a, slope_b), in_buf, out_buf, total, None, last)
     count = len(outs) // 2
     padded = outs[0].shape[0] - 16
     tail = pack_sums(*sums)
@@ -373,25 +348,29 @@
     sums_out[1:2, :] = sums[1]
 
 
-def backward_last(order, grad, before, slope_a, slope_b, acts, stats, mod, w_in, w_out, start, blocks, name):
+def backward(order, gathered, slope_a, slope_b, acts, stats, mod, w_in, w_out, name):
     hidden, features = w_in.shape[1:]
-    tokens, part, rows, count = before.shape[0], hidden - start, features // blocks, blocks // 2
+    blocks, (rows, tokens) = len(gathered), gathered[0].shape
+    count = blocks // 2
     outs = pl.pallas_call(
-        functools.partial(backward_last_kernel, start, rows),
+        functools.partial(backward_kernel, blocks, rows),
         out_shape=[struct((-(-rows // 16) * 16 + 16, tokens), BF16)] * count
         + [struct((rows, tokens), F32)] * count
         + [struct((2, tokens), F32)],
-        in_specs=[SCALARS] + [WHOLE] * 7 + [HELD, HELD],
+        in_specs=[SCALARS] + [WHOLE] * (blocks + 5) + [HELD, HELD],
         out_specs=[WHOLE] * (blocks + 1),
-        scratch_shapes=layer_scratch(part, features)
+        scratch_shapes=layer_scratch(hidden, features)
         + [
             pltpu.VMEM((tokens, features), F32),
             pltpu.VMEM((features, tokens), F32),
-            pltpu.SemaphoreType.DMA((2 * len(pieces(start, hidden)),)),
+            pltpu.VMEM((tokens, features), BF16),
+            pltpu.VMEM((features, tokens), BF16),
+            staging(rows, features, tokens),
+            pltpu.SemaphoreType.DMA((2 * len(pieces(0, hidden)),)),
         ],
         name=name,
-        **layer_params(part, features, tokens, 0),
-    )(order, grad, before, slope_a, slope_b, acts, stats, mod, w_in, w_out)
+        **layer_params(hidden, features, tokens, 0),
+    )(order, *gathered, slope_a, slope_b, acts, stats, mod, w_in, w_out)
     return outs[:count], outs[count:-1], outs[-1]
 
 
@@ -473,13 +452,13 @@
 
 def residual_kernel(order, weight, *refs):
     stack, (result, full, stage) = refs[:-3], refs[-3:]
-    values = [lambda value=value: value[0] for value in stack]
-    place_blocks(full, slice(None), stage, order, values, stack[0].shape[1])
+    values = [lambda value=value: value[...] for value in stack]
+    place_blocks(full, slice(None), stage, order, values, stack[0].shape[0])
     result[...] = jnp.dot(weight[...], full[...], preferred_element_type=F32)
 
 
 def residual_rows(order, weight, stack):
-    blocks, (_, rows, half) = len(stack), stack[0].shape
+    blocks, (rows, half) = len(stack), stack[0].shape
     return pl.pallas_call(
         residual_kernel,
         out_shape=struct((rows, half), F32),
@@ -493,13 +472,16 @@
 
 def zero_grad_kernel(blocks, first, count, order, dp_order, *refs):
     cots, refs = refs[:count], refs[count:]
-    sides, refs = (refs[:blocks], refs[blocks : 2 * blocks]), refs[2 * blocks :]
+    stacks = []
+    while len(refs) > (9 if first else 6):
+        stacks.append((refs[:blocks], refs[blocks : 2 * blocks]))
+        refs = refs[2 * blocks :]
     before = None
     if first:
         before, out, lhs, rhs, stage, parked, loads, buf, sems = refs
     else:
         buf, lhs, rhs, stage, parked, loads = refs
-    rows, half = sides[0][0].shape[1:]
+    rows, half = stacks[0][0][0].shape[-2:]
     group = order[blocks]
     moves, places = [], []
     for part in range(count):
@@ -517,7 +499,8 @@
                 else:
                     offset = pl.multiple_of(order[side * (blocks + 1) + place] * rows, 16)
                     target = rhs.at[pl.ds(offset, rows), lanes]
-                moves.append((sides[side][place].at[part], target))
+                source = stacks[part][side][place] if len(stacks) == count else stacks[0][side][place].at[part]
+                moves.append((source, target))
             places.append((lanes, values, side * (blocks + 1)))
     moves = [pltpu.make_async_copy(a, b, loads.at[k]) for k, (a, b) in enumerate(moves)]
     for move in moves:
@@ -539,8 +522,10 @@
         copy.wait()
 
 
-def zero_projection_grad(order, dp_order, first, cots, mine, other, before, name):
-    blocks, (count, rows, half) = len(mine), mine[0].shape
+def zero_projection_grad(order, dp_order, first, cots, stacks, before, name):
+    blocks, (rows, half) = len(stacks[0][0]), stacks[0][0][0].shape[-2:]
+    count = len(cots)
+    flat = [block for pair in stacks for side in pair for block in side]
     features, tokens = blocks * rows, count * 2 * half
     extra = [] if before is None else [before]
     scratch = [
@@ -558,12 +543,12 @@
     return pl.pallas_call(
         functools.partial(zero_grad_kernel, blocks, first, count),
         out_shape=struct((rows, features), F32),
-        in_specs=[SCALARS] * 2 + [ANYWHERE] * (count + 2 * blocks) + [WHOLE] * len(extra),
+        in_specs=[SCALARS] * 2 + [ANYWHERE] * (count + len(flat)) + [WHOLE] * len(extra),
         out_specs=HELD if extra else WHOLE,
         scratch_shapes=scratch,
         name=name,
         **params(2 * tokens * rows * features, 4 * rows * features + 2 * tokens * (rows + features), grant=28),
-    )(order, dp_order, *cots, *mine, *other, *extra)
+    )(order, dp_order, *cots, *flat, *extra)
 
 
 def steps(values, level, *during):
@@ -595,7 +580,7 @@
     own_term, sent, normed, stats, cot0, cot1_rows = prepare(
         order, acts, modulation, own_cot, arrived, zero_weight, blocks
     )
-    split, cut = split_rows(hidden)
+    split = split_rows(hidden)
     slope_a, total, mod = forward_first(after(normed, *sent), modulation, w_in, w_out, split, "forward_first")
     own_mod = block_of(mod, me, rows)
     own_gate = own_mod[:, 2:3]
@@ -607,29 +592,38 @@
     slope_b, kept, sent = forward_last(
         order, after(normed, grad_rows), total, w_in, w_out, split, blocks, "forward_last"
     )
-    gathered = [grad_rows] + direct([grad_rows] * (blocks - 1), kept)
-    grad, total = backward_first(
-        order, after(gathered, *sent), slope_a, slope_b, w_in, w_out, cut, "backward_first"
+    got, cot_near = lax.optimization_barrier((
+        [send(grad_rows, place) for place in range(1, blocks)], gather_dp(cot1_rows, 1, 2), kept
+    ))[:2]
+    gathered, cots = [grad_rows] + got, [cot1_rows] + cot_near
+    norm_sent, norm_kept, token_sums = backward(
+        order, after(gathered, *sent), slope_a, slope_b, acts, stats, mod, w_in, w_out, "backward"
     )
-    got = direct(sent, total)
+    got, cot_far = lax.optimization_barrier((
+        [send(value, place + 1) for place, value in enumerate(sent)], gather_dp(cots[0], 2, 3), token_sums
+    ))[:2]
+    cots = cots + cot_far
     own_values = block_of(acts[0], me, rows).astype(F32)
     sums = own_values + own_gate * (kept + sum(value.astype(F32) for value in got))
     out_rows = sums.astype(BF16)
 
     out_half = jnp.where(is_control, out_rows[:, :half], swap_grp(out_rows[:, half:]))
-    far = gather_dp(out_half)[1:]
-    sent, kept, token_sums = backward_last(
-        order, after(grad, out_half), total, slope_a, slope_b, acts, stats, mod, w_in, w_out, cut, blocks, "backward_last"
-    )
-    far, out_half, sent, kept, token_sums = lax.optimization_barrier((far, out_half, sent, kept, token_sums))
-
-    gathers = [[jnp.stack([out_half, far[0]])], [jnp.stack(far[1:])]]
-    cots = gather_dp(after(cot1_rows, token_sums))
+    far = gather_dp(out_half)
+    sent, kept = after((norm_sent, norm_kept), out_half)
     for level in range(levels):
         got = steps(sent, level)
-        gathers = [gather + steps(gather, level) for gather in gathers]
+        if level == 0:
+            got, nearest = lax.optimization_barrier((got, far[0]))
+            near = [after(out_half, got[0])]
+        near = near + steps(near, level)
         if level + 1 < levels:
             sent, kept, token_sums = fold(got, kept, token_sums)
+    gathers = [[nearest], [jnp.stack(far[1:])]]
+    for level in range(levels):
+        gathers = [gather + steps(gather, level) for gather in gathers]
+        if level == 0:
+            gathers, first = lax.optimization_barrier((gathers, cots[0]))
+            cots = cots + gather_dp(first, 3)
     more = unpack_sums(got[0][-16:])
     plain, along = token_sums[0:1] + more[0], token_sums[1:2] + more[1]
     kept = [kept[0] + got[0][:rows].astype(F32)]
@@ -637,17 +631,13 @@
     back = inv * (
         kept[0] * (1.0 + own_mod[:, 1:2]) - plain / features - (own_values - mean) * inv * (along / features)
     )
-    residual = residual_rows(order, zero_weight, gathers[0])
+    residual = residual_rows(order, zero_weight, near)
     residual = jnp.concatenate([swap_grp(residual), residual], 1)
     block_rows = jnp.where(is_control, out_rows, (sums + residual).astype(BF16))
 
-    others = [[swap_grp(value) for value in gather] for gather in gathers]
-    zero_grad = zero_projection_grad(
-        order, dp_order, 0, cots[:2], gathers[0], others[0], None, "zero_projection_grad_first"
-    )
-    zero_grad = zero_projection_grad(
-        order, dp_order, 2, cots[2:], gathers[1], others[1], zero_grad, "zero_projection_grad_last"
-    )
+    stacks = [(mine, [swap_grp(value) for value in mine]) for mine in [near] + gathers]
+    zero_grad = zero_projection_grad(order, dp_order, 0, cots[:2], stacks[:2], None, "zero_projection_grad_first")
+    zero_grad = zero_projection_grad(order, dp_order, 2, cots[2:], stacks[2:], zero_grad, "zero_projection_grad_last")
     return (block_rows[None], (up_rows + back)[None], zero_grad)
 
 

time: 152 us -> 129 us (0.85)
  waiting for transfers between devices: 52.6 us -> 25.8 us
  starting transfers between devices: 31.6 us -> 38.2 us
  Pallas kernels: 53.3 us -> 47.5 us
  local copies, waits for them, and re-layouts: 2.61 us -> 8.35 us
  other arithmetic: 10.4 us -> 7.54 us
    ppermute x6, waiting for transfers between devices: 31 us -> 12.8 us  [gather_dp(): lax.ppermute(value, 'dp', [(i, i ^ mask) for i in range(length)])]
    ppermute x9 -> x12, waiting for transfers between devices: 17.1 us -> 10.6 us  [step(): return lax.ppermute(value, ('grp', 'fsdp'), pairs)]
    unnamed x25 -> x53, local copies, waits for them, and re-layouts: 2.6 us -> 8.33 us
    pallas_call x2 -> x1, Pallas kernels: 18.9 us -> 13.9 us  [backward(): pl.pallas_call(functools.partial(backward_kernel, blocks, rows), out_shap...]
    ppermute x6, starting transfers between devices: 7 us -> 10.5 us  [gather_dp(): lax.ppermute(value, 'dp', [(i, i ^ mask) for i in range(length)])]
    ppermute x9 -> x12, starting transfers between devices: 10.7 us -> 12.1 us  [step(): return lax.ppermute(value, ('grp', 'fsdp'), pairs)]
    ppermute x12 -> x16, starting transfers between devices: 2.32 us -> 3.43 us  [swap_grp(): return lax.ppermute(value, 'grp', [(0, 1), (1, 0)])]
  transfers between devices with their start and end apart: 36 -> 43, of which waited for: 13 -> 10; matrix products, arithmetic and copies ran while one was open for 5% -> 5% of each run, Pallas kernels for 30% -> 30%
where the time goes in v11:
time: 129 us
  Pallas kernels  47.5 us (37%)
  starting transfers between devices  38.2 us (30%)
  waiting for transfers between devices  25.8 us (20%)
  local copies, waits for them, and re-layouts  8.35 us (6%)
  other arithmetic  7.54 us (6%)
    pallas_call x1, Pallas kernels, backward(): pl.pallas_call(functools.partial(backward_kernel, blocks, rows), out_shap...  13.9 us
    ppermute x6, waiting for transfers between devices, gather_dp(): lax.ppermute(value, 'dp', [(i, i ^ mask) for i in range(length)])  12.8 us
    ppermute x9, starting transfers between devices, send(): return lax.ppermute(value, ('grp', 'fsdp'), pairs)  12.2 us
    ppermute x12, starting transfers between devices, step(): return lax.ppermute(value, ('grp', 'fsdp'), pairs)  12.1 us
    pallas_call x1, Pallas kernels, forward_last(): pl.pallas_call(functools.partial(forward_last_kernel, start), out_shape=[...  11.4 us
    ppermute x12, waiting for transfers between devices, step(): return lax.ppermute(value, ('grp', 'fsdp'), pairs)  10.6 us
    ppermute x6, starting transfers between devices, gather_dp(): lax.ppermute(value, 'dp', [(i, i ^ mask) for i in range(length)])  10.5 us
    pallas_call x2, Pallas kernels, zero_projection_grad(): pl.pallas_call(functools.partial(zero_grad_kernel, blocks, first, count),...  8.68 us
  transfers between devices with their start and end apart: 43, of which 10 were waited for; matrix products, arithmetic and copies ran while one was open for 5% of the time, Pallas kernels for 30%

profile of v11, /device:TPU:0, one launch (start us, length us, event | category | flops | bytes accessed | tf_op | source)
XLA Modules:
  0.0 128.6 jit_solution(8357215517979629797)
XLA Ops:
  2.7 1.0 copy-done.2
  3.6 4.0 %prepare.1 = (f32[608,128]{1,0:T(8,128)S(1)}, bf16[608,128]{1,0:T(8,128)(2,1)S(1)}, bf16[608,128]{1,0:T(8,128)(2,1)S(1)}, bf16[608,128]{1,0:T(8,128)(2,1)S(1)}, ...) custom-call(s32[9]{0:T(128)S(1)} %pad_add_fusion.order, ...), custom_call_target="tpu_custom_call" | custom-call | flops 378535936 | bytes 4202496 | tf_op jit(solution)/shard_map/prepare/pallas_call | solution.py:430
  7.6 2.9 %collective-permute-start.1 = (bf16[608,128]{1,0:T(8,128)(2,1)S(1)}, bf16[608,128]{1,0:T(8,128)(2,1)S(1)}, u32[]{:S(2)}, u32[]{:S(2)}) collective-permute-start(bf16[608,128]{1,0:T(8,128)(2,1)S(1)} %get-tuple-element.58), channel_id=1, source_target_pairs={{0,4},{4,0},{8,12},{12,8},{16,24},{20,28},{24,16},{28,20},{1,5},{5... | collective-permute-start | bytes 466952 | tf_op jit(solution)/shard_map/ppermute | solution.py:63
  10.5 1.5 %collective-permute-start.2 = (bf16[608,128]{1,0:T(8,128)(2,1)S(1)}, bf16[608,128]{1,0:T(8,128)(2,1)S(1)}, u32[]{:S(2)}, u32[]{:S(2)}) collective-permute-start(bf16[608,128]{1,0:T(8,128)(2,1)S(1)} %get-tuple-element.59), channel_id=1, source_target_pairs={{0,8},{4,12},{8,0},{12,4},{16,20},{20,16},{24,28},{28,24},{1,9},{5... | collective-permute-start | bytes 466952 | tf_op jit(solution)/shard_map/ppermute | solution.py:63
  12.0 7.4 %forward_first.1 = (f32[256,1024]{1,0:T(8,128)S(1)}, f32[256,2432]{1,0:T(8,128)}, f32[2432,8]{1,0:T(8,128)S(1)}) custom-call(bf16[256,2432]{1,0:T(8,128)(2,1)S(1)} %get-tuple-element.69.normed, f32[1,3,2432]{2,1,0:T(4,128)S(1)} %copy.13.modulation, bf16[1,2432,2432]{2,1,0:T(8,128)(2,1)} %refs_9_.1, bf16[1,2432,2432]{2,1,0:T(8,128)(2,1)} %refs_10_.1), custom_call_target="tpu_custom_call" | custom-call | flops 2550136832 | bytes 12451840 | tf_op jit(solution)/shard_map/forward_first/pallas_call | solution.py:253
  19.5 1.0 copy-done.4
  20.6 2.1 %collective-permute-start.12 = (bf16[608,256]{1,0:T(8,128)(2,1)}, bf16[608,256]{1,0:T(8,128)(2,1)S(1)}, u32[]{:S(2)}, u32[]{:S(2)}) collective-permute-start(bf16[608,256]{1,0:T(8,128)(2,1)} %get-tuple-element.105.refs_0_), channel_id=1, source_target_pairs={{0,1},{1,0},{2,3},{3,2},{4,5},{5,4},{6,7},{7,6},{8,9},{9,8},{10,11... | collective-permute-start | bytes 933896 | tf_op jit(solution)/shard_map/ppermute | solution.py:69
  22.7 2.6 %collective-permute-start.8 = (bf16[608,256]{1,0:T(8,128)(2,1)}, bf16[608,256]{1,0:T(8,128)(2,1)S(1)}, u32[]{:S(2)}, u32[]{:S(2)}) collective-permute-start(bf16[608,256]{1,0:T(8,128)(2,1)} %get-tuple-element.105.refs_0_), channel_id=1, source_target_pairs={{0,2},{1,3},{2,0},{3,1},{4,6},{5,7},{6,4},{7,5},{8,10},{9,11},{10,... | collective-permute-start | bytes 933896 | tf_op jit(solution)/shard_map/ppermute | solution.py:69
  26.0 2.5 %collective-permute-start.11 = (bf16[608,256]{1,0:T(8,128)(2,1)S(1)}, bf16[608,256]{1,0:T(8,128)(2,1)S(1)}, u32[]{:S(2)}, u32[]{:S(2)}) collective-permute-start(bf16[608,256]{1,0:T(8,128)(2,1)S(1)} %multiply_convert_fusion.refs_0_), channel_id=1, source_target_pairs={{0,12},{4,8},{8,4},{12,0},{16,28},{20,24},{24,20},{28,16},{1,13},{... | collective-permute-start | bytes 933896 | tf_op jit(solution)/shard_map/ppermute | solution.py:63
  29.5 11.4 %forward_last.1 = (f32[256,1408]{1,0:T(8,128)}, f32[608,256]{1,0:T(8,128)S(1)}, bf16[608,256]{1,0:T(8,128)(2,1)S(1)}, bf16[608,256]{1,0:T(8,128)(2,1)S(1)}, bf16[608,256]{1,0:T(8,128)(2,1)S(1)}) custom-call(s32[9]{0:T(128)S(1)} %pad_add_fusion.order, bf16[256,2432]{1,0:T(8,128)(2,1)S(1)} %get-tuple-element.69.normed, f32[256,2432]{1,0:T(8,128)} %get-tuple-element.65.before, ...), custom_call_target="tpu_custom_call" | custom-call | flops 3506438144 | bytes 16187392 | tf_op jit(solution)/shard_map/forward_last/pallas_call | solution.py:267
  40.9 1.5 %collective-permute-start.5 = (bf16[608,256]{1,0:T(8,128)(2,1)S(1)}, bf16[608,256]{1,0:T(8,128)(2,1)S(1)}, u32[]{:S(2)}, u32[]{:S(2)}) collective-permute-start(bf16[608,256]{1,0:T(8,128)(2,1)S(1)} %get-tuple-element.71), channel_id=1, source_target_pairs={{0,4},{4,0},{8,12},{12,8},{16,24},{20,28},{24,16},{28,20},{1,5},{5... | collective-permute-start | bytes 933896 | tf_op jit(solution)/shard_map/ppermute | solution.py:63
  42.5 1.5 %collective-permute-start.6 = (bf16[608,256]{1,0:T(8,128)(2,1)S(1)}, bf16[608,256]{1,0:T(8,128)(2,1)S(1)}, u32[]{:S(2)}, u32[]{:S(2)}) collective-permute-start(bf16[608,256]{1,0:T(8,128)(2,1)S(1)} %get-tuple-element.72), channel_id=1, source_target_pairs={{0,8},{4,12},{8,0},{12,4},{16,20},{20,16},{24,28},{28,24},{1,9},{5... | collective-permute-start | bytes 933896 | tf_op jit(solution)/shard_map/ppermute | solution.py:63
  44.0 1.2 collective-permute-start.7
  45.2 13.9 %backward.1 = (bf16[624,256]{1,0:T(8,128)(2,1)S(1)}, bf16[624,256]{1,0:T(8,128)(2,1)S(1)}, f32[608,256]{1,0:T(8,128)S(1)}, f32[608,256]{1,0:T(8,128)S(1)}, f32[2,256]{1,0:T(2,128)S(1)}) custom-call(s32[9]{0:T(128)S(1)} %pad_add_fusion.order, bf16[608,256]{1,0:T(8,128)(2,1)S(1)} %multiply_convert_fusion.refs_0_, ...), custom_call_target="tpu_custom_call" | custom-call | flops 6056574976 | bytes 26148864 | tf_op jit(solution)/shard_map/backward/pallas_call | solution.py:355
  59.2 2.2 %fusion.16 = (bf16[608,256]{1,0:T(8,128)(2,1)S(1)}, f32[608,256]{1,0:T(8,128)}) fusion(f32[608,256]{1,0:T(8,128)S(1)} %get-tuple-element.70, bf16[608,256]{1,0:T(8,128)(2,1)S(1)} %collective-permute-done.7, bf16[608,256]{1,0:T(8,128)(2,1)S(1)} %collective-permute-done.6, bf16[608,256]{1,0:T(8,128)(2,1)S(1)} %collective-permute-done.5, ...), kind=kLoop, calls=%fused_computation.35 | loop fusion | flops 1556480 | bytes 2804100 | tf_op jit(solution)/shard_map/convert_element_type | solution.py:608
  61.6 1.4 %collective-permute-done.13 = bf16[608,128]{1,0:T(8,128)(2,1)S(1)} collective-permute-done((bf16[608,128]{1,0:T(8,128)(2,1)S(1)}, bf16[608,128]{1,0:T(8,128)(2,1)S(1)}, u32[]{:S(2)}, u32[]{:S(2)}) %collective-permute-start.13) | collective-permute-done | bytes 155680 | tf_op jit(solution)/shard_map/ppermute | solution.py:35
  63.0 0.8 collective-permute-start.24
  63.8 1.2 collective-permute-start.23
  65.8 1.2 collective-permute-start.15
  67.0 2.5 %collective-permute-start.16 = (bf16[608,128]{1,0:T(8,128)(2,1)S(1)}, bf16[608,128]{1,0:T(8,128)(2,1)S(1)}, u32[]{:S(2)}, u32[]{:S(2)}) collective-permute-start(bf16[608,128]{1,0:T(8,128)(2,1)S(1)} %slice_select_fusion.refs_0_.refs_2_), channel_id=1, source_target_pairs={{0,1},{1,0},{2,3},{3,2},{4,5},{5,4},{6,7},{7,6},{8,9},{9,8},{10,11... | collective-permute-start | bytes 466952 | tf_op jit(solution)/shard_map/ppermute | solution.py:69
  69.5 2.4 %collective-permute-done.24 = bf16[608,128]{1,0:T(8,128)(2,1)S(1)} collective-permute-done((bf16[608,128]{1,0:T(8,128)(2,1)S(1)}, bf16[608,128]{1,0:T(8,128)(2,1)S(1)}, u32[]{:S(2)}, u32[]{:S(2)}) %collective-permute-start.24) | collective-permute-done | bytes 155680 | tf_op jit(solution)/shard_map/ppermute | solution.py:69
  71.8 7.2 %collective-permute-done.23 = bf16[608,128]{1,0:T(8,128)(2,1)S(1)} collective-permute-done((bf16[608,128]{1,0:T(8,128)(2,1)S(1)}, bf16[608,128]{1,0:T(8,128)(2,1)S(1)}, u32[]{:S(2)}, u32[]{:S(2)}) %collective-permute-start.23) | collective-permute-done | bytes 155680 | tf_op jit(solution)/shard_map/ppermute | solution.py:69
  82.1 1.2 collective-permute-start.17
  83.3 1.1 copy-done.6
  84.4 1.1 copy-done.8
  85.5 1.0 copy-done.10
  86.4 1.0 copy-done.12
  87.6 0.9 collective-permute-start.21
  88.4 1.2 collective-permute-start.18
  89.7 0.8 collective-permute-start.22
  90.5 1.5 %collective-permute-start.19 = (bf16[608,128]{1,0:T(8,128)(2,1)}, bf16[608,128]{1,0:T(8,128)(2,1)S(1)}, u32[]{:S(2)}, u32[]{:S(2)}) collective-permute-start(bf16[608,128]{1,0:T(8,128)(2,1)} %collective-permute-done.17.refs_1_.refs_3_), channel_id=1, source_target_pairs={{0,8},{4,12},{8,0},{12,4},{16,20},{20,16},{24,28},{28,24},{1,9},{5... | collective-permute-start | bytes 466952 | tf_op jit(solution)/shard_map/ppermute | solution.py:47
  92.0 4.8 %collective-permute-done.22.refs_11_ = bf16[608,128]{1,0:T(8,128)(2,1)S(1)} collective-permute-done((bf16[608,128]{1,0:T(8,128)(2,1)}, bf16[608,128]{1,0:T(8,128)(2,1)S(1)}, u32[]{:S(2)}, u32[]{:S(2)}) %collective-permute-start.22) | collective-permute-done | bytes 155680 | tf_op jit(solution)/shard_map/ppermute | solution.py:47
  96.8 1.1 collective-permute-done.18.refs_2_.refs_4_
  97.9 0.8 collective-permute-start.37
  98.8 0.8 collective-permute-done.19.refs_3_.refs_5_
  99.6 1.9 %residual_rows.1 = f32[608,128]{1,0:T(8,128)S(1)} custom-call(s32[9]{0:T(128)S(1)} %pad_add_fusion.order, bf16[608,2432]{1,0:T(8,128)(2,1)S(1)} %copy-done, bf16[608,128]{1,0:T(8,128)(2,1)S(1)} %slice_select_fusion.refs_0_.refs_2_, bf16[608,128]{1,0:T(8,128)(2,1)} %collective-permute-done.17.refs_1_.refs_3_, ...), custom_call_target="tpu_custom_call" | custom-call | flops 378535936 | bytes 4202496 | tf_op jit(solution)/shard_map/residual_rows/pallas_call | solution.py:462
  102.2 0.9 collective-permute-done.35.refs_8_
  103.1 0.8 collective-permute-start.38
  104.0 1.2 collective-permute-start.27
  105.2 0.8 collective-permute-start.28
  106.5 1.8 %collective-permute-done.38.refs_13_ = bf16[608,128]{1,0:T(8,128)(2,1)S(1)} collective-permute-done((bf16[608,128]{1,0:T(8,128)(2,1)S(1)}, bf16[608,128]{1,0:T(8,128)(2,1)S(1)}, u32[]{:S(2)}, u32[]{:S(2)}) %collective-permute-start.38) | collective-permute-done | bytes 155680 | tf_op jit(solution)/shard_map/ppermute | solution.py:47
  108.9 2.3 %fusion.5 = f32[1,608,256]{2,1,0:T(8,128)} fusion(f32[608,256]{1,0:T(8,128)S(1)} %get-tuple-element.100, f32[608,128]{1,0:T(8,128)S(1)} %copy-done.25, f32[608,128]{1,0:T(8,128)S(1)} %copy-done.20, bf16[624,256]{1,0:T(8,128)(2,1)S(1)} %collective-permute-done.21, f32[256]{0:T(256)S(1)} %bitcast.24, f32[256]{0:T(256)S(1)} %bitcast.26, f32[256]{0:T(256)S(1)} %bitcast.23, ...), kind=kLoop, calls=%fused_computation.7 | loop fusion | flops 2179072 | bytes 2808197 | tf_op jit(solution)/shard_map/broadcast_in_dim | solution.py:641
  111.8 1.3 %collective-permute-start.26 = (bf16[608,256]{1,0:T(8,128)(2,1)}, bf16[608,256]{1,0:T(8,128)(2,1)S(1)}, u32[]{:S(2)}, u32[]{:S(2)}) collective-permute-start(bf16[608,256]{1,0:T(8,128)(2,1)} %get-tuple-element.105.refs_0_), channel_id=1, source_target_pairs={{0,3},{1,2},{2,1},{3,0},{4,7},{5,6},{6,5},{7,4},{8,11},{9,10},{10,... | collective-permute-start | bytes 933896 | tf_op jit(solution)/shard_map/ppermute | solution.py:69
  113.1 1.9 %collective-permute-done.28.refs_5_ = bf16[2,608,128]{2,1,0:T(8,128)(2,1)S(1)} collective-permute-done((bf16[2,608,128]{2,1,0:T(8,128)(2,1)}, bf16[2,608,128]{2,1,0:T(8,128)(2,1)S(1)}, u32[]{:S(2)}, u32[]{:S(2)}) %collective-permute-start.28) | collective-permute-done | bytes 311328 | tf_op jit(solution)/shard_map/ppermute | solution.py:47
  115.6 3.6 %zero_projection_grad_first.1.refs_10_ = f32[608,2432]{1,0:T(8,128)S(1)} custom-call(s32[9]{0:T(128)S(1)} %pad_add_fusion.order, s32[4]{0:T(128)S(1)} %iota_xor_fusion.dp_order, bf16[608,256]{1,0:T(8,128)(2,1)} %get-tuple-element.105.refs_0_, bf16[608,256]{1,0:T(8,128)(2,1)S(1)} %copy-done.14, bf16[608,128]{1,0:T(8,128)(2,1)S(1)} %slice_select_fusion.refs_0_.refs_2_, ...), custom_call_target="tpu_custom_call" | custom-call | flops 1514143744 | bytes 9027584 | tf_op jit(solution)/shard_map/zero_projection_grad_first/pallas_call | solution.py:543
  119.2 0.8 fusion.8
  120.0 3.2 %collective-permute-done.26.refs_1_ = bf16[608,256]{1,0:T(8,128)(2,1)S(1)} collective-permute-done((bf16[608,256]{1,0:T(8,128)(2,1)}, bf16[608,256]{1,0:T(8,128)(2,1)S(1)}, u32[]{:S(2)}, u32[]{:S(2)}) %collective-permute-start.26) | collective-permute-done | bytes 311328 | tf_op jit(solution)/shard_map/ppermute | solution.py:69
  123.3 5.1 %zero_projection_grad_last.1 = f32[608,2432]{1,0:T(8,128)} custom-call(s32[9]{0:T(128)S(1)} %pad_add_fusion.order, s32[4]{0:T(128)S(1)} %iota_xor_fusion.dp_order, bf16[608,256]{1,0:T(8,128)(2,1)S(1)} %copy-done.16, bf16[608,256]{1,0:T(8,128)(2,1)S(1)} %collective-permute-done.26.refs_1_, bf16[2,608,128]{2,1,0:T(8,128)(2,1)} %pad_maximum_fusion.refs_2_, ...), custom_call_target="tpu_custom_call" | custom-call | flops 1514143744 | bytes 9027584 | tf_op jit(solution)/shard_map/zero_projection_grad_last/pallas_call | solution.py:543
  (114 shorter events, 10.9 us)
Async XLA Ops:
  0.6 2.0 %collective-permute-start = (bf16[608,256]{1,0:T(8,128)(2,1)}, bf16[608,256]{1,0:T(8,128)(2,1)S(1)}, u32[]{:S(2)}, u32[]{:S(2)}) collective-permute-start(bf16[608,256]{1,0:T(8,128)(2,1)} %bitcast.19), channel_id=1, source_target_pairs={{0,16},{16,0},{1,17},{17,1},{2,18},{18,2},{3,19},{19,3},{4,20},{20... | collective-permute-start | bytes 933896 | tf_op jit(solution)/shard_map/ppermute | solution.py:35
  7.6 12.8 %collective-permute-start.1 = (bf16[608,128]{1,0:T(8,128)(2,1)S(1)}, bf16[608,128]{1,0:T(8,128)(2,1)S(1)}, u32[]{:S(2)}, u32[]{:S(2)}) collective-permute-start(bf16[608,128]{1,0:T(8,128)(2,1)S(1)} %get-tuple-element.58), channel_id=1, source_target_pairs={{0,4},{4,0},{8,12},{12,8},{16,24},{20,28},{24,16},{28,20},{1,5},{5... | collective-permute-start | bytes 466952 | tf_op jit(solution)/shard_map/ppermute | solution.py:63
  10.5 9.9 %collective-permute-start.2 = (bf16[608,128]{1,0:T(8,128)(2,1)S(1)}, bf16[608,128]{1,0:T(8,128)(2,1)S(1)}, u32[]{:S(2)}, u32[]{:S(2)}) collective-permute-start(bf16[608,128]{1,0:T(8,128)(2,1)S(1)} %get-tuple-element.59), channel_id=1, source_target_pairs={{0,8},{4,12},{8,0},{12,4},{16,20},{20,16},{24,28},{28,24},{1,9},{5... | collective-permute-start | bytes 466952 | tf_op jit(solution)/shard_map/ppermute | solution.py:63
  12.0 8.4 %collective-permute-start.3 = (bf16[608,128]{1,0:T(8,128)(2,1)S(1)}, bf16[608,128]{1,0:T(8,128)(2,1)S(1)}, u32[]{:S(2)}, u32[]{:S(2)}) collective-permute-start(bf16[608,128]{1,0:T(8,128)(2,1)S(1)} %get-tuple-element.60), channel_id=1, source_target_pairs={{0,12},{4,8},{8,4},{12,0},{16,28},{20,24},{24,20},{28,16},{1,13},{... | collective-permute-start | bytes 466952 | tf_op jit(solution)/shard_map/ppermute | solution.py:63
  20.5 20.4 %copy-start.19 = (f32[608,128]{1,0:T(8,128)}, f32[608,128]{1,0:T(8,128)S(1)}, u32[]{:S(2)}) copy-start(f32[608,128]{1,0:T(8,128)S(1)} %add_add_fusion) | copy-start | bytes 933892
  20.6 5.2 %collective-permute-start.4 = (f32[608,128]{1,0:T(8,128)S(1)}, f32[608,128]{1,0:T(8,128)S(1)}, u32[]{:S(2)}, u32[]{:S(2)}) collective-permute-start(f32[608,128]{1,0:T(8,128)S(1)} %add_add_fusion), channel_id=1, source_target_pairs={{0,16},{16,0},{1,17},{17,1},{2,18},{18,2},{3,19},{19,3},{4,20},{20... | collective-permute-start | bytes 933896 | tf_op jit(solution)/shard_map/ppermute | solution.py:35
  20.6 20.3 %collective-permute-start.12 = (bf16[608,256]{1,0:T(8,128)(2,1)}, bf16[608,256]{1,0:T(8,128)(2,1)S(1)}, u32[]{:S(2)}, u32[]{:S(2)}) collective-permute-start(bf16[608,256]{1,0:T(8,128)(2,1)} %get-tuple-element.105.refs_0_), channel_id=1, source_target_pairs={{0,1},{1,0},{2,3},{3,2},{4,5},{5,4},{6,7},{7,6},{8,9},{9,8},{10,11... | collective-permute-start | bytes 933896 | tf_op jit(solution)/shard_map/ppermute | solution.py:69
  22.7 36.4 %collective-permute-start.8 = (bf16[608,256]{1,0:T(8,128)(2,1)}, bf16[608,256]{1,0:T(8,128)(2,1)S(1)}, u32[]{:S(2)}, u32[]{:S(2)}) collective-permute-start(bf16[608,256]{1,0:T(8,128)(2,1)} %get-tuple-element.105.refs_0_), channel_id=1, source_target_pairs={{0,2},{1,3},{2,0},{3,1},{4,6},{5,7},{6,4},{7,5},{8,10},{9,11},{10,... | collective-permute-start | bytes 933896 | tf_op jit(solution)/shard_map/ppermute | solution.py:69
  26.0 16.5 %collective-permute-start.11 = (bf16[608,256]{1,0:T(8,128)(2,1)S(1)}, bf16[608,256]{1,0:T(8,128)(2,1)S(1)}, u32[]{:S(2)}, u32[]{:S(2)}) collective-permute-start(bf16[608,256]{1,0:T(8,128)(2,1)S(1)} %multiply_convert_fusion.refs_0_), channel_id=1, source_target_pairs={{0,12},{4,8},{8,4},{12,0},{16,28},{20,24},{24,20},{28,16},{1,13},{... | collective-permute-start | bytes 933896 | tf_op jit(solution)/shard_map/ppermute | solution.py:63
  28.4 15.6 %collective-permute-start.10 = (bf16[608,256]{1,0:T(8,128)(2,1)S(1)}, bf16[608,256]{1,0:T(8,128)(2,1)S(1)}, u32[]{:S(2)}, u32[]{:S(2)}) collective-permute-start(bf16[608,256]{1,0:T(8,128)(2,1)S(1)} %multiply_convert_fusion.refs_0_), channel_id=1, source_target_pairs={{0,8},{4,12},{8,0},{12,4},{16,20},{20,16},{24,28},{28,24},{1,9},{5... | collective-permute-start | bytes 933896 | tf_op jit(solution)/shard_map/ppermute | solution.py:63
  29.0 16.2 %collective-permute-start.9 = (bf16[608,256]{1,0:T(8,128)(2,1)S(1)}, bf16[608,256]{1,0:T(8,128)(2,1)S(1)}, u32[]{:S(2)}, u32[]{:S(2)}) collective-permute-start(bf16[608,256]{1,0:T(8,128)(2,1)S(1)} %multiply_convert_fusion.refs_0_), channel_id=1, source_target_pairs={{0,4},{4,0},{8,12},{12,8},{16,24},{20,28},{24,16},{28,20},{1,5},{5... | collective-permute-start | bytes 933896 | tf_op jit(solution)/shard_map/ppermute | solution.py:63
  40.9 18.2 %copy-start.13 = (bf16[608,256]{1,0:T(8,128)(2,1)}, bf16[608,256]{1,0:T(8,128)(2,1)S(1)}, u32[]{:S(2)}) copy-start(bf16[608,256]{1,0:T(8,128)(2,1)S(1)} %collective-permute-done.12.refs_1_) | copy-start | bytes 933892
  40.9 18.2 %collective-permute-start.5 = (bf16[608,256]{1,0:T(8,128)(2,1)S(1)}, bf16[608,256]{1,0:T(8,128)(2,1)S(1)}, u32[]{:S(2)}, u32[]{:S(2)}) collective-permute-start(bf16[608,256]{1,0:T(8,128)(2,1)S(1)} %get-tuple-element.71), channel_id=1, source_target_pairs={{0,4},{4,0},{8,12},{12,8},{16,24},{20,28},{24,16},{28,20},{1,5},{5... | collective-permute-start | bytes 933896 | tf_op jit(solution)/shard_map/ppermute | solution.py:63
  42.5 16.7 %collective-permute-start.6 = (bf16[608,256]{1,0:T(8,128)(2,1)S(1)}, bf16[608,256]{1,0:T(8,128)(2,1)S(1)}, u32[]{:S(2)}, u32[]{:S(2)}) collective-permute-start(bf16[608,256]{1,0:T(8,128)(2,1)S(1)} %get-tuple-element.72), channel_id=1, source_target_pairs={{0,8},{4,12},{8,0},{12,4},{16,20},{20,16},{24,28},{28,24},{1,9},{5... | collective-permute-start | bytes 933896 | tf_op jit(solution)/shard_map/ppermute | solution.py:63
  44.0 15.2 %collective-permute-start.7 = (bf16[608,256]{1,0:T(8,128)(2,1)S(1)}, bf16[608,256]{1,0:T(8,128)(2,1)S(1)}, u32[]{:S(2)}, u32[]{:S(2)}) collective-permute-start(bf16[608,256]{1,0:T(8,128)(2,1)S(1)} %get-tuple-element.73), channel_id=1, source_target_pairs={{0,12},{4,8},{8,4},{12,0},{16,28},{20,24},{24,20},{28,16},{1,13},{... | collective-permute-start | bytes 933896 | tf_op jit(solution)/shard_map/ppermute | solution.py:63
  61.4 19.9 %copy-start.21 = (bf16[608,256]{1,0:T(8,128)(2,1)}, bf16[608,256]{1,0:T(8,128)(2,1)S(1)}, u32[]{:S(2)}) copy-start(bf16[608,256]{1,0:T(8,128)(2,1)S(1)} %get-tuple-element.113) | copy-start | bytes 933892
  61.5 38.1 %copy-start = (bf16[608,2432]{1,0:T(8,128)(2,1)S(1)}, bf16[608,2432]{1,0:T(8,128)(2,1)}, u32[]{:S(2)}) copy-start(bf16[608,2432]{1,0:T(8,128)(2,1)} %weight.3) | copy-start | bytes 8871940
  61.5 1.4 %collective-permute-start.13 = (bf16[608,128]{1,0:T(8,128)(2,1)S(1)}, bf16[608,128]{1,0:T(8,128)(2,1)S(1)}, u32[]{:S(2)}, u32[]{:S(2)}) collective-permute-start(bf16[608,128]{1,0:T(8,128)(2,1)S(1)} %slice.65), channel_id=1, source_target_pairs={{0,16},{16,0},{1,17},{17,1},{2,18},{18,2},{3,19},{19,3},{4,20},{20... | collective-permute-start | bytes 466952 | tf_op jit(solution)/shard_map/ppermute | solution.py:35
  63.0 8.8 %collective-permute-start.24 = (bf16[608,128]{1,0:T(8,128)(2,1)S(1)}, bf16[608,128]{1,0:T(8,128)(2,1)S(1)}, u32[]{:S(2)}, u32[]{:S(2)}) collective-permute-start(bf16[608,128]{1,0:T(8,128)(2,1)S(1)} %slice_select_fusion.refs_0_.refs_2_), channel_id=1, source_target_pairs={{0,3},{1,2},{2,1},{3,0},{4,7},{5,6},{6,5},{7,4},{8,11},{9,10},{10,... | collective-permute-start | bytes 466952 | tf_op jit(solution)/shard_map/ppermute | solution.py:69
  63.8 15.2 %collective-permute-start.23 = (bf16[608,128]{1,0:T(8,128)(2,1)S(1)}, bf16[608,128]{1,0:T(8,128)(2,1)S(1)}, u32[]{:S(2)}, u32[]{:S(2)}) collective-permute-start(bf16[608,128]{1,0:T(8,128)(2,1)S(1)} %slice_select_fusion.refs_0_.refs_2_), channel_id=1, source_target_pairs={{0,2},{1,3},{2,0},{3,1},{4,6},{5,7},{6,4},{7,5},{8,10},{9,11},{10,... | collective-permute-start | bytes 466952 | tf_op jit(solution)/shard_map/ppermute | solution.py:69
  65.0 15.6 %collective-permute-start.14 = (bf16[624,256]{1,0:T(8,128)(2,1)S(1)}, bf16[624,256]{1,0:T(8,128)(2,1)S(1)}, u32[]{:S(2)}, u32[]{:S(2)}) collective-permute-start(bf16[624,256]{1,0:T(8,128)(2,1)S(1)} %get-tuple-element.93), channel_id=1, source_target_pairs={{0,4},{4,0},{8,12},{12,8},{16,24},{20,28},{24,16},{28,20},{1,5},{5... | collective-permute-start | bytes 958472 | tf_op jit(solution)/shard_map/ppermute | solution.py:47
  65.8 15.6 %collective-permute-start.15 = (bf16[624,256]{1,0:T(8,128)(2,1)S(1)}, bf16[624,256]{1,0:T(8,128)(2,1)S(1)}, u32[]{:S(2)}, u32[]{:S(2)}) collective-permute-start(bf16[624,256]{1,0:T(8,128)(2,1)S(1)} %get-tuple-element.94), channel_id=1, source_target_pairs={{0,4},{4,0},{8,12},{12,8},{16,24},{20,28},{24,16},{28,20},{1,5},{5... | collective-permute-start | bytes 958472 | tf_op jit(solution)/shard_map/ppermute | solution.py:47
  67.0 13.6 %collective-permute-start.16 = (bf16[608,128]{1,0:T(8,128)(2,1)S(1)}, bf16[608,128]{1,0:T(8,128)(2,1)S(1)}, u32[]{:S(2)}, u32[]{:S(2)}) collective-permute-start(bf16[608,128]{1,0:T(8,128)(2,1)S(1)} %slice_select_fusion.refs_0_.refs_2_), channel_id=1, source_target_pairs={{0,1},{1,0},{2,3},{3,2},{4,5},{5,4},{6,7},{7,6},{8,9},{9,8},{10,11... | collective-permute-start | bytes 466952 | tf_op jit(solution)/shard_map/ppermute | solution.py:69
  79.8 9.9 %collective-permute-start.25 = (bf16[2,608,128]{2,1,0:T(8,128)(2,1)}, bf16[2,608,128]{2,1,0:T(8,128)(2,1)}, u32[]{:S(2)}, u32[]{:S(2)}) collective-permute-start(bf16[2,608,128]{2,1,0:T(8,128)(2,1)} %pad_maximum_fusion.refs_2_), channel_id=1, source_target_pairs={{0,4},{4,0},{8,12},{12,8},{16,24},{20,28},{24,16},{28,20},{1,5},{5... | collective-permute-start | bytes 933896 | tf_op jit(solution)/shard_map/ppermute | solution.py:47
  82.1 8.4 %collective-permute-start.17 = (bf16[608,128]{1,0:T(8,128)(2,1)S(1)}, bf16[608,128]{1,0:T(8,128)(2,1)}, u32[]{:S(2)}, u32[]{:S(2)}) collective-permute-start(bf16[608,128]{1,0:T(8,128)(2,1)S(1)} %slice_select_fusion.refs_0_.refs_2_), channel_id=1, source_target_pairs={{0,4},{4,0},{8,12},{12,8},{16,24},{20,28},{24,16},{28,20},{1,5},{5... | collective-permute-start | bytes 466952 | tf_op jit(solution)/shard_map/ppermute | solution.py:47
  87.6 14.6 %collective-permute-start.21 = (bf16[624,256]{1,0:T(8,128)(2,1)S(1)}, bf16[624,256]{1,0:T(8,128)(2,1)S(1)}, u32[]{:S(2)}, u32[]{:S(2)}) collective-permute-start(bf16[624,256]{1,0:T(8,128)(2,1)S(1)} %get-tuple-element.101), channel_id=1, source_target_pairs={{0,8},{4,12},{8,0},{12,4},{16,20},{20,16},{24,28},{28,24},{1,9},{5... | collective-permute-start | bytes 958472 | tf_op jit(solution)/shard_map/ppermute | solution.py:47
  88.4 13.1 %collective-permute-start.33 = (bf16[608,128]{1,0:T(8,128)(2,1)S(1)}, bf16[608,128]{1,0:T(8,128)(2,1)S(1)}, u32[]{:S(2)}, u32[]{:S(2)}) collective-permute-start(bf16[608,128]{1,0:T(8,128)(2,1)S(1)} %slice_select_fusion.refs_0_.refs_2_), channel_id=1, source_target_pairs={{0,16},{16,0},{1,17},{17,1},{2,18},{18,2},{3,19},{19,3},{4,20},{20... | collective-permute-start | bytes 466952 | tf_op jit(solution)/shard_map/ppermute | solution.py:35
  88.4 9.5 %collective-permute-start.18 = (bf16[608,128]{1,0:T(8,128)(2,1)S(1)}, bf16[608,128]{1,0:T(8,128)(2,1)S(1)}, u32[]{:S(2)}, u32[]{:S(2)}) collective-permute-start(bf16[608,128]{1,0:T(8,128)(2,1)S(1)} %slice_select_fusion.refs_0_.refs_2_), channel_id=1, source_target_pairs={{0,8},{4,12},{8,0},{12,4},{16,20},{20,16},{24,28},{28,24},{1,9},{5... | collective-permute-start | bytes 466952 | tf_op jit(solution)/shard_map/ppermute | solution.py:47
  89.7 7.2 %collective-permute-start.22 = (bf16[608,128]{1,0:T(8,128)(2,1)}, bf16[608,128]{1,0:T(8,128)(2,1)S(1)}, u32[]{:S(2)}, u32[]{:S(2)}) collective-permute-start(bf16[608,128]{1,0:T(8,128)(2,1)} %copy-done.17), channel_id=1, source_target_pairs={{0,4},{4,0},{8,12},{12,8},{16,24},{20,28},{24,16},{28,20},{1,5},{5... | collective-permute-start | bytes 466952 | tf_op jit(solution)/shard_map/ppermute | solution.py:47
  90.5 9.2 %collective-permute-start.19 = (bf16[608,128]{1,0:T(8,128)(2,1)}, bf16[608,128]{1,0:T(8,128)(2,1)S(1)}, u32[]{:S(2)}, u32[]{:S(2)}) collective-permute-start(bf16[608,128]{1,0:T(8,128)(2,1)} %collective-permute-done.17.refs_1_.refs_3_), channel_id=1, source_target_pairs={{0,8},{4,12},{8,0},{12,4},{16,20},{20,16},{24,28},{28,24},{1,9},{5... | collective-permute-start | bytes 466952 | tf_op jit(solution)/shard_map/ppermute | solution.py:47
  92.0 16.9 %copy-start.25 = (f32[608,128]{1,0:T(8,128)S(1)}, f32[608,128]{1,0:T(8,128)}, u32[]{:S(2)}) copy-start(f32[608,128]{1,0:T(8,128)} %copy-done.24) | copy-start | bytes 933892
  96.8 8.3 %collective-permute-start.39 = (bf16[608,128]{1,0:T(8,128)(2,1)}, bf16[608,128]{1,0:T(8,128)(2,1)S(1)}, u32[]{:S(2)}, u32[]{:S(2)}) collective-permute-start(bf16[608,128]{1,0:T(8,128)(2,1)} %copy-done.17), channel_id=1, source_target_pairs={{0,16},{16,0},{1,17},{17,1},{2,18},{18,2},{3,19},{19,3},{4,20},{20... | collective-permute-start | bytes 466952 | tf_op jit(solution)/shard_map/ppermute | solution.py:35
  97.9 8.1 %collective-permute-start.37 = (bf16[608,128]{1,0:T(8,128)(2,1)}, bf16[608,128]{1,0:T(8,128)(2,1)S(1)}, u32[]{:S(2)}, u32[]{:S(2)}) collective-permute-start(bf16[608,128]{1,0:T(8,128)(2,1)} %copy-done.17), channel_id=1, source_target_pairs={{0,8},{4,12},{8,0},{12,4},{16,20},{20,16},{24,28},{28,24},{1,9},{5... | collective-permute-start | bytes 466952 | tf_op jit(solution)/shard_map/ppermute | solution.py:47
  99.6 6.4 %collective-permute-start.40 = (bf16[608,128]{1,0:T(8,128)(2,1)S(1)}, bf16[608,128]{1,0:T(8,128)(2,1)S(1)}, u32[]{:S(2)}, u32[]{:S(2)}) collective-permute-start(bf16[608,128]{1,0:T(8,128)(2,1)S(1)} %collective-permute-done.22.refs_11_), channel_id=1, source_target_pairs={{0,16},{16,0},{1,17},{17,1},{2,18},{18,2},{3,19},{19,3},{4,20},{20... | collective-permute-start | bytes 466952 | tf_op jit(solution)/shard_map/ppermute | solution.py:35
  101.5 1.6 %collective-permute-start.35 = (bf16[608,128]{1,0:T(8,128)(2,1)S(1)}, bf16[608,128]{1,0:T(8,128)(2,1)S(1)}, u32[]{:S(2)}, u32[]{:S(2)}) collective-permute-start(bf16[608,128]{1,0:T(8,128)(2,1)S(1)} %collective-permute-done.18.refs_2_.refs_4_), channel_id=1, source_target_pairs={{0,16},{16,0},{1,17},{17,1},{2,18},{18,2},{3,19},{19,3},{4,20},{20... | collective-permute-start | bytes 466952 | tf_op jit(solution)/shard_map/ppermute | solution.py:35
  102.1 1.8 %collective-permute-start.34 = (bf16[608,128]{1,0:T(8,128)(2,1)}, bf16[608,128]{1,0:T(8,128)(2,1)S(1)}, u32[]{:S(2)}, u32[]{:S(2)}) collective-permute-start(bf16[608,128]{1,0:T(8,128)(2,1)} %collective-permute-done.17.refs_1_.refs_3_), channel_id=1, source_target_pairs={{0,16},{16,0},{1,17},{17,1},{2,18},{18,2},{3,19},{19,3},{4,20},{20... | collective-permute-start | bytes 466952 | tf_op jit(solution)/shard_map/ppermute | solution.py:35
  103.1 5.2 %collective-permute-start.38 = (bf16[608,128]{1,0:T(8,128)(2,1)S(1)}, bf16[608,128]{1,0:T(8,128)(2,1)S(1)}, u32[]{:S(2)}, u32[]{:S(2)}) collective-permute-start(bf16[608,128]{1,0:T(8,128)(2,1)S(1)} %collective-permute-done.22.refs_11_), channel_id=1, source_target_pairs={{0,8},{4,12},{8,0},{12,4},{16,20},{20,16},{24,28},{28,24},{1,9},{5... | collective-permute-start | bytes 466952 | tf_op jit(solution)/shard_map/ppermute | solution.py:47
  104.0 7.8 %collective-permute-start.27 = (bf16[2,608,128]{2,1,0:T(8,128)(2,1)}, bf16[2,608,128]{2,1,0:T(8,128)(2,1)S(1)}, u32[]{:S(2)}, u32[]{:S(2)}) collective-permute-start(bf16[2,608,128]{2,1,0:T(8,128)(2,1)} %pad_maximum_fusion.refs_2_), channel_id=1, source_target_pairs={{0,8},{4,12},{8,0},{12,4},{16,20},{20,16},{24,28},{28,24},{1,9},{5... | collective-permute-start | bytes 933896 | tf_op jit(solution)/shard_map/ppermute | solution.py:47
  105.2 9.9 %collective-permute-start.28 = (bf16[2,608,128]{2,1,0:T(8,128)(2,1)}, bf16[2,608,128]{2,1,0:T(8,128)(2,1)S(1)}, u32[]{:S(2)}, u32[]{:S(2)}) collective-permute-start(bf16[2,608,128]{2,1,0:T(8,128)(2,1)} %collective-permute-done.25.refs_3_), channel_id=1, source_target_pairs={{0,8},{4,12},{8,0},{12,4},{16,20},{20,16},{24,28},{28,24},{1,9},{5... | collective-permute-start | bytes 933896 | tf_op jit(solution)/shard_map/ppermute | solution.py:47
  106.0 9.0 %collective-permute-start.20 = (f32[608,128]{1,0:T(8,128)S(1)}, f32[608,128]{1,0:T(8,128)S(1)}, u32[]{:S(2)}, u32[]{:S(2)}) collective-permute-start(f32[608,128]{1,0:T(8,128)S(1)} %residual_rows.1), channel_id=1, source_target_pairs={{0,16},{16,0},{1,17},{17,1},{2,18},{18,2},{3,19},{19,3},{4,20},{20... | collective-permute-start | bytes 933896 | tf_op jit(solution)/shard_map/ppermute | solution.py:35
  106.0 2.4 %collective-permute-start.36 = (bf16[608,128]{1,0:T(8,128)(2,1)S(1)}, bf16[608,128]{1,0:T(8,128)(2,1)S(1)}, u32[]{:S(2)}, u32[]{:S(2)}) collective-permute-start(bf16[608,128]{1,0:T(8,128)(2,1)S(1)} %collective-permute-done.19.refs_3_.refs_5_), channel_id=1, source_target_pairs={{0,16},{16,0},{1,17},{17,1},{2,18},{18,2},{3,19},{19,3},{4,20},{20... | collective-permute-start | bytes 466952 | tf_op jit(solution)/shard_map/ppermute | solution.py:35
  108.4 2.8 %collective-permute-start.41 = (bf16[608,128]{1,0:T(8,128)(2,1)S(1)}, bf16[608,128]{1,0:T(8,128)(2,1)S(1)}, u32[]{:S(2)}, u32[]{:S(2)}) collective-permute-start(bf16[608,128]{1,0:T(8,128)(2,1)S(1)} %collective-permute-done.37.refs_12_), channel_id=1, source_target_pairs={{0,16},{16,0},{1,17},{17,1},{2,18},{18,2},{3,19},{19,3},{4,20},{20... | collective-permute-start | bytes 466952 | tf_op jit(solution)/shard_map/ppermute | solution.py:35
  108.4 2.9 %collective-permute-start.42 = (bf16[608,128]{1,0:T(8,128)(2,1)S(1)}, bf16[608,128]{1,0:T(8,128)(2,1)S(1)}, u32[]{:S(2)}, u32[]{:S(2)}) collective-permute-start(bf16[608,128]{1,0:T(8,128)(2,1)S(1)} %collective-permute-done.38.refs_13_), channel_id=1, source_target_pairs={{0,16},{16,0},{1,17},{17,1},{2,18},{18,2},{3,19},{19,3},{4,20},{20... | collective-permute-start | bytes 466952 | tf_op jit(solution)/shard_map/ppermute | solution.py:35
  111.2 12.0 %collective-permute-start.29 = (bf16[2,608,128]{2,1,0:T(8,128)(2,1)}, bf16[2,608,128]{2,1,0:T(8,128)(2,1)S(1)}, u32[]{:S(2)}, u32[]{:S(2)}) collective-permute-start(bf16[2,608,128]{2,1,0:T(8,128)(2,1)} %pad_maximum_fusion.refs_2_), channel_id=1, source_target_pairs={{0,16},{16,0},{1,17},{17,1},{2,18},{18,2},{3,19},{19,3},{4,20},{20... | collective-permute-start | bytes 933896 | tf_op jit(solution)/shard_map/ppermute | solution.py:35
  111.3 12.0 %collective-permute-start.30 = (bf16[2,608,128]{2,1,0:T(8,128)(2,1)}, bf16[2,608,128]{2,1,0:T(8,128)(2,1)S(1)}, u32[]{:S(2)}, u32[]{:S(2)}) collective-permute-start(bf16[2,608,128]{2,1,0:T(8,128)(2,1)} %collective-permute-done.25.refs_3_), channel_id=1, source_target_pairs={{0,16},{16,0},{1,17},{17,1},{2,18},{18,2},{3,19},{19,3},{4,20},{20... | collective-permute-start | bytes 933896 | tf_op jit(solution)/shard_map/ppermute | solution.py:35
  111.8 11.5 %collective-permute-start.26 = (bf16[608,256]{1,0:T(8,128)(2,1)}, bf16[608,256]{1,0:T(8,128)(2,1)S(1)}, u32[]{:S(2)}, u32[]{:S(2)}) collective-permute-start(bf16[608,256]{1,0:T(8,128)(2,1)} %get-tuple-element.105.refs_0_), channel_id=1, source_target_pairs={{0,3},{1,2},{2,1},{3,0},{4,7},{5,6},{6,5},{7,4},{8,11},{9,10},{10,... | collective-permute-start | bytes 933896 | tf_op jit(solution)/shard_map/ppermute | solution.py:69
  115.0 8.2 %collective-permute-start.31 = (bf16[2,608,128]{2,1,0:T(8,128)(2,1)S(1)}, bf16[2,608,128]{2,1,0:T(8,128)(2,1)S(1)}, u32[]{:S(2)}, u32[]{:S(2)}) collective-permute-start(bf16[2,608,128]{2,1,0:T(8,128)(2,1)S(1)} %collective-permute-done.27.refs_4_), channel_id=1, source_target_pairs={{0,16},{16,0},{1,17},{17,1},{2,18},{18,2},{3,19},{19,3},{4,20},{20... | collective-permute-start | bytes 933896 | tf_op jit(solution)/shard_map/ppermute | solution.py:35
  115.1 8.2 %collective-permute-start.32 = (bf16[2,608,128]{2,1,0:T(8,128)(2,1)S(1)}, bf16[2,608,128]{2,1,0:T(8,128)(2,1)S(1)}, u32[]{:S(2)}, u32[]{:S(2)}) collective-permute-start(bf16[2,608,128]{2,1,0:T(8,128)(2,1)S(1)} %collective-permute-done.28.refs_5_), channel_id=1, source_target_pairs={{0,16},{16,0},{1,17},{17,1},{2,18},{18,2},{3,19},{19,3},{4,20},{20... | collective-permute-start | bytes 933896 | tf_op jit(solution)/shard_map/ppermute | solution.py:35
  (21 other events, 106.3 us)

commit v12 on v11

--- a/solution.py
+++ b/solution.py
@@ -470,26 +470,19 @@
     )(order, weight, *stack)
 
 
-def zero_grad_kernel(blocks, first, count, order, dp_order, *refs):
+def zero_grad_kernel(blocks, order, dp_order, *refs):
+    refs, (out, lhs, rhs, stage, parked, loads, buf, sems) = refs[:-8], refs[-8:]
+    count = len(refs) - 4 * blocks
     cots, refs = refs[:count], refs[count:]
-    stacks = []
-    while len(refs) > (9 if first else 6):
-        stacks.append((refs[:blocks], refs[blocks : 2 * blocks]))
-        refs = refs[2 * blocks :]
-    before = None
-    if first:
-        before, out, lhs, rhs, stage, parked, loads, buf, sems = refs
-    else:
-        buf, lhs, rhs, stage, parked, loads = refs
-    rows, half = stacks[0][0][0].shape[-2:]
+    near, far = [[refs[(k + side) * blocks : (k + side + 1) * blocks] for side in range(2)] for k in (0, 2)]
+    rows, half = near[0][0].shape
     group = order[blocks]
     moves, places = [], []
     for part in range(count):
-        slot = part // 2 * 2 + (dp_order[first + part] & 1)
-        both = pl.ds(pl.multiple_of(slot * 2 * half, 2 * half), 2 * half)
+        both = pl.ds(pl.multiple_of(dp_order[part] * 2 * half, 2 * half), 2 * half)
         moves.append((cots[part], lhs.at[:, both]))
         for side, owner in enumerate((group, 1 - group)):
-            lanes = pl.ds(pl.multiple_of((slot * 2 + owner) * half, half), half)
+            lanes = pl.ds(pl.multiple_of((dp_order[part] * 2 + owner) * half, half), half)
             values = []
             for place in range(blocks):
                 if rows % 16:
@@ -499,8 +492,7 @@
                 else:
                     offset = pl.multiple_of(order[side * (blocks + 1) + place] * rows, 16)
                     target = rhs.at[pl.ds(offset, rows), lanes]
-                source = stacks[part][side][place] if len(stacks) == count else stacks[0][side][place].at[part]
-                moves.append((source, target))
+                moves.append((near[side][place] if part == 0 else far[side][place].at[part - 1], target))
             places.append((lanes, values, side * (blocks + 1)))
     moves = [pltpu.make_async_copy(a, b, loads.at[k]) for k, (a, b) in enumerate(moves)]
     for move in moves:
@@ -514,41 +506,35 @@
     for k, (start, size) in enumerate(pieces(0, blocks * rows)):
         columns = pl.ds(start, size)
         value = against_rows(lhs[...], rhs[columns, :])
-        buf[:, columns] = value if before is None else before[:, columns] + value
-        if before is not None:
-            copies.append(pltpu.make_async_copy(buf.at[:, columns], out.at[:, columns], sems.at[k]))
-            copies[-1].start()
+        buf[:, columns] = value
+        copies.append(pltpu.make_async_copy(buf.at[:, columns], out.at[:, columns], sems.at[k]))
+        copies[-1].start()
     for copy in copies:
         copy.wait()
 
 
-def zero_projection_grad(order, dp_order, first, cots, stacks, before, name):
-    blocks, (rows, half) = len(stacks[0][0]), stacks[0][0][0].shape[-2:]
+def zero_projection_grad(order, dp_order, cots, near, far, name):
+    blocks, (rows, half) = len(near[0]), near[0][0].shape
     count = len(cots)
-    flat = [block for pair in stacks for side in pair for block in side]
     features, tokens = blocks * rows, count * 2 * half
-    extra = [] if before is None else [before]
-    scratch = [
-        pltpu.VMEM((rows, tokens), BF16),
-        pltpu.VMEM((features, tokens), BF16),
-        staging(rows, features, half),
-        pltpu.VMEM((count * 2 * blocks, rows, half) if rows % 16 else (1, 8, 128), BF16),
-        pltpu.SemaphoreType.DMA((count * (2 * blocks + 1),)),
-    ]
-    if extra:
-        scratch += [
+    flat = [block for pair in (near, far) for side in pair for block in side]
+    return pl.pallas_call(
+        functools.partial(zero_grad_kernel, blocks),
+        out_shape=struct((rows, features), F32),
+        in_specs=[SCALARS] * 2 + [ANYWHERE] * (count + len(flat)),
+        out_specs=HELD,
+        scratch_shapes=[
+            pltpu.VMEM((rows, tokens), BF16),
+            pltpu.VMEM((features, tokens), BF16),
+            staging(rows, features, half),
+            pltpu.VMEM((count * 2 * blocks, rows, half) if rows % 16 else (1, 8, 128), BF16),
+            pltpu.SemaphoreType.DMA((count * (2 * blocks + 1),)),
             pltpu.VMEM((rows, features), F32),
             pltpu.SemaphoreType.DMA((len(pieces(0, features)),)),
-        ]
-    return pl.pallas_call(
-        functools.partial(zero_grad_kernel, blocks, first, count),
-        out_shape=struct((rows, features), F32),
-        in_specs=[SCALARS] * 2 + [ANYWHERE] * (count + len(flat)) + [WHOLE] * len(extra),
-        out_specs=HELD if extra else WHOLE,
-        scratch_shapes=scratch,
+        ],
         name=name,
-        **params(2 * tokens * rows * features, 4 * rows * features + 2 * tokens * (rows + features), grant=28),
-    )(order, dp_order, *cots, *flat, *extra)
+        **params(2 * tokens * rows * features, 4 * rows * features + 2 * tokens * (rows + features), grant=32),
+    )(order, dp_order, *cots, *flat)
 
 
 def steps(values, level, *during):
@@ -592,17 +578,11 @@
     slope_b, kept, sent = forward_last(
         order, after(normed, grad_rows), total, w_in, w_out, split, blocks, "forward_last"
     )
-    got, cot_near = lax.optimization_barrier((
-        [send(grad_rows, place) for place in range(1, blocks)], gather_dp(cot1_rows, 1, 2), kept
-    ))[:2]
-    gathered, cots = [grad_rows] + got, [cot1_rows] + cot_near
+    gathered = [grad_rows] + direct([grad_rows] * (blocks - 1), kept)
     norm_sent, norm_kept, token_sums = backward(
         order, after(gathered, *sent), slope_a, slope_b, acts, stats, mod, w_in, w_out, "backward"
     )
-    got, cot_far = lax.optimization_barrier((
-        [send(value, place + 1) for place, value in enumerate(sent)], gather_dp(cots[0], 2, 3), token_sums
-    ))[:2]
-    cots = cots + cot_far
+    got = direct(sent, token_sums)
     own_values = block_of(acts[0], me, rows).astype(F32)
     sums = own_values + own_gate * (kept + sum(value.astype(F32) for value in got))
     out_rows = sums.astype(BF16)
@@ -618,12 +598,15 @@
         near = near + steps(near, level)
         if level + 1 < levels:
             sent, kept, token_sums = fold(got, kept, token_sums)
-    gathers = [[nearest], [jnp.stack(far[1:])]]
+    others = [jnp.stack([nearest] + far[1:])]
+    cots = [cot1_rows]
     for level in range(levels):
-        gathers = [gather + steps(gather, level) for gather in gathers]
-        if level == 0:
-            gathers, first = lax.optimization_barrier((gathers, cots[0]))
-            cots = cots + gather_dp(first, 3)
+        others = others + steps(others, level)
+        if level < 2:
+            tied = after(cot1_rows, far if level == 0 else cots[-1])
+            arrived = gather_dp(tied, 1, 3) if level == 0 else gather_dp(tied, 3)
+            others, arrived = lax.optimization_barrier((others, arrived))
+            cots = cots + arrived
     more = unpack_sums(got[0][-16:])
     plain, along = token_sums[0:1] + more[0], token_sums[1:2] + more[1]
     kept = [kept[0] + got[0][:rows].astype(F32)]
@@ -635,9 +618,8 @@
     residual = jnp.concatenate([swap_grp(residual), residual], 1)
     block_rows = jnp.where(is_control, out_rows, (sums + residual).astype(BF16))
 
-    stacks = [(mine, [swap_grp(value) for value in mine]) for mine in [near] + gathers]
-    zero_grad = zero_projection_grad(order, dp_order, 0, cots[:2], stacks[:2], None, "zero_projection_grad_first")
-    zero_grad = zero_projection_grad(order, dp_order, 2, cots[2:], stacks[2:], zero_grad, "zero_projection_grad_last")
+    near, far = [(mine, [swap_grp(value) for value in mine]) for mine in (near, others)]
+    zero_grad = zero_projection_grad(order, dp_order, cots, near, far, "zero_projection_grad")
     return (block_rows[None], (up_rows + back)[None], zero_grad)
 
 

time: 129 us -> 129 us (level)
  starting transfers between devices: 38.2 us -> 31.6 us
  waiting for transfers between devices: 25.8 us -> 31.5 us
  other arithmetic: 7.54 us -> 9.68 us
  Pallas kernels: 47.5 us -> 46.1 us
    ppermute x6, waiting for transfers between devices: 12.8 us -> 20 us  [gather_dp(): lax.ppermute(value, 'dp', [(i, i ^ mask) for i in range(length)])]
    ppermute x12 -> x9, starting transfers between devices: 12.1 us -> 8.81 us  [step(): return lax.ppermute(value, ('grp', 'fsdp'), pairs)]
    ppermute x12 -> x9, waiting for transfers between devices: 10.6 us -> 8.38 us  [step(): return lax.ppermute(value, ('grp', 'fsdp'), pairs)]
    ppermute x6, starting transfers between devices: 10.5 us -> 8.95 us  [gather_dp(): lax.ppermute(value, 'dp', [(i, i ^ mask) for i in range(length)])]
    pallas_call x2 -> x1, Pallas kernels: 8.68 us -> 7.31 us  [zero_projection_grad(): pl.pallas_call(functools.partial(zero_grad_kernel, blocks), out_shape=str...]
    ppermute x16 -> x12, starting transfers between devices: 3.43 us -> 2.27 us  [swap_grp(): return lax.ppermute(value, 'grp', [(0, 1), (1, 0)])]
    ppermute x16 -> x12, waiting for transfers between devices: 2.33 us -> 3.16 us  [swap_grp(): return lax.ppermute(value, 'grp', [(0, 1), (1, 0)])]
    unnamed x53 -> x33, local copies, waits for them, and re-layouts: 8.33 us -> 8.28 us
  transfers between devices with their start and end apart: 43 -> 36, of which waited for: 10 -> 12; matrix products, arithmetic and copies ran while one was open for 5% -> 4% of each run, Pallas kernels for 30% -> 27%
where the time goes in v12:
time: 129 us; the launch traced here: 128 us
  Pallas kernels  46.1 us (36%)
  starting transfers between devices  31.6 us (24%)
  waiting for transfers between devices  31.5 us (24%)
  other arithmetic  9.68 us (8%)
  local copies, waits for them, and re-layouts  8.3 us (6%)
    ppermute x6, waiting for transfers between devices, gather_dp(): lax.ppermute(value, 'dp', [(i, i ^ mask) for i in range(length)])  20 us
    pallas_call x1, Pallas kernels, backward(): pl.pallas_call(functools.partial(backward_kernel, blocks, rows), out_shap...  13.9 us
    ppermute x9, starting transfers between devices, send(): return lax.ppermute(value, ('grp', 'fsdp'), pairs)  11.6 us
    pallas_call x1, Pallas kernels, forward_last(): pl.pallas_call(functools.partial(forward_last_kernel, start), out_shape=[...  11.4 us
    ppermute x6, starting transfers between devices, gather_dp(): lax.ppermute(value, 'dp', [(i, i ^ mask) for i in range(length)])  8.95 us
    ppermute x9, starting transfers between devices, step(): return lax.ppermute(value, ('grp', 'fsdp'), pairs)  8.81 us
    ppermute x9, waiting for transfers between devices, step(): return lax.ppermute(value, ('grp', 'fsdp'), pairs)  8.38 us
    unnamed x33, local copies, waits for them, and re-layouts  8.28 us
  transfers between devices with their start and end apart: 36, of which 12 were waited for; matrix products, arithmetic and copies ran while one was open for 4% of the time, Pallas kernels for 27%

profile of v12, /device:TPU:0, one launch (start us, length us, event | category | flops | bytes accessed | tf_op | source)
XLA Modules:
  0.0 128.2 jit_solution(11600073560947119134)
XLA Ops:
  1.1 0.8 copy.13.modulation
  1.9 0.7 fusion.14
  2.7 1.0 copy-done.2
  3.6 4.0 %prepare.1 = (f32[608,128]{1,0:T(8,128)S(1)}, bf16[608,128]{1,0:T(8,128)(2,1)S(1)}, bf16[608,128]{1,0:T(8,128)(2,1)S(1)}, bf16[608,128]{1,0:T(8,128)(2,1)S(1)}, ...) custom-call(s32[9]{0:T(128)S(1)} %pad_add_fusion.order, ...), custom_call_target="tpu_custom_call" | custom-call | flops 378535936 | bytes 4202496 | tf_op jit(solution)/shard_map/prepare/pallas_call | solution.py:430
  7.6 2.9 %collective-permute-start.1 = (bf16[608,128]{1,0:T(8,128)(2,1)S(1)}, bf16[608,128]{1,0:T(8,128)(2,1)S(1)}, u32[]{:S(2)}, u32[]{:S(2)}) collective-permute-start(bf16[608,128]{1,0:T(8,128)(2,1)S(1)} %get-tuple-element.62), channel_id=1, source_target_pairs={{0,4},{4,0},{8,12},{12,8},{16,24},{20,28},{24,16},{28,20},{1,5},{5... | collective-permute-start | bytes 466952 | tf_op jit(solution)/shard_map/ppermute | solution.py:63
  10.5 1.5 %collective-permute-start.2 = (bf16[608,128]{1,0:T(8,128)(2,1)S(1)}, bf16[608,128]{1,0:T(8,128)(2,1)S(1)}, u32[]{:S(2)}, u32[]{:S(2)}) collective-permute-start(bf16[608,128]{1,0:T(8,128)(2,1)S(1)} %get-tuple-element.63), channel_id=1, source_target_pairs={{0,8},{4,12},{8,0},{12,4},{16,20},{20,16},{24,28},{28,24},{1,9},{5... | collective-permute-start | bytes 466952 | tf_op jit(solution)/shard_map/ppermute | solution.py:63
  12.0 7.4 %forward_first.1 = (f32[256,1024]{1,0:T(8,128)S(1)}, f32[256,2432]{1,0:T(8,128)}, f32[2432,8]{1,0:T(8,128)S(1)}) custom-call(bf16[256,2432]{1,0:T(8,128)(2,1)S(1)} %get-tuple-element.73.normed, f32[1,3,2432]{2,1,0:T(4,128)S(1)} %copy.13.modulation, bf16[1,2432,2432]{2,1,0:T(8,128)(2,1)} %refs_9_.1, bf16[1,2432,2432]{2,1,0:T(8,128)(2,1)} %refs_10_.1), custom_call_target="tpu_custom_call" | custom-call | flops 2550136832 | bytes 12451840 | tf_op jit(solution)/shard_map/forward_first/pallas_call | solution.py:253
  19.5 1.0 copy-done.4
  20.4 0.8 add_add_fusion
  21.7 1.5 %collective-permute-done.4 = f32[608,128]{1,0:T(8,128)} collective-permute-done((f32[608,128]{1,0:T(8,128)}, f32[608,128]{1,0:T(8,128)}, u32[]{:S(2)}, u32[]{:S(2)}) %collective-permute-start.4) | collective-permute-done | bytes 311328 | tf_op jit(solution)/shard_map/ppermute | solution.py:35
  23.2 1.2 multiply_convert_fusion.refs_0_
  24.4 3.0 %collective-permute-start.10 = (bf16[608,256]{1,0:T(8,128)(2,1)S(1)}, bf16[608,256]{1,0:T(8,128)(2,1)S(1)}, u32[]{:S(2)}, u32[]{:S(2)}) collective-permute-start(bf16[608,256]{1,0:T(8,128)(2,1)S(1)} %multiply_convert_fusion.refs_0_), channel_id=1, source_target_pairs={{0,12},{4,8},{8,4},{12,0},{16,28},{20,24},{24,20},{28,16},{1,13},{... | collective-permute-start | bytes 933896 | tf_op jit(solution)/shard_map/ppermute | solution.py:63
  28.1 11.4 %forward_last.1 = (f32[256,1408]{1,0:T(8,128)}, f32[608,256]{1,0:T(8,128)S(1)}, bf16[608,256]{1,0:T(8,128)(2,1)S(1)}, bf16[608,256]{1,0:T(8,128)(2,1)S(1)}, bf16[608,256]{1,0:T(8,128)(2,1)S(1)}) custom-call(s32[9]{0:T(128)S(1)} %pad_add_fusion.order, bf16[256,2432]{1,0:T(8,128)(2,1)S(1)} %get-tuple-element.73.normed, f32[256,2432]{1,0:T(8,128)} %get-tuple-element.69.before, ...), custom_call_target="tpu_custom_call" | custom-call | flops 3506438144 | bytes 16187392 | tf_op jit(solution)/shard_map/forward_last/pallas_call | solution.py:267
  39.4 1.9 %collective-permute-start.5 = (bf16[608,256]{1,0:T(8,128)(2,1)S(1)}, bf16[608,256]{1,0:T(8,128)(2,1)S(1)}, u32[]{:S(2)}, u32[]{:S(2)}) collective-permute-start(bf16[608,256]{1,0:T(8,128)(2,1)S(1)} %get-tuple-element.75), channel_id=1, source_target_pairs={{0,4},{4,0},{8,12},{12,8},{16,24},{20,28},{24,16},{28,20},{1,5},{5... | collective-permute-start | bytes 933896 | tf_op jit(solution)/shard_map/ppermute | solution.py:63
  41.4 1.5 %collective-permute-start.6 = (bf16[608,256]{1,0:T(8,128)(2,1)S(1)}, bf16[608,256]{1,0:T(8,128)(2,1)S(1)}, u32[]{:S(2)}, u32[]{:S(2)}) collective-permute-start(bf16[608,256]{1,0:T(8,128)(2,1)S(1)} %get-tuple-element.76), channel_id=1, source_target_pairs={{0,8},{4,12},{8,0},{12,4},{16,20},{20,16},{24,28},{28,24},{1,9},{5... | collective-permute-start | bytes 933896 | tf_op jit(solution)/shard_map/ppermute | solution.py:63
  43.0 13.9 %backward.1 = (bf16[624,256]{1,0:T(8,128)(2,1)S(1)}, bf16[624,256]{1,0:T(8,128)(2,1)S(1)}, f32[608,256]{1,0:T(8,128)S(1)}, f32[608,256]{1,0:T(8,128)S(1)}, f32[2,256]{1,0:T(2,128)S(1)}) custom-call(s32[9]{0:T(128)S(1)} %pad_add_fusion.order, bf16[608,256]{1,0:T(8,128)(2,1)S(1)} %multiply_convert_fusion.refs_0_, ...), custom_call_target="tpu_custom_call" | custom-call | flops 6056574976 | bytes 26148864 | tf_op jit(solution)/shard_map/backward/pallas_call | solution.py:355
  57.0 2.2 %fusion.16 = (bf16[608,256]{1,0:T(8,128)(2,1)S(1)}, f32[608,256]{1,0:T(8,128)}) fusion(f32[608,256]{1,0:T(8,128)S(1)} %get-tuple-element.74, bf16[608,256]{1,0:T(8,128)(2,1)S(1)} %collective-permute-done.7, bf16[608,256]{1,0:T(8,128)(2,1)S(1)} %collective-permute-done.6, bf16[608,256]{1,0:T(8,128)(2,1)S(1)} %collective-permute-done.5, ...), kind=kLoop, calls=%fused_computation.35 | loop fusion | flops 1556480 | bytes 2804100 | tf_op jit(solution)/shard_map/convert_element_type | solution.py:588
  59.4 1.4 %collective-permute-done.11 = bf16[608,128]{1,0:T(8,128)(2,1)S(1)} collective-permute-done((bf16[608,128]{1,0:T(8,128)(2,1)S(1)}, bf16[608,128]{1,0:T(8,128)(2,1)S(1)}, u32[]{:S(2)}, u32[]{:S(2)}) %collective-permute-start.11) | collective-permute-done | bytes 155680 | tf_op jit(solution)/shard_map/ppermute | solution.py:35
  60.8 1.9 %collective-permute-start.12 = (bf16[624,256]{1,0:T(8,128)(2,1)S(1)}, bf16[624,256]{1,0:T(8,128)(2,1)S(1)}, u32[]{:S(2)}, u32[]{:S(2)}) collective-permute-start(bf16[624,256]{1,0:T(8,128)(2,1)S(1)} %get-tuple-element.96), channel_id=1, source_target_pairs={{0,4},{4,0},{8,12},{12,8},{16,24},{20,28},{24,16},{28,20},{1,5},{5... | collective-permute-start | bytes 958472 | tf_op jit(solution)/shard_map/ppermute | solution.py:47
  62.8 2.0 %collective-permute-start.14 = (bf16[608,128]{1,0:T(8,128)(2,1)S(1)}, bf16[608,128]{1,0:T(8,128)(2,1)S(1)}, u32[]{:S(2)}, u32[]{:S(2)}) collective-permute-start(bf16[608,128]{1,0:T(8,128)(2,1)S(1)} %slice_select_fusion.refs_0_.refs_4_), channel_id=1, source_target_pairs={{0,1},{1,0},{2,3},{3,2},{4,5},{5,4},{6,7},{7,6},{8,9},{9,8},{10,11... | collective-permute-start | bytes 466952 | tf_op jit(solution)/shard_map/ppermute | solution.py:69
  64.8 2.5 %collective-permute-start.21 = (bf16[608,128]{1,0:T(8,128)(2,1)S(1)}, bf16[608,128]{1,0:T(8,128)(2,1)S(1)}, u32[]{:S(2)}, u32[]{:S(2)}) collective-permute-start(bf16[608,128]{1,0:T(8,128)(2,1)S(1)} %slice_select_fusion.refs_0_.refs_4_), channel_id=1, source_target_pairs={{0,3},{1,2},{2,1},{3,0},{4,7},{5,6},{6,5},{7,4},{8,11},{9,10},{10,... | collective-permute-start | bytes 466952 | tf_op jit(solution)/shard_map/ppermute | solution.py:69
  67.4 1.6 %collective-permute-done.14 = bf16[608,128]{1,0:T(8,128)(2,1)S(1)} collective-permute-done((bf16[608,128]{1,0:T(8,128)(2,1)S(1)}, bf16[608,128]{1,0:T(8,128)(2,1)S(1)}, u32[]{:S(2)}, u32[]{:S(2)}) %collective-permute-start.14) | collective-permute-done | bytes 155680 | tf_op jit(solution)/shard_map/ppermute | solution.py:69
  69.0 0.7 copy-done.9
  69.7 1.5 %collective-permute-done.13.refs_1_ = bf16[624,256]{1,0:T(8,128)(2,1)S(1)} collective-permute-done((bf16[624,256]{1,0:T(8,128)(2,1)S(1)}, bf16[624,256]{1,0:T(8,128)(2,1)S(1)}, u32[]{:S(2)}, u32[]{:S(2)}) %collective-permute-start.13) | collective-permute-done | bytes 319520 | tf_op jit(solution)/shard_map/ppermute | solution.py:47
  71.2 0.7 copy-done.11
  72.0 3.7 %collective-permute-done.21 = bf16[608,128]{1,0:T(8,128)(2,1)S(1)} collective-permute-done((bf16[608,128]{1,0:T(8,128)(2,1)S(1)}, bf16[608,128]{1,0:T(8,128)(2,1)S(1)}, u32[]{:S(2)}, u32[]{:S(2)}) %collective-permute-start.21) | collective-permute-done | bytes 155680 | tf_op jit(solution)/shard_map/ppermute | solution.py:69
  75.6 5.3 %collective-permute-done.20 = bf16[608,128]{1,0:T(8,128)(2,1)S(1)} collective-permute-done((bf16[608,128]{1,0:T(8,128)(2,1)S(1)}, bf16[608,128]{1,0:T(8,128)(2,1)S(1)}, u32[]{:S(2)}, u32[]{:S(2)}) %collective-permute-start.20) | collective-permute-done | bytes 155680 | tf_op jit(solution)/shard_map/ppermute | solution.py:69
  80.9 0.8 pad_maximum_fusion.refs_12_
  81.7 1.5 %collective-permute-start.22 = (bf16[3,608,128]{2,1,0:T(8,128)(2,1)}, bf16[3,608,128]{2,1,0:T(8,128)(2,1)}, u32[]{:S(2)}, u32[]{:S(2)}) collective-permute-start(bf16[3,608,128]{2,1,0:T(8,128)(2,1)} %pad_maximum_fusion.refs_12_), channel_id=1, source_target_pairs={{0,4},{4,0},{8,12},{12,8},{16,24},{20,28},{24,16},{28,20},{1,5},{5... | collective-permute-start | bytes 1400840 | tf_op jit(solution)/shard_map/ppermute | solution.py:47
  83.2 3.2 %collective-permute-start.23 = (bf16[608,256]{1,0:T(8,128)(2,1)}, bf16[608,256]{1,0:T(8,128)(2,1)}, u32[]{:S(2)}, u32[]{:S(2)}) collective-permute-start(bf16[608,256]{1,0:T(8,128)(2,1)} %get-tuple-element.113.refs_0_), channel_id=1, source_target_pairs={{0,1},{1,0},{2,3},{3,2},{4,5},{5,4},{6,7},{7,6},{8,9},{9,8},{10,11... | collective-permute-start | bytes 933896 | tf_op jit(solution)/shard_map/ppermute | solution.py:69
  86.4 0.6 collective-permute-start.15
  87.0 1.1 copy-done.6
  88.1 1.1 copy-done.8
  89.1 1.0 copy-done.10
  90.1 1.0 copy-done.12
  91.2 1.6 %collective-permute-start.19 = (bf16[624,256]{1,0:T(8,128)(2,1)S(1)}, bf16[624,256]{1,0:T(8,128)(2,1)S(1)}, u32[]{:S(2)}, u32[]{:S(2)}) collective-permute-start(bf16[624,256]{1,0:T(8,128)(2,1)S(1)} %get-tuple-element.104), channel_id=1, source_target_pairs={{0,8},{4,12},{8,0},{12,4},{16,20},{20,16},{24,28},{28,24},{1,9},{5... | collective-permute-start | bytes 958472 | tf_op jit(solution)/shard_map/ppermute | solution.py:47
  92.8 6.2 %collective-permute-done.24.refs_2_ = bf16[608,256]{1,0:T(8,128)(2,1)} collective-permute-done((bf16[608,256]{1,0:T(8,128)(2,1)}, bf16[608,256]{1,0:T(8,128)(2,1)}, u32[]{:S(2)}, u32[]{:S(2)}) %collective-permute-start.24) | collective-permute-done | bytes 311328 | tf_op jit(solution)/shard_map/ppermute | solution.py:69
  99.5 1.5 %collective-permute-start.17 = (bf16[608,128]{1,0:T(8,128)(2,1)}, bf16[608,128]{1,0:T(8,128)(2,1)S(1)}, u32[]{:S(2)}, u32[]{:S(2)}) collective-permute-start(bf16[608,128]{1,0:T(8,128)(2,1)} %collective-permute-done.15.refs_1_.refs_5_), channel_id=1, source_target_pairs={{0,8},{4,12},{8,0},{12,4},{16,20},{20,16},{24,28},{28,24},{1,9},{5... | collective-permute-start | bytes 466952 | tf_op jit(solution)/shard_map/ppermute | solution.py:47
  101.0 1.2 collective-permute-start.27
  102.8 1.5 %collective-permute-done.16.refs_2_.refs_6_ = bf16[608,128]{1,0:T(8,128)(2,1)S(1)} collective-permute-done((bf16[608,128]{1,0:T(8,128)(2,1)S(1)}, bf16[608,128]{1,0:T(8,128)(2,1)S(1)}, u32[]{:S(2)}, u32[]{:S(2)}) %collective-permute-start.16) | collective-permute-done | bytes 155680 | tf_op jit(solution)/shard_map/ppermute | solution.py:47
  104.2 1.7 %collective-permute-done.17.refs_3_.refs_7_ = bf16[608,128]{1,0:T(8,128)(2,1)S(1)} collective-permute-done((bf16[608,128]{1,0:T(8,128)(2,1)}, bf16[608,128]{1,0:T(8,128)(2,1)S(1)}, u32[]{:S(2)}, u32[]{:S(2)}) %collective-permute-start.17) | collective-permute-done | bytes 155680 | tf_op jit(solution)/shard_map/ppermute | solution.py:47
  105.9 0.6 collective-permute-start.26
  106.5 1.9 %residual_rows.1 = f32[608,128]{1,0:T(8,128)S(1)} custom-call(s32[9]{0:T(128)S(1)} %pad_add_fusion.order, bf16[608,2432]{1,0:T(8,128)(2,1)S(1)} %copy-done, bf16[608,128]{1,0:T(8,128)(2,1)S(1)} %slice_select_fusion.refs_0_.refs_4_, bf16[608,128]{1,0:T(8,128)(2,1)} %collective-permute-done.15.refs_1_.refs_5_, ...), custom_call_target="tpu_custom_call" | custom-call | flops 378535936 | bytes 4202496 | tf_op jit(solution)/shard_map/residual_rows/pallas_call | solution.py:462
  108.5 3.2 %collective-permute-done.27.refs_3_ = bf16[608,256]{1,0:T(8,128)(2,1)S(1)} collective-permute-done((bf16[608,256]{1,0:T(8,128)(2,1)}, bf16[608,256]{1,0:T(8,128)(2,1)S(1)}, u32[]{:S(2)}, u32[]{:S(2)}) %collective-permute-start.27) | collective-permute-done | bytes 311328 | tf_op jit(solution)/shard_map/ppermute | solution.py:69
  112.3 3.7 %collective-permute-done.26.refs_15_ = bf16[3,608,128]{2,1,0:T(8,128)(2,1)S(1)} collective-permute-done((bf16[3,608,128]{2,1,0:T(8,128)(2,1)}, bf16[3,608,128]{2,1,0:T(8,128)(2,1)S(1)}, u32[]{:S(2)}, u32[]{:S(2)}) %collective-permute-start.26) | collective-permute-done | bytes 466976 | tf_op jit(solution)/shard_map/ppermute | solution.py:47
  117.0 2.3 %fusion.5 = f32[1,608,256]{2,1,0:T(8,128)} fusion(f32[608,256]{1,0:T(8,128)S(1)} %get-tuple-element.103, f32[608,128]{1,0:T(8,128)} %collective-permute-done.4, f32[608,128]{1,0:T(8,128)} %add_add_fusion, bf16[624,256]{1,0:T(8,128)(2,1)S(1)} %collective-permute-done.19, f32[256]{0:T(256)S(1)} %bitcast.26, f32[256]{0:T(256)S(1)} %bitcast.28, ...), kind=kLoop, calls=%fused_computation.7 | loop fusion | flops 2179072 | bytes 2808197 | tf_op jit(solution)/shard_map/broadcast_in_dim | solution.py:623
  119.4 1.1 fusion.8
  120.7 7.3 %zero_projection_grad.1 = f32[608,2432]{1,0:T(8,128)} custom-call(s32[9]{0:T(128)S(1)} %pad_add_fusion.order, s32[4]{0:T(128)S(1)} %iota_xor_fusion.dp_order, bf16[608,256]{1,0:T(8,128)(2,1)} %get-tuple-element.113.refs_0_, bf16[608,256]{1,0:T(8,128)(2,1)} %collective-permute-done.23.refs_1_, bf16[608,256]{1,0:T(8,128)(2,1)} %collective-permute-done.24.refs_2_, ...), custom_call_target="tpu_custom_call" | custom-call | flops 3028287488 | bytes 12140544 | tf_op jit(solution)/shard_map/zero_projection_grad/pallas_call | solution.py:521
  (79 shorter events, 5.4 us)
Async XLA Ops:
  0.6 2.0 %collective-permute-start = (bf16[608,256]{1,0:T(8,128)(2,1)}, bf16[608,256]{1,0:T(8,128)(2,1)S(1)}, u32[]{:S(2)}, u32[]{:S(2)}) collective-permute-start(bf16[608,256]{1,0:T(8,128)(2,1)} %bitcast.20), channel_id=1, source_target_pairs={{0,16},{16,0},{1,17},{17,1},{2,18},{18,2},{3,19},{19,3},{4,20},{20... | collective-permute-start | bytes 933896 | tf_op jit(solution)/shard_map/ppermute | solution.py:35
  2.7 1.0 copy-start.2
  7.6 12.8 %collective-permute-start.1 = (bf16[608,128]{1,0:T(8,128)(2,1)S(1)}, bf16[608,128]{1,0:T(8,128)(2,1)S(1)}, u32[]{:S(2)}, u32[]{:S(2)}) collective-permute-start(bf16[608,128]{1,0:T(8,128)(2,1)S(1)} %get-tuple-element.62), channel_id=1, source_target_pairs={{0,4},{4,0},{8,12},{12,8},{16,24},{20,28},{24,16},{28,20},{1,5},{5... | collective-permute-start | bytes 466952 | tf_op jit(solution)/shard_map/ppermute | solution.py:63
  10.5 9.9 %collective-permute-start.2 = (bf16[608,128]{1,0:T(8,128)(2,1)S(1)}, bf16[608,128]{1,0:T(8,128)(2,1)S(1)}, u32[]{:S(2)}, u32[]{:S(2)}) collective-permute-start(bf16[608,128]{1,0:T(8,128)(2,1)S(1)} %get-tuple-element.63), channel_id=1, source_target_pairs={{0,8},{4,12},{8,0},{12,4},{16,20},{20,16},{24,28},{28,24},{1,9},{5... | collective-permute-start | bytes 466952 | tf_op jit(solution)/shard_map/ppermute | solution.py:63
  12.0 8.4 %collective-permute-start.3 = (bf16[608,128]{1,0:T(8,128)(2,1)S(1)}, bf16[608,128]{1,0:T(8,128)(2,1)S(1)}, u32[]{:S(2)}, u32[]{:S(2)}) collective-permute-start(bf16[608,128]{1,0:T(8,128)(2,1)S(1)} %get-tuple-element.64), channel_id=1, source_target_pairs={{0,12},{4,8},{8,4},{12,0},{16,28},{20,24},{24,20},{28,16},{1,13},{... | collective-permute-start | bytes 466952 | tf_op jit(solution)/shard_map/ppermute | solution.py:63
  20.4 4.0 %copy-start.1 = (f32[2432,8]{1,0:T(8,128)}, f32[2432,8]{1,0:T(8,128)S(1)}, u32[]{:S(2)}) copy-start(f32[2432,8]{1,0:T(8,128)S(1)} %get-tuple-element.66.refs_8_) | copy-start | bytes 233476
  20.4 2.8 %copy-start.3 = (bf16[1,608,256]{2,1,0:T(8,128)(2,1)S(1)}, bf16[1,608,256]{2,1,0:T(8,128)(2,1)}, u32[]{:S(2)}) copy-start(bf16[1,608,256]{2,1,0:T(8,128)(2,1)} %param.13) | copy-start | bytes 933892
  21.3 1.9 %collective-permute-start.4 = (f32[608,128]{1,0:T(8,128)}, f32[608,128]{1,0:T(8,128)}, u32[]{:S(2)}, u32[]{:S(2)}) collective-permute-start(f32[608,128]{1,0:T(8,128)} %add_add_fusion), channel_id=1, source_target_pairs={{0,16},{16,0},{1,17},{17,1},{2,18},{18,2},{3,19},{19,3},{4,20},{20... | collective-permute-start | bytes 933896 | tf_op jit(solution)/shard_map/ppermute | solution.py:35
  24.4 18.5 %collective-permute-start.10 = (bf16[608,256]{1,0:T(8,128)(2,1)S(1)}, bf16[608,256]{1,0:T(8,128)(2,1)S(1)}, u32[]{:S(2)}, u32[]{:S(2)}) collective-permute-start(bf16[608,256]{1,0:T(8,128)(2,1)S(1)} %multiply_convert_fusion.refs_0_), channel_id=1, source_target_pairs={{0,12},{4,8},{8,4},{12,0},{16,28},{20,24},{24,20},{28,16},{1,13},{... | collective-permute-start | bytes 933896 | tf_op jit(solution)/shard_map/ppermute | solution.py:63
  27.4 15.6 %collective-permute-start.9 = (bf16[608,256]{1,0:T(8,128)(2,1)S(1)}, bf16[608,256]{1,0:T(8,128)(2,1)S(1)}, u32[]{:S(2)}, u32[]{:S(2)}) collective-permute-start(bf16[608,256]{1,0:T(8,128)(2,1)S(1)} %multiply_convert_fusion.refs_0_), channel_id=1, source_target_pairs={{0,8},{4,12},{8,0},{12,4},{16,20},{20,16},{24,28},{28,24},{1,9},{5... | collective-permute-start | bytes 933896 | tf_op jit(solution)/shard_map/ppermute | solution.py:63
  27.9 15.1 %collective-permute-start.8 = (bf16[608,256]{1,0:T(8,128)(2,1)S(1)}, bf16[608,256]{1,0:T(8,128)(2,1)S(1)}, u32[]{:S(2)}, u32[]{:S(2)}) collective-permute-start(bf16[608,256]{1,0:T(8,128)(2,1)S(1)} %multiply_convert_fusion.refs_0_), channel_id=1, source_target_pairs={{0,4},{4,0},{8,12},{12,8},{16,24},{20,28},{24,16},{28,20},{1,5},{5... | collective-permute-start | bytes 933896 | tf_op jit(solution)/shard_map/ppermute | solution.py:63
  39.4 17.5 %collective-permute-start.5 = (bf16[608,256]{1,0:T(8,128)(2,1)S(1)}, bf16[608,256]{1,0:T(8,128)(2,1)S(1)}, u32[]{:S(2)}, u32[]{:S(2)}) collective-permute-start(bf16[608,256]{1,0:T(8,128)(2,1)S(1)} %get-tuple-element.75), channel_id=1, source_target_pairs={{0,4},{4,0},{8,12},{12,8},{16,24},{20,28},{24,16},{28,20},{1,5},{5... | collective-permute-start | bytes 933896 | tf_op jit(solution)/shard_map/ppermute | solution.py:63
  41.4 15.6 %collective-permute-start.6 = (bf16[608,256]{1,0:T(8,128)(2,1)S(1)}, bf16[608,256]{1,0:T(8,128)(2,1)S(1)}, u32[]{:S(2)}, u32[]{:S(2)}) collective-permute-start(bf16[608,256]{1,0:T(8,128)(2,1)S(1)} %get-tuple-element.76), channel_id=1, source_target_pairs={{0,8},{4,12},{8,0},{12,4},{16,20},{20,16},{24,28},{28,24},{1,9},{5... | collective-permute-start | bytes 933896 | tf_op jit(solution)/shard_map/ppermute | solution.py:63
  42.9 14.1 %collective-permute-start.7 = (bf16[608,256]{1,0:T(8,128)(2,1)S(1)}, bf16[608,256]{1,0:T(8,128)(2,1)S(1)}, u32[]{:S(2)}, u32[]{:S(2)}) collective-permute-start(bf16[608,256]{1,0:T(8,128)(2,1)S(1)} %get-tuple-element.77), channel_id=1, source_target_pairs={{0,12},{4,8},{8,4},{12,0},{16,28},{20,24},{24,20},{28,16},{1,13},{... | collective-permute-start | bytes 933896 | tf_op jit(solution)/shard_map/ppermute | solution.py:63
  57.0 2.3 %copy-start.5 = (f32[608,256]{1,0:T(8,128)}, f32[608,256]{1,0:T(8,128)S(1)}, u32[]{:S(2)}) copy-start(f32[608,256]{1,0:T(8,128)S(1)} %get-tuple-element.101.refs_2_) | copy-start | bytes 1867780
  57.0 2.3 %copy-start.7 = (f32[608,256]{1,0:T(8,128)}, f32[608,256]{1,0:T(8,128)S(1)}, u32[]{:S(2)}) copy-start(f32[608,256]{1,0:T(8,128)S(1)} %get-tuple-element.102.refs_3_) | copy-start | bytes 1867780
  59.2 24.0 %copy-start.13 = (bf16[608,256]{1,0:T(8,128)(2,1)}, bf16[608,256]{1,0:T(8,128)(2,1)S(1)}, u32[]{:S(2)}) copy-start(bf16[608,256]{1,0:T(8,128)(2,1)S(1)} %get-tuple-element.121) | copy-start | bytes 933892
  59.3 1.4 %collective-permute-start.11 = (bf16[608,128]{1,0:T(8,128)(2,1)S(1)}, bf16[608,128]{1,0:T(8,128)(2,1)S(1)}, u32[]{:S(2)}, u32[]{:S(2)}) collective-permute-start(bf16[608,128]{1,0:T(8,128)(2,1)S(1)} %slice.65), channel_id=1, source_target_pairs={{0,16},{16,0},{1,17},{17,1},{2,18},{18,2},{3,19},{19,3},{4,20},{20... | collective-permute-start | bytes 466952 | tf_op jit(solution)/shard_map/ppermute | solution.py:35
  60.7 45.7 %copy-start = (bf16[608,2432]{1,0:T(8,128)(2,1)S(1)}, bf16[608,2432]{1,0:T(8,128)(2,1)}, u32[]{:S(2)}) copy-start(bf16[608,2432]{1,0:T(8,128)(2,1)} %weight.3) | copy-start | bytes 8871940
  60.8 8.2 %collective-permute-start.12 = (bf16[624,256]{1,0:T(8,128)(2,1)S(1)}, bf16[624,256]{1,0:T(8,128)(2,1)S(1)}, u32[]{:S(2)}, u32[]{:S(2)}) collective-permute-start(bf16[624,256]{1,0:T(8,128)(2,1)S(1)} %get-tuple-element.96), channel_id=1, source_target_pairs={{0,4},{4,0},{8,12},{12,8},{16,24},{20,28},{24,16},{28,20},{1,5},{5... | collective-permute-start | bytes 958472 | tf_op jit(solution)/shard_map/ppermute | solution.py:47
  62.7 8.5 %collective-permute-start.13 = (bf16[624,256]{1,0:T(8,128)(2,1)S(1)}, bf16[624,256]{1,0:T(8,128)(2,1)S(1)}, u32[]{:S(2)}, u32[]{:S(2)}) collective-permute-start(bf16[624,256]{1,0:T(8,128)(2,1)S(1)} %get-tuple-element.97), channel_id=1, source_target_pairs={{0,4},{4,0},{8,12},{12,8},{16,24},{20,28},{24,16},{28,20},{1,5},{5... | collective-permute-start | bytes 958472 | tf_op jit(solution)/shard_map/ppermute | solution.py:47
  62.8 6.2 %collective-permute-start.14 = (bf16[608,128]{1,0:T(8,128)(2,1)S(1)}, bf16[608,128]{1,0:T(8,128)(2,1)S(1)}, u32[]{:S(2)}, u32[]{:S(2)}) collective-permute-start(bf16[608,128]{1,0:T(8,128)(2,1)S(1)} %slice_select_fusion.refs_0_.refs_4_), channel_id=1, source_target_pairs={{0,1},{1,0},{2,3},{3,2},{4,5},{5,4},{6,7},{7,6},{8,9},{9,8},{10,11... | collective-permute-start | bytes 466952 | tf_op jit(solution)/shard_map/ppermute | solution.py:69
  64.8 10.8 %collective-permute-start.21 = (bf16[608,128]{1,0:T(8,128)(2,1)S(1)}, bf16[608,128]{1,0:T(8,128)(2,1)S(1)}, u32[]{:S(2)}, u32[]{:S(2)}) collective-permute-start(bf16[608,128]{1,0:T(8,128)(2,1)S(1)} %slice_select_fusion.refs_0_.refs_4_), channel_id=1, source_target_pairs={{0,3},{1,2},{2,1},{3,0},{4,7},{5,6},{6,5},{7,4},{8,11},{9,10},{10,... | collective-permute-start | bytes 466952 | tf_op jit(solution)/shard_map/ppermute | solution.py:69
  67.3 13.6 %collective-permute-start.20 = (bf16[608,128]{1,0:T(8,128)(2,1)S(1)}, bf16[608,128]{1,0:T(8,128)(2,1)S(1)}, u32[]{:S(2)}, u32[]{:S(2)}) collective-permute-start(bf16[608,128]{1,0:T(8,128)(2,1)S(1)} %slice_select_fusion.refs_0_.refs_4_), channel_id=1, source_target_pairs={{0,2},{1,3},{2,0},{3,1},{4,6},{5,7},{6,4},{7,5},{8,10},{9,11},{10,... | collective-permute-start | bytes 466952 | tf_op jit(solution)/shard_map/ppermute | solution.py:69
  81.7 19.3 %collective-permute-start.22 = (bf16[3,608,128]{2,1,0:T(8,128)(2,1)}, bf16[3,608,128]{2,1,0:T(8,128)(2,1)}, u32[]{:S(2)}, u32[]{:S(2)}) collective-permute-start(bf16[3,608,128]{2,1,0:T(8,128)(2,1)} %pad_maximum_fusion.refs_12_), channel_id=1, source_target_pairs={{0,4},{4,0},{8,12},{12,8},{16,24},{20,28},{24,16},{28,20},{1,5},{5... | collective-permute-start | bytes 1400840 | tf_op jit(solution)/shard_map/ppermute | solution.py:47
  83.2 15.8 %collective-permute-start.24 = (bf16[608,256]{1,0:T(8,128)(2,1)}, bf16[608,256]{1,0:T(8,128)(2,1)}, u32[]{:S(2)}, u32[]{:S(2)}) collective-permute-start(bf16[608,256]{1,0:T(8,128)(2,1)} %get-tuple-element.113.refs_0_), channel_id=1, source_target_pairs={{0,2},{1,3},{2,0},{3,1},{4,6},{5,7},{6,4},{7,5},{8,10},{9,11},{10,... | collective-permute-start | bytes 933896 | tf_op jit(solution)/shard_map/ppermute | solution.py:69
  83.2 17.8 %collective-permute-start.23 = (bf16[608,256]{1,0:T(8,128)(2,1)}, bf16[608,256]{1,0:T(8,128)(2,1)}, u32[]{:S(2)}, u32[]{:S(2)}) collective-permute-start(bf16[608,256]{1,0:T(8,128)(2,1)} %get-tuple-element.113.refs_0_), channel_id=1, source_target_pairs={{0,1},{1,0},{2,3},{3,2},{4,5},{5,4},{6,7},{7,6},{8,9},{9,8},{10,11... | collective-permute-start | bytes 933896 | tf_op jit(solution)/shard_map/ppermute | solution.py:69
  86.4 13.1 %collective-permute-start.15 = (bf16[608,128]{1,0:T(8,128)(2,1)S(1)}, bf16[608,128]{1,0:T(8,128)(2,1)}, u32[]{:S(2)}, u32[]{:S(2)}) collective-permute-start(bf16[608,128]{1,0:T(8,128)(2,1)S(1)} %slice_select_fusion.refs_0_.refs_4_), channel_id=1, source_target_pairs={{0,4},{4,0},{8,12},{12,8},{16,24},{20,28},{24,16},{28,20},{1,5},{5... | collective-permute-start | bytes 466952 | tf_op jit(solution)/shard_map/ppermute | solution.py:47
  87.0 1.1 copy-start.6
  88.1 1.1 copy-start.8
  89.1 1.0 copy-start.10
  91.2 17.2 %collective-permute-start.19 = (bf16[624,256]{1,0:T(8,128)(2,1)S(1)}, bf16[624,256]{1,0:T(8,128)(2,1)S(1)}, u32[]{:S(2)}, u32[]{:S(2)}) collective-permute-start(bf16[624,256]{1,0:T(8,128)(2,1)S(1)} %get-tuple-element.104), channel_id=1, source_target_pairs={{0,8},{4,12},{8,0},{12,4},{16,20},{20,16},{24,28},{28,24},{1,9},{5... | collective-permute-start | bytes 958472 | tf_op jit(solution)/shard_map/ppermute | solution.py:47
  99.0 5.2 %collective-permute-start.16 = (bf16[608,128]{1,0:T(8,128)(2,1)S(1)}, bf16[608,128]{1,0:T(8,128)(2,1)S(1)}, u32[]{:S(2)}, u32[]{:S(2)}) collective-permute-start(bf16[608,128]{1,0:T(8,128)(2,1)S(1)} %slice_select_fusion.refs_0_.refs_4_), channel_id=1, source_target_pairs={{0,8},{4,12},{8,0},{12,4},{16,20},{20,16},{24,28},{28,24},{1,9},{5... | collective-permute-start | bytes 466952 | tf_op jit(solution)/shard_map/ppermute | solution.py:47
  99.5 6.4 %collective-permute-start.17 = (bf16[608,128]{1,0:T(8,128)(2,1)}, bf16[608,128]{1,0:T(8,128)(2,1)S(1)}, u32[]{:S(2)}, u32[]{:S(2)}) collective-permute-start(bf16[608,128]{1,0:T(8,128)(2,1)} %collective-permute-done.15.refs_1_.refs_5_), channel_id=1, source_target_pairs={{0,8},{4,12},{8,0},{12,4},{16,20},{20,16},{24,28},{28,24},{1,9},{5... | collective-permute-start | bytes 466952 | tf_op jit(solution)/shard_map/ppermute | solution.py:47
  101.0 10.7 %collective-permute-start.27 = (bf16[608,256]{1,0:T(8,128)(2,1)}, bf16[608,256]{1,0:T(8,128)(2,1)S(1)}, u32[]{:S(2)}, u32[]{:S(2)}) collective-permute-start(bf16[608,256]{1,0:T(8,128)(2,1)} %get-tuple-element.113.refs_0_), channel_id=1, source_target_pairs={{0,3},{1,2},{2,1},{3,0},{4,7},{5,6},{6,5},{7,4},{8,11},{9,10},{10,... | collective-permute-start | bytes 933896 | tf_op jit(solution)/shard_map/ppermute | solution.py:69
  102.2 9.5 %collective-permute-start.25 = (bf16[3,608,128]{2,1,0:T(8,128)(2,1)}, bf16[3,608,128]{2,1,0:T(8,128)(2,1)S(1)}, u32[]{:S(2)}, u32[]{:S(2)}) collective-permute-start(bf16[3,608,128]{2,1,0:T(8,128)(2,1)} %pad_maximum_fusion.refs_12_), channel_id=1, source_target_pairs={{0,8},{4,12},{8,0},{12,4},{16,20},{20,16},{24,28},{28,24},{1,9},{5... | collective-permute-start | bytes 1400840 | tf_op jit(solution)/shard_map/ppermute | solution.py:47
  104.2 11.8 %collective-permute-start.28 = (bf16[608,128]{1,0:T(8,128)(2,1)S(1)}, bf16[608,128]{1,0:T(8,128)(2,1)S(1)}, u32[]{:S(2)}, u32[]{:S(2)}) collective-permute-start(bf16[608,128]{1,0:T(8,128)(2,1)S(1)} %slice_select_fusion.refs_0_.refs_4_), channel_id=1, source_target_pairs={{0,16},{16,0},{1,17},{17,1},{2,18},{18,2},{3,19},{19,3},{4,20},{20... | collective-permute-start | bytes 466952 | tf_op jit(solution)/shard_map/ppermute | solution.py:35
  105.9 10.1 %collective-permute-start.26 = (bf16[3,608,128]{2,1,0:T(8,128)(2,1)}, bf16[3,608,128]{2,1,0:T(8,128)(2,1)S(1)}, u32[]{:S(2)}, u32[]{:S(2)}) collective-permute-start(bf16[3,608,128]{2,1,0:T(8,128)(2,1)} %collective-permute-done.22.refs_13_), channel_id=1, source_target_pairs={{0,8},{4,12},{8,0},{12,4},{16,20},{20,16},{24,28},{28,24},{1,9},{5... | collective-permute-start | bytes 1400840 | tf_op jit(solution)/shard_map/ppermute | solution.py:47
  108.4 11.0 %copy-start.14 = (bf16[608,256]{1,0:T(8,128)(2,1)S(1)}, bf16[608,256]{1,0:T(8,128)(2,1)}, u32[]{:S(2)}) copy-start(bf16[608,256]{1,0:T(8,128)(2,1)} %copy-done.13) | copy-start | bytes 933892
  108.4 11.0 %copy-start.15 = (f32[608,256]{1,0:T(8,128)S(1)}, f32[608,256]{1,0:T(8,128)}, u32[]{:S(2)}) copy-start(f32[608,256]{1,0:T(8,128)} %get-tuple-element.122) | copy-start | bytes 1867780
  108.4 8.1 %collective-permute-start.30 = (bf16[608,128]{1,0:T(8,128)(2,1)S(1)}, bf16[608,128]{1,0:T(8,128)(2,1)S(1)}, u32[]{:S(2)}, u32[]{:S(2)}) collective-permute-start(bf16[608,128]{1,0:T(8,128)(2,1)S(1)} %collective-permute-done.16.refs_2_.refs_6_), channel_id=1, source_target_pairs={{0,16},{16,0},{1,17},{17,1},{2,18},{18,2},{3,19},{19,3},{4,20},{20... | collective-permute-start | bytes 466952 | tf_op jit(solution)/shard_map/ppermute | solution.py:35
  111.7 4.8 %collective-permute-start.29 = (bf16[608,128]{1,0:T(8,128)(2,1)}, bf16[608,128]{1,0:T(8,128)(2,1)S(1)}, u32[]{:S(2)}, u32[]{:S(2)}) collective-permute-start(bf16[608,128]{1,0:T(8,128)(2,1)} %collective-permute-done.15.refs_1_.refs_5_), channel_id=1, source_target_pairs={{0,16},{16,0},{1,17},{17,1},{2,18},{18,2},{3,19},{19,3},{4,20},{20... | collective-permute-start | bytes 466952 | tf_op jit(solution)/shard_map/ppermute | solution.py:35
  111.8 7.6 %collective-permute-start.18 = (f32[608,128]{1,0:T(8,128)S(1)}, f32[608,128]{1,0:T(8,128)S(1)}, u32[]{:S(2)}, u32[]{:S(2)}) collective-permute-start(f32[608,128]{1,0:T(8,128)S(1)} %residual_rows.1), channel_id=1, source_target_pairs={{0,16},{16,0},{1,17},{17,1},{2,18},{18,2},{3,19},{19,3},{4,20},{20... | collective-permute-start | bytes 933896 | tf_op jit(solution)/shard_map/ppermute | solution.py:35
  116.0 4.7 %collective-permute-start.32 = (bf16[3,608,128]{2,1,0:T(8,128)(2,1)}, bf16[3,608,128]{2,1,0:T(8,128)(2,1)S(1)}, u32[]{:S(2)}, u32[]{:S(2)}) collective-permute-start(bf16[3,608,128]{2,1,0:T(8,128)(2,1)} %pad_maximum_fusion.refs_12_), channel_id=1, source_target_pairs={{0,16},{16,0},{1,17},{17,1},{2,18},{18,2},{3,19},{19,3},{4,20},{20... | collective-permute-start | bytes 1400840 | tf_op jit(solution)/shard_map/ppermute | solution.py:35
  116.0 4.7 %collective-permute-start.33 = (bf16[3,608,128]{2,1,0:T(8,128)(2,1)}, bf16[3,608,128]{2,1,0:T(8,128)(2,1)S(1)}, u32[]{:S(2)}, u32[]{:S(2)}) collective-permute-start(bf16[3,608,128]{2,1,0:T(8,128)(2,1)} %collective-permute-done.22.refs_13_), channel_id=1, source_target_pairs={{0,16},{16,0},{1,17},{17,1},{2,18},{18,2},{3,19},{19,3},{4,20},{20... | collective-permute-start | bytes 1400840 | tf_op jit(solution)/shard_map/ppermute | solution.py:35
  116.5 4.2 %collective-permute-start.34 = (bf16[3,608,128]{2,1,0:T(8,128)(2,1)S(1)}, bf16[3,608,128]{2,1,0:T(8,128)(2,1)S(1)}, u32[]{:S(2)}, u32[]{:S(2)}) collective-permute-start(bf16[3,608,128]{2,1,0:T(8,128)(2,1)S(1)} %collective-permute-done.25.refs_14_), channel_id=1, source_target_pairs={{0,16},{16,0},{1,17},{17,1},{2,18},{18,2},{3,19},{19,3},{4,20},{20... | collective-permute-start | bytes 1400840 | tf_op jit(solution)/shard_map/ppermute | solution.py:35
  116.6 4.1 %collective-permute-start.35 = (bf16[3,608,128]{2,1,0:T(8,128)(2,1)S(1)}, bf16[3,608,128]{2,1,0:T(8,128)(2,1)S(1)}, u32[]{:S(2)}, u32[]{:S(2)}) collective-permute-start(bf16[3,608,128]{2,1,0:T(8,128)(2,1)S(1)} %collective-permute-done.26.refs_15_), channel_id=1, source_target_pairs={{0,16},{16,0},{1,17},{17,1},{2,18},{18,2},{3,19},{19,3},{4,20},{20... | collective-permute-start | bytes 1400840 | tf_op jit(solution)/shard_map/ppermute | solution.py:35
  119.3 1.4 %collective-permute-start.31 = (bf16[608,128]{1,0:T(8,128)(2,1)S(1)}, bf16[608,128]{1,0:T(8,128)(2,1)S(1)}, u32[]{:S(2)}, u32[]{:S(2)}) collective-permute-start(bf16[608,128]{1,0:T(8,128)(2,1)S(1)} %collective-permute-done.17.refs_3_.refs_7_), channel_id=1, source_target_pairs={{0,16},{16,0},{1,17},{17,1},{2,18},{18,2},{3,19},{19,3},{4,20},{20... | collective-permute-start | bytes 466952 | tf_op jit(solution)/shard_map/ppermute | solution.py:35
  (4 other events, 3.4 us)

commit v13 on v12

--- a/solution.py
+++ b/solution.py
@@ -332,18 +332,17 @@
         sums[1] += jnp.sum(scaled * xhat, 0, keepdims=True)
 
     backward_products(stream, parts, 0, grad, (slope_a, slope_b), in_buf, out_buf, total, None, last)
-    count = len(outs) // 2
-    padded = outs[0].shape[0] - 16
+    padded = outs[-1].shape[0] - 16
     tail = pack_sums(*sums)
-    for place in range(count):
-        offset = pl.multiple_of(order[2 * place] * rows, 8)
-        outs[count + place][...] = full[pl.ds(offset, rows), :]
-        offset = pl.multiple_of(order[2 * place + 1] * rows, 8)
-        block = full[pl.ds(offset, rows), :]
+    for place, target in enumerate(outs):
+        block = full[pl.ds(pl.multiple_of(order[place] * rows, 8), rows), :]
+        if place == 0:
+            target[...] = block
+            continue
         if padded > rows:
             block = jnp.concatenate([block, jnp.zeros((padded - rows, tokens), F32)], 0)
-        outs[place][:padded, :] = block.astype(BF16)
-        outs[place][padded:, :] = tail
+        target[:padded, :] = block.astype(BF16)
+        target[padded:, :] = tail
     sums_out[0:1, :] = sums[0]
     sums_out[1:2, :] = sums[1]
 
@@ -351,11 +350,10 @@
 def backward(order, gathered, slope_a, slope_b, acts, stats, mod, w_in, w_out, name):
     hidden, features = w_in.shape[1:]
     blocks, (rows, tokens) = len(gathered), gathered[0].shape
-    count = blocks // 2
     outs = pl.pallas_call(
         functools.partial(backward_kernel, blocks, rows),
-        out_shape=[struct((-(-rows // 16) * 16 + 16, tokens), BF16)] * count
-        + [struct((rows, tokens), F32)] * count
+        out_shape=[struct((rows, tokens), F32)]
+        + [struct((-(-rows // 16) * 16 + 16, tokens), BF16)] * (blocks - 1)
         + [struct((2, tokens), F32)],
         in_specs=[SCALARS] + [WHOLE] * (blocks + 5) + [HELD, HELD],
         out_specs=[WHOLE] * (blocks + 1),
@@ -371,40 +369,7 @@
         name=name,
         **layer_params(hidden, features, tokens, 0),
     )(order, *gathered, slope_a, slope_b, acts, stats, mod, w_in, w_out)
-    return outs[:count], outs[count:-1], outs[-1]
-
-
-def fold_kernel(rows, count, *refs):
-    got, kept, (sums, *outs) = refs[:count], refs[count : 2 * count], refs[2 * count :]
-    more = unpack_sums(got[0][-16:, :])
-    plain, along = sums[0:1, :] + more[0], sums[1:2, :] + more[1]
-    tail = pack_sums(plain, along)
-    padded = got[0].shape[0] - 16
-    for place in range(count // 2):
-        even, odd = 2 * place, 2 * place + 1
-        outs[count // 2 + place][...] = kept[even][...] + got[even][:rows, :].astype(F32)
-        block = kept[odd][...] + got[odd][:rows, :].astype(F32)
-        if padded > rows:
-            block = jnp.concatenate([block, jnp.zeros((padded - rows, block.shape[1]), F32)], 0)
-        outs[place][:padded, :] = block.astype(BF16)
-        outs[place][padded:, :] = tail
-    outs[-1][0:1, :] = plain
-    outs[-1][1:2, :] = along
-
-
-def fold(got, kept, sums):
-    count, (rows, tokens) = len(kept), kept[0].shape
-    outs = pl.pallas_call(
-        functools.partial(fold_kernel, rows, count),
-        out_shape=[struct(got[0].shape, BF16)] * (count // 2)
-        + [struct((rows, tokens), F32)] * (count // 2)
-        + [struct((2, tokens), F32)],
-        in_specs=[WHOLE] * (2 * count + 1),
-        out_specs=[WHOLE] * (count + 1),
-        name="fold",
-        **params(2 * count * rows * tokens, 8 * count * rows * tokens, grant=12),
-    )(*got, *kept, sums)
-    return outs[: count // 2], outs[count // 2 : -1], outs[-1]
+    return outs[0], outs[1:-1], outs[-1]
 
 
 def prepare_kernel(blocks, order, acts, modulation, own, arrived, weight, *refs):
@@ -579,7 +544,7 @@
         order, after(normed, grad_rows), total, w_in, w_out, split, blocks, "forward_last"
     )
     gathered = [grad_rows] + direct([grad_rows] * (blocks - 1), kept)
-    norm_sent, norm_kept, token_sums = backward(
+    norm_grad, sent_norm, token_sums = backward(
         order, after(gathered, *sent), slope_a, slope_b, acts, stats, mod, w_in, w_out, "backward"
     )
     got = direct(sent, token_sums)
@@ -588,31 +553,27 @@
     out_rows = sums.astype(BF16)
 
     out_half = jnp.where(is_control, out_rows[:, :half], swap_grp(out_rows[:, half:]))
-    far = gather_dp(out_half)
-    sent, kept = after((norm_sent, norm_kept), out_half)
+    far = gather_dp(out_half, 1, 3)
+    far = far + gather_dp(after(out_half, far[-1]), 3)
+    got = [send(value, place + 1) for place, value in enumerate(after(sent_norm, out_half))]
+    got, far = lax.optimization_barrier((got, far))
+    plain, along = token_sums[0:1], token_sums[1:2]
+    for value in got:
+        more = unpack_sums(value[-16:])
+        plain, along = plain + more[0], along + more[1]
+        norm_grad = norm_grad + value[:rows].astype(F32)
+    near, others, cots = [after(out_half, got[0])], [jnp.stack(far)], [cot1_rows]
     for level in range(levels):
-        got = steps(sent, level)
-        if level == 0:
-            got, nearest = lax.optimization_barrier((got, far[0]))
-            near = [after(out_half, got[0])]
         near = near + steps(near, level)
-        if level + 1 < levels:
-            sent, kept, token_sums = fold(got, kept, token_sums)
-    others = [jnp.stack([nearest] + far[1:])]
-    cots = [cot1_rows]
-    for level in range(levels):
         others = others + steps(others, level)
         if level < 2:
             tied = after(cot1_rows, far if level == 0 else cots[-1])
             arrived = gather_dp(tied, 1, 3) if level == 0 else gather_dp(tied, 3)
-            others, arrived = lax.optimization_barrier((others, arrived))
+            near, others, arrived = lax.optimization_barrier((near, others, arrived))
             cots = cots + arrived
-    more = unpack_sums(got[0][-16:])
-    plain, along = token_sums[0:1] + more[0], token_sums[1:2] + more[1]
-    kept = [kept[0] + got[0][:rows].astype(F32)]
     mean, inv = stats[0:1], stats[1:2]
     back = inv * (
-        kept[0] * (1.0 + own_mod[:, 1:2]) - plain / features - (own_values - mean) * inv * (along / features)
+        norm_grad * (1.0 + own_mod[:, 1:2]) - plain / features - (own_values - mean) * inv * (along / features)
     )
     residual = residual_rows(order, zero_weight, near)
     residual = jnp.concatenate([swap_grp(residual), residual], 1)

time: 129 us -> 132 us (1.023)
  starting transfers between devices: 31.6 us -> 39.6 us
  local copies, waits for them, and re-layouts: 8.3 us -> 4.45 us
    ppermute x6, starting transfers between devices: 8.95 us -> 15.5 us  [gather_dp(): lax.ppermute(value, 'dp', [(i, i ^ mask) for i in range(length)])]
    ppermute x9 -> x6, waiting for transfers between devices: 8.38 us -> 12.7 us  [step(): return lax.ppermute(value, ('grp', 'fsdp'), pairs)]
    unnamed x33 -> x47, local copies, waits for them, and re-layouts: 8.28 us -> 4.43 us
    ppermute x6, waiting for transfers between devices: 20 us -> 16.2 us  [gather_dp(): lax.ppermute(value, 'dp', [(i, i ^ mask) for i in range(length)])]
    ppermute x9 -> x12, starting transfers between devices: 11.6 us -> 15.1 us  [send(): return lax.ppermute(value, ('grp', 'fsdp'), pairs)]
    ppermute x9 -> x6, starting transfers between devices: 8.81 us -> 6.08 us  [step(): return lax.ppermute(value, ('grp', 'fsdp'), pairs)]
    convert_element_type x1 -> x2, other arithmetic: 0.01 us -> 1.42 us  [unpack_sums(): tail = tail.astype(F32)]
  transfers between devices with their start and end apart: 36 -> 36, of which waited for: 12 -> 10; matrix products, arithmetic and copies ran while one was open for 4% -> 5% of each run, Pallas kernels for 27% -> 26%
where the time goes in v13:
time: 132 us
  Pallas kernels  45.4 us (34%)
  starting transfers between devices  39.6 us (30%)
  waiting for transfers between devices  32.2 us (24%)
  other arithmetic  9.05 us (7%)
  local copies, waits for them, and re-layouts  4.45 us (3%)
    ppermute x6, waiting for transfers between devices, gather_dp(): lax.ppermute(value, 'dp', [(i, i ^ mask) for i in range(length)])  16.2 us
    ppermute x6, starting transfers between devices, gather_dp(): lax.ppermute(value, 'dp', [(i, i ^ mask) for i in range(length)])  15.5 us
    ppermute x12, starting transfers between devices, send(): return lax.ppermute(value, ('grp', 'fsdp'), pairs)  15.1 us
    pallas_call x1, Pallas kernels, backward(): pl.pallas_call(functools.partial(backward_kernel, blocks, rows), out_shap...  13.7 us
    ppermute x6, waiting for transfers between devices, step(): return lax.ppermute(value, ('grp', 'fsdp'), pairs)  12.7 us
    pallas_call x1, Pallas kernels, forward_last(): pl.pallas_call(functools.partial(forward_last_kernel, start), out_shape=[...  11.4 us
    pallas_call x1, Pallas kernels, forward_first(): pl.pallas_call(forward_first_kernel, out_shape=(struct((tokens, part), F3...  7.42 us
    pallas_call x1, Pallas kernels, zero_projection_grad(): pl.pallas_call(functools.partial(zero_grad_kernel, blocks), out_shape=str...  7.42 us
  transfers between devices with their start and end apart: 36, of which 10 were waited for; matrix products, arithmetic and copies ran while one was open for 5% of the time, Pallas kernels for 26%

profile of v13, /device:TPU:0, one launch (start us, length us, event | category | flops | bytes accessed | tf_op | source)
XLA Modules:
  0.0 131.9 jit_solution(5173563351971372558)
XLA Ops:
  0.6 0.5 collective-permute-start
  1.1 0.8 copy.13.modulation
  1.9 0.7 fusion.18
  2.7 1.0 copy-done.2
  3.6 4.0 %prepare.1 = (f32[608,128]{1,0:T(8,128)S(1)}, bf16[608,128]{1,0:T(8,128)(2,1)S(1)}, bf16[608,128]{1,0:T(8,128)(2,1)S(1)}, bf16[608,128]{1,0:T(8,128)(2,1)S(1)}, ...) custom-call(s32[9]{0:T(128)S(1)} %pad_add_fusion.order, ...), custom_call_target="tpu_custom_call" | custom-call | flops 378535936 | bytes 4202496 | tf_op jit(solution)/shard_map/prepare/pallas_call | solution.py:395
  7.6 0.7 copy-done.8
  8.4 2.8 %collective-permute-start.1 = (bf16[608,128]{1,0:T(8,128)(2,1)S(1)}, bf16[608,128]{1,0:T(8,128)(2,1)S(1)}, u32[]{:S(2)}, u32[]{:S(2)}) collective-permute-start(bf16[608,128]{1,0:T(8,128)(2,1)S(1)} %get-tuple-element.68), channel_id=1, source_target_pairs={{0,4},{4,0},{8,12},{12,8},{16,24},{20,28},{24,16},{28,20},{1,5},{5... | collective-permute-start | bytes 466952 | tf_op jit(solution)/shard_map/ppermute | solution.py:63
  11.2 1.5 %collective-permute-start.2 = (bf16[608,128]{1,0:T(8,128)(2,1)S(1)}, bf16[608,128]{1,0:T(8,128)(2,1)S(1)}, u32[]{:S(2)}, u32[]{:S(2)}) collective-permute-start(bf16[608,128]{1,0:T(8,128)(2,1)S(1)} %get-tuple-element.69), channel_id=1, source_target_pairs={{0,8},{4,12},{8,0},{12,4},{16,20},{20,16},{24,28},{28,24},{1,9},{5... | collective-permute-start | bytes 466952 | tf_op jit(solution)/shard_map/ppermute | solution.py:63
  12.7 7.4 %forward_first.1 = (f32[256,1024]{1,0:T(8,128)S(1)}, f32[256,2432]{1,0:T(8,128)}, f32[2432,8]{1,0:T(8,128)S(1)}) custom-call(bf16[256,2432]{1,0:T(8,128)(2,1)S(1)} %get-tuple-element.79.normed, f32[1,3,2432]{2,1,0:T(4,128)S(1)} %copy.13.modulation, bf16[1,2432,2432]{2,1,0:T(8,128)(2,1)} %refs_9_.1, bf16[1,2432,2432]{2,1,0:T(8,128)(2,1)} %refs_10_.1), custom_call_target="tpu_custom_call" | custom-call | flops 2550136832 | bytes 12451840 | tf_op jit(solution)/shard_map/forward_first/pallas_call | solution.py:253
  20.1 1.0 copy-done.4
  21.7 1.2 collective-permute-done.4
  23.1 3.0 %collective-permute-start.10 = (bf16[608,256]{1,0:T(8,128)(2,1)S(1)}, bf16[608,256]{1,0:T(8,128)(2,1)S(1)}, u32[]{:S(2)}, u32[]{:S(2)}) collective-permute-start(bf16[608,256]{1,0:T(8,128)(2,1)S(1)} %multiply_convert_fusion.refs_0_), channel_id=1, source_target_pairs={{0,12},{4,8},{8,4},{12,0},{16,28},{20,24},{24,20},{28,16},{1,13},{... | collective-permute-start | bytes 933896 | tf_op jit(solution)/shard_map/ppermute | solution.py:63
  26.1 0.5 collective-permute-start.9
  26.7 11.4 %forward_last.1 = (f32[256,1408]{1,0:T(8,128)}, f32[608,256]{1,0:T(8,128)S(1)}, bf16[608,256]{1,0:T(8,128)(2,1)S(1)}, bf16[608,256]{1,0:T(8,128)(2,1)S(1)}, bf16[608,256]{1,0:T(8,128)(2,1)S(1)}) custom-call(s32[9]{0:T(128)S(1)} %pad_add_fusion.order, bf16[256,2432]{1,0:T(8,128)(2,1)S(1)} %get-tuple-element.79.normed, f32[256,2432]{1,0:T(8,128)} %get-tuple-element.75.before, ...), custom_call_target="tpu_custom_call" | custom-call | flops 3506438144 | bytes 16187392 | tf_op jit(solution)/shard_map/forward_last/pallas_call | solution.py:267
  38.1 2.0 %collective-permute-start.5 = (bf16[608,256]{1,0:T(8,128)(2,1)S(1)}, bf16[608,256]{1,0:T(8,128)(2,1)S(1)}, u32[]{:S(2)}, u32[]{:S(2)}) collective-permute-start(bf16[608,256]{1,0:T(8,128)(2,1)S(1)} %get-tuple-element.81), channel_id=1, source_target_pairs={{0,4},{4,0},{8,12},{12,8},{16,24},{20,28},{24,16},{28,20},{1,5},{5... | collective-permute-start | bytes 933896 | tf_op jit(solution)/shard_map/ppermute | solution.py:63
  40.1 1.5 %collective-permute-start.6 = (bf16[608,256]{1,0:T(8,128)(2,1)S(1)}, bf16[608,256]{1,0:T(8,128)(2,1)S(1)}, u32[]{:S(2)}, u32[]{:S(2)}) collective-permute-start(bf16[608,256]{1,0:T(8,128)(2,1)S(1)} %get-tuple-element.82), channel_id=1, source_target_pairs={{0,8},{4,12},{8,0},{12,4},{16,20},{20,16},{24,28},{28,24},{1,9},{5... | collective-permute-start | bytes 933896 | tf_op jit(solution)/shard_map/ppermute | solution.py:63
  41.7 13.7 %backward.1 = (f32[608,256]{1,0:T(8,128)S(1)}, bf16[624,256]{1,0:T(8,128)(2,1)S(1)}, bf16[624,256]{1,0:T(8,128)(2,1)S(1)}, bf16[624,256]{1,0:T(8,128)(2,1)S(1)}, f32[2,256]{1,0:T(2,128)S(1)}) custom-call(s32[9]{0:T(128)S(1)} %pad_add_fusion.order, bf16[608,256]{1,0:T(8,128)(2,1)S(1)} %multiply_convert_fusion.refs_0_, ...), custom_call_target="tpu_custom_call" | custom-call | flops 6056574976 | bytes 26148864 | tf_op jit(solution)/shard_map/backward/pallas_call | solution.py:353
  55.4 2.2 %fusion.20 = (bf16[608,256]{1,0:T(8,128)(2,1)S(1)}, f32[608,256]{1,0:T(8,128)}) fusion(f32[608,256]{1,0:T(8,128)S(1)} %get-tuple-element.80, bf16[608,256]{1,0:T(8,128)(2,1)S(1)} %collective-permute-done.7, bf16[608,256]{1,0:T(8,128)(2,1)S(1)} %collective-permute-done.6, bf16[608,256]{1,0:T(8,128)(2,1)S(1)} %collective-permute-done.5, ...), kind=kLoop, calls=%fused_computation.49 | loop fusion | flops 1556480 | bytes 2804100 | tf_op jit(solution)/shard_map/convert_element_type | solution.py:553
  57.8 1.4 %collective-permute-done.11 = bf16[608,128]{1,0:T(8,128)(2,1)S(1)} collective-permute-done((bf16[608,128]{1,0:T(8,128)(2,1)S(1)}, bf16[608,128]{1,0:T(8,128)(2,1)S(1)}, u32[]{:S(2)}, u32[]{:S(2)}) %collective-permute-start.11) | collective-permute-done | bytes 155680 | tf_op jit(solution)/shard_map/ppermute | solution.py:35
  59.2 2.0 %collective-permute-start.12 = (bf16[624,256]{1,0:T(8,128)(2,1)S(1)}, bf16[624,256]{1,0:T(8,128)(2,1)S(1)}, u32[]{:S(2)}, u32[]{:S(2)}) collective-permute-start(bf16[624,256]{1,0:T(8,128)(2,1)S(1)} %get-tuple-element.101), channel_id=1, source_target_pairs={{0,4},{4,0},{8,12},{12,8},{16,24},{20,28},{24,16},{28,20},{1,5},{5... | collective-permute-start | bytes 958472 | tf_op jit(solution)/shard_map/ppermute | solution.py:63
  61.1 1.5 %collective-permute-start.13 = (bf16[624,256]{1,0:T(8,128)(2,1)S(1)}, bf16[624,256]{1,0:T(8,128)(2,1)S(1)}, u32[]{:S(2)}, u32[]{:S(2)}) collective-permute-start(bf16[624,256]{1,0:T(8,128)(2,1)S(1)} %get-tuple-element.102), channel_id=1, source_target_pairs={{0,8},{4,12},{8,0},{12,4},{16,20},{20,16},{24,28},{28,24},{1,9},{5... | collective-permute-start | bytes 958472 | tf_op jit(solution)/shard_map/ppermute | solution.py:63
  62.7 3.0 %collective-permute-start.16 = (bf16[608,128]{1,0:T(8,128)(2,1)S(1)}, bf16[608,128]{1,0:T(8,128)(2,1)S(1)}, u32[]{:S(2)}, u32[]{:S(2)}) collective-permute-start(bf16[608,128]{1,0:T(8,128)(2,1)S(1)} %slice_select_fusion.refs_0_.refs_4_), channel_id=1, source_target_pairs={{0,2},{1,3},{2,0},{3,1},{4,6},{5,7},{6,4},{7,5},{8,10},{9,11},{10,... | collective-permute-start | bytes 466952 | tf_op jit(solution)/shard_map/ppermute | solution.py:69
  65.7 1.6 %collective-permute-start.15 = (bf16[608,128]{1,0:T(8,128)(2,1)S(1)}, bf16[608,128]{1,0:T(8,128)(2,1)S(1)}, u32[]{:S(2)}, u32[]{:S(2)}) collective-permute-start(bf16[608,128]{1,0:T(8,128)(2,1)S(1)} %slice_select_fusion.refs_0_.refs_4_), channel_id=1, source_target_pairs={{0,1},{1,0},{2,3},{3,2},{4,5},{5,4},{6,7},{7,6},{8,9},{9,8},{10,11... | collective-permute-start | bytes 466952 | tf_op jit(solution)/shard_map/ppermute | solution.py:69
  67.3 5.3 %collective-permute-done.16 = bf16[608,128]{1,0:T(8,128)(2,1)S(1)} collective-permute-done((bf16[608,128]{1,0:T(8,128)(2,1)S(1)}, bf16[608,128]{1,0:T(8,128)(2,1)S(1)}, u32[]{:S(2)}, u32[]{:S(2)}) %collective-permute-start.16) | collective-permute-done | bytes 155680 | tf_op jit(solution)/shard_map/ppermute | solution.py:69
  72.6 3.4 %collective-permute-start.17 = (bf16[608,128]{1,0:T(8,128)(2,1)S(1)}, bf16[608,128]{1,0:T(8,128)(2,1)S(1)}, u32[]{:S(2)}, u32[]{:S(2)}) collective-permute-start(bf16[608,128]{1,0:T(8,128)(2,1)S(1)} %slice_select_fusion.refs_0_.refs_4_), channel_id=1, source_target_pairs={{0,3},{1,2},{2,1},{3,0},{4,7},{5,6},{6,5},{7,4},{8,11},{9,10},{10,... | collective-permute-start | bytes 466952 | tf_op jit(solution)/shard_map/ppermute | solution.py:69
  76.1 4.3 %collective-permute-done.17 = bf16[608,128]{1,0:T(8,128)(2,1)S(1)} collective-permute-done((bf16[608,128]{1,0:T(8,128)(2,1)S(1)}, bf16[608,128]{1,0:T(8,128)(2,1)S(1)}, u32[]{:S(2)}, u32[]{:S(2)}) %collective-permute-start.17) | collective-permute-done | bytes 155680 | tf_op jit(solution)/shard_map/ppermute | solution.py:69
  80.4 0.7 copy-done.17
  81.3 0.8 pad_maximum_fusion.refs_12_
  82.2 1.5 %collective-permute-start.19 = (bf16[3,608,128]{2,1,0:T(8,128)(2,1)}, bf16[3,608,128]{2,1,0:T(8,128)(2,1)}, u32[]{:S(2)}, u32[]{:S(2)}) collective-permute-start(bf16[3,608,128]{2,1,0:T(8,128)(2,1)} %pad_maximum_fusion.refs_12_), channel_id=1, source_target_pairs={{0,4},{4,0},{8,12},{12,8},{16,24},{20,28},{24,16},{28,20},{1,5},{5... | collective-permute-start | bytes 1400840 | tf_op jit(solution)/shard_map/ppermute | solution.py:47
  83.7 1.1 collective-permute-start.21
  84.8 2.9 %collective-permute-start.20 = (bf16[608,256]{1,0:T(8,128)(2,1)}, bf16[608,256]{1,0:T(8,128)(2,1)S(1)}, u32[]{:S(2)}, u32[]{:S(2)}) collective-permute-start(bf16[608,256]{1,0:T(8,128)(2,1)} %copy-done.8), channel_id=1, source_target_pairs={{0,1},{1,0},{2,3},{3,2},{4,5},{5,4},{6,7},{7,6},{8,9},{9,8},{10,11... | collective-permute-start | bytes 933896 | tf_op jit(solution)/shard_map/ppermute | solution.py:69
  87.7 0.5 collective-permute-start.18
  88.2 4.7 %collective-permute-done.18.refs_1_.refs_5_ = bf16[608,128]{1,0:T(8,128)(2,1)S(1)} collective-permute-done((bf16[608,128]{1,0:T(8,128)(2,1)S(1)}, bf16[608,128]{1,0:T(8,128)(2,1)S(1)}, u32[]{:S(2)}, u32[]{:S(2)}) %collective-permute-start.18) | collective-permute-done | bytes 155680 | tf_op jit(solution)/shard_map/ppermute | solution.py:47
  92.9 6.5 %collective-permute-done.21.refs_2_ = bf16[608,256]{1,0:T(8,128)(2,1)S(1)} collective-permute-done((bf16[608,256]{1,0:T(8,128)(2,1)}, bf16[608,256]{1,0:T(8,128)(2,1)S(1)}, u32[]{:S(2)}, u32[]{:S(2)}) %collective-permute-start.21) | collective-permute-done | bytes 311328 | tf_op jit(solution)/shard_map/ppermute | solution.py:69
  99.4 0.6 collective-permute-start.24
  100.0 1.4 %collective-permute-start.25 = (bf16[3,608,128]{2,1,0:T(8,128)(2,1)}, bf16[3,608,128]{2,1,0:T(8,128)(2,1)S(1)}, u32[]{:S(2)}, u32[]{:S(2)}) collective-permute-start(bf16[3,608,128]{2,1,0:T(8,128)(2,1)} %collective-permute-done.19.refs_13_), channel_id=1, source_target_pairs={{0,8},{4,12},{8,0},{12,4},{16,20},{20,16},{24,28},{28,24},{1,9},{5... | collective-permute-start | bytes 1400840 | tf_op jit(solution)/shard_map/ppermute | solution.py:47
  101.5 0.7 slice_convert_fusion
  102.2 3.5 %collective-permute-start.26 = (bf16[608,256]{1,0:T(8,128)(2,1)}, bf16[608,256]{1,0:T(8,128)(2,1)S(1)}, u32[]{:S(2)}, u32[]{:S(2)}) collective-permute-start(bf16[608,256]{1,0:T(8,128)(2,1)} %copy-done.8), channel_id=1, source_target_pairs={{0,3},{1,2},{2,1},{3,0},{4,7},{5,6},{6,5},{7,4},{8,11},{9,10},{10,... | collective-permute-start | bytes 933896 | tf_op jit(solution)/shard_map/ppermute | solution.py:69
  105.7 0.7 slice_convert_fusion.2
  106.4 0.5 collective-permute-start.22
  106.9 1.5 %collective-permute-start.23 = (bf16[608,128]{1,0:T(8,128)(2,1)S(1)}, bf16[608,128]{1,0:T(8,128)(2,1)S(1)}, u32[]{:S(2)}, u32[]{:S(2)}) collective-permute-start(bf16[608,128]{1,0:T(8,128)(2,1)S(1)} %collective-permute-done.18.refs_1_.refs_5_), channel_id=1, source_target_pairs={{0,8},{4,12},{8,0},{12,4},{16,20},{20,16},{24,28},{28,24},{1,9},{5... | collective-permute-start | bytes 466952 | tf_op jit(solution)/shard_map/ppermute | solution.py:47
  108.5 6.4 %collective-permute-done.22.refs_2_.refs_6_ = bf16[608,128]{1,0:T(8,128)(2,1)S(1)} collective-permute-done((bf16[608,128]{1,0:T(8,128)(2,1)S(1)}, bf16[608,128]{1,0:T(8,128)(2,1)S(1)}, u32[]{:S(2)}, u32[]{:S(2)}) %collective-permute-start.22) | collective-permute-done | bytes 155680 | tf_op jit(solution)/shard_map/ppermute | solution.py:47
  114.9 1.7 %collective-permute-done.23.refs_3_.refs_7_ = bf16[608,128]{1,0:T(8,128)(2,1)S(1)} collective-permute-done((bf16[608,128]{1,0:T(8,128)(2,1)S(1)}, bf16[608,128]{1,0:T(8,128)(2,1)S(1)}, u32[]{:S(2)}, u32[]{:S(2)}) %collective-permute-start.23) | collective-permute-done | bytes 155680 | tf_op jit(solution)/shard_map/ppermute | solution.py:47
  116.6 0.5 collective-permute-start.29
  117.2 1.5 %residual_rows.1 = f32[608,128]{1,0:T(8,128)S(1)} custom-call(s32[9]{0:T(128)S(1)} %pad_add_fusion.order, bf16[608,2432]{1,0:T(8,128)(2,1)S(1)} %copy-done, bf16[608,128]{1,0:T(8,128)(2,1)S(1)} %slice_select_fusion.refs_0_.refs_4_, bf16[608,128]{1,0:T(8,128)(2,1)S(1)} %collective-permute-done.18.refs_1_.refs_5_, ...), custom_call_target="tpu_custom_call" | custom-call | flops 378535936 | bytes 4202496 | tf_op jit(solution)/shard_map/residual_rows/pallas_call | solution.py:427
  120.4 2.3 %fusion.5 = f32[1,608,256]{2,1,0:T(8,128)} fusion(f32[608,256]{1,0:T(8,128)S(1)} %copy-done.7, f32[608,128]{1,0:T(8,128)S(1)} %copy-done.16, f32[608,128]{1,0:T(8,128)S(1)} %copy-done.11, f32[256]{0:T(256)S(1)} %bitcast.27, f32[256]{0:T(256)S(1)} %bitcast.26, f32[256]{0:T(256)S(1)} %bitcast.28, f32[608]{0:T(1024)S(1)} %get-tuple-element.131, ...), kind=kLoop, calls=%fused_computation.7 | loop fusion | flops 2801664 | bytes 3430789 | tf_op jit(solution)/shard_map/broadcast_in_dim | solution.py:584
  122.8 0.8 fusion.8
  124.3 7.4 %zero_projection_grad.1 = f32[608,2432]{1,0:T(8,128)} custom-call(s32[9]{0:T(128)S(1)} %pad_add_fusion.order, s32[4]{0:T(128)S(1)} %iota_xor_fusion.dp_order, bf16[608,256]{1,0:T(8,128)(2,1)S(1)} %copy-done.9, bf16[608,256]{1,0:T(8,128)(2,1)S(1)} %collective-permute-done.20.refs_1_, bf16[608,256]{1,0:T(8,128)(2,1)S(1)} %collective-permute-done.21.refs_2_, ...), custom_call_target="tpu_custom_call" | custom-call | flops 3028287488 | bytes 12140544 | tf_op jit(solution)/shard_map/zero_projection_grad/pallas_call | solution.py:486
  (94 shorter events, 4.1 us)
Async XLA Ops:
  0.6 2.0 %collective-permute-start = (bf16[608,256]{1,0:T(8,128)(2,1)}, bf16[608,256]{1,0:T(8,128)(2,1)S(1)}, u32[]{:S(2)}, u32[]{:S(2)}) collective-permute-start(bf16[608,256]{1,0:T(8,128)(2,1)} %bitcast.20), channel_id=1, source_target_pairs={{0,16},{16,0},{1,17},{17,1},{2,18},{18,2},{3,19},{19,3},{4,20},{20... | collective-permute-start | bytes 933896 | tf_op jit(solution)/shard_map/ppermute | solution.py:35
  8.4 12.7 %collective-permute-start.1 = (bf16[608,128]{1,0:T(8,128)(2,1)S(1)}, bf16[608,128]{1,0:T(8,128)(2,1)S(1)}, u32[]{:S(2)}, u32[]{:S(2)}) collective-permute-start(bf16[608,128]{1,0:T(8,128)(2,1)S(1)} %get-tuple-element.68), channel_id=1, source_target_pairs={{0,4},{4,0},{8,12},{12,8},{16,24},{20,28},{24,16},{28,20},{1,5},{5... | collective-permute-start | bytes 466952 | tf_op jit(solution)/shard_map/ppermute | solution.py:63
  11.2 9.9 %collective-permute-start.2 = (bf16[608,128]{1,0:T(8,128)(2,1)S(1)}, bf16[608,128]{1,0:T(8,128)(2,1)S(1)}, u32[]{:S(2)}, u32[]{:S(2)}) collective-permute-start(bf16[608,128]{1,0:T(8,128)(2,1)S(1)} %get-tuple-element.69), channel_id=1, source_target_pairs={{0,8},{4,12},{8,0},{12,4},{16,20},{20,16},{24,28},{28,24},{1,9},{5... | collective-permute-start | bytes 466952 | tf_op jit(solution)/shard_map/ppermute | solution.py:63
  12.7 8.4 %collective-permute-start.3 = (bf16[608,128]{1,0:T(8,128)(2,1)S(1)}, bf16[608,128]{1,0:T(8,128)(2,1)S(1)}, u32[]{:S(2)}, u32[]{:S(2)}) collective-permute-start(bf16[608,128]{1,0:T(8,128)(2,1)S(1)} %get-tuple-element.70), channel_id=1, source_target_pairs={{0,12},{4,8},{8,4},{12,0},{16,28},{20,24},{24,20},{28,16},{1,13},{... | collective-permute-start | bytes 466952 | tf_op jit(solution)/shard_map/ppermute | solution.py:63
  21.2 16.9 %copy-start.10 = (f32[608,128]{1,0:T(8,128)}, f32[608,128]{1,0:T(8,128)S(1)}, u32[]{:S(2)}) copy-start(f32[608,128]{1,0:T(8,128)S(1)} %add_add_fusion) | copy-start | bytes 933892
  21.2 1.7 %collective-permute-start.4 = (f32[608,128]{1,0:T(8,128)S(1)}, f32[608,128]{1,0:T(8,128)S(1)}, u32[]{:S(2)}, u32[]{:S(2)}) collective-permute-start(f32[608,128]{1,0:T(8,128)S(1)} %add_add_fusion), channel_id=1, source_target_pairs={{0,16},{16,0},{1,17},{17,1},{2,18},{18,2},{3,19},{19,3},{4,20},{20... | collective-permute-start | bytes 933896 | tf_op jit(solution)/shard_map/ppermute | solution.py:35
  22.9 15.2 %copy-start.15 = (f32[608,128]{1,0:T(8,128)}, f32[608,128]{1,0:T(8,128)S(1)}, u32[]{:S(2)}) copy-start(f32[608,128]{1,0:T(8,128)S(1)} %collective-permute-done.4) | copy-start | bytes 933892
  23.1 18.6 %copy-start.5 = (f32[256,1024]{1,0:T(8,128)S(1)}, f32[256,1024]{1,0:T(8,128)}, u32[]{:S(2)}) copy-start(f32[256,1024]{1,0:T(8,128)} %copy-done.4) | copy-start | bytes 3145732
  23.1 18.5 %collective-permute-start.10 = (bf16[608,256]{1,0:T(8,128)(2,1)S(1)}, bf16[608,256]{1,0:T(8,128)(2,1)S(1)}, u32[]{:S(2)}, u32[]{:S(2)}) collective-permute-start(bf16[608,256]{1,0:T(8,128)(2,1)S(1)} %multiply_convert_fusion.refs_0_), channel_id=1, source_target_pairs={{0,12},{4,8},{8,4},{12,0},{16,28},{20,24},{24,20},{28,16},{1,13},{... | collective-permute-start | bytes 933896 | tf_op jit(solution)/shard_map/ppermute | solution.py:63
  26.1 15.6 %collective-permute-start.9 = (bf16[608,256]{1,0:T(8,128)(2,1)S(1)}, bf16[608,256]{1,0:T(8,128)(2,1)S(1)}, u32[]{:S(2)}, u32[]{:S(2)}) collective-permute-start(bf16[608,256]{1,0:T(8,128)(2,1)S(1)} %multiply_convert_fusion.refs_0_), channel_id=1, source_target_pairs={{0,8},{4,12},{8,0},{12,4},{16,20},{20,16},{24,28},{28,24},{1,9},{5... | collective-permute-start | bytes 933896 | tf_op jit(solution)/shard_map/ppermute | solution.py:63
  26.6 15.1 %collective-permute-start.8 = (bf16[608,256]{1,0:T(8,128)(2,1)S(1)}, bf16[608,256]{1,0:T(8,128)(2,1)S(1)}, u32[]{:S(2)}, u32[]{:S(2)}) collective-permute-start(bf16[608,256]{1,0:T(8,128)(2,1)S(1)} %multiply_convert_fusion.refs_0_), channel_id=1, source_target_pairs={{0,4},{4,0},{8,12},{12,8},{16,24},{20,28},{24,16},{28,20},{1,5},{5... | collective-permute-start | bytes 933896 | tf_op jit(solution)/shard_map/ppermute | solution.py:63
  38.1 17.3 %collective-permute-start.5 = (bf16[608,256]{1,0:T(8,128)(2,1)S(1)}, bf16[608,256]{1,0:T(8,128)(2,1)S(1)}, u32[]{:S(2)}, u32[]{:S(2)}) collective-permute-start(bf16[608,256]{1,0:T(8,128)(2,1)S(1)} %get-tuple-element.81), channel_id=1, source_target_pairs={{0,4},{4,0},{8,12},{12,8},{16,24},{20,28},{24,16},{28,20},{1,5},{5... | collective-permute-start | bytes 933896 | tf_op jit(solution)/shard_map/ppermute | solution.py:63
  40.1 15.3 %collective-permute-start.6 = (bf16[608,256]{1,0:T(8,128)(2,1)S(1)}, bf16[608,256]{1,0:T(8,128)(2,1)S(1)}, u32[]{:S(2)}, u32[]{:S(2)}) collective-permute-start(bf16[608,256]{1,0:T(8,128)(2,1)S(1)} %get-tuple-element.82), channel_id=1, source_target_pairs={{0,8},{4,12},{8,0},{12,4},{16,20},{20,16},{24,28},{28,24},{1,9},{5... | collective-permute-start | bytes 933896 | tf_op jit(solution)/shard_map/ppermute | solution.py:63
  41.6 13.8 %collective-permute-start.7 = (bf16[608,256]{1,0:T(8,128)(2,1)S(1)}, bf16[608,256]{1,0:T(8,128)(2,1)S(1)}, u32[]{:S(2)}, u32[]{:S(2)}) collective-permute-start(bf16[608,256]{1,0:T(8,128)(2,1)S(1)} %get-tuple-element.83), channel_id=1, source_target_pairs={{0,12},{4,8},{8,4},{12,0},{16,28},{20,24},{24,20},{28,16},{1,13},{... | collective-permute-start | bytes 933896 | tf_op jit(solution)/shard_map/ppermute | solution.py:63
  55.4 61.8 %copy-start = (bf16[608,2432]{1,0:T(8,128)(2,1)S(1)}, bf16[608,2432]{1,0:T(8,128)(2,1)}, u32[]{:S(2)}) copy-start(bf16[608,2432]{1,0:T(8,128)(2,1)} %weight.3) | copy-start | bytes 8871940
  57.7 22.8 %copy-start.12 = (bf16[608,256]{1,0:T(8,128)(2,1)}, bf16[608,256]{1,0:T(8,128)(2,1)S(1)}, u32[]{:S(2)}) copy-start(bf16[608,256]{1,0:T(8,128)(2,1)S(1)} %get-tuple-element.133) | copy-start | bytes 933892
  57.7 1.4 %collective-permute-start.11 = (bf16[608,128]{1,0:T(8,128)(2,1)S(1)}, bf16[608,128]{1,0:T(8,128)(2,1)S(1)}, u32[]{:S(2)}, u32[]{:S(2)}) collective-permute-start(bf16[608,128]{1,0:T(8,128)(2,1)S(1)} %slice.129), channel_id=1, source_target_pairs={{0,16},{16,0},{1,17},{17,1},{2,18},{18,2},{3,19},{19,3},{4,20},{20... | collective-permute-start | bytes 466952 | tf_op jit(solution)/shard_map/ppermute | solution.py:35
  59.2 21.2 %collective-permute-start.12 = (bf16[624,256]{1,0:T(8,128)(2,1)S(1)}, bf16[624,256]{1,0:T(8,128)(2,1)S(1)}, u32[]{:S(2)}, u32[]{:S(2)}) collective-permute-start(bf16[624,256]{1,0:T(8,128)(2,1)S(1)} %get-tuple-element.101), channel_id=1, source_target_pairs={{0,4},{4,0},{8,12},{12,8},{16,24},{20,28},{24,16},{28,20},{1,5},{5... | collective-permute-start | bytes 958472 | tf_op jit(solution)/shard_map/ppermute | solution.py:63
  61.1 19.3 %collective-permute-start.13 = (bf16[624,256]{1,0:T(8,128)(2,1)S(1)}, bf16[624,256]{1,0:T(8,128)(2,1)S(1)}, u32[]{:S(2)}, u32[]{:S(2)}) collective-permute-start(bf16[624,256]{1,0:T(8,128)(2,1)S(1)} %get-tuple-element.102), channel_id=1, source_target_pairs={{0,8},{4,12},{8,0},{12,4},{16,20},{20,16},{24,28},{28,24},{1,9},{5... | collective-permute-start | bytes 958472 | tf_op jit(solution)/shard_map/ppermute | solution.py:63
  62.6 17.8 %collective-permute-start.14 = (bf16[624,256]{1,0:T(8,128)(2,1)S(1)}, bf16[624,256]{1,0:T(8,128)(2,1)S(1)}, u32[]{:S(2)}, u32[]{:S(2)}) collective-permute-start(bf16[624,256]{1,0:T(8,128)(2,1)S(1)} %get-tuple-element.103), channel_id=1, source_target_pairs={{0,12},{4,8},{8,4},{12,0},{16,28},{20,24},{24,20},{28,16},{1,13},{... | collective-permute-start | bytes 958472 | tf_op jit(solution)/shard_map/ppermute | solution.py:63
  62.7 9.9 %collective-permute-start.16 = (bf16[608,128]{1,0:T(8,128)(2,1)S(1)}, bf16[608,128]{1,0:T(8,128)(2,1)S(1)}, u32[]{:S(2)}, u32[]{:S(2)}) collective-permute-start(bf16[608,128]{1,0:T(8,128)(2,1)S(1)} %slice_select_fusion.refs_0_.refs_4_), channel_id=1, source_target_pairs={{0,2},{1,3},{2,0},{3,1},{4,6},{5,7},{6,4},{7,5},{8,10},{9,11},{10,... | collective-permute-start | bytes 466952 | tf_op jit(solution)/shard_map/ppermute | solution.py:69
  65.7 10.4 %collective-permute-start.15 = (bf16[608,128]{1,0:T(8,128)(2,1)S(1)}, bf16[608,128]{1,0:T(8,128)(2,1)S(1)}, u32[]{:S(2)}, u32[]{:S(2)}) collective-permute-start(bf16[608,128]{1,0:T(8,128)(2,1)S(1)} %slice_select_fusion.refs_0_.refs_4_), channel_id=1, source_target_pairs={{0,1},{1,0},{2,3},{3,2},{4,5},{5,4},{6,7},{7,6},{8,9},{9,8},{10,11... | collective-permute-start | bytes 466952 | tf_op jit(solution)/shard_map/ppermute | solution.py:69
  72.6 7.7 %collective-permute-start.17 = (bf16[608,128]{1,0:T(8,128)(2,1)S(1)}, bf16[608,128]{1,0:T(8,128)(2,1)S(1)}, u32[]{:S(2)}, u32[]{:S(2)}) collective-permute-start(bf16[608,128]{1,0:T(8,128)(2,1)S(1)} %slice_select_fusion.refs_0_.refs_4_), channel_id=1, source_target_pairs={{0,3},{1,2},{2,1},{3,0},{4,7},{5,6},{6,5},{7,4},{8,11},{9,10},{10,... | collective-permute-start | bytes 466952 | tf_op jit(solution)/shard_map/ppermute | solution.py:69
  82.2 17.2 %collective-permute-start.19 = (bf16[3,608,128]{2,1,0:T(8,128)(2,1)}, bf16[3,608,128]{2,1,0:T(8,128)(2,1)}, u32[]{:S(2)}, u32[]{:S(2)}) collective-permute-start(bf16[3,608,128]{2,1,0:T(8,128)(2,1)} %pad_maximum_fusion.refs_12_), channel_id=1, source_target_pairs={{0,4},{4,0},{8,12},{12,8},{16,24},{20,28},{24,16},{28,20},{1,5},{5... | collective-permute-start | bytes 1400840 | tf_op jit(solution)/shard_map/ppermute | solution.py:47
  83.7 15.7 %collective-permute-start.21 = (bf16[608,256]{1,0:T(8,128)(2,1)}, bf16[608,256]{1,0:T(8,128)(2,1)S(1)}, u32[]{:S(2)}, u32[]{:S(2)}) collective-permute-start(bf16[608,256]{1,0:T(8,128)(2,1)} %copy-done.8), channel_id=1, source_target_pairs={{0,2},{1,3},{2,0},{3,1},{4,6},{5,7},{6,4},{7,5},{8,10},{9,11},{10,... | collective-permute-start | bytes 933896 | tf_op jit(solution)/shard_map/ppermute | solution.py:69
  84.8 14.6 %collective-permute-start.20 = (bf16[608,256]{1,0:T(8,128)(2,1)}, bf16[608,256]{1,0:T(8,128)(2,1)S(1)}, u32[]{:S(2)}, u32[]{:S(2)}) collective-permute-start(bf16[608,256]{1,0:T(8,128)(2,1)} %copy-done.8), channel_id=1, source_target_pairs={{0,1},{1,0},{2,3},{3,2},{4,5},{5,4},{6,7},{7,6},{8,9},{9,8},{10,11... | collective-permute-start | bytes 933896 | tf_op jit(solution)/shard_map/ppermute | solution.py:69
  87.7 5.2 %collective-permute-start.18 = (bf16[608,128]{1,0:T(8,128)(2,1)S(1)}, bf16[608,128]{1,0:T(8,128)(2,1)S(1)}, u32[]{:S(2)}, u32[]{:S(2)}) collective-permute-start(bf16[608,128]{1,0:T(8,128)(2,1)S(1)} %slice_select_fusion.refs_0_.refs_4_), channel_id=1, source_target_pairs={{0,4},{4,0},{8,12},{12,8},{16,24},{20,28},{24,16},{28,20},{1,5},{5... | collective-permute-start | bytes 466952 | tf_op jit(solution)/shard_map/ppermute | solution.py:47
  99.4 17.1 %collective-permute-start.24 = (bf16[3,608,128]{2,1,0:T(8,128)(2,1)}, bf16[3,608,128]{2,1,0:T(8,128)(2,1)S(1)}, u32[]{:S(2)}, u32[]{:S(2)}) collective-permute-start(bf16[3,608,128]{2,1,0:T(8,128)(2,1)} %pad_maximum_fusion.refs_12_), channel_id=1, source_target_pairs={{0,8},{4,12},{8,0},{12,4},{16,20},{20,16},{24,28},{28,24},{1,9},{5... | collective-permute-start | bytes 1400840 | tf_op jit(solution)/shard_map/ppermute | solution.py:47
  100.0 16.5 %collective-permute-start.25 = (bf16[3,608,128]{2,1,0:T(8,128)(2,1)}, bf16[3,608,128]{2,1,0:T(8,128)(2,1)S(1)}, u32[]{:S(2)}, u32[]{:S(2)}) collective-permute-start(bf16[3,608,128]{2,1,0:T(8,128)(2,1)} %collective-permute-done.19.refs_13_), channel_id=1, source_target_pairs={{0,8},{4,12},{8,0},{12,4},{16,20},{20,16},{24,28},{28,24},{1,9},{5... | collective-permute-start | bytes 1400840 | tf_op jit(solution)/shard_map/ppermute | solution.py:47
  102.2 14.4 %collective-permute-start.26 = (bf16[608,256]{1,0:T(8,128)(2,1)}, bf16[608,256]{1,0:T(8,128)(2,1)S(1)}, u32[]{:S(2)}, u32[]{:S(2)}) collective-permute-start(bf16[608,256]{1,0:T(8,128)(2,1)} %copy-done.8), channel_id=1, source_target_pairs={{0,3},{1,2},{2,1},{3,0},{4,7},{5,6},{6,5},{7,4},{8,11},{9,10},{10,... | collective-permute-start | bytes 933896 | tf_op jit(solution)/shard_map/ppermute | solution.py:69
  106.4 8.5 %collective-permute-start.22 = (bf16[608,128]{1,0:T(8,128)(2,1)S(1)}, bf16[608,128]{1,0:T(8,128)(2,1)S(1)}, u32[]{:S(2)}, u32[]{:S(2)}) collective-permute-start(bf16[608,128]{1,0:T(8,128)(2,1)S(1)} %slice_select_fusion.refs_0_.refs_4_), channel_id=1, source_target_pairs={{0,8},{4,12},{8,0},{12,4},{16,20},{20,16},{24,28},{28,24},{1,9},{5... | collective-permute-start | bytes 466952 | tf_op jit(solution)/shard_map/ppermute | solution.py:47
  106.9 9.6 %collective-permute-start.23 = (bf16[608,128]{1,0:T(8,128)(2,1)S(1)}, bf16[608,128]{1,0:T(8,128)(2,1)S(1)}, u32[]{:S(2)}, u32[]{:S(2)}) collective-permute-start(bf16[608,128]{1,0:T(8,128)(2,1)S(1)} %collective-permute-done.18.refs_1_.refs_5_), channel_id=1, source_target_pairs={{0,8},{4,12},{8,0},{12,4},{16,20},{20,16},{24,28},{28,24},{1,9},{5... | collective-permute-start | bytes 466952 | tf_op jit(solution)/shard_map/ppermute | solution.py:47
  108.4 11.9 %copy-start.7 = (f32[608,256]{1,0:T(8,128)S(1)}, f32[608,256]{1,0:T(8,128)}, u32[]{:S(2)}) copy-start(f32[608,256]{1,0:T(8,128)} %copy-done.6) | copy-start | bytes 1867780
  108.5 11.9 %copy-start.11 = (f32[608,128]{1,0:T(8,128)S(1)}, f32[608,128]{1,0:T(8,128)}, u32[]{:S(2)}) copy-start(f32[608,128]{1,0:T(8,128)} %copy-done.10) | copy-start | bytes 933892
  108.5 11.9 %copy-start.16 = (f32[608,128]{1,0:T(8,128)S(1)}, f32[608,128]{1,0:T(8,128)}, u32[]{:S(2)}) copy-start(f32[608,128]{1,0:T(8,128)} %copy-done.15) | copy-start | bytes 933892
  108.5 11.9 %copy-start.18 = (bf16[624,256]{1,0:T(8,128)(2,1)S(1)}, bf16[624,256]{1,0:T(8,128)(2,1)}, u32[]{:S(2)}) copy-start(bf16[624,256]{1,0:T(8,128)(2,1)} %copy-done.17) | copy-start | bytes 958468
  108.5 11.9 %copy-start.20 = (bf16[624,256]{1,0:T(8,128)(2,1)S(1)}, bf16[624,256]{1,0:T(8,128)(2,1)}, u32[]{:S(2)}) copy-start(bf16[624,256]{1,0:T(8,128)(2,1)} %copy-done.19) | copy-start | bytes 958468
  108.5 11.9 %copy-start.22 = (bf16[624,256]{1,0:T(8,128)(2,1)S(1)}, bf16[624,256]{1,0:T(8,128)(2,1)}, u32[]{:S(2)}) copy-start(bf16[624,256]{1,0:T(8,128)(2,1)} %copy-done.21) | copy-start | bytes 958468
  116.6 2.8 %collective-permute-start.28 = (bf16[608,128]{1,0:T(8,128)(2,1)S(1)}, bf16[608,128]{1,0:T(8,128)(2,1)S(1)}, u32[]{:S(2)}, u32[]{:S(2)}) collective-permute-start(bf16[608,128]{1,0:T(8,128)(2,1)S(1)} %slice_select_fusion.refs_0_.refs_4_), channel_id=1, source_target_pairs={{0,16},{16,0},{1,17},{17,1},{2,18},{18,2},{3,19},{19,3},{4,20},{20... | collective-permute-start | bytes 466952 | tf_op jit(solution)/shard_map/ppermute | solution.py:35
  116.6 3.2 %collective-permute-start.29 = (bf16[608,128]{1,0:T(8,128)(2,1)S(1)}, bf16[608,128]{1,0:T(8,128)(2,1)S(1)}, u32[]{:S(2)}, u32[]{:S(2)}) collective-permute-start(bf16[608,128]{1,0:T(8,128)(2,1)S(1)} %collective-permute-done.18.refs_1_.refs_5_), channel_id=1, source_target_pairs={{0,16},{16,0},{1,17},{17,1},{2,18},{18,2},{3,19},{19,3},{4,20},{20... | collective-permute-start | bytes 466952 | tf_op jit(solution)/shard_map/ppermute | solution.py:35
  117.1 2.8 %collective-permute-start.30 = (bf16[608,128]{1,0:T(8,128)(2,1)S(1)}, bf16[608,128]{1,0:T(8,128)(2,1)S(1)}, u32[]{:S(2)}, u32[]{:S(2)}) collective-permute-start(bf16[608,128]{1,0:T(8,128)(2,1)S(1)} %collective-permute-done.22.refs_2_.refs_6_), channel_id=1, source_target_pairs={{0,16},{16,0},{1,17},{17,1},{2,18},{18,2},{3,19},{19,3},{4,20},{20... | collective-permute-start | bytes 466952 | tf_op jit(solution)/shard_map/ppermute | solution.py:35
  118.7 3.9 %collective-permute-start.27 = (f32[608,128]{1,0:T(8,128)S(1)}, f32[608,128]{1,0:T(8,128)S(1)}, u32[]{:S(2)}, u32[]{:S(2)}) collective-permute-start(f32[608,128]{1,0:T(8,128)S(1)} %residual_rows.1), channel_id=1, source_target_pairs={{0,16},{16,0},{1,17},{17,1},{2,18},{18,2},{3,19},{19,3},{4,20},{20... | collective-permute-start | bytes 933896 | tf_op jit(solution)/shard_map/ppermute | solution.py:35
  119.2 4.8 %collective-permute-start.32 = (bf16[3,608,128]{2,1,0:T(8,128)(2,1)}, bf16[3,608,128]{2,1,0:T(8,128)(2,1)S(1)}, u32[]{:S(2)}, u32[]{:S(2)}) collective-permute-start(bf16[3,608,128]{2,1,0:T(8,128)(2,1)} %pad_maximum_fusion.refs_12_), channel_id=1, source_target_pairs={{0,16},{16,0},{1,17},{17,1},{2,18},{18,2},{3,19},{19,3},{4,20},{20... | collective-permute-start | bytes 1400840 | tf_op jit(solution)/shard_map/ppermute | solution.py:35
  119.4 4.7 %collective-permute-start.33 = (bf16[3,608,128]{2,1,0:T(8,128)(2,1)}, bf16[3,608,128]{2,1,0:T(8,128)(2,1)S(1)}, u32[]{:S(2)}, u32[]{:S(2)}) collective-permute-start(bf16[3,608,128]{2,1,0:T(8,128)(2,1)} %collective-permute-done.19.refs_13_), channel_id=1, source_target_pairs={{0,16},{16,0},{1,17},{17,1},{2,18},{18,2},{3,19},{19,3},{4,20},{20... | collective-permute-start | bytes 1400840 | tf_op jit(solution)/shard_map/ppermute | solution.py:35
  119.8 4.2 %collective-permute-start.34 = (bf16[3,608,128]{2,1,0:T(8,128)(2,1)S(1)}, bf16[3,608,128]{2,1,0:T(8,128)(2,1)S(1)}, u32[]{:S(2)}, u32[]{:S(2)}) collective-permute-start(bf16[3,608,128]{2,1,0:T(8,128)(2,1)S(1)} %collective-permute-done.24.refs_14_), channel_id=1, source_target_pairs={{0,16},{16,0},{1,17},{17,1},{2,18},{18,2},{3,19},{19,3},{4,20},{20... | collective-permute-start | bytes 1400840 | tf_op jit(solution)/shard_map/ppermute | solution.py:35
  119.9 4.4 %collective-permute-start.35 = (bf16[3,608,128]{2,1,0:T(8,128)(2,1)S(1)}, bf16[3,608,128]{2,1,0:T(8,128)(2,1)S(1)}, u32[]{:S(2)}, u32[]{:S(2)}) collective-permute-start(bf16[3,608,128]{2,1,0:T(8,128)(2,1)S(1)} %collective-permute-done.25.refs_15_), channel_id=1, source_target_pairs={{0,16},{16,0},{1,17},{17,1},{2,18},{18,2},{3,19},{19,3},{4,20},{20... | collective-permute-start | bytes 1400840 | tf_op jit(solution)/shard_map/ppermute | solution.py:35
  120.4 2.4 %copy-start.13 = (bf16[608,256]{1,0:T(8,128)(2,1)S(1)}, bf16[608,256]{1,0:T(8,128)(2,1)}, u32[]{:S(2)}) copy-start(bf16[608,256]{1,0:T(8,128)(2,1)} %copy-done.12) | copy-start | bytes 933892
  122.7 1.4 %collective-permute-start.31 = (bf16[608,128]{1,0:T(8,128)(2,1)S(1)}, bf16[608,128]{1,0:T(8,128)(2,1)S(1)}, u32[]{:S(2)}, u32[]{:S(2)}) collective-permute-start(bf16[608,128]{1,0:T(8,128)(2,1)S(1)} %collective-permute-done.23.refs_3_.refs_7_), channel_id=1, source_target_pairs={{0,16},{16,0},{1,17},{17,1},{2,18},{18,2},{3,19},{19,3},{4,20},{20... | collective-permute-start | bytes 466952 | tf_op jit(solution)/shard_map/ppermute | solution.py:35
  (11 other events, 15.2 us)

commit v14 on v7

--- a/solution.py
+++ b/solution.py
@@ -15,6 +15,7 @@
 F32, BF16 = jnp.float32, jnp.bfloat16
 WHOLE = pl.BlockSpec(memory_space=pltpu.VMEM)
 HELD = pl.BlockSpec(memory_space=pltpu.HBM)
+ANYWHERE = pl.BlockSpec(memory_space=pl.ANY)
 SCALARS = pl.BlockSpec(memory_space=pltpu.SMEM)
 
 
@@ -562,7 +563,7 @@
     return pl.pallas_call(
         functools.partial(zero_grad_kernel, blocks, first, count),
         out_shape=struct((rows, features), F32),
-        in_specs=[SCALARS] * 2 + [HELD] * (2 * count + len(flat)) + [WHOLE] * len(extra),
+        in_specs=[SCALARS] * 2 + [ANYWHERE] * (2 * count + len(flat)) + [WHOLE] * len(extra),
         out_specs=HELD if extra else WHOLE,
         scratch_shapes=scratch,
         name=name,

time: 128 us -> 128 us (level)
  no operation moved by 1% of the time
where the time goes in v14:
time: 128 us
  Pallas kernels  53.8 us (42%)
  starting transfers between devices  35.9 us (28%)
  waiting for transfers between devices  20.1 us (16%)
  other arithmetic  8.66 us (7%)
  local copies, waits for them, and re-layouts  8.09 us (6%)
    pallas_call x1, Pallas kernels, backward_first(): pl.pallas_call(functools.partial(backward_first_kernel, blocks, part), ou...  11.7 us
    ppermute x12, starting transfers between devices, step(): return lax.ppermute(value, ('grp', 'fsdp'), pairs)  11.7 us
    ppermute x9, starting transfers between devices, send(): return lax.ppermute(value, ('grp', 'fsdp'), pairs)  11.6 us
    pallas_call x1, Pallas kernels, forward_last(): pl.pallas_call(functools.partial(forward_last_kernel, start), out_shape=[...  11.3 us
    ppermute x6, waiting for transfers between devices, gather_dp(): lax.ppermute(value, 'dp', [(i, i ^ mask) for i in range(length)])  8.59 us
    pallas_call x2, Pallas kernels, zero_projection_grad(): pl.pallas_call(functools.partial(zero_grad_kernel, blocks, first, count),...  8.51 us
    ppermute x6, starting transfers between devices, gather_dp(): lax.ppermute(value, 'dp', [(i, i ^ mask) for i in range(length)])  8.27 us
    pallas_call x1, Pallas kernels, backward_last(): pl.pallas_call(functools.partial(backward_last_kernel, start, rows), out_...  8.14 us
  transfers between devices with their start and end apart: 47, of which 10 were waited for; matrix products, arithmetic and copies ran while one was open for 4% of the time, Pallas kernels for 35%

profile of v14, /device:TPU:0, one launch (start us, length us, event | category | flops | bytes accessed | tf_op | source)
XLA Modules:
  0.0 127.9 jit_solution(17922772615845848210)
XLA Ops:
  1.1 0.8 copy.13.modulation
  1.9 0.7 fusion.14
  2.7 1.0 copy-done.4
  3.6 4.0 %prepare.1 = (f32[608,128]{1,0:T(8,128)S(1)}, bf16[608,128]{1,0:T(8,128)(2,1)S(1)}, bf16[608,128]{1,0:T(8,128)(2,1)S(1)}, bf16[608,128]{1,0:T(8,128)(2,1)S(1)}, ...) custom-call(s32[9]{0:T(128)S(1)} %pad_add_fusion.order, ...), custom_call_target="tpu_custom_call" | custom-call | flops 378535936 | bytes 4202496 | tf_op jit(solution)/shard_map/prepare/pallas_call | solution.py:451
  7.6 2.9 %collective-permute-start.1 = (bf16[608,128]{1,0:T(8,128)(2,1)S(1)}, bf16[608,128]{1,0:T(8,128)(2,1)S(1)}, u32[]{:S(2)}, u32[]{:S(2)}) collective-permute-start(bf16[608,128]{1,0:T(8,128)(2,1)S(1)} %get-tuple-element.57), channel_id=1, source_target_pairs={{0,4},{4,0},{8,12},{12,8},{16,24},{20,28},{24,16},{28,20},{1,5},{5... | collective-permute-start | bytes 466952 | tf_op jit(solution)/shard_map/ppermute | solution.py:64
  10.5 1.5 %collective-permute-start.2 = (bf16[608,128]{1,0:T(8,128)(2,1)S(1)}, bf16[608,128]{1,0:T(8,128)(2,1)S(1)}, u32[]{:S(2)}, u32[]{:S(2)}) collective-permute-start(bf16[608,128]{1,0:T(8,128)(2,1)S(1)} %get-tuple-element.58), channel_id=1, source_target_pairs={{0,8},{4,12},{8,0},{12,4},{16,20},{20,16},{24,28},{28,24},{1,9},{5... | collective-permute-start | bytes 466952 | tf_op jit(solution)/shard_map/ppermute | solution.py:64
  12.0 7.4 %forward_first.1 = (f32[256,1024]{1,0:T(8,128)S(1)}, f32[256,2432]{1,0:T(8,128)}, f32[2432,8]{1,0:T(8,128)S(1)}) custom-call(bf16[256,2432]{1,0:T(8,128)(2,1)S(1)} %get-tuple-element.68.normed, f32[1,3,2432]{2,1,0:T(4,128)S(1)} %copy.13.modulation, bf16[1,2432,2432]{2,1,0:T(8,128)(2,1)} %w_in.5, bf16[1,2432,2432]{2,1,0:T(8,128)(2,1)} %w_out.5), custom_call_target="tpu_custom_call" | custom-call | flops 2550136832 | bytes 12451840 | tf_op jit(solution)/shard_map/forward_first/pallas_call | solution.py:254
  19.5 0.9 add_add_fusion
  20.9 1.5 %collective-permute-done.4 = f32[608,128]{1,0:T(8,128)} collective-permute-done((f32[608,128]{1,0:T(8,128)}, f32[608,128]{1,0:T(8,128)}, u32[]{:S(2)}, u32[]{:S(2)}) %collective-permute-start.4) | collective-permute-done | bytes 311328 | tf_op jit(solution)/shard_map/ppermute | solution.py:36
  22.4 1.3 %multiply_convert_fusion.refs_0_ = bf16[608,256]{1,0:T(8,128)(2,1)S(1)} fusion(f32[608,128]{1,0:T(8,128)} %collective-permute-done.4, f32[608,128]{1,0:T(8,128)} %add_add_fusion, f32[608]{0:T(1024)S(1)} %get-tuple-element.110, pred[]{:T(512)S(6)} %eq.7, bf16[1,608,256]{2,1,0:T(8,128)(2,1)} %param.13), kind=kLoop, calls=%fused_computation.11 | loop fusion | flops 778240 | bytes 1247617 | tf_op jit(solution)/shard_map/convert_element_type | solution.py:610
  23.7 3.0 %collective-permute-start.10 = (bf16[608,256]{1,0:T(8,128)(2,1)S(1)}, bf16[608,256]{1,0:T(8,128)(2,1)S(1)}, u32[]{:S(2)}, u32[]{:S(2)}) collective-permute-start(bf16[608,256]{1,0:T(8,128)(2,1)S(1)} %multiply_convert_fusion.refs_0_), channel_id=1, source_target_pairs={{0,12},{4,8},{8,4},{12,0},{16,28},{20,24},{24,20},{28,16},{1,13},{... | collective-permute-start | bytes 933896 | tf_op jit(solution)/shard_map/ppermute | solution.py:64
  27.3 11.3 %forward_last.1 = (f32[256,1408]{1,0:T(8,128)}, f32[608,256]{1,0:T(8,128)S(1)}, bf16[608,256]{1,0:T(8,128)(2,1)S(1)}, bf16[608,256]{1,0:T(8,128)(2,1)S(1)}, bf16[608,256]{1,0:T(8,128)(2,1)S(1)}) custom-call(s32[9]{0:T(128)S(1)} %pad_add_fusion.order, bf16[256,2432]{1,0:T(8,128)(2,1)S(1)} %get-tuple-element.68.normed, f32[256,2432]{1,0:T(8,128)} %get-tuple-element.64.before, ...), custom_call_target="tpu_custom_call" | custom-call | flops 3506438144 | bytes 16187392 | tf_op jit(solution)/shard_map/forward_last/pallas_call | solution.py:268
  38.7 2.0 %collective-permute-start.5 = (bf16[608,256]{1,0:T(8,128)(2,1)S(1)}, bf16[608,256]{1,0:T(8,128)(2,1)S(1)}, u32[]{:S(2)}, u32[]{:S(2)}) collective-permute-start(bf16[608,256]{1,0:T(8,128)(2,1)S(1)} %get-tuple-element.70), channel_id=1, source_target_pairs={{0,4},{4,0},{8,12},{12,8},{16,24},{20,28},{24,16},{28,20},{1,5},{5... | collective-permute-start | bytes 933896 | tf_op jit(solution)/shard_map/ppermute | solution.py:64
  40.6 1.5 %collective-permute-start.6 = (bf16[608,256]{1,0:T(8,128)(2,1)S(1)}, bf16[608,256]{1,0:T(8,128)(2,1)S(1)}, u32[]{:S(2)}, u32[]{:S(2)}) collective-permute-start(bf16[608,256]{1,0:T(8,128)(2,1)S(1)} %get-tuple-element.71), channel_id=1, source_target_pairs={{0,8},{4,12},{8,0},{12,4},{16,20},{20,16},{24,28},{28,24},{1,9},{5... | collective-permute-start | bytes 933896 | tf_op jit(solution)/shard_map/ppermute | solution.py:64
  42.2 11.7 %backward_first.1 = (bf16[256,2432]{1,0:T(8,128)(2,1)S(1)}, f32[256,2432]{1,0:T(8,128)}) custom-call(s32[9]{0:T(128)S(1)} %pad_add_fusion.order, bf16[608,256]{1,0:T(8,128)(2,1)S(1)} %multiply_convert_fusion.refs_0_, bf16[608,256]{1,0:T(8,128)(2,1)S(1)} %collective-permute-done.8.refs_1_, bf16[608,256]{1,0:T(8,128)(2,1)S(1)} %collective-permute-done.9.refs_2_, ...), custom_call_target="tpu_custom_call" | custom-call | flops 5100273664 | bytes 22413312 | tf_op jit(solution)/shard_map/backward_first/pallas_call | solution.py:326
  54.0 1.0 copy-done.6
  55.5 2.1 %fusion.16 = (bf16[608,256]{1,0:T(8,128)(2,1)S(1)}, f32[608,256]{1,0:T(8,128)}) fusion(f32[608,256]{1,0:T(8,128)S(1)} %get-tuple-element.69, bf16[608,256]{1,0:T(8,128)(2,1)S(1)} %collective-permute-done.7, bf16[608,256]{1,0:T(8,128)(2,1)S(1)} %collective-permute-done.6, bf16[608,256]{1,0:T(8,128)(2,1)S(1)} %collective-permute-done.5, ...), kind=kLoop, calls=%fused_computation.35 | loop fusion | flops 1556480 | bytes 2804100 | tf_op jit(solution)/shard_map/convert_element_type | solution.py:622
  57.6 1.4 %collective-permute-done.11 = bf16[608,128]{1,0:T(8,128)(2,1)S(1)} collective-permute-done((bf16[608,128]{1,0:T(8,128)(2,1)S(1)}, bf16[608,128]{1,0:T(8,128)(2,1)S(1)}, u32[]{:S(2)}, u32[]{:S(2)}) %collective-permute-start.11) | collective-permute-done | bytes 155680 | tf_op jit(solution)/shard_map/ppermute | solution.py:36
  59.0 1.7 %collective-permute-start.15 = (bf16[608,128]{1,0:T(8,128)(2,1)S(1)}, bf16[608,128]{1,0:T(8,128)(2,1)S(1)}, u32[]{:S(2)}, u32[]{:S(2)}) collective-permute-start(bf16[608,128]{1,0:T(8,128)(2,1)S(1)} %slice_select_fusion.refs_0_.refs_4_), channel_id=1, source_target_pairs={{0,4},{4,0},{8,12},{12,8},{16,24},{20,28},{24,16},{28,20},{1,5},{5... | collective-permute-start | bytes 466952 | tf_op jit(solution)/shard_map/ppermute | solution.py:48
  60.7 3.6 %collective-permute-start.14 = (bf16[608,128]{1,0:T(8,128)(2,1)S(1)}, bf16[608,128]{1,0:T(8,128)(2,1)S(1)}, u32[]{:S(2)}, u32[]{:S(2)}) collective-permute-start(bf16[608,128]{1,0:T(8,128)(2,1)S(1)} %slice_select_fusion.refs_0_.refs_4_), channel_id=1, source_target_pairs={{0,3},{1,2},{2,1},{3,0},{4,7},{5,6},{6,5},{7,4},{8,11},{9,10},{10,... | collective-permute-start | bytes 466952 | tf_op jit(solution)/shard_map/ppermute | solution.py:70
  64.3 0.8 collective-permute-start.12
  65.1 8.1 %backward_last.1 = (bf16[624,256]{1,0:T(8,128)(2,1)}, bf16[624,256]{1,0:T(8,128)(2,1)}, f32[608,256]{1,0:T(8,128)S(1)}, f32[608,256]{1,0:T(8,128)S(1)}, f32[2,256]{1,0:T(2,128)S(1)}) custom-call(s32[9]{0:T(128)S(1)} %pad_add_fusion.order, bf16[256,2432]{1,0:T(8,128)(2,1)} %copy-done.6, f32[256,2432]{1,0:T(8,128)} %get-tuple-element.82.before, ...), custom_call_target="tpu_custom_call" | custom-call | flops 956301312 | bytes 6225920 | tf_op jit(solution)/shard_map/backward_last/pallas_call | solution.py:379
  73.3 0.8 copy-done.10
  74.1 0.9 copy-done.12
  74.9 2.6 %collective-permute-done.13 = bf16[608,128]{1,0:T(8,128)(2,1)S(1)} collective-permute-done((bf16[608,128]{1,0:T(8,128)(2,1)S(1)}, bf16[608,128]{1,0:T(8,128)(2,1)S(1)}, u32[]{:S(2)}, u32[]{:S(2)}) %collective-permute-start.13) | collective-permute-done | bytes 155680 | tf_op jit(solution)/shard_map/ppermute | solution.py:70
  78.6 0.9 collective-permute-start.37
  79.5 0.7 copy-done.17
  80.8 3.2 %collective-permute-done.33.refs_1_ = bf16[608,128]{1,0:T(8,128)(2,1)S(1)} collective-permute-done((bf16[608,128]{1,0:T(8,128)(2,1)S(1)}, bf16[608,128]{1,0:T(8,128)(2,1)S(1)}, u32[]{:S(2)}, u32[]{:S(2)}) %collective-permute-start.33) | collective-permute-done | bytes 155680 | tf_op jit(solution)/shard_map/ppermute | solution.py:70
  84.1 1.5 %collective-permute-start.19 = (bf16[624,256]{1,0:T(8,128)(2,1)}, bf16[624,256]{1,0:T(8,128)(2,1)}, u32[]{:S(2)}, u32[]{:S(2)}) collective-permute-start(bf16[624,256]{1,0:T(8,128)(2,1)} %get-tuple-element.96), channel_id=1, source_target_pairs={{0,4},{4,0},{8,12},{12,8},{16,24},{20,28},{24,16},{28,20},{1,5},{5... | collective-permute-start | bytes 958472 | tf_op jit(solution)/shard_map/ppermute | solution.py:48
  88.6 1.5 %collective-permute-start.40 = (bf16[608,128]{1,0:T(8,128)(2,1)}, bf16[608,128]{1,0:T(8,128)(2,1)}, u32[]{:S(2)}, u32[]{:S(2)}) collective-permute-start(bf16[608,128]{1,0:T(8,128)(2,1)} %collective-permute-done.12.refs_12_), channel_id=1, source_target_pairs={{0,4},{4,0},{8,12},{12,8},{16,24},{20,28},{24,16},{28,20},{1,5},{5... | collective-permute-start | bytes 466952 | tf_op jit(solution)/shard_map/ppermute | solution.py:48
  90.1 4.6 %collective-permute-done.41.refs_14_ = bf16[608,128]{1,0:T(8,128)(2,1)} collective-permute-done((bf16[608,128]{1,0:T(8,128)(2,1)}, bf16[608,128]{1,0:T(8,128)(2,1)}, u32[]{:S(2)}, u32[]{:S(2)}) %collective-permute-start.41) | collective-permute-done | bytes 155680 | tf_op jit(solution)/shard_map/ppermute | solution.py:48
  94.7 0.9 copy-done.8
  95.6 1.5 %residual_rows.1 = f32[608,128]{1,0:T(8,128)S(1)} custom-call(s32[9]{0:T(128)S(1)} %pad_add_fusion.order, bf16[608,2432]{1,0:T(8,128)(2,1)S(1)} %copy-done, bf16[608,128]{1,0:T(8,128)(2,1)S(1)} %slice_select_fusion.refs_0_.refs_4_, bf16[608,128]{1,0:T(8,128)(2,1)S(1)} %collective-permute-done.15.refs_1_.refs_5_, ...), custom_call_target="tpu_custom_call" | custom-call | flops 378535936 | bytes 4202496 | tf_op jit(solution)/shard_map/residual_rows/pallas_call | solution.py:483
  97.2 0.9 collective-permute-done.40.refs_13_
  98.2 1.6 %collective-permute-start.26 = (bf16[2,608,128]{2,1,0:T(8,128)(2,1)S(1)}, bf16[2,608,128]{2,1,0:T(8,128)(2,1)S(1)}, u32[]{:S(2)}, u32[]{:S(2)}) collective-permute-start(bf16[2,608,128]{2,1,0:T(8,128)(2,1)S(1)} %pad_maximum_fusion.refs_4_), channel_id=1, source_target_pairs={{0,4},{4,0},{8,12},{12,8},{16,24},{20,28},{24,16},{28,20},{1,5},{5... | collective-permute-start | bytes 933896 | tf_op jit(solution)/shard_map/ppermute | solution.py:48
  100.8 1.3 fold.1
  102.1 2.5 %collective-permute-start.23 = (bf16[608,128]{1,0:T(8,128)(2,1)S(1)}, bf16[608,128]{1,0:T(8,128)(2,1)S(1)}, u32[]{:S(2)}, u32[]{:S(2)}) collective-permute-start(bf16[608,128]{1,0:T(8,128)(2,1)S(1)} %copy-done.16), channel_id=1, source_target_pairs={{0,3},{1,2},{2,1},{3,0},{4,7},{5,6},{6,5},{7,4},{8,11},{9,10},{10,... | collective-permute-start | bytes 466952 | tf_op jit(solution)/shard_map/ppermute | solution.py:70
  104.7 1.7 %collective-permute-done.42.refs_15_ = bf16[608,128]{1,0:T(8,128)(2,1)S(1)} collective-permute-done((bf16[608,128]{1,0:T(8,128)(2,1)}, bf16[608,128]{1,0:T(8,128)(2,1)S(1)}, u32[]{:S(2)}, u32[]{:S(2)}) %collective-permute-start.42) | collective-permute-done | bytes 155680 | tf_op jit(solution)/shard_map/ppermute | solution.py:48
  106.6 0.7 collective-permute-start.21
  107.4 0.8 fusion.8
  108.2 1.3 %collective-permute-start.22 = (bf16[608,128]{1,0:T(8,128)(2,1)S(1)}, bf16[608,128]{1,0:T(8,128)(2,1)S(1)}, u32[]{:S(2)}, u32[]{:S(2)}) collective-permute-start(bf16[608,128]{1,0:T(8,128)(2,1)S(1)} %copy-done.16), channel_id=1, source_target_pairs={{0,2},{1,3},{2,0},{3,1},{4,6},{5,7},{6,4},{7,5},{8,10},{9,11},{10,... | collective-permute-start | bytes 466952 | tf_op jit(solution)/shard_map/ppermute | solution.py:70
  109.5 1.3 %collective-permute-start.27 = (bf16[2,608,128]{2,1,0:T(8,128)(2,1)S(1)}, bf16[2,608,128]{2,1,0:T(8,128)(2,1)S(1)}, u32[]{:S(2)}, u32[]{:S(2)}) collective-permute-start(bf16[2,608,128]{2,1,0:T(8,128)(2,1)S(1)} %pad_maximum_fusion.refs_4_), channel_id=1, source_target_pairs={{0,8},{4,12},{8,0},{12,4},{16,20},{20,16},{24,28},{28,24},{1,9},{5... | collective-permute-start | bytes 933896 | tf_op jit(solution)/shard_map/ppermute | solution.py:48
  110.8 0.7 collective-permute-start.28
  111.5 4.0 %zero_projection_grad_first.1.refs_12_ = f32[608,2432]{1,0:T(8,128)S(1)} custom-call(s32[9]{0:T(128)S(1)} %pad_add_fusion.order, s32[4]{0:T(128)S(1)} %iota_xor_fusion.dp_order, bf16[608,128]{1,0:T(8,128)(2,1)S(1)} %copy-done.16, bf16[608,128]{1,0:T(8,128)(2,1)S(1)} %copy-done.20, bf16[608,128]{1,0:T(8,128)(2,1)S(1)} %copy-done.18, ...), custom_call_target="tpu_custom_call" | custom-call | flops 1514143744 | bytes 9027584 | tf_op jit(solution)/shard_map/zero_projection_grad_first/pallas_call | solution.py:563
  116.2 2.8 %collective-permute-done.22.refs_0_ = bf16[608,128]{1,0:T(8,128)(2,1)S(1)} collective-permute-done((bf16[608,128]{1,0:T(8,128)(2,1)S(1)}, bf16[608,128]{1,0:T(8,128)(2,1)S(1)}, u32[]{:S(2)}, u32[]{:S(2)}) %collective-permute-start.22) | collective-permute-done | bytes 155680 | tf_op jit(solution)/shard_map/ppermute | solution.py:70
  119.4 0.9 collective-permute-done.28.refs_7_
  120.9 2.3 %fusion.5 = f32[1,608,256]{2,1,0:T(8,128)} fusion(f32[608,256]{1,0:T(8,128)S(1)} %get-tuple-element.101, f32[608,128]{1,0:T(8,128)} %collective-permute-done.4, f32[608,128]{1,0:T(8,128)} %add_add_fusion, bf16[624,256]{1,0:T(8,128)(2,1)S(1)} %collective-permute-done.21, f32[256]{0:T(256)S(1)} %bitcast.24, f32[256]{0:T(256)S(1)} %bitcast.26, ...), kind=kLoop, calls=%fused_computation.7 | loop fusion | flops 2179072 | bytes 2808197 | tf_op jit(solution)/shard_map/broadcast_in_dim | solution.py:661
  123.2 4.5 %zero_projection_grad_last.1 = f32[608,2432]{1,0:T(8,128)} custom-call(s32[9]{0:T(128)S(1)} %pad_add_fusion.order, s32[4]{0:T(128)S(1)} %iota_xor_fusion.dp_order, bf16[608,128]{1,0:T(8,128)(2,1)S(1)} %collective-permute-done.22.refs_0_, bf16[608,128]{1,0:T(8,128)(2,1)S(1)} %collective-permute-done.23.refs_1_, ...), custom_call_target="tpu_custom_call" | custom-call | flops 1514143744 | bytes 9027584 | tf_op jit(solution)/shard_map/zero_projection_grad_last/pallas_call | solution.py:563
  (135 shorter events, 10.3 us)
Async XLA Ops:
  0.6 2.0 %collective-permute-start = (bf16[608,256]{1,0:T(8,128)(2,1)}, bf16[608,256]{1,0:T(8,128)(2,1)S(1)}, u32[]{:S(2)}, u32[]{:S(2)}) collective-permute-start(bf16[608,256]{1,0:T(8,128)(2,1)} %bitcast.19), channel_id=1, source_target_pairs={{0,16},{16,0},{1,17},{17,1},{2,18},{18,2},{3,19},{19,3},{4,20},{20... | collective-permute-start | bytes 933896 | tf_op jit(solution)/shard_map/ppermute | solution.py:36
  7.6 11.8 %collective-permute-start.1 = (bf16[608,128]{1,0:T(8,128)(2,1)S(1)}, bf16[608,128]{1,0:T(8,128)(2,1)S(1)}, u32[]{:S(2)}, u32[]{:S(2)}) collective-permute-start(bf16[608,128]{1,0:T(8,128)(2,1)S(1)} %get-tuple-element.57), channel_id=1, source_target_pairs={{0,4},{4,0},{8,12},{12,8},{16,24},{20,28},{24,16},{28,20},{1,5},{5... | collective-permute-start | bytes 466952 | tf_op jit(solution)/shard_map/ppermute | solution.py:64
  10.5 9.0 %collective-permute-start.2 = (bf16[608,128]{1,0:T(8,128)(2,1)S(1)}, bf16[608,128]{1,0:T(8,128)(2,1)S(1)}, u32[]{:S(2)}, u32[]{:S(2)}) collective-permute-start(bf16[608,128]{1,0:T(8,128)(2,1)S(1)} %get-tuple-element.58), channel_id=1, source_target_pairs={{0,8},{4,12},{8,0},{12,4},{16,20},{20,16},{24,28},{28,24},{1,9},{5... | collective-permute-start | bytes 466952 | tf_op jit(solution)/shard_map/ppermute | solution.py:64
  12.0 7.5 %collective-permute-start.3 = (bf16[608,128]{1,0:T(8,128)(2,1)S(1)}, bf16[608,128]{1,0:T(8,128)(2,1)S(1)}, u32[]{:S(2)}, u32[]{:S(2)}) collective-permute-start(bf16[608,128]{1,0:T(8,128)(2,1)S(1)} %get-tuple-element.59), channel_id=1, source_target_pairs={{0,12},{4,8},{8,4},{12,0},{16,28},{20,24},{24,20},{28,16},{1,13},{... | collective-permute-start | bytes 466952 | tf_op jit(solution)/shard_map/ppermute | solution.py:64
  20.5 1.9 %collective-permute-start.4 = (f32[608,128]{1,0:T(8,128)}, f32[608,128]{1,0:T(8,128)}, u32[]{:S(2)}, u32[]{:S(2)}) collective-permute-start(f32[608,128]{1,0:T(8,128)} %add_add_fusion), channel_id=1, source_target_pairs={{0,16},{16,0},{1,17},{17,1},{2,18},{18,2},{3,19},{19,3},{4,20},{20... | collective-permute-start | bytes 933896 | tf_op jit(solution)/shard_map/ppermute | solution.py:36
  23.7 18.4 %collective-permute-start.10 = (bf16[608,256]{1,0:T(8,128)(2,1)S(1)}, bf16[608,256]{1,0:T(8,128)(2,1)S(1)}, u32[]{:S(2)}, u32[]{:S(2)}) collective-permute-start(bf16[608,256]{1,0:T(8,128)(2,1)S(1)} %multiply_convert_fusion.refs_0_), channel_id=1, source_target_pairs={{0,12},{4,8},{8,4},{12,0},{16,28},{20,24},{24,20},{28,16},{1,13},{... | collective-permute-start | bytes 933896 | tf_op jit(solution)/shard_map/ppermute | solution.py:64
  26.7 15.5 %collective-permute-start.9 = (bf16[608,256]{1,0:T(8,128)(2,1)S(1)}, bf16[608,256]{1,0:T(8,128)(2,1)S(1)}, u32[]{:S(2)}, u32[]{:S(2)}) collective-permute-start(bf16[608,256]{1,0:T(8,128)(2,1)S(1)} %multiply_convert_fusion.refs_0_), channel_id=1, source_target_pairs={{0,8},{4,12},{8,0},{12,4},{16,20},{20,16},{24,28},{28,24},{1,9},{5... | collective-permute-start | bytes 933896 | tf_op jit(solution)/shard_map/ppermute | solution.py:64
  27.2 15.0 %collective-permute-start.8 = (bf16[608,256]{1,0:T(8,128)(2,1)S(1)}, bf16[608,256]{1,0:T(8,128)(2,1)S(1)}, u32[]{:S(2)}, u32[]{:S(2)}) collective-permute-start(bf16[608,256]{1,0:T(8,128)(2,1)S(1)} %multiply_convert_fusion.refs_0_), channel_id=1, source_target_pairs={{0,4},{4,0},{8,12},{12,8},{16,24},{20,28},{24,16},{28,20},{1,5},{5... | collective-permute-start | bytes 933896 | tf_op jit(solution)/shard_map/ppermute | solution.py:64
  38.7 16.3 %collective-permute-start.5 = (bf16[608,256]{1,0:T(8,128)(2,1)S(1)}, bf16[608,256]{1,0:T(8,128)(2,1)S(1)}, u32[]{:S(2)}, u32[]{:S(2)}) collective-permute-start(bf16[608,256]{1,0:T(8,128)(2,1)S(1)} %get-tuple-element.70), channel_id=1, source_target_pairs={{0,4},{4,0},{8,12},{12,8},{16,24},{20,28},{24,16},{28,20},{1,5},{5... | collective-permute-start | bytes 933896 | tf_op jit(solution)/shard_map/ppermute | solution.py:64
  40.6 14.4 %collective-permute-start.6 = (bf16[608,256]{1,0:T(8,128)(2,1)S(1)}, bf16[608,256]{1,0:T(8,128)(2,1)S(1)}, u32[]{:S(2)}, u32[]{:S(2)}) collective-permute-start(bf16[608,256]{1,0:T(8,128)(2,1)S(1)} %get-tuple-element.71), channel_id=1, source_target_pairs={{0,8},{4,12},{8,0},{12,4},{16,20},{20,16},{24,28},{28,24},{1,9},{5... | collective-permute-start | bytes 933896 | tf_op jit(solution)/shard_map/ppermute | solution.py:64
  42.2 13.3 %collective-permute-start.7 = (bf16[608,256]{1,0:T(8,128)(2,1)S(1)}, bf16[608,256]{1,0:T(8,128)(2,1)S(1)}, u32[]{:S(2)}, u32[]{:S(2)}) collective-permute-start(bf16[608,256]{1,0:T(8,128)(2,1)S(1)} %get-tuple-element.72), channel_id=1, source_target_pairs={{0,12},{4,8},{8,4},{12,0},{16,28},{20,24},{24,20},{28,16},{1,13},{... | collective-permute-start | bytes 933896 | tf_op jit(solution)/shard_map/ppermute | solution.py:64
  57.6 1.4 %collective-permute-start.11 = (bf16[608,128]{1,0:T(8,128)(2,1)S(1)}, bf16[608,128]{1,0:T(8,128)(2,1)S(1)}, u32[]{:S(2)}, u32[]{:S(2)}) collective-permute-start(bf16[608,128]{1,0:T(8,128)(2,1)S(1)} %slice.65), channel_id=1, source_target_pairs={{0,16},{16,0},{1,17},{17,1},{2,18},{18,2},{3,19},{19,3},{4,20},{20... | collective-permute-start | bytes 466952 | tf_op jit(solution)/shard_map/ppermute | solution.py:36
  59.0 15.9 %collective-permute-start.15 = (bf16[608,128]{1,0:T(8,128)(2,1)S(1)}, bf16[608,128]{1,0:T(8,128)(2,1)S(1)}, u32[]{:S(2)}, u32[]{:S(2)}) collective-permute-start(bf16[608,128]{1,0:T(8,128)(2,1)S(1)} %slice_select_fusion.refs_0_.refs_4_), channel_id=1, source_target_pairs={{0,4},{4,0},{8,12},{12,8},{16,24},{20,28},{24,16},{28,20},{1,5},{5... | collective-permute-start | bytes 466952 | tf_op jit(solution)/shard_map/ppermute | solution.py:48
  60.7 14.2 %collective-permute-start.14 = (bf16[608,128]{1,0:T(8,128)(2,1)S(1)}, bf16[608,128]{1,0:T(8,128)(2,1)S(1)}, u32[]{:S(2)}, u32[]{:S(2)}) collective-permute-start(bf16[608,128]{1,0:T(8,128)(2,1)S(1)} %slice_select_fusion.refs_0_.refs_4_), channel_id=1, source_target_pairs={{0,3},{1,2},{2,1},{3,0},{4,7},{5,6},{6,5},{7,4},{8,11},{9,10},{10,... | collective-permute-start | bytes 466952 | tf_op jit(solution)/shard_map/ppermute | solution.py:70
  64.3 13.2 %collective-permute-start.13 = (bf16[608,128]{1,0:T(8,128)(2,1)S(1)}, bf16[608,128]{1,0:T(8,128)(2,1)S(1)}, u32[]{:S(2)}, u32[]{:S(2)}) collective-permute-start(bf16[608,128]{1,0:T(8,128)(2,1)S(1)} %slice_select_fusion.refs_0_.refs_4_), channel_id=1, source_target_pairs={{0,2},{1,3},{2,0},{3,1},{4,6},{5,7},{6,4},{7,5},{8,10},{9,11},{10,... | collective-permute-start | bytes 466952 | tf_op jit(solution)/shard_map/ppermute | solution.py:70
  64.3 13.2 %collective-permute-start.12 = (bf16[608,128]{1,0:T(8,128)(2,1)S(1)}, bf16[608,128]{1,0:T(8,128)(2,1)}, u32[]{:S(2)}, u32[]{:S(2)}) collective-permute-start(bf16[608,128]{1,0:T(8,128)(2,1)S(1)} %slice_select_fusion.refs_0_.refs_4_), channel_id=1, source_target_pairs={{0,1},{1,0},{2,3},{3,2},{4,5},{5,4},{6,7},{7,6},{8,9},{9,8},{10,11... | collective-permute-start | bytes 466952 | tf_op jit(solution)/shard_map/ppermute | solution.py:70
  65.1 29.6 %copy-start = (bf16[608,2432]{1,0:T(8,128)(2,1)S(1)}, bf16[608,2432]{1,0:T(8,128)(2,1)}, u32[]{:S(2)}) copy-start(bf16[608,2432]{1,0:T(8,128)(2,1)} %weight.3) | copy-start | bytes 8871940
  77.5 2.0 %collective-permute-start.34 = (bf16[608,128]{1,0:T(8,128)(2,1)S(1)}, bf16[608,128]{1,0:T(8,128)(2,1)S(1)}, u32[]{:S(2)}, u32[]{:S(2)}) collective-permute-start(bf16[608,128]{1,0:T(8,128)(2,1)S(1)} %copy-done.15), channel_id=1, source_target_pairs={{0,16},{16,0},{1,17},{17,1},{2,18},{18,2},{3,19},{19,3},{4,20},{20... | collective-permute-start | bytes 466952 | tf_op jit(solution)/shard_map/ppermute | solution.py:36
  77.6 6.4 %collective-permute-start.33 = (bf16[608,128]{1,0:T(8,128)(2,1)S(1)}, bf16[608,128]{1,0:T(8,128)(2,1)S(1)}, u32[]{:S(2)}, u32[]{:S(2)}) collective-permute-start(bf16[608,128]{1,0:T(8,128)(2,1)S(1)} %copy-done.15), channel_id=1, source_target_pairs={{0,1},{1,0},{2,3},{3,2},{4,5},{5,4},{6,7},{7,6},{8,9},{9,8},{10,11... | collective-permute-start | bytes 466952 | tf_op jit(solution)/shard_map/ppermute | solution.py:70
  77.7 7.9 %collective-permute-start.36 = (bf16[608,128]{1,0:T(8,128)(2,1)S(1)}, bf16[608,128]{1,0:T(8,128)(2,1)S(1)}, u32[]{:S(2)}, u32[]{:S(2)}) collective-permute-start(bf16[608,128]{1,0:T(8,128)(2,1)S(1)} %slice_select_fusion.refs_0_.refs_4_), channel_id=1, source_target_pairs={{0,16},{16,0},{1,17},{17,1},{2,18},{18,2},{3,19},{19,3},{4,20},{20... | collective-permute-start | bytes 466952 | tf_op jit(solution)/shard_map/ppermute | solution.py:36
  78.1 8.6 %collective-permute-start.16 = (bf16[608,128]{1,0:T(8,128)(2,1)S(1)}, bf16[608,128]{1,0:T(8,128)(2,1)S(1)}, u32[]{:S(2)}, u32[]{:S(2)}) collective-permute-start(bf16[608,128]{1,0:T(8,128)(2,1)S(1)} %slice_select_fusion.refs_0_.refs_4_), channel_id=1, source_target_pairs={{0,8},{4,12},{8,0},{12,4},{16,20},{20,16},{24,28},{28,24},{1,9},{5... | collective-permute-start | bytes 466952 | tf_op jit(solution)/shard_map/ppermute | solution.py:48
  78.6 8.1 %collective-permute-start.37 = (bf16[608,128]{1,0:T(8,128)(2,1)S(1)}, bf16[608,128]{1,0:T(8,128)(2,1)S(1)}, u32[]{:S(2)}, u32[]{:S(2)}) collective-permute-start(bf16[608,128]{1,0:T(8,128)(2,1)S(1)} %collective-permute-done.15.refs_1_.refs_5_), channel_id=1, source_target_pairs={{0,16},{16,0},{1,17},{17,1},{2,18},{18,2},{3,19},{19,3},{4,20},{20... | collective-permute-start | bytes 466952 | tf_op jit(solution)/shard_map/ppermute | solution.py:36
  80.2 7.8 %collective-permute-start.17 = (bf16[608,128]{1,0:T(8,128)(2,1)S(1)}, bf16[608,128]{1,0:T(8,128)(2,1)S(1)}, u32[]{:S(2)}, u32[]{:S(2)}) collective-permute-start(bf16[608,128]{1,0:T(8,128)(2,1)S(1)} %collective-permute-done.15.refs_1_.refs_5_), channel_id=1, source_target_pairs={{0,8},{4,12},{8,0},{12,4},{16,20},{20,16},{24,28},{28,24},{1,9},{5... | collective-permute-start | bytes 466952 | tf_op jit(solution)/shard_map/ppermute | solution.py:48
  84.1 15.7 %collective-permute-start.19 = (bf16[624,256]{1,0:T(8,128)(2,1)}, bf16[624,256]{1,0:T(8,128)(2,1)}, u32[]{:S(2)}, u32[]{:S(2)}) collective-permute-start(bf16[624,256]{1,0:T(8,128)(2,1)} %get-tuple-element.96), channel_id=1, source_target_pairs={{0,4},{4,0},{8,12},{12,8},{16,24},{20,28},{24,16},{28,20},{1,5},{5... | collective-permute-start | bytes 958472 | tf_op jit(solution)/shard_map/ppermute | solution.py:48
  86.2 14.1 %collective-permute-start.20 = (bf16[624,256]{1,0:T(8,128)(2,1)}, bf16[624,256]{1,0:T(8,128)(2,1)}, u32[]{:S(2)}, u32[]{:S(2)}) collective-permute-start(bf16[624,256]{1,0:T(8,128)(2,1)} %get-tuple-element.97), channel_id=1, source_target_pairs={{0,4},{4,0},{8,12},{12,8},{16,24},{20,28},{24,16},{28,20},{1,5},{5... | collective-permute-start | bytes 958472 | tf_op jit(solution)/shard_map/ppermute | solution.py:48
  86.8 3.4 %collective-permute-start.43 = (bf16[608,128]{1,0:T(8,128)(2,1)}, bf16[608,128]{1,0:T(8,128)(2,1)}, u32[]{:S(2)}, u32[]{:S(2)}) collective-permute-start(bf16[608,128]{1,0:T(8,128)(2,1)} %collective-permute-done.12.refs_12_), channel_id=1, source_target_pairs={{0,16},{16,0},{1,17},{17,1},{2,18},{18,2},{3,19},{19,3},{4,20},{20... | collective-permute-start | bytes 466952 | tf_op jit(solution)/shard_map/ppermute | solution.py:36
  87.4 7.3 %collective-permute-start.41 = (bf16[608,128]{1,0:T(8,128)(2,1)}, bf16[608,128]{1,0:T(8,128)(2,1)}, u32[]{:S(2)}, u32[]{:S(2)}) collective-permute-start(bf16[608,128]{1,0:T(8,128)(2,1)} %collective-permute-done.12.refs_12_), channel_id=1, source_target_pairs={{0,8},{4,12},{8,0},{12,4},{16,20},{20,16},{24,28},{28,24},{1,9},{5... | collective-permute-start | bytes 466952 | tf_op jit(solution)/shard_map/ppermute | solution.py:48
  88.6 9.5 %collective-permute-start.40 = (bf16[608,128]{1,0:T(8,128)(2,1)}, bf16[608,128]{1,0:T(8,128)(2,1)}, u32[]{:S(2)}, u32[]{:S(2)}) collective-permute-start(bf16[608,128]{1,0:T(8,128)(2,1)} %collective-permute-done.12.refs_12_), channel_id=1, source_target_pairs={{0,4},{4,0},{8,12},{12,8},{16,24},{20,28},{24,16},{28,20},{1,5},{5... | collective-permute-start | bytes 466952 | tf_op jit(solution)/shard_map/ppermute | solution.py:48
  90.1 8.1 %collective-permute-start.35 = (bf16[608,128]{1,0:T(8,128)(2,1)}, bf16[608,128]{1,0:T(8,128)(2,1)S(1)}, u32[]{:S(2)}, u32[]{:S(2)}) collective-permute-start(bf16[608,128]{1,0:T(8,128)(2,1)} %copy-done.19), channel_id=1, source_target_pairs={{0,16},{16,0},{1,17},{17,1},{2,18},{18,2},{3,19},{19,3},{4,20},{20... | collective-permute-start | bytes 466952 | tf_op jit(solution)/shard_map/ppermute | solution.py:36
  94.7 5.1 %collective-permute-start.38 = (bf16[608,128]{1,0:T(8,128)(2,1)S(1)}, bf16[608,128]{1,0:T(8,128)(2,1)S(1)}, u32[]{:S(2)}, u32[]{:S(2)}) collective-permute-start(bf16[608,128]{1,0:T(8,128)(2,1)S(1)} %collective-permute-done.16.refs_2_.refs_6_), channel_id=1, source_target_pairs={{0,16},{16,0},{1,17},{17,1},{2,18},{18,2},{3,19},{19,3},{4,20},{20... | collective-permute-start | bytes 466952 | tf_op jit(solution)/shard_map/ppermute | solution.py:36
  98.1 8.5 %collective-permute-start.18 = (f32[608,128]{1,0:T(8,128)S(1)}, f32[608,128]{1,0:T(8,128)S(1)}, u32[]{:S(2)}, u32[]{:S(2)}) collective-permute-start(f32[608,128]{1,0:T(8,128)S(1)} %residual_rows.1), channel_id=1, source_target_pairs={{0,16},{16,0},{1,17},{17,1},{2,18},{18,2},{3,19},{19,3},{4,20},{20... | collective-permute-start | bytes 933896 | tf_op jit(solution)/shard_map/ppermute | solution.py:36
  98.2 11.3 %collective-permute-start.26 = (bf16[2,608,128]{2,1,0:T(8,128)(2,1)S(1)}, bf16[2,608,128]{2,1,0:T(8,128)(2,1)S(1)}, u32[]{:S(2)}, u32[]{:S(2)}) collective-permute-start(bf16[2,608,128]{2,1,0:T(8,128)(2,1)S(1)} %pad_maximum_fusion.refs_4_), channel_id=1, source_target_pairs={{0,4},{4,0},{8,12},{12,8},{16,24},{20,28},{24,16},{28,20},{1,5},{5... | collective-permute-start | bytes 933896 | tf_op jit(solution)/shard_map/ppermute | solution.py:48
  99.8 2.3 %collective-permute-start.39 = (bf16[608,128]{1,0:T(8,128)(2,1)S(1)}, bf16[608,128]{1,0:T(8,128)(2,1)S(1)}, u32[]{:S(2)}, u32[]{:S(2)}) collective-permute-start(bf16[608,128]{1,0:T(8,128)(2,1)S(1)} %copy-done.9), channel_id=1, source_target_pairs={{0,16},{16,0},{1,17},{17,1},{2,18},{18,2},{3,19},{19,3},{4,20},{20... | collective-permute-start | bytes 466952 | tf_op jit(solution)/shard_map/ppermute | solution.py:36
  99.8 4.9 %collective-permute-start.45 = (bf16[608,128]{1,0:T(8,128)(2,1)}, bf16[608,128]{1,0:T(8,128)(2,1)S(1)}, u32[]{:S(2)}, u32[]{:S(2)}) collective-permute-start(bf16[608,128]{1,0:T(8,128)(2,1)} %collective-permute-done.41.refs_14_), channel_id=1, source_target_pairs={{0,16},{16,0},{1,17},{17,1},{2,18},{18,2},{3,19},{19,3},{4,20},{20... | collective-permute-start | bytes 466952 | tf_op jit(solution)/shard_map/ppermute | solution.py:36
  100.3 6.1 %collective-permute-start.42 = (bf16[608,128]{1,0:T(8,128)(2,1)}, bf16[608,128]{1,0:T(8,128)(2,1)S(1)}, u32[]{:S(2)}, u32[]{:S(2)}) collective-permute-start(bf16[608,128]{1,0:T(8,128)(2,1)} %collective-permute-done.40.refs_13_), channel_id=1, source_target_pairs={{0,8},{4,12},{8,0},{12,4},{16,20},{20,16},{24,28},{28,24},{1,9},{5... | collective-permute-start | bytes 466952 | tf_op jit(solution)/shard_map/ppermute | solution.py:48
  102.1 13.5 %collective-permute-start.23 = (bf16[608,128]{1,0:T(8,128)(2,1)S(1)}, bf16[608,128]{1,0:T(8,128)(2,1)S(1)}, u32[]{:S(2)}, u32[]{:S(2)}) collective-permute-start(bf16[608,128]{1,0:T(8,128)(2,1)S(1)} %copy-done.16), channel_id=1, source_target_pairs={{0,3},{1,2},{2,1},{3,0},{4,7},{5,6},{6,5},{7,4},{8,11},{9,10},{10,... | collective-permute-start | bytes 466952 | tf_op jit(solution)/shard_map/ppermute | solution.py:70
  104.7 3.5 %collective-permute-start.44 = (bf16[608,128]{1,0:T(8,128)(2,1)}, bf16[608,128]{1,0:T(8,128)(2,1)S(1)}, u32[]{:S(2)}, u32[]{:S(2)}) collective-permute-start(bf16[608,128]{1,0:T(8,128)(2,1)} %collective-permute-done.40.refs_13_), channel_id=1, source_target_pairs={{0,16},{16,0},{1,17},{17,1},{2,18},{18,2},{3,19},{19,3},{4,20},{20... | collective-permute-start | bytes 466952 | tf_op jit(solution)/shard_map/ppermute | solution.py:36
  106.4 4.5 %collective-permute-start.46 = (bf16[608,128]{1,0:T(8,128)(2,1)S(1)}, bf16[608,128]{1,0:T(8,128)(2,1)S(1)}, u32[]{:S(2)}, u32[]{:S(2)}) collective-permute-start(bf16[608,128]{1,0:T(8,128)(2,1)S(1)} %collective-permute-done.42.refs_15_), channel_id=1, source_target_pairs={{0,16},{16,0},{1,17},{17,1},{2,18},{18,2},{3,19},{19,3},{4,20},{20... | collective-permute-start | bytes 466952 | tf_op jit(solution)/shard_map/ppermute | solution.py:36
  106.6 9.0 %collective-permute-start.21 = (bf16[624,256]{1,0:T(8,128)(2,1)S(1)}, bf16[624,256]{1,0:T(8,128)(2,1)S(1)}, u32[]{:S(2)}, u32[]{:S(2)}) collective-permute-start(bf16[624,256]{1,0:T(8,128)(2,1)S(1)} %get-tuple-element.102), channel_id=1, source_target_pairs={{0,8},{4,12},{8,0},{12,4},{16,20},{20,16},{24,28},{28,24},{1,9},{5... | collective-permute-start | bytes 958472 | tf_op jit(solution)/shard_map/ppermute | solution.py:48
  108.2 10.7 %collective-permute-start.22 = (bf16[608,128]{1,0:T(8,128)(2,1)S(1)}, bf16[608,128]{1,0:T(8,128)(2,1)S(1)}, u32[]{:S(2)}, u32[]{:S(2)}) collective-permute-start(bf16[608,128]{1,0:T(8,128)(2,1)S(1)} %copy-done.16), channel_id=1, source_target_pairs={{0,2},{1,3},{2,0},{3,1},{4,6},{5,7},{6,4},{7,5},{8,10},{9,11},{10,... | collective-permute-start | bytes 466952 | tf_op jit(solution)/shard_map/ppermute | solution.py:70
  109.5 9.5 %collective-permute-start.27 = (bf16[2,608,128]{2,1,0:T(8,128)(2,1)S(1)}, bf16[2,608,128]{2,1,0:T(8,128)(2,1)S(1)}, u32[]{:S(2)}, u32[]{:S(2)}) collective-permute-start(bf16[2,608,128]{2,1,0:T(8,128)(2,1)S(1)} %pad_maximum_fusion.refs_4_), channel_id=1, source_target_pairs={{0,8},{4,12},{8,0},{12,4},{16,20},{20,16},{24,28},{28,24},{1,9},{5... | collective-permute-start | bytes 933896 | tf_op jit(solution)/shard_map/ppermute | solution.py:48
  110.8 9.5 %collective-permute-start.28 = (bf16[2,608,128]{2,1,0:T(8,128)(2,1)S(1)}, bf16[2,608,128]{2,1,0:T(8,128)(2,1)S(1)}, u32[]{:S(2)}, u32[]{:S(2)}) collective-permute-start(bf16[2,608,128]{2,1,0:T(8,128)(2,1)S(1)} %collective-permute-done.26.refs_5_), channel_id=1, source_target_pairs={{0,8},{4,12},{8,0},{12,4},{16,20},{20,16},{24,28},{28,24},{1,9},{5... | collective-permute-start | bytes 933896 | tf_op jit(solution)/shard_map/ppermute | solution.py:48
  115.6 7.6 %collective-permute-start.29 = (bf16[2,608,128]{2,1,0:T(8,128)(2,1)S(1)}, bf16[2,608,128]{2,1,0:T(8,128)(2,1)S(1)}, u32[]{:S(2)}, u32[]{:S(2)}) collective-permute-start(bf16[2,608,128]{2,1,0:T(8,128)(2,1)S(1)} %pad_maximum_fusion.refs_4_), channel_id=1, source_target_pairs={{0,16},{16,0},{1,17},{17,1},{2,18},{18,2},{3,19},{19,3},{4,20},{20... | collective-permute-start | bytes 933896 | tf_op jit(solution)/shard_map/ppermute | solution.py:36
  115.7 4.7 %collective-permute-start.25 = (bf16[608,128]{1,0:T(8,128)(2,1)S(1)}, bf16[608,128]{1,0:T(8,128)(2,1)S(1)}, u32[]{:S(2)}, u32[]{:S(2)}) collective-permute-start(bf16[608,128]{1,0:T(8,128)(2,1)S(1)} %collective-permute-done.23.refs_1_), channel_id=1, source_target_pairs={{0,16},{16,0},{1,17},{17,1},{2,18},{18,2},{3,19},{19,3},{4,20},{20... | collective-permute-start | bytes 466952 | tf_op jit(solution)/shard_map/ppermute | solution.py:36
  118.9 4.3 %collective-permute-start.30 = (bf16[2,608,128]{2,1,0:T(8,128)(2,1)S(1)}, bf16[2,608,128]{2,1,0:T(8,128)(2,1)S(1)}, u32[]{:S(2)}, u32[]{:S(2)}) collective-permute-start(bf16[2,608,128]{2,1,0:T(8,128)(2,1)S(1)} %collective-permute-done.26.refs_5_), channel_id=1, source_target_pairs={{0,16},{16,0},{1,17},{17,1},{2,18},{18,2},{3,19},{19,3},{4,20},{20... | collective-permute-start | bytes 933896 | tf_op jit(solution)/shard_map/ppermute | solution.py:36
  119.0 4.2 %collective-permute-start.31 = (bf16[2,608,128]{2,1,0:T(8,128)(2,1)S(1)}, bf16[2,608,128]{2,1,0:T(8,128)(2,1)S(1)}, u32[]{:S(2)}, u32[]{:S(2)}) collective-permute-start(bf16[2,608,128]{2,1,0:T(8,128)(2,1)S(1)} %collective-permute-done.27.refs_6_), channel_id=1, source_target_pairs={{0,16},{16,0},{1,17},{17,1},{2,18},{18,2},{3,19},{19,3},{4,20},{20... | collective-permute-start | bytes 933896 | tf_op jit(solution)/shard_map/ppermute | solution.py:36
  120.3 2.9 %collective-permute-start.32 = (bf16[2,608,128]{2,1,0:T(8,128)(2,1)S(1)}, bf16[2,608,128]{2,1,0:T(8,128)(2,1)S(1)}, u32[]{:S(2)}, u32[]{:S(2)}) collective-permute-start(bf16[2,608,128]{2,1,0:T(8,128)(2,1)S(1)} %collective-permute-done.28.refs_7_), channel_id=1, source_target_pairs={{0,16},{16,0},{1,17},{17,1},{2,18},{18,2},{3,19},{19,3},{4,20},{20... | collective-permute-start | bytes 933896 | tf_op jit(solution)/shard_map/ppermute | solution.py:36
  120.3 2.8 %collective-permute-start.24 = (bf16[608,128]{1,0:T(8,128)(2,1)S(1)}, bf16[608,128]{1,0:T(8,128)(2,1)S(1)}, u32[]{:S(2)}, u32[]{:S(2)}) collective-permute-start(bf16[608,128]{1,0:T(8,128)(2,1)S(1)} %collective-permute-done.22.refs_0_), channel_id=1, source_target_pairs={{0,16},{16,0},{1,17},{17,1},{2,18},{18,2},{3,19},{19,3},{4,20},{20... | collective-permute-start | bytes 466952 | tf_op jit(solution)/shard_map/ppermute | solution.py:36
  (31 other events, 187.1 us)
